TPU v7x, 32 devices: a whole 2x2x4 slice. The times are simulated.
32 devices in a mesh: pp: 4 (over z), ep: 8 (over y, x, core).
Axes of the slice: x: 2, y: 2, z: 4, core: 2. Of those that a mesh axis runs over, the one named last changes fastest.
Arguments:
- fwd_act: bfloat16 [2048, 3584], P(('pp', 'ep')), may hold values from -6 to 6
- fwd_ids: int32 [2048, 1], P(('pp', 'ep')), may hold values from 0 to 3; in each aligned block of 64 rows (0 to 63, 64 to 127, ...) at most 17 rows name the same one
- bwd_act: bfloat16 [2048, 3584], P(('pp', 'ep')), may hold values from -6 to 6
- bwd_ids: int32 [2048, 1], P(('pp', 'ep')), may hold values from 0 to 3; in each aligned block of 64 rows (0 to 63, 64 to 127, ...) at most 17 rows name the same one
- bwd_grad: bfloat16 [2048, 3584], P(('pp', 'ep')), may hold values from -6 to 6
- norm_gain: bfloat16 [4, 3584], P('pp'), may hold values from 0.099609375 to 1.8984375
- router: bfloat16 [4, 3584, 4], P('pp'), may hold values from -0.09375 to 0.09375
- w_gate: bfloat16 [32, 3584, 512], P(('pp', 'ep')), may hold values from -0.09375 to 0.09375
- w_down: bfloat16 [32, 512, 3584], P(('pp', 'ep')), may hold values from -0.1875 to 0.1875
- saved_gate: bfloat16 [4, 8, 136, 512], P('pp', 'ep'), may hold values from -6 to 6
Outputs:
- fwd_next: bfloat16 [2048, 3584], P(('pp', 'ep'))
- bwd_next: bfloat16 [2048, 3584], P(('pp', 'ep'))
Inputs may be any that keep to these rules, and one draw needn't show every extreme that they name: `fwd_ids`: each row names one held expert. Among the rows of one device no expert is named by more than 17 rows; some device names some expert exactly 17 times. `bwd_ids`: as for fwd_ids.
All inputs are finite; a program needn't handle non-finite values.
Results may differ from a plain program's by a relative error of at most 0.015.
Values may be sent and summed in bfloat16 or wider, within the bound.
No kernel may reach another device: no remote copies, remote signals or barrier semaphores. Data moves between devices by JAX's collectives and lax.ppermute only.
A program may use at most 128 MiB of HBM per device.

v0:
```python
import jax
import jax.numpy as jnp
from jax import lax
from jax.sharding import PartitionSpec as P

epsilon = 1e-06
route_scale = 2.5


def shifted(shard, axis, by):
    peers = lax.axis_size(axis)
    return lax.ppermute(shard, axis, [(i, (i + by) % peers) for i in range(peers)])


def normalize(act, gain_row):
    values = act.astype(jnp.float32)
    scaled = lax.rsqrt(jnp.mean(values * values, axis=-1, keepdims=True) + epsilon)
    return ((values * scaled * gain_row.astype(jnp.float32)).astype(jnp.bfloat16), scaled)


def gating(normed, router_table, ids):
    logits = jnp.dot(normed, router_table, preferred_element_type=jnp.float32)
    affinity = jax.nn.sigmoid(logits)
    selected = (
        ids[:, :, None] == jnp.arange(router_table.shape[1], dtype=jnp.int32)[None, None, :]
    ).astype(jnp.float32)
    gates = jnp.sum(selected * affinity[:, None, :], axis=-1)
    return (gates, affinity, selected)


def positions(flat_ids, experts):
    onehot = (flat_ids[..., None] == jnp.arange(experts, dtype=jnp.int32)).astype(jnp.int32)
    earlier = jnp.cumsum(onehot, axis=-2) - onehot
    return jnp.sum(earlier * onehot, axis=-1)


def build_send(rows, slot_index, route_count, experts, capacity, split_count):
    repeated = jnp.repeat(rows, route_count, axis=0)
    placed = jnp.zeros((experts * capacity, rows.shape[1]), rows.dtype).at[slot_index].set(repeated)
    return jnp.repeat(placed.reshape(experts, capacity, rows.shape[1]), split_count, axis=0)


def fold_slices(returned, experts, split_count):
    wide = returned.astype(jnp.float32).reshape((experts, split_count) + returned.shape[1:])
    return jnp.sum(wide, axis=1).reshape((-1,) + returned.shape[2:])


def slice_forward(slot_rows, gate_part, down_part):
    gate_proj = jnp.einsum("scd,dh->sch", slot_rows, gate_part, preferred_element_type=jnp.float32)
    hidden = jax.nn.silu(gate_proj).astype(jnp.bfloat16)
    return jnp.einsum("sch,hd->scd", hidden, down_part, preferred_element_type=jnp.float32).astype(
        jnp.bfloat16
    )


def slice_backward(slot_grads, saved_rows, gate_part, down_part):
    gate_proj = saved_rows.astype(jnp.float32)
    hidden = jax.nn.silu(gate_proj).astype(jnp.bfloat16)
    output = jnp.einsum(
        "sch,hd->scd", hidden, down_part, preferred_element_type=jnp.float32
    ).astype(jnp.bfloat16)
    dot_part = jnp.sum(slot_grads.astype(jnp.float32) * output.astype(jnp.float32), axis=-1).astype(
        jnp.bfloat16
    )
    grad_hidden = jnp.einsum(
        "scd,hd->sch", slot_grads, down_part, preferred_element_type=jnp.float32
    )
    sigmoid_gate = jax.nn.sigmoid(gate_proj)
    grad_gate = (grad_hidden * sigmoid_gate * (1.0 + gate_proj * (1.0 - sigmoid_gate))).astype(
        jnp.bfloat16
    )
    grad_part = jnp.einsum(
        "sch,dh->scd", grad_gate, gate_part, preferred_element_type=jnp.float32
    ).astype(jnp.bfloat16)
    return (grad_part, dot_part)


def finish_forward(act, gates, gathered):
    mixed = jnp.sum(gates[:, :, None] * gathered, axis=1)
    return (act.astype(jnp.float32) + route_scale * mixed).astype(jnp.bfloat16)


def finish_backward(
    act, grad, scaled, gain_row, router_table, gates, affinity, selected, grad_rows, dot_terms
):
    route_coef = route_scale * gates
    grad_normed = jnp.sum(route_coef[:, :, None] * grad_rows, axis=1)
    grad_gates = route_scale * dot_terms
    grad_affinity = jnp.sum(selected * grad_gates[:, :, None], axis=1)
    grad_logits = (grad_affinity * affinity * (1.0 - affinity)).astype(jnp.bfloat16)
    grad_normed = grad_normed + jnp.dot(
        grad_logits, router_table.T, preferred_element_type=jnp.float32
    )
    values = act.astype(jnp.float32)
    grad_pre = grad_normed * gain_row.astype(jnp.float32)
    grad_act = scaled * (
        grad_pre - values * scaled * scaled * jnp.mean(grad_pre * values, axis=-1, keepdims=True)
    )
    return (grad.astype(jnp.float32) + grad_act).astype(jnp.bfloat16)


def on_device(
    fwd_act, fwd_ids, bwd_act, bwd_ids, bwd_grad, norm_gain, router, w_gate, w_down, saved_gate
):
    groups = lax.axis_size("ep")
    gain_row = norm_gain[0]
    router_table = router[0]
    experts = router_table.shape[1]
    split_count = groups // experts
    tok_rows, route_count = fwd_ids.shape
    model_width = fwd_act.shape[1]
    capacity = tok_rows // experts + 1
    gate_part = w_gate[0]
    down_part = w_down[0]
    saved_rows = saved_gate.reshape(groups, capacity, saved_gate.shape[-1])
    fwd_normed, fwd_scaled = normalize(fwd_act, gain_row)
    fwd_gates, fwd_aff, fwd_sel = gating(fwd_normed, router_table, fwd_ids)
    fwd_flat = fwd_ids.reshape(-1)
    fwd_place = positions(fwd_flat, experts)
    fwd_slot = fwd_flat * capacity + fwd_place
    bwd_normed, bwd_scaled = normalize(bwd_act, gain_row)
    bwd_gates, bwd_aff, bwd_sel = gating(bwd_normed, router_table, bwd_ids)
    bwd_flat = bwd_ids.reshape(-1)
    bwd_place = positions(bwd_flat, experts)
    bwd_slot = bwd_flat * capacity + bwd_place
    fwd_send = build_send(fwd_normed, fwd_slot, route_count, experts, capacity, split_count)
    grad_send = build_send(bwd_grad, bwd_slot, route_count, experts, capacity, split_count)
    fwd_back = lax.all_to_all(
        slice_forward(
            lax.all_to_all(fwd_send, "ep", split_axis=0, concat_axis=0, tiled=True),
            gate_part,
            down_part,
        ),
        "ep",
        split_axis=0,
        concat_axis=0,
        tiled=True,
    )
    got_grads = lax.all_to_all(grad_send, "ep", split_axis=0, concat_axis=0, tiled=True)
    grad_part, dot_part = slice_backward(got_grads, saved_rows, gate_part, down_part)
    bwd_back, dots_back = (
        lax.all_to_all(grad_part, "ep", split_axis=0, concat_axis=0, tiled=True),
        lax.all_to_all(dot_part, "ep", split_axis=0, concat_axis=0, tiled=True),
    )
    fwd_gathered = fold_slices(fwd_back, experts, split_count)[fwd_slot].reshape(
        tok_rows, route_count, model_width
    )
    fwd_result = finish_forward(fwd_act, fwd_gates, fwd_gathered)
    bwd_rows = fold_slices(bwd_back, experts, split_count)[bwd_slot].reshape(
        tok_rows, route_count, model_width
    )
    bwd_dots = fold_slices(dots_back, experts, split_count)[bwd_slot].reshape(tok_rows, route_count)
    bwd_result = finish_backward(
        bwd_act,
        bwd_grad,
        bwd_scaled,
        gain_row,
        router_table,
        bwd_gates,
        bwd_aff,
        bwd_sel,
        bwd_rows,
        bwd_dots,
    )
    fwd_next = shifted(fwd_result, "pp", 1)
    bwd_next = shifted(bwd_result, "pp", -1)
    return (fwd_next, bwd_next)


def solution(mesh):
    return jax.shard_map(
        on_device,
        mesh=mesh,
        in_specs=(
            P(("pp", "ep"), None),
            P(("pp", "ep"), None),
            P(("pp", "ep"), None),
            P(("pp", "ep"), None),
            P(("pp", "ep"), None),
            P("pp", None),
            P("pp", None, None),
            P(("pp", "ep"), None, None),
            P(("pp", "ep"), None, None),
            P("pp", "ep", None, None),
        ),
        out_specs=(P(("pp", "ep"), None), P(("pp", "ep"), None)),
        check_vma=False,
    )
```

profile of v0, /device:TPU:0, one launch (start us, length us, event | category | flops | bytes accessed | tf_op | source)
XLA Modules:
  0.0 127.7 jit_solution(1769097074928051907)
XLA Ops:
  1.6 0.7 select_reduce_fusion
  2.9 1.8 %scatter_custom_fusion.1 = bf16[68,3584]{1,0:T(8,128)(2,1)S(1)} fusion(s32[64]{0:T(128)S(1)} %fusion.78, bf16[64,3584]{1,0:T(8,128)(2,1)} %param.14, bf16[]{:T(256)} %constant.31.clone.1), kind=kCustom, calls=%fused_computation.66 | custom fusion | bytes 487936 | tf_op jit(solution)/shard_map/scatter | solution.py:39
  5.0 1.2 broadcast_in_dim.5
  6.2 5.3 %all-to-all-start.2 = ((bf16[8,17,3584]{2,1,0:T(8,128)(2,1)}), bf16[8,17,3584]{2,1,0:T(8,128)(2,1)S(1)}, u32[]{:S(2)}, u32[]{:S(2)}) async-start(bf16[8,17,3584]{2,1,0:T(8,128)(2,1)} %bitcast.13), calls=%async_computation.2 | async-start | bytes 2752512 | tf_op jit(solution)/shard_map/all_to_all | solution.py:139
  12.6 1.5 %scatter_custom_fusion = bf16[68,3584]{1,0:T(8,128)(2,1)S(1)} fusion(s32[64]{0:T(128)S(1)} %fusion.77, bf16[]{:T(256)} %constant.31.clone.1, bf16[64,3584]{1,0:T(8,128)(2,1)S(1)} %copy-done.1, f32[3584]{0:T(1024)S(1)} %convert_reduce_fusion.2, f32[64]{0:T(128)S(1)} %add_rsqrt_fusion.1), kind=kCustom, calls=%fused_computation.68 | custom fusion | flops 917504 | bytes 963074 | tf_op jit(solution)/shard_map/scatter | solution.py:39
  14.4 0.9 fusion.29
  15.3 1.1 multiply_convert_fusion.1
  16.4 14.0 %all-to-all-done.2 = bf16[8,17,3584]{2,1,0:T(8,128)(2,1)S(1)} async-done(((bf16[8,17,3584]{2,1,0:T(8,128)(2,1)}), bf16[8,17,3584]{2,1,0:T(8,128)(2,1)S(1)}, u32[]{:S(2)}, u32[]{:S(2)}) %all-to-all-start.2) | async-done | bytes 974880 | tf_op jit(solution)/shard_map/all_to_all | solution.py:139
  30.4 1.2 broadcast_in_dim.4
  31.6 4.3 %all-to-all-start = ((bf16[8,17,3584]{2,1,0:T(8,128)(2,1)}), bf16[8,17,3584]{2,1,0:T(8,128)(2,1)}, u32[]{:S(2)}, u32[]{:S(2)}) async-start(bf16[8,17,3584]{2,1,0:T(8,128)(2,1)} %bitcast.4), calls=%async_computation | async-start | bytes 2752512 | tf_op jit(solution)/shard_map/all_to_all | solution.py:130
  36.4 3.1 %fusion.10 = bf16[8,17]{1,0:T(8,128)(2,1)S(1)} fusion(bf16[8,17,512]{2,1,0:T(8,128)(2,1)S(1)} %convert_element_type.117, bf16[1,512,3584]{2,1,0:T(8,128)(2,1)} %param.18, bf16[8,17,3584]{2,1,0:T(8,128)(2,1)S(1)} %all-to-all-done.2), kind=kOutput, calls=%fused_computation.21 | convolution fusion | flops 501559168 | bytes 4784400 | tf_op jit(solution)/shard_map/sch,hd->scd/dot_general | solution.py:59
  40.1 14.7 %all-to-all-done = bf16[8,17,3584]{2,1,0:T(8,128)(2,1)} async-done(((bf16[8,17,3584]{2,1,0:T(8,128)(2,1)}), bf16[8,17,3584]{2,1,0:T(8,128)(2,1)}, u32[]{:S(2)}, u32[]{:S(2)}) %all-to-all-start) | async-done | bytes 974880 | tf_op jit(solution)/shard_map/all_to_all | solution.py:130
  54.8 3.3 %all-to-all-start.4 = ((bf16[8,1,17]{2,1,0:T(2,128)(2,1)}), bf16[8,1,17]{2,1,0:T(2,128)(2,1)S(1)}, u32[]{:S(2)}, u32[]{:S(2)}) async-start(bf16[8,1,17]{2,1,0:T(2,128)(2,1)} %copy.28), calls=%async_computation.4 | async-start | bytes 8192 | tf_op jit(solution)/shard_map/all_to_all | solution.py:143
  58.1 6.8 %convolution_convert_fusion.1 = bf16[8,17,3584]{2,1,0:T(8,128)(2,1)} fusion(bf16[1,3584,512]{2,1,0:T(8,128)(2,1)} %param.17, bf16[8,17,3584]{2,1,0:T(8,128)(2,1)S(1)} %all-to-all-done.2, bf16[1,512,3584]{2,1,0:T(8,128)(2,1)} %param.18, f32[8,17,512]{2,1,0:T(8,128)S(1)} %reshape.165), kind=kOutput, calls=%fused_computation.8 | convolution fusion | flops 999358464 | bytes 9568256 | tf_op jit(solution)/shard_map/sch,dh->scd/dot_general | solution.py:72
  65.0 4.3 %all-to-all-start.3 = ((bf16[8,17,3584]{2,1,0:T(8,128)(2,1)}), bf16[8,17,3584]{2,1,0:T(8,128)(2,1)S(1)}, u32[]{:S(2)}, u32[]{:S(2)}) async-start(bf16[8,17,3584]{2,1,0:T(8,128)(2,1)} %convolution_convert_fusion.1), calls=%async_computation.3 | async-start | bytes 2752512 | tf_op jit(solution)/shard_map/all_to_all | solution.py:142
  69.2 6.4 %convolution_convert_fusion.2 = bf16[8,17,3584]{2,1,0:T(8,128)(2,1)} fusion(bf16[1,512,3584]{2,1,0:T(8,128)(2,1)} %param.18, bf16[8,17,3584]{2,1,0:T(8,128)(2,1)} %all-to-all-done, bf16[1,3584,512]{2,1,0:T(8,128)(2,1)} %param.17), kind=kOutput, calls=%fused_computation.9 | convolution fusion | flops 999079936 | bytes 9289728 | tf_op jit(solution)/shard_map/sch,hd->scd/dot_general | solution.py:51
  75.8 0.8 gather_fusion.2
  76.6 11.6 %all-to-all-done.3 = bf16[8,17,3584]{2,1,0:T(8,128)(2,1)S(1)} async-done(((bf16[8,17,3584]{2,1,0:T(8,128)(2,1)}), bf16[8,17,3584]{2,1,0:T(8,128)(2,1)S(1)}, u32[]{:S(2)}, u32[]{:S(2)}) %all-to-all-start.3) | async-done | bytes 974880 | tf_op jit(solution)/shard_map/all_to_all | solution.py:142
  88.1 3.6 %all-to-all-start.1 = ((bf16[8,17,3584]{2,1,0:T(8,128)(2,1)}), bf16[8,17,3584]{2,1,0:T(8,128)(2,1)S(1)}, u32[]{:S(2)}, u32[]{:S(2)}) async-start(bf16[8,17,3584]{2,1,0:T(8,128)(2,1)} %convolution_convert_fusion.2), calls=%async_computation.1 | async-start | bytes 2752512 | tf_op jit(solution)/shard_map/all_to_all | solution.py:128
  91.7 1.4 %convert_reduce_fusion = f32[4,17,3584]{2,1,0:T(8,128)} fusion(bf16[8,17,3584]{2,1,0:T(8,128)(2,1)S(1)} %all-to-all-done.3), kind=kLoop, calls=%fused_computation.19 | loop fusion | flops 731136 | bytes 1949696 | tf_op jit(solution)/shard_map/reduce_sum | solution.py:45
  93.1 1.5 %reshape.160 = f32[68,3584]{1,0:T(8,128)S(1)} reshape(f32[4,17,3584]{2,1,0:T(8,128)} %convert_reduce_fusion) | data formatting | bytes 1949696 | tf_op jit(solution)/shard_map/reshape | solution.py:45
  94.6 1.8 %gather_fusion.1 = f32[64,3584]{1,0:T(8,128)} fusion(f32[68,3584]{1,0:T(8,128)S(1)} %reshape.160, s32[1024]{0:T(1024)S(1)} %pad_clamp_fusion), kind=kCustom, calls=%fused_computation.1 | custom fusion | bytes 1835264 | tf_op jit(solution)/shard_map/gather | solution.py:149
  96.4 1.7 %fusion.43 = (f32[64]{0:T(128)S(1)}, f32[64,3584]{1,0:T(8,128)S(1)}) fusion(bf16[64,3584]{1,0:T(8,128)(2,1)S(1)} %copy-done.3, f32[3584]{0:T(1024)S(1)} %convert_reduce_fusion.2, bf16[1,3584,4]{1,2,0:T(4,128)(2,1)S(1)} %copy-done, f32[64,4]{0,1:T(4,128)S(1)} %get-tuple-element.3, f32[64]{0:T(128)S(1)} %get-tuple-element.6, s32[64]{0:T(128)S(1)} %bitcast.76, ...), kind=kOutput, calls=%fused_computation.54 | convolution fusion | flops 3212736 | bytes 2338816 | tf_op jit(solution)/shard_map/dot_general | solution.py:91
  98.1 2.1 %fusion.37 = bf16[64,3584]{1,0:T(8,128)(2,1)} fusion(f32[64,3584]{1,0:T(8,128)S(1)} %get-tuple-element.5, bf16[64,3584]{1,0:T(8,128)(2,1)S(1)} %copy-done.3, bf16[64,3584]{1,0:T(8,128)(2,1)} %param.14, f32[64]{0:T(128)S(1)} %broadcast_multiply_fusion.2, f32[64]{0:T(128)S(1)} %copy-done.12), kind=kLoop, calls=%fused_computation.48 | loop fusion | flops 2064384 | bytes 2294272 | tf_op jit(solution)/shard_map/convert_element_type | solution.py:99
  100.3 3.6 %collective-permute-start.1 = (bf16[64,3584]{1,0:T(8,128)(2,1)}, bf16[64,3584]{1,0:T(8,128)(2,1)}, u32[]{:S(2)}, u32[]{:S(2)}) collective-permute-start(bf16[64,3584]{1,0:T(8,128)(2,1)} %fusion.37), channel_id=1, source_target_pairs={{0,24},{8,0},{16,8},{24,16},{1,25},{9,1},{17,9},{25,17},{2,26},{10... | collective-permute-start | bytes 1376264 | tf_op jit(solution)/shard_map/ppermute | solution.py:12
  103.9 6.7 %all-to-all-done.1 = bf16[8,17,3584]{2,1,0:T(8,128)(2,1)S(1)} async-done(((bf16[8,17,3584]{2,1,0:T(8,128)(2,1)}), bf16[8,17,3584]{2,1,0:T(8,128)(2,1)S(1)}, u32[]{:S(2)}, u32[]{:S(2)}) %all-to-all-start.1) | async-done | bytes 974880 | tf_op jit(solution)/shard_map/all_to_all | solution.py:128
  111.0 0.9 gather_fusion
  112.1 1.6 %collective-permute-start = (bf16[64,3584]{1,0:T(8,128)(2,1)S(1)}, bf16[64,3584]{1,0:T(8,128)(2,1)S(1)}, u32[]{:S(2)}, u32[]{:S(2)}) collective-permute-start(bf16[64,3584]{1,0:T(8,128)(2,1)S(1)} %fusion.41), channel_id=1, source_target_pairs={{0,8},{8,16},{16,24},{24,0},{1,9},{9,17},{17,25},{25,1},{2,10},{10... | collective-permute-start | bytes 1376264 | tf_op jit(solution)/shard_map/ppermute | solution.py:12
  113.8 1.3 %collective-permute-done.1 = bf16[64,3584]{1,0:T(8,128)(2,1)} collective-permute-done((bf16[64,3584]{1,0:T(8,128)(2,1)}, bf16[64,3584]{1,0:T(8,128)(2,1)}, u32[]{:S(2)}, u32[]{:S(2)}) %collective-permute-start.1) | collective-permute-done | bytes 458784 | tf_op jit(solution)/shard_map/ppermute | solution.py:12
  115.1 10.0 %collective-permute-done = bf16[64,3584]{1,0:T(8,128)(2,1)S(1)} collective-permute-done((bf16[64,3584]{1,0:T(8,128)(2,1)S(1)}, bf16[64,3584]{1,0:T(8,128)(2,1)S(1)}, u32[]{:S(2)}, u32[]{:S(2)}) %collective-permute-start) | collective-permute-done | bytes 458784 | tf_op jit(solution)/shard_map/ppermute | solution.py:12
  125.1 0.8 copy.31
  125.9 1.8 %copy.32 = bf16[64,3584]{1,0:T(8,128)(2,1)} copy(bf16[64,3584]{1,0:T(8,128)(2,1)} %collective-permute-done.1) | data formatting | bytes 917504
  (59 shorter events, 5.0 us)
Async XLA Ops:
  0.6 13.8 %copy-start = (bf16[1,3584,4]{1,2,0:T(4,128)(2,1)S(1)}, bf16[1,3584,4]{1,2,0:T(4,128)(2,1)}, u32[]{:S(2)}) copy-start(bf16[1,3584,4]{1,2,0:T(4,128)(2,1)} %param.16) | copy-start | bytes 86020
  4.8 6.7 %copy-start.5 = (bf16[1,3584]{1,0:T(2,128)(2,1)S(1)}, bf16[1,3584]{1,0:T(2,128)(2,1)}, u32[]{:S(2)}) copy-start(bf16[1,3584]{1,0:T(2,128)(2,1)} %param.15) | copy-start | bytes 21508
  4.8 6.7 %copy-start.7 = (s32[64,1]{0,1:T(1,128)S(1)}, s32[64,1]{0,1:T(1,128)}, u32[]{:S(2)}) copy-start(s32[64,1]{0,1:T(1,128)} %param.11) | copy-start | bytes 772
  5.0 6.8 %copy-start.1 = (bf16[64,3584]{1,0:T(8,128)(2,1)S(1)}, bf16[64,3584]{1,0:T(8,128)(2,1)}, u32[]{:S(2)}) copy-start(bf16[64,3584]{1,0:T(8,128)(2,1)} %param.10) | copy-start | bytes 1376260
  6.2 8.1 %copy-start.2 = (bf16[64,3584]{1,0:T(8,128)(2,1)S(1)}, bf16[64,3584]{1,0:T(8,128)(2,1)}, u32[]{:S(2)}) copy-start(bf16[64,3584]{1,0:T(8,128)(2,1)} %param.12) | copy-start | bytes 1376260
  6.2 24.2 %all-to-all-start.2 = ((bf16[8,17,3584]{2,1,0:T(8,128)(2,1)}), bf16[8,17,3584]{2,1,0:T(8,128)(2,1)S(1)}, u32[]{:S(2)}, u32[]{:S(2)}) async-start(bf16[8,17,3584]{2,1,0:T(8,128)(2,1)} %bitcast.13), calls=%async_computation.2 | async-start | bytes 2752512 | tf_op jit(solution)/shard_map/all_to_all | solution.py:139
  12.1 0.5 copy-start.8
  15.3 20.6 %copy-start.4 = (bf16[1,1,136,512]{3,2,1,0:T(8,128)(2,1)S(1)}, bf16[1,1,136,512]{3,2,1,0:T(8,128)(2,1)}, u32[]{:S(2)}) copy-start(bf16[1,1,136,512]{3,2,1,0:T(8,128)(2,1)} %param.19) | copy-start | bytes 417796
  16.4 19.6 %copy-start.6 = (s32[64,1]{0,1:T(1,128)S(1)}, s32[64,1]{0,1:T(1,128)}, u32[]{:S(2)}) copy-start(s32[64,1]{0,1:T(1,128)} %param.13) | copy-start | bytes 772
  31.6 23.2 %all-to-all-start = ((bf16[8,17,3584]{2,1,0:T(8,128)(2,1)}), bf16[8,17,3584]{2,1,0:T(8,128)(2,1)}, u32[]{:S(2)}, u32[]{:S(2)}) async-start(bf16[8,17,3584]{2,1,0:T(8,128)(2,1)} %bitcast.4), calls=%async_computation | async-start | bytes 2752512 | tf_op jit(solution)/shard_map/all_to_all | solution.py:130
  36.0 3.4 %copy-start.11 = (f32[64]{0:T(128)}, f32[64]{0:T(128)S(1)}, u32[]{:S(2)}) copy-start(f32[64]{0:T(128)S(1)} %add_rsqrt_fusion) | copy-start | bytes 772
  54.8 10.2 %all-to-all-start.4 = ((bf16[8,1,17]{2,1,0:T(2,128)(2,1)}), bf16[8,1,17]{2,1,0:T(2,128)(2,1)S(1)}, u32[]{:S(2)}, u32[]{:S(2)}) async-start(bf16[8,1,17]{2,1,0:T(2,128)(2,1)} %copy.28), calls=%async_computation.4 | async-start | bytes 8192 | tf_op jit(solution)/shard_map/all_to_all | solution.py:143
  65.0 4.3 %copy-start.9 = (s32[64]{0:T(128)S(1)}, s32[64]{0:T(128)}, u32[]{:S(2)}) copy-start(s32[64]{0:T(128)} %copy-done.8) | copy-start | bytes 772
  65.0 23.2 %all-to-all-start.3 = ((bf16[8,17,3584]{2,1,0:T(8,128)(2,1)}), bf16[8,17,3584]{2,1,0:T(8,128)(2,1)S(1)}, u32[]{:S(2)}, u32[]{:S(2)}) async-start(bf16[8,17,3584]{2,1,0:T(8,128)(2,1)} %convolution_convert_fusion.1), calls=%async_computation.3 | async-start | bytes 2752512 | tf_op jit(solution)/shard_map/all_to_all | solution.py:142
  88.1 22.4 %all-to-all-start.1 = ((bf16[8,17,3584]{2,1,0:T(8,128)(2,1)}), bf16[8,17,3584]{2,1,0:T(8,128)(2,1)S(1)}, u32[]{:S(2)}, u32[]{:S(2)}) async-start(bf16[8,17,3584]{2,1,0:T(8,128)(2,1)} %convolution_convert_fusion.2), calls=%async_computation.1 | async-start | bytes 2752512 | tf_op jit(solution)/shard_map/all_to_all | solution.py:128
  94.6 1.8 %copy-start.3 = (bf16[64,3584]{1,0:T(8,128)(2,1)S(1)}, bf16[64,3584]{1,0:T(8,128)(2,1)}, u32[]{:S(2)}) copy-start(bf16[64,3584]{1,0:T(8,128)(2,1)} %param.12) | copy-start | bytes 1376260
  94.6 3.5 %copy-start.12 = (f32[64]{0:T(128)S(1)}, f32[64]{0:T(128)}, u32[]{:S(2)}) copy-start(f32[64]{0:T(128)} %copy-done.11) | copy-start | bytes 772
  100.3 14.8 %collective-permute-start.1 = (bf16[64,3584]{1,0:T(8,128)(2,1)}, bf16[64,3584]{1,0:T(8,128)(2,1)}, u32[]{:S(2)}, u32[]{:S(2)}) collective-permute-start(bf16[64,3584]{1,0:T(8,128)(2,1)} %fusion.37), channel_id=1, source_target_pairs={{0,24},{8,0},{16,8},{24,16},{1,25},{9,1},{17,9},{25,17},{2,26},{10... | collective-permute-start | bytes 1376264 | tf_op jit(solution)/shard_map/ppermute | solution.py:12
  111.0 0.9 copy-start.10
  112.1 13.0 %collective-permute-start = (bf16[64,3584]{1,0:T(8,128)(2,1)S(1)}, bf16[64,3584]{1,0:T(8,128)(2,1)S(1)}, u32[]{:S(2)}, u32[]{:S(2)}) collective-permute-start(bf16[64,3584]{1,0:T(8,128)(2,1)S(1)} %fusion.41), channel_id=1, source_target_pairs={{0,8},{8,16},{16,24},{24,0},{1,9},{9,17},{17,25},{25,1},{2,10},{10... | collective-permute-start | bytes 1376264 | tf_op jit(solution)/shard_map/ppermute | solution.py:12
where the time goes:
time: 128 us
  waiting for transfers between devices  58.4 us (46%)
  starting transfers between devices  26 us (20%)
  matrix products  19.3 us (15%)
  local copies, waits for them, and re-layouts  13.9 us (11%)
  other arithmetic  9.21 us (7%)
    all_to_all x1, waiting for transfers between devices, on_device(): lax.all_to_all(fwd_send, 'ep', split_axis=0, concat_axis=0, tiled=True)  14.7 us
    all_to_all x1, waiting for transfers between devices, on_device(): lax.all_to_all(grad_send, 'ep', split_axis=0, concat_axis=0, tiled=True)  14 us
    all_to_all x1, waiting for transfers between devices, on_device(): lax.all_to_all(grad_part, 'ep', split_axis=0, concat_axis=0, tiled=True)  11.6 us
    ppermute x2, waiting for transfers between devices, shifted(): lax.ppermute(shard, axis, [(i, (i + by) % peers) for i in range(peers)])  11.4 us
    dot_general x1, matrix products, slice_backward(): jnp.einsum('sch,dh->scd', grad_gate, gate_part, preferred_element_type=jn...  6.84 us
    all_to_all x1, waiting for transfers between devices, on_device(): lax.all_to_all(slice_forward(lax.all_to_all(fwd_send, 'ep', split_axis=0,...  6.69 us
    dot_general x1, matrix products, slice_forward(): jnp.einsum('sch,hd->scd', hidden, down_part, preferred_element_type=jnp.f...  6.44 us
    all_to_all x1, starting transfers between devices, on_device(): lax.all_to_all(grad_send, 'ep', split_axis=0, concat_axis=0, tiled=True)  5.3 us
  transfers between devices with their start and end apart: 7, of which 6 were waited for; matrix products, arithmetic and copies ran while one was open for 26% of the time, Pallas kernels for 0%

commit v1 on v0

v1 whole, which is shorter than its diff:
```python
import jax
import jax.numpy as jnp
from jax import lax
from jax.experimental import pallas as pl
from jax.experimental.pallas import tpu as pltpu
from jax.sharding import PartitionSpec as P

epsilon = 1e-06
route_scale = 2.5
fold = 256
none = 255.0
f32 = jnp.float32
bf16 = jnp.bfloat16


def call(body, outs, scratch, flops, nbytes, name):
    return pl.pallas_call(
        body,
        out_shape=outs,
        scratch_shapes=scratch,
        compiler_params=pltpu.CompilerParams(vmem_limit_bytes=48 * 1024 * 1024),
        cost_estimate=pl.CostEstimate(flops=flops, bytes_accessed=nbytes, transcendentals=0),
        name=name,
    )


def shape(dims, kind=bf16):
    return jax.ShapeDtypeStruct(dims, kind)


class Sizes:
    def __init__(self, groups, experts, tokens, width):
        self.experts = experts
        self.split = groups // experts
        self.tokens = tokens
        self.width = width
        self.main = tokens // experts
        self.cap = self.main + 1
        self.pieces = width // fold
        self.wide = width + fold
        self.rows = tokens + 16
        self.extra = max(16, 8 * self.split)
        assert self.main == 16 and self.pieces <= 14 and width % fold == 0
        assert experts <= 8 and experts & (experts - 1) == 0 and self.split & (self.split - 1) == 0


def pack_last(row, tile):
    for i in range(row.shape[1] // fold):
        tile[i : i + 1, :] = row[:, i * fold : (i + 1) * fold]


def unpack_last(chunk, z, tile, target, at):
    tile[...] = chunk[:, z.width :].astype(f32)
    for i in range(z.pieces):
        target[at : at + 1, i * fold : (i + 1) * fold] = tile[i : i + 1, :]


def slot_matrices(ids, block, z):
    tokens = z.tokens
    sub = lax.broadcasted_iota(jnp.int32, (tokens, tokens), 0)
    lane = lax.broadcasted_iota(jnp.int32, (tokens, tokens), 1)
    column = jnp.bitwise_xor(ids, block)
    row = jnp.sum(jnp.where(sub == lane, column, 0), axis=0, keepdims=True)
    same = column == row
    place_row = jnp.sum(jnp.where(same & (sub < lane), 1, 0), axis=0, keepdims=True)
    place_column = jnp.sum(jnp.where(same & (lane < sub), 1, 0), axis=1, keepdims=True)

    def slot(expert, place):
        return jnp.where(place < z.main, expert * z.main + place, tokens + expert)

    slot_row = slot(row, place_row)
    slot_column = slot(column, place_column)
    by_slot = lax.broadcasted_iota(jnp.int32, (z.rows, tokens), 0) == slot_row
    by_token = lax.broadcasted_iota(jnp.int32, (tokens, fold), 1) == slot_column
    token = lax.broadcasted_iota(jnp.int32, (tokens, fold), 0).astype(f32)
    token_row = jnp.sum(jnp.where(by_token, token - none, 0.0), axis=0, keepdims=True) + none
    return jnp.where(by_slot, 1.0, 0.0).astype(bf16), token_row


def write_chunks(z, selector, token_row, rows_ref, tile, chunks):
    last = jnp.dot(
        selector[z.tokens :, :], rows_ref[...], preferred_element_type=f32
    )
    step = z.width // 4
    for col in range(0, z.width, step):
        got = jnp.dot(
            selector[: z.tokens, :], rows_ref[:, col : col + step], preferred_element_type=f32
        ).astype(bf16)
        for k in range(z.experts):
            chunks[k][:, col : col + step] = got[k * z.main : (k + 1) * z.main]
    for k in range(z.experts):
        tile[...] = jnp.zeros_like(tile)
        pack_last(last[k : k + 1, :], tile)
        tile[z.pieces : z.pieces + 1, :] = token_row
        chunks[k][:, z.width :] = tile[...].astype(bf16)


def chunk_body(z, count, block, ids, *refs):
    sources, outs, tile = refs[:count], refs[count:-1], refs[-1]
    selector, token_row = slot_matrices(ids[...], block[0], z)
    for j in range(count):
        write_chunks(
            z, selector, token_row, sources[j], tile, outs[j * z.experts : (j + 1) * z.experts]
        )


def make_chunks(z, block, ids, sources, name):
    count = len(sources)

    def body(*refs):
        chunk_body(z, count, *refs)

    outs = call_with_scalar(
        body,
        [shape((z.main, z.wide))] * (z.experts * count),
        [pltpu.VMEM((16, fold), f32)],
        1 + count,
        2 * count * z.rows * z.tokens * z.width,
        4 * count * z.tokens * z.width,
        name,
    )(block, ids, *sources)
    return [outs[j * z.experts : (j + 1) * z.experts] for j in range(count)]


def call_with_scalar(body, outs, scratch, arrays, flops, nbytes, name):
    return pl.pallas_call(
        body,
        out_shape=outs,
        in_specs=[pl.BlockSpec(memory_space=pltpu.SMEM)]
        + [pl.BlockSpec(memory_space=pltpu.VMEM)] * arrays,
        scratch_shapes=scratch,
        compiler_params=pltpu.CompilerParams(vmem_limit_bytes=48 * 1024 * 1024),
        cost_estimate=pl.CostEstimate(flops=flops, bytes_accessed=nbytes, transcendentals=0),
        name=name,
    )


def collect_rows(z, chunks, held, last, tile):
    last[...] = jnp.zeros_like(last)
    for m in range(z.split):
        for k in range(z.experts):
            chunk = chunks[m * z.experts + k]
            at = m * z.tokens + k * z.main
            held[at : at + z.main, :] = chunk[:, : z.width]
            unpack_last(chunk, z, tile, last, m * 8 + k)
    held[z.split * z.tokens :, :] = last[...].astype(bf16)


def write_parts(z, values, outs, col):
    step = values.shape[1]
    for m in range(z.split):
        outs[m][: z.tokens, col : col + step] = values[
            m * z.tokens : (m + 1) * z.tokens
        ].astype(bf16)
        at = z.split * z.tokens + m * 8
        tail = values[at : at + 8]
        outs[m][z.tokens :, col : col + step] = jnp.concatenate(
            [tail, jnp.zeros((8, step), f32)], axis=0
        ).astype(bf16)


def norm_rows(h, gain):
    inv = lax.rsqrt(jnp.mean(h * h, axis=-1, keepdims=True) + epsilon)
    return (h * inv * gain).astype(bf16), inv


def forward_body(z, *refs):
    count = z.split * z.experts
    chunks = refs[:count]
    gain_ref, router_ref, gate_ref, down_ref = refs[count : count + 4]
    outs = refs[count + 4 : count + 4 + z.split]
    gates, held, last, tile = refs[count + 4 + z.split :]
    collect_rows(z, chunks, held, last, tile)
    gain = gain_ref[...].astype(f32)
    router = router_ref[...].astype(f32)
    total = held.shape[0]
    for at in range(0, total, 16):
        normed, _ = norm_rows(held[at : at + 16, :].astype(f32), gain)
        held[at : at + 16, :] = normed
        own = at if at < z.tokens else (z.tokens if at == z.split * z.tokens else None)
        if own is not None:
            logits = jnp.sum(normed.astype(f32) * router, axis=-1, keepdims=True)
            gates[own : own + 16, :] = jnp.broadcast_to(jax.nn.sigmoid(logits), (16, 128))
    gate_proj = jnp.dot(held[...], gate_ref[0], preferred_element_type=f32)
    hidden = jax.nn.silu(gate_proj).astype(bf16)
    step = 512
    for col in range(0, z.width, step):
        part = jnp.dot(hidden, down_ref[0, :, col : col + step], preferred_element_type=f32)
        write_parts(z, part, outs, col)


def experts_forward(z, chunks, gain, router_row, w_gate, w_down):
    total = z.split * z.tokens + z.extra

    def body(*refs):
        forward_body(z, *refs)

    outs = call(
        body,
        [shape((z.rows, z.width))] * z.split + [shape((z.rows, 128), f32)],
        [
            pltpu.VMEM((total, z.width), bf16),
            pltpu.VMEM((z.extra, z.width), f32),
            pltpu.VMEM((16, fold), f32),
        ],
        4 * total * w_gate.shape[1] * w_gate.shape[2],
        4 * w_gate.shape[1] * w_gate.shape[2],
        "experts_forward",
    )(*chunks, gain, router_row, w_gate, w_down)
    return outs[: z.split], outs[z.split]


def saved_selector(z, block, core, total, slots):
    row = lax.broadcasted_iota(jnp.int32, (total, slots), 0)
    slot = lax.broadcasted_iota(jnp.int32, (total, slots), 1)
    tail = row - z.split * z.tokens
    is_main = tail < 0
    m = jnp.where(is_main, row // z.tokens, tail // 8)
    k = jnp.where(is_main, row % z.tokens // z.main, tail % 8)
    p = jnp.where(is_main, row % z.main, z.main)
    source = jnp.bitwise_xor(k, block) * z.split + jnp.bitwise_xor(m, core)
    wanted = jnp.where((k < z.experts) & (m < z.split), source * z.cap + p, -1)
    return jnp.where(slot == wanted, 1.0, 0.0).astype(bf16)


nt = (((1,), (1,)), ((), ()))


def backward_body(z, where, *refs):
    count = z.split * z.experts
    chunks = refs[:count]
    saved_ref, gate_ref, down_ref = refs[count : count + 3]
    outs = refs[count + 3 : count + 3 + z.split]
    held, last, tile = refs[count + 3 + z.split :]
    total = held.shape[0]
    selector = saved_selector(z, where[0], where[1], total, saved_ref.shape[2])
    gate_proj = jnp.dot(selector, saved_ref[0, 0], preferred_element_type=f32)
    sg = jax.nn.sigmoid(gate_proj)
    hidden = (gate_proj * sg).astype(bf16).astype(f32)
    slope = sg * (1.0 + gate_proj * (1.0 - sg))
    collect_rows(z, chunks, held, last, tile)
    grad_hidden = lax.dot_general(held[...], down_ref[0], nt, preferred_element_type=f32)
    dots = jnp.sum(grad_hidden * hidden, axis=-1, keepdims=True)
    grad_gate = (grad_hidden * slope).astype(bf16)
    step = 512
    for col in range(0, z.width, step):
        part = lax.dot_general(
            grad_gate, gate_ref[0, col : col + step, :], nt, preferred_element_type=f32
        )
        write_parts(z, part, outs, col)
    write_parts(z, jnp.broadcast_to(dots, (total, 128)), outs, z.width)


def experts_backward(z, where, chunks, saved, w_gate, w_down):
    total = z.split * z.tokens + z.extra

    def body(*refs):
        backward_body(z, *refs)

    return call_with_scalar(
        body,
        [shape((z.rows, z.width + 128))] * z.split,
        [
            pltpu.VMEM((total, z.width), bf16),
            pltpu.VMEM((z.extra, z.width), f32),
            pltpu.VMEM((16, fold), f32),
        ],
        z.split * z.experts + 3,
        4 * total * w_gate.shape[1] * w_gate.shape[2],
        4 * w_gate.shape[1] * w_gate.shape[2],
        "experts_backward",
    )(where, *chunks, saved, w_gate, w_down)


def put_last(z, values, k, source_chunk, tile, out):
    tile[...] = jnp.zeros_like(tile)
    pack_last(values, tile)
    tokens = source_chunk[:, z.width :].astype(f32)
    tile[z.pieces : z.pieces + 1, :] = tokens[z.pieces : z.pieces + 1, :]
    out[:, z.width :] = tile[...].astype(bf16)


def finish_forward_body(z, *refs):
    e = z.experts
    chunks, parts = refs[:e], refs[e : e + z.split]
    gates = refs[e + z.split]
    outs = refs[e + z.split + 1 : 2 * e + z.split + 1]
    last, tile = refs[2 * e + z.split + 1 :]

    def mixed(at):
        y = parts[0][at : at + 16, :].astype(f32)
        for part in parts[1:]:
            y = y + part[at : at + 16, :].astype(f32)
        return route_scale * (gates[at : at + 16, 0:1] * y)

    last[...] = jnp.zeros_like(last)
    for k in range(e):
        h = chunks[k][:, : z.width].astype(f32)
        outs[k][:, : z.width] = (h + mixed(k * z.main)).astype(bf16)
        unpack_last(chunks[k], z, tile, last, k)
    last[...] = last[...] + mixed(z.tokens)
    for k in range(e):
        put_last(z, last[k : k + 1, :], k, chunks[k], tile, outs[k])


def finish_forward(z, chunks, parts, gates):
    def body(*refs):
        finish_forward_body(z, *refs)

    return call(
        body,
        [shape((z.main, z.wide))] * z.experts,
        [pltpu.VMEM((16, z.width), f32), pltpu.VMEM((16, fold), f32)],
        8 * z.rows * z.width,
        8 * z.rows * z.width,
        "finish_forward",
    )(*chunks, *parts, gates)


def finish_backward_body(z, *refs):
    e = z.experts
    acts, grads, parts = refs[:e], refs[e : 2 * e], refs[2 * e : 2 * e + z.split]
    gain_ref, router_ref = refs[2 * e + z.split : 2 * e + z.split + 2]
    outs = refs[2 * e + z.split + 2 : 3 * e + z.split + 2]
    last_act, last_grad, tile = refs[3 * e + z.split + 2 :]
    gain = gain_ref[...].astype(f32)
    router = router_ref[...].astype(f32)

    def finished(h, g, at):
        normed, inv = norm_rows(h, gain)
        logits = jnp.sum(normed.astype(f32) * router, axis=-1, keepdims=True)
        affinity = jax.nn.sigmoid(logits)
        rows = parts[0][at : at + 16, : z.width].astype(f32)
        dot = parts[0][at : at + 16, z.width :].astype(f32)
        for part in parts[1:]:
            rows = rows + part[at : at + 16, : z.width].astype(f32)
            dot = dot + part[at : at + 16, z.width :].astype(f32)
        dot = dot[:, 0:1]
        grad_logits = (route_scale * dot * affinity * (1.0 - affinity)).astype(bf16).astype(f32)
        grad_pre = (route_scale * affinity * rows + grad_logits * router) * gain
        centre = jnp.mean(grad_pre * h, axis=-1, keepdims=True)
        return g + inv * (grad_pre - h * (inv * inv * centre))

    last_act[...] = jnp.zeros_like(last_act)
    last_grad[...] = jnp.zeros_like(last_grad)
    for k in range(e):
        h = acts[k][:, : z.width].astype(f32)
        g = grads[k][:, : z.width].astype(f32)
        outs[k][:, : z.width] = finished(h, g, k * z.main).astype(bf16)
        unpack_last(acts[k], z, tile, last_act, k)
        unpack_last(grads[k], z, tile, last_grad, k)
    last_act[...] = finished(last_act[...], last_grad[...], z.tokens)
    for k in range(e):
        put_last(z, last_act[k : k + 1, :], k, grads[k], tile, outs[k])


def finish_backward(z, acts, grads, parts, gain, router_row):
    def body(*refs):
        finish_backward_body(z, *refs)

    return call(
        body,
        [shape((z.main, z.wide))] * z.experts,
        [
            pltpu.VMEM((16, z.width), f32),
            pltpu.VMEM((16, z.width), f32),
            pltpu.VMEM((16, fold), f32),
        ],
        30 * z.rows * z.width,
        10 * z.rows * z.width,
        "finish_backward",
    )(*acts, *grads, *parts, gain, router_row)


def order_body(z, *refs):
    chunks, out, held, last, tile = refs[: z.experts], *refs[z.experts :]
    last[...] = jnp.zeros_like(last)
    for k in range(z.experts):
        held[k * z.main : (k + 1) * z.main, :] = chunks[k][:, : z.width]
        unpack_last(chunks[k], z, tile, last, k)
    held[z.tokens :, :] = last[...].astype(bf16)
    token_row = chunks[0][:, z.width :].astype(f32)[z.pieces : z.pieces + 1, : z.rows]
    token = lax.broadcasted_iota(jnp.int32, (z.tokens, z.rows), 0).astype(f32)
    selector = jnp.where(token == token_row, 1.0, 0.0).astype(bf16)
    out[...] = jnp.dot(selector, held[...], preferred_element_type=f32).astype(bf16)


def order_rows(z, chunks, name):
    def body(*refs):
        order_body(z, *refs)

    return call(
        body,
        shape((z.tokens, z.width)),
        [
            pltpu.VMEM((z.rows, z.width), bf16),
            pltpu.VMEM((16, z.width), f32),
            pltpu.VMEM((16, fold), f32),
        ],
        2 * z.rows * z.tokens * z.width,
        4 * z.tokens * z.width,
        name,
    )(*chunks)


def dispatch(z, chunks):
    groups = z.experts * z.split
    got = [chunks[0]] + [None] * (z.experts - 1)
    for k in reversed(range(1, z.experts)):
        pairs = [(i, ((i // z.split) ^ k) * z.split + i % z.split) for i in range(groups)]
        got[k] = lax.ppermute(chunks[k], "ep", pairs)
    return got


def to_core(z, array, m):
    groups = z.experts * z.split
    pairs = [(i, i // z.split * z.split + ((i % z.split) ^ m)) for i in range(groups)]
    return lax.ppermute(array, "ep", pairs)


def to_section(z, chunks, by):
    groups = z.experts * z.split
    sections = lax.axis_size("pp")
    got = [None] * z.experts
    for k in reversed(range(z.experts)):
        pairs = [
            (s * groups + i, (s + by) % sections * groups + ((i // z.split) ^ k) * z.split + i % z.split)
            for s in range(sections)
            for i in range(groups)
        ]
        got[k] = lax.ppermute(chunks[k], ("pp", "ep"), pairs)
    return got


def on_device(
    fwd_act, fwd_ids, bwd_act, bwd_ids, bwd_grad, norm_gain, router, w_gate, w_down, saved_gate
):
    groups = lax.axis_size("ep")
    assert fwd_ids.shape[1] == 1
    z = Sizes(groups, router.shape[2], fwd_act.shape[0], fwd_act.shape[1])
    index = lax.axis_index("ep")
    block, core = index // z.split, index % z.split
    where = jnp.stack([block, core]).astype(jnp.int32)
    mine = jnp.arange(z.experts, dtype=jnp.int32) == block
    router_row = jnp.sum(jnp.where(mine, router[0].astype(f32), 0.0), axis=1)[None, :]

    (fwd_chunks,) = make_chunks(z, where, fwd_ids, [fwd_act], "forward_chunks")
    fwd_own = dispatch(z, fwd_chunks)
    grad_chunks, act_chunks = make_chunks(z, where, bwd_ids, [bwd_grad, bwd_act], "backward_chunks")
    grad_own = dispatch(z, grad_chunks)
    act_own = dispatch(z, act_chunks)

    fwd_all = list(fwd_own)
    for m in range(1, z.split):
        fwd_all += [to_core(z, chunk, m) for chunk in fwd_own]
    fwd_parts, fwd_gates = experts_forward(z, fwd_all, norm_gain, router_row, w_gate, w_down)
    fwd_parts = [fwd_parts[0]] + [to_core(z, fwd_parts[m], m) for m in range(1, z.split)]
    fwd_done = to_section(z, finish_forward(z, fwd_own, fwd_parts, fwd_gates), 1)

    grad_all = list(grad_own)
    for m in range(1, z.split):
        grad_all += [to_core(z, chunk, m) for chunk in grad_own]
    bwd_parts = experts_backward(z, where, grad_all, saved_gate, w_gate, w_down)
    bwd_parts = [bwd_parts[0]] + [to_core(z, bwd_parts[m], m) for m in range(1, z.split)]
    bwd_done = to_section(
        z, finish_backward(z, act_own, grad_own, bwd_parts, norm_gain, router_row), -1
    )
    return (order_rows(z, fwd_done, "forward_rows"), order_rows(z, bwd_done, "backward_rows"))


def solution(mesh):
    return jax.shard_map(
        on_device,
        mesh=mesh,
        in_specs=(
            P(("pp", "ep"), None),
            P(("pp", "ep"), None),
            P(("pp", "ep"), None),
            P(("pp", "ep"), None),
            P(("pp", "ep"), None),
            P("pp", None),
            P("pp", None, None),
            P(("pp", "ep"), None, None),
            P(("pp", "ep"), None, None),
            P("pp", "ep", None, None),
        ),
        out_specs=(P(("pp", "ep"), None), P(("pp", "ep"), None)),
        check_vma=False,
    )
```

time: 128 us -> 69.7 us (0.54)
  waiting for transfers between devices: 58.4 us -> 15 us
  matrix products: 19.3 us -> 0 us
  Pallas kernels: 0 us -> 14.6 us
  other arithmetic: 9.21 us -> 0.94 us
  local copies, waits for them, and re-layouts: 13.9 us -> 7.31 us
  starting transfers between devices: 26 us -> 30.6 us
    all_to_all x5 -> x0, waiting for transfers between devices: 47 us -> none  [the longest x1 14.7 us: on_device(): lax.all_to_all(fwd_send, 'ep', split_axis=0, concat_axis=0, tiled=True)]
    ppermute x2 -> x27, starting transfers between devices: 5.27 us -> 30.6 us  [the longest x8 16.9 us: to_section(): got[k] = lax.ppermute(chunks[k], ('pp', 'ep'), pairs)]
    all_to_all x5 -> x0, starting transfers between devices: 20.7 us -> none  [the longest x1 5.3 us: on_device(): lax.all_to_all(grad_send, 'ep', split_axis=0, concat_axis=0, tiled=True)]
    dot_general x6 -> x0, matrix products: 19.3 us -> none  [the longest x1 6.84 us: slice_backward(): jnp.einsum('sch,dh->scd', grad_gate, gate_part, preferred_element_type=jn...]
    pallas_call x0 -> x8, Pallas kernels: none -> 14.6 us  [the longest x1 4.69 us: experts_backward(): call_with_scalar(body, [shape((z.rows, z.width + 128))] * z.split, [pltpu...]
    unnamed x28 -> x16, local copies, waits for them, and re-layouts: 3.15 us -> 7.3 us
    convert_element_type x6 -> x0, other arithmetic: 4.07 us -> none  [the longest x1 2.12 us: finish_backward(): return (grad.astype(jnp.float32) + grad_act).astype(jnp.bfloat16)]
    ppermute x2 -> x27, waiting for transfers between devices: 11.4 us -> 15 us  [the longest x9 9.84 us: dispatch(): got[k] = lax.ppermute(chunks[k], 'ep', pairs)]
  transfers between devices with their start and end apart: 7 -> 27, of which waited for: 6 -> 7; matrix products, arithmetic and copies ran while one was open for 26% -> 2% of each run, Pallas kernels for 0% -> 18%
where the time goes in v1:
time: 69.7 us; the launch traced here: 69.2 us
  starting transfers between devices  30.6 us (44%)
  waiting for transfers between devices  15 us (22%)
  Pallas kernels  14.6 us (21%)
  local copies, waits for them, and re-layouts  7.31 us (10%)
  other arithmetic  0.94 us (1%)
  between operations  0.78 us (1%)
    ppermute x8, starting transfers between devices, to_section(): got[k] = lax.ppermute(chunks[k], ('pp', 'ep'), pairs)  16.9 us
    ppermute x9, starting transfers between devices, dispatch(): got[k] = lax.ppermute(chunks[k], 'ep', pairs)  11.6 us
    ppermute x9, waiting for transfers between devices, dispatch(): got[k] = lax.ppermute(chunks[k], 'ep', pairs)  9.84 us
    unnamed x16, local copies, waits for them, and re-layouts  7.3 us
    ppermute x8, waiting for transfers between devices, to_section(): got[k] = lax.ppermute(chunks[k], ('pp', 'ep'), pairs)  5.01 us
    pallas_call x1, Pallas kernels, experts_backward(): call_with_scalar(body, [shape((z.rows, z.width + 128))] * z.split, [pltpu...  4.69 us
    pallas_call x1, Pallas kernels, experts_forward(): call(body, [shape((z.rows, z.width))] * z.split + [shape((z.rows, 128), f...  3.99 us
    pallas_call x2, Pallas kernels, order_rows(): call(body, shape((z.tokens, z.width)), [pltpu.VMEM((z.rows, z.width), bf1...  2.17 us
  transfers between devices with their start and end apart: 27, of which 7 were waited for; matrix products, arithmetic and copies ran while one was open for 2% of the time, Pallas kernels for 18%

profile of v1, /device:TPU:0, one launch (start us, length us, event | category | flops | bytes accessed | tf_op | source)
XLA Modules:
  0.0 69.2 jit_solution(11110542043791984213)
XLA Ops:
  0.6 0.7 %copy.13.refs_1_ = s32[64,1]{1,0:T(8,128)S(1)} copy(s32[64,1]{0,1:T(1,128)} %param.13) | data formatting | bytes 512 | tf_op args[3]
  1.5 1.0 %copy-done.2 = bf16[64,3584]{1,0:T(8,128)(2,1)S(1)} copy-done((bf16[64,3584]{1,0:T(8,128)(2,1)S(1)}, bf16[64,3584]{1,0:T(8,128)(2,1)}, u32[]{:S(2)}) %copy-start.2) | copy-done | bytes 458776
  2.5 1.0 %copy-done.3 = bf16[64,3584]{1,0:T(8,128)(2,1)S(1)} copy-done((bf16[64,3584]{1,0:T(8,128)(2,1)S(1)}, bf16[64,3584]{1,0:T(8,128)(2,1)}, u32[]{:S(2)}) %copy-start.3) | copy-done | bytes 458776
  3.5 1.2 %backward_chunks.1 = (bf16[16,3840]{1,0:T(8,128)(2,1)S(1)}, bf16[16,3840]{1,0:T(8,128)(2,1)S(1)}, bf16[16,3840]{1,0:T(8,128)(2,1)S(1)}, bf16[16,3840]{1,0:T(8,12...) custom-call(s32[2]{0:T(128)S(1)} %pad_add_fusion.refs_0_, ...), custom_call_target="tpu_custom_call" | custom-call | flops 73400320 | bytes 1835008 | tf_op jit(solution)/shard_map/backward_chunks/pallas_call | solution.py:113
  4.7 3.0 %collective-permute-start.15 = (bf16[16,3840]{1,0:T(8,128)(2,1)S(1)}, bf16[16,3840]{1,0:T(8,128)(2,1)S(1)}, u32[]{:S(2)}, u32[]{:S(2)}) collective-permute-start(bf16[16,3840]{1,0:T(8,128)(2,1)S(1)} %get-tuple-element.43), channel_id=1, source_target_pairs={{0,2},{1,3},{2,0},{3,1},{4,6},{5,7},{6,4},{7,5},{8,10},{9,11},{10,... | collective-permute-start | bytes 368648 | tf_op jit(solution)/shard_map/ppermute | solution.py:411
  7.7 1.5 %collective-permute-start.16 = (bf16[16,3840]{1,0:T(8,128)(2,1)S(1)}, bf16[16,3840]{1,0:T(8,128)(2,1)S(1)}, u32[]{:S(2)}, u32[]{:S(2)}) collective-permute-start(bf16[16,3840]{1,0:T(8,128)(2,1)S(1)} %get-tuple-element.44), channel_id=1, source_target_pairs={{0,4},{1,5},{2,6},{3,7},{4,0},{5,1},{6,2},{7,3},{8,12},{9,13},{10,... | collective-permute-start | bytes 368648 | tf_op jit(solution)/shard_map/ppermute | solution.py:411
  9.2 0.7 %copy.12.refs_1_ = s32[64,1]{1,0:T(8,128)S(1)} copy(s32[64,1]{0,1:T(1,128)} %param.11) | data formatting | bytes 512 | tf_op args[1]
  10.0 1.0 %copy-done.4 = bf16[64,3584]{1,0:T(8,128)(2,1)S(1)} copy-done((bf16[64,3584]{1,0:T(8,128)(2,1)S(1)}, bf16[64,3584]{1,0:T(8,128)(2,1)}, u32[]{:S(2)}) %copy-start.4) | copy-done | bytes 458776
  11.0 1.0 %forward_chunks.1 = (bf16[16,3840]{1,0:T(8,128)(2,1)S(1)}, bf16[16,3840]{1,0:T(8,128)(2,1)S(1)}, bf16[16,3840]{1,0:T(8,128)(2,1)S(1)}, bf16[16,3840]{1,0:T(8,128)(2,1)S(1)}) custom-call(s32[2]{0:T(128)S(1)} %pad_add_fusion.refs_0_, s32[64,1]{1,0:T(8,128)S(1)} %copy.12.refs_1_, bf16[64,3584]{1,0:T(8,128)(2,1)S(1)} %copy-done.4), custom_call_target="tpu_custom_call" | custom-call | flops 36700160 | bytes 917504 | tf_op jit(solution)/shard_map/forward_chunks/pallas_call | solution.py:113
  12.6 2.9 %collective-permute-start.2 = (bf16[16,3840]{1,0:T(8,128)(2,1)S(1)}, bf16[16,3840]{1,0:T(8,128)(2,1)S(1)}, u32[]{:S(2)}, u32[]{:S(2)}) collective-permute-start(bf16[16,3840]{1,0:T(8,128)(2,1)S(1)} %get-tuple-element.30), channel_id=1, source_target_pairs={{0,6},{1,7},{2,4},{3,5},{4,2},{5,3},{6,0},{7,1},{8,14},{9,15},{10,... | collective-permute-start | bytes 368648 | tf_op jit(solution)/shard_map/ppermute | solution.py:411
  15.6 2.6 %collective-permute-done.refs_1_ = bf16[16,3840]{1,0:T(8,128)(2,1)S(1)} collective-permute-done((bf16[16,3840]{1,0:T(8,128)(2,1)S(1)}, bf16[16,3840]{1,0:T(8,128)(2,1)S(1)}, u32[]{:S(2)}, u32[]{:S(2)}) %collective-permute-start) | collective-permute-done | bytes 122912 | tf_op jit(solution)/shard_map/ppermute | solution.py:411
  18.2 3.8 %collective-permute-done.1.refs_2_ = bf16[16,3840]{1,0:T(8,128)(2,1)S(1)} collective-permute-done((bf16[16,3840]{1,0:T(8,128)(2,1)S(1)}, bf16[16,3840]{1,0:T(8,128)(2,1)S(1)}, u32[]{:S(2)}, u32[]{:S(2)}) %collective-permute-start.1) | collective-permute-done | bytes 122912 | tf_op jit(solution)/shard_map/ppermute | solution.py:411
  23.7 0.9 %fusion = f32[3584]{0:T(1024)S(1)} fusion(bf16[1,3584,4]{1,2,0:T(4,128)(2,1)} %param.16, pred[4]{0:T(512)(128)(4,1)S(1)} %iota_compare_fusion), kind=kLoop, calls=%fused_computation.1 | loop fusion | flops 39424 | bytes 43012 | tf_op jit(solution)/shard_map/reduce_sum | solution.py:445
  24.6 2.0 %copy-done = bf16[1,3584,512]{2,1,0:T(8,128)(2,1)S(1)} copy-done((bf16[1,3584,512]{2,1,0:T(8,128)(2,1)S(1)}, bf16[1,3584,512]{2,1,0:T(8,128)(2,1)}, u32[]{:S(2)}) %copy-start) | copy-done | bytes 3670040
  27.3 4.0 %experts_forward.1 = (bf16[80,3584]{1,0:T(8,128)(2,1)S(1)}, bf16[80,3584]{1,0:T(8,128)(2,1)S(1)}, f32[80,128]{1,0:T(8,128)S(1)}) custom-call(bf16[16,3840]{1,0:T(8,128)(2,1)S(1)} %get-tuple-element.27.refs_0_, bf16[16,3840]{1,0:T(8,128)(2,1)S(1)} %collective-permute-done.refs_1_, bf16[16,3840]{1,0:T(8,128)(2,1)S(1)} %collective-permute-done.1.refs_2_, ...), custom_call_target="tpu_custom_call" | custom-call | flops 1056964608 | bytes 7340032 | tf_op jit(solution)/shard_map/experts_forward/pallas_call | solution.py:198
  31.6 4.7 %experts_backward.1 = (bf16[80,3712]{1,0:T(8,128)(2,1)S(1)}, bf16[80,3712]{1,0:T(8,128)(2,1)S(1)}) custom-call(s32[2]{0:T(128)S(1)} %pad_add_fusion.refs_0_, bf16[16,3840]{1,0:T(8,128)(2,1)S(1)} %get-tuple-element.42.refs_1_.refs_4_, bf16[16,3840]{1,0:T(8,128)(2,1)S(1)} %collective-permute-done.15.refs_2_.refs_5_, ...), custom_call_target="tpu_custom_call" | custom-call | flops 1056964608 | bytes 7340032 | tf_op jit(solution)/shard_map/experts_backward/pallas_call | solution.py:260
  36.7 1.5 %collective-permute-start.12 = (bf16[16,3840]{1,0:T(8,128)(2,1)S(1)}, bf16[16,3840]{1,0:T(8,128)(2,1)S(1)}, u32[]{:S(2)}, u32[]{:S(2)}) collective-permute-start(bf16[16,3840]{1,0:T(8,128)(2,1)S(1)} %get-tuple-element.39), channel_id=1, source_target_pairs={{0,2},{1,3},{2,0},{3,1},{4,6},{5,7},{6,4},{7,5},{8,10},{9,11},{10,... | collective-permute-start | bytes 368648 | tf_op jit(solution)/shard_map/ppermute | solution.py:411
  38.2 1.2 %collective-permute-start.13 = (bf16[16,3840]{1,0:T(8,128)(2,1)S(1)}, bf16[16,3840]{1,0:T(8,128)(2,1)S(1)}, u32[]{:S(2)}, u32[]{:S(2)}) collective-permute-start(bf16[16,3840]{1,0:T(8,128)(2,1)S(1)} %get-tuple-element.40), channel_id=1, source_target_pairs={{0,4},{1,5},{2,6},{3,7},{4,0},{5,1},{6,2},{7,3},{8,12},{9,13},{10,... | collective-permute-start | bytes 368648 | tf_op jit(solution)/shard_map/ppermute | solution.py:411
  39.3 0.8 %collective-permute-start.14 = (bf16[16,3840]{1,0:T(8,128)(2,1)S(1)}, bf16[16,3840]{1,0:T(8,128)(2,1)S(1)}, u32[]{:S(2)}, u32[]{:S(2)}) collective-permute-start(bf16[16,3840]{1,0:T(8,128)(2,1)S(1)} %get-tuple-element.41), channel_id=1, source_target_pairs={{0,6},{1,7},{2,4},{3,5},{4,2},{5,3},{6,0},{7,1},{8,14},{9,15},{10,... | collective-permute-start | bytes 368648 | tf_op jit(solution)/shard_map/ppermute | solution.py:411
  40.6 1.8 %collective-permute-start.10 = (bf16[16,3840]{1,0:T(8,128)(2,1)S(1)}, bf16[16,3840]{1,0:T(8,128)(2,1)S(1)}, u32[]{:S(2)}, u32[]{:S(2)}) collective-permute-start(bf16[16,3840]{1,0:T(8,128)(2,1)S(1)} %get-tuple-element.36), channel_id=1, source_target_pairs={{0,12},{1,13},{2,14},{3,15},{4,8},{5,9},{6,10},{7,11},{8,20},{9,21... | collective-permute-start | bytes 368648 | tf_op jit(solution)/shard_map/ppermute | solution.py:431
  42.4 3.5 %collective-permute-start.11 = (bf16[16,3840]{1,0:T(8,128)(2,1)S(1)}, bf16[16,3840]{1,0:T(8,128)(2,1)S(1)}, u32[]{:S(2)}, u32[]{:S(2)}) collective-permute-start(bf16[16,3840]{1,0:T(8,128)(2,1)S(1)} %get-tuple-element.37), channel_id=1, source_target_pairs={{0,14},{1,15},{2,12},{3,13},{4,10},{5,11},{6,8},{7,9},{8,22},{9,23... | collective-permute-start | bytes 368648 | tf_op jit(solution)/shard_map/ppermute | solution.py:431
  45.9 3.4 %collective-permute-done.13.refs_2_ = bf16[16,3840]{1,0:T(8,128)(2,1)S(1)} collective-permute-done((bf16[16,3840]{1,0:T(8,128)(2,1)S(1)}, bf16[16,3840]{1,0:T(8,128)(2,1)S(1)}, u32[]{:S(2)}, u32[]{:S(2)}) %collective-permute-start.13) | collective-permute-done | bytes 122912 | tf_op jit(solution)/shard_map/ppermute | solution.py:411
  49.3 3.6 %collective-permute-start.8 = (bf16[16,3840]{1,0:T(8,128)(2,1)S(1)}, bf16[16,3840]{1,0:T(8,128)(2,1)S(1)}, u32[]{:S(2)}, u32[]{:S(2)}) collective-permute-start(bf16[16,3840]{1,0:T(8,128)(2,1)S(1)} %get-tuple-element.34), channel_id=1, source_target_pairs={{0,8},{1,9},{2,10},{3,11},{4,12},{5,13},{6,14},{7,15},{8,16},{9,17... | collective-permute-start | bytes 368648 | tf_op jit(solution)/shard_map/ppermute | solution.py:431
  52.9 1.2 %finish_backward.1 = (bf16[16,3840]{1,0:T(8,128)(2,1)S(1)}, bf16[16,3840]{1,0:T(8,128)(2,1)S(1)}, bf16[16,3840]{1,0:T(8,128)(2,1)S(1)}, bf16[16,3840]{1,0:T(8,128)(2,1)S(1)}) custom-call(bf16[16,3840]{1,0:T(8,128)(2,1)S(1)} %get-tuple-element.38.refs_0_, bf16[16,3840]{1,0:T(8,128)(2,1)S(1)} %collective-permute-done.12.refs_1_, ...), custom_call_target="tpu_custom_call" | custom-call | flops 8601600 | bytes 2867200 | tf_op jit(solution)/shard_map/finish_backward/pallas_call | solution.py:361
  54.0 2.1 %collective-permute-start.23 = (bf16[16,3840]{1,0:T(8,128)(2,1)S(1)}, bf16[16,3840]{1,0:T(8,128)(2,1)S(1)}, u32[]{:S(2)}, u32[]{:S(2)}) collective-permute-start(bf16[16,3840]{1,0:T(8,128)(2,1)S(1)} %get-tuple-element.48), channel_id=1, source_target_pairs={{0,24},{1,25},{2,26},{3,27},{4,28},{5,29},{6,30},{7,31},{8,0},{9,1... | collective-permute-start | bytes 368648 | tf_op jit(solution)/shard_map/ppermute | solution.py:431
  56.1 2.9 %collective-permute-start.24 = (bf16[16,3840]{1,0:T(8,128)(2,1)S(1)}, bf16[16,3840]{1,0:T(8,128)(2,1)S(1)}, u32[]{:S(2)}, u32[]{:S(2)}) collective-permute-start(bf16[16,3840]{1,0:T(8,128)(2,1)S(1)} %get-tuple-element.49), channel_id=1, source_target_pairs={{0,26},{1,27},{2,24},{3,25},{4,30},{5,31},{6,28},{7,29},{8,2},{9,3... | collective-permute-start | bytes 368648 | tf_op jit(solution)/shard_map/ppermute | solution.py:431
  59.1 2.4 %collective-permute-start.25 = (bf16[16,3840]{1,0:T(8,128)(2,1)S(1)}, bf16[16,3840]{1,0:T(8,128)(2,1)S(1)}, u32[]{:S(2)}, u32[]{:S(2)}) collective-permute-start(bf16[16,3840]{1,0:T(8,128)(2,1)S(1)} %get-tuple-element.50), channel_id=1, source_target_pairs={{0,28},{1,29},{2,30},{3,31},{4,24},{5,25},{6,26},{7,27},{8,4},{9,5... | collective-permute-start | bytes 368648 | tf_op jit(solution)/shard_map/ppermute | solution.py:431
  62.0 1.1 %forward_rows.1 = bf16[64,3584]{1,0:T(8,128)(2,1)} custom-call(bf16[16,3840]{1,0:T(8,128)(2,1)S(1)} %collective-permute-done.8.refs_0_, bf16[16,3840]{1,0:T(8,128)(2,1)S(1)} %collective-permute-done.9.refs_1_, bf16[16,3840]{1,0:T(8,128)(2,1)S(1)} %collective-permute-done.10.refs_2_, bf16[16,3840]{1,0:T(8,128)(2,1)S(1)} %collective-permute-done.11.refs_3_), custom_call_target="tpu_custom_call" | custom-call | flops 36700160 | bytes 917504 | tf_op jit(solution)/shard_map/forward_rows/pallas_call | solution.py:392
  63.1 1.5 %collective-permute-done.24.refs_1_ = bf16[16,3840]{1,0:T(8,128)(2,1)S(1)} collective-permute-done((bf16[16,3840]{1,0:T(8,128)(2,1)S(1)}, bf16[16,3840]{1,0:T(8,128)(2,1)S(1)}, u32[]{:S(2)}, u32[]{:S(2)}) %collective-permute-start.24) | collective-permute-done | bytes 122912 | tf_op jit(solution)/shard_map/ppermute | solution.py:431
  64.7 0.8 %collective-permute-done.25.refs_2_ = bf16[16,3840]{1,0:T(8,128)(2,1)S(1)} collective-permute-done((bf16[16,3840]{1,0:T(8,128)(2,1)S(1)}, bf16[16,3840]{1,0:T(8,128)(2,1)S(1)}, u32[]{:S(2)}, u32[]{:S(2)}) %collective-permute-start.25) | collective-permute-done | bytes 122912 | tf_op jit(solution)/shard_map/ppermute | solution.py:431
  65.4 2.7 %collective-permute-done.26.refs_3_ = bf16[16,3840]{1,0:T(8,128)(2,1)S(1)} collective-permute-done((bf16[16,3840]{1,0:T(8,128)(2,1)S(1)}, bf16[16,3840]{1,0:T(8,128)(2,1)S(1)}, u32[]{:S(2)}, u32[]{:S(2)}) %collective-permute-start.26) | collective-permute-done | bytes 122912 | tf_op jit(solution)/shard_map/ppermute | solution.py:431
  68.1 1.1 %backward_rows.1 = bf16[64,3584]{1,0:T(8,128)(2,1)} custom-call(bf16[16,3840]{1,0:T(8,128)(2,1)S(1)} %collective-permute-done.23.refs_0_, bf16[16,3840]{1,0:T(8,128)(2,1)S(1)} %collective-permute-done.24.refs_1_, bf16[16,3840]{1,0:T(8,128)(2,1)S(1)} %collective-permute-done.25.refs_2_, bf16[16,3840]{1,0:T(8,128)(2,1)S(1)} %collective-permute-done.26.refs_3_), custom_call_target="tpu_custom_call" | custom-call | flops 36700160 | bytes 917504 | tf_op jit(solution)/shard_map/backward_rows/pallas_call | solution.py:392
  (50 shorter events, 4.9 us)
Async XLA Ops:
  1.5 1.0 %copy-start.2 = (bf16[64,3584]{1,0:T(8,128)(2,1)S(1)}, bf16[64,3584]{1,0:T(8,128)(2,1)}, u32[]{:S(2)}) copy-start(bf16[64,3584]{1,0:T(8,128)(2,1)} %refs_2_.3) | copy-start | bytes 1376260
  4.7 10.8 %collective-permute-start.15 = (bf16[16,3840]{1,0:T(8,128)(2,1)S(1)}, bf16[16,3840]{1,0:T(8,128)(2,1)S(1)}, u32[]{:S(2)}, u32[]{:S(2)}) collective-permute-start(bf16[16,3840]{1,0:T(8,128)(2,1)S(1)} %get-tuple-element.43), channel_id=1, source_target_pairs={{0,2},{1,3},{2,0},{3,1},{4,6},{5,7},{6,4},{7,5},{8,10},{9,11},{10,... | collective-permute-start | bytes 368648 | tf_op jit(solution)/shard_map/ppermute | solution.py:411
  7.7 7.8 %collective-permute-start.16 = (bf16[16,3840]{1,0:T(8,128)(2,1)S(1)}, bf16[16,3840]{1,0:T(8,128)(2,1)S(1)}, u32[]{:S(2)}, u32[]{:S(2)}) collective-permute-start(bf16[16,3840]{1,0:T(8,128)(2,1)S(1)} %get-tuple-element.44), channel_id=1, source_target_pairs={{0,4},{1,5},{2,6},{3,7},{4,0},{5,1},{6,2},{7,3},{8,12},{9,13},{10,... | collective-permute-start | bytes 368648 | tf_op jit(solution)/shard_map/ppermute | solution.py:411
  10.0 1.0 %copy-start.4 = (bf16[64,3584]{1,0:T(8,128)(2,1)S(1)}, bf16[64,3584]{1,0:T(8,128)(2,1)}, u32[]{:S(2)}) copy-start(bf16[64,3584]{1,0:T(8,128)(2,1)} %refs_2_.2) | copy-start | bytes 1376260
  11.9 6.3 %collective-permute-start = (bf16[16,3840]{1,0:T(8,128)(2,1)S(1)}, bf16[16,3840]{1,0:T(8,128)(2,1)S(1)}, u32[]{:S(2)}, u32[]{:S(2)}) collective-permute-start(bf16[16,3840]{1,0:T(8,128)(2,1)S(1)} %get-tuple-element.28), channel_id=1, source_target_pairs={{0,2},{1,3},{2,0},{3,1},{4,6},{5,7},{6,4},{7,5},{8,10},{9,11},{10,... | collective-permute-start | bytes 368648 | tf_op jit(solution)/shard_map/ppermute | solution.py:411
  12.6 9.5 %collective-permute-start.1 = (bf16[16,3840]{1,0:T(8,128)(2,1)S(1)}, bf16[16,3840]{1,0:T(8,128)(2,1)S(1)}, u32[]{:S(2)}, u32[]{:S(2)}) collective-permute-start(bf16[16,3840]{1,0:T(8,128)(2,1)S(1)} %get-tuple-element.29), channel_id=1, source_target_pairs={{0,4},{1,5},{2,6},{3,7},{4,0},{5,1},{6,2},{7,3},{8,12},{9,13},{10,... | collective-permute-start | bytes 368648 | tf_op jit(solution)/shard_map/ppermute | solution.py:411
  12.6 9.4 %collective-permute-start.2 = (bf16[16,3840]{1,0:T(8,128)(2,1)S(1)}, bf16[16,3840]{1,0:T(8,128)(2,1)S(1)}, u32[]{:S(2)}, u32[]{:S(2)}) collective-permute-start(bf16[16,3840]{1,0:T(8,128)(2,1)S(1)} %get-tuple-element.30), channel_id=1, source_target_pairs={{0,6},{1,7},{2,4},{3,5},{4,2},{5,3},{6,0},{7,1},{8,14},{9,15},{10,... | collective-permute-start | bytes 368648 | tf_op jit(solution)/shard_map/ppermute | solution.py:411
  15.5 7.1 %collective-permute-start.17 = (bf16[16,3840]{1,0:T(8,128)(2,1)S(1)}, bf16[16,3840]{1,0:T(8,128)(2,1)S(1)}, u32[]{:S(2)}, u32[]{:S(2)}) collective-permute-start(bf16[16,3840]{1,0:T(8,128)(2,1)S(1)} %get-tuple-element.45), channel_id=1, source_target_pairs={{0,6},{1,7},{2,4},{3,5},{4,2},{5,3},{6,0},{7,1},{8,14},{9,15},{10,... | collective-permute-start | bytes 368648 | tf_op jit(solution)/shard_map/ppermute | solution.py:411
  15.5 7.1 %collective-permute-start.3 = (bf16[16,3840]{1,0:T(8,128)(2,1)S(1)}, bf16[16,3840]{1,0:T(8,128)(2,1)S(1)}, u32[]{:S(2)}, u32[]{:S(2)}) collective-permute-start(bf16[16,3840]{1,0:T(8,128)(2,1)S(1)} %get-tuple-element.27.refs_0_), channel_id=1, source_target_pairs={{0,1},{1,0},{2,3},{3,2},{4,5},{5,4},{6,7},{7,6},{8,9},{9,8},{10,11... | collective-permute-start | bytes 368648 | tf_op jit(solution)/shard_map/ppermute | solution.py:418
  18.2 4.9 %collective-permute-start.4 = (bf16[16,3840]{1,0:T(8,128)(2,1)S(1)}, bf16[16,3840]{1,0:T(8,128)(2,1)S(1)}, u32[]{:S(2)}, u32[]{:S(2)}) collective-permute-start(bf16[16,3840]{1,0:T(8,128)(2,1)S(1)} %collective-permute-done.refs_1_), channel_id=1, source_target_pairs={{0,1},{1,0},{2,3},{3,2},{4,5},{5,4},{6,7},{7,6},{8,9},{9,8},{10,11... | collective-permute-start | bytes 368648 | tf_op jit(solution)/shard_map/ppermute | solution.py:418
  22.0 1.3 %collective-permute-start.5 = (bf16[16,3840]{1,0:T(8,128)(2,1)S(1)}, bf16[16,3840]{1,0:T(8,128)(2,1)S(1)}, u32[]{:S(2)}, u32[]{:S(2)}) collective-permute-start(bf16[16,3840]{1,0:T(8,128)(2,1)S(1)} %collective-permute-done.1.refs_2_), channel_id=1, source_target_pairs={{0,1},{1,0},{2,3},{3,2},{4,5},{5,4},{6,7},{7,6},{8,9},{9,8},{10,11... | collective-permute-start | bytes 368648 | tf_op jit(solution)/shard_map/ppermute | solution.py:418
  22.0 2.5 %collective-permute-start.6 = (bf16[16,3840]{1,0:T(8,128)(2,1)S(1)}, bf16[16,3840]{1,0:T(8,128)(2,1)S(1)}, u32[]{:S(2)}, u32[]{:S(2)}) collective-permute-start(bf16[16,3840]{1,0:T(8,128)(2,1)S(1)} %collective-permute-done.2.refs_3_), channel_id=1, source_target_pairs={{0,1},{1,0},{2,3},{3,2},{4,5},{5,4},{6,7},{7,6},{8,9},{9,8},{10,11... | collective-permute-start | bytes 368648 | tf_op jit(solution)/shard_map/ppermute | solution.py:418
  22.6 9.0 %collective-permute-start.18 = (bf16[16,3840]{1,0:T(8,128)(2,1)S(1)}, bf16[16,3840]{1,0:T(8,128)(2,1)S(1)}, u32[]{:S(2)}, u32[]{:S(2)}) collective-permute-start(bf16[16,3840]{1,0:T(8,128)(2,1)S(1)} %get-tuple-element.42.refs_1_.refs_4_), channel_id=1, source_target_pairs={{0,1},{1,0},{2,3},{3,2},{4,5},{5,4},{6,7},{7,6},{8,9},{9,8},{10,11... | collective-permute-start | bytes 368648 | tf_op jit(solution)/shard_map/ppermute | solution.py:418
  22.6 9.0 %collective-permute-start.19 = (bf16[16,3840]{1,0:T(8,128)(2,1)S(1)}, bf16[16,3840]{1,0:T(8,128)(2,1)S(1)}, u32[]{:S(2)}, u32[]{:S(2)}) collective-permute-start(bf16[16,3840]{1,0:T(8,128)(2,1)S(1)} %collective-permute-done.15.refs_2_.refs_5_), channel_id=1, source_target_pairs={{0,1},{1,0},{2,3},{3,2},{4,5},{5,4},{6,7},{7,6},{8,9},{9,8},{10,11... | collective-permute-start | bytes 368648 | tf_op jit(solution)/shard_map/ppermute | solution.py:418
  23.1 8.5 %collective-permute-start.20 = (bf16[16,3840]{1,0:T(8,128)(2,1)S(1)}, bf16[16,3840]{1,0:T(8,128)(2,1)S(1)}, u32[]{:S(2)}, u32[]{:S(2)}) collective-permute-start(bf16[16,3840]{1,0:T(8,128)(2,1)S(1)} %collective-permute-done.16.refs_3_.refs_6_), channel_id=1, source_target_pairs={{0,1},{1,0},{2,3},{3,2},{4,5},{5,4},{6,7},{7,6},{8,9},{9,8},{10,11... | collective-permute-start | bytes 368648 | tf_op jit(solution)/shard_map/ppermute | solution.py:418
  23.4 8.2 %collective-permute-start.21 = (bf16[16,3840]{1,0:T(8,128)(2,1)S(1)}, bf16[16,3840]{1,0:T(8,128)(2,1)S(1)}, u32[]{:S(2)}, u32[]{:S(2)}) collective-permute-start(bf16[16,3840]{1,0:T(8,128)(2,1)S(1)} %collective-permute-done.17.refs_4_.refs_7_), channel_id=1, source_target_pairs={{0,1},{1,0},{2,3},{3,2},{4,5},{5,4},{6,7},{7,6},{8,9},{9,8},{10,11... | collective-permute-start | bytes 368648 | tf_op jit(solution)/shard_map/ppermute | solution.py:418
  24.5 2.0 %copy-start = (bf16[1,3584,512]{2,1,0:T(8,128)(2,1)S(1)}, bf16[1,3584,512]{2,1,0:T(8,128)(2,1)}, u32[]{:S(2)}) copy-start(bf16[1,3584,512]{2,1,0:T(8,128)(2,1)} %refs_10_.4) | copy-start | bytes 11010052
  27.3 4.3 %copy-start.1 = (bf16[1,3584,512]{2,1,0:T(8,128)(2,1)S(1)}, bf16[1,3584,512]{2,1,0:T(8,128)(2,1)}, u32[]{:S(2)}) copy-start(bf16[1,3584,512]{2,1,0:T(8,128)(2,1)} %refs_10_.4) | copy-start | bytes 11010052
  27.3 4.3 %copy-start.5 = (bf16[1,1,136,512]{3,2,1,0:T(8,128)(2,1)S(1)}, bf16[1,1,136,512]{3,2,1,0:T(8,128)(2,1)}, u32[]{:S(2)}) copy-start(bf16[1,1,136,512]{3,2,1,0:T(8,128)(2,1)} %refs_9_.1) | copy-start | bytes 417796
  31.3 8.9 %collective-permute-start.7 = (bf16[80,3584]{1,0:T(8,128)(2,1)S(1)}, bf16[80,3584]{1,0:T(8,128)(2,1)S(1)}, u32[]{:S(2)}, u32[]{:S(2)}) collective-permute-start(bf16[80,3584]{1,0:T(8,128)(2,1)S(1)} %get-tuple-element.32), channel_id=1, source_target_pairs={{0,1},{1,0},{2,3},{3,2},{4,5},{5,4},{6,7},{7,6},{8,9},{9,8},{10,11... | collective-permute-start | bytes 1720328 | tf_op jit(solution)/shard_map/ppermute | solution.py:418
  36.3 16.5 %collective-permute-start.22 = (bf16[80,3712]{1,0:T(8,128)(2,1)S(1)}, bf16[80,3712]{1,0:T(8,128)(2,1)S(1)}, u32[]{:S(2)}, u32[]{:S(2)}) collective-permute-start(bf16[80,3712]{1,0:T(8,128)(2,1)S(1)} %get-tuple-element.47), channel_id=1, source_target_pairs={{0,1},{1,0},{2,3},{3,2},{4,5},{5,4},{6,7},{7,6},{8,9},{9,8},{10,11... | collective-permute-start | bytes 1781768 | tf_op jit(solution)/shard_map/ppermute | solution.py:418
  36.7 5.7 %collective-permute-start.12 = (bf16[16,3840]{1,0:T(8,128)(2,1)S(1)}, bf16[16,3840]{1,0:T(8,128)(2,1)S(1)}, u32[]{:S(2)}, u32[]{:S(2)}) collective-permute-start(bf16[16,3840]{1,0:T(8,128)(2,1)S(1)} %get-tuple-element.39), channel_id=1, source_target_pairs={{0,2},{1,3},{2,0},{3,1},{4,6},{5,7},{6,4},{7,5},{8,10},{9,11},{10,... | collective-permute-start | bytes 368648 | tf_op jit(solution)/shard_map/ppermute | solution.py:411
  38.2 11.2 %collective-permute-start.13 = (bf16[16,3840]{1,0:T(8,128)(2,1)S(1)}, bf16[16,3840]{1,0:T(8,128)(2,1)S(1)}, u32[]{:S(2)}, u32[]{:S(2)}) collective-permute-start(bf16[16,3840]{1,0:T(8,128)(2,1)S(1)} %get-tuple-element.40), channel_id=1, source_target_pairs={{0,4},{1,5},{2,6},{3,7},{4,0},{5,1},{6,2},{7,3},{8,12},{9,13},{10,... | collective-permute-start | bytes 368648 | tf_op jit(solution)/shard_map/ppermute | solution.py:411
  39.3 13.5 %collective-permute-start.14 = (bf16[16,3840]{1,0:T(8,128)(2,1)S(1)}, bf16[16,3840]{1,0:T(8,128)(2,1)S(1)}, u32[]{:S(2)}, u32[]{:S(2)}) collective-permute-start(bf16[16,3840]{1,0:T(8,128)(2,1)S(1)} %get-tuple-element.41), channel_id=1, source_target_pairs={{0,6},{1,7},{2,4},{3,5},{4,2},{5,3},{6,0},{7,1},{8,14},{9,15},{10,... | collective-permute-start | bytes 368648 | tf_op jit(solution)/shard_map/ppermute | solution.py:411
  40.6 15.6 %collective-permute-start.10 = (bf16[16,3840]{1,0:T(8,128)(2,1)S(1)}, bf16[16,3840]{1,0:T(8,128)(2,1)S(1)}, u32[]{:S(2)}, u32[]{:S(2)}) collective-permute-start(bf16[16,3840]{1,0:T(8,128)(2,1)S(1)} %get-tuple-element.36), channel_id=1, source_target_pairs={{0,12},{1,13},{2,14},{3,15},{4,8},{5,9},{6,10},{7,11},{8,20},{9,21... | collective-permute-start | bytes 368648 | tf_op jit(solution)/shard_map/ppermute | solution.py:431
  42.4 16.7 %collective-permute-start.11 = (bf16[16,3840]{1,0:T(8,128)(2,1)S(1)}, bf16[16,3840]{1,0:T(8,128)(2,1)S(1)}, u32[]{:S(2)}, u32[]{:S(2)}) collective-permute-start(bf16[16,3840]{1,0:T(8,128)(2,1)S(1)} %get-tuple-element.37), channel_id=1, source_target_pairs={{0,14},{1,15},{2,12},{3,13},{4,10},{5,11},{6,8},{7,9},{8,22},{9,23... | collective-permute-start | bytes 368648 | tf_op jit(solution)/shard_map/ppermute | solution.py:431
  49.3 12.1 %collective-permute-start.8 = (bf16[16,3840]{1,0:T(8,128)(2,1)S(1)}, bf16[16,3840]{1,0:T(8,128)(2,1)S(1)}, u32[]{:S(2)}, u32[]{:S(2)}) collective-permute-start(bf16[16,3840]{1,0:T(8,128)(2,1)S(1)} %get-tuple-element.34), channel_id=1, source_target_pairs={{0,8},{1,9},{2,10},{3,11},{4,12},{5,13},{6,14},{7,15},{8,16},{9,17... | collective-permute-start | bytes 368648 | tf_op jit(solution)/shard_map/ppermute | solution.py:431
  52.9 9.2 %collective-permute-start.9 = (bf16[16,3840]{1,0:T(8,128)(2,1)S(1)}, bf16[16,3840]{1,0:T(8,128)(2,1)S(1)}, u32[]{:S(2)}, u32[]{:S(2)}) collective-permute-start(bf16[16,3840]{1,0:T(8,128)(2,1)S(1)} %get-tuple-element.35), channel_id=1, source_target_pairs={{0,10},{1,11},{2,8},{3,9},{4,14},{5,15},{6,12},{7,13},{8,18},{9,19... | collective-permute-start | bytes 368648 | tf_op jit(solution)/shard_map/ppermute | solution.py:431
  54.0 9.1 %collective-permute-start.23 = (bf16[16,3840]{1,0:T(8,128)(2,1)S(1)}, bf16[16,3840]{1,0:T(8,128)(2,1)S(1)}, u32[]{:S(2)}, u32[]{:S(2)}) collective-permute-start(bf16[16,3840]{1,0:T(8,128)(2,1)S(1)} %get-tuple-element.48), channel_id=1, source_target_pairs={{0,24},{1,25},{2,26},{3,27},{4,28},{5,29},{6,30},{7,31},{8,0},{9,1... | collective-permute-start | bytes 368648 | tf_op jit(solution)/shard_map/ppermute | solution.py:431
  56.1 8.5 %collective-permute-start.24 = (bf16[16,3840]{1,0:T(8,128)(2,1)S(1)}, bf16[16,3840]{1,0:T(8,128)(2,1)S(1)}, u32[]{:S(2)}, u32[]{:S(2)}) collective-permute-start(bf16[16,3840]{1,0:T(8,128)(2,1)S(1)} %get-tuple-element.49), channel_id=1, source_target_pairs={{0,26},{1,27},{2,24},{3,25},{4,30},{5,31},{6,28},{7,29},{8,2},{9,3... | collective-permute-start | bytes 368648 | tf_op jit(solution)/shard_map/ppermute | solution.py:431
  59.1 6.4 %collective-permute-start.25 = (bf16[16,3840]{1,0:T(8,128)(2,1)S(1)}, bf16[16,3840]{1,0:T(8,128)(2,1)S(1)}, u32[]{:S(2)}, u32[]{:S(2)}) collective-permute-start(bf16[16,3840]{1,0:T(8,128)(2,1)S(1)} %get-tuple-element.50), channel_id=1, source_target_pairs={{0,28},{1,29},{2,30},{3,31},{4,24},{5,25},{6,26},{7,27},{8,4},{9,5... | collective-permute-start | bytes 368648 | tf_op jit(solution)/shard_map/ppermute | solution.py:431
  61.5 6.7 %collective-permute-start.26 = (bf16[16,3840]{1,0:T(8,128)(2,1)S(1)}, bf16[16,3840]{1,0:T(8,128)(2,1)S(1)}, u32[]{:S(2)}, u32[]{:S(2)}) collective-permute-start(bf16[16,3840]{1,0:T(8,128)(2,1)S(1)} %get-tuple-element.51), channel_id=1, source_target_pairs={{0,30},{1,31},{2,28},{3,29},{4,26},{5,27},{6,24},{7,25},{8,6},{9,7... | collective-permute-start | bytes 368648 | tf_op jit(solution)/shard_map/ppermute | solution.py:431
  (2 other events, 1.7 us)

commit v2 on v1

v2 whole, which is shorter than its diff:
```python
import jax
import jax.numpy as jnp
from jax import lax
from jax.experimental import pallas as pl
from jax.experimental.pallas import tpu as pltpu
from jax.sharding import PartitionSpec as P

epsilon = 1e-06
route_scale = 2.5
fold = 256
none = 255.0
f32 = jnp.float32
bf16 = jnp.bfloat16
nt = (((1,), (1,)), ((), ()))
spaces = {
    "s": pl.BlockSpec(memory_space=pltpu.SMEM),
    "v": pl.BlockSpec(memory_space=pltpu.VMEM),
    "a": pl.BlockSpec(memory_space=pl.ANY),
    "h": pl.BlockSpec(memory_space=pltpu.HBM),
}


def call(body, places, outs, scratch, megabytes, name):
    def run(*arrays):
        arrays = [
            pltpu.with_memory_space_constraint(array, pltpu.HBM) if place == "h" else array
            for array, place in zip(arrays, places, strict=True)
        ]
        return kernel(*arrays)

    kernel = pl.pallas_call(
        body,
        out_shape=outs,
        in_specs=[spaces[place] for place in places],
        scratch_shapes=scratch,
        compiler_params=pltpu.CompilerParams(vmem_limit_bytes=megabytes * 1024 * 1024),
        cost_estimate=pl.CostEstimate(flops=1000, bytes_accessed=1000, transcendentals=0),
        name=name,
    )
    return run


def shape(dims, kind=bf16):
    return jax.ShapeDtypeStruct(dims, kind)


class Sizes:
    def __init__(self, groups, experts, tokens, width):
        self.experts = experts
        self.split = groups // experts
        self.tokens = tokens
        self.width = width
        self.main = tokens // experts
        self.cap = self.main + 1
        self.pieces = width // fold
        self.wide = width + fold
        self.rows = tokens + 16
        assert self.main == 16 and self.pieces <= 14 and width % fold == 0
        assert experts <= 8 and experts & (experts - 1) == 0 and self.split & (self.split - 1) == 0


def pack_last(row, tile, first=0):
    for i in range(row.shape[1] // fold):
        tile[first + i : first + i + 1, :] = row[:, i * fold : (i + 1) * fold]


def unpack_last(chunk, z, tile, target, at):
    tile[...] = chunk[:, z.width :].astype(f32)
    for i in range(z.pieces):
        target[at : at + 1, i * fold : (i + 1) * fold] = tile[i : i + 1, :]


def slot_matrices(ids_row, block, z):
    tokens = z.tokens
    sub = lax.broadcasted_iota(jnp.int32, (tokens, tokens), 0)
    lane = lax.broadcasted_iota(jnp.int32, (tokens, tokens), 1)
    row = jnp.bitwise_xor(ids_row, block)
    column = jnp.sum(jnp.where(sub == lane, row, 0), axis=1, keepdims=True)
    same = column == row
    place_row = jnp.sum(jnp.where(same & (sub < lane), 1, 0), axis=0, keepdims=True)
    place_column = jnp.sum(jnp.where(same & (lane < sub), 1, 0), axis=1, keepdims=True)

    def slot(expert, place):
        return jnp.where(place < z.main, expert * z.main + place, tokens + expert)

    slot_row = slot(row, place_row)
    slot_column = slot(column, place_column)
    by_slot = lax.broadcasted_iota(jnp.int32, (z.rows, tokens), 0) == slot_row
    by_token = lax.broadcasted_iota(jnp.int32, (tokens, fold), 1) == slot_column
    token = lax.broadcasted_iota(jnp.int32, (tokens, fold), 0).astype(f32)
    token_row = jnp.sum(jnp.where(by_token, token - none, 0.0), axis=0, keepdims=True) + none
    return jnp.where(by_slot, 1.0, 0.0).astype(bf16), token_row


def write_chunks(z, selector, token_row, rows_ref, tiles, chunks):
    step = z.width // 2
    tiles[...] = jnp.zeros_like(tiles)
    for half in range(2):
        col = half * step
        got = jnp.dot(selector, rows_ref[:, col : col + step], preferred_element_type=f32)
        packed = got[: z.tokens].astype(bf16)
        for k in range(z.experts):
            chunks[k][:, col : col + step] = packed[k * z.main : (k + 1) * z.main]
            pack_last(got[z.tokens + k : z.tokens + k + 1], tiles.at[k], half * z.pieces // 2)
    for k in range(z.experts):
        tiles[k, z.pieces : z.pieces + 1, :] = token_row
        chunks[k][:, z.width :] = tiles[k].astype(bf16)


def make_chunks(z, where, ids, sources, after, name):
    count = len(sources)

    def body(where, ids_any, *refs):
        anys, outs = refs[:count], refs[count + len(after) : -4]
        ids, rows, tiles, sems = refs[-4:]
        copies = [pltpu.make_async_copy(ids_any, ids, sems.at[count])]
        copies += [pltpu.make_async_copy(anys[j], rows.at[j], sems.at[j]) for j in range(count)]
        for copy in copies:
            copy.start()
        copies[0].wait()
        selector, token_row = slot_matrices(ids[...], where[0], z)
        for j in range(count):
            copies[1 + j].wait()
            write_chunks(
                z, selector, token_row, rows.at[j], tiles, outs[j * z.experts : (j + 1) * z.experts]
            )

    outs = call(
        body,
        "sh" + "h" * count + "a" * len(after),
        [shape((z.main, z.wide))] * (z.experts * count),
        [
            pltpu.VMEM((1, z.tokens), jnp.int32),
            pltpu.VMEM((count, z.tokens, z.width), bf16),
            pltpu.VMEM((z.experts, 16, fold), f32),
            pltpu.SemaphoreType.DMA((count + 1,)),
        ],
        8,
        name,
    )(where, ids.reshape(1, z.tokens), *sources, *after)
    return [outs[j * z.experts : (j + 1) * z.experts] for j in range(count)]


def collect_rows(z, chunks, last, tile):
    last[...] = jnp.zeros_like(last)
    for k in range(z.experts):
        unpack_last(chunks[k], z, tile, last, k)


def norm_rows(h, gain):
    inv = lax.rsqrt(jnp.mean(h * h, axis=-1, keepdims=True) + epsilon)
    return (h * inv * gain).astype(bf16), inv


def normed_rows(z, chunks, vectors, after):
    def body(*refs):
        chunks, vectors = refs[: z.experts], refs[z.experts]
        normed_ref, gates_ref, last, tile = refs[z.experts + 1 + len(after) :]
        gain, router = vectors[0:1, :], vectors[1:2, :]
        collect_rows(z, chunks, last, tile)
        for k in range(z.experts + 1):
            h = last[...] if k == z.experts else chunks[k][:, : z.width].astype(f32)
            at = k * z.main
            normed, _ = norm_rows(h, gain)
            normed_ref[at : at + 16, :] = normed
            logits = jnp.sum(normed.astype(f32) * router, axis=-1, keepdims=True)
            gates_ref[at : at + 16, :] = jnp.broadcast_to(jax.nn.sigmoid(logits), (16, 128))

    return call(
        body,
        "v" * (z.experts + 1) + "a" * len(after),
        [shape((z.rows, z.width)), shape((z.rows, 128), f32)],
        [pltpu.VMEM((16, z.width), f32), pltpu.VMEM((16, fold), f32)],
        8,
        "normed_rows",
    )(*chunks, vectors, *after)


def grad_rows_of(z, chunks):
    def body(*refs):
        chunks, (rows, last, tile) = refs[: z.experts], refs[z.experts :]
        for k in range(z.experts):
            rows[k * z.main : (k + 1) * z.main, :] = chunks[k][:, : z.width]
        collect_rows(z, chunks, last, tile)
        rows[z.tokens :, :] = last[...].astype(bf16)

    return call(
        body,
        "v" * z.experts,
        shape((z.rows, z.width)),
        [pltpu.VMEM((16, z.width), f32), pltpu.VMEM((16, fold), f32)],
        8,
        "grad_rows",
    )(*chunks)


def write_parts(z, values, outs, col):
    values = values.astype(bf16)
    for m in range(z.split):
        outs[m][:, col : col + values.shape[1]] = values[m * z.rows : (m + 1) * z.rows]


def experts_forward(z, rows, w_gate, w_down):
    def body(*refs):
        rows, (gate_ref, down_ref), outs = (
            refs[: z.split],
            refs[z.split : z.split + 2],
            refs[z.split + 2 :],
        )
        held = jnp.concatenate([part[...] for part in rows], axis=0)
        gate_proj = jnp.dot(held, gate_ref[...], preferred_element_type=f32)
        hidden = jax.nn.silu(gate_proj).astype(bf16)
        step = 512
        for col in range(0, z.width, step):
            part = jnp.dot(hidden, down_ref[:, col : col + step], preferred_element_type=f32)
            write_parts(z, part, outs, col)

    return call(
        body,
        "v" * (z.split + 2),
        [shape((z.rows, z.width))] * z.split,
        [],
        16,
        "experts_forward",
    )(*rows, w_gate, w_down)


def load_section(z, where, gain, router, w_gate, w_down, saved, after):
    total, slots, width = z.split * z.rows, saved.shape[2], saved.shape[3]

    def body(where, gain_any, router_any, gate_any, down_any, saved_any, *refs):
        refs = refs[len(after) :]
        gate_ref, down_ref, vectors, hidden_ref, slope_ref = refs[:5]
        gain_ref, router_ref, saved_ref, sems = refs[5:]
        pairs = [(saved_any.at[0, 0], saved_ref), (gain_any, gain_ref), (router_any.at[0], router_ref)]
        for source, target in ((gate_any.at[0], gate_ref), (down_any.at[0], down_ref)):
            step = target.shape[0] // 4
            for at in range(0, target.shape[0], step):
                pairs.append((source.at[pl.ds(at, step)], target.at[pl.ds(at, step)]))
        copies = [
            pltpu.make_async_copy(source, target, sems.at[i])
            for i, (source, target) in enumerate(pairs)
        ]
        for copy in copies:
            copy.start()
        row = lax.broadcasted_iota(jnp.int32, (total, slots), 0)
        slot = lax.broadcasted_iota(jnp.int32, (total, slots), 1)
        m, at = row // z.rows, row % z.rows
        is_main = at < z.tokens
        k = jnp.where(is_main, at // z.main, at - z.tokens)
        p = jnp.where(is_main, at % z.main, z.main)
        source = jnp.bitwise_xor(k, where[0]) * z.split + jnp.bitwise_xor(m, where[1])
        wanted = jnp.where(k < z.experts, source * z.cap + p, -1)
        selector = jnp.where(slot == wanted, 1.0, 0.0).astype(bf16)
        copies[0].wait()
        gate_proj = jnp.dot(selector, saved_ref[...], preferred_element_type=f32)
        sg = jax.nn.sigmoid(gate_proj)
        hidden_ref[...] = (gate_proj * sg).astype(bf16)
        slope_ref[...] = sg * (1.0 + gate_proj * (1.0 - sg))
        copies[1].wait()
        copies[2].wait()
        vectors[...] = jnp.zeros_like(vectors)
        vectors[0:1, :] = gain_ref[...].astype(f32)
        table = router_ref[...].astype(f32)
        mine = lax.broadcasted_iota(jnp.int32, (z.experts, 1), 0) == where[0]
        vectors[1:2, :] = jnp.sum(jnp.where(mine, table, 0.0), axis=0, keepdims=True)
        for copy in copies[3:]:
            copy.wait()

    return call(
        body,
        "shhhhh" + "a" * len(after),
        [
            shape(w_gate.shape[1:]),
            shape(w_down.shape[1:]),
            shape((8, z.width), f32),
            shape((total, width)),
            shape((total, width), f32),
        ],
        [
            pltpu.VMEM((1, z.width), bf16),
            pltpu.VMEM((z.experts, z.width), bf16),
            pltpu.VMEM((slots, width), bf16),
            pltpu.SemaphoreType.DMA((11,)),
        ],
        24,
        "load_section",
    )(where, gain, router, w_gate, w_down, saved, *after)


def experts_backward(z, rows, hidden, slope, w_gate, w_down, after):
    def body(*refs):
        rows = refs[: z.split]
        hidden_ref, slope_ref, gate_ref, down_ref = refs[z.split : z.split + 4]
        outs = refs[z.split + 4 + len(after) :]
        held = jnp.concatenate([part[...] for part in rows], axis=0)
        grad_hidden = lax.dot_general(held, down_ref[...], nt, preferred_element_type=f32)
        dots = jnp.sum(grad_hidden * hidden_ref[...].astype(f32), axis=-1, keepdims=True)
        grad_gate = (grad_hidden * slope_ref[...]).astype(bf16)
        step = 512
        for col in range(0, z.width, step):
            part = lax.dot_general(
                grad_gate, gate_ref[col : col + step, :], nt, preferred_element_type=f32
            )
            write_parts(z, part, outs, col)
        write_parts(z, jnp.broadcast_to(dots, (dots.shape[0], 128)), outs, z.width)

    return call(
        body,
        "v" * (z.split + 4) + "a" * len(after),
        [shape((z.rows, z.width + 128))] * z.split,
        [],
        16,
        "experts_backward",
    )(*rows, hidden, slope, w_gate, w_down, *after)


def put_last(z, values, source_chunk, tile, out):
    tile[...] = jnp.zeros_like(tile)
    pack_last(values, tile)
    tokens = source_chunk[:, z.width :].astype(f32)
    tile[z.pieces : z.pieces + 1, :] = tokens[z.pieces : z.pieces + 1, :]
    out[:, z.width :] = tile[...].astype(bf16)


def finish_forward(z, chunks, parts, gates):
    def body(*refs):
        e = z.experts
        chunks, parts = refs[:e], refs[e : e + z.split]
        gates = refs[e + z.split]
        outs = refs[e + z.split + 1 : 2 * e + z.split + 1]
        last, tile = refs[2 * e + z.split + 1 :]

        def mixed(at):
            y = parts[0][at : at + 16, :].astype(f32)
            for part in parts[1:]:
                y = y + part[at : at + 16, :].astype(f32)
            return route_scale * (gates[at : at + 16, 0:1] * y)

        for k in range(e):
            h = chunks[k][:, : z.width].astype(f32)
            outs[k][:, : z.width] = (h + mixed(k * z.main)).astype(bf16)
        collect_rows(z, chunks, last, tile)
        last[...] = last[...] + mixed(z.tokens)
        for k in range(e):
            put_last(z, last[k : k + 1, :], chunks[k], tile, outs[k])

    return call(
        body,
        "v" * (z.experts + z.split + 1),
        [shape((z.main, z.wide))] * z.experts,
        [pltpu.VMEM((16, z.width), f32), pltpu.VMEM((16, fold), f32)],
        8,
        "finish_forward",
    )(*chunks, *parts, gates)


def finish_backward(z, acts, grads, parts, vectors):
    def body(*refs):
        e = z.experts
        acts, grads, parts = refs[:e], refs[e : 2 * e], refs[2 * e : 2 * e + z.split]
        vectors = refs[2 * e + z.split]
        outs = refs[2 * e + z.split + 1 : 3 * e + z.split + 1]
        last_act, last_grad, tile = refs[3 * e + z.split + 1 :]
        gain, router = vectors[0:1, :], vectors[1:2, :]

        def finished(h, g, at):
            normed, inv = norm_rows(h, gain)
            logits = jnp.sum(normed.astype(f32) * router, axis=-1, keepdims=True)
            affinity = jax.nn.sigmoid(logits)
            rows = parts[0][at : at + 16, : z.width].astype(f32)
            dot = parts[0][at : at + 16, z.width :].astype(f32)
            for part in parts[1:]:
                rows = rows + part[at : at + 16, : z.width].astype(f32)
                dot = dot + part[at : at + 16, z.width :].astype(f32)
            dot = dot[:, 0:1]
            grad_logits = (route_scale * dot * affinity * (1.0 - affinity)).astype(bf16).astype(f32)
            grad_pre = (route_scale * affinity * rows + grad_logits * router) * gain
            centre = jnp.mean(grad_pre * h, axis=-1, keepdims=True)
            return g + inv * (grad_pre - h * (inv * inv * centre))

        for k in range(e):
            h = acts[k][:, : z.width].astype(f32)
            g = grads[k][:, : z.width].astype(f32)
            outs[k][:, : z.width] = finished(h, g, k * z.main).astype(bf16)
        collect_rows(z, acts, last_act, tile)
        collect_rows(z, grads, last_grad, tile)
        last_act[...] = finished(last_act[...], last_grad[...], z.tokens)
        for k in range(e):
            put_last(z, last_act[k : k + 1, :], grads[k], tile, outs[k])

    return call(
        body,
        "v" * (2 * z.experts + z.split + 1),
        [shape((z.main, z.wide))] * z.experts,
        [
            pltpu.VMEM((16, z.width), f32),
            pltpu.VMEM((16, z.width), f32),
            pltpu.VMEM((16, fold), f32),
        ],
        8,
        "finish_backward",
    )(*acts, *grads, *parts, vectors)


def order_rows(z, chunks, name):
    def body(*refs):
        chunks, (out, held, last, tile) = refs[: z.experts], refs[z.experts :]
        for k in range(z.experts):
            held[k * z.main : (k + 1) * z.main, :] = chunks[k][:, : z.width]
        collect_rows(z, chunks, last, tile)
        held[z.tokens :, :] = last[...].astype(bf16)
        token_row = chunks[0][:, z.width :].astype(f32)[z.pieces : z.pieces + 1, : z.rows]
        token = lax.broadcasted_iota(jnp.int32, (z.tokens, z.rows), 0).astype(f32)
        selector = jnp.where(token == token_row, 1.0, 0.0).astype(bf16)
        out[...] = jnp.dot(selector, held[...], preferred_element_type=f32).astype(bf16)

    return call(
        body,
        "v" * z.experts,
        shape((z.tokens, z.width)),
        [
            pltpu.VMEM((z.rows, z.width), bf16),
            pltpu.VMEM((16, z.width), f32),
            pltpu.VMEM((16, fold), f32),
        ],
        8,
        name,
    )(*chunks)


def dispatch(z, chunks):
    groups = z.experts * z.split
    got = [chunks[0]] + [None] * (z.experts - 1)
    for k in reversed(range(1, z.experts)):
        pairs = [(i, ((i // z.split) ^ k) * z.split + i % z.split) for i in range(groups)]
        got[k] = lax.ppermute(chunks[k], "ep", pairs)
    return got


def to_core(z, array, m):
    groups = z.experts * z.split
    pairs = [(i, i // z.split * z.split + ((i % z.split) ^ m)) for i in range(groups)]
    return lax.ppermute(array, "ep", pairs)


def to_section(z, chunks, by):
    groups = z.experts * z.split
    sections = lax.axis_size("pp")
    got = [None] * z.experts
    for k in reversed(range(z.experts)):
        pairs = [
            (s * groups + i, (s + by) % sections * groups + ((i // z.split) ^ k) * z.split + i % z.split)
            for s in range(sections)
            for i in range(groups)
        ]
        got[k] = lax.ppermute(chunks[k], ("pp", "ep"), pairs)
    return got


def on_device(
    fwd_act, fwd_ids, bwd_act, bwd_ids, bwd_grad, norm_gain, router, w_gate, w_down, saved_gate
):
    groups = lax.axis_size("ep")
    assert fwd_ids.shape[1] == 1
    z = Sizes(groups, router.shape[2], fwd_act.shape[0], fwd_act.shape[1])
    index = lax.axis_index("ep")
    where = jnp.stack([index // z.split, index % z.split]).astype(jnp.int32)
    router = jnp.swapaxes(router, 1, 2)
    others = range(1, z.split)

    (fwd_chunks,) = make_chunks(z, where, fwd_ids, [fwd_act], [], "forward_chunks")
    fwd_own = dispatch(z, fwd_chunks)
    grad_chunks, act_chunks = make_chunks(
        z, where, bwd_ids, [bwd_grad, bwd_act], [fwd_chunks[0]], "backward_chunks"
    )
    grad_own = dispatch(z, grad_chunks)
    gate, down, vectors, hidden, slope = load_section(
        z, where, norm_gain, router, w_gate, w_down, saved_gate, [grad_chunks[0]]
    )

    normed, gates = normed_rows(z, fwd_own, vectors, [gate])
    fwd_all = [normed] + [to_core(z, normed, m) for m in others]
    fwd_parts = experts_forward(z, fwd_all, gate, down)
    fwd_parts = [fwd_parts[0]] + [to_core(z, fwd_parts[m], m) for m in others]
    fwd_out = finish_forward(z, fwd_own, fwd_parts, gates)
    fwd_done = to_section(z, fwd_out, 1)

    act_own = dispatch(z, act_chunks)
    grads = grad_rows_of(z, grad_own)
    grad_all = [grads] + [to_core(z, grads, m) for m in others]
    bwd_parts = experts_backward(
        z, grad_all, hidden, slope, gate, down, [*act_own[1:], fwd_out[0]]
    )
    bwd_parts = [bwd_parts[0]] + [to_core(z, bwd_parts[m], m) for m in others]
    bwd_done = to_section(z, finish_backward(z, act_own, grad_own, bwd_parts, vectors), -1)
    return (order_rows(z, fwd_done, "forward_rows"), order_rows(z, bwd_done, "backward_rows"))


def solution(mesh):
    return jax.shard_map(
        on_device,
        mesh=mesh,
        in_specs=(
            P(("pp", "ep"), None),
            P(("pp", "ep"), None),
            P(("pp", "ep"), None),
            P(("pp", "ep"), None),
            P(("pp", "ep"), None),
            P("pp", None),
            P("pp", None, None),
            P(("pp", "ep"), None, None),
            P(("pp", "ep"), None, None),
            P("pp", "ep", None, None),
        ),
        out_specs=(P(("pp", "ep"), None), P(("pp", "ep"), None)),
        check_vma=False,
    )
```

time: 69.7 us -> 64.5 us (0.925)
  local copies, waits for them, and re-layouts: 7.31 us -> 0 us
  waiting for transfers between devices: 15 us -> 20.7 us
  starting transfers between devices: 30.6 us -> 26.4 us
  Pallas kernels: 14.6 us -> 16.3 us
  other arithmetic: 0.94 us -> 0.08 us
    unnamed x16 -> x0, local copies, waits for them, and re-layouts: 7.3 us -> none
    ppermute x8, waiting for transfers between devices: 5.01 us -> 10.2 us  [to_section(): got[k] = lax.ppermute(chunks[k], ('pp', 'ep'), pairs)]
    ppermute x8, starting transfers between devices: 16.9 us -> 14.5 us  [to_section(): got[k] = lax.ppermute(chunks[k], ('pp', 'ep'), pairs)]
    ppermute x10 -> x4, starting transfers between devices: 2.11 us -> 0.23 us  [to_core(): return lax.ppermute(array, 'ep', pairs)]
    pallas_call x8 -> x11, Pallas kernels: 14.6 us -> 16.3 us  [run(): return kernel(*arrays)]
    reduce_sum x1 -> x0, other arithmetic: 0.86 us -> none  [on_device(): jnp.sum(jnp.where(mine, router[0].astype(f32), 0.0), axis=1)[None, :]]
  transfers between devices with their start and end apart: 27 -> 21, of which waited for: 7 -> 11; matrix products, arithmetic and copies ran while one was open for 2% -> 0% of each run, Pallas kernels for 18% -> 16%
where the time goes in v2:
time: 64.5 us; the launch traced here: 64.3 us
  starting transfers between devices  26.4 us (41%)
  waiting for transfers between devices  20.7 us (32%)
  Pallas kernels  16.3 us (25%)
  between operations  0.76 us (1%)
    pallas_call x11, Pallas kernels, run(): return kernel(*arrays)  16.3 us
    ppermute x8, starting transfers between devices, to_section(): got[k] = lax.ppermute(chunks[k], ('pp', 'ep'), pairs)  14.5 us
    ppermute x9, starting transfers between devices, dispatch(): got[k] = lax.ppermute(chunks[k], 'ep', pairs)  11.7 us
    ppermute x9, waiting for transfers between devices, dispatch(): got[k] = lax.ppermute(chunks[k], 'ep', pairs)  10.5 us
    ppermute x8, waiting for transfers between devices, to_section(): got[k] = lax.ppermute(chunks[k], ('pp', 'ep'), pairs)  10.2 us
  transfers between devices with their start and end apart: 21, of which 11 were waited for; matrix products, arithmetic and copies ran while one was open for 0% of the time, Pallas kernels for 16%

profile of v2, /device:TPU:0, one launch (start us, length us, event | category | flops | bytes accessed | tf_op | source)
XLA Modules:
  0.0 64.3 jit_solution(16245702882747370367)
XLA Ops:
  0.7 1.9 %forward_chunks.1 = (bf16[16,3840]{1,0:T(8,128)(2,1)S(1)}, bf16[16,3840]{1,0:T(8,128)(2,1)S(1)}, bf16[16,3840]{1,0:T(8,128)(2,1)S(1)}, bf16[16,3840]{1,0:T(8,128)(2,1)S(1)}) custom-call(s32[2]{0:T(128)S(1)} %pad_add_fusion.where, s32[1,64]{1,0:T(1,128)} %bitcast.7, bf16[64,3584]{1,0:T(8,128)(2,1)} %refs_0_.2), custom_call_target="tpu_custom_call" | custom-call | flops 1000 | bytes 1000 | tf_op jit(solution)/shard_map/forward_chunks/pallas_call | solution.py:29
  2.6 3.0 %collective-permute-start = (bf16[16,3840]{1,0:T(8,128)(2,1)S(1)}, bf16[16,3840]{1,0:T(8,128)(2,1)S(1)}, u32[]{:S(2)}, u32[]{:S(2)}) collective-permute-start(bf16[16,3840]{1,0:T(8,128)(2,1)S(1)} %get-tuple-element.34), channel_id=1, source_target_pairs={{0,2},{1,3},{2,0},{3,1},{4,6},{5,7},{6,4},{7,5},{8,10},{9,11},{10,... | collective-permute-start | bytes 368648 | tf_op jit(solution)/shard_map/ppermute | solution.py:437
  5.6 1.5 %collective-permute-start.1 = (bf16[16,3840]{1,0:T(8,128)(2,1)S(1)}, bf16[16,3840]{1,0:T(8,128)(2,1)S(1)}, u32[]{:S(2)}, u32[]{:S(2)}) collective-permute-start(bf16[16,3840]{1,0:T(8,128)(2,1)S(1)} %get-tuple-element.35), channel_id=1, source_target_pairs={{0,4},{1,5},{2,6},{3,7},{4,0},{5,1},{6,2},{7,3},{8,12},{9,13},{10,... | collective-permute-start | bytes 368648 | tf_op jit(solution)/shard_map/ppermute | solution.py:437
  7.2 2.2 %backward_chunks.1 = (bf16[16,3840]{1,0:T(8,128)(2,1)S(1)}, bf16[16,3840]{1,0:T(8,128)(2,1)S(1)}, bf16[16,3840]{1,0:T(8,128)(2,1)S(1)}, bf16[16,3840]{1,0:T(8,12...) custom-call(s32[2]{0:T(128)S(1)} %pad_add_fusion.where, ...), custom_call_target="tpu_custom_call" | custom-call | flops 1000 | bytes 1000 | tf_op jit(solution)/shard_map/backward_chunks/pallas_call | solution.py:29
  9.4 3.8 %load_section.1 = (bf16[3584,512]{1,0:T(8,128)(2,1)S(1)}, bf16[512,3584]{1,0:T(8,128)(2,1)S(1)}, f32[8,3584]{1,0:T(8,128)S(1)}, bf16[160,512]{1,0:T(8,128)(2,1)S(1)}, f32[160,512]{1,0:T(8,128)S(1)}) custom-call(s32[2]{0:T(128)S(1)} %pad_add_fusion.where, bf16[1,3584]{1,0:T(2,128)(2,1)} %gain_any.1, bf16[1,4,3584]{2,1,0:T(4,128)(2,1)} %bitcast.5, ...), custom_call_target="tpu_custom_call" | custom-call | flops 1000 | bytes 1000 | tf_op jit(solution)/shard_map/load_section/pallas_call | solution.py:29
  13.8 2.0 %collective-permute-start.12 = (bf16[16,3840]{1,0:T(8,128)(2,1)S(1)}, bf16[16,3840]{1,0:T(8,128)(2,1)S(1)}, u32[]{:S(2)}, u32[]{:S(2)}) collective-permute-start(bf16[16,3840]{1,0:T(8,128)(2,1)S(1)} %get-tuple-element.53), channel_id=1, source_target_pairs={{0,2},{1,3},{2,0},{3,1},{4,6},{5,7},{6,4},{7,5},{8,10},{9,11},{10,... | collective-permute-start | bytes 368648 | tf_op jit(solution)/shard_map/ppermute | solution.py:437
  15.8 1.5 %collective-permute-start.13 = (bf16[16,3840]{1,0:T(8,128)(2,1)S(1)}, bf16[16,3840]{1,0:T(8,128)(2,1)S(1)}, u32[]{:S(2)}, u32[]{:S(2)}) collective-permute-start(bf16[16,3840]{1,0:T(8,128)(2,1)S(1)} %get-tuple-element.54), channel_id=1, source_target_pairs={{0,4},{1,5},{2,6},{3,7},{4,0},{5,1},{6,2},{7,3},{8,12},{9,13},{10,... | collective-permute-start | bytes 368648 | tf_op jit(solution)/shard_map/ppermute | solution.py:437
  17.4 1.5 %experts_forward.1 = (bf16[80,3584]{1,0:T(8,128)(2,1)S(1)}, bf16[80,3584]{1,0:T(8,128)(2,1)S(1)}) custom-call(bf16[80,3584]{1,0:T(8,128)(2,1)S(1)} %get-tuple-element.40.refs_0_, bf16[80,3584]{1,0:T(8,128)(2,1)S(1)} %collective-permute-done.3.refs_1_, bf16[3584,512]{1,0:T(8,128)(2,1)S(1)} %get-tuple-element.39.refs_5_.refs_2_.refs_4_, ...), custom_call_target="tpu_custom_call" | custom-call | flops 1000 | bytes 1000 | tf_op jit(solution)/shard_map/experts_forward/pallas_call | solution.py:29
  18.9 0.8 %collective-permute-done.12.refs_1_.refs_5_ = bf16[16,3840]{1,0:T(8,128)(2,1)S(1)} collective-permute-done((bf16[16,3840]{1,0:T(8,128)(2,1)S(1)}, bf16[16,3840]{1,0:T(8,128)(2,1)S(1)}, u32[]{:S(2)}, u32[]{:S(2)}) %collective-permute-start.12) | collective-permute-done | bytes 122912 | tf_op jit(solution)/shard_map/ppermute | solution.py:437
  19.7 4.1 %collective-permute-done.13.refs_2_.refs_6_ = bf16[16,3840]{1,0:T(8,128)(2,1)S(1)} collective-permute-done((bf16[16,3840]{1,0:T(8,128)(2,1)S(1)}, bf16[16,3840]{1,0:T(8,128)(2,1)S(1)}, u32[]{:S(2)}, u32[]{:S(2)}) %collective-permute-start.13) | collective-permute-done | bytes 122912 | tf_op jit(solution)/shard_map/ppermute | solution.py:437
  24.0 1.6 %collective-permute-start.10 = (bf16[16,3840]{1,0:T(8,128)(2,1)S(1)}, bf16[16,3840]{1,0:T(8,128)(2,1)S(1)}, u32[]{:S(2)}, u32[]{:S(2)}) collective-permute-start(bf16[16,3840]{1,0:T(8,128)(2,1)S(1)} %get-tuple-element.51), channel_id=1, source_target_pairs={{0,4},{1,5},{2,6},{3,7},{4,0},{5,1},{6,2},{7,3},{8,12},{9,13},{10,... | collective-permute-start | bytes 368648 | tf_op jit(solution)/shard_map/ppermute | solution.py:437
  25.6 1.2 %collective-permute-start.11 = (bf16[16,3840]{1,0:T(8,128)(2,1)S(1)}, bf16[16,3840]{1,0:T(8,128)(2,1)S(1)}, u32[]{:S(2)}, u32[]{:S(2)}) collective-permute-start(bf16[16,3840]{1,0:T(8,128)(2,1)S(1)} %get-tuple-element.52), channel_id=1, source_target_pairs={{0,6},{1,7},{2,4},{3,5},{4,2},{5,3},{6,0},{7,1},{8,14},{9,15},{10,... | collective-permute-start | bytes 368648 | tf_op jit(solution)/shard_map/ppermute | solution.py:437
  26.8 0.8 %collective-permute-start.9 = (bf16[16,3840]{1,0:T(8,128)(2,1)S(1)}, bf16[16,3840]{1,0:T(8,128)(2,1)S(1)}, u32[]{:S(2)}, u32[]{:S(2)}) collective-permute-start(bf16[16,3840]{1,0:T(8,128)(2,1)S(1)} %get-tuple-element.50), channel_id=1, source_target_pairs={{0,2},{1,3},{2,0},{3,1},{4,6},{5,7},{6,4},{7,5},{8,10},{9,11},{10,... | collective-permute-start | bytes 368648 | tf_op jit(solution)/shard_map/ppermute | solution.py:437
  28.0 4.0 %collective-permute-done.10.refs_7_.refs_2_ = bf16[16,3840]{1,0:T(8,128)(2,1)S(1)} collective-permute-done((bf16[16,3840]{1,0:T(8,128)(2,1)S(1)}, bf16[16,3840]{1,0:T(8,128)(2,1)S(1)}, u32[]{:S(2)}, u32[]{:S(2)}) %collective-permute-start.10) | collective-permute-done | bytes 122912 | tf_op jit(solution)/shard_map/ppermute | solution.py:437
  32.1 0.7 %collective-permute-done.11.refs_8_.refs_3_ = bf16[16,3840]{1,0:T(8,128)(2,1)S(1)} collective-permute-done((bf16[16,3840]{1,0:T(8,128)(2,1)S(1)}, bf16[16,3840]{1,0:T(8,128)(2,1)S(1)}, u32[]{:S(2)}, u32[]{:S(2)}) %collective-permute-start.11) | collective-permute-done | bytes 122912 | tf_op jit(solution)/shard_map/ppermute | solution.py:437
  32.7 0.9 %collective-permute-done.9.refs_6_.refs_1_ = bf16[16,3840]{1,0:T(8,128)(2,1)S(1)} collective-permute-done((bf16[16,3840]{1,0:T(8,128)(2,1)S(1)}, bf16[16,3840]{1,0:T(8,128)(2,1)S(1)}, u32[]{:S(2)}, u32[]{:S(2)}) %collective-permute-start.9) | collective-permute-done | bytes 122912 | tf_op jit(solution)/shard_map/ppermute | solution.py:437
  33.6 2.6 %experts_backward.1 = (bf16[80,3712]{1,0:T(8,128)(2,1)S(1)}, bf16[80,3712]{1,0:T(8,128)(2,1)S(1)}) custom-call(bf16[80,3584]{1,0:T(8,128)(2,1)S(1)} %grad_rows.1.refs_0_, bf16[80,3584]{1,0:T(8,128)(2,1)S(1)} %collective-permute-done.15.refs_1_, bf16[160,512]{1,0:T(8,128)(2,1)S(1)} %get-tuple-element.56.refs_2_, f32[160,512]{1,0:T(8,128)S(1)} %get-tuple-element.57.refs_3_, ...), custom_call_target="tpu_custom_call" | custom-call | flops 1000 | bytes 1000 | tf_op jit(solution)/shard_map/experts_backward/pallas_call | solution.py:29
  36.3 1.6 %collective-permute-start.5 = (bf16[16,3840]{1,0:T(8,128)(2,1)S(1)}, bf16[16,3840]{1,0:T(8,128)(2,1)S(1)}, u32[]{:S(2)}, u32[]{:S(2)}) collective-permute-start(bf16[16,3840]{1,0:T(8,128)(2,1)S(1)} %get-tuple-element.45.refs_9_), channel_id=1, source_target_pairs={{0,8},{1,9},{2,10},{3,11},{4,12},{5,13},{6,14},{7,15},{8,16},{9,17... | collective-permute-start | bytes 368648 | tf_op jit(solution)/shard_map/ppermute | solution.py:457
  37.9 2.2 %collective-permute-start.6 = (bf16[16,3840]{1,0:T(8,128)(2,1)S(1)}, bf16[16,3840]{1,0:T(8,128)(2,1)S(1)}, u32[]{:S(2)}, u32[]{:S(2)}) collective-permute-start(bf16[16,3840]{1,0:T(8,128)(2,1)S(1)} %get-tuple-element.46), channel_id=1, source_target_pairs={{0,10},{1,11},{2,8},{3,9},{4,14},{5,15},{6,12},{7,13},{8,18},{9,19... | collective-permute-start | bytes 368648 | tf_op jit(solution)/shard_map/ppermute | solution.py:457
  40.1 1.8 %collective-permute-start.7 = (bf16[16,3840]{1,0:T(8,128)(2,1)S(1)}, bf16[16,3840]{1,0:T(8,128)(2,1)S(1)}, u32[]{:S(2)}, u32[]{:S(2)}) collective-permute-start(bf16[16,3840]{1,0:T(8,128)(2,1)S(1)} %get-tuple-element.47), channel_id=1, source_target_pairs={{0,12},{1,13},{2,14},{3,15},{4,8},{5,9},{6,10},{7,11},{8,20},{9,21... | collective-permute-start | bytes 368648 | tf_op jit(solution)/shard_map/ppermute | solution.py:457
  42.0 1.1 %collective-permute-start.8 = (bf16[16,3840]{1,0:T(8,128)(2,1)S(1)}, bf16[16,3840]{1,0:T(8,128)(2,1)S(1)}, u32[]{:S(2)}, u32[]{:S(2)}) collective-permute-start(bf16[16,3840]{1,0:T(8,128)(2,1)S(1)} %get-tuple-element.48), channel_id=1, source_target_pairs={{0,14},{1,15},{2,12},{3,13},{4,10},{5,11},{6,8},{7,9},{8,22},{9,23... | collective-permute-start | bytes 368648 | tf_op jit(solution)/shard_map/ppermute | solution.py:457
  43.1 1.1 %finish_backward.1 = (bf16[16,3840]{1,0:T(8,128)(2,1)S(1)}, bf16[16,3840]{1,0:T(8,128)(2,1)S(1)}, bf16[16,3840]{1,0:T(8,128)(2,1)S(1)}, bf16[16,3840]{1,0:T(8,128)(2,1)S(1)}) custom-call(bf16[16,3840]{1,0:T(8,128)(2,1)S(1)} %get-tuple-element.49.refs_0_, bf16[16,3840]{1,0:T(8,128)(2,1)S(1)} %collective-permute-done.9.refs_6_.refs_1_, ...), custom_call_target="tpu_custom_call" | custom-call | flops 1000 | bytes 1000 | tf_op jit(solution)/shard_map/finish_backward/pallas_call | solution.py:29
  44.2 3.6 %collective-permute-start.17 = (bf16[16,3840]{1,0:T(8,128)(2,1)S(1)}, bf16[16,3840]{1,0:T(8,128)(2,1)S(1)}, u32[]{:S(2)}, u32[]{:S(2)}) collective-permute-start(bf16[16,3840]{1,0:T(8,128)(2,1)S(1)} %get-tuple-element.60), channel_id=1, source_target_pairs={{0,24},{1,25},{2,26},{3,27},{4,28},{5,29},{6,30},{7,31},{8,0},{9,1... | collective-permute-start | bytes 368648 | tf_op jit(solution)/shard_map/ppermute | solution.py:457
  47.9 1.1 %collective-permute-start.18 = (bf16[16,3840]{1,0:T(8,128)(2,1)S(1)}, bf16[16,3840]{1,0:T(8,128)(2,1)S(1)}, u32[]{:S(2)}, u32[]{:S(2)}) collective-permute-start(bf16[16,3840]{1,0:T(8,128)(2,1)S(1)} %get-tuple-element.61), channel_id=1, source_target_pairs={{0,26},{1,27},{2,24},{3,25},{4,30},{5,31},{6,28},{7,29},{8,2},{9,3... | collective-permute-start | bytes 368648 | tf_op jit(solution)/shard_map/ppermute | solution.py:457
  49.0 0.7 %collective-permute-start.19 = (bf16[16,3840]{1,0:T(8,128)(2,1)S(1)}, bf16[16,3840]{1,0:T(8,128)(2,1)S(1)}, u32[]{:S(2)}, u32[]{:S(2)}) collective-permute-start(bf16[16,3840]{1,0:T(8,128)(2,1)S(1)} %get-tuple-element.62), channel_id=1, source_target_pairs={{0,28},{1,29},{2,30},{3,31},{4,24},{5,25},{6,26},{7,27},{8,4},{9,5... | collective-permute-start | bytes 368648 | tf_op jit(solution)/shard_map/ppermute | solution.py:457
  49.7 0.9 %collective-permute-done.7.refs_2_ = bf16[16,3840]{1,0:T(8,128)(2,1)S(1)} collective-permute-done((bf16[16,3840]{1,0:T(8,128)(2,1)S(1)}, bf16[16,3840]{1,0:T(8,128)(2,1)S(1)}, u32[]{:S(2)}, u32[]{:S(2)}) %collective-permute-start.7) | collective-permute-done | bytes 122912 | tf_op jit(solution)/shard_map/ppermute | solution.py:457
  50.7 2.2 %collective-permute-start.20 = (bf16[16,3840]{1,0:T(8,128)(2,1)S(1)}, bf16[16,3840]{1,0:T(8,128)(2,1)S(1)}, u32[]{:S(2)}, u32[]{:S(2)}) collective-permute-start(bf16[16,3840]{1,0:T(8,128)(2,1)S(1)} %get-tuple-element.63), channel_id=1, source_target_pairs={{0,30},{1,31},{2,28},{3,29},{4,26},{5,27},{6,24},{7,25},{8,6},{9,7... | collective-permute-start | bytes 368648 | tf_op jit(solution)/shard_map/ppermute | solution.py:457
  53.1 1.1 %forward_rows.1 = bf16[64,3584]{1,0:T(8,128)(2,1)} custom-call(bf16[16,3840]{1,0:T(8,128)(2,1)S(1)} %collective-permute-done.5.refs_0_, bf16[16,3840]{1,0:T(8,128)(2,1)S(1)} %collective-permute-done.6.refs_1_, bf16[16,3840]{1,0:T(8,128)(2,1)S(1)} %collective-permute-done.7.refs_2_, bf16[16,3840]{1,0:T(8,128)(2,1)S(1)} %collective-permute-done.8.refs_3_), custom_call_target="tpu_custom_call" | custom-call | flops 1000 | bytes 1000 | tf_op jit(solution)/shard_map/forward_rows/pallas_call | solution.py:29
  54.5 3.3 %collective-permute-done.18.refs_1_ = bf16[16,3840]{1,0:T(8,128)(2,1)S(1)} collective-permute-done((bf16[16,3840]{1,0:T(8,128)(2,1)S(1)}, bf16[16,3840]{1,0:T(8,128)(2,1)S(1)}, u32[]{:S(2)}, u32[]{:S(2)}) %collective-permute-start.18) | collective-permute-done | bytes 122912 | tf_op jit(solution)/shard_map/ppermute | solution.py:457
  57.8 3.0 %collective-permute-done.19.refs_2_ = bf16[16,3840]{1,0:T(8,128)(2,1)S(1)} collective-permute-done((bf16[16,3840]{1,0:T(8,128)(2,1)S(1)}, bf16[16,3840]{1,0:T(8,128)(2,1)S(1)}, u32[]{:S(2)}, u32[]{:S(2)}) %collective-permute-start.19) | collective-permute-done | bytes 122912 | tf_op jit(solution)/shard_map/ppermute | solution.py:457
  60.8 2.5 %collective-permute-done.20.refs_3_ = bf16[16,3840]{1,0:T(8,128)(2,1)S(1)} collective-permute-done((bf16[16,3840]{1,0:T(8,128)(2,1)S(1)}, bf16[16,3840]{1,0:T(8,128)(2,1)S(1)}, u32[]{:S(2)}, u32[]{:S(2)}) %collective-permute-start.20) | collective-permute-done | bytes 122912 | tf_op jit(solution)/shard_map/ppermute | solution.py:457
  63.3 1.1 %backward_rows.1 = bf16[64,3584]{1,0:T(8,128)(2,1)} custom-call(bf16[16,3840]{1,0:T(8,128)(2,1)S(1)} %collective-permute-done.17.refs_0_, bf16[16,3840]{1,0:T(8,128)(2,1)S(1)} %collective-permute-done.18.refs_1_, bf16[16,3840]{1,0:T(8,128)(2,1)S(1)} %collective-permute-done.19.refs_2_, bf16[16,3840]{1,0:T(8,128)(2,1)S(1)} %collective-permute-done.20.refs_3_), custom_call_target="tpu_custom_call" | custom-call | flops 1000 | bytes 1000 | tf_op jit(solution)/shard_map/backward_rows/pallas_call | solution.py:29
  (22 shorter events, 2.0 us)
Async XLA Ops:
  2.6 10.6 %collective-permute-start = (bf16[16,3840]{1,0:T(8,128)(2,1)S(1)}, bf16[16,3840]{1,0:T(8,128)(2,1)S(1)}, u32[]{:S(2)}, u32[]{:S(2)}) collective-permute-start(bf16[16,3840]{1,0:T(8,128)(2,1)S(1)} %get-tuple-element.34), channel_id=1, source_target_pairs={{0,2},{1,3},{2,0},{3,1},{4,6},{5,7},{6,4},{7,5},{8,10},{9,11},{10,... | collective-permute-start | bytes 368648 | tf_op jit(solution)/shard_map/ppermute | solution.py:437
  5.6 7.6 %collective-permute-start.1 = (bf16[16,3840]{1,0:T(8,128)(2,1)S(1)}, bf16[16,3840]{1,0:T(8,128)(2,1)S(1)}, u32[]{:S(2)}, u32[]{:S(2)}) collective-permute-start(bf16[16,3840]{1,0:T(8,128)(2,1)S(1)} %get-tuple-element.35), channel_id=1, source_target_pairs={{0,4},{1,5},{2,6},{3,7},{4,0},{5,1},{6,2},{7,3},{8,12},{9,13},{10,... | collective-permute-start | bytes 368648 | tf_op jit(solution)/shard_map/ppermute | solution.py:437
  7.1 6.1 %collective-permute-start.2 = (bf16[16,3840]{1,0:T(8,128)(2,1)S(1)}, bf16[16,3840]{1,0:T(8,128)(2,1)S(1)}, u32[]{:S(2)}, u32[]{:S(2)}) collective-permute-start(bf16[16,3840]{1,0:T(8,128)(2,1)S(1)} %get-tuple-element.36), channel_id=1, source_target_pairs={{0,6},{1,7},{2,4},{3,5},{4,2},{5,3},{6,0},{7,1},{8,14},{9,15},{10,... | collective-permute-start | bytes 368648 | tf_op jit(solution)/shard_map/ppermute | solution.py:437
  13.8 3.6 %collective-permute-start.3 = (bf16[80,3584]{1,0:T(8,128)(2,1)S(1)}, bf16[80,3584]{1,0:T(8,128)(2,1)S(1)}, u32[]{:S(2)}, u32[]{:S(2)}) collective-permute-start(bf16[80,3584]{1,0:T(8,128)(2,1)S(1)} %get-tuple-element.40.refs_0_), channel_id=1, source_target_pairs={{0,1},{1,0},{2,3},{3,2},{4,5},{5,4},{6,7},{7,6},{8,9},{9,8},{10,11... | collective-permute-start | bytes 1720328 | tf_op jit(solution)/shard_map/ppermute | solution.py:444
  13.8 5.9 %collective-permute-start.12 = (bf16[16,3840]{1,0:T(8,128)(2,1)S(1)}, bf16[16,3840]{1,0:T(8,128)(2,1)S(1)}, u32[]{:S(2)}, u32[]{:S(2)}) collective-permute-start(bf16[16,3840]{1,0:T(8,128)(2,1)S(1)} %get-tuple-element.53), channel_id=1, source_target_pairs={{0,2},{1,3},{2,0},{3,1},{4,6},{5,7},{6,4},{7,5},{8,10},{9,11},{10,... | collective-permute-start | bytes 368648 | tf_op jit(solution)/shard_map/ppermute | solution.py:437
  15.8 8.0 %collective-permute-start.13 = (bf16[16,3840]{1,0:T(8,128)(2,1)S(1)}, bf16[16,3840]{1,0:T(8,128)(2,1)S(1)}, u32[]{:S(2)}, u32[]{:S(2)}) collective-permute-start(bf16[16,3840]{1,0:T(8,128)(2,1)S(1)} %get-tuple-element.54), channel_id=1, source_target_pairs={{0,4},{1,5},{2,6},{3,7},{4,0},{5,1},{6,2},{7,3},{8,12},{9,13},{10,... | collective-permute-start | bytes 368648 | tf_op jit(solution)/shard_map/ppermute | solution.py:437
  17.3 6.5 %collective-permute-start.14 = (bf16[16,3840]{1,0:T(8,128)(2,1)S(1)}, bf16[16,3840]{1,0:T(8,128)(2,1)S(1)}, u32[]{:S(2)}, u32[]{:S(2)}) collective-permute-start(bf16[16,3840]{1,0:T(8,128)(2,1)S(1)} %get-tuple-element.55), channel_id=1, source_target_pairs={{0,6},{1,7},{2,4},{3,5},{4,2},{5,3},{6,0},{7,1},{8,14},{9,15},{10,... | collective-permute-start | bytes 368648 | tf_op jit(solution)/shard_map/ppermute | solution.py:437
  18.9 8.7 %collective-permute-start.4 = (bf16[80,3584]{1,0:T(8,128)(2,1)S(1)}, bf16[80,3584]{1,0:T(8,128)(2,1)S(1)}, u32[]{:S(2)}, u32[]{:S(2)}) collective-permute-start(bf16[80,3584]{1,0:T(8,128)(2,1)S(1)} %get-tuple-element.43), channel_id=1, source_target_pairs={{0,1},{1,0},{2,3},{3,2},{4,5},{5,4},{6,7},{7,6},{8,9},{9,8},{10,11... | collective-permute-start | bytes 1720328 | tf_op jit(solution)/shard_map/ppermute | solution.py:444
  23.9 9.7 %collective-permute-start.15 = (bf16[80,3584]{1,0:T(8,128)(2,1)S(1)}, bf16[80,3584]{1,0:T(8,128)(2,1)S(1)}, u32[]{:S(2)}, u32[]{:S(2)}) collective-permute-start(bf16[80,3584]{1,0:T(8,128)(2,1)S(1)} %grad_rows.1.refs_0_), channel_id=1, source_target_pairs={{0,1},{1,0},{2,3},{3,2},{4,5},{5,4},{6,7},{7,6},{8,9},{9,8},{10,11... | collective-permute-start | bytes 1720328 | tf_op jit(solution)/shard_map/ppermute | solution.py:444
  24.0 8.0 %collective-permute-start.10 = (bf16[16,3840]{1,0:T(8,128)(2,1)S(1)}, bf16[16,3840]{1,0:T(8,128)(2,1)S(1)}, u32[]{:S(2)}, u32[]{:S(2)}) collective-permute-start(bf16[16,3840]{1,0:T(8,128)(2,1)S(1)} %get-tuple-element.51), channel_id=1, source_target_pairs={{0,4},{1,5},{2,6},{3,7},{4,0},{5,1},{6,2},{7,3},{8,12},{9,13},{10,... | collective-permute-start | bytes 368648 | tf_op jit(solution)/shard_map/ppermute | solution.py:437
  25.6 7.1 %collective-permute-start.11 = (bf16[16,3840]{1,0:T(8,128)(2,1)S(1)}, bf16[16,3840]{1,0:T(8,128)(2,1)S(1)}, u32[]{:S(2)}, u32[]{:S(2)}) collective-permute-start(bf16[16,3840]{1,0:T(8,128)(2,1)S(1)} %get-tuple-element.52), channel_id=1, source_target_pairs={{0,6},{1,7},{2,4},{3,5},{4,2},{5,3},{6,0},{7,1},{8,14},{9,15},{10,... | collective-permute-start | bytes 368648 | tf_op jit(solution)/shard_map/ppermute | solution.py:437
  26.8 6.8 %collective-permute-start.9 = (bf16[16,3840]{1,0:T(8,128)(2,1)S(1)}, bf16[16,3840]{1,0:T(8,128)(2,1)S(1)}, u32[]{:S(2)}, u32[]{:S(2)}) collective-permute-start(bf16[16,3840]{1,0:T(8,128)(2,1)S(1)} %get-tuple-element.50), channel_id=1, source_target_pairs={{0,2},{1,3},{2,0},{3,1},{4,6},{5,7},{6,4},{7,5},{8,10},{9,11},{10,... | collective-permute-start | bytes 368648 | tf_op jit(solution)/shard_map/ppermute | solution.py:437
  36.2 6.9 %collective-permute-start.16 = (bf16[80,3712]{1,0:T(8,128)(2,1)S(1)}, bf16[80,3712]{1,0:T(8,128)(2,1)S(1)}, u32[]{:S(2)}, u32[]{:S(2)}) collective-permute-start(bf16[80,3712]{1,0:T(8,128)(2,1)S(1)} %get-tuple-element.59), channel_id=1, source_target_pairs={{0,1},{1,0},{2,3},{3,2},{4,5},{5,4},{6,7},{7,6},{8,9},{9,8},{10,11... | collective-permute-start | bytes 1781768 | tf_op jit(solution)/shard_map/ppermute | solution.py:444
  36.3 11.6 %collective-permute-start.5 = (bf16[16,3840]{1,0:T(8,128)(2,1)S(1)}, bf16[16,3840]{1,0:T(8,128)(2,1)S(1)}, u32[]{:S(2)}, u32[]{:S(2)}) collective-permute-start(bf16[16,3840]{1,0:T(8,128)(2,1)S(1)} %get-tuple-element.45.refs_9_), channel_id=1, source_target_pairs={{0,8},{1,9},{2,10},{3,11},{4,12},{5,13},{6,14},{7,15},{8,16},{9,17... | collective-permute-start | bytes 368648 | tf_op jit(solution)/shard_map/ppermute | solution.py:457
  37.9 11.1 %collective-permute-start.6 = (bf16[16,3840]{1,0:T(8,128)(2,1)S(1)}, bf16[16,3840]{1,0:T(8,128)(2,1)S(1)}, u32[]{:S(2)}, u32[]{:S(2)}) collective-permute-start(bf16[16,3840]{1,0:T(8,128)(2,1)S(1)} %get-tuple-element.46), channel_id=1, source_target_pairs={{0,10},{1,11},{2,8},{3,9},{4,14},{5,15},{6,12},{7,13},{8,18},{9,19... | collective-permute-start | bytes 368648 | tf_op jit(solution)/shard_map/ppermute | solution.py:457
  40.1 10.5 %collective-permute-start.7 = (bf16[16,3840]{1,0:T(8,128)(2,1)S(1)}, bf16[16,3840]{1,0:T(8,128)(2,1)S(1)}, u32[]{:S(2)}, u32[]{:S(2)}) collective-permute-start(bf16[16,3840]{1,0:T(8,128)(2,1)S(1)} %get-tuple-element.47), channel_id=1, source_target_pairs={{0,12},{1,13},{2,14},{3,15},{4,8},{5,9},{6,10},{7,11},{8,20},{9,21... | collective-permute-start | bytes 368648 | tf_op jit(solution)/shard_map/ppermute | solution.py:457
  42.0 11.1 %collective-permute-start.8 = (bf16[16,3840]{1,0:T(8,128)(2,1)S(1)}, bf16[16,3840]{1,0:T(8,128)(2,1)S(1)}, u32[]{:S(2)}, u32[]{:S(2)}) collective-permute-start(bf16[16,3840]{1,0:T(8,128)(2,1)S(1)} %get-tuple-element.48), channel_id=1, source_target_pairs={{0,14},{1,15},{2,12},{3,13},{4,10},{5,11},{6,8},{7,9},{8,22},{9,23... | collective-permute-start | bytes 368648 | tf_op jit(solution)/shard_map/ppermute | solution.py:457
  44.2 10.3 %collective-permute-start.17 = (bf16[16,3840]{1,0:T(8,128)(2,1)S(1)}, bf16[16,3840]{1,0:T(8,128)(2,1)S(1)}, u32[]{:S(2)}, u32[]{:S(2)}) collective-permute-start(bf16[16,3840]{1,0:T(8,128)(2,1)S(1)} %get-tuple-element.60), channel_id=1, source_target_pairs={{0,24},{1,25},{2,26},{3,27},{4,28},{5,29},{6,30},{7,31},{8,0},{9,1... | collective-permute-start | bytes 368648 | tf_op jit(solution)/shard_map/ppermute | solution.py:457
  47.9 9.9 %collective-permute-start.18 = (bf16[16,3840]{1,0:T(8,128)(2,1)S(1)}, bf16[16,3840]{1,0:T(8,128)(2,1)S(1)}, u32[]{:S(2)}, u32[]{:S(2)}) collective-permute-start(bf16[16,3840]{1,0:T(8,128)(2,1)S(1)} %get-tuple-element.61), channel_id=1, source_target_pairs={{0,26},{1,27},{2,24},{3,25},{4,30},{5,31},{6,28},{7,29},{8,2},{9,3... | collective-permute-start | bytes 368648 | tf_op jit(solution)/shard_map/ppermute | solution.py:457
  49.0 11.8 %collective-permute-start.19 = (bf16[16,3840]{1,0:T(8,128)(2,1)S(1)}, bf16[16,3840]{1,0:T(8,128)(2,1)S(1)}, u32[]{:S(2)}, u32[]{:S(2)}) collective-permute-start(bf16[16,3840]{1,0:T(8,128)(2,1)S(1)} %get-tuple-element.62), channel_id=1, source_target_pairs={{0,28},{1,29},{2,30},{3,31},{4,24},{5,25},{6,26},{7,27},{8,4},{9,5... | collective-permute-start | bytes 368648 | tf_op jit(solution)/shard_map/ppermute | solution.py:457
  50.7 12.6 %collective-permute-start.20 = (bf16[16,3840]{1,0:T(8,128)(2,1)S(1)}, bf16[16,3840]{1,0:T(8,128)(2,1)S(1)}, u32[]{:S(2)}, u32[]{:S(2)}) collective-permute-start(bf16[16,3840]{1,0:T(8,128)(2,1)S(1)} %get-tuple-element.63), channel_id=1, source_target_pairs={{0,30},{1,31},{2,28},{3,29},{4,26},{5,27},{6,24},{7,25},{8,6},{9,7... | collective-permute-start | bytes 368648 | tf_op jit(solution)/shard_map/ppermute | solution.py:457

commit v3 on v2

v3 whole, which is shorter than its diff:
```python
import jax
import jax.numpy as jnp
from jax import lax
from jax.experimental import pallas as pl
from jax.experimental.pallas import tpu as pltpu
from jax.sharding import PartitionSpec as P

epsilon = 1e-06
route_scale = 2.5
fold = 256
none = 255.0
f32 = jnp.float32
bf16 = jnp.bfloat16
nt = (((1,), (1,)), ((), ()))
spaces = {
    "s": pl.BlockSpec(memory_space=pltpu.SMEM),
    "v": pl.BlockSpec(memory_space=pltpu.VMEM),
    "a": pl.BlockSpec(memory_space=pl.ANY),
    "h": pl.BlockSpec(memory_space=pltpu.HBM),
}


cost = {
    "backward_chunks": 10,
    "saved_rows": 40,
    "saved_terms": 40,
    "act_norms": 40,
    "act_gates": 40,
}


def call(body, places, outs, scratch, megabytes, name):
    def run(*arrays):
        arrays = [
            pltpu.with_memory_space_constraint(array, pltpu.HBM) if place == "h" else array
            for array, place in zip(arrays, places, strict=True)
        ]
        return kernel(*arrays)

    kernel = pl.pallas_call(
        body,
        out_shape=outs,
        in_specs=[spaces[place] for place in places],
        scratch_shapes=scratch,
        compiler_params=pltpu.CompilerParams(vmem_limit_bytes=megabytes * 1024 * 1024),
        cost_estimate=pl.CostEstimate(
            flops=int(cost.get(name, 0.1) * 1e9), bytes_accessed=1000, transcendentals=0
        ),
        name=name,
    )
    return run


def shape(dims, kind=bf16):
    return jax.ShapeDtypeStruct(dims, kind)


class Sizes:
    def __init__(self, groups, experts, tokens, width):
        self.experts = experts
        self.split = groups // experts
        self.tokens = tokens
        self.width = width
        self.main = tokens // experts
        self.cap = self.main + 1
        self.pieces = width // fold
        self.wide = width + fold
        self.rows = tokens + 16
        assert self.main == 16 and self.pieces <= 14 and width % fold == 0
        assert experts <= 8 and experts & (experts - 1) == 0 and self.split & (self.split - 1) == 0


def pack_last(row, tile, first=0):
    for i in range(row.shape[1] // fold):
        tile[first + i : first + i + 1, :] = row[:, i * fold : (i + 1) * fold]


def unpack_last(chunk, z, tile, target, at, base=0):
    tile[...] = chunk[base : base + 16, z.width :].astype(f32)
    for i in range(z.pieces):
        target[at : at + 1, i * fold : (i + 1) * fold] = tile[i : i + 1, :]


def slot_matrices(ids_row, block, z):
    tokens = z.tokens
    sub = lax.broadcasted_iota(jnp.int32, (tokens, tokens), 0)
    lane = lax.broadcasted_iota(jnp.int32, (tokens, tokens), 1)
    row = jnp.bitwise_xor(ids_row, block)
    column = jnp.sum(jnp.where(sub == lane, row, 0), axis=1, keepdims=True)
    same = column == row
    place_row = jnp.sum(jnp.where(same & (sub < lane), 1, 0), axis=0, keepdims=True)
    place_column = jnp.sum(jnp.where(same & (lane < sub), 1, 0), axis=1, keepdims=True)

    def slot(expert, place):
        return jnp.where(place < z.main, expert * z.main + place, tokens + expert)

    slot_row = slot(row, place_row)
    slot_column = slot(column, place_column)
    by_slot = lax.broadcasted_iota(jnp.int32, (z.rows, tokens), 0) == slot_row
    by_token = lax.broadcasted_iota(jnp.int32, (tokens, fold), 1) == slot_column
    token = lax.broadcasted_iota(jnp.int32, (tokens, fold), 0).astype(f32)
    token_row = jnp.sum(jnp.where(by_token, token - none, 0.0), axis=0, keepdims=True) + none
    return jnp.where(by_slot, 1.0, 0.0).astype(bf16), token_row


def write_chunks(z, selector, token_row, rows_ref, ready, tiles, chunks, base):
    step = z.width // 2
    tiles[...] = jnp.zeros_like(tiles)
    for half in range(2):
        ready[half].wait()
        col = half * step
        got = jnp.dot(selector, rows_ref[:, col : col + step], preferred_element_type=f32)
        packed = got[: z.tokens].astype(bf16)
        for k in range(z.experts):
            chunks[k][base : base + 16, col : col + step] = packed[k * z.main : (k + 1) * z.main]
            pack_last(got[z.tokens + k : z.tokens + k + 1], tiles.at[k], half * z.pieces // 2)
    for k in range(z.experts):
        tiles[k, z.pieces : z.pieces + 1, :] = token_row
        chunks[k][base : base + 16, z.width :] = tiles[k].astype(bf16)


def make_chunks(z, where, ids, sources, tables, after, name):
    count = len(sources)

    def body(where, ids_any, *refs):
        anys, tables_any = refs[:count], refs[count : count + len(tables)]
        outs, held = refs[count + len(tables) + len(after) :], ()
        if tables:
            *outs, gain_ref, router_ref, ids, rows, tiles, sems = outs
            *outs, vectors = outs
            held = (gain_ref, router_ref)
        else:
            *outs, ids, rows, tiles, sems = outs
        copies = [pltpu.make_async_copy(ids_any, ids, sems.at[2 * count])]
        step = z.width // 2
        for j in range(count):
            for half in range(2):
                cols = pl.ds(half * step, step)
                copies.append(
                    pltpu.make_async_copy(
                        anys[j].at[:, cols], rows.at[j, :, cols], sems.at[2 * j + half]
                    )
                )
        for i, (source, target) in enumerate(zip(tables_any, held)):
            copies.append(pltpu.make_async_copy(source, target, sems.at[2 * count + 1 + i]))
        for copy in copies:
            copy.start()
        copies[0].wait()
        selector, token_row = slot_matrices(ids[...], where[0], z)
        for j in range(count):
            ready = copies[1 + 2 * j : 3 + 2 * j]
            write_chunks(z, selector, token_row, rows.at[j], ready, tiles, outs, 16 * j)
        if tables:
            for copy in copies[1 + 2 * count :]:
                copy.wait()
            vectors[...] = jnp.zeros_like(vectors)
            vectors[0:1, :] = gain_ref[...].astype(f32)
            mine = lax.broadcasted_iota(jnp.int32, (z.experts, 1), 0) == where[0]
            table = jnp.where(mine, router_ref[0].astype(f32), 0.0)
            vectors[1:2, :] = jnp.sum(table, axis=0, keepdims=True)

    return call(
        body,
        "sh" + "h" * (count + len(tables)) + "a" * len(after),
        [shape((z.main * count, z.wide))] * z.experts
        + [shape((8, z.width), f32) for _ in tables[:1]],
        [pltpu.VMEM(table.shape, bf16) for table in tables]
        + [
            pltpu.VMEM((1, z.tokens), jnp.int32),
            pltpu.VMEM((count, z.tokens, z.width), bf16),
            pltpu.VMEM((z.experts, 16, fold), f32),
            pltpu.SemaphoreType.DMA((2 * count + 1 + len(tables),)),
        ],
        8,
        name,
    )(where, ids.reshape(1, z.tokens), *sources, *tables, *after)


def collect_rows(z, chunks, last, tile, base=0):
    last[...] = jnp.zeros_like(last)
    for k in range(z.experts):
        unpack_last(chunks[k], z, tile, last, k, base)


def norm_rows(h, gain):
    inv = lax.rsqrt(jnp.mean(h * h, axis=-1, keepdims=True) + epsilon)
    return (h * inv * gain).astype(bf16), inv


def normed_rows(z, chunks, vectors):
    def body(*refs):
        chunks, (vectors, normed_ref, gates_ref, last, tile) = refs[: z.experts], refs[z.experts :]
        gain, router = vectors[0:1, :], vectors[1:2, :]
        collect_rows(z, chunks, last, tile)
        for k in range(z.experts + 1):
            h = last[...] if k == z.experts else chunks[k][:, : z.width].astype(f32)
            at = k * z.main
            normed, _ = norm_rows(h, gain)
            normed_ref[at : at + 16, :] = normed
            logits = jnp.sum(normed.astype(f32) * router, axis=-1, keepdims=True)
            gates_ref[at : at + 16, :] = jnp.broadcast_to(jax.nn.sigmoid(logits), (16, 128))

    return call(
        body,
        "v" * (z.experts + 1),
        [shape((z.rows, z.width)), shape((z.rows, 128), f32), shape((16, z.width), f32)],
        [pltpu.VMEM((16, fold), f32)],
        8,
        "normed_rows",
    )(*chunks, vectors)


def grad_rows_of(z, chunks, after):
    def body(*refs):
        chunks, (rows, last, tile) = refs[: z.experts], refs[z.experts + len(after) :]
        for k in range(z.experts):
            rows[k * z.main : (k + 1) * z.main, :] = chunks[k][:16, : z.width]
        collect_rows(z, chunks, last, tile)
        rows[z.tokens :, :] = last[...].astype(bf16)

    return call(
        body,
        "v" * z.experts + "a" * len(after),
        [shape((z.rows, z.width)), shape((16, z.width), f32)],
        [pltpu.VMEM((16, fold), f32)],
        8,
        "grad_rows",
    )(*chunks, *after)


def act_norms(z, chunks, after):
    def body(*refs):
        chunks, (inv_ref, last, tile) = refs[: z.experts], refs[z.experts + len(after) :]
        collect_rows(z, chunks, last, tile, 16)
        for k in range(z.experts + 1):
            h = last[...] if k == z.experts else chunks[k][16:32, : z.width].astype(f32)
            at = k * z.main
            inv = lax.rsqrt(jnp.mean(h * h, axis=-1, keepdims=True) + epsilon)
            inv_ref[at : at + 16, :] = jnp.broadcast_to(inv, (16, 128))

    return call(
        body,
        "v" * z.experts + "a" * len(after),
        [shape((z.rows, 128), f32), shape((16, z.width), f32)],
        [pltpu.VMEM((16, fold), f32)],
        8,
        "act_norms",
    )(*chunks, *after)


def act_gates(z, chunks, last, inv, vectors, after):
    def body(*refs):
        chunks, (last, inv_ref, vectors) = refs[: z.experts], refs[z.experts : z.experts + 3]
        affinity_ref = refs[-1]
        gain, router = vectors[0:1, :], vectors[1:2, :]
        for k in range(z.experts + 1):
            h = last[...] if k == z.experts else chunks[k][16:32, : z.width].astype(f32)
            at = k * z.main
            normed = (h * inv_ref[at : at + 16, 0:1] * gain).astype(bf16).astype(f32)
            logits = jnp.sum(normed * router, axis=-1, keepdims=True)
            affinity_ref[at : at + 16, :] = jnp.broadcast_to(jax.nn.sigmoid(logits), (16, 128))

    return call(
        body,
        "v" * (z.experts + 3) + "a" * len(after),
        shape((z.rows, 128), f32),
        [],
        8,
        "act_gates",
    )(*chunks, last, inv, vectors, *after)


def write_parts(z, values, outs, col):
    values = values.astype(bf16)
    for m in range(z.split):
        outs[m][:, col : col + values.shape[1]] = values[m * z.rows : (m + 1) * z.rows]


def experts_forward(z, rows, w_gate, w_down, after):
    def body(*refs):
        rows, (gate_ref, down_ref), outs = (
            refs[: z.split],
            refs[z.split : z.split + 2],
            refs[z.split + 2 + len(after) :],
        )
        held = jnp.concatenate([part[...] for part in rows], axis=0)
        gate_proj = jnp.dot(held, gate_ref[0], preferred_element_type=f32)
        hidden = jax.nn.silu(gate_proj).astype(bf16)
        step = 512
        for col in range(0, z.width, step):
            part = jnp.dot(hidden, down_ref[0, :, col : col + step], preferred_element_type=f32)
            write_parts(z, part, outs, col)

    return call(
        body,
        "v" * (z.split + 2) + "a" * len(after),
        [shape((z.rows, z.width))] * z.split,
        [],
        16,
        "experts_forward",
    )(*rows, w_gate, w_down, *after)


def saved_rows(z, where, saved, weights, after):
    total, slots, width = z.split * z.rows, saved.shape[2], saved.shape[3]

    def body(where, saved_any, *refs):
        ordered_ref, saved_ref, sem = refs[len(weights) + len(after) :]
        copy = pltpu.make_async_copy(saved_any.at[0, 0], saved_ref, sem)
        copy.start()
        row = lax.broadcasted_iota(jnp.int32, (total, slots), 0)
        slot = lax.broadcasted_iota(jnp.int32, (total, slots), 1)
        m, at = row // z.rows, row % z.rows
        is_main = at < z.tokens
        k = jnp.where(is_main, at // z.main, at - z.tokens)
        p = jnp.where(is_main, at % z.main, z.main)
        source = jnp.bitwise_xor(k, where[0]) * z.split + jnp.bitwise_xor(m, where[1])
        wanted = jnp.where(k < z.experts, source * z.cap + p, -1)
        selector = jnp.where(slot == wanted, 1.0, 0.0).astype(bf16)
        copy.wait()
        ordered_ref[...] = jnp.dot(selector, saved_ref[...], preferred_element_type=f32)

    return call(
        body,
        "sh" + "v" * len(weights) + "a" * len(after),
        shape((total, width), f32),
        [pltpu.VMEM((slots, width), bf16), pltpu.SemaphoreType.DMA],
        8,
        "saved_rows",
    )(where, saved, *weights, *after)


def saved_terms(z, ordered, after):
    def body(ordered_ref, *refs):
        hidden_ref, slope_ref = refs[len(after) :]
        gate_proj = ordered_ref[...]
        sg = jax.nn.sigmoid(gate_proj)
        hidden_ref[...] = (gate_proj * sg).astype(bf16)
        slope_ref[...] = sg * (1.0 + gate_proj * (1.0 - sg))

    return call(
        body,
        "v" + "a" * len(after),
        [shape(ordered.shape), shape(ordered.shape, f32)],
        [],
        8,
        "saved_terms",
    )(ordered, *after)


def experts_backward(z, rows, hidden, slope, w_gate, w_down, after):
    def body(*refs):
        rows = refs[: z.split]
        hidden_ref, slope_ref, gate_ref, down_ref = refs[z.split : z.split + 4]
        outs = refs[z.split + 4 + len(after) :]
        held = jnp.concatenate([part[...] for part in rows], axis=0)
        grad_hidden = lax.dot_general(held, down_ref[0], nt, preferred_element_type=f32)
        dots = jnp.sum(grad_hidden * hidden_ref[...].astype(f32), axis=-1, keepdims=True)
        grad_gate = (grad_hidden * slope_ref[...]).astype(bf16)
        step = 512
        for col in range(0, z.width, step):
            part = lax.dot_general(
                grad_gate, gate_ref[0, col : col + step, :], nt, preferred_element_type=f32
            )
            write_parts(z, part, outs, col)
        write_parts(z, jnp.broadcast_to(dots, (dots.shape[0], 128)), outs, z.width)

    return call(
        body,
        "v" * (z.split + 4) + "a" * len(after),
        [shape((z.rows, z.width + 128))] * z.split,
        [],
        16,
        "experts_backward",
    )(*rows, hidden, slope, w_gate, w_down, *after)


def put_last(z, values, source_chunk, tile, out):
    tile[...] = jnp.zeros_like(tile)
    pack_last(values, tile)
    tokens = source_chunk[:16, z.width :].astype(f32)
    tile[z.pieces : z.pieces + 1, :] = tokens[z.pieces : z.pieces + 1, :]
    out[:, z.width :] = tile[...].astype(bf16)


def finish_forward(z, chunks, last, parts, gates, after):
    def body(*refs):
        e = z.experts
        chunks, last, parts = refs[:e], refs[e], refs[e + 1 : e + 1 + z.split]
        gates, outs, (tile,) = refs[e + 1 + z.split], refs[-1 - e : -1], refs[-1:]

        def mixed(at):
            y = parts[0][at : at + 16, :].astype(f32)
            for part in parts[1:]:
                y = y + part[at : at + 16, :].astype(f32)
            return route_scale * (gates[at : at + 16, 0:1] * y)

        tail = last[...] + mixed(z.tokens)
        for k in range(e):
            h = chunks[k][:, : z.width].astype(f32)
            outs[k][:, : z.width] = (h + mixed(k * z.main)).astype(bf16)
            put_last(z, tail[k : k + 1, :], chunks[k], tile, outs[k])

    return call(
        body,
        "v" * (z.experts + z.split + 2) + "a" * len(after),
        [shape((z.main, z.wide))] * z.experts,
        [pltpu.VMEM((16, fold), f32)],
        8,
        "finish_forward",
    )(*chunks, last, *parts, gates, *after)


def finish_backward(z, chunks, lasts, terms, parts, vectors):
    def body(*refs):
        e = z.experts
        chunks, (last_grad, last_act, inv_ref, affinity_ref) = refs[:e], refs[e : e + 4]
        parts, vectors = refs[e + 4 : e + 4 + z.split], refs[e + 4 + z.split]
        outs, (tile,) = refs[-1 - e : -1], refs[-1:]
        gain, router = vectors[0:1, :], vectors[1:2, :]

        def finished(h, g, at):
            inv, affinity = inv_ref[at : at + 16, 0:1], affinity_ref[at : at + 16, 0:1]
            rows = parts[0][at : at + 16, : z.width].astype(f32)
            dot = parts[0][at : at + 16, z.width :].astype(f32)
            for part in parts[1:]:
                rows = rows + part[at : at + 16, : z.width].astype(f32)
                dot = dot + part[at : at + 16, z.width :].astype(f32)
            dot = dot[:, 0:1]
            grad_logits = (route_scale * dot * affinity * (1.0 - affinity)).astype(bf16).astype(f32)
            grad_pre = (route_scale * affinity * rows + grad_logits * router) * gain
            centre = jnp.mean(grad_pre * h, axis=-1, keepdims=True)
            return g + inv * (grad_pre - h * (inv * inv * centre))

        tail = finished(last_act[...], last_grad[...], z.tokens)
        for k in range(e):
            g = chunks[k][:16, : z.width].astype(f32)
            h = chunks[k][16:32, : z.width].astype(f32)
            outs[k][:, : z.width] = finished(h, g, k * z.main).astype(bf16)
            put_last(z, tail[k : k + 1, :], chunks[k], tile, outs[k])

    return call(
        body,
        "v" * (z.experts + z.split + 5),
        [shape((z.main, z.wide))] * z.experts,
        [pltpu.VMEM((16, fold), f32)],
        8,
        "finish_backward",
    )(*chunks, *lasts, *terms, *parts, vectors)


def order_rows(z, chunks, name):
    def body(*refs):
        chunks, (out, held, last, tile) = refs[: z.experts], refs[z.experts :]
        for k in range(z.experts):
            held[k * z.main : (k + 1) * z.main, :] = chunks[k][:, : z.width]
        collect_rows(z, chunks, last, tile)
        held[z.tokens :, :] = last[...].astype(bf16)
        token_row = chunks[0][:, z.width :].astype(f32)[z.pieces : z.pieces + 1, : z.rows]
        token = lax.broadcasted_iota(jnp.int32, (z.tokens, z.rows), 0).astype(f32)
        selector = jnp.where(token == token_row, 1.0, 0.0).astype(bf16)
        out[...] = jnp.dot(selector, held[...], preferred_element_type=f32).astype(bf16)

    return call(
        body,
        "v" * z.experts,
        shape((z.tokens, z.width)),
        [
            pltpu.VMEM((z.rows, z.width), bf16),
            pltpu.VMEM((16, z.width), f32),
            pltpu.VMEM((16, fold), f32),
        ],
        8,
        name,
    )(*chunks)


def dispatch(z, chunks):
    groups = z.experts * z.split
    got = [chunks[0]] + [None] * (z.experts - 1)
    for k in reversed(range(1, z.experts)):
        pairs = [(i, ((i // z.split) ^ k) * z.split + i % z.split) for i in range(groups)]
        got[k] = lax.ppermute(chunks[k], "ep", pairs)
    return got


def to_core(z, array, m):
    groups = z.experts * z.split
    pairs = [(i, i // z.split * z.split + ((i % z.split) ^ m)) for i in range(groups)]
    return lax.ppermute(array, "ep", pairs)


def to_section(z, chunks, by):
    groups = z.experts * z.split
    sections = lax.axis_size("pp")
    got = [None] * z.experts
    for k in reversed(range(z.experts)):
        pairs = [
            (s * groups + i, (s + by) % sections * groups + ((i // z.split) ^ k) * z.split + i % z.split)
            for s in range(sections)
            for i in range(groups)
        ]
        got[k] = lax.ppermute(chunks[k], ("pp", "ep"), pairs)
    return got


def on_device(
    fwd_act, fwd_ids, bwd_act, bwd_ids, bwd_grad, norm_gain, router, w_gate, w_down, saved_gate
):
    groups = lax.axis_size("ep")
    assert fwd_ids.shape[1] == 1
    z = Sizes(groups, router.shape[2], fwd_act.shape[0], fwd_act.shape[1])
    index = lax.axis_index("ep")
    where = jnp.stack([index // z.split, index % z.split]).astype(jnp.int32)
    router = jnp.swapaxes(router, 1, 2)
    others = range(1, z.split)

    fwd_chunks = make_chunks(z, where, fwd_ids, [fwd_act], [], [], "forward_chunks")
    fwd_own = dispatch(z, fwd_chunks)
    *bwd_chunks, vectors = make_chunks(
        z,
        where,
        bwd_ids,
        [bwd_grad, bwd_act],
        [norm_gain, router],
        [fwd_chunks[0]],
        "backward_chunks",
    )
    bwd_own = dispatch(z, bwd_chunks)

    normed, gates, fwd_last = normed_rows(z, fwd_own, vectors)
    fwd_all = [normed] + [to_core(z, normed, m) for m in others]
    ordered = saved_rows(z, where, saved_gate, [w_gate, w_down], [gates])
    fwd_parts = experts_forward(z, fwd_all, w_gate, w_down, [ordered])
    hidden, slope = saved_terms(z, ordered, [fwd_parts[0]])
    fwd_parts = [fwd_parts[0]] + [to_core(z, fwd_parts[m], m) for m in others]
    fwd_out = finish_forward(z, fwd_own, fwd_last, fwd_parts, gates, [hidden])
    fwd_done = to_section(z, fwd_out, 1)

    grads, grad_last = grad_rows_of(z, bwd_own, [fwd_out[0]])
    grad_all = [grads] + [to_core(z, grads, m) for m in others]
    inv, act_last = act_norms(z, bwd_own, [grads])
    bwd_parts = experts_backward(z, grad_all, hidden, slope, w_gate, w_down, [inv])
    affinity = act_gates(z, bwd_own, act_last, inv, vectors, [bwd_parts[0]])
    bwd_parts = [bwd_parts[0]] + [to_core(z, bwd_parts[m], m) for m in others]
    bwd_out = finish_backward(
        z, bwd_own, [grad_last, act_last], [inv, affinity], bwd_parts, vectors
    )
    bwd_done = to_section(z, bwd_out, -1)
    return (order_rows(z, fwd_done, "forward_rows"), order_rows(z, bwd_done, "backward_rows"))


def solution(mesh):
    return jax.shard_map(
        on_device,
        mesh=mesh,
        in_specs=(
            P(("pp", "ep"), None),
            P(("pp", "ep"), None),
            P(("pp", "ep"), None),
            P(("pp", "ep"), None),
            P(("pp", "ep"), None),
            P("pp", None),
            P("pp", None, None),
            P(("pp", "ep"), None, None),
            P(("pp", "ep"), None, None),
            P("pp", "ep", None, None),
        ),
        out_specs=(P(("pp", "ep"), None), P(("pp", "ep"), None)),
        check_vma=False,
    )
```

time: 64.5 us -> 52 us (0.81)
  waiting for transfers between devices: 20.7 us -> 13.3 us
  starting transfers between devices: 26.4 us -> 22.6 us
  Pallas kernels: 16.3 us -> 15.1 us
    ppermute x9 -> x6, waiting for transfers between devices: 10.5 us -> 0.02 us  [dispatch(): got[k] = lax.ppermute(chunks[k], 'ep', pairs)]
    ppermute x4, waiting for transfers between devices: 0.01 us -> 5.2 us  [to_core(): return lax.ppermute(array, 'ep', pairs)]
    ppermute x9 -> x6, starting transfers between devices: 11.7 us -> 8.1 us  [dispatch(): got[k] = lax.ppermute(chunks[k], 'ep', pairs)]
    ppermute x8, waiting for transfers between devices: 10.2 us -> 8.08 us  [to_section(): got[k] = lax.ppermute(chunks[k], ('pp', 'ep'), pairs)]
    pallas_call x11 -> x14, Pallas kernels: 16.3 us -> 15.1 us  [run(): return kernel(*arrays)]
  transfers between devices with their start and end apart: 21 -> 18, of which waited for: 11 -> 7; matrix products, arithmetic and copies ran while one was open for 0% -> 0% of each run, Pallas kernels for 16% -> 23%
where the time goes in v3:
time: 52 us; the launch traced here: 51.8 us
  starting transfers between devices  22.6 us (43%)
  Pallas kernels  15.1 us (29%)
  waiting for transfers between devices  13.3 us (26%)
  between operations  0.75 us (1%)
    pallas_call x14, Pallas kernels, run(): return kernel(*arrays)  15.1 us
    ppermute x8, starting transfers between devices, to_section(): got[k] = lax.ppermute(chunks[k], ('pp', 'ep'), pairs)  14 us
    ppermute x6, starting transfers between devices, dispatch(): got[k] = lax.ppermute(chunks[k], 'ep', pairs)  8.1 us
    ppermute x8, waiting for transfers between devices, to_section(): got[k] = lax.ppermute(chunks[k], ('pp', 'ep'), pairs)  8.08 us
    ppermute x4, waiting for transfers between devices, to_core(): return lax.ppermute(array, 'ep', pairs)  5.2 us
  transfers between devices with their start and end apart: 18, of which 7 were waited for; matrix products, arithmetic and copies ran while one was open for 0% of the time, Pallas kernels for 23%

profile of v3, /device:TPU:0, one launch (start us, length us, event | category | flops | bytes accessed | tf_op | source)
XLA Modules:
  0.0 51.8 jit_solution(15435153941031860444)
XLA Ops:
  0.7 2.0 %forward_chunks.1 = (bf16[16,3840]{1,0:T(8,128)(2,1)S(1)}, bf16[16,3840]{1,0:T(8,128)(2,1)S(1)}, bf16[16,3840]{1,0:T(8,128)(2,1)S(1)}, bf16[16,3840]{1,0:T(8,128)(2,1)S(1)}) custom-call(s32[2]{0:T(128)S(1)} %pad_add_fusion.where, s32[1,64]{1,0:T(1,128)} %bitcast.5, bf16[64,3584]{1,0:T(8,128)(2,1)} %refs_0_.3), custom_call_target="tpu_custom_call" | custom-call | flops 100000000 | bytes 1000 | tf_op jit(solution)/shard_map/forward_chunks/pallas_call | solution.py:38
  2.7 3.0 %collective-permute-start = (bf16[16,3840]{1,0:T(8,128)(2,1)S(1)}, bf16[16,3840]{1,0:T(8,128)(2,1)S(1)}, u32[]{:S(2)}, u32[]{:S(2)}) collective-permute-start(bf16[16,3840]{1,0:T(8,128)(2,1)S(1)} %get-tuple-element.33), channel_id=1, source_target_pairs={{0,2},{1,3},{2,0},{3,1},{4,6},{5,7},{6,4},{7,5},{8,10},{9,11},{10,... | collective-permute-start | bytes 368648 | tf_op jit(solution)/shard_map/ppermute | solution.py:483
  5.7 1.5 %collective-permute-start.1 = (bf16[16,3840]{1,0:T(8,128)(2,1)S(1)}, bf16[16,3840]{1,0:T(8,128)(2,1)S(1)}, u32[]{:S(2)}, u32[]{:S(2)}) collective-permute-start(bf16[16,3840]{1,0:T(8,128)(2,1)S(1)} %get-tuple-element.34), channel_id=1, source_target_pairs={{0,4},{1,5},{2,6},{3,7},{4,0},{5,1},{6,2},{7,3},{8,12},{9,13},{10,... | collective-permute-start | bytes 368648 | tf_op jit(solution)/shard_map/ppermute | solution.py:483
  7.3 2.8 %backward_chunks.1 = (bf16[32,3840]{1,0:T(8,128)(2,1)S(1)}, bf16[32,3840]{1,0:T(8,128)(2,1)S(1)}, bf16[32,3840]{1,0:T(8,128)(2,1)S(1)}, bf16[32,3840]{1,0:T(8,128)(2,1)S(1)}, f32[8,3584]{1,0:T(8,128)S(1)}) custom-call(s32[2]{0:T(128)S(1)} %pad_add_fusion.where, s32[1,64]{1,0:T(1,128)} %bitcast.7, bf16[64,3584]{1,0:T(8,128)(2,1)} %refs_0_.4, ...), custom_call_target="tpu_custom_call" | custom-call | flops 10000000000 | bytes 1000 | tf_op jit(solution)/shard_map/backward_chunks/pallas_call | solution.py:38
  10.1 2.0 %collective-permute-start.9 = (bf16[32,3840]{1,0:T(8,128)(2,1)S(1)}, bf16[32,3840]{1,0:T(8,128)(2,1)S(1)}, u32[]{:S(2)}, u32[]{:S(2)}) collective-permute-start(bf16[32,3840]{1,0:T(8,128)(2,1)S(1)} %get-tuple-element.48), channel_id=1, source_target_pairs={{0,2},{1,3},{2,0},{3,1},{4,6},{5,7},{6,4},{7,5},{8,10},{9,11},{10,... | collective-permute-start | bytes 737288 | tf_op jit(solution)/shard_map/ppermute | solution.py:483
  12.1 1.5 %collective-permute-start.10 = (bf16[32,3840]{1,0:T(8,128)(2,1)S(1)}, bf16[32,3840]{1,0:T(8,128)(2,1)S(1)}, u32[]{:S(2)}, u32[]{:S(2)}) collective-permute-start(bf16[32,3840]{1,0:T(8,128)(2,1)S(1)} %get-tuple-element.49), channel_id=1, source_target_pairs={{0,4},{1,5},{2,6},{3,7},{4,0},{5,1},{6,2},{7,3},{8,12},{9,13},{10,... | collective-permute-start | bytes 737288 | tf_op jit(solution)/shard_map/ppermute | solution.py:483
  13.6 0.5 normed_rows.1
  14.2 1.6 %saved_rows.1.refs_4_.ordered_ref = f32[160,512]{1,0:T(8,128)S(1)} custom-call(s32[2]{0:T(128)S(1)} %pad_add_fusion.where, bf16[1,1,136,512]{3,2,1,0:T(8,128)(2,1)} %saved_any.1, bf16[1,3584,512]{2,1,0:T(8,128)(2,1)S(1)} %copy-done, bf16[1,512,3584]{2,1,0:T(8,128)(2,1)S(1)} %copy-done.1, f32[80,128]{1,0:T(8,128)S(1)} %get-tuple-element.39.refs_2_.refs_7_), custom_call_target="tpu_custom_call" | custom-call | flops 40000000000 | bytes 1000 | tf_op jit(solution)/shard_map/saved_rows/pallas_call | solution.py:38
  15.9 0.3 collective-permute-done.3.refs_1_
  16.2 1.5 %experts_forward.1 = (bf16[80,3584]{1,0:T(8,128)(2,1)S(1)}, bf16[80,3584]{1,0:T(8,128)(2,1)S(1)}) custom-call(bf16[80,3584]{1,0:T(8,128)(2,1)S(1)} %get-tuple-element.38.refs_0_, bf16[80,3584]{1,0:T(8,128)(2,1)S(1)} %collective-permute-done.3.refs_1_, bf16[1,3584,512]{2,1,0:T(8,128)(2,1)S(1)} %copy-done, bf16[1,512,3584]{2,1,0:T(8,128)(2,1)S(1)} %copy-done.1, ...), custom_call_target="tpu_custom_call" | custom-call | flops 100000000 | bytes 1000 | tf_op jit(solution)/shard_map/experts_forward/pallas_call | solution.py:38
  17.6 0.3 collective-permute-start.4
  18.0 1.7 %collective-permute-done.4.refs_6_ = bf16[80,3584]{1,0:T(8,128)(2,1)S(1)} collective-permute-done((bf16[80,3584]{1,0:T(8,128)(2,1)S(1)}, bf16[80,3584]{1,0:T(8,128)(2,1)S(1)}, u32[]{:S(2)}, u32[]{:S(2)}) %collective-permute-start.4) | collective-permute-done | bytes 573472 | tf_op jit(solution)/shard_map/ppermute | solution.py:490
  19.7 0.4 finish_forward.1
  20.1 3.0 %collective-permute-start.6 = (bf16[16,3840]{1,0:T(8,128)(2,1)S(1)}, bf16[16,3840]{1,0:T(8,128)(2,1)S(1)}, u32[]{:S(2)}, u32[]{:S(2)}) collective-permute-start(bf16[16,3840]{1,0:T(8,128)(2,1)S(1)} %get-tuple-element.44), channel_id=1, source_target_pairs={{0,10},{1,11},{2,8},{3,9},{4,14},{5,15},{6,12},{7,13},{8,18},{9,19... | collective-permute-start | bytes 368648 | tf_op jit(solution)/shard_map/ppermute | solution.py:503
  23.1 2.5 %collective-permute-start.7 = (bf16[16,3840]{1,0:T(8,128)(2,1)S(1)}, bf16[16,3840]{1,0:T(8,128)(2,1)S(1)}, u32[]{:S(2)}, u32[]{:S(2)}) collective-permute-start(bf16[16,3840]{1,0:T(8,128)(2,1)S(1)} %get-tuple-element.45), channel_id=1, source_target_pairs={{0,12},{1,13},{2,14},{3,15},{4,8},{5,9},{6,10},{7,11},{8,20},{9,21... | collective-permute-start | bytes 368648 | tf_op jit(solution)/shard_map/ppermute | solution.py:503
  25.6 1.5 %collective-permute-start.8 = (bf16[16,3840]{1,0:T(8,128)(2,1)S(1)}, bf16[16,3840]{1,0:T(8,128)(2,1)S(1)}, u32[]{:S(2)}, u32[]{:S(2)}) collective-permute-start(bf16[16,3840]{1,0:T(8,128)(2,1)S(1)} %get-tuple-element.46), channel_id=1, source_target_pairs={{0,14},{1,15},{2,12},{3,13},{4,10},{5,11},{6,8},{7,9},{8,22},{9,23... | collective-permute-start | bytes 368648 | tf_op jit(solution)/shard_map/ppermute | solution.py:503
  27.4 0.2 act_norms.1
  27.7 1.7 %collective-permute-done.12.refs_1_ = bf16[80,3584]{1,0:T(8,128)(2,1)S(1)} collective-permute-done((bf16[80,3584]{1,0:T(8,128)(2,1)S(1)}, bf16[80,3584]{1,0:T(8,128)(2,1)S(1)}, u32[]{:S(2)}, u32[]{:S(2)}) %collective-permute-start.12) | collective-permute-done | bytes 573472 | tf_op jit(solution)/shard_map/ppermute | solution.py:490
  29.4 2.6 %experts_backward.1 = (bf16[80,3712]{1,0:T(8,128)(2,1)S(1)}, bf16[80,3712]{1,0:T(8,128)(2,1)S(1)}) custom-call(bf16[80,3584]{1,0:T(8,128)(2,1)S(1)} %get-tuple-element.52.refs_4_.refs_0_, bf16[80,3584]{1,0:T(8,128)(2,1)S(1)} %collective-permute-done.12.refs_1_, bf16[160,512]{1,0:T(8,128)(2,1)S(1)} %get-tuple-element.42.refs_8_.refs_2_, ...), custom_call_target="tpu_custom_call" | custom-call | flops 100000000 | bytes 1000 | tf_op jit(solution)/shard_map/experts_backward/pallas_call | solution.py:38
  32.0 0.2 collective-permute-start.13
  32.2 0.4 act_gates.1.refs_7_
  32.6 1.5 %collective-permute-done.13.refs_9_ = bf16[80,3712]{1,0:T(8,128)(2,1)S(1)} collective-permute-done((bf16[80,3712]{1,0:T(8,128)(2,1)S(1)}, bf16[80,3712]{1,0:T(8,128)(2,1)S(1)}, u32[]{:S(2)}, u32[]{:S(2)}) %collective-permute-start.13) | collective-permute-done | bytes 593952 | tf_op jit(solution)/shard_map/ppermute | solution.py:490
  34.1 0.7 %finish_backward.1 = (bf16[16,3840]{1,0:T(8,128)(2,1)S(1)}, bf16[16,3840]{1,0:T(8,128)(2,1)S(1)}, bf16[16,3840]{1,0:T(8,128)(2,1)S(1)}, bf16[16,3840]{1,0:T(8,128)(2,1)S(1)}) custom-call(bf16[32,3840]{1,0:T(8,128)(2,1)S(1)} %get-tuple-element.47.refs_0_, bf16[32,3840]{1,0:T(8,128)(2,1)S(1)} %collective-permute-done.9.refs_1_, ...), custom_call_target="tpu_custom_call" | custom-call | flops 100000000 | bytes 1000 | tf_op jit(solution)/shard_map/finish_backward/pallas_call | solution.py:38
  34.8 3.7 %collective-permute-start.14 = (bf16[16,3840]{1,0:T(8,128)(2,1)S(1)}, bf16[16,3840]{1,0:T(8,128)(2,1)S(1)}, u32[]{:S(2)}, u32[]{:S(2)}) collective-permute-start(bf16[16,3840]{1,0:T(8,128)(2,1)S(1)} %get-tuple-element.58), channel_id=1, source_target_pairs={{0,24},{1,25},{2,26},{3,27},{4,28},{5,29},{6,30},{7,31},{8,0},{9,1... | collective-permute-start | bytes 368648 | tf_op jit(solution)/shard_map/ppermute | solution.py:503
  38.5 1.4 %collective-permute-start.15 = (bf16[16,3840]{1,0:T(8,128)(2,1)S(1)}, bf16[16,3840]{1,0:T(8,128)(2,1)S(1)}, u32[]{:S(2)}, u32[]{:S(2)}) collective-permute-start(bf16[16,3840]{1,0:T(8,128)(2,1)S(1)} %get-tuple-element.59), channel_id=1, source_target_pairs={{0,26},{1,27},{2,24},{3,25},{4,30},{5,31},{6,28},{7,29},{8,2},{9,3... | collective-permute-start | bytes 368648 | tf_op jit(solution)/shard_map/ppermute | solution.py:503
  39.9 1.4 %collective-permute-start.16 = (bf16[16,3840]{1,0:T(8,128)(2,1)S(1)}, bf16[16,3840]{1,0:T(8,128)(2,1)S(1)}, u32[]{:S(2)}, u32[]{:S(2)}) collective-permute-start(bf16[16,3840]{1,0:T(8,128)(2,1)S(1)} %get-tuple-element.60), channel_id=1, source_target_pairs={{0,28},{1,29},{2,30},{3,31},{4,24},{5,25},{6,26},{7,27},{8,4},{9,5... | collective-permute-start | bytes 368648 | tf_op jit(solution)/shard_map/ppermute | solution.py:503
  41.3 0.3 collective-permute-start.17
  41.6 1.1 %forward_rows.1 = bf16[64,3584]{1,0:T(8,128)(2,1)} custom-call(bf16[16,3840]{1,0:T(8,128)(2,1)S(1)} %collective-permute-done.5.refs_0_, bf16[16,3840]{1,0:T(8,128)(2,1)S(1)} %collective-permute-done.6.refs_1_, bf16[16,3840]{1,0:T(8,128)(2,1)S(1)} %collective-permute-done.7.refs_2_, bf16[16,3840]{1,0:T(8,128)(2,1)S(1)} %collective-permute-done.8.refs_3_), custom_call_target="tpu_custom_call" | custom-call | flops 100000000 | bytes 1000 | tf_op jit(solution)/shard_map/forward_rows/pallas_call | solution.py:38
  42.7 2.9 %collective-permute-done.15.refs_1_ = bf16[16,3840]{1,0:T(8,128)(2,1)S(1)} collective-permute-done((bf16[16,3840]{1,0:T(8,128)(2,1)S(1)}, bf16[16,3840]{1,0:T(8,128)(2,1)S(1)}, u32[]{:S(2)}, u32[]{:S(2)}) %collective-permute-start.15) | collective-permute-done | bytes 122912 | tf_op jit(solution)/shard_map/ppermute | solution.py:503
  45.6 3.6 %collective-permute-done.16.refs_2_ = bf16[16,3840]{1,0:T(8,128)(2,1)S(1)} collective-permute-done((bf16[16,3840]{1,0:T(8,128)(2,1)S(1)}, bf16[16,3840]{1,0:T(8,128)(2,1)S(1)}, u32[]{:S(2)}, u32[]{:S(2)}) %collective-permute-start.16) | collective-permute-done | bytes 122912 | tf_op jit(solution)/shard_map/ppermute | solution.py:503
  49.2 1.5 %collective-permute-done.17.refs_3_ = bf16[16,3840]{1,0:T(8,128)(2,1)S(1)} collective-permute-done((bf16[16,3840]{1,0:T(8,128)(2,1)S(1)}, bf16[16,3840]{1,0:T(8,128)(2,1)S(1)}, u32[]{:S(2)}, u32[]{:S(2)}) %collective-permute-start.17) | collective-permute-done | bytes 122912 | tf_op jit(solution)/shard_map/ppermute | solution.py:503
  50.7 1.1 %backward_rows.1 = bf16[64,3584]{1,0:T(8,128)(2,1)} custom-call(bf16[16,3840]{1,0:T(8,128)(2,1)S(1)} %collective-permute-done.14.refs_0_, bf16[16,3840]{1,0:T(8,128)(2,1)S(1)} %collective-permute-done.15.refs_1_, bf16[16,3840]{1,0:T(8,128)(2,1)S(1)} %collective-permute-done.16.refs_2_, bf16[16,3840]{1,0:T(8,128)(2,1)S(1)} %collective-permute-done.17.refs_3_), custom_call_target="tpu_custom_call" | custom-call | flops 100000000 | bytes 1000 | tf_op jit(solution)/shard_map/backward_rows/pallas_call | solution.py:38
  (23 shorter events, 0.6 us)
Async XLA Ops:
  2.7 10.9 %collective-permute-start = (bf16[16,3840]{1,0:T(8,128)(2,1)S(1)}, bf16[16,3840]{1,0:T(8,128)(2,1)S(1)}, u32[]{:S(2)}, u32[]{:S(2)}) collective-permute-start(bf16[16,3840]{1,0:T(8,128)(2,1)S(1)} %get-tuple-element.33), channel_id=1, source_target_pairs={{0,2},{1,3},{2,0},{3,1},{4,6},{5,7},{6,4},{7,5},{8,10},{9,11},{10,... | collective-permute-start | bytes 368648 | tf_op jit(solution)/shard_map/ppermute | solution.py:483
  5.7 7.9 %collective-permute-start.1 = (bf16[16,3840]{1,0:T(8,128)(2,1)S(1)}, bf16[16,3840]{1,0:T(8,128)(2,1)S(1)}, u32[]{:S(2)}, u32[]{:S(2)}) collective-permute-start(bf16[16,3840]{1,0:T(8,128)(2,1)S(1)} %get-tuple-element.34), channel_id=1, source_target_pairs={{0,4},{1,5},{2,6},{3,7},{4,0},{5,1},{6,2},{7,3},{8,12},{9,13},{10,... | collective-permute-start | bytes 368648 | tf_op jit(solution)/shard_map/ppermute | solution.py:483
  7.2 6.4 %collective-permute-start.2 = (bf16[16,3840]{1,0:T(8,128)(2,1)S(1)}, bf16[16,3840]{1,0:T(8,128)(2,1)S(1)}, u32[]{:S(2)}, u32[]{:S(2)}) collective-permute-start(bf16[16,3840]{1,0:T(8,128)(2,1)S(1)} %get-tuple-element.35), channel_id=1, source_target_pairs={{0,6},{1,7},{2,4},{3,5},{4,2},{5,3},{6,0},{7,1},{8,14},{9,15},{10,... | collective-permute-start | bytes 368648 | tf_op jit(solution)/shard_map/ppermute | solution.py:483
  7.3 6.9 %copy-start = (bf16[1,3584,512]{2,1,0:T(8,128)(2,1)S(1)}, bf16[1,3584,512]{2,1,0:T(8,128)(2,1)}, u32[]{:S(2)}) copy-start(bf16[1,3584,512]{2,1,0:T(8,128)(2,1)} %refs_4_.1) | copy-start | bytes 11010052
  7.3 6.9 %copy-start.1 = (bf16[1,512,3584]{2,1,0:T(8,128)(2,1)S(1)}, bf16[1,512,3584]{2,1,0:T(8,128)(2,1)}, u32[]{:S(2)}) copy-start(bf16[1,512,3584]{2,1,0:T(8,128)(2,1)} %refs_5_.1) | copy-start | bytes 11010052
  10.1 15.6 %collective-permute-start.9 = (bf16[32,3840]{1,0:T(8,128)(2,1)S(1)}, bf16[32,3840]{1,0:T(8,128)(2,1)S(1)}, u32[]{:S(2)}, u32[]{:S(2)}) collective-permute-start(bf16[32,3840]{1,0:T(8,128)(2,1)S(1)} %get-tuple-element.48), channel_id=1, source_target_pairs={{0,2},{1,3},{2,0},{3,1},{4,6},{5,7},{6,4},{7,5},{8,10},{9,11},{10,... | collective-permute-start | bytes 737288 | tf_op jit(solution)/shard_map/ppermute | solution.py:483
  12.1 15.0 %collective-permute-start.10 = (bf16[32,3840]{1,0:T(8,128)(2,1)S(1)}, bf16[32,3840]{1,0:T(8,128)(2,1)S(1)}, u32[]{:S(2)}, u32[]{:S(2)}) collective-permute-start(bf16[32,3840]{1,0:T(8,128)(2,1)S(1)} %get-tuple-element.49), channel_id=1, source_target_pairs={{0,4},{1,5},{2,6},{3,7},{4,0},{5,1},{6,2},{7,3},{8,12},{9,13},{10,... | collective-permute-start | bytes 737288 | tf_op jit(solution)/shard_map/ppermute | solution.py:483
  13.6 13.7 %collective-permute-start.11 = (bf16[32,3840]{1,0:T(8,128)(2,1)S(1)}, bf16[32,3840]{1,0:T(8,128)(2,1)S(1)}, u32[]{:S(2)}, u32[]{:S(2)}) collective-permute-start(bf16[32,3840]{1,0:T(8,128)(2,1)S(1)} %get-tuple-element.50), channel_id=1, source_target_pairs={{0,6},{1,7},{2,4},{3,5},{4,2},{5,3},{6,0},{7,1},{8,14},{9,15},{10,... | collective-permute-start | bytes 737288 | tf_op jit(solution)/shard_map/ppermute | solution.py:483
  14.1 2.0 %collective-permute-start.3 = (bf16[80,3584]{1,0:T(8,128)(2,1)S(1)}, bf16[80,3584]{1,0:T(8,128)(2,1)S(1)}, u32[]{:S(2)}, u32[]{:S(2)}) collective-permute-start(bf16[80,3584]{1,0:T(8,128)(2,1)S(1)} %get-tuple-element.38.refs_0_), channel_id=1, source_target_pairs={{0,1},{1,0},{2,3},{3,2},{4,5},{5,4},{6,7},{7,6},{8,9},{9,8},{10,11... | collective-permute-start | bytes 1720328 | tf_op jit(solution)/shard_map/ppermute | solution.py:490
  17.6 2.0 %collective-permute-start.4 = (bf16[80,3584]{1,0:T(8,128)(2,1)S(1)}, bf16[80,3584]{1,0:T(8,128)(2,1)S(1)}, u32[]{:S(2)}, u32[]{:S(2)}) collective-permute-start(bf16[80,3584]{1,0:T(8,128)(2,1)S(1)} %get-tuple-element.41), channel_id=1, source_target_pairs={{0,1},{1,0},{2,3},{3,2},{4,5},{5,4},{6,7},{7,6},{8,9},{9,8},{10,11... | collective-permute-start | bytes 1720328 | tf_op jit(solution)/shard_map/ppermute | solution.py:490
  20.1 18.4 %collective-permute-start.6 = (bf16[16,3840]{1,0:T(8,128)(2,1)S(1)}, bf16[16,3840]{1,0:T(8,128)(2,1)S(1)}, u32[]{:S(2)}, u32[]{:S(2)}) collective-permute-start(bf16[16,3840]{1,0:T(8,128)(2,1)S(1)} %get-tuple-element.44), channel_id=1, source_target_pairs={{0,10},{1,11},{2,8},{3,9},{4,14},{5,15},{6,12},{7,13},{8,18},{9,19... | collective-permute-start | bytes 368648 | tf_op jit(solution)/shard_map/ppermute | solution.py:503
  23.1 16.8 %collective-permute-start.7 = (bf16[16,3840]{1,0:T(8,128)(2,1)S(1)}, bf16[16,3840]{1,0:T(8,128)(2,1)S(1)}, u32[]{:S(2)}, u32[]{:S(2)}) collective-permute-start(bf16[16,3840]{1,0:T(8,128)(2,1)S(1)} %get-tuple-element.45), channel_id=1, source_target_pairs={{0,12},{1,13},{2,14},{3,15},{4,8},{5,9},{6,10},{7,11},{8,20},{9,21... | collective-permute-start | bytes 368648 | tf_op jit(solution)/shard_map/ppermute | solution.py:503
  25.6 15.7 %collective-permute-start.8 = (bf16[16,3840]{1,0:T(8,128)(2,1)S(1)}, bf16[16,3840]{1,0:T(8,128)(2,1)S(1)}, u32[]{:S(2)}, u32[]{:S(2)}) collective-permute-start(bf16[16,3840]{1,0:T(8,128)(2,1)S(1)} %get-tuple-element.46), channel_id=1, source_target_pairs={{0,14},{1,15},{2,12},{3,13},{4,10},{5,11},{6,8},{7,9},{8,22},{9,23... | collective-permute-start | bytes 368648 | tf_op jit(solution)/shard_map/ppermute | solution.py:503
  27.1 14.5 %collective-permute-start.5 = (bf16[16,3840]{1,0:T(8,128)(2,1)S(1)}, bf16[16,3840]{1,0:T(8,128)(2,1)S(1)}, u32[]{:S(2)}, u32[]{:S(2)}) collective-permute-start(bf16[16,3840]{1,0:T(8,128)(2,1)S(1)} %get-tuple-element.43.refs_4_), channel_id=1, source_target_pairs={{0,8},{1,9},{2,10},{3,11},{4,12},{5,13},{6,14},{7,15},{8,16},{9,17... | collective-permute-start | bytes 368648 | tf_op jit(solution)/shard_map/ppermute | solution.py:503
  27.4 2.0 %collective-permute-start.12 = (bf16[80,3584]{1,0:T(8,128)(2,1)S(1)}, bf16[80,3584]{1,0:T(8,128)(2,1)S(1)}, u32[]{:S(2)}, u32[]{:S(2)}) collective-permute-start(bf16[80,3584]{1,0:T(8,128)(2,1)S(1)} %get-tuple-element.52.refs_4_.refs_0_), channel_id=1, source_target_pairs={{0,1},{1,0},{2,3},{3,2},{4,5},{5,4},{6,7},{7,6},{8,9},{9,8},{10,11... | collective-permute-start | bytes 1720328 | tf_op jit(solution)/shard_map/ppermute | solution.py:490
  32.0 2.1 %collective-permute-start.13 = (bf16[80,3712]{1,0:T(8,128)(2,1)S(1)}, bf16[80,3712]{1,0:T(8,128)(2,1)S(1)}, u32[]{:S(2)}, u32[]{:S(2)}) collective-permute-start(bf16[80,3712]{1,0:T(8,128)(2,1)S(1)} %get-tuple-element.57), channel_id=1, source_target_pairs={{0,1},{1,0},{2,3},{3,2},{4,5},{5,4},{6,7},{7,6},{8,9},{9,8},{10,11... | collective-permute-start | bytes 1781768 | tf_op jit(solution)/shard_map/ppermute | solution.py:490
  34.8 7.9 %collective-permute-start.14 = (bf16[16,3840]{1,0:T(8,128)(2,1)S(1)}, bf16[16,3840]{1,0:T(8,128)(2,1)S(1)}, u32[]{:S(2)}, u32[]{:S(2)}) collective-permute-start(bf16[16,3840]{1,0:T(8,128)(2,1)S(1)} %get-tuple-element.58), channel_id=1, source_target_pairs={{0,24},{1,25},{2,26},{3,27},{4,28},{5,29},{6,30},{7,31},{8,0},{9,1... | collective-permute-start | bytes 368648 | tf_op jit(solution)/shard_map/ppermute | solution.py:503
  38.5 7.1 %collective-permute-start.15 = (bf16[16,3840]{1,0:T(8,128)(2,1)S(1)}, bf16[16,3840]{1,0:T(8,128)(2,1)S(1)}, u32[]{:S(2)}, u32[]{:S(2)}) collective-permute-start(bf16[16,3840]{1,0:T(8,128)(2,1)S(1)} %get-tuple-element.59), channel_id=1, source_target_pairs={{0,26},{1,27},{2,24},{3,25},{4,30},{5,31},{6,28},{7,29},{8,2},{9,3... | collective-permute-start | bytes 368648 | tf_op jit(solution)/shard_map/ppermute | solution.py:503
  39.9 9.4 %collective-permute-start.16 = (bf16[16,3840]{1,0:T(8,128)(2,1)S(1)}, bf16[16,3840]{1,0:T(8,128)(2,1)S(1)}, u32[]{:S(2)}, u32[]{:S(2)}) collective-permute-start(bf16[16,3840]{1,0:T(8,128)(2,1)S(1)} %get-tuple-element.60), channel_id=1, source_target_pairs={{0,28},{1,29},{2,30},{3,31},{4,24},{5,25},{6,26},{7,27},{8,4},{9,5... | collective-permute-start | bytes 368648 | tf_op jit(solution)/shard_map/ppermute | solution.py:503
  41.3 9.4 %collective-permute-start.17 = (bf16[16,3840]{1,0:T(8,128)(2,1)S(1)}, bf16[16,3840]{1,0:T(8,128)(2,1)S(1)}, u32[]{:S(2)}, u32[]{:S(2)}) collective-permute-start(bf16[16,3840]{1,0:T(8,128)(2,1)S(1)} %get-tuple-element.61), channel_id=1, source_target_pairs={{0,30},{1,31},{2,28},{3,29},{4,26},{5,27},{6,24},{7,25},{8,6},{9,7... | collective-permute-start | bytes 368648 | tf_op jit(solution)/shard_map/ppermute | solution.py:503

commit v4 on v3

--- a/solution.py
+++ b/solution.py
@@ -21,15 +21,14 @@
 
 
 cost = {
-    "backward_chunks": 10,
-    "saved_rows": 40,
+    "normed_rows": 5,
     "saved_terms": 40,
     "act_norms": 40,
     "act_gates": 40,
 }
 
 
-def call(body, places, outs, scratch, megabytes, name):
+def call(body, places, outs, scratch, megabytes, name, out_specs=None):
     def run(*arrays):
         arrays = [
             pltpu.with_memory_space_constraint(array, pltpu.HBM) if place == "h" else array
@@ -37,10 +36,12 @@
         ]
         return kernel(*arrays)
 
+    where_to = {} if out_specs is None else {"out_specs": out_specs}
     kernel = pl.pallas_call(
         body,
         out_shape=outs,
         in_specs=[spaces[place] for place in places],
+        **where_to,
         scratch_shapes=scratch,
         compiler_params=pltpu.CompilerParams(vmem_limit_bytes=megabytes * 1024 * 1024),
         cost_estimate=pl.CostEstimate(
@@ -97,7 +98,8 @@
     slot_row = slot(row, place_row)
     slot_column = slot(column, place_column)
     by_slot = lax.broadcasted_iota(jnp.int32, (z.rows, tokens), 0) == slot_row
-    by_token = lax.broadcasted_iota(jnp.int32, (tokens, fold), 1) == slot_column
+    lane = lax.broadcasted_iota(jnp.int32, (tokens, fold), 1)
+    by_token = jnp.where(lane < tokens, lane, tokens + (lane - tokens) // 16) == slot_column
     token = lax.broadcasted_iota(jnp.int32, (tokens, fold), 0).astype(f32)
     token_row = jnp.sum(jnp.where(by_token, token - none, 0.0), axis=0, keepdims=True) + none
     return jnp.where(by_slot, 1.0, 0.0).astype(bf16), token_row
@@ -301,11 +303,11 @@
     )(*rows, w_gate, w_down, *after)
 
 
-def saved_rows(z, where, saved, weights, after):
+def saved_terms(z, where, saved, after):
     total, slots, width = z.split * z.rows, saved.shape[2], saved.shape[3]
 
     def body(where, saved_any, *refs):
-        ordered_ref, saved_ref, sem = refs[len(weights) + len(after) :]
+        hidden_ref, slope_ref, saved_ref, sem = refs[len(after) :]
         copy = pltpu.make_async_copy(saved_any.at[0, 0], saved_ref, sem)
         copy.start()
         row = lax.broadcasted_iota(jnp.int32, (total, slots), 0)
@@ -318,34 +320,19 @@
         wanted = jnp.where(k < z.experts, source * z.cap + p, -1)
         selector = jnp.where(slot == wanted, 1.0, 0.0).astype(bf16)
         copy.wait()
-        ordered_ref[...] = jnp.dot(selector, saved_ref[...], preferred_element_type=f32)
-
-    return call(
-        body,
-        "sh" + "v" * len(weights) + "a" * len(after),
-        shape((total, width), f32),
-        [pltpu.VMEM((slots, width), bf16), pltpu.SemaphoreType.DMA],
-        8,
-        "saved_rows",
-    )(where, saved, *weights, *after)
-
-
-def saved_terms(z, ordered, after):
-    def body(ordered_ref, *refs):
-        hidden_ref, slope_ref = refs[len(after) :]
-        gate_proj = ordered_ref[...]
+        gate_proj = jnp.dot(selector, saved_ref[...], preferred_element_type=f32)
         sg = jax.nn.sigmoid(gate_proj)
         hidden_ref[...] = (gate_proj * sg).astype(bf16)
         slope_ref[...] = sg * (1.0 + gate_proj * (1.0 - sg))
 
     return call(
         body,
-        "v" + "a" * len(after),
-        [shape(ordered.shape), shape(ordered.shape, f32)],
-        [],
+        "sh" + "a" * len(after),
+        [shape((total, width)), shape((total, width), f32)],
+        [pltpu.VMEM((slots, width), bf16), pltpu.SemaphoreType.DMA],
         8,
         "saved_terms",
-    )(ordered, *after)
+    )(where, saved, *after)
 
 
 def experts_backward(z, rows, hidden, slope, w_gate, w_down, after):
@@ -383,11 +370,12 @@
     out[:, z.width :] = tile[...].astype(bf16)
 
 
-def finish_forward(z, chunks, last, parts, gates, after):
-    def body(*refs):
-        e = z.experts
-        chunks, last, parts = refs[:e], refs[e], refs[e + 1 : e + 1 + z.split]
-        gates, outs, (tile,) = refs[e + 1 + z.split], refs[-1 - e : -1], refs[-1:]
+def finish_forward(z, ks, chunks, last, parts, gates, after):
+    count = len(ks)
+
+    def body(*refs):
+        chunks, last, parts = refs[:count], refs[count], refs[count + 1 : count + 1 + z.split]
+        gates, outs, tile = refs[count + 1 + z.split], refs[-1 - count : -1], refs[-1]
 
         def mixed(at):
             y = parts[0][at : at + 16, :].astype(f32)
@@ -396,27 +384,28 @@
             return route_scale * (gates[at : at + 16, 0:1] * y)
 
         tail = last[...] + mixed(z.tokens)
-        for k in range(e):
-            h = chunks[k][:, : z.width].astype(f32)
-            outs[k][:, : z.width] = (h + mixed(k * z.main)).astype(bf16)
-            put_last(z, tail[k : k + 1, :], chunks[k], tile, outs[k])
-
-    return call(
-        body,
-        "v" * (z.experts + z.split + 2) + "a" * len(after),
-        [shape((z.main, z.wide))] * z.experts,
+        for k, chunk, out in zip(ks, chunks, outs):
+            h = chunk[:, : z.width].astype(f32)
+            out[:, : z.width] = (h + mixed(k * z.main)).astype(bf16)
+            put_last(z, tail[k : k + 1, :], chunk, tile, out)
+
+    return call(
+        body,
+        "v" * (count + z.split + 2) + "a" * len(after),
+        [shape((z.main, z.wide))] * count,
         [pltpu.VMEM((16, fold), f32)],
         8,
-        "finish_forward",
-    )(*chunks, last, *parts, gates, *after)
-
-
-def finish_backward(z, chunks, lasts, terms, parts, vectors):
+        "finish_forward_" + "".join(map(str, ks)),
+    )(*[chunks[k] for k in ks], last, *parts, gates, *after)
+
+
+def finish_backward(z, order, chunks, lasts, terms, parts, vectors, after):
     def body(*refs):
         e = z.experts
         chunks, (last_grad, last_act, inv_ref, affinity_ref) = refs[:e], refs[e : e + 4]
         parts, vectors = refs[e + 4 : e + 4 + z.split], refs[e + 4 + z.split]
         outs, (tile,) = refs[-1 - e : -1], refs[-1:]
+        outs = [outs[order.index(k)] for k in range(e)]
         gain, router = vectors[0:1, :], vectors[1:2, :]
 
         def finished(h, g, at):
@@ -441,37 +430,49 @@
 
     return call(
         body,
-        "v" * (z.experts + z.split + 5),
+        "v" * (z.experts + z.split + 5) + "a" * len(after),
         [shape((z.main, z.wide))] * z.experts,
         [pltpu.VMEM((16, fold), f32)],
         8,
         "finish_backward",
-    )(*chunks, *lasts, *terms, *parts, vectors)
+    )(*chunks, *lasts, *terms, *parts, vectors, *after)
 
 
 def order_rows(z, chunks, name):
-    def body(*refs):
-        chunks, (out, held, last, tile) = refs[: z.experts], refs[z.experts :]
-        for k in range(z.experts):
-            held[k * z.main : (k + 1) * z.main, :] = chunks[k][:, : z.width]
-        collect_rows(z, chunks, last, tile)
-        held[z.tokens :, :] = last[...].astype(bf16)
-        token_row = chunks[0][:, z.width :].astype(f32)[z.pieces : z.pieces + 1, : z.rows]
-        token = lax.broadcasted_iota(jnp.int32, (z.tokens, z.rows), 0).astype(f32)
-        selector = jnp.where(token == token_row, 1.0, 0.0).astype(bf16)
-        out[...] = jnp.dot(selector, held[...], preferred_element_type=f32).astype(bf16)
+    lanes = z.tokens + 16 * z.experts
+    steps = 7 if z.pieces % 7 == 0 else z.pieces
+
+    def body(*refs):
+        chunks, (out_any, out, sems) = refs[: z.experts], refs[z.experts :]
+        tiles = [chunk[:, z.width :] for chunk in chunks]
+        token_row = tiles[0].astype(f32)[z.pieces : z.pieces + 1, :lanes]
+        token = lax.broadcasted_iota(jnp.int32, (z.tokens, lanes), 0).astype(f32)
+        lane = lax.broadcasted_iota(jnp.int32, (z.tokens, lanes), 1)
+        piece = jnp.where(lane < z.tokens, -1, lane % 16)
+        ours = token == token_row
+        copies = []
+        for i in range(z.pieces):
+            cols = pl.ds(i * fold, fold)
+            mine = ours & ((piece < 0) | (piece == i))
+            selector = jnp.where(mine, 1.0, 0.0).astype(bf16)
+            rows = jnp.concatenate([chunk[:, cols] for chunk in chunks] + tiles, axis=0)
+            out[:, cols] = jnp.dot(selector, rows, preferred_element_type=f32).astype(bf16)
+            if (i + 1) % (z.pieces // steps) == 0:
+                done = pl.ds((i + 1) * fold - z.width // steps, z.width // steps)
+                copy = pltpu.make_async_copy(out.at[:, done], out_any.at[:, done], sems.at[len(copies)])
+                copy.start()
+                copies.append(copy)
+        for copy in copies:
+            copy.wait()
 
     return call(
         body,
         "v" * z.experts,
         shape((z.tokens, z.width)),
-        [
-            pltpu.VMEM((z.rows, z.width), bf16),
-            pltpu.VMEM((16, z.width), f32),
-            pltpu.VMEM((16, fold), f32),
-        ],
+        [pltpu.VMEM((z.tokens, z.width), bf16), pltpu.SemaphoreType.DMA((steps,))],
         8,
         name,
+        spaces["a"],
     )(*chunks)
 
 
@@ -490,18 +491,15 @@
     return lax.ppermute(array, "ep", pairs)
 
 
-def to_section(z, chunks, by):
+def to_section(z, chunk, k, by):
     groups = z.experts * z.split
     sections = lax.axis_size("pp")
-    got = [None] * z.experts
-    for k in reversed(range(z.experts)):
-        pairs = [
-            (s * groups + i, (s + by) % sections * groups + ((i // z.split) ^ k) * z.split + i % z.split)
-            for s in range(sections)
-            for i in range(groups)
-        ]
-        got[k] = lax.ppermute(chunks[k], ("pp", "ep"), pairs)
-    return got
+    pairs = [
+        (s * groups + i, (s + by) % sections * groups + ((i // z.split) ^ k) * z.split + i % z.split)
+        for s in range(sections)
+        for i in range(groups)
+    ]
+    return lax.ppermute(chunk, ("pp", "ep"), pairs)
 
 
 def on_device(
@@ -530,23 +528,32 @@
 
     normed, gates, fwd_last = normed_rows(z, fwd_own, vectors)
     fwd_all = [normed] + [to_core(z, normed, m) for m in others]
-    ordered = saved_rows(z, where, saved_gate, [w_gate, w_down], [gates])
-    fwd_parts = experts_forward(z, fwd_all, w_gate, w_down, [ordered])
-    hidden, slope = saved_terms(z, ordered, [fwd_parts[0]])
+    fwd_parts = experts_forward(z, fwd_all, w_gate, w_down, [])
+    hidden, slope = saved_terms(z, where, saved_gate, [fwd_parts[0]])
     fwd_parts = [fwd_parts[0]] + [to_core(z, fwd_parts[m], m) for m in others]
-    fwd_out = finish_forward(z, fwd_own, fwd_last, fwd_parts, gates, [hidden])
-    fwd_done = to_section(z, fwd_out, 1)
-
-    grads, grad_last = grad_rows_of(z, bwd_own, [fwd_out[0]])
+    fwd_done = {}
+
+    def finish(ks, after):
+        outs = finish_forward(z, ks, [fwd_own[k] for k in range(z.experts)], fwd_last, fwd_parts, gates, after)
+        for k, out in zip(ks, outs):
+            fwd_done[k] = to_section(z, out, k, 1)
+        return outs[0]
+
+    order = [*range(z.experts - 1, 0, -1), 0]
+    first = finish(order[:-1], [hidden])
+    grads, grad_last = grad_rows_of(z, bwd_own, [first])
     grad_all = [grads] + [to_core(z, grads, m) for m in others]
     inv, act_last = act_norms(z, bwd_own, [grads])
     bwd_parts = experts_backward(z, grad_all, hidden, slope, w_gate, w_down, [inv])
     affinity = act_gates(z, bwd_own, act_last, inv, vectors, [bwd_parts[0]])
+    third = finish(order[-1:], [affinity])
     bwd_parts = [bwd_parts[0]] + [to_core(z, bwd_parts[m], m) for m in others]
     bwd_out = finish_backward(
-        z, bwd_own, [grad_last, act_last], [inv, affinity], bwd_parts, vectors
+        z, order, bwd_own, [grad_last, act_last], [inv, affinity], bwd_parts, vectors, [third]
     )
-    bwd_done = to_section(z, bwd_out, -1)
+    bwd_done = {k: to_section(z, out, k, -1) for k, out in zip(order, bwd_out)}
+    bwd_done = [bwd_done[k] for k in range(z.experts)]
+    fwd_done = [fwd_done[k] for k in range(z.experts)]
     return (order_rows(z, fwd_done, "forward_rows"), order_rows(z, bwd_done, "backward_rows"))
 
 

time: 52 us -> 60.6 us (1.17)
  starting transfers between devices: 22.6 us -> 27.3 us
  waiting for transfers between devices: 13.3 us -> 17.6 us
    ppermute x6, waiting for transfers between devices: 0.02 us -> 6.88 us  [dispatch(): got[k] = lax.ppermute(chunks[k], 'ep', pairs)]
    ppermute x8, starting transfers between devices: 14 us -> 18.8 us  [to_section(): return lax.ppermute(chunk, ('pp', 'ep'), pairs)]
    ppermute x4, waiting for transfers between devices: 5.2 us -> 2 us  [to_core(): return lax.ppermute(array, 'ep', pairs)]
    ppermute x8, waiting for transfers between devices: 8.08 us -> 8.75 us  [to_section(): return lax.ppermute(chunk, ('pp', 'ep'), pairs)]
  transfers between devices with their start and end apart: 18 -> 18, of which waited for: 7 -> 8; matrix products, arithmetic and copies ran while one was open for 0% -> 0% of each run, Pallas kernels for 23% -> 18%
where the time goes in v4:
time: 60.6 us; the launch traced here: 60.4 us
  starting transfers between devices  27.3 us (45%)
  waiting for transfers between devices  17.6 us (29%)
  Pallas kernels  14.6 us (24%)
  between operations  0.76 us (1%)
    ppermute x8, starting transfers between devices, to_section(): return lax.ppermute(chunk, ('pp', 'ep'), pairs)  18.8 us
    pallas_call x14, Pallas kernels, run(): return kernel(*arrays)  14.6 us
    ppermute x8, waiting for transfers between devices, to_section(): return lax.ppermute(chunk, ('pp', 'ep'), pairs)  8.75 us
    ppermute x6, starting transfers between devices, dispatch(): got[k] = lax.ppermute(chunks[k], 'ep', pairs)  8.1 us
    ppermute x6, waiting for transfers between devices, dispatch(): got[k] = lax.ppermute(chunks[k], 'ep', pairs)  6.88 us
    ppermute x4, waiting for transfers between devices, to_core(): return lax.ppermute(array, 'ep', pairs)  2 us
  transfers between devices with their start and end apart: 18, of which 8 were waited for; matrix products, arithmetic and copies ran while one was open for 0% of the time, Pallas kernels for 18%

profile of v4, /device:TPU:0, one launch (start us, length us, event | category | flops | bytes accessed | tf_op | source)
XLA Modules:
  0.0 60.4 jit_solution(2945089333807962734)
XLA Ops:
  0.7 2.0 %forward_chunks.1 = (bf16[16,3840]{1,0:T(8,128)(2,1)S(1)}, bf16[16,3840]{1,0:T(8,128)(2,1)S(1)}, bf16[16,3840]{1,0:T(8,128)(2,1)S(1)}, bf16[16,3840]{1,0:T(8,128)(2,1)S(1)}) custom-call(s32[2]{0:T(128)S(1)} %pad_add_fusion.where, s32[1,64]{1,0:T(1,128)} %bitcast.7, bf16[64,3584]{1,0:T(8,128)(2,1)} %refs_0_.2), custom_call_target="tpu_custom_call" | custom-call | flops 100000000 | bytes 1000 | tf_op jit(solution)/shard_map/forward_chunks/pallas_call | solution.py:37
  2.7 3.0 %collective-permute-start = (bf16[16,3840]{1,0:T(8,128)(2,1)S(1)}, bf16[16,3840]{1,0:T(8,128)(2,1)S(1)}, u32[]{:S(2)}, u32[]{:S(2)}) collective-permute-start(bf16[16,3840]{1,0:T(8,128)(2,1)S(1)} %get-tuple-element.32), channel_id=1, source_target_pairs={{0,2},{1,3},{2,0},{3,1},{4,6},{5,7},{6,4},{7,5},{8,10},{9,11},{10,... | collective-permute-start | bytes 368648 | tf_op jit(solution)/shard_map/ppermute | solution.py:484
  5.7 1.5 %collective-permute-start.1 = (bf16[16,3840]{1,0:T(8,128)(2,1)S(1)}, bf16[16,3840]{1,0:T(8,128)(2,1)S(1)}, u32[]{:S(2)}, u32[]{:S(2)}) collective-permute-start(bf16[16,3840]{1,0:T(8,128)(2,1)S(1)} %get-tuple-element.33), channel_id=1, source_target_pairs={{0,4},{1,5},{2,6},{3,7},{4,0},{5,1},{6,2},{7,3},{8,12},{9,13},{10,... | collective-permute-start | bytes 368648 | tf_op jit(solution)/shard_map/ppermute | solution.py:484
  7.3 2.5 %backward_chunks.1 = (bf16[32,3840]{1,0:T(8,128)(2,1)S(1)}, bf16[32,3840]{1,0:T(8,128)(2,1)S(1)}, bf16[32,3840]{1,0:T(8,128)(2,1)S(1)}, bf16[32,3840]{1,0:T(8,128)(2,1)S(1)}, f32[8,3584]{1,0:T(8,128)S(1)}) custom-call(s32[2]{0:T(128)S(1)} %pad_add_fusion.where, s32[1,64]{1,0:T(1,128)} %bitcast.6, bf16[64,3584]{1,0:T(8,128)(2,1)} %refs_0_.3, ...), custom_call_target="tpu_custom_call" | custom-call | flops 100000000 | bytes 1000 | tf_op jit(solution)/shard_map/backward_chunks/pallas_call | solution.py:37
  9.8 3.4 %collective-permute-done.1.refs_2_.refs_1_ = bf16[16,3840]{1,0:T(8,128)(2,1)S(1)} collective-permute-done((bf16[16,3840]{1,0:T(8,128)(2,1)S(1)}, bf16[16,3840]{1,0:T(8,128)(2,1)S(1)}, u32[]{:S(2)}, u32[]{:S(2)}) %collective-permute-start.1) | collective-permute-done | bytes 122912 | tf_op jit(solution)/shard_map/ppermute | solution.py:484
  13.2 0.5 normed_rows.1
  13.8 1.2 %collective-permute-start.5 = (bf16[32,3840]{1,0:T(8,128)(2,1)S(1)}, bf16[32,3840]{1,0:T(8,128)(2,1)S(1)}, u32[]{:S(2)}, u32[]{:S(2)}) collective-permute-start(bf16[32,3840]{1,0:T(8,128)(2,1)S(1)} %get-tuple-element.42), channel_id=1, source_target_pairs={{0,2},{1,3},{2,0},{3,1},{4,6},{5,7},{6,4},{7,5},{8,10},{9,11},{10,... | collective-permute-start | bytes 737288 | tf_op jit(solution)/shard_map/ppermute | solution.py:484
  15.0 0.8 %collective-permute-start.6 = (bf16[32,3840]{1,0:T(8,128)(2,1)S(1)}, bf16[32,3840]{1,0:T(8,128)(2,1)S(1)}, u32[]{:S(2)}, u32[]{:S(2)}) collective-permute-start(bf16[32,3840]{1,0:T(8,128)(2,1)S(1)} %get-tuple-element.43), channel_id=1, source_target_pairs={{0,4},{1,5},{2,6},{3,7},{4,0},{5,1},{6,2},{7,3},{8,12},{9,13},{10,... | collective-permute-start | bytes 737288 | tf_op jit(solution)/shard_map/ppermute | solution.py:484
  15.8 1.5 %collective-permute-start.7 = (bf16[32,3840]{1,0:T(8,128)(2,1)S(1)}, bf16[32,3840]{1,0:T(8,128)(2,1)S(1)}, u32[]{:S(2)}, u32[]{:S(2)}) collective-permute-start(bf16[32,3840]{1,0:T(8,128)(2,1)S(1)} %get-tuple-element.44), channel_id=1, source_target_pairs={{0,6},{1,7},{2,4},{3,5},{4,2},{5,3},{6,0},{7,1},{8,14},{9,15},{10,... | collective-permute-start | bytes 737288 | tf_op jit(solution)/shard_map/ppermute | solution.py:484
  17.4 1.5 %experts_forward.1 = (bf16[80,3584]{1,0:T(8,128)(2,1)S(1)}, bf16[80,3584]{1,0:T(8,128)(2,1)S(1)}) custom-call(bf16[80,3584]{1,0:T(8,128)(2,1)S(1)} %get-tuple-element.37.refs_0_, bf16[80,3584]{1,0:T(8,128)(2,1)S(1)} %collective-permute-done.3.refs_1_, bf16[1,3584,512]{2,1,0:T(8,128)(2,1)S(1)} %copy-done, bf16[1,512,3584]{2,1,0:T(8,128)(2,1)S(1)} %copy-done.1), custom_call_target="tpu_custom_call" | custom-call | flops 100000000 | bytes 1000 | tf_op jit(solution)/shard_map/experts_forward/pallas_call | solution.py:37
  18.9 1.7 %saved_terms.1 = (bf16[160,512]{1,0:T(8,128)(2,1)S(1)}, f32[160,512]{1,0:T(8,128)S(1)}) custom-call(s32[2]{0:T(128)S(1)} %pad_add_fusion.where, bf16[1,1,136,512]{3,2,1,0:T(8,128)(2,1)} %saved_any.1, bf16[80,3584]{1,0:T(8,128)(2,1)S(1)} %get-tuple-element.38.refs_0_.refs_4_.refs_2_), custom_call_target="tpu_custom_call" | custom-call | flops 40000000000 | bytes 1000 | tf_op jit(solution)/shard_map/saved_terms/pallas_call | solution.py:37
  20.6 0.3 collective-permute-done.4.refs_5_.refs_3_
  20.9 0.3 finish_forward_321.1
  21.2 2.2 %collective-permute-start.10 = (bf16[16,3840]{1,0:T(8,128)(2,1)S(1)}, bf16[16,3840]{1,0:T(8,128)(2,1)S(1)}, u32[]{:S(2)}, u32[]{:S(2)}) collective-permute-start(bf16[16,3840]{1,0:T(8,128)(2,1)S(1)} %get-tuple-element.52), channel_id=1, source_target_pairs={{0,10},{1,11},{2,8},{3,9},{4,14},{5,15},{6,12},{7,13},{8,18},{9,19... | collective-permute-start | bytes 368648 | tf_op jit(solution)/shard_map/ppermute | solution.py:502
  23.4 1.8 %collective-permute-start.11 = (bf16[16,3840]{1,0:T(8,128)(2,1)S(1)}, bf16[16,3840]{1,0:T(8,128)(2,1)S(1)}, u32[]{:S(2)}, u32[]{:S(2)}) collective-permute-start(bf16[16,3840]{1,0:T(8,128)(2,1)S(1)} %get-tuple-element.53), channel_id=1, source_target_pairs={{0,12},{1,13},{2,14},{3,15},{4,8},{5,9},{6,10},{7,11},{8,20},{9,21... | collective-permute-start | bytes 368648 | tf_op jit(solution)/shard_map/ppermute | solution.py:502
  25.2 2.5 %collective-permute-start.12 = (bf16[16,3840]{1,0:T(8,128)(2,1)S(1)}, bf16[16,3840]{1,0:T(8,128)(2,1)S(1)}, u32[]{:S(2)}, u32[]{:S(2)}) collective-permute-start(bf16[16,3840]{1,0:T(8,128)(2,1)S(1)} %get-tuple-element.46.refs_4_), channel_id=1, source_target_pairs={{0,14},{1,15},{2,12},{3,13},{4,10},{5,11},{6,8},{7,9},{8,22},{9,23... | collective-permute-start | bytes 368648 | tf_op jit(solution)/shard_map/ppermute | solution.py:502
  27.8 3.4 %collective-permute-done.7.refs_3_ = bf16[32,3840]{1,0:T(8,128)(2,1)S(1)} collective-permute-done((bf16[32,3840]{1,0:T(8,128)(2,1)S(1)}, bf16[32,3840]{1,0:T(8,128)(2,1)S(1)}, u32[]{:S(2)}, u32[]{:S(2)}) %collective-permute-start.7) | collective-permute-done | bytes 245792 | tf_op jit(solution)/shard_map/ppermute | solution.py:484
  31.4 0.2 act_norms.1
  31.6 1.7 %collective-permute-done.8.refs_1_ = bf16[80,3584]{1,0:T(8,128)(2,1)S(1)} collective-permute-done((bf16[80,3584]{1,0:T(8,128)(2,1)S(1)}, bf16[80,3584]{1,0:T(8,128)(2,1)S(1)}, u32[]{:S(2)}, u32[]{:S(2)}) %collective-permute-start.8) | collective-permute-done | bytes 573472 | tf_op jit(solution)/shard_map/ppermute | solution.py:491
  33.4 2.6 %experts_backward.1 = (bf16[80,3712]{1,0:T(8,128)(2,1)S(1)}, bf16[80,3712]{1,0:T(8,128)(2,1)S(1)}) custom-call(bf16[80,3584]{1,0:T(8,128)(2,1)S(1)} %get-tuple-element.47.refs_4_.refs_0_, bf16[80,3584]{1,0:T(8,128)(2,1)S(1)} %collective-permute-done.8.refs_1_, bf16[160,512]{1,0:T(8,128)(2,1)S(1)} %get-tuple-element.45.refs_7_.refs_2_, ...), custom_call_target="tpu_custom_call" | custom-call | flops 100000000 | bytes 1000 | tf_op jit(solution)/shard_map/experts_backward/pallas_call | solution.py:37
  36.2 0.4 act_gates.1.refs_5_.refs_7_
  36.7 5.5 %collective-permute-start.9 = (bf16[16,3840]{1,0:T(8,128)(2,1)S(1)}, bf16[16,3840]{1,0:T(8,128)(2,1)S(1)}, u32[]{:S(2)}, u32[]{:S(2)}) collective-permute-start(bf16[16,3840]{1,0:T(8,128)(2,1)S(1)} %finish_forward_0.1.refs_11_), channel_id=1, source_target_pairs={{0,8},{1,9},{2,10},{3,11},{4,12},{5,13},{6,14},{7,15},{8,16},{9,17... | collective-permute-start | bytes 368648 | tf_op jit(solution)/shard_map/ppermute | solution.py:502
  42.2 0.7 %finish_backward.1 = (bf16[16,3840]{1,0:T(8,128)(2,1)S(1)}, bf16[16,3840]{1,0:T(8,128)(2,1)S(1)}, bf16[16,3840]{1,0:T(8,128)(2,1)S(1)}, bf16[16,3840]{1,0:T(8,128)(2,1)S(1)}) custom-call(bf16[32,3840]{1,0:T(8,128)(2,1)S(1)} %get-tuple-element.41.refs_0_, bf16[32,3840]{1,0:T(8,128)(2,1)S(1)} %collective-permute-done.5.refs_1_, ...), custom_call_target="tpu_custom_call" | custom-call | flops 100000000 | bytes 1000 | tf_op jit(solution)/shard_map/finish_backward/pallas_call | solution.py:37
  42.8 3.3 %collective-permute-start.14 = (bf16[16,3840]{1,0:T(8,128)(2,1)S(1)}, bf16[16,3840]{1,0:T(8,128)(2,1)S(1)}, u32[]{:S(2)}, u32[]{:S(2)}) collective-permute-start(bf16[16,3840]{1,0:T(8,128)(2,1)S(1)} %get-tuple-element.56), channel_id=1, source_target_pairs={{0,24},{1,25},{2,26},{3,27},{4,28},{5,29},{6,30},{7,31},{8,0},{9,1... | collective-permute-start | bytes 368648 | tf_op jit(solution)/shard_map/ppermute | solution.py:502
  46.2 1.3 %collective-permute-start.15 = (bf16[16,3840]{1,0:T(8,128)(2,1)S(1)}, bf16[16,3840]{1,0:T(8,128)(2,1)S(1)}, u32[]{:S(2)}, u32[]{:S(2)}) collective-permute-start(bf16[16,3840]{1,0:T(8,128)(2,1)S(1)} %get-tuple-element.57), channel_id=1, source_target_pairs={{0,26},{1,27},{2,24},{3,25},{4,30},{5,31},{6,28},{7,29},{8,2},{9,3... | collective-permute-start | bytes 368648 | tf_op jit(solution)/shard_map/ppermute | solution.py:502
  47.5 0.9 %collective-permute-start.16 = (bf16[16,3840]{1,0:T(8,128)(2,1)S(1)}, bf16[16,3840]{1,0:T(8,128)(2,1)S(1)}, u32[]{:S(2)}, u32[]{:S(2)}) collective-permute-start(bf16[16,3840]{1,0:T(8,128)(2,1)S(1)} %get-tuple-element.58), channel_id=1, source_target_pairs={{0,28},{1,29},{2,30},{3,31},{4,24},{5,25},{6,26},{7,27},{8,4},{9,5... | collective-permute-start | bytes 368648 | tf_op jit(solution)/shard_map/ppermute | solution.py:502
  48.4 1.3 %collective-permute-start.17 = (bf16[16,3840]{1,0:T(8,128)(2,1)S(1)}, bf16[16,3840]{1,0:T(8,128)(2,1)S(1)}, u32[]{:S(2)}, u32[]{:S(2)}) collective-permute-start(bf16[16,3840]{1,0:T(8,128)(2,1)S(1)} %get-tuple-element.59), channel_id=1, source_target_pairs={{0,30},{1,31},{2,28},{3,29},{4,26},{5,27},{6,24},{7,25},{8,6},{9,7... | collective-permute-start | bytes 368648 | tf_op jit(solution)/shard_map/ppermute | solution.py:502
  49.7 1.0 %forward_rows.1 = bf16[64,3584]{1,0:T(8,128)(2,1)} custom-call(bf16[16,3840]{1,0:T(8,128)(2,1)S(1)} %collective-permute-done.9.refs_0_, bf16[16,3840]{1,0:T(8,128)(2,1)S(1)} %collective-permute-done.10.refs_1_, bf16[16,3840]{1,0:T(8,128)(2,1)S(1)} %collective-permute-done.11.refs_2_, bf16[16,3840]{1,0:T(8,128)(2,1)S(1)} %collective-permute-done.12.refs_3_), custom_call_target="tpu_custom_call" | custom-call | flops 100000000 | bytes 1000 | tf_op jit(solution)/shard_map/forward_rows/pallas_call | solution.py:37
  50.7 3.1 %collective-permute-done.15.refs_1_ = bf16[16,3840]{1,0:T(8,128)(2,1)S(1)} collective-permute-done((bf16[16,3840]{1,0:T(8,128)(2,1)S(1)}, bf16[16,3840]{1,0:T(8,128)(2,1)S(1)}, u32[]{:S(2)}, u32[]{:S(2)}) %collective-permute-start.15) | collective-permute-done | bytes 122912 | tf_op jit(solution)/shard_map/ppermute | solution.py:502
  53.9 2.5 %collective-permute-done.16.refs_2_ = bf16[16,3840]{1,0:T(8,128)(2,1)S(1)} collective-permute-done((bf16[16,3840]{1,0:T(8,128)(2,1)S(1)}, bf16[16,3840]{1,0:T(8,128)(2,1)S(1)}, u32[]{:S(2)}, u32[]{:S(2)}) %collective-permute-start.16) | collective-permute-done | bytes 122912 | tf_op jit(solution)/shard_map/ppermute | solution.py:502
  56.4 3.0 %collective-permute-done.17.refs_3_ = bf16[16,3840]{1,0:T(8,128)(2,1)S(1)} collective-permute-done((bf16[16,3840]{1,0:T(8,128)(2,1)S(1)}, bf16[16,3840]{1,0:T(8,128)(2,1)S(1)}, u32[]{:S(2)}, u32[]{:S(2)}) %collective-permute-start.17) | collective-permute-done | bytes 122912 | tf_op jit(solution)/shard_map/ppermute | solution.py:502
  59.4 1.0 %backward_rows.1 = bf16[64,3584]{1,0:T(8,128)(2,1)} custom-call(bf16[16,3840]{1,0:T(8,128)(2,1)S(1)} %collective-permute-done.14.refs_0_, bf16[16,3840]{1,0:T(8,128)(2,1)S(1)} %collective-permute-done.15.refs_1_, bf16[16,3840]{1,0:T(8,128)(2,1)S(1)} %collective-permute-done.16.refs_2_, bf16[16,3840]{1,0:T(8,128)(2,1)S(1)} %collective-permute-done.17.refs_3_), custom_call_target="tpu_custom_call" | custom-call | flops 100000000 | bytes 1000 | tf_op jit(solution)/shard_map/backward_rows/pallas_call | solution.py:37
  (23 shorter events, 0.8 us)
Async XLA Ops:
  2.7 7.1 %collective-permute-start = (bf16[16,3840]{1,0:T(8,128)(2,1)S(1)}, bf16[16,3840]{1,0:T(8,128)(2,1)S(1)}, u32[]{:S(2)}, u32[]{:S(2)}) collective-permute-start(bf16[16,3840]{1,0:T(8,128)(2,1)S(1)} %get-tuple-element.32), channel_id=1, source_target_pairs={{0,2},{1,3},{2,0},{3,1},{4,6},{5,7},{6,4},{7,5},{8,10},{9,11},{10,... | collective-permute-start | bytes 368648 | tf_op jit(solution)/shard_map/ppermute | solution.py:484
  5.7 7.5 %collective-permute-start.1 = (bf16[16,3840]{1,0:T(8,128)(2,1)S(1)}, bf16[16,3840]{1,0:T(8,128)(2,1)S(1)}, u32[]{:S(2)}, u32[]{:S(2)}) collective-permute-start(bf16[16,3840]{1,0:T(8,128)(2,1)S(1)} %get-tuple-element.33), channel_id=1, source_target_pairs={{0,4},{1,5},{2,6},{3,7},{4,0},{5,1},{6,2},{7,3},{8,12},{9,13},{10,... | collective-permute-start | bytes 368648 | tf_op jit(solution)/shard_map/ppermute | solution.py:484
  7.2 6.0 %collective-permute-start.2 = (bf16[16,3840]{1,0:T(8,128)(2,1)S(1)}, bf16[16,3840]{1,0:T(8,128)(2,1)S(1)}, u32[]{:S(2)}, u32[]{:S(2)}) collective-permute-start(bf16[16,3840]{1,0:T(8,128)(2,1)S(1)} %get-tuple-element.34), channel_id=1, source_target_pairs={{0,6},{1,7},{2,4},{3,5},{4,2},{5,3},{6,0},{7,1},{8,14},{9,15},{10,... | collective-permute-start | bytes 368648 | tf_op jit(solution)/shard_map/ppermute | solution.py:484
  13.2 4.1 %copy-start = (bf16[1,3584,512]{2,1,0:T(8,128)(2,1)S(1)}, bf16[1,3584,512]{2,1,0:T(8,128)(2,1)}, u32[]{:S(2)}) copy-start(bf16[1,3584,512]{2,1,0:T(8,128)(2,1)} %refs_4_.1) | copy-start | bytes 11010052
  13.2 4.1 %copy-start.1 = (bf16[1,512,3584]{2,1,0:T(8,128)(2,1)S(1)}, bf16[1,512,3584]{2,1,0:T(8,128)(2,1)}, u32[]{:S(2)}) copy-start(bf16[1,512,3584]{2,1,0:T(8,128)(2,1)} %refs_5_.1) | copy-start | bytes 11010052
  13.8 3.6 %collective-permute-start.3 = (bf16[80,3584]{1,0:T(8,128)(2,1)S(1)}, bf16[80,3584]{1,0:T(8,128)(2,1)S(1)}, u32[]{:S(2)}, u32[]{:S(2)}) collective-permute-start(bf16[80,3584]{1,0:T(8,128)(2,1)S(1)} %get-tuple-element.37.refs_0_), channel_id=1, source_target_pairs={{0,1},{1,0},{2,3},{3,2},{4,5},{5,4},{6,7},{7,6},{8,9},{9,8},{10,11... | collective-permute-start | bytes 1720328 | tf_op jit(solution)/shard_map/ppermute | solution.py:491
  13.8 11.4 %collective-permute-start.5 = (bf16[32,3840]{1,0:T(8,128)(2,1)S(1)}, bf16[32,3840]{1,0:T(8,128)(2,1)S(1)}, u32[]{:S(2)}, u32[]{:S(2)}) collective-permute-start(bf16[32,3840]{1,0:T(8,128)(2,1)S(1)} %get-tuple-element.42), channel_id=1, source_target_pairs={{0,2},{1,3},{2,0},{3,1},{4,6},{5,7},{6,4},{7,5},{8,10},{9,11},{10,... | collective-permute-start | bytes 737288 | tf_op jit(solution)/shard_map/ppermute | solution.py:484
  15.0 12.8 %collective-permute-start.6 = (bf16[32,3840]{1,0:T(8,128)(2,1)S(1)}, bf16[32,3840]{1,0:T(8,128)(2,1)S(1)}, u32[]{:S(2)}, u32[]{:S(2)}) collective-permute-start(bf16[32,3840]{1,0:T(8,128)(2,1)S(1)} %get-tuple-element.43), channel_id=1, source_target_pairs={{0,4},{1,5},{2,6},{3,7},{4,0},{5,1},{6,2},{7,3},{8,12},{9,13},{10,... | collective-permute-start | bytes 737288 | tf_op jit(solution)/shard_map/ppermute | solution.py:484
  15.8 15.4 %collective-permute-start.7 = (bf16[32,3840]{1,0:T(8,128)(2,1)S(1)}, bf16[32,3840]{1,0:T(8,128)(2,1)S(1)}, u32[]{:S(2)}, u32[]{:S(2)}) collective-permute-start(bf16[32,3840]{1,0:T(8,128)(2,1)S(1)} %get-tuple-element.44), channel_id=1, source_target_pairs={{0,6},{1,7},{2,4},{3,5},{4,2},{5,3},{6,0},{7,1},{8,14},{9,15},{10,... | collective-permute-start | bytes 737288 | tf_op jit(solution)/shard_map/ppermute | solution.py:484
  18.8 2.0 %collective-permute-start.4 = (bf16[80,3584]{1,0:T(8,128)(2,1)S(1)}, bf16[80,3584]{1,0:T(8,128)(2,1)S(1)}, u32[]{:S(2)}, u32[]{:S(2)}) collective-permute-start(bf16[80,3584]{1,0:T(8,128)(2,1)S(1)} %get-tuple-element.39), channel_id=1, source_target_pairs={{0,1},{1,0},{2,3},{3,2},{4,5},{5,4},{6,7},{7,6},{8,9},{9,8},{10,11... | collective-permute-start | bytes 1720328 | tf_op jit(solution)/shard_map/ppermute | solution.py:491
  21.2 25.0 %collective-permute-start.10 = (bf16[16,3840]{1,0:T(8,128)(2,1)S(1)}, bf16[16,3840]{1,0:T(8,128)(2,1)S(1)}, u32[]{:S(2)}, u32[]{:S(2)}) collective-permute-start(bf16[16,3840]{1,0:T(8,128)(2,1)S(1)} %get-tuple-element.52), channel_id=1, source_target_pairs={{0,10},{1,11},{2,8},{3,9},{4,14},{5,15},{6,12},{7,13},{8,18},{9,19... | collective-permute-start | bytes 368648 | tf_op jit(solution)/shard_map/ppermute | solution.py:502
  23.4 24.1 %collective-permute-start.11 = (bf16[16,3840]{1,0:T(8,128)(2,1)S(1)}, bf16[16,3840]{1,0:T(8,128)(2,1)S(1)}, u32[]{:S(2)}, u32[]{:S(2)}) collective-permute-start(bf16[16,3840]{1,0:T(8,128)(2,1)S(1)} %get-tuple-element.53), channel_id=1, source_target_pairs={{0,12},{1,13},{2,14},{3,15},{4,8},{5,9},{6,10},{7,11},{8,20},{9,21... | collective-permute-start | bytes 368648 | tf_op jit(solution)/shard_map/ppermute | solution.py:502
  25.2 23.1 %collective-permute-start.12 = (bf16[16,3840]{1,0:T(8,128)(2,1)S(1)}, bf16[16,3840]{1,0:T(8,128)(2,1)S(1)}, u32[]{:S(2)}, u32[]{:S(2)}) collective-permute-start(bf16[16,3840]{1,0:T(8,128)(2,1)S(1)} %get-tuple-element.46.refs_4_), channel_id=1, source_target_pairs={{0,14},{1,15},{2,12},{3,13},{4,10},{5,11},{6,8},{7,9},{8,22},{9,23... | collective-permute-start | bytes 368648 | tf_op jit(solution)/shard_map/ppermute | solution.py:502
  31.3 2.0 %collective-permute-start.8 = (bf16[80,3584]{1,0:T(8,128)(2,1)S(1)}, bf16[80,3584]{1,0:T(8,128)(2,1)S(1)}, u32[]{:S(2)}, u32[]{:S(2)}) collective-permute-start(bf16[80,3584]{1,0:T(8,128)(2,1)S(1)} %get-tuple-element.47.refs_4_.refs_0_), channel_id=1, source_target_pairs={{0,1},{1,0},{2,3},{3,2},{4,5},{5,4},{6,7},{7,6},{8,9},{9,8},{10,11... | collective-permute-start | bytes 1720328 | tf_op jit(solution)/shard_map/ppermute | solution.py:491
  36.0 6.2 %collective-permute-start.13 = (bf16[80,3712]{1,0:T(8,128)(2,1)S(1)}, bf16[80,3712]{1,0:T(8,128)(2,1)S(1)}, u32[]{:S(2)}, u32[]{:S(2)}) collective-permute-start(bf16[80,3712]{1,0:T(8,128)(2,1)S(1)} %get-tuple-element.55), channel_id=1, source_target_pairs={{0,1},{1,0},{2,3},{3,2},{4,5},{5,4},{6,7},{7,6},{8,9},{9,8},{10,11... | collective-permute-start | bytes 1781768 | tf_op jit(solution)/shard_map/ppermute | solution.py:491
  36.7 13.0 %collective-permute-start.9 = (bf16[16,3840]{1,0:T(8,128)(2,1)S(1)}, bf16[16,3840]{1,0:T(8,128)(2,1)S(1)}, u32[]{:S(2)}, u32[]{:S(2)}) collective-permute-start(bf16[16,3840]{1,0:T(8,128)(2,1)S(1)} %finish_forward_0.1.refs_11_), channel_id=1, source_target_pairs={{0,8},{1,9},{2,10},{3,11},{4,12},{5,13},{6,14},{7,15},{8,16},{9,17... | collective-permute-start | bytes 368648 | tf_op jit(solution)/shard_map/ppermute | solution.py:502
  42.8 7.9 %collective-permute-start.14 = (bf16[16,3840]{1,0:T(8,128)(2,1)S(1)}, bf16[16,3840]{1,0:T(8,128)(2,1)S(1)}, u32[]{:S(2)}, u32[]{:S(2)}) collective-permute-start(bf16[16,3840]{1,0:T(8,128)(2,1)S(1)} %get-tuple-element.56), channel_id=1, source_target_pairs={{0,24},{1,25},{2,26},{3,27},{4,28},{5,29},{6,30},{7,31},{8,0},{9,1... | collective-permute-start | bytes 368648 | tf_op jit(solution)/shard_map/ppermute | solution.py:502
  46.2 7.7 %collective-permute-start.15 = (bf16[16,3840]{1,0:T(8,128)(2,1)S(1)}, bf16[16,3840]{1,0:T(8,128)(2,1)S(1)}, u32[]{:S(2)}, u32[]{:S(2)}) collective-permute-start(bf16[16,3840]{1,0:T(8,128)(2,1)S(1)} %get-tuple-element.57), channel_id=1, source_target_pairs={{0,26},{1,27},{2,24},{3,25},{4,30},{5,31},{6,28},{7,29},{8,2},{9,3... | collective-permute-start | bytes 368648 | tf_op jit(solution)/shard_map/ppermute | solution.py:502
  47.5 8.9 %collective-permute-start.16 = (bf16[16,3840]{1,0:T(8,128)(2,1)S(1)}, bf16[16,3840]{1,0:T(8,128)(2,1)S(1)}, u32[]{:S(2)}, u32[]{:S(2)}) collective-permute-start(bf16[16,3840]{1,0:T(8,128)(2,1)S(1)} %get-tuple-element.58), channel_id=1, source_target_pairs={{0,28},{1,29},{2,30},{3,31},{4,24},{5,25},{6,26},{7,27},{8,4},{9,5... | collective-permute-start | bytes 368648 | tf_op jit(solution)/shard_map/ppermute | solution.py:502
  48.4 11.0 %collective-permute-start.17 = (bf16[16,3840]{1,0:T(8,128)(2,1)S(1)}, bf16[16,3840]{1,0:T(8,128)(2,1)S(1)}, u32[]{:S(2)}, u32[]{:S(2)}) collective-permute-start(bf16[16,3840]{1,0:T(8,128)(2,1)S(1)} %get-tuple-element.59), channel_id=1, source_target_pairs={{0,30},{1,31},{2,28},{3,29},{4,26},{5,27},{6,24},{7,25},{8,6},{9,7... | collective-permute-start | bytes 368648 | tf_op jit(solution)/shard_map/ppermute | solution.py:502

commit v5 on v4

--- a/solution.py
+++ b/solution.py
@@ -23,8 +23,9 @@
 cost = {
     "normed_rows": 5,
     "saved_terms": 40,
+    "grad_rows": 40,
+    "finish_forward_32": 4,
     "act_norms": 40,
-    "act_gates": 40,
 }
 
 
@@ -102,80 +103,132 @@
     by_token = jnp.where(lane < tokens, lane, tokens + (lane - tokens) // 16) == slot_column
     token = lax.broadcasted_iota(jnp.int32, (tokens, fold), 0).astype(f32)
     token_row = jnp.sum(jnp.where(by_token, token - none, 0.0), axis=0, keepdims=True) + none
-    return jnp.where(by_slot, 1.0, 0.0).astype(bf16), token_row
-
-
-def write_chunks(z, selector, token_row, rows_ref, ready, tiles, chunks, base):
+    return jnp.where(by_slot, 1.0, 0.0).astype(bf16), column, slot_column, token_row
+
+
+def write_chunks(z, selector, rows_ref, ready, tiles, chunks):
     step = z.width // 2
-    tiles[...] = jnp.zeros_like(tiles)
     for half in range(2):
         ready[half].wait()
         col = half * step
         got = jnp.dot(selector, rows_ref[:, col : col + step], preferred_element_type=f32)
         packed = got[: z.tokens].astype(bf16)
         for k in range(z.experts):
-            chunks[k][base : base + 16, col : col + step] = packed[k * z.main : (k + 1) * z.main]
+            chunks[k][:, col : col + step] = packed[k * z.main : (k + 1) * z.main]
             pack_last(got[z.tokens + k : z.tokens + k + 1], tiles.at[k], half * z.pieces // 2)
-    for k in range(z.experts):
-        tiles[k, z.pieces : z.pieces + 1, :] = token_row
-        chunks[k][base : base + 16, z.width :] = tiles[k].astype(bf16)
-
-
-def make_chunks(z, where, ids, sources, tables, after, name):
-    count = len(sources)
-
-    def body(where, ids_any, *refs):
-        anys, tables_any = refs[:count], refs[count : count + len(tables)]
-        outs, held = refs[count + len(tables) + len(after) :], ()
-        if tables:
-            *outs, gain_ref, router_ref, ids, rows, tiles, sems = outs
-            *outs, vectors = outs
-            held = (gain_ref, router_ref)
-        else:
-            *outs, ids, rows, tiles, sems = outs
-        copies = [pltpu.make_async_copy(ids_any, ids, sems.at[2 * count])]
-        step = z.width // 2
-        for j in range(count):
-            for half in range(2):
-                cols = pl.ds(half * step, step)
-                copies.append(
-                    pltpu.make_async_copy(
-                        anys[j].at[:, cols], rows.at[j, :, cols], sems.at[2 * j + half]
-                    )
-                )
-        for i, (source, target) in enumerate(zip(tables_any, held)):
-            copies.append(pltpu.make_async_copy(source, target, sems.at[2 * count + 1 + i]))
-        for copy in copies:
+
+
+def halves(z, source, target, sems, at):
+    step = z.width // 2
+    return [
+        pltpu.make_async_copy(
+            source.at[:, pl.ds(i * step, step)], target.at[:, pl.ds(i * step, step)], sems.at[at + i]
+        )
+        for i in range(2)
+    ]
+
+
+def forward_chunks(z, where, ids, act, held):
+    def body(where, ids_any, act_any, held_any, *refs):
+        *chunks, held, ids, rows, tiles, sems = refs
+        first = pltpu.make_async_copy(ids_any, ids, sems.at[2])
+        ready = halves(z, act_any, rows, sems, 0)
+        extra = pltpu.make_async_copy(held_any, held, sems.at[3])
+        for copy in [first, *ready, extra]:
             copy.start()
-        copies[0].wait()
-        selector, token_row = slot_matrices(ids[...], where[0], z)
-        for j in range(count):
-            ready = copies[1 + 2 * j : 3 + 2 * j]
-            write_chunks(z, selector, token_row, rows.at[j], ready, tiles, outs, 16 * j)
-        if tables:
-            for copy in copies[1 + 2 * count :]:
-                copy.wait()
-            vectors[...] = jnp.zeros_like(vectors)
-            vectors[0:1, :] = gain_ref[...].astype(f32)
-            mine = lax.broadcasted_iota(jnp.int32, (z.experts, 1), 0) == where[0]
-            table = jnp.where(mine, router_ref[0].astype(f32), 0.0)
-            vectors[1:2, :] = jnp.sum(table, axis=0, keepdims=True)
-
-    return call(
-        body,
-        "sh" + "h" * (count + len(tables)) + "a" * len(after),
-        [shape((z.main * count, z.wide))] * z.experts
-        + [shape((8, z.width), f32) for _ in tables[:1]],
-        [pltpu.VMEM(table.shape, bf16) for table in tables]
-        + [
+        tiles[...] = jnp.zeros_like(tiles)
+        first.wait()
+        selector, _, _, token_row = slot_matrices(ids[...], where[0], z)
+        write_chunks(z, selector, rows, ready, tiles, chunks)
+        for k in range(z.experts):
+            tiles[k, z.pieces : z.pieces + 1, :] = token_row
+            chunks[k][:, z.width :] = tiles[k].astype(bf16)
+        extra.wait()
+
+    *chunks, held = call(
+        body,
+        "shhh",
+        [shape((z.main, z.wide))] * z.experts + [shape(held.shape)],
+        [
             pltpu.VMEM((1, z.tokens), jnp.int32),
-            pltpu.VMEM((count, z.tokens, z.width), bf16),
+            pltpu.VMEM((z.tokens, z.width), bf16),
             pltpu.VMEM((z.experts, 16, fold), f32),
-            pltpu.SemaphoreType.DMA((2 * count + 1 + len(tables),)),
+            pltpu.SemaphoreType.DMA((4,)),
         ],
         8,
-        name,
-    )(where, ids.reshape(1, z.tokens), *sources, *tables, *after)
+        "forward_chunks",
+    )(where, ids.reshape(1, z.tokens), act, held)
+    return chunks, held
+
+
+def two_parts(value):
+    high = value.astype(bf16).astype(f32)
+    return [high, (value - high).astype(bf16).astype(f32)]
+
+
+def backward_chunks(z, where, ids, grad, act, gain, router):
+    def body(where, ids_any, grad_any, act_ref, gain_any, router_any, *refs):
+        *chunks, vectors, ids, rows, tiles, gain_ref, router_ref, sems = refs
+        first = pltpu.make_async_copy(ids_any, ids, sems.at[2])
+        ready = halves(z, grad_any, rows, sems, 0)
+        tables = [
+            pltpu.make_async_copy(gain_any, gain_ref, sems.at[3]),
+            pltpu.make_async_copy(router_any.at[0], router_ref, sems.at[4]),
+        ]
+        for copy in [first, *tables, *ready]:
+            copy.start()
+        tiles[...] = jnp.zeros_like(tiles)
+        first.wait()
+        selector, column, slot_column, token_row = slot_matrices(ids[...], where[0], z)
+        for copy in tables:
+            copy.wait()
+        gain = gain_ref[...].astype(f32)
+        h = act_ref[...].astype(f32)
+        normed, inv = norm_rows(h, gain)
+        logits = lax.dot_general(normed, router_ref[...], nt, preferred_element_type=f32)
+        expert = lax.broadcasted_iota(jnp.int32, logits.shape, 1)
+        named = jnp.bitwise_xor(column, where[0])
+        logit = jnp.sum(jnp.where(expert == named, logits, 0.0), axis=-1, keepdims=True)
+        write_chunks(z, selector, rows, ready, tiles, chunks)
+        centre = jnp.mean(rows[...].astype(f32) * h, axis=-1, keepdims=True)
+        parts = two_parts(inv) + two_parts(jax.nn.sigmoid(logit)) + two_parts(centre)
+        lane = lax.broadcasted_iota(jnp.int32, (z.tokens, fold), 1)
+        token = lax.broadcasted_iota(jnp.int32, (z.tokens, fold), 0).astype(f32)
+        values = jnp.zeros((z.tokens, fold), f32)
+        for i, part in enumerate(parts):
+            values = jnp.where(lane // 32 == i, part, values)
+        place = lane % 32
+        for k in range(z.experts):
+            slot = jnp.where(place < z.main, k * z.main + place, z.tokens + k)
+            mine = (slot == slot_column) & (place <= z.main)
+            own_tokens = jnp.sum(jnp.where(mine, token - none, 0.0), axis=0, keepdims=True) + none
+            scalars = jnp.sum(jnp.where(mine, values, 0.0), axis=0, keepdims=True)
+            both = jnp.where(lane[0:1] < 128, token_row, own_tokens)
+            tiles[k, z.pieces : z.pieces + 1, :] = both
+            tiles[k, z.pieces + 1 : z.pieces + 2, :] = scalars
+            chunks[k][:, z.width :] = tiles[k].astype(bf16)
+        vectors[...] = jnp.zeros_like(vectors)
+        vectors[0:1, :] = gain
+        mine = lax.broadcasted_iota(jnp.int32, (z.experts, 1), 0) == where[0]
+        table = jnp.where(mine, router_ref[...].astype(f32), 0.0)
+        vectors[1:2, :] = jnp.sum(table, axis=0, keepdims=True)
+
+    *chunks, vectors = call(
+        body,
+        "shhvhh",
+        [shape((z.main, z.wide))] * z.experts + [shape((8, z.width), f32)],
+        [
+            pltpu.VMEM((1, z.tokens), jnp.int32),
+            pltpu.VMEM((z.tokens, z.width), bf16),
+            pltpu.VMEM((z.experts, 16, fold), f32),
+            pltpu.VMEM((1, z.width), bf16),
+            pltpu.VMEM((z.experts, z.width), bf16),
+            pltpu.SemaphoreType.DMA((5,)),
+        ],
+        12,
+        "backward_chunks",
+    )(where, ids.reshape(1, z.tokens), grad, act, gain, router)
+    return chunks, vectors
 
 
 def collect_rows(z, chunks, last, tile, base=0):
@@ -214,62 +267,55 @@
 
 def grad_rows_of(z, chunks, after):
     def body(*refs):
-        chunks, (rows, last, tile) = refs[: z.experts], refs[z.experts + len(after) :]
+        chunks, (rows, last, inv_ref, affinity_ref, tile) = (
+            refs[: z.experts],
+            refs[z.experts + len(after) :],
+        )
         for k in range(z.experts):
-            rows[k * z.main : (k + 1) * z.main, :] = chunks[k][:16, : z.width]
+            rows[k * z.main : (k + 1) * z.main, :] = chunks[k][:, : z.width]
         collect_rows(z, chunks, last, tile)
         rows[z.tokens :, :] = last[...].astype(bf16)
+        sub = lax.broadcasted_iota(jnp.int32, (16, fold), 0)
+        lane = lax.broadcasted_iota(jnp.int32, (16, fold), 1)
+        scalars = [
+            chunk[:, z.width :].astype(f32)[z.pieces + 1 : z.pieces + 2, :] for chunk in chunks
+        ]
+        for first, out in ((0, inv_ref), (64, affinity_ref)):
+            place = lane - first
+            tail = jnp.zeros((16, fold), f32)
+            for k in range(z.experts):
+                mine = (place == sub) | (place == sub + 32)
+                column = jnp.sum(jnp.where(mine, scalars[k], 0.0), axis=-1, keepdims=True)
+                out[k * z.main : (k + 1) * z.main, :] = jnp.broadcast_to(column, (16, 128))
+                mine = ((place == z.main) | (place == z.main + 32)) & (sub == k)
+                tail = tail + jnp.where(mine, scalars[k], 0.0)
+            column = jnp.sum(tail, axis=-1, keepdims=True)
+            out[z.tokens :, :] = jnp.broadcast_to(column, (16, 128))
 
     return call(
         body,
         "v" * z.experts + "a" * len(after),
-        [shape((z.rows, z.width)), shape((16, z.width), f32)],
+        [shape((z.rows, z.width)), shape((16, z.width), f32)] + [shape((z.rows, 128), f32)] * 2,
         [pltpu.VMEM((16, fold), f32)],
         8,
         "grad_rows",
     )(*chunks, *after)
 
 
-def act_norms(z, chunks, after):
-    def body(*refs):
-        chunks, (inv_ref, last, tile) = refs[: z.experts], refs[z.experts + len(after) :]
-        collect_rows(z, chunks, last, tile, 16)
-        for k in range(z.experts + 1):
-            h = last[...] if k == z.experts else chunks[k][16:32, : z.width].astype(f32)
-            at = k * z.main
-            inv = lax.rsqrt(jnp.mean(h * h, axis=-1, keepdims=True) + epsilon)
-            inv_ref[at : at + 16, :] = jnp.broadcast_to(inv, (16, 128))
-
-    return call(
-        body,
-        "v" * z.experts + "a" * len(after),
-        [shape((z.rows, 128), f32), shape((16, z.width), f32)],
-        [pltpu.VMEM((16, fold), f32)],
+def act_norms(z, act, after):
+    def body(act_ref, *refs):
+        h = act_ref[...].astype(f32)
+        square = 1.0 / (jnp.mean(h * h, axis=-1, keepdims=True) + epsilon)
+        refs[-1][...] = jnp.broadcast_to(square, (z.tokens, 128))
+
+    return call(
+        body,
+        "v" + "a" * len(after),
+        shape((z.tokens, 128), f32),
+        [],
         8,
         "act_norms",
-    )(*chunks, *after)
-
-
-def act_gates(z, chunks, last, inv, vectors, after):
-    def body(*refs):
-        chunks, (last, inv_ref, vectors) = refs[: z.experts], refs[z.experts : z.experts + 3]
-        affinity_ref = refs[-1]
-        gain, router = vectors[0:1, :], vectors[1:2, :]
-        for k in range(z.experts + 1):
-            h = last[...] if k == z.experts else chunks[k][16:32, : z.width].astype(f32)
-            at = k * z.main
-            normed = (h * inv_ref[at : at + 16, 0:1] * gain).astype(bf16).astype(f32)
-            logits = jnp.sum(normed * router, axis=-1, keepdims=True)
-            affinity_ref[at : at + 16, :] = jnp.broadcast_to(jax.nn.sigmoid(logits), (16, 128))
-
-    return call(
-        body,
-        "v" * (z.experts + 3) + "a" * len(after),
-        shape((z.rows, 128), f32),
-        [],
-        8,
-        "act_gates",
-    )(*chunks, last, inv, vectors, *after)
+    )(act, *after)
 
 
 def write_parts(z, values, outs, col):
@@ -363,10 +409,8 @@
 
 
 def put_last(z, values, source_chunk, tile, out):
-    tile[...] = jnp.zeros_like(tile)
+    tile[...] = source_chunk[:, z.width :].astype(f32)
     pack_last(values, tile)
-    tokens = source_chunk[:16, z.width :].astype(f32)
-    tile[z.pieces : z.pieces + 1, :] = tokens[z.pieces : z.pieces + 1, :]
     out[:, z.width :] = tile[...].astype(bf16)
 
 
@@ -399,16 +443,16 @@
     )(*[chunks[k] for k in ks], last, *parts, gates, *after)
 
 
-def finish_backward(z, order, chunks, lasts, terms, parts, vectors, after):
+def finish_backward(z, order, chunks, last, terms, parts, vectors, after):
     def body(*refs):
         e = z.experts
-        chunks, (last_grad, last_act, inv_ref, affinity_ref) = refs[:e], refs[e : e + 4]
-        parts, vectors = refs[e + 4 : e + 4 + z.split], refs[e + 4 + z.split]
+        chunks, (last, inv_ref, affinity_ref) = refs[:e], refs[e : e + 3]
+        parts, vectors = refs[e + 3 : e + 3 + z.split], refs[e + 3 + z.split]
         outs, (tile,) = refs[-1 - e : -1], refs[-1:]
-        outs = [outs[order.index(k)] for k in range(e)]
         gain, router = vectors[0:1, :], vectors[1:2, :]
-
-        def finished(h, g, at):
+        gain_router = gain * router
+
+        def finished(g, at):
             inv, affinity = inv_ref[at : at + 16, 0:1], affinity_ref[at : at + 16, 0:1]
             rows = parts[0][at : at + 16, : z.width].astype(f32)
             dot = parts[0][at : at + 16, z.width :].astype(f32)
@@ -417,51 +461,63 @@
                 dot = dot + part[at : at + 16, z.width :].astype(f32)
             dot = dot[:, 0:1]
             grad_logits = (route_scale * dot * affinity * (1.0 - affinity)).astype(bf16).astype(f32)
-            grad_pre = (route_scale * affinity * rows + grad_logits * router) * gain
-            centre = jnp.mean(grad_pre * h, axis=-1, keepdims=True)
-            return g + inv * (grad_pre - h * (inv * inv * centre))
-
-        tail = finished(last_act[...], last_grad[...], z.tokens)
-        for k in range(e):
-            g = chunks[k][:16, : z.width].astype(f32)
-            h = chunks[k][16:32, : z.width].astype(f32)
-            outs[k][:, : z.width] = finished(h, g, k * z.main).astype(bf16)
-            put_last(z, tail[k : k + 1, :], chunks[k], tile, outs[k])
-
-    return call(
-        body,
-        "v" * (z.experts + z.split + 5) + "a" * len(after),
+            rows = rows * gain * (inv * route_scale * affinity)
+            return g + (rows + gain_router * (inv * grad_logits))
+
+        tail = finished(last[...], z.tokens)
+        for k, out in zip(order, outs):
+            g = chunks[k][:, : z.width].astype(f32)
+            out[:, : z.width] = finished(g, k * z.main).astype(bf16)
+            put_last(z, tail[k : k + 1, :], chunks[k], tile, out)
+
+    return call(
+        body,
+        "v" * (z.experts + z.split + 4) + "a" * len(after),
         [shape((z.main, z.wide))] * z.experts,
         [pltpu.VMEM((16, fold), f32)],
         8,
         "finish_backward",
-    )(*chunks, *lasts, *terms, *parts, vectors, *after)
-
-
-def order_rows(z, chunks, name):
+    )(*chunks, last, *terms, *parts, vectors, *after)
+
+
+def order_matrices(z, chunks):
     lanes = z.tokens + 16 * z.experts
+    tiles = [chunk[:, z.width :] for chunk in chunks]
+    token_row = tiles[0].astype(f32)[z.pieces : z.pieces + 1, :lanes]
+    token = lax.broadcasted_iota(jnp.int32, (z.tokens, lanes), 0).astype(f32)
+    lane = lax.broadcasted_iota(jnp.int32, (z.tokens, lanes), 1)
+    piece = jnp.where(lane < z.tokens, -1, lane % 16)
+    ours = token == token_row
+    for i in range(z.pieces):
+        cols = pl.ds(i * fold, fold)
+        selector = jnp.where(ours & ((piece < 0) | (piece == i)), 1.0, 0.0).astype(bf16)
+        rows = jnp.concatenate([chunk[:, cols] for chunk in chunks] + tiles, axis=0)
+        yield cols, jnp.dot(selector, rows, preferred_element_type=f32)
+
+
+def write_out(z, out, out_any, sems, steps):
+    width = z.width // steps
+    copies = []
+
+    def next_copy():
+        cols = pl.ds(len(copies) * width, width)
+        copy = pltpu.make_async_copy(out.at[:, cols], out_any.at[:, cols], sems.at[len(copies)])
+        copy.start()
+        copies.append(copy)
+
+    return copies, next_copy
+
+
+def order_forward(z, chunks):
     steps = 7 if z.pieces % 7 == 0 else z.pieces
 
     def body(*refs):
         chunks, (out_any, out, sems) = refs[: z.experts], refs[z.experts :]
-        tiles = [chunk[:, z.width :] for chunk in chunks]
-        token_row = tiles[0].astype(f32)[z.pieces : z.pieces + 1, :lanes]
-        token = lax.broadcasted_iota(jnp.int32, (z.tokens, lanes), 0).astype(f32)
-        lane = lax.broadcasted_iota(jnp.int32, (z.tokens, lanes), 1)
-        piece = jnp.where(lane < z.tokens, -1, lane % 16)
-        ours = token == token_row
-        copies = []
-        for i in range(z.pieces):
-            cols = pl.ds(i * fold, fold)
-            mine = ours & ((piece < 0) | (piece == i))
-            selector = jnp.where(mine, 1.0, 0.0).astype(bf16)
-            rows = jnp.concatenate([chunk[:, cols] for chunk in chunks] + tiles, axis=0)
-            out[:, cols] = jnp.dot(selector, rows, preferred_element_type=f32).astype(bf16)
+        copies, next_copy = write_out(z, out, out_any, sems, steps)
+        for i, (cols, rows) in enumerate(order_matrices(z, chunks)):
+            out[:, cols] = rows.astype(bf16)
             if (i + 1) % (z.pieces // steps) == 0:
-                done = pl.ds((i + 1) * fold - z.width // steps, z.width // steps)
-                copy = pltpu.make_async_copy(out.at[:, done], out_any.at[:, done], sems.at[len(copies)])
-                copy.start()
-                copies.append(copy)
+                next_copy()
         for copy in copies:
             copy.wait()
 
@@ -471,9 +527,53 @@
         shape((z.tokens, z.width)),
         [pltpu.VMEM((z.tokens, z.width), bf16), pltpu.SemaphoreType.DMA((steps,))],
         8,
-        name,
+        "forward_rows",
         spaces["a"],
     )(*chunks)
+
+
+def order_backward(z, chunks, act, squares):
+    steps = 7 if z.pieces % 7 == 0 else z.pieces
+
+    def body(*refs):
+        chunks = refs[: z.experts]
+        act, squares, out_any, out, held, sems = refs[z.experts :]
+        copies, next_copy = write_out(z, out, out_any, sems, steps)
+        total = jnp.zeros((z.tokens, fold), f32)
+        for cols, rows in order_matrices(z, chunks):
+            held[:, cols] = rows
+            total = total + rows * act[:, cols].astype(f32)
+        lanes = pl.ds(z.width + 128, 128)
+        token = lax.broadcasted_iota(jnp.int32, (z.tokens, 128), 0).astype(f32)
+        lane = lax.broadcasted_iota(jnp.int32, (z.tokens, 128), 1)
+        centre = jnp.zeros((z.tokens, 128), f32)
+        for chunk in chunks:
+            tile = chunk[:, lanes].astype(f32)
+            mine = (tile[z.pieces : z.pieces + 1, :] == token) & (lane < 64)
+            centre = centre + jnp.where(mine, tile[z.pieces + 1 : z.pieces + 2, :], 0.0)
+        mean = jnp.sum(total, axis=-1, keepdims=True) * (1.0 / z.width)
+        scale = squares[:, 0:1] * (mean - jnp.sum(centre, axis=-1, keepdims=True))
+        width = z.width // steps
+        for i in range(steps):
+            cols = pl.ds(i * width, width)
+            out[:, cols] = (held[:, cols] - act[:, cols].astype(f32) * scale).astype(bf16)
+            next_copy()
+        for copy in copies:
+            copy.wait()
+
+    return call(
+        body,
+        "v" * (z.experts + 2),
+        shape((z.tokens, z.width)),
+        [
+            pltpu.VMEM((z.tokens, z.width), bf16),
+            pltpu.VMEM((z.tokens, z.width), f32),
+            pltpu.SemaphoreType.DMA((steps,)),
+        ],
+        8,
+        "backward_rows",
+        spaces["a"],
+    )(*chunks, act, squares)
 
 
 def dispatch(z, chunks):
@@ -513,48 +613,41 @@
     router = jnp.swapaxes(router, 1, 2)
     others = range(1, z.split)
 
-    fwd_chunks = make_chunks(z, where, fwd_ids, [fwd_act], [], [], "forward_chunks")
+    fwd_chunks, held = forward_chunks(z, where, fwd_ids, fwd_act, bwd_act)
     fwd_own = dispatch(z, fwd_chunks)
-    *bwd_chunks, vectors = make_chunks(
-        z,
-        where,
-        bwd_ids,
-        [bwd_grad, bwd_act],
-        [norm_gain, router],
-        [fwd_chunks[0]],
-        "backward_chunks",
-    )
+    next_act = to_section(z, held, 0, -1)
+    bwd_chunks, vectors = backward_chunks(z, where, bwd_ids, bwd_grad, held, norm_gain, router)
     bwd_own = dispatch(z, bwd_chunks)
 
     normed, gates, fwd_last = normed_rows(z, fwd_own, vectors)
     fwd_all = [normed] + [to_core(z, normed, m) for m in others]
-    fwd_parts = experts_forward(z, fwd_all, w_gate, w_down, [])
-    hidden, slope = saved_terms(z, where, saved_gate, [fwd_parts[0]])
+    hidden, slope = saved_terms(z, where, saved_gate, [gates])
+    fwd_parts = experts_forward(z, fwd_all, w_gate, w_down, [hidden])
+    grads, grad_last, inv, affinity = grad_rows_of(z, bwd_own, [fwd_parts[0]])
+    grad_all = [grads] + [to_core(z, grads, m) for m in others]
     fwd_parts = [fwd_parts[0]] + [to_core(z, fwd_parts[m], m) for m in others]
     fwd_done = {}
 
     def finish(ks, after):
-        outs = finish_forward(z, ks, [fwd_own[k] for k in range(z.experts)], fwd_last, fwd_parts, gates, after)
+        outs = finish_forward(z, ks, fwd_own, fwd_last, fwd_parts, gates, after)
         for k, out in zip(ks, outs):
             fwd_done[k] = to_section(z, out, k, 1)
         return outs[0]
 
     order = [*range(z.experts - 1, 0, -1), 0]
-    first = finish(order[:-1], [hidden])
-    grads, grad_last = grad_rows_of(z, bwd_own, [first])
-    grad_all = [grads] + [to_core(z, grads, m) for m in others]
-    inv, act_last = act_norms(z, bwd_own, [grads])
-    bwd_parts = experts_backward(z, grad_all, hidden, slope, w_gate, w_down, [inv])
-    affinity = act_gates(z, bwd_own, act_last, inv, vectors, [bwd_parts[0]])
-    third = finish(order[-1:], [affinity])
+    first = finish(order[:2], [grads, next_act])
+    bwd_parts = experts_backward(z, grad_all, hidden, slope, w_gate, w_down, [first])
+    squares = act_norms(z, next_act, [bwd_parts[0], *fwd_done.values()])
+    second = finish(order[2:], [squares])
     bwd_parts = [bwd_parts[0]] + [to_core(z, bwd_parts[m], m) for m in others]
     bwd_out = finish_backward(
-        z, order, bwd_own, [grad_last, act_last], [inv, affinity], bwd_parts, vectors, [third]
+        z, order, bwd_own, grad_last, [inv, affinity], bwd_parts, vectors, [second]
     )
     bwd_done = {k: to_section(z, out, k, -1) for k, out in zip(order, bwd_out)}
-    bwd_done = [bwd_done[k] for k in range(z.experts)]
-    fwd_done = [fwd_done[k] for k in range(z.experts)]
-    return (order_rows(z, fwd_done, "forward_rows"), order_rows(z, bwd_done, "backward_rows"))
+    return (
+        order_forward(z, [fwd_done[k] for k in range(z.experts)]),
+        order_backward(z, [bwd_done[k] for k in range(z.experts)], next_act, squares),
+    )
 
 
 def solution(mesh):

time: 60.6 us -> 59.2 us (0.977)
  starting transfers between devices: 27.3 us -> 24.1 us
  local copies, waits for them, and re-layouts: 0.01 us -> 1.22 us
    ppermute x8 -> x9, waiting for transfers between devices: 8.75 us -> 16.7 us  [to_section(): return lax.ppermute(chunk, ('pp', 'ep'), pairs)]
    ppermute x6, waiting for transfers between devices: 6.88 us -> 0.02 us  [dispatch(): got[k] = lax.ppermute(chunks[k], 'ep', pairs)]
    ppermute x8 -> x9, starting transfers between devices: 18.8 us -> 15.2 us  [to_section(): return lax.ppermute(chunk, ('pp', 'ep'), pairs)]
    unnamed x4, local copies, waits for them, and re-layouts: 0.01 us -> 1.22 us
    ppermute x4, waiting for transfers between devices: 2 us -> 1.32 us  [to_core(): return lax.ppermute(array, 'ep', pairs)]
    pallas_call x14 -> x13, Pallas kernels: 14.6 us -> 14.8 us  [run(): return kernel(*arrays)]
  transfers between devices with their start and end apart: 18 -> 19, of which waited for: 8 -> 7; matrix products, arithmetic and copies ran while one was open for 0% -> 0% of each run, Pallas kernels for 18% -> 19%
where the time goes in v5:
time: 59.2 us; the launch traced here: 59 us
  starting transfers between devices  24.1 us (41%)
  waiting for transfers between devices  18.1 us (31%)
  Pallas kernels  14.8 us (25%)
  local copies, waits for them, and re-layouts  1.22 us (2%)
  between operations  0.8 us (1%)
    ppermute x9, waiting for transfers between devices, to_section(): return lax.ppermute(chunk, ('pp', 'ep'), pairs)  16.7 us
    ppermute x9, starting transfers between devices, to_section(): return lax.ppermute(chunk, ('pp', 'ep'), pairs)  15.2 us
    pallas_call x13, Pallas kernels, run(): return kernel(*arrays)  14.8 us
    ppermute x6, starting transfers between devices, dispatch(): got[k] = lax.ppermute(chunks[k], 'ep', pairs)  8.1 us
    ppermute x4, waiting for transfers between devices, to_core(): return lax.ppermute(array, 'ep', pairs)  1.32 us
    unnamed x4, local copies, waits for them, and re-layouts  1.22 us
  transfers between devices with their start and end apart: 19, of which 7 were waited for; matrix products, arithmetic and copies ran while one was open for 0% of the time, Pallas kernels for 19%

profile of v5, /device:TPU:0, one launch (start us, length us, event | category | flops | bytes accessed | tf_op | source)
XLA Modules:
  0.0 59.0 jit_solution(12569633102473718707)
XLA Ops:
  0.7 2.0 %forward_chunks.1 = (bf16[16,3840]{1,0:T(8,128)(2,1)S(1)}, bf16[16,3840]{1,0:T(8,128)(2,1)S(1)}, bf16[16,3840]{1,0:T(8,128)(2,1)S(1)}, bf16[16,3840]{1,0:T(8,128)(2,1)S(1)}, bf16[64,3584]{1,0:T(8,128)(2,1)S(1)}) custom-call(s32[2]{0:T(128)S(1)} %pad_add_fusion.where, s32[1,64]{1,0:T(1,128)} %bitcast.6, bf16[64,3584]{1,0:T(8,128)(2,1)} %act_any.1, ...), custom_call_target="tpu_custom_call" | custom-call | flops 100000000 | bytes 1000 | tf_op jit(solution)/shard_map/forward_chunks/pallas_call | solution.py:38
  2.7 3.0 %collective-permute-start = (bf16[16,3840]{1,0:T(8,128)(2,1)S(1)}, bf16[16,3840]{1,0:T(8,128)(2,1)S(1)}, u32[]{:S(2)}, u32[]{:S(2)}) collective-permute-start(bf16[16,3840]{1,0:T(8,128)(2,1)S(1)} %get-tuple-element.33), channel_id=1, source_target_pairs={{0,2},{1,3},{2,0},{3,1},{4,6},{5,7},{6,4},{7,5},{8,10},{9,11},{10,... | collective-permute-start | bytes 368648 | tf_op jit(solution)/shard_map/ppermute | solution.py:584
  5.7 1.5 %collective-permute-start.1 = (bf16[16,3840]{1,0:T(8,128)(2,1)S(1)}, bf16[16,3840]{1,0:T(8,128)(2,1)S(1)}, u32[]{:S(2)}, u32[]{:S(2)}) collective-permute-start(bf16[16,3840]{1,0:T(8,128)(2,1)S(1)} %get-tuple-element.35), channel_id=1, source_target_pairs={{0,4},{1,5},{2,6},{3,7},{4,0},{5,1},{6,2},{7,3},{8,12},{9,13},{10,... | collective-permute-start | bytes 368648 | tf_op jit(solution)/shard_map/ppermute | solution.py:584
  7.3 4.1 %collective-permute-start.5 = (bf16[64,3584]{1,0:T(8,128)(2,1)S(1)}, bf16[64,3584]{1,0:T(8,128)(2,1)S(1)}, u32[]{:S(2)}, u32[]{:S(2)}) collective-permute-start(bf16[64,3584]{1,0:T(8,128)(2,1)S(1)} %get-tuple-element.37.act_ref), channel_id=1, source_target_pairs={{0,24},{1,25},{2,26},{3,27},{4,28},{5,29},{6,30},{7,31},{8,0},{9,1... | collective-permute-start | bytes 1376264 | tf_op jit(solution)/shard_map/ppermute | solution.py:602
  11.3 2.6 %backward_chunks.1 = (bf16[16,3840]{1,0:T(8,128)(2,1)S(1)}, bf16[16,3840]{1,0:T(8,128)(2,1)S(1)}, bf16[16,3840]{1,0:T(8,128)(2,1)S(1)}, bf16[16,3840]{1,0:T(8,128)(2,1)S(1)}, f32[8,3584]{1,0:T(8,128)S(1)}) custom-call(s32[2]{0:T(128)S(1)} %pad_add_fusion.where, s32[1,64]{1,0:T(1,128)} %bitcast.7, bf16[64,3584]{1,0:T(8,128)(2,1)} %grad_any.1, ...), custom_call_target="tpu_custom_call" | custom-call | flops 100000000 | bytes 1000 | tf_op jit(solution)/shard_map/backward_chunks/pallas_call | solution.py:38
  14.0 1.6 %collective-permute-start.6 = (bf16[16,3840]{1,0:T(8,128)(2,1)S(1)}, bf16[16,3840]{1,0:T(8,128)(2,1)S(1)}, u32[]{:S(2)}, u32[]{:S(2)}) collective-permute-start(bf16[16,3840]{1,0:T(8,128)(2,1)S(1)} %get-tuple-element.46), channel_id=1, source_target_pairs={{0,2},{1,3},{2,0},{3,1},{4,6},{5,7},{6,4},{7,5},{8,10},{9,11},{10,... | collective-permute-start | bytes 368648 | tf_op jit(solution)/shard_map/ppermute | solution.py:584
  15.5 1.5 %collective-permute-start.7 = (bf16[16,3840]{1,0:T(8,128)(2,1)S(1)}, bf16[16,3840]{1,0:T(8,128)(2,1)S(1)}, u32[]{:S(2)}, u32[]{:S(2)}) collective-permute-start(bf16[16,3840]{1,0:T(8,128)(2,1)S(1)} %get-tuple-element.47), channel_id=1, source_target_pairs={{0,4},{1,5},{2,6},{3,7},{4,0},{5,1},{6,2},{7,3},{8,12},{9,13},{10,... | collective-permute-start | bytes 368648 | tf_op jit(solution)/shard_map/ppermute | solution.py:584
  17.0 0.5 collective-permute-start.8
  17.5 0.5 normed_rows.1
  18.1 2.0 %saved_terms.1 = (bf16[160,512]{1,0:T(8,128)(2,1)S(1)}, f32[160,512]{1,0:T(8,128)S(1)}) custom-call(s32[2]{0:T(128)S(1)} %pad_add_fusion.where, bf16[1,1,136,512]{3,2,1,0:T(8,128)(2,1)} %saved_any.1, f32[80,128]{1,0:T(8,128)S(1)} %get-tuple-element.41.refs_0_.refs_5_), custom_call_target="tpu_custom_call" | custom-call | flops 40000000000 | bytes 1000 | tf_op jit(solution)/shard_map/saved_terms/pallas_call | solution.py:38
  20.2 1.1 %copy-done.1 = bf16[1,512,3584]{2,1,0:T(8,128)(2,1)S(1)} copy-done((bf16[1,512,3584]{2,1,0:T(8,128)(2,1)S(1)}, bf16[1,512,3584]{2,1,0:T(8,128)(2,1)}, u32[]{:S(2)}) %copy-start.1) | copy-done | bytes 3670040
  21.3 1.5 %experts_forward.1 = (bf16[80,3584]{1,0:T(8,128)(2,1)S(1)}, bf16[80,3584]{1,0:T(8,128)(2,1)S(1)}) custom-call(bf16[80,3584]{1,0:T(8,128)(2,1)S(1)} %get-tuple-element.40.refs_0_, bf16[80,3584]{1,0:T(8,128)(2,1)S(1)} %collective-permute-done.3.refs_1_, bf16[1,3584,512]{2,1,0:T(8,128)(2,1)S(1)} %copy-done, bf16[1,512,3584]{2,1,0:T(8,128)(2,1)S(1)} %copy-done.1, ...), custom_call_target="tpu_custom_call" | custom-call | flops 100000000 | bytes 1000 | tf_op jit(solution)/shard_map/experts_forward/pallas_call | solution.py:38
  22.8 0.6 collective-permute-start.4
  23.6 1.3 %collective-permute-done.4.refs_4_ = bf16[80,3584]{1,0:T(8,128)(2,1)S(1)} collective-permute-done((bf16[80,3584]{1,0:T(8,128)(2,1)S(1)}, bf16[80,3584]{1,0:T(8,128)(2,1)S(1)}, u32[]{:S(2)}, u32[]{:S(2)}) %collective-permute-start.4) | collective-permute-done | bytes 573472 | tf_op jit(solution)/shard_map/ppermute | solution.py:591
  24.9 0.2 finish_forward_32.1
  25.2 0.4 collective-permute-start.10
  25.5 1.8 %collective-permute-start.11 = (bf16[16,3840]{1,0:T(8,128)(2,1)S(1)}, bf16[16,3840]{1,0:T(8,128)(2,1)S(1)}, u32[]{:S(2)}, u32[]{:S(2)}) collective-permute-start(bf16[16,3840]{1,0:T(8,128)(2,1)S(1)} %get-tuple-element.53), channel_id=1, source_target_pairs={{0,12},{1,13},{2,14},{3,15},{4,8},{5,9},{6,10},{7,11},{8,20},{9,21... | collective-permute-start | bytes 368648 | tf_op jit(solution)/shard_map/ppermute | solution.py:602
  27.3 2.6 %experts_backward.1 = (bf16[80,3712]{1,0:T(8,128)(2,1)S(1)}, bf16[80,3712]{1,0:T(8,128)(2,1)S(1)}) custom-call(bf16[80,3584]{1,0:T(8,128)(2,1)S(1)} %get-tuple-element.49.refs_6_.refs_0_, bf16[80,3584]{1,0:T(8,128)(2,1)S(1)} %collective-permute-done.9.refs_1_, bf16[160,512]{1,0:T(8,128)(2,1)S(1)} %get-tuple-element.42.refs_4_.refs_2_, ...), custom_call_target="tpu_custom_call" | custom-call | flops 100000000 | bytes 1000 | tf_op jit(solution)/shard_map/experts_backward/pallas_call | solution.py:38
  30.0 5.0 %collective-permute-done.10.refs_1_.refs_3_ = bf16[16,3840]{1,0:T(8,128)(2,1)S(1)} collective-permute-done((bf16[16,3840]{1,0:T(8,128)(2,1)S(1)}, bf16[16,3840]{1,0:T(8,128)(2,1)S(1)}, u32[]{:S(2)}, u32[]{:S(2)}) %collective-permute-start.10) | collective-permute-done | bytes 122912 | tf_op jit(solution)/shard_map/ppermute | solution.py:602
  35.0 2.1 %collective-permute-done.11.refs_2_ = bf16[16,3840]{1,0:T(8,128)(2,1)S(1)} collective-permute-done((bf16[16,3840]{1,0:T(8,128)(2,1)S(1)}, bf16[16,3840]{1,0:T(8,128)(2,1)S(1)}, u32[]{:S(2)}, u32[]{:S(2)}) %collective-permute-start.11) | collective-permute-done | bytes 122912 | tf_op jit(solution)/shard_map/ppermute | solution.py:602
  37.2 0.2 finish_forward_10.1
  37.6 0.5 finish_backward.1
  38.2 4.8 %collective-permute-start.15 = (bf16[16,3840]{1,0:T(8,128)(2,1)S(1)}, bf16[16,3840]{1,0:T(8,128)(2,1)S(1)}, u32[]{:S(2)}, u32[]{:S(2)}) collective-permute-start(bf16[16,3840]{1,0:T(8,128)(2,1)S(1)} %get-tuple-element.60), channel_id=1, source_target_pairs={{0,24},{1,25},{2,26},{3,27},{4,28},{5,29},{6,30},{7,31},{8,0},{9,1... | collective-permute-start | bytes 368648 | tf_op jit(solution)/shard_map/ppermute | solution.py:602
  42.9 2.0 %collective-permute-start.16 = (bf16[16,3840]{1,0:T(8,128)(2,1)S(1)}, bf16[16,3840]{1,0:T(8,128)(2,1)S(1)}, u32[]{:S(2)}, u32[]{:S(2)}) collective-permute-start(bf16[16,3840]{1,0:T(8,128)(2,1)S(1)} %get-tuple-element.61), channel_id=1, source_target_pairs={{0,26},{1,27},{2,24},{3,25},{4,30},{5,31},{6,28},{7,29},{8,2},{9,3... | collective-permute-start | bytes 368648 | tf_op jit(solution)/shard_map/ppermute | solution.py:602
  44.9 1.0 %collective-permute-start.17 = (bf16[16,3840]{1,0:T(8,128)(2,1)S(1)}, bf16[16,3840]{1,0:T(8,128)(2,1)S(1)}, u32[]{:S(2)}, u32[]{:S(2)}) collective-permute-start(bf16[16,3840]{1,0:T(8,128)(2,1)S(1)} %get-tuple-element.62), channel_id=1, source_target_pairs={{0,28},{1,29},{2,30},{3,31},{4,24},{5,25},{6,26},{7,27},{8,4},{9,5... | collective-permute-start | bytes 368648 | tf_op jit(solution)/shard_map/ppermute | solution.py:602
  45.9 1.2 %collective-permute-start.18 = (bf16[16,3840]{1,0:T(8,128)(2,1)S(1)}, bf16[16,3840]{1,0:T(8,128)(2,1)S(1)}, u32[]{:S(2)}, u32[]{:S(2)}) collective-permute-start(bf16[16,3840]{1,0:T(8,128)(2,1)S(1)} %get-tuple-element.63), channel_id=1, source_target_pairs={{0,30},{1,31},{2,28},{3,29},{4,26},{5,27},{6,24},{7,25},{8,6},{9,7... | collective-permute-start | bytes 368648 | tf_op jit(solution)/shard_map/ppermute | solution.py:602
  47.1 2.1 %collective-permute-done.13.refs_1_ = bf16[16,3840]{1,0:T(8,128)(2,1)S(1)} collective-permute-done((bf16[16,3840]{1,0:T(8,128)(2,1)S(1)}, bf16[16,3840]{1,0:T(8,128)(2,1)S(1)}, u32[]{:S(2)}, u32[]{:S(2)}) %collective-permute-start.13) | collective-permute-done | bytes 122912 | tf_op jit(solution)/shard_map/ppermute | solution.py:602
  49.2 1.0 %forward_rows.1 = bf16[64,3584]{1,0:T(8,128)(2,1)} custom-call(bf16[16,3840]{1,0:T(8,128)(2,1)S(1)} %collective-permute-done.12.refs_0_, bf16[16,3840]{1,0:T(8,128)(2,1)S(1)} %collective-permute-done.13.refs_1_, bf16[16,3840]{1,0:T(8,128)(2,1)S(1)} %collective-permute-done.11.refs_2_, bf16[16,3840]{1,0:T(8,128)(2,1)S(1)} %collective-permute-done.10.refs_1_.refs_3_), custom_call_target="tpu_custom_call" | custom-call | flops 100000000 | bytes 1000 | tf_op jit(solution)/shard_map/forward_rows/pallas_call | solution.py:38
  50.2 2.6 %collective-permute-done.16.refs_1_ = bf16[16,3840]{1,0:T(8,128)(2,1)S(1)} collective-permute-done((bf16[16,3840]{1,0:T(8,128)(2,1)S(1)}, bf16[16,3840]{1,0:T(8,128)(2,1)S(1)}, u32[]{:S(2)}, u32[]{:S(2)}) %collective-permute-start.16) | collective-permute-done | bytes 122912 | tf_op jit(solution)/shard_map/ppermute | solution.py:602
  52.8 3.0 %collective-permute-done.17.refs_2_ = bf16[16,3840]{1,0:T(8,128)(2,1)S(1)} collective-permute-done((bf16[16,3840]{1,0:T(8,128)(2,1)S(1)}, bf16[16,3840]{1,0:T(8,128)(2,1)S(1)}, u32[]{:S(2)}, u32[]{:S(2)}) %collective-permute-start.17) | collective-permute-done | bytes 122912 | tf_op jit(solution)/shard_map/ppermute | solution.py:602
  55.7 2.0 %collective-permute-done.18.refs_3_ = bf16[16,3840]{1,0:T(8,128)(2,1)S(1)} collective-permute-done((bf16[16,3840]{1,0:T(8,128)(2,1)S(1)}, bf16[16,3840]{1,0:T(8,128)(2,1)S(1)}, u32[]{:S(2)}, u32[]{:S(2)}) %collective-permute-start.18) | collective-permute-done | bytes 122912 | tf_op jit(solution)/shard_map/ppermute | solution.py:602
  57.7 1.3 %backward_rows.1 = bf16[64,3584]{1,0:T(8,128)(2,1)} custom-call(bf16[16,3840]{1,0:T(8,128)(2,1)S(1)} %collective-permute-done.15.refs_0_, bf16[16,3840]{1,0:T(8,128)(2,1)S(1)} %collective-permute-done.16.refs_1_, bf16[16,3840]{1,0:T(8,128)(2,1)S(1)} %collective-permute-done.17.refs_2_, bf16[16,3840]{1,0:T(8,128)(2,1)S(1)} %collective-permute-done.18.refs_3_, ...), custom_call_target="tpu_custom_call" | custom-call | flops 100000000 | bytes 1000 | tf_op jit(solution)/shard_map/backward_rows/pallas_call | solution.py:38
  (24 shorter events, 0.9 us)
Async XLA Ops:
  2.7 12.8 %collective-permute-start = (bf16[16,3840]{1,0:T(8,128)(2,1)S(1)}, bf16[16,3840]{1,0:T(8,128)(2,1)S(1)}, u32[]{:S(2)}, u32[]{:S(2)}) collective-permute-start(bf16[16,3840]{1,0:T(8,128)(2,1)S(1)} %get-tuple-element.33), channel_id=1, source_target_pairs={{0,2},{1,3},{2,0},{3,1},{4,6},{5,7},{6,4},{7,5},{8,10},{9,11},{10,... | collective-permute-start | bytes 368648 | tf_op jit(solution)/shard_map/ppermute | solution.py:584
  5.7 11.3 %collective-permute-start.1 = (bf16[16,3840]{1,0:T(8,128)(2,1)S(1)}, bf16[16,3840]{1,0:T(8,128)(2,1)S(1)}, u32[]{:S(2)}, u32[]{:S(2)}) collective-permute-start(bf16[16,3840]{1,0:T(8,128)(2,1)S(1)} %get-tuple-element.35), channel_id=1, source_target_pairs={{0,4},{1,5},{2,6},{3,7},{4,0},{5,1},{6,2},{7,3},{8,12},{9,13},{10,... | collective-permute-start | bytes 368648 | tf_op jit(solution)/shard_map/ppermute | solution.py:584
  7.2 10.3 %collective-permute-start.2 = (bf16[16,3840]{1,0:T(8,128)(2,1)S(1)}, bf16[16,3840]{1,0:T(8,128)(2,1)S(1)}, u32[]{:S(2)}, u32[]{:S(2)}) collective-permute-start(bf16[16,3840]{1,0:T(8,128)(2,1)S(1)} %get-tuple-element.36), channel_id=1, source_target_pairs={{0,6},{1,7},{2,4},{3,5},{4,2},{5,3},{6,0},{7,1},{8,14},{9,15},{10,... | collective-permute-start | bytes 368648 | tf_op jit(solution)/shard_map/ppermute | solution.py:584
  7.3 16.4 %collective-permute-start.5 = (bf16[64,3584]{1,0:T(8,128)(2,1)S(1)}, bf16[64,3584]{1,0:T(8,128)(2,1)S(1)}, u32[]{:S(2)}, u32[]{:S(2)}) collective-permute-start(bf16[64,3584]{1,0:T(8,128)(2,1)S(1)} %get-tuple-element.37.act_ref), channel_id=1, source_target_pairs={{0,24},{1,25},{2,26},{3,27},{4,28},{5,29},{6,30},{7,31},{8,0},{9,1... | collective-permute-start | bytes 1376264 | tf_op jit(solution)/shard_map/ppermute | solution.py:602
  14.0 9.4 %collective-permute-start.6 = (bf16[16,3840]{1,0:T(8,128)(2,1)S(1)}, bf16[16,3840]{1,0:T(8,128)(2,1)S(1)}, u32[]{:S(2)}, u32[]{:S(2)}) collective-permute-start(bf16[16,3840]{1,0:T(8,128)(2,1)S(1)} %get-tuple-element.46), channel_id=1, source_target_pairs={{0,2},{1,3},{2,0},{3,1},{4,6},{5,7},{6,4},{7,5},{8,10},{9,11},{10,... | collective-permute-start | bytes 368648 | tf_op jit(solution)/shard_map/ppermute | solution.py:584
  15.5 7.8 %collective-permute-start.7 = (bf16[16,3840]{1,0:T(8,128)(2,1)S(1)}, bf16[16,3840]{1,0:T(8,128)(2,1)S(1)}, u32[]{:S(2)}, u32[]{:S(2)}) collective-permute-start(bf16[16,3840]{1,0:T(8,128)(2,1)S(1)} %get-tuple-element.47), channel_id=1, source_target_pairs={{0,4},{1,5},{2,6},{3,7},{4,0},{5,1},{6,2},{7,3},{8,12},{9,13},{10,... | collective-permute-start | bytes 368648 | tf_op jit(solution)/shard_map/ppermute | solution.py:584
  17.0 6.3 %collective-permute-start.8 = (bf16[16,3840]{1,0:T(8,128)(2,1)S(1)}, bf16[16,3840]{1,0:T(8,128)(2,1)S(1)}, u32[]{:S(2)}, u32[]{:S(2)}) collective-permute-start(bf16[16,3840]{1,0:T(8,128)(2,1)S(1)} %get-tuple-element.48), channel_id=1, source_target_pairs={{0,6},{1,7},{2,4},{3,5},{4,2},{5,3},{6,0},{7,1},{8,14},{9,15},{10,... | collective-permute-start | bytes 368648 | tf_op jit(solution)/shard_map/ppermute | solution.py:584
  18.0 2.0 %collective-permute-start.3 = (bf16[80,3584]{1,0:T(8,128)(2,1)S(1)}, bf16[80,3584]{1,0:T(8,128)(2,1)S(1)}, u32[]{:S(2)}, u32[]{:S(2)}) collective-permute-start(bf16[80,3584]{1,0:T(8,128)(2,1)S(1)} %get-tuple-element.40.refs_0_), channel_id=1, source_target_pairs={{0,1},{1,0},{2,3},{3,2},{4,5},{5,4},{6,7},{7,6},{8,9},{9,8},{10,11... | collective-permute-start | bytes 1720328 | tf_op jit(solution)/shard_map/ppermute | solution.py:591
  18.1 2.1 %copy-start = (bf16[1,3584,512]{2,1,0:T(8,128)(2,1)S(1)}, bf16[1,3584,512]{2,1,0:T(8,128)(2,1)}, u32[]{:S(2)}) copy-start(bf16[1,3584,512]{2,1,0:T(8,128)(2,1)} %refs_4_.1) | copy-start | bytes 11010052
  18.1 3.2 %copy-start.1 = (bf16[1,512,3584]{2,1,0:T(8,128)(2,1)S(1)}, bf16[1,512,3584]{2,1,0:T(8,128)(2,1)}, u32[]{:S(2)}) copy-start(bf16[1,512,3584]{2,1,0:T(8,128)(2,1)} %refs_5_.1) | copy-start | bytes 11010052
  22.8 2.2 %collective-permute-start.4 = (bf16[80,3584]{1,0:T(8,128)(2,1)S(1)}, bf16[80,3584]{1,0:T(8,128)(2,1)S(1)}, u32[]{:S(2)}, u32[]{:S(2)}) collective-permute-start(bf16[80,3584]{1,0:T(8,128)(2,1)S(1)} %get-tuple-element.44), channel_id=1, source_target_pairs={{0,1},{1,0},{2,3},{3,2},{4,5},{5,4},{6,7},{7,6},{8,9},{9,8},{10,11... | collective-permute-start | bytes 1720328 | tf_op jit(solution)/shard_map/ppermute | solution.py:591
  23.5 3.8 %collective-permute-start.9 = (bf16[80,3584]{1,0:T(8,128)(2,1)S(1)}, bf16[80,3584]{1,0:T(8,128)(2,1)S(1)}, u32[]{:S(2)}, u32[]{:S(2)}) collective-permute-start(bf16[80,3584]{1,0:T(8,128)(2,1)S(1)} %get-tuple-element.49.refs_6_.refs_0_), channel_id=1, source_target_pairs={{0,1},{1,0},{2,3},{3,2},{4,5},{5,4},{6,7},{7,6},{8,9},{9,8},{10,11... | collective-permute-start | bytes 1720328 | tf_op jit(solution)/shard_map/ppermute | solution.py:591
  25.2 9.8 %collective-permute-start.10 = (bf16[16,3840]{1,0:T(8,128)(2,1)S(1)}, bf16[16,3840]{1,0:T(8,128)(2,1)S(1)}, u32[]{:S(2)}, u32[]{:S(2)}) collective-permute-start(bf16[16,3840]{1,0:T(8,128)(2,1)S(1)} %get-tuple-element.51.refs_6_), channel_id=1, source_target_pairs={{0,14},{1,15},{2,12},{3,13},{4,10},{5,11},{6,8},{7,9},{8,22},{9,23... | collective-permute-start | bytes 368648 | tf_op jit(solution)/shard_map/ppermute | solution.py:602
  25.5 11.5 %collective-permute-start.11 = (bf16[16,3840]{1,0:T(8,128)(2,1)S(1)}, bf16[16,3840]{1,0:T(8,128)(2,1)S(1)}, u32[]{:S(2)}, u32[]{:S(2)}) collective-permute-start(bf16[16,3840]{1,0:T(8,128)(2,1)S(1)} %get-tuple-element.53), channel_id=1, source_target_pairs={{0,12},{1,13},{2,14},{3,15},{4,8},{5,9},{6,10},{7,11},{8,20},{9,21... | collective-permute-start | bytes 368648 | tf_op jit(solution)/shard_map/ppermute | solution.py:602
  29.9 7.7 %collective-permute-start.14 = (bf16[80,3712]{1,0:T(8,128)(2,1)S(1)}, bf16[80,3712]{1,0:T(8,128)(2,1)S(1)}, u32[]{:S(2)}, u32[]{:S(2)}) collective-permute-start(bf16[80,3712]{1,0:T(8,128)(2,1)S(1)} %get-tuple-element.59), channel_id=1, source_target_pairs={{0,1},{1,0},{2,3},{3,2},{4,5},{5,4},{6,7},{7,6},{8,9},{9,8},{10,11... | collective-permute-start | bytes 1781768 | tf_op jit(solution)/shard_map/ppermute | solution.py:591
  37.5 8.4 %collective-permute-start.12 = (bf16[16,3840]{1,0:T(8,128)(2,1)S(1)}, bf16[16,3840]{1,0:T(8,128)(2,1)S(1)}, u32[]{:S(2)}, u32[]{:S(2)}) collective-permute-start(bf16[16,3840]{1,0:T(8,128)(2,1)S(1)} %get-tuple-element.54), channel_id=1, source_target_pairs={{0,8},{1,9},{2,10},{3,11},{4,12},{5,13},{6,14},{7,15},{8,16},{9,17... | collective-permute-start | bytes 368648 | tf_op jit(solution)/shard_map/ppermute | solution.py:602
  37.5 11.7 %collective-permute-start.13 = (bf16[16,3840]{1,0:T(8,128)(2,1)S(1)}, bf16[16,3840]{1,0:T(8,128)(2,1)S(1)}, u32[]{:S(2)}, u32[]{:S(2)}) collective-permute-start(bf16[16,3840]{1,0:T(8,128)(2,1)S(1)} %get-tuple-element.55.refs_10_), channel_id=1, source_target_pairs={{0,10},{1,11},{2,8},{3,9},{4,14},{5,15},{6,12},{7,13},{8,18},{9,19... | collective-permute-start | bytes 368648 | tf_op jit(solution)/shard_map/ppermute | solution.py:602
  38.2 12.0 %collective-permute-start.15 = (bf16[16,3840]{1,0:T(8,128)(2,1)S(1)}, bf16[16,3840]{1,0:T(8,128)(2,1)S(1)}, u32[]{:S(2)}, u32[]{:S(2)}) collective-permute-start(bf16[16,3840]{1,0:T(8,128)(2,1)S(1)} %get-tuple-element.60), channel_id=1, source_target_pairs={{0,24},{1,25},{2,26},{3,27},{4,28},{5,29},{6,30},{7,31},{8,0},{9,1... | collective-permute-start | bytes 368648 | tf_op jit(solution)/shard_map/ppermute | solution.py:602
  42.9 9.9 %collective-permute-start.16 = (bf16[16,3840]{1,0:T(8,128)(2,1)S(1)}, bf16[16,3840]{1,0:T(8,128)(2,1)S(1)}, u32[]{:S(2)}, u32[]{:S(2)}) collective-permute-start(bf16[16,3840]{1,0:T(8,128)(2,1)S(1)} %get-tuple-element.61), channel_id=1, source_target_pairs={{0,26},{1,27},{2,24},{3,25},{4,30},{5,31},{6,28},{7,29},{8,2},{9,3... | collective-permute-start | bytes 368648 | tf_op jit(solution)/shard_map/ppermute | solution.py:602
  44.9 10.9 %collective-permute-start.17 = (bf16[16,3840]{1,0:T(8,128)(2,1)S(1)}, bf16[16,3840]{1,0:T(8,128)(2,1)S(1)}, u32[]{:S(2)}, u32[]{:S(2)}) collective-permute-start(bf16[16,3840]{1,0:T(8,128)(2,1)S(1)} %get-tuple-element.62), channel_id=1, source_target_pairs={{0,28},{1,29},{2,30},{3,31},{4,24},{5,25},{6,26},{7,27},{8,4},{9,5... | collective-permute-start | bytes 368648 | tf_op jit(solution)/shard_map/ppermute | solution.py:602
  45.9 11.8 %collective-permute-start.18 = (bf16[16,3840]{1,0:T(8,128)(2,1)S(1)}, bf16[16,3840]{1,0:T(8,128)(2,1)S(1)}, u32[]{:S(2)}, u32[]{:S(2)}) collective-permute-start(bf16[16,3840]{1,0:T(8,128)(2,1)S(1)} %get-tuple-element.63), channel_id=1, source_target_pairs={{0,30},{1,31},{2,28},{3,29},{4,26},{5,27},{6,24},{7,25},{8,6},{9,7... | collective-permute-start | bytes 368648 | tf_op jit(solution)/shard_map/ppermute | solution.py:602

commit v6 on v4

--- a/solution.py
+++ b/solution.py
@@ -21,10 +21,11 @@
 
 
 cost = {
-    "normed_rows": 5,
-    "saved_terms": 40,
-    "act_norms": 40,
-    "act_gates": 40,
+    "backward_chunks": 10,
+    "later": 15,
+    "saved_terms": 15,
+    "act_norms": 15,
+    "act_gates": 15,
 }
 
 
@@ -67,6 +68,7 @@
         self.pieces = width // fold
         self.wide = width + fold
         self.rows = tokens + 16
+        self.order = [experts - 1, *range(1, experts - 1), 0]
         assert self.main == 16 and self.pieces <= 14 and width % fold == 0
         assert experts <= 8 and experts & (experts - 1) == 0 and self.split & (self.split - 1) == 0
 
@@ -178,6 +180,14 @@
     )(where, ids.reshape(1, z.tokens), *sources, *tables, *after)
 
 
+def later(chunk, weights, after):
+    def body(chunk, *refs):
+        refs[-1][...] = chunk[...]
+
+    places = "v" + "v" * len(weights) + "a" * len(after)
+    return call(body, places, shape(chunk.shape), [], 8, "later")(chunk, *weights, *after)
+
+
 def collect_rows(z, chunks, last, tile, base=0):
     last[...] = jnp.zeros_like(last)
     for k in range(z.experts):
@@ -190,8 +200,11 @@
 
 
 def normed_rows(z, chunks, vectors):
+    order = z.order
+
     def body(*refs):
         chunks, (vectors, normed_ref, gates_ref, last, tile) = refs[: z.experts], refs[z.experts :]
+        chunks = [chunks[order.index(k)] for k in range(z.experts)]
         gain, router = vectors[0:1, :], vectors[1:2, :]
         collect_rows(z, chunks, last, tile)
         for k in range(z.experts + 1):
@@ -209,7 +222,7 @@
         [pltpu.VMEM((16, fold), f32)],
         8,
         "normed_rows",
-    )(*chunks, vectors)
+    )(*[chunks[k] for k in order], vectors)
 
 
 def grad_rows_of(z, chunks, after):
@@ -439,11 +452,13 @@
 
 
 def order_rows(z, chunks, name):
+    order = z.order
     lanes = z.tokens + 16 * z.experts
     steps = 7 if z.pieces % 7 == 0 else z.pieces
 
     def body(*refs):
         chunks, (out_any, out, sems) = refs[: z.experts], refs[z.experts :]
+        chunks = [chunks[order.index(k)] for k in range(z.experts)]
         tiles = [chunk[:, z.width :] for chunk in chunks]
         token_row = tiles[0].astype(f32)[z.pieces : z.pieces + 1, :lanes]
         token = lax.broadcasted_iota(jnp.int32, (z.tokens, lanes), 0).astype(f32)
@@ -473,7 +488,7 @@
         8,
         name,
         spaces["a"],
-    )(*chunks)
+    )(*[chunks[k] for k in order])
 
 
 def dispatch(z, chunks):
@@ -524,9 +539,9 @@
         [fwd_chunks[0]],
         "backward_chunks",
     )
+    normed, gates, fwd_last = normed_rows(z, fwd_own, vectors)
+    bwd_chunks[z.experts // 2] = later(bwd_chunks[z.experts // 2], [w_gate, w_down], [gates])
     bwd_own = dispatch(z, bwd_chunks)
-
-    normed, gates, fwd_last = normed_rows(z, fwd_own, vectors)
     fwd_all = [normed] + [to_core(z, normed, m) for m in others]
     fwd_parts = experts_forward(z, fwd_all, w_gate, w_down, [])
     hidden, slope = saved_terms(z, where, saved_gate, [fwd_parts[0]])
@@ -534,26 +549,28 @@
     fwd_done = {}
 
     def finish(ks, after):
-        outs = finish_forward(z, ks, [fwd_own[k] for k in range(z.experts)], fwd_last, fwd_parts, gates, after)
+        outs = finish_forward(z, ks, fwd_own, fwd_last, fwd_parts, gates, after)
         for k, out in zip(ks, outs):
             fwd_done[k] = to_section(z, out, k, 1)
         return outs[0]
 
-    order = [*range(z.experts - 1, 0, -1), 0]
-    first = finish(order[:-1], [hidden])
+    order = z.order
+    first = finish(order[:2], [hidden])
     grads, grad_last = grad_rows_of(z, bwd_own, [first])
     grad_all = [grads] + [to_core(z, grads, m) for m in others]
     inv, act_last = act_norms(z, bwd_own, [grads])
     bwd_parts = experts_backward(z, grad_all, hidden, slope, w_gate, w_down, [inv])
-    affinity = act_gates(z, bwd_own, act_last, inv, vectors, [bwd_parts[0]])
-    third = finish(order[-1:], [affinity])
+    affinity = act_gates(
+        z, bwd_own, act_last, inv, vectors, [bwd_parts[0], *fwd_done.values()]
+    )
+    second = finish(order[2:], [affinity])
     bwd_parts = [bwd_parts[0]] + [to_core(z, bwd_parts[m], m) for m in others]
     bwd_out = finish_backward(
-        z, order, bwd_own, [grad_last, act_last], [inv, affinity], bwd_parts, vectors, [third]
+        z, order, bwd_own, [grad_last, act_last], [inv, affinity], bwd_parts, vectors, [second]
     )
     bwd_done = {k: to_section(z, out, k, -1) for k, out in zip(order, bwd_out)}
+    fwd_done = [fwd_done[k] for k in range(z.experts)]
     bwd_done = [bwd_done[k] for k in range(z.experts)]
-    fwd_done = [fwd_done[k] for k in range(z.experts)]
     return (order_rows(z, fwd_done, "forward_rows"), order_rows(z, bwd_done, "backward_rows"))
 
 

time: 60.6 us -> 57.4 us (0.947)
  waiting for transfers between devices: 17.6 us -> 14.7 us
    ppermute x6, waiting for transfers between devices: 6.88 us -> 3.33 us  [dispatch(): got[k] = lax.ppermute(chunks[k], 'ep', pairs)]
    ppermute x8, starting transfers between devices: 18.8 us -> 17.5 us  [to_section(): return lax.ppermute(chunk, ('pp', 'ep'), pairs)]
    ppermute x4, waiting for transfers between devices: 2 us -> 3.02 us  [to_core(): return lax.ppermute(array, 'ep', pairs)]
    ppermute x6, starting transfers between devices: 8.1 us -> 8.82 us  [dispatch(): got[k] = lax.ppermute(chunks[k], 'ep', pairs)]
    pallas_call x14 -> x15, Pallas kernels: 14.6 us -> 14.9 us  [run(): return kernel(*arrays)]
  transfers between devices with their start and end apart: 18 -> 18, of which waited for: 8 -> 9; matrix products, arithmetic and copies ran while one was open for 0% -> 0% of each run, Pallas kernels for 18% -> 21%
where the time goes in v6:
time: 57.4 us; the launch traced here: 57.2 us
  starting transfers between devices  26.9 us (47%)
  Pallas kernels  14.9 us (26%)
  waiting for transfers between devices  14.7 us (26%)
  between operations  0.77 us (1%)
    ppermute x8, starting transfers between devices, to_section(): return lax.ppermute(chunk, ('pp', 'ep'), pairs)  17.5 us
    pallas_call x15, Pallas kernels, run(): return kernel(*arrays)  14.9 us
    ppermute x6, starting transfers between devices, dispatch(): got[k] = lax.ppermute(chunks[k], 'ep', pairs)  8.82 us
    ppermute x8, waiting for transfers between devices, to_section(): return lax.ppermute(chunk, ('pp', 'ep'), pairs)  8.32 us
    ppermute x6, waiting for transfers between devices, dispatch(): got[k] = lax.ppermute(chunks[k], 'ep', pairs)  3.33 us
    ppermute x4, waiting for transfers between devices, to_core(): return lax.ppermute(array, 'ep', pairs)  3.02 us
  transfers between devices with their start and end apart: 18, of which 9 were waited for; matrix products, arithmetic and copies ran while one was open for 0% of the time, Pallas kernels for 21%

profile of v6, /device:TPU:0, one launch (start us, length us, event | category | flops | bytes accessed | tf_op | source)
XLA Modules:
  0.0 57.2 jit_solution(15530626557156211541)
XLA Ops:
  0.7 2.0 %forward_chunks.1 = (bf16[16,3840]{1,0:T(8,128)(2,1)S(1)}, bf16[16,3840]{1,0:T(8,128)(2,1)S(1)}, bf16[16,3840]{1,0:T(8,128)(2,1)S(1)}, bf16[16,3840]{1,0:T(8,128)(2,1)S(1)}) custom-call(s32[2]{0:T(128)S(1)} %pad_add_fusion.where, s32[1,64]{1,0:T(1,128)} %bitcast.5, bf16[64,3584]{1,0:T(8,128)(2,1)} %refs_0_.3), custom_call_target="tpu_custom_call" | custom-call | flops 100000000 | bytes 1000 | tf_op jit(solution)/shard_map/forward_chunks/pallas_call | solution.py:38
  2.7 4.0 %collective-permute-start = (bf16[16,3840]{1,0:T(8,128)(2,1)S(1)}, bf16[16,3840]{1,0:T(8,128)(2,1)S(1)}, u32[]{:S(2)}, u32[]{:S(2)}) collective-permute-start(bf16[16,3840]{1,0:T(8,128)(2,1)S(1)} %get-tuple-element.32), channel_id=1, source_target_pairs={{0,6},{1,7},{2,4},{3,5},{4,2},{5,3},{6,0},{7,1},{8,14},{9,15},{10,... | collective-permute-start | bytes 368648 | tf_op jit(solution)/shard_map/ppermute | solution.py:499
  6.7 0.5 collective-permute-start.1
  7.3 2.8 %backward_chunks.1 = (bf16[32,3840]{1,0:T(8,128)(2,1)S(1)}, bf16[32,3840]{1,0:T(8,128)(2,1)S(1)}, bf16[32,3840]{1,0:T(8,128)(2,1)S(1)}, bf16[32,3840]{1,0:T(8,128)(2,1)S(1)}, f32[8,3584]{1,0:T(8,128)S(1)}) custom-call(s32[2]{0:T(128)S(1)} %pad_add_fusion.where, s32[1,64]{1,0:T(1,128)} %bitcast.7, bf16[64,3584]{1,0:T(8,128)(2,1)} %refs_0_.4, ...), custom_call_target="tpu_custom_call" | custom-call | flops 10000000000 | bytes 1000 | tf_op jit(solution)/shard_map/backward_chunks/pallas_call | solution.py:38
  10.1 2.0 %collective-permute-start.7 = (bf16[32,3840]{1,0:T(8,128)(2,1)S(1)}, bf16[32,3840]{1,0:T(8,128)(2,1)S(1)}, u32[]{:S(2)}, u32[]{:S(2)}) collective-permute-start(bf16[32,3840]{1,0:T(8,128)(2,1)S(1)} %get-tuple-element.46), channel_id=1, source_target_pairs={{0,2},{1,3},{2,0},{3,1},{4,6},{5,7},{6,4},{7,5},{8,10},{9,11},{10,... | collective-permute-start | bytes 737288 | tf_op jit(solution)/shard_map/ppermute | solution.py:499
  12.1 1.5 %collective-permute-start.9 = (bf16[32,3840]{1,0:T(8,128)(2,1)S(1)}, bf16[32,3840]{1,0:T(8,128)(2,1)S(1)}, u32[]{:S(2)}, u32[]{:S(2)}) collective-permute-start(bf16[32,3840]{1,0:T(8,128)(2,1)S(1)} %get-tuple-element.48), channel_id=1, source_target_pairs={{0,6},{1,7},{2,4},{3,5},{4,2},{5,3},{6,0},{7,1},{8,14},{9,15},{10,... | collective-permute-start | bytes 737288 | tf_op jit(solution)/shard_map/ppermute | solution.py:499
  13.6 0.5 normed_rows.1
  14.2 0.8 %collective-permute-start.8 = (bf16[32,3840]{1,0:T(8,128)(2,1)S(1)}, bf16[32,3840]{1,0:T(8,128)(2,1)S(1)}, u32[]{:S(2)}, u32[]{:S(2)}) collective-permute-start(bf16[32,3840]{1,0:T(8,128)(2,1)S(1)} %later.1), channel_id=1, source_target_pairs={{0,4},{1,5},{2,6},{3,7},{4,0},{5,1},{6,2},{7,3},{8,12},{9,13},{10,... | collective-permute-start | bytes 737288 | tf_op jit(solution)/shard_map/ppermute | solution.py:499
  15.0 1.2 %collective-permute-done.3.refs_1_ = bf16[80,3584]{1,0:T(8,128)(2,1)S(1)} collective-permute-done((bf16[80,3584]{1,0:T(8,128)(2,1)S(1)}, bf16[80,3584]{1,0:T(8,128)(2,1)S(1)}, u32[]{:S(2)}, u32[]{:S(2)}) %collective-permute-start.3) | collective-permute-done | bytes 573472 | tf_op jit(solution)/shard_map/ppermute | solution.py:506
  16.1 1.5 %experts_forward.1 = (bf16[80,3584]{1,0:T(8,128)(2,1)S(1)}, bf16[80,3584]{1,0:T(8,128)(2,1)S(1)}) custom-call(bf16[80,3584]{1,0:T(8,128)(2,1)S(1)} %get-tuple-element.38.refs_0_, bf16[80,3584]{1,0:T(8,128)(2,1)S(1)} %collective-permute-done.3.refs_1_, bf16[1,3584,512]{2,1,0:T(8,128)(2,1)S(1)} %copy-done, bf16[1,512,3584]{2,1,0:T(8,128)(2,1)S(1)} %copy-done.1), custom_call_target="tpu_custom_call" | custom-call | flops 100000000 | bytes 1000 | tf_op jit(solution)/shard_map/experts_forward/pallas_call | solution.py:38
  17.8 1.7 %saved_terms.1 = (bf16[160,512]{1,0:T(8,128)(2,1)S(1)}, f32[160,512]{1,0:T(8,128)S(1)}) custom-call(s32[2]{0:T(128)S(1)} %pad_add_fusion.where, bf16[1,1,136,512]{3,2,1,0:T(8,128)(2,1)} %saved_any.1, bf16[80,3584]{1,0:T(8,128)(2,1)S(1)} %get-tuple-element.39.refs_0_.refs_3_), custom_call_target="tpu_custom_call" | custom-call | flops 15000000512 | bytes 1000 | tf_op jit(solution)/shard_map/saved_terms/pallas_call | solution.py:38
  19.9 2.5 %collective-permute-start.6 = (bf16[16,3840]{1,0:T(8,128)(2,1)S(1)}, bf16[16,3840]{1,0:T(8,128)(2,1)S(1)}, u32[]{:S(2)}, u32[]{:S(2)}) collective-permute-start(bf16[16,3840]{1,0:T(8,128)(2,1)S(1)} %get-tuple-element.44), channel_id=1, source_target_pairs={{0,10},{1,11},{2,8},{3,9},{4,14},{5,15},{6,12},{7,13},{8,18},{9,19... | collective-permute-start | bytes 368648 | tf_op jit(solution)/shard_map/ppermute | solution.py:517
  22.4 1.7 %collective-permute-start.5 = (bf16[16,3840]{1,0:T(8,128)(2,1)S(1)}, bf16[16,3840]{1,0:T(8,128)(2,1)S(1)}, u32[]{:S(2)}, u32[]{:S(2)}) collective-permute-start(bf16[16,3840]{1,0:T(8,128)(2,1)S(1)} %get-tuple-element.43.refs_4_), channel_id=1, source_target_pairs={{0,14},{1,15},{2,12},{3,13},{4,10},{5,11},{6,8},{7,9},{8,22},{9,23... | collective-permute-start | bytes 368648 | tf_op jit(solution)/shard_map/ppermute | solution.py:517
  24.1 3.3 %collective-permute-done.8.refs_2_ = bf16[32,3840]{1,0:T(8,128)(2,1)S(1)} collective-permute-done((bf16[32,3840]{1,0:T(8,128)(2,1)S(1)}, bf16[32,3840]{1,0:T(8,128)(2,1)S(1)}, u32[]{:S(2)}, u32[]{:S(2)}) %collective-permute-start.8) | collective-permute-done | bytes 245792 | tf_op jit(solution)/shard_map/ppermute | solution.py:499
  27.6 0.2 act_norms.1
  27.8 1.7 %collective-permute-done.10.refs_1_ = bf16[80,3584]{1,0:T(8,128)(2,1)S(1)} collective-permute-done((bf16[80,3584]{1,0:T(8,128)(2,1)S(1)}, bf16[80,3584]{1,0:T(8,128)(2,1)S(1)}, u32[]{:S(2)}, u32[]{:S(2)}) %collective-permute-start.10) | collective-permute-done | bytes 573472 | tf_op jit(solution)/shard_map/ppermute | solution.py:506
  29.5 2.6 %experts_backward.1 = (bf16[80,3712]{1,0:T(8,128)(2,1)S(1)}, bf16[80,3712]{1,0:T(8,128)(2,1)S(1)}) custom-call(bf16[80,3584]{1,0:T(8,128)(2,1)S(1)} %get-tuple-element.49.refs_4_.refs_0_, bf16[80,3584]{1,0:T(8,128)(2,1)S(1)} %collective-permute-done.10.refs_1_, bf16[160,512]{1,0:T(8,128)(2,1)S(1)} %get-tuple-element.42.refs_6_.refs_2_, ...), custom_call_target="tpu_custom_call" | custom-call | flops 100000000 | bytes 1000 | tf_op jit(solution)/shard_map/experts_backward/pallas_call | solution.py:38
  32.3 0.4 act_gates.1.refs_6_.refs_7_
  32.7 0.2 finish_forward_20.1
  33.0 4.3 %collective-permute-start.12 = (bf16[16,3840]{1,0:T(8,128)(2,1)S(1)}, bf16[16,3840]{1,0:T(8,128)(2,1)S(1)}, u32[]{:S(2)}, u32[]{:S(2)}) collective-permute-start(bf16[16,3840]{1,0:T(8,128)(2,1)S(1)} %get-tuple-element.55), channel_id=1, source_target_pairs={{0,8},{1,9},{2,10},{3,11},{4,12},{5,13},{6,14},{7,15},{8,16},{9,17... | collective-permute-start | bytes 368648 | tf_op jit(solution)/shard_map/ppermute | solution.py:517
  37.2 2.2 %collective-permute-start.11 = (bf16[16,3840]{1,0:T(8,128)(2,1)S(1)}, bf16[16,3840]{1,0:T(8,128)(2,1)S(1)}, u32[]{:S(2)}, u32[]{:S(2)}) collective-permute-start(bf16[16,3840]{1,0:T(8,128)(2,1)S(1)} %get-tuple-element.54.refs_11_), channel_id=1, source_target_pairs={{0,12},{1,13},{2,14},{3,15},{4,8},{5,9},{6,10},{7,11},{8,20},{9,21... | collective-permute-start | bytes 368648 | tf_op jit(solution)/shard_map/ppermute | solution.py:517
  39.5 0.7 %finish_backward.1 = (bf16[16,3840]{1,0:T(8,128)(2,1)S(1)}, bf16[16,3840]{1,0:T(8,128)(2,1)S(1)}, bf16[16,3840]{1,0:T(8,128)(2,1)S(1)}, bf16[16,3840]{1,0:T(8,128)(2,1)S(1)}) custom-call(bf16[32,3840]{1,0:T(8,128)(2,1)S(1)} %get-tuple-element.45.refs_0_, bf16[32,3840]{1,0:T(8,128)(2,1)S(1)} %collective-permute-done.7.refs_1_, ...), custom_call_target="tpu_custom_call" | custom-call | flops 100000000 | bytes 1000 | tf_op jit(solution)/shard_map/finish_backward/pallas_call | solution.py:38
  40.1 3.5 %collective-permute-start.14 = (bf16[16,3840]{1,0:T(8,128)(2,1)S(1)}, bf16[16,3840]{1,0:T(8,128)(2,1)S(1)}, u32[]{:S(2)}, u32[]{:S(2)}) collective-permute-start(bf16[16,3840]{1,0:T(8,128)(2,1)S(1)} %get-tuple-element.58), channel_id=1, source_target_pairs={{0,30},{1,31},{2,28},{3,29},{4,26},{5,27},{6,24},{7,25},{8,6},{9,7... | collective-permute-start | bytes 368648 | tf_op jit(solution)/shard_map/ppermute | solution.py:517
  43.6 0.3 collective-permute-start.15
  43.9 2.6 %collective-permute-start.16 = (bf16[16,3840]{1,0:T(8,128)(2,1)S(1)}, bf16[16,3840]{1,0:T(8,128)(2,1)S(1)}, u32[]{:S(2)}, u32[]{:S(2)}) collective-permute-start(bf16[16,3840]{1,0:T(8,128)(2,1)S(1)} %get-tuple-element.60), channel_id=1, source_target_pairs={{0,28},{1,29},{2,30},{3,31},{4,24},{5,25},{6,26},{7,27},{8,4},{9,5... | collective-permute-start | bytes 368648 | tf_op jit(solution)/shard_map/ppermute | solution.py:517
  46.5 0.4 collective-permute-start.17
  46.9 1.0 %forward_rows.1 = bf16[64,3584]{1,0:T(8,128)(2,1)} custom-call(bf16[16,3840]{1,0:T(8,128)(2,1)S(1)} %collective-permute-done.5.refs_8_.refs_0_, bf16[16,3840]{1,0:T(8,128)(2,1)S(1)} %collective-permute-done.6.refs_9_.refs_1_, bf16[16,3840]{1,0:T(8,128)(2,1)S(1)} %collective-permute-done.11.refs_2_, bf16[16,3840]{1,0:T(8,128)(2,1)S(1)} %collective-permute-done.12.refs_3_), custom_call_target="tpu_custom_call" | custom-call | flops 100000000 | bytes 1000 | tf_op jit(solution)/shard_map/forward_rows/pallas_call | solution.py:38
  47.9 2.1 %collective-permute-done.14.refs_0_ = bf16[16,3840]{1,0:T(8,128)(2,1)S(1)} collective-permute-done((bf16[16,3840]{1,0:T(8,128)(2,1)S(1)}, bf16[16,3840]{1,0:T(8,128)(2,1)S(1)}, u32[]{:S(2)}, u32[]{:S(2)}) %collective-permute-start.14) | collective-permute-done | bytes 122912 | tf_op jit(solution)/shard_map/ppermute | solution.py:517
  50.0 2.0 %collective-permute-done.15.refs_1_ = bf16[16,3840]{1,0:T(8,128)(2,1)S(1)} collective-permute-done((bf16[16,3840]{1,0:T(8,128)(2,1)S(1)}, bf16[16,3840]{1,0:T(8,128)(2,1)S(1)}, u32[]{:S(2)}, u32[]{:S(2)}) %collective-permute-start.15) | collective-permute-done | bytes 122912 | tf_op jit(solution)/shard_map/ppermute | solution.py:517
  52.0 2.4 %collective-permute-done.16.refs_2_ = bf16[16,3840]{1,0:T(8,128)(2,1)S(1)} collective-permute-done((bf16[16,3840]{1,0:T(8,128)(2,1)S(1)}, bf16[16,3840]{1,0:T(8,128)(2,1)S(1)}, u32[]{:S(2)}, u32[]{:S(2)}) %collective-permute-start.16) | collective-permute-done | bytes 122912 | tf_op jit(solution)/shard_map/ppermute | solution.py:517
  54.4 1.9 %collective-permute-done.17.refs_3_ = bf16[16,3840]{1,0:T(8,128)(2,1)S(1)} collective-permute-done((bf16[16,3840]{1,0:T(8,128)(2,1)S(1)}, bf16[16,3840]{1,0:T(8,128)(2,1)S(1)}, u32[]{:S(2)}, u32[]{:S(2)}) %collective-permute-start.17) | collective-permute-done | bytes 122912 | tf_op jit(solution)/shard_map/ppermute | solution.py:517
  56.3 1.0 %backward_rows.1 = bf16[64,3584]{1,0:T(8,128)(2,1)} custom-call(bf16[16,3840]{1,0:T(8,128)(2,1)S(1)} %collective-permute-done.14.refs_0_, bf16[16,3840]{1,0:T(8,128)(2,1)S(1)} %collective-permute-done.15.refs_1_, bf16[16,3840]{1,0:T(8,128)(2,1)S(1)} %collective-permute-done.16.refs_2_, bf16[16,3840]{1,0:T(8,128)(2,1)S(1)} %collective-permute-done.17.refs_3_), custom_call_target="tpu_custom_call" | custom-call | flops 100000000 | bytes 1000 | tf_op jit(solution)/shard_map/backward_rows/pallas_call | solution.py:38
  (24 shorter events, 1.2 us)
Async XLA Ops:
  2.7 10.9 %collective-permute-start = (bf16[16,3840]{1,0:T(8,128)(2,1)S(1)}, bf16[16,3840]{1,0:T(8,128)(2,1)S(1)}, u32[]{:S(2)}, u32[]{:S(2)}) collective-permute-start(bf16[16,3840]{1,0:T(8,128)(2,1)S(1)} %get-tuple-element.32), channel_id=1, source_target_pairs={{0,6},{1,7},{2,4},{3,5},{4,2},{5,3},{6,0},{7,1},{8,14},{9,15},{10,... | collective-permute-start | bytes 368648 | tf_op jit(solution)/shard_map/ppermute | solution.py:499
  6.7 7.0 %collective-permute-start.1 = (bf16[16,3840]{1,0:T(8,128)(2,1)S(1)}, bf16[16,3840]{1,0:T(8,128)(2,1)S(1)}, u32[]{:S(2)}, u32[]{:S(2)}) collective-permute-start(bf16[16,3840]{1,0:T(8,128)(2,1)S(1)} %get-tuple-element.33), channel_id=1, source_target_pairs={{0,2},{1,3},{2,0},{3,1},{4,6},{5,7},{6,4},{7,5},{8,10},{9,11},{10,... | collective-permute-start | bytes 368648 | tf_op jit(solution)/shard_map/ppermute | solution.py:499
  7.2 6.4 %collective-permute-start.2 = (bf16[16,3840]{1,0:T(8,128)(2,1)S(1)}, bf16[16,3840]{1,0:T(8,128)(2,1)S(1)}, u32[]{:S(2)}, u32[]{:S(2)}) collective-permute-start(bf16[16,3840]{1,0:T(8,128)(2,1)S(1)} %get-tuple-element.34), channel_id=1, source_target_pairs={{0,4},{1,5},{2,6},{3,7},{4,0},{5,1},{6,2},{7,3},{8,12},{9,13},{10,... | collective-permute-start | bytes 368648 | tf_op jit(solution)/shard_map/ppermute | solution.py:499
  7.3 6.9 %copy-start = (bf16[1,3584,512]{2,1,0:T(8,128)(2,1)S(1)}, bf16[1,3584,512]{2,1,0:T(8,128)(2,1)}, u32[]{:S(2)}) copy-start(bf16[1,3584,512]{2,1,0:T(8,128)(2,1)} %refs_4_.1) | copy-start | bytes 11010052
  7.3 6.9 %copy-start.1 = (bf16[1,512,3584]{2,1,0:T(8,128)(2,1)S(1)}, bf16[1,512,3584]{2,1,0:T(8,128)(2,1)}, u32[]{:S(2)}) copy-start(bf16[1,512,3584]{2,1,0:T(8,128)(2,1)} %refs_5_.1) | copy-start | bytes 11010052
  10.1 14.0 %collective-permute-start.7 = (bf16[32,3840]{1,0:T(8,128)(2,1)S(1)}, bf16[32,3840]{1,0:T(8,128)(2,1)S(1)}, u32[]{:S(2)}, u32[]{:S(2)}) collective-permute-start(bf16[32,3840]{1,0:T(8,128)(2,1)S(1)} %get-tuple-element.46), channel_id=1, source_target_pairs={{0,2},{1,3},{2,0},{3,1},{4,6},{5,7},{6,4},{7,5},{8,10},{9,11},{10,... | collective-permute-start | bytes 737288 | tf_op jit(solution)/shard_map/ppermute | solution.py:499
  12.1 12.1 %collective-permute-start.9 = (bf16[32,3840]{1,0:T(8,128)(2,1)S(1)}, bf16[32,3840]{1,0:T(8,128)(2,1)S(1)}, u32[]{:S(2)}, u32[]{:S(2)}) collective-permute-start(bf16[32,3840]{1,0:T(8,128)(2,1)S(1)} %get-tuple-element.48), channel_id=1, source_target_pairs={{0,6},{1,7},{2,4},{3,5},{4,2},{5,3},{6,0},{7,1},{8,14},{9,15},{10,... | collective-permute-start | bytes 737288 | tf_op jit(solution)/shard_map/ppermute | solution.py:499
  14.1 2.0 %collective-permute-start.3 = (bf16[80,3584]{1,0:T(8,128)(2,1)S(1)}, bf16[80,3584]{1,0:T(8,128)(2,1)S(1)}, u32[]{:S(2)}, u32[]{:S(2)}) collective-permute-start(bf16[80,3584]{1,0:T(8,128)(2,1)S(1)} %get-tuple-element.38.refs_0_), channel_id=1, source_target_pairs={{0,1},{1,0},{2,3},{3,2},{4,5},{5,4},{6,7},{7,6},{8,9},{9,8},{10,11... | collective-permute-start | bytes 1720328 | tf_op jit(solution)/shard_map/ppermute | solution.py:506
  14.2 13.2 %collective-permute-start.8 = (bf16[32,3840]{1,0:T(8,128)(2,1)S(1)}, bf16[32,3840]{1,0:T(8,128)(2,1)S(1)}, u32[]{:S(2)}, u32[]{:S(2)}) collective-permute-start(bf16[32,3840]{1,0:T(8,128)(2,1)S(1)} %later.1), channel_id=1, source_target_pairs={{0,4},{1,5},{2,6},{3,7},{4,0},{5,1},{6,2},{7,3},{8,12},{9,13},{10,... | collective-permute-start | bytes 737288 | tf_op jit(solution)/shard_map/ppermute | solution.py:499
  17.6 2.0 %collective-permute-start.4 = (bf16[80,3584]{1,0:T(8,128)(2,1)S(1)}, bf16[80,3584]{1,0:T(8,128)(2,1)S(1)}, u32[]{:S(2)}, u32[]{:S(2)}) collective-permute-start(bf16[80,3584]{1,0:T(8,128)(2,1)S(1)} %get-tuple-element.40), channel_id=1, source_target_pairs={{0,1},{1,0},{2,3},{3,2},{4,5},{5,4},{6,7},{7,6},{8,9},{9,8},{10,11... | collective-permute-start | bytes 1720328 | tf_op jit(solution)/shard_map/ppermute | solution.py:506
  19.9 12.4 %collective-permute-start.6 = (bf16[16,3840]{1,0:T(8,128)(2,1)S(1)}, bf16[16,3840]{1,0:T(8,128)(2,1)S(1)}, u32[]{:S(2)}, u32[]{:S(2)}) collective-permute-start(bf16[16,3840]{1,0:T(8,128)(2,1)S(1)} %get-tuple-element.44), channel_id=1, source_target_pairs={{0,10},{1,11},{2,8},{3,9},{4,14},{5,15},{6,12},{7,13},{8,18},{9,19... | collective-permute-start | bytes 368648 | tf_op jit(solution)/shard_map/ppermute | solution.py:517
  22.4 9.9 %collective-permute-start.5 = (bf16[16,3840]{1,0:T(8,128)(2,1)S(1)}, bf16[16,3840]{1,0:T(8,128)(2,1)S(1)}, u32[]{:S(2)}, u32[]{:S(2)}) collective-permute-start(bf16[16,3840]{1,0:T(8,128)(2,1)S(1)} %get-tuple-element.43.refs_4_), channel_id=1, source_target_pairs={{0,14},{1,15},{2,12},{3,13},{4,10},{5,11},{6,8},{7,9},{8,22},{9,23... | collective-permute-start | bytes 368648 | tf_op jit(solution)/shard_map/ppermute | solution.py:517
  27.5 2.0 %collective-permute-start.10 = (bf16[80,3584]{1,0:T(8,128)(2,1)S(1)}, bf16[80,3584]{1,0:T(8,128)(2,1)S(1)}, u32[]{:S(2)}, u32[]{:S(2)}) collective-permute-start(bf16[80,3584]{1,0:T(8,128)(2,1)S(1)} %get-tuple-element.49.refs_4_.refs_0_), channel_id=1, source_target_pairs={{0,1},{1,0},{2,3},{3,2},{4,5},{5,4},{6,7},{7,6},{8,9},{9,8},{10,11... | collective-permute-start | bytes 1720328 | tf_op jit(solution)/shard_map/ppermute | solution.py:506
  32.1 7.3 %collective-permute-start.13 = (bf16[80,3712]{1,0:T(8,128)(2,1)S(1)}, bf16[80,3712]{1,0:T(8,128)(2,1)S(1)}, u32[]{:S(2)}, u32[]{:S(2)}) collective-permute-start(bf16[80,3712]{1,0:T(8,128)(2,1)S(1)} %get-tuple-element.57), channel_id=1, source_target_pairs={{0,1},{1,0},{2,3},{3,2},{4,5},{5,4},{6,7},{7,6},{8,9},{9,8},{10,11... | collective-permute-start | bytes 1781768 | tf_op jit(solution)/shard_map/ppermute | solution.py:506
  33.0 13.5 %collective-permute-start.12 = (bf16[16,3840]{1,0:T(8,128)(2,1)S(1)}, bf16[16,3840]{1,0:T(8,128)(2,1)S(1)}, u32[]{:S(2)}, u32[]{:S(2)}) collective-permute-start(bf16[16,3840]{1,0:T(8,128)(2,1)S(1)} %get-tuple-element.55), channel_id=1, source_target_pairs={{0,8},{1,9},{2,10},{3,11},{4,12},{5,13},{6,14},{7,15},{8,16},{9,17... | collective-permute-start | bytes 368648 | tf_op jit(solution)/shard_map/ppermute | solution.py:517
  37.2 9.7 %collective-permute-start.11 = (bf16[16,3840]{1,0:T(8,128)(2,1)S(1)}, bf16[16,3840]{1,0:T(8,128)(2,1)S(1)}, u32[]{:S(2)}, u32[]{:S(2)}) collective-permute-start(bf16[16,3840]{1,0:T(8,128)(2,1)S(1)} %get-tuple-element.54.refs_11_), channel_id=1, source_target_pairs={{0,12},{1,13},{2,14},{3,15},{4,8},{5,9},{6,10},{7,11},{8,20},{9,21... | collective-permute-start | bytes 368648 | tf_op jit(solution)/shard_map/ppermute | solution.py:517
  40.1 9.9 %collective-permute-start.14 = (bf16[16,3840]{1,0:T(8,128)(2,1)S(1)}, bf16[16,3840]{1,0:T(8,128)(2,1)S(1)}, u32[]{:S(2)}, u32[]{:S(2)}) collective-permute-start(bf16[16,3840]{1,0:T(8,128)(2,1)S(1)} %get-tuple-element.58), channel_id=1, source_target_pairs={{0,30},{1,31},{2,28},{3,29},{4,26},{5,27},{6,24},{7,25},{8,6},{9,7... | collective-permute-start | bytes 368648 | tf_op jit(solution)/shard_map/ppermute | solution.py:517
  43.6 8.4 %collective-permute-start.15 = (bf16[16,3840]{1,0:T(8,128)(2,1)S(1)}, bf16[16,3840]{1,0:T(8,128)(2,1)S(1)}, u32[]{:S(2)}, u32[]{:S(2)}) collective-permute-start(bf16[16,3840]{1,0:T(8,128)(2,1)S(1)} %get-tuple-element.59), channel_id=1, source_target_pairs={{0,26},{1,27},{2,24},{3,25},{4,30},{5,31},{6,28},{7,29},{8,2},{9,3... | collective-permute-start | bytes 368648 | tf_op jit(solution)/shard_map/ppermute | solution.py:517
  43.9 10.5 %collective-permute-start.16 = (bf16[16,3840]{1,0:T(8,128)(2,1)S(1)}, bf16[16,3840]{1,0:T(8,128)(2,1)S(1)}, u32[]{:S(2)}, u32[]{:S(2)}) collective-permute-start(bf16[16,3840]{1,0:T(8,128)(2,1)S(1)} %get-tuple-element.60), channel_id=1, source_target_pairs={{0,28},{1,29},{2,30},{3,31},{4,24},{5,25},{6,26},{7,27},{8,4},{9,5... | collective-permute-start | bytes 368648 | tf_op jit(solution)/shard_map/ppermute | solution.py:517
  46.5 9.8 %collective-permute-start.17 = (bf16[16,3840]{1,0:T(8,128)(2,1)S(1)}, bf16[16,3840]{1,0:T(8,128)(2,1)S(1)}, u32[]{:S(2)}, u32[]{:S(2)}) collective-permute-start(bf16[16,3840]{1,0:T(8,128)(2,1)S(1)} %get-tuple-element.61), channel_id=1, source_target_pairs={{0,24},{1,25},{2,26},{3,27},{4,28},{5,29},{6,30},{7,31},{8,0},{9,1... | collective-permute-start | bytes 368648 | tf_op jit(solution)/shard_map/ppermute | solution.py:517

commit v7 on v6

--- a/solution.py
+++ b/solution.py
@@ -22,7 +22,7 @@
 
 cost = {
     "backward_chunks": 10,
-    "later": 15,
+    "saved_rows": 15,
     "saved_terms": 15,
     "act_norms": 15,
     "act_gates": 15,
@@ -180,14 +180,6 @@
     )(where, ids.reshape(1, z.tokens), *sources, *tables, *after)
 
 
-def later(chunk, weights, after):
-    def body(chunk, *refs):
-        refs[-1][...] = chunk[...]
-
-    places = "v" + "v" * len(weights) + "a" * len(after)
-    return call(body, places, shape(chunk.shape), [], 8, "later")(chunk, *weights, *after)
-
-
 def collect_rows(z, chunks, last, tile, base=0):
     last[...] = jnp.zeros_like(last)
     for k in range(z.experts):
@@ -316,11 +308,11 @@
     )(*rows, w_gate, w_down, *after)
 
 
-def saved_terms(z, where, saved, after):
+def saved_rows(z, where, saved, weights, after):
     total, slots, width = z.split * z.rows, saved.shape[2], saved.shape[3]
 
     def body(where, saved_any, *refs):
-        hidden_ref, slope_ref, saved_ref, sem = refs[len(after) :]
+        ordered_ref, saved_ref, sem = refs[len(weights) + len(after) :]
         copy = pltpu.make_async_copy(saved_any.at[0, 0], saved_ref, sem)
         copy.start()
         row = lax.broadcasted_iota(jnp.int32, (total, slots), 0)
@@ -333,19 +325,34 @@
         wanted = jnp.where(k < z.experts, source * z.cap + p, -1)
         selector = jnp.where(slot == wanted, 1.0, 0.0).astype(bf16)
         copy.wait()
-        gate_proj = jnp.dot(selector, saved_ref[...], preferred_element_type=f32)
+        ordered_ref[...] = jnp.dot(selector, saved_ref[...], preferred_element_type=f32)
+
+    return call(
+        body,
+        "sh" + "v" * len(weights) + "a" * len(after),
+        shape((total, width), f32),
+        [pltpu.VMEM((slots, width), bf16), pltpu.SemaphoreType.DMA],
+        8,
+        "saved_rows",
+    )(where, saved, *weights, *after)
+
+
+def saved_terms(z, ordered, after):
+    def body(ordered_ref, *refs):
+        hidden_ref, slope_ref = refs[len(after) :]
+        gate_proj = ordered_ref[...]
         sg = jax.nn.sigmoid(gate_proj)
         hidden_ref[...] = (gate_proj * sg).astype(bf16)
         slope_ref[...] = sg * (1.0 + gate_proj * (1.0 - sg))
 
     return call(
         body,
-        "sh" + "a" * len(after),
-        [shape((total, width)), shape((total, width), f32)],
-        [pltpu.VMEM((slots, width), bf16), pltpu.SemaphoreType.DMA],
+        "v" + "a" * len(after),
+        [shape(ordered.shape), shape(ordered.shape, f32)],
+        [],
         8,
         "saved_terms",
-    )(where, saved, *after)
+    )(ordered, *after)
 
 
 def experts_backward(z, rows, hidden, slope, w_gate, w_down, after):
@@ -388,7 +395,7 @@
 
     def body(*refs):
         chunks, last, parts = refs[:count], refs[count], refs[count + 1 : count + 1 + z.split]
-        gates, outs, tile = refs[count + 1 + z.split], refs[-1 - count : -1], refs[-1]
+        gates, out, tile = refs[count + 1 + z.split], refs[-2], refs[-1]
 
         def mixed(at):
             y = parts[0][at : at + 16, :].astype(f32)
@@ -397,19 +404,28 @@
             return route_scale * (gates[at : at + 16, 0:1] * y)
 
         tail = last[...] + mixed(z.tokens)
-        for k, chunk, out in zip(ks, chunks, outs):
+        for i, (k, chunk) in enumerate(zip(ks, chunks)):
             h = chunk[:, : z.width].astype(f32)
-            out[:, : z.width] = (h + mixed(k * z.main)).astype(bf16)
-            put_last(z, tail[k : k + 1, :], chunk, tile, out)
+            rows = out.at[pl.ds(i * 16, 16)]
+            rows[:, : z.width] = (h + mixed(k * z.main)).astype(bf16)
+            put_last(z, tail[k : k + 1, :], chunk, tile, rows)
 
     return call(
         body,
         "v" * (count + z.split + 2) + "a" * len(after),
-        [shape((z.main, z.wide))] * count,
+        shape((count * z.main, z.wide)),
         [pltpu.VMEM((16, fold), f32)],
         8,
         "finish_forward_" + "".join(map(str, ks)),
     )(*[chunks[k] for k in ks], last, *parts, gates, *after)
+
+
+def lower_chunk(z, double, after):
+    def body(double, *refs):
+        refs[-1][...] = double[16:32, :]
+
+    places = "v" + "a" * len(after)
+    return call(body, places, shape((16, z.wide)), [], 8, "lower_chunk")(double, *after)
 
 
 def finish_backward(z, order, chunks, lasts, terms, parts, vectors, after):
@@ -451,14 +467,14 @@
     )(*chunks, *lasts, *terms, *parts, vectors, *after)
 
 
-def order_rows(z, chunks, name):
-    order = z.order
+def order_rows(z, arrays, places, after, name):
+    count = len(arrays)
     lanes = z.tokens + 16 * z.experts
     steps = 7 if z.pieces % 7 == 0 else z.pieces
 
     def body(*refs):
-        chunks, (out_any, out, sems) = refs[: z.experts], refs[z.experts :]
-        chunks = [chunks[order.index(k)] for k in range(z.experts)]
+        arrays, (out_any, out, sems) = refs[:count], refs[count + len(after) :]
+        chunks = [arrays[i].at[pl.ds(at, 16)] for i, at in places]
         tiles = [chunk[:, z.width :] for chunk in chunks]
         token_row = tiles[0].astype(f32)[z.pieces : z.pieces + 1, :lanes]
         token = lax.broadcasted_iota(jnp.int32, (z.tokens, lanes), 0).astype(f32)
@@ -482,22 +498,23 @@
 
     return call(
         body,
-        "v" * z.experts,
+        "v" * count + "a" * len(after),
         shape((z.tokens, z.width)),
         [pltpu.VMEM((z.tokens, z.width), bf16), pltpu.SemaphoreType.DMA((steps,))],
         8,
         name,
         spaces["a"],
-    )(*[chunks[k] for k in order])
+    )(*arrays, *after)
+
+
+def permute_blocks(z, arrays, k):
+    groups = z.experts * z.split
+    pairs = [(i, ((i // z.split) ^ k) * z.split + i % z.split) for i in range(groups)]
+    return [lax.ppermute(array, "ep", pairs) for array in arrays]
 
 
 def dispatch(z, chunks):
-    groups = z.experts * z.split
-    got = [chunks[0]] + [None] * (z.experts - 1)
-    for k in reversed(range(1, z.experts)):
-        pairs = [(i, ((i // z.split) ^ k) * z.split + i % z.split) for i in range(groups)]
-        got[k] = lax.ppermute(chunks[k], "ep", pairs)
-    return got
+    return [chunks[0]] + [permute_blocks(z, [chunks[k]], k)[0] for k in range(1, z.experts)]
 
 
 def to_core(z, array, m):
@@ -539,39 +556,41 @@
         [fwd_chunks[0]],
         "backward_chunks",
     )
+    bwd_own = dispatch(z, bwd_chunks)
+
     normed, gates, fwd_last = normed_rows(z, fwd_own, vectors)
-    bwd_chunks[z.experts // 2] = later(bwd_chunks[z.experts // 2], [w_gate, w_down], [gates])
-    bwd_own = dispatch(z, bwd_chunks)
     fwd_all = [normed] + [to_core(z, normed, m) for m in others]
-    fwd_parts = experts_forward(z, fwd_all, w_gate, w_down, [])
-    hidden, slope = saved_terms(z, where, saved_gate, [fwd_parts[0]])
+    ordered = saved_rows(z, where, saved_gate, [w_gate, w_down], [gates])
+    fwd_parts = experts_forward(z, fwd_all, w_gate, w_down, [ordered])
+    hidden, slope = saved_terms(z, ordered, [fwd_parts[0]])
     fwd_parts = [fwd_parts[0]] + [to_core(z, fwd_parts[m], m) for m in others]
-    fwd_done = {}
 
     def finish(ks, after):
-        outs = finish_forward(z, ks, fwd_own, fwd_last, fwd_parts, gates, after)
-        for k, out in zip(ks, outs):
-            fwd_done[k] = to_section(z, out, k, 1)
-        return outs[0]
-
-    order = z.order
-    first = finish(order[:2], [hidden])
-    grads, grad_last = grad_rows_of(z, bwd_own, [first])
+        return finish_forward(z, ks, fwd_own, fwd_last, fwd_parts, gates, after)
+
+    half = max(3, z.experts // 2 + 1)
+    double = finish([0, 1], [hidden])
+    got = to_section(z, double, 0, 1)
+    grads, grad_last = grad_rows_of(z, bwd_own, [double])
     grad_all = [grads] + [to_core(z, grads, m) for m in others]
     inv, act_last = act_norms(z, bwd_own, [grads])
+    fwd_done = [to_section(z, finish([k], [inv]), k, 1) for k in range(2, half)]
     bwd_parts = experts_backward(z, grad_all, hidden, slope, w_gate, w_down, [inv])
-    affinity = act_gates(
-        z, bwd_own, act_last, inv, vectors, [bwd_parts[0], *fwd_done.values()]
-    )
-    second = finish(order[2:], [affinity])
+    affinity = act_gates(z, bwd_own, act_last, inv, vectors, [bwd_parts[0], got])
+    (relayed,) = permute_blocks(z, [lower_chunk(z, got, [affinity])], 1)
+    third = [finish([k], [affinity]) for k in range(half, z.experts)]
+    fwd_done += [to_section(z, out, k, 1) for k, out in zip(range(half, z.experts), third)]
     bwd_parts = [bwd_parts[0]] + [to_core(z, bwd_parts[m], m) for m in others]
     bwd_out = finish_backward(
-        z, order, bwd_own, [grad_last, act_last], [inv, affinity], bwd_parts, vectors, [second]
+        z, z.order, bwd_own, [grad_last, act_last], [inv, affinity], bwd_parts, vectors, third
     )
-    bwd_done = {k: to_section(z, out, k, -1) for k, out in zip(order, bwd_out)}
-    fwd_done = [fwd_done[k] for k in range(z.experts)]
-    bwd_done = [bwd_done[k] for k in range(z.experts)]
-    return (order_rows(z, fwd_done, "forward_rows"), order_rows(z, bwd_done, "backward_rows"))
+    bwd_done = {k: to_section(z, out, k, -1) for k, out in zip(z.order, bwd_out)}
+
+    places = [(k, 0) for k in range(z.experts)]
+    fwd_next = order_rows(z, [got, relayed, *fwd_done], places, [], "forward_rows")
+    places = [(z.order.index(k), 0) for k in range(z.experts)]
+    bwd_next = order_rows(z, [bwd_done[k] for k in z.order], places, [], "backward_rows")
+    return (fwd_next, bwd_next)
 
 
 def solution(mesh):

time: 57.4 us -> 51.8 us (0.902)
  starting transfers between devices: 26.9 us -> 20.7 us
    ppermute x8 -> x7, starting transfers between devices: 17.5 us -> 10.4 us  [to_section(): return lax.ppermute(chunk, ('pp', 'ep'), pairs)]
    ppermute x8 -> x7, waiting for transfers between devices: 8.32 us -> 9.66 us  [to_section(): return lax.ppermute(chunk, ('pp', 'ep'), pairs)]
    ppermute x4, waiting for transfers between devices: 3.02 us -> 1.96 us  [to_core(): return lax.ppermute(array, 'ep', pairs)]
    ppermute x6 -> x7, starting transfers between devices: 8.82 us -> 9.66 us  [permute_blocks(): return [lax.ppermute(array, 'ep', pairs) for array in arrays]]
    pallas_call x15 -> x17, Pallas kernels: 14.9 us -> 15 us  [run(): return kernel(*arrays)]
    ppermute x6 -> x7, waiting for transfers between devices: 3.33 us -> 3.36 us  [permute_blocks(): return [lax.ppermute(array, 'ep', pairs) for array in arrays]]
  transfers between devices with their start and end apart: 18 -> 18, of which waited for: 9 -> 9; matrix products, arithmetic and copies ran while one was open for 0% -> 0% of each run, Pallas kernels for 21% -> 23%
where the time goes in v7:
time: 51.8 us; the launch traced here: 51.6 us
  starting transfers between devices  20.7 us (40%)
  Pallas kernels  15 us (29%)
  waiting for transfers between devices  15 us (29%)
  between operations  0.78 us (2%)
    pallas_call x17, Pallas kernels, run(): return kernel(*arrays)  15 us
    ppermute x7, starting transfers between devices, to_section(): return lax.ppermute(chunk, ('pp', 'ep'), pairs)  10.4 us
    ppermute x7, waiting for transfers between devices, to_section(): return lax.ppermute(chunk, ('pp', 'ep'), pairs)  9.66 us
    ppermute x7, starting transfers between devices, permute_blocks(): return [lax.ppermute(array, 'ep', pairs) for array in arrays]  9.66 us
    ppermute x7, waiting for transfers between devices, permute_blocks(): return [lax.ppermute(array, 'ep', pairs) for array in arrays]  3.36 us
    ppermute x4, waiting for transfers between devices, to_core(): return lax.ppermute(array, 'ep', pairs)  1.96 us
  transfers between devices with their start and end apart: 18, of which 9 were waited for; matrix products, arithmetic and copies ran while one was open for 0% of the time, Pallas kernels for 23%

profile of v7, /device:TPU:0, one launch (start us, length us, event | category | flops | bytes accessed | tf_op | source)
XLA Modules:
  0.0 51.6 jit_solution(13605176118059113402)
XLA Ops:
  0.7 2.0 %forward_chunks.1 = (bf16[16,3840]{1,0:T(8,128)(2,1)S(1)}, bf16[16,3840]{1,0:T(8,128)(2,1)S(1)}, bf16[16,3840]{1,0:T(8,128)(2,1)S(1)}, bf16[16,3840]{1,0:T(8,128)(2,1)S(1)}) custom-call(s32[2]{0:T(128)S(1)} %pad_add_fusion.where, s32[1,64]{1,0:T(1,128)} %bitcast.5, bf16[64,3584]{1,0:T(8,128)(2,1)} %refs_0_.3), custom_call_target="tpu_custom_call" | custom-call | flops 100000000 | bytes 1000 | tf_op jit(solution)/shard_map/forward_chunks/pallas_call | solution.py:38
  2.7 3.0 %collective-permute-start = (bf16[16,3840]{1,0:T(8,128)(2,1)S(1)}, bf16[16,3840]{1,0:T(8,128)(2,1)S(1)}, u32[]{:S(2)}, u32[]{:S(2)}) collective-permute-start(bf16[16,3840]{1,0:T(8,128)(2,1)S(1)} %get-tuple-element.29), channel_id=1, source_target_pairs={{0,2},{1,3},{2,0},{3,1},{4,6},{5,7},{6,4},{7,5},{8,10},{9,11},{10,... | collective-permute-start | bytes 368648 | tf_op jit(solution)/shard_map/ppermute | solution.py:513
  5.7 1.5 %collective-permute-start.1 = (bf16[16,3840]{1,0:T(8,128)(2,1)S(1)}, bf16[16,3840]{1,0:T(8,128)(2,1)S(1)}, u32[]{:S(2)}, u32[]{:S(2)}) collective-permute-start(bf16[16,3840]{1,0:T(8,128)(2,1)S(1)} %get-tuple-element.30), channel_id=1, source_target_pairs={{0,6},{1,7},{2,4},{3,5},{4,2},{5,3},{6,0},{7,1},{8,14},{9,15},{10,... | collective-permute-start | bytes 368648 | tf_op jit(solution)/shard_map/ppermute | solution.py:513
  7.3 2.8 %backward_chunks.1 = (bf16[32,3840]{1,0:T(8,128)(2,1)S(1)}, bf16[32,3840]{1,0:T(8,128)(2,1)S(1)}, bf16[32,3840]{1,0:T(8,128)(2,1)S(1)}, bf16[32,3840]{1,0:T(8,128)(2,1)S(1)}, f32[8,3584]{1,0:T(8,128)S(1)}) custom-call(s32[2]{0:T(128)S(1)} %pad_add_fusion.where, s32[1,64]{1,0:T(1,128)} %bitcast.7, bf16[64,3584]{1,0:T(8,128)(2,1)} %refs_0_.4, ...), custom_call_target="tpu_custom_call" | custom-call | flops 10000000000 | bytes 1000 | tf_op jit(solution)/shard_map/backward_chunks/pallas_call | solution.py:38
  10.1 2.0 %collective-permute-start.6 = (bf16[32,3840]{1,0:T(8,128)(2,1)S(1)}, bf16[32,3840]{1,0:T(8,128)(2,1)S(1)}, u32[]{:S(2)}, u32[]{:S(2)}) collective-permute-start(bf16[32,3840]{1,0:T(8,128)(2,1)S(1)} %get-tuple-element.40), channel_id=1, source_target_pairs={{0,2},{1,3},{2,0},{3,1},{4,6},{5,7},{6,4},{7,5},{8,10},{9,11},{10,... | collective-permute-start | bytes 737288 | tf_op jit(solution)/shard_map/ppermute | solution.py:513
  12.1 1.5 %collective-permute-start.7 = (bf16[32,3840]{1,0:T(8,128)(2,1)S(1)}, bf16[32,3840]{1,0:T(8,128)(2,1)S(1)}, u32[]{:S(2)}, u32[]{:S(2)}) collective-permute-start(bf16[32,3840]{1,0:T(8,128)(2,1)S(1)} %get-tuple-element.41), channel_id=1, source_target_pairs={{0,4},{1,5},{2,6},{3,7},{4,0},{5,1},{6,2},{7,3},{8,12},{9,13},{10,... | collective-permute-start | bytes 737288 | tf_op jit(solution)/shard_map/ppermute | solution.py:513
  13.6 1.6 %collective-permute-done.2.refs_2_.refs_0_ = bf16[16,3840]{1,0:T(8,128)(2,1)S(1)} collective-permute-done((bf16[16,3840]{1,0:T(8,128)(2,1)S(1)}, bf16[16,3840]{1,0:T(8,128)(2,1)S(1)}, u32[]{:S(2)}, u32[]{:S(2)}) %collective-permute-start.2) | collective-permute-done | bytes 122912 | tf_op jit(solution)/shard_map/ppermute | solution.py:513
  15.3 0.5 %normed_rows.1 = (bf16[80,3584]{1,0:T(8,128)(2,1)S(1)}, f32[80,128]{1,0:T(8,128)S(1)}, f32[16,3584]{1,0:T(8,128)S(1)}) custom-call(bf16[16,3840]{1,0:T(8,128)(2,1)S(1)} %collective-permute-done.1.refs_0_, bf16[16,3840]{1,0:T(8,128)(2,1)S(1)} %collective-permute-done.refs_1_, bf16[16,3840]{1,0:T(8,128)(2,1)S(1)} %collective-permute-done.2.refs_2_.refs_0_, ...), custom_call_target="tpu_custom_call" | custom-call | flops 100000000 | bytes 1000 | tf_op jit(solution)/shard_map/normed_rows/pallas_call | solution.py:38
  15.8 1.6 %saved_rows.1.refs_4_.ordered_ref = f32[160,512]{1,0:T(8,128)S(1)} custom-call(s32[2]{0:T(128)S(1)} %pad_add_fusion.where, bf16[1,1,136,512]{3,2,1,0:T(8,128)(2,1)} %saved_any.1, bf16[1,3584,512]{2,1,0:T(8,128)(2,1)S(1)} %copy-done, bf16[1,512,3584]{2,1,0:T(8,128)(2,1)S(1)} %copy-done.1, f32[80,128]{1,0:T(8,128)S(1)} %get-tuple-element.35.refs_2_.refs_5_.refs_4_), custom_call_target="tpu_custom_call" | custom-call | flops 15000000512 | bytes 1000 | tf_op jit(solution)/shard_map/saved_rows/pallas_call | solution.py:38
  17.5 0.3 collective-permute-done.3.refs_1_
  17.8 1.5 %experts_forward.1 = (bf16[80,3584]{1,0:T(8,128)(2,1)S(1)}, bf16[80,3584]{1,0:T(8,128)(2,1)S(1)}) custom-call(bf16[80,3584]{1,0:T(8,128)(2,1)S(1)} %get-tuple-element.34.refs_0_, bf16[80,3584]{1,0:T(8,128)(2,1)S(1)} %collective-permute-done.3.refs_1_, bf16[1,3584,512]{2,1,0:T(8,128)(2,1)S(1)} %copy-done, bf16[1,512,3584]{2,1,0:T(8,128)(2,1)S(1)} %copy-done.1, ...), custom_call_target="tpu_custom_call" | custom-call | flops 100000000 | bytes 1000 | tf_op jit(solution)/shard_map/experts_forward/pallas_call | solution.py:38
  19.3 0.3 collective-permute-start.4
  19.6 1.7 %collective-permute-done.4.refs_4_.refs_3_ = bf16[80,3584]{1,0:T(8,128)(2,1)S(1)} collective-permute-done((bf16[80,3584]{1,0:T(8,128)(2,1)S(1)}, bf16[80,3584]{1,0:T(8,128)(2,1)S(1)}, u32[]{:S(2)}, u32[]{:S(2)}) %collective-permute-start.4) | collective-permute-done | bytes 573472 | tf_op jit(solution)/shard_map/ppermute | solution.py:523
  21.5 1.6 %collective-permute-start.5 = (bf16[32,3840]{1,0:T(8,128)(2,1)S(1)}, bf16[32,3840]{1,0:T(8,128)(2,1)S(1)}, u32[]{:S(2)}, u32[]{:S(2)}) collective-permute-start(bf16[32,3840]{1,0:T(8,128)(2,1)S(1)} %finish_forward_01.1.refs_4_), channel_id=1, source_target_pairs={{0,8},{1,9},{2,10},{3,11},{4,12},{5,13},{6,14},{7,15},{8,16},{9,17... | collective-permute-start | bytes 737288 | tf_op jit(solution)/shard_map/ppermute | solution.py:534
  23.2 1.7 %collective-permute-done.7.refs_2_ = bf16[32,3840]{1,0:T(8,128)(2,1)S(1)} collective-permute-done((bf16[32,3840]{1,0:T(8,128)(2,1)S(1)}, bf16[32,3840]{1,0:T(8,128)(2,1)S(1)}, u32[]{:S(2)}, u32[]{:S(2)}) %collective-permute-start.7) | collective-permute-done | bytes 245792 | tf_op jit(solution)/shard_map/ppermute | solution.py:513
  25.5 1.6 %collective-permute-start.11 = (bf16[16,3840]{1,0:T(8,128)(2,1)S(1)}, bf16[16,3840]{1,0:T(8,128)(2,1)S(1)}, u32[]{:S(2)}, u32[]{:S(2)}) collective-permute-start(bf16[16,3840]{1,0:T(8,128)(2,1)S(1)} %finish_forward_2.1), channel_id=1, source_target_pairs={{0,12},{1,13},{2,14},{3,15},{4,8},{5,9},{6,10},{7,11},{8,20},{9,21... | collective-permute-start | bytes 368648 | tf_op jit(solution)/shard_map/ppermute | solution.py:534
  27.1 2.6 %experts_backward.1 = (bf16[80,3712]{1,0:T(8,128)(2,1)S(1)}, bf16[80,3712]{1,0:T(8,128)(2,1)S(1)}) custom-call(bf16[80,3584]{1,0:T(8,128)(2,1)S(1)} %get-tuple-element.43.refs_4_.refs_0_, bf16[80,3584]{1,0:T(8,128)(2,1)S(1)} %collective-permute-done.9.refs_1_, bf16[160,512]{1,0:T(8,128)(2,1)S(1)} %get-tuple-element.38.refs_6_.refs_2_, ...), custom_call_target="tpu_custom_call" | custom-call | flops 100000000 | bytes 1000 | tf_op jit(solution)/shard_map/experts_backward/pallas_call | solution.py:38
  29.7 0.3 collective-permute-start.13
  29.9 2.2 %collective-permute-done.5.refs_8_.double.refs_0_ = bf16[32,3840]{1,0:T(8,128)(2,1)S(1)} collective-permute-done((bf16[32,3840]{1,0:T(8,128)(2,1)S(1)}, bf16[32,3840]{1,0:T(8,128)(2,1)S(1)}, u32[]{:S(2)}, u32[]{:S(2)}) %collective-permute-start.5) | collective-permute-done | bytes 245792 | tf_op jit(solution)/shard_map/ppermute | solution.py:534
  32.1 0.4 act_gates.1.refs_0_.refs_5_.refs_7_
  32.6 1.6 %collective-permute-start.10 = (bf16[16,3840]{1,0:T(8,128)(2,1)S(1)}, bf16[16,3840]{1,0:T(8,128)(2,1)S(1)}, u32[]{:S(2)}, u32[]{:S(2)}) collective-permute-start(bf16[16,3840]{1,0:T(8,128)(2,1)S(1)} %lower_chunk.1), channel_id=1, source_target_pairs={{0,2},{1,3},{2,0},{3,1},{4,6},{5,7},{6,4},{7,5},{8,10},{9,11},{10,... | collective-permute-start | bytes 368648 | tf_op jit(solution)/shard_map/ppermute | solution.py:513
  34.3 0.3 collective-permute-start.12
  34.6 0.7 %finish_backward.1 = (bf16[16,3840]{1,0:T(8,128)(2,1)S(1)}, bf16[16,3840]{1,0:T(8,128)(2,1)S(1)}, bf16[16,3840]{1,0:T(8,128)(2,1)S(1)}, bf16[16,3840]{1,0:T(8,128)(2,1)S(1)}) custom-call(bf16[32,3840]{1,0:T(8,128)(2,1)S(1)} %get-tuple-element.39.refs_0_, bf16[32,3840]{1,0:T(8,128)(2,1)S(1)} %collective-permute-done.6.refs_1_, ...), custom_call_target="tpu_custom_call" | custom-call | flops 100000000 | bytes 1000 | tf_op jit(solution)/shard_map/finish_backward/pallas_call | solution.py:38
  35.3 5.4 %collective-permute-start.14 = (bf16[16,3840]{1,0:T(8,128)(2,1)S(1)}, bf16[16,3840]{1,0:T(8,128)(2,1)S(1)}, u32[]{:S(2)}, u32[]{:S(2)}) collective-permute-start(bf16[16,3840]{1,0:T(8,128)(2,1)S(1)} %get-tuple-element.50), channel_id=1, source_target_pairs={{0,30},{1,31},{2,28},{3,29},{4,26},{5,27},{6,24},{7,25},{8,6},{9,7... | collective-permute-start | bytes 368648 | tf_op jit(solution)/shard_map/ppermute | solution.py:534
  40.7 0.9 %collective-permute-start.16 = (bf16[16,3840]{1,0:T(8,128)(2,1)S(1)}, bf16[16,3840]{1,0:T(8,128)(2,1)S(1)}, u32[]{:S(2)}, u32[]{:S(2)}) collective-permute-start(bf16[16,3840]{1,0:T(8,128)(2,1)S(1)} %get-tuple-element.52), channel_id=1, source_target_pairs={{0,28},{1,29},{2,30},{3,31},{4,24},{5,25},{6,26},{7,27},{8,4},{9,5... | collective-permute-start | bytes 368648 | tf_op jit(solution)/shard_map/ppermute | solution.py:534
  41.6 0.5 %collective-permute-start.17 = (bf16[16,3840]{1,0:T(8,128)(2,1)S(1)}, bf16[16,3840]{1,0:T(8,128)(2,1)S(1)}, u32[]{:S(2)}, u32[]{:S(2)}) collective-permute-start(bf16[16,3840]{1,0:T(8,128)(2,1)S(1)} %get-tuple-element.53), channel_id=1, source_target_pairs={{0,24},{1,25},{2,26},{3,27},{4,28},{5,29},{6,30},{7,31},{8,0},{9,1... | collective-permute-start | bytes 368648 | tf_op jit(solution)/shard_map/ppermute | solution.py:534
  42.1 1.6 %collective-permute-done.12.refs_3_ = bf16[16,3840]{1,0:T(8,128)(2,1)S(1)} collective-permute-done((bf16[16,3840]{1,0:T(8,128)(2,1)S(1)}, bf16[16,3840]{1,0:T(8,128)(2,1)S(1)}, u32[]{:S(2)}, u32[]{:S(2)}) %collective-permute-start.12) | collective-permute-done | bytes 122912 | tf_op jit(solution)/shard_map/ppermute | solution.py:534
  43.7 1.0 %forward_rows.1 = bf16[64,3584]{1,0:T(8,128)(2,1)} custom-call(bf16[32,3840]{1,0:T(8,128)(2,1)S(1)} %collective-permute-done.5.refs_8_.double.refs_0_, bf16[16,3840]{1,0:T(8,128)(2,1)S(1)} %collective-permute-done.10.refs_1_, bf16[16,3840]{1,0:T(8,128)(2,1)S(1)} %collective-permute-done.11.refs_2_, bf16[16,3840]{1,0:T(8,128)(2,1)S(1)} %collective-permute-done.12.refs_3_), custom_call_target="tpu_custom_call" | custom-call | flops 100000000 | bytes 1000 | tf_op jit(solution)/shard_map/forward_rows/pallas_call | solution.py:38
  44.8 3.1 %collective-permute-done.15.refs_1_ = bf16[16,3840]{1,0:T(8,128)(2,1)S(1)} collective-permute-done((bf16[16,3840]{1,0:T(8,128)(2,1)S(1)}, bf16[16,3840]{1,0:T(8,128)(2,1)S(1)}, u32[]{:S(2)}, u32[]{:S(2)}) %collective-permute-start.15) | collective-permute-done | bytes 122912 | tf_op jit(solution)/shard_map/ppermute | solution.py:534
  47.8 2.0 %collective-permute-done.16.refs_2_ = bf16[16,3840]{1,0:T(8,128)(2,1)S(1)} collective-permute-done((bf16[16,3840]{1,0:T(8,128)(2,1)S(1)}, bf16[16,3840]{1,0:T(8,128)(2,1)S(1)}, u32[]{:S(2)}, u32[]{:S(2)}) %collective-permute-start.16) | collective-permute-done | bytes 122912 | tf_op jit(solution)/shard_map/ppermute | solution.py:534
  49.8 0.8 %collective-permute-done.17.refs_3_ = bf16[16,3840]{1,0:T(8,128)(2,1)S(1)} collective-permute-done((bf16[16,3840]{1,0:T(8,128)(2,1)S(1)}, bf16[16,3840]{1,0:T(8,128)(2,1)S(1)}, u32[]{:S(2)}, u32[]{:S(2)}) %collective-permute-start.17) | collective-permute-done | bytes 122912 | tf_op jit(solution)/shard_map/ppermute | solution.py:534
  50.6 1.0 %backward_rows.1 = bf16[64,3584]{1,0:T(8,128)(2,1)} custom-call(bf16[16,3840]{1,0:T(8,128)(2,1)S(1)} %collective-permute-done.14.refs_0_, bf16[16,3840]{1,0:T(8,128)(2,1)S(1)} %collective-permute-done.15.refs_1_, bf16[16,3840]{1,0:T(8,128)(2,1)S(1)} %collective-permute-done.16.refs_2_, bf16[16,3840]{1,0:T(8,128)(2,1)S(1)} %collective-permute-done.17.refs_3_), custom_call_target="tpu_custom_call" | custom-call | flops 100000000 | bytes 1000 | tf_op jit(solution)/shard_map/backward_rows/pallas_call | solution.py:38
  (26 shorter events, 1.3 us)
Async XLA Ops:
  2.7 10.9 %collective-permute-start = (bf16[16,3840]{1,0:T(8,128)(2,1)S(1)}, bf16[16,3840]{1,0:T(8,128)(2,1)S(1)}, u32[]{:S(2)}, u32[]{:S(2)}) collective-permute-start(bf16[16,3840]{1,0:T(8,128)(2,1)S(1)} %get-tuple-element.29), channel_id=1, source_target_pairs={{0,2},{1,3},{2,0},{3,1},{4,6},{5,7},{6,4},{7,5},{8,10},{9,11},{10,... | collective-permute-start | bytes 368648 | tf_op jit(solution)/shard_map/ppermute | solution.py:513
  5.7 7.9 %collective-permute-start.1 = (bf16[16,3840]{1,0:T(8,128)(2,1)S(1)}, bf16[16,3840]{1,0:T(8,128)(2,1)S(1)}, u32[]{:S(2)}, u32[]{:S(2)}) collective-permute-start(bf16[16,3840]{1,0:T(8,128)(2,1)S(1)} %get-tuple-element.30), channel_id=1, source_target_pairs={{0,6},{1,7},{2,4},{3,5},{4,2},{5,3},{6,0},{7,1},{8,14},{9,15},{10,... | collective-permute-start | bytes 368648 | tf_op jit(solution)/shard_map/ppermute | solution.py:513
  7.2 8.1 %collective-permute-start.2 = (bf16[16,3840]{1,0:T(8,128)(2,1)S(1)}, bf16[16,3840]{1,0:T(8,128)(2,1)S(1)}, u32[]{:S(2)}, u32[]{:S(2)}) collective-permute-start(bf16[16,3840]{1,0:T(8,128)(2,1)S(1)} %get-tuple-element.31), channel_id=1, source_target_pairs={{0,4},{1,5},{2,6},{3,7},{4,0},{5,1},{6,2},{7,3},{8,12},{9,13},{10,... | collective-permute-start | bytes 368648 | tf_op jit(solution)/shard_map/ppermute | solution.py:513
  7.3 8.6 %copy-start = (bf16[1,3584,512]{2,1,0:T(8,128)(2,1)S(1)}, bf16[1,3584,512]{2,1,0:T(8,128)(2,1)}, u32[]{:S(2)}) copy-start(bf16[1,3584,512]{2,1,0:T(8,128)(2,1)} %refs_4_.1) | copy-start | bytes 11010052
  7.3 8.6 %copy-start.1 = (bf16[1,512,3584]{2,1,0:T(8,128)(2,1)S(1)}, bf16[1,512,3584]{2,1,0:T(8,128)(2,1)}, u32[]{:S(2)}) copy-start(bf16[1,512,3584]{2,1,0:T(8,128)(2,1)} %refs_5_.1) | copy-start | bytes 11010052
  10.1 13.1 %collective-permute-start.6 = (bf16[32,3840]{1,0:T(8,128)(2,1)S(1)}, bf16[32,3840]{1,0:T(8,128)(2,1)S(1)}, u32[]{:S(2)}, u32[]{:S(2)}) collective-permute-start(bf16[32,3840]{1,0:T(8,128)(2,1)S(1)} %get-tuple-element.40), channel_id=1, source_target_pairs={{0,2},{1,3},{2,0},{3,1},{4,6},{5,7},{6,4},{7,5},{8,10},{9,11},{10,... | collective-permute-start | bytes 737288 | tf_op jit(solution)/shard_map/ppermute | solution.py:513
  12.1 12.8 %collective-permute-start.7 = (bf16[32,3840]{1,0:T(8,128)(2,1)S(1)}, bf16[32,3840]{1,0:T(8,128)(2,1)S(1)}, u32[]{:S(2)}, u32[]{:S(2)}) collective-permute-start(bf16[32,3840]{1,0:T(8,128)(2,1)S(1)} %get-tuple-element.41), channel_id=1, source_target_pairs={{0,4},{1,5},{2,6},{3,7},{4,0},{5,1},{6,2},{7,3},{8,12},{9,13},{10,... | collective-permute-start | bytes 737288 | tf_op jit(solution)/shard_map/ppermute | solution.py:513
  13.6 11.3 %collective-permute-start.8 = (bf16[32,3840]{1,0:T(8,128)(2,1)S(1)}, bf16[32,3840]{1,0:T(8,128)(2,1)S(1)}, u32[]{:S(2)}, u32[]{:S(2)}) collective-permute-start(bf16[32,3840]{1,0:T(8,128)(2,1)S(1)} %get-tuple-element.42), channel_id=1, source_target_pairs={{0,6},{1,7},{2,4},{3,5},{4,2},{5,3},{6,0},{7,1},{8,14},{9,15},{10,... | collective-permute-start | bytes 737288 | tf_op jit(solution)/shard_map/ppermute | solution.py:513
  15.8 2.0 %collective-permute-start.3 = (bf16[80,3584]{1,0:T(8,128)(2,1)S(1)}, bf16[80,3584]{1,0:T(8,128)(2,1)S(1)}, u32[]{:S(2)}, u32[]{:S(2)}) collective-permute-start(bf16[80,3584]{1,0:T(8,128)(2,1)S(1)} %get-tuple-element.34.refs_0_), channel_id=1, source_target_pairs={{0,1},{1,0},{2,3},{3,2},{4,5},{5,4},{6,7},{7,6},{8,9},{9,8},{10,11... | collective-permute-start | bytes 1720328 | tf_op jit(solution)/shard_map/ppermute | solution.py:523
  19.3 2.0 %collective-permute-start.4 = (bf16[80,3584]{1,0:T(8,128)(2,1)S(1)}, bf16[80,3584]{1,0:T(8,128)(2,1)S(1)}, u32[]{:S(2)}, u32[]{:S(2)}) collective-permute-start(bf16[80,3584]{1,0:T(8,128)(2,1)S(1)} %get-tuple-element.37), channel_id=1, source_target_pairs={{0,1},{1,0},{2,3},{3,2},{4,5},{5,4},{6,7},{7,6},{8,9},{9,8},{10,11... | collective-permute-start | bytes 1720328 | tf_op jit(solution)/shard_map/ppermute | solution.py:523
  21.5 10.6 %collective-permute-start.5 = (bf16[32,3840]{1,0:T(8,128)(2,1)S(1)}, bf16[32,3840]{1,0:T(8,128)(2,1)S(1)}, u32[]{:S(2)}, u32[]{:S(2)}) collective-permute-start(bf16[32,3840]{1,0:T(8,128)(2,1)S(1)} %finish_forward_01.1.refs_4_), channel_id=1, source_target_pairs={{0,8},{1,9},{2,10},{3,11},{4,12},{5,13},{6,14},{7,15},{8,16},{9,17... | collective-permute-start | bytes 737288 | tf_op jit(solution)/shard_map/ppermute | solution.py:534
  25.0 2.1 %collective-permute-start.9 = (bf16[80,3584]{1,0:T(8,128)(2,1)S(1)}, bf16[80,3584]{1,0:T(8,128)(2,1)S(1)}, u32[]{:S(2)}, u32[]{:S(2)}) collective-permute-start(bf16[80,3584]{1,0:T(8,128)(2,1)S(1)} %get-tuple-element.43.refs_4_.refs_0_), channel_id=1, source_target_pairs={{0,1},{1,0},{2,3},{3,2},{4,5},{5,4},{6,7},{7,6},{8,9},{9,8},{10,11... | collective-permute-start | bytes 1720328 | tf_op jit(solution)/shard_map/ppermute | solution.py:523
  25.5 15.2 %collective-permute-start.11 = (bf16[16,3840]{1,0:T(8,128)(2,1)S(1)}, bf16[16,3840]{1,0:T(8,128)(2,1)S(1)}, u32[]{:S(2)}, u32[]{:S(2)}) collective-permute-start(bf16[16,3840]{1,0:T(8,128)(2,1)S(1)} %finish_forward_2.1), channel_id=1, source_target_pairs={{0,12},{1,13},{2,14},{3,15},{4,8},{5,9},{6,10},{7,11},{8,20},{9,21... | collective-permute-start | bytes 368648 | tf_op jit(solution)/shard_map/ppermute | solution.py:534
  29.7 4.9 %collective-permute-start.13 = (bf16[80,3712]{1,0:T(8,128)(2,1)S(1)}, bf16[80,3712]{1,0:T(8,128)(2,1)S(1)}, u32[]{:S(2)}, u32[]{:S(2)}) collective-permute-start(bf16[80,3712]{1,0:T(8,128)(2,1)S(1)} %get-tuple-element.49), channel_id=1, source_target_pairs={{0,1},{1,0},{2,3},{3,2},{4,5},{5,4},{6,7},{7,6},{8,9},{9,8},{10,11... | collective-permute-start | bytes 1781768 | tf_op jit(solution)/shard_map/ppermute | solution.py:523
  32.6 9.0 %collective-permute-start.10 = (bf16[16,3840]{1,0:T(8,128)(2,1)S(1)}, bf16[16,3840]{1,0:T(8,128)(2,1)S(1)}, u32[]{:S(2)}, u32[]{:S(2)}) collective-permute-start(bf16[16,3840]{1,0:T(8,128)(2,1)S(1)} %lower_chunk.1), channel_id=1, source_target_pairs={{0,2},{1,3},{2,0},{3,1},{4,6},{5,7},{6,4},{7,5},{8,10},{9,11},{10,... | collective-permute-start | bytes 368648 | tf_op jit(solution)/shard_map/ppermute | solution.py:513
  34.3 9.5 %collective-permute-start.12 = (bf16[16,3840]{1,0:T(8,128)(2,1)S(1)}, bf16[16,3840]{1,0:T(8,128)(2,1)S(1)}, u32[]{:S(2)}, u32[]{:S(2)}) collective-permute-start(bf16[16,3840]{1,0:T(8,128)(2,1)S(1)} %finish_forward_3.1.refs_11_), channel_id=1, source_target_pairs={{0,14},{1,15},{2,12},{3,13},{4,10},{5,11},{6,8},{7,9},{8,22},{9,23... | collective-permute-start | bytes 368648 | tf_op jit(solution)/shard_map/ppermute | solution.py:534
  35.3 9.5 %collective-permute-start.14 = (bf16[16,3840]{1,0:T(8,128)(2,1)S(1)}, bf16[16,3840]{1,0:T(8,128)(2,1)S(1)}, u32[]{:S(2)}, u32[]{:S(2)}) collective-permute-start(bf16[16,3840]{1,0:T(8,128)(2,1)S(1)} %get-tuple-element.50), channel_id=1, source_target_pairs={{0,30},{1,31},{2,28},{3,29},{4,26},{5,27},{6,24},{7,25},{8,6},{9,7... | collective-permute-start | bytes 368648 | tf_op jit(solution)/shard_map/ppermute | solution.py:534
  40.7 7.2 %collective-permute-start.15 = (bf16[16,3840]{1,0:T(8,128)(2,1)S(1)}, bf16[16,3840]{1,0:T(8,128)(2,1)S(1)}, u32[]{:S(2)}, u32[]{:S(2)}) collective-permute-start(bf16[16,3840]{1,0:T(8,128)(2,1)S(1)} %get-tuple-element.51), channel_id=1, source_target_pairs={{0,26},{1,27},{2,24},{3,25},{4,30},{5,31},{6,28},{7,29},{8,2},{9,3... | collective-permute-start | bytes 368648 | tf_op jit(solution)/shard_map/ppermute | solution.py:534
  40.7 9.1 %collective-permute-start.16 = (bf16[16,3840]{1,0:T(8,128)(2,1)S(1)}, bf16[16,3840]{1,0:T(8,128)(2,1)S(1)}, u32[]{:S(2)}, u32[]{:S(2)}) collective-permute-start(bf16[16,3840]{1,0:T(8,128)(2,1)S(1)} %get-tuple-element.52), channel_id=1, source_target_pairs={{0,28},{1,29},{2,30},{3,31},{4,24},{5,25},{6,26},{7,27},{8,4},{9,5... | collective-permute-start | bytes 368648 | tf_op jit(solution)/shard_map/ppermute | solution.py:534
  41.6 9.0 %collective-permute-start.17 = (bf16[16,3840]{1,0:T(8,128)(2,1)S(1)}, bf16[16,3840]{1,0:T(8,128)(2,1)S(1)}, u32[]{:S(2)}, u32[]{:S(2)}) collective-permute-start(bf16[16,3840]{1,0:T(8,128)(2,1)S(1)} %get-tuple-element.53), channel_id=1, source_target_pairs={{0,24},{1,25},{2,26},{3,27},{4,28},{5,29},{6,30},{7,31},{8,0},{9,1... | collective-permute-start | bytes 368648 | tf_op jit(solution)/shard_map/ppermute | solution.py:534

commit v8 on v7

--- a/solution.py
+++ b/solution.py
@@ -192,11 +192,8 @@
 
 
 def normed_rows(z, chunks, vectors):
-    order = z.order
-
     def body(*refs):
         chunks, (vectors, normed_ref, gates_ref, last, tile) = refs[: z.experts], refs[z.experts :]
-        chunks = [chunks[order.index(k)] for k in range(z.experts)]
         gain, router = vectors[0:1, :], vectors[1:2, :]
         collect_rows(z, chunks, last, tile)
         for k in range(z.experts + 1):
@@ -214,7 +211,7 @@
         [pltpu.VMEM((16, fold), f32)],
         8,
         "normed_rows",
-    )(*[chunks[k] for k in order], vectors)
+    )(*chunks, vectors)
 
 
 def grad_rows_of(z, chunks, after):
@@ -565,24 +562,26 @@
     hidden, slope = saved_terms(z, ordered, [fwd_parts[0]])
     fwd_parts = [fwd_parts[0]] + [to_core(z, fwd_parts[m], m) for m in others]
 
+    assert z.experts == 4
     def finish(ks, after):
         return finish_forward(z, ks, fwd_own, fwd_last, fwd_parts, gates, after)
 
-    half = max(3, z.experts // 2 + 1)
     double = finish([0, 1], [hidden])
     got = to_section(z, double, 0, 1)
-    grads, grad_last = grad_rows_of(z, bwd_own, [double])
+    out2 = finish([2], [hidden, double])
+    got2 = to_section(z, out2, 2, 1)
+    grads, grad_last = grad_rows_of(z, bwd_own, [out2])
     grad_all = [grads] + [to_core(z, grads, m) for m in others]
     inv, act_last = act_norms(z, bwd_own, [grads])
-    fwd_done = [to_section(z, finish([k], [inv]), k, 1) for k in range(2, half)]
+    out3 = finish([3], [inv])
+    got3 = to_section(z, out3, 3, 1)
     bwd_parts = experts_backward(z, grad_all, hidden, slope, w_gate, w_down, [inv])
     affinity = act_gates(z, bwd_own, act_last, inv, vectors, [bwd_parts[0], got])
     (relayed,) = permute_blocks(z, [lower_chunk(z, got, [affinity])], 1)
-    third = [finish([k], [affinity]) for k in range(half, z.experts)]
-    fwd_done += [to_section(z, out, k, 1) for k, out in zip(range(half, z.experts), third)]
+    fwd_done = [got2, got3]
     bwd_parts = [bwd_parts[0]] + [to_core(z, bwd_parts[m], m) for m in others]
     bwd_out = finish_backward(
-        z, z.order, bwd_own, [grad_last, act_last], [inv, affinity], bwd_parts, vectors, third
+        z, z.order, bwd_own, [grad_last, act_last], [inv, affinity], bwd_parts, vectors, []
     )
     bwd_done = {k: to_section(z, out, k, -1) for k, out in zip(z.order, bwd_out)}
 

time: 51.8 us -> 48.9 us (0.944)
  waiting for transfers between devices: 15 us -> 8.31 us
  starting transfers between devices: 20.7 us -> 24.5 us
    ppermute x7, waiting for transfers between devices: 9.66 us -> 2.63 us  [to_section(): return lax.ppermute(chunk, ('pp', 'ep'), pairs)]
    ppermute x7, starting transfers between devices: 10.4 us -> 14 us  [to_section(): return lax.ppermute(chunk, ('pp', 'ep'), pairs)]
  transfers between devices with their start and end apart: 18 -> 18, of which waited for: 9 -> 6; matrix products, arithmetic and copies ran while one was open for 0% -> 0% of each run, Pallas kernels for 23% -> 25%
where the time goes in v8:
time: 48.9 us; the launch traced here: 48.7 us
  starting transfers between devices  24.5 us (50%)
  Pallas kernels  15 us (31%)
  waiting for transfers between devices  8.31 us (17%)
  between operations  0.79 us (2%)
    pallas_call x17, Pallas kernels, run(): return kernel(*arrays)  15 us
    ppermute x7, starting transfers between devices, to_section(): return lax.ppermute(chunk, ('pp', 'ep'), pairs)  14 us
    ppermute x7, starting transfers between devices, permute_blocks(): return [lax.ppermute(array, 'ep', pairs) for array in arrays]  9.9 us
    ppermute x7, waiting for transfers between devices, permute_blocks(): return [lax.ppermute(array, 'ep', pairs) for array in arrays]  3.71 us
    ppermute x7, waiting for transfers between devices, to_section(): return lax.ppermute(chunk, ('pp', 'ep'), pairs)  2.63 us
    ppermute x4, waiting for transfers between devices, to_core(): return lax.ppermute(array, 'ep', pairs)  1.98 us
  transfers between devices with their start and end apart: 18, of which 6 were waited for; matrix products, arithmetic and copies ran while one was open for 0% of the time, Pallas kernels for 25%

profile of v8, /device:TPU:0, one launch (start us, length us, event | category | flops | bytes accessed | tf_op | source)
XLA Modules:
  0.0 48.7 jit_solution(1649201108039062932)
XLA Ops:
  0.7 2.0 %forward_chunks.1 = (bf16[16,3840]{1,0:T(8,128)(2,1)S(1)}, bf16[16,3840]{1,0:T(8,128)(2,1)S(1)}, bf16[16,3840]{1,0:T(8,128)(2,1)S(1)}, bf16[16,3840]{1,0:T(8,128)(2,1)S(1)}) custom-call(s32[2]{0:T(128)S(1)} %pad_add_fusion.where, s32[1,64]{1,0:T(1,128)} %bitcast.5, bf16[64,3584]{1,0:T(8,128)(2,1)} %refs_0_.3), custom_call_target="tpu_custom_call" | custom-call | flops 100000000 | bytes 1000 | tf_op jit(solution)/shard_map/forward_chunks/pallas_call | solution.py:38
  2.7 3.0 %collective-permute-start = (bf16[16,3840]{1,0:T(8,128)(2,1)S(1)}, bf16[16,3840]{1,0:T(8,128)(2,1)S(1)}, u32[]{:S(2)}, u32[]{:S(2)}) collective-permute-start(bf16[16,3840]{1,0:T(8,128)(2,1)S(1)} %get-tuple-element.29), channel_id=1, source_target_pairs={{0,2},{1,3},{2,0},{3,1},{4,6},{5,7},{6,4},{7,5},{8,10},{9,11},{10,... | collective-permute-start | bytes 368648 | tf_op jit(solution)/shard_map/ppermute | solution.py:510
  5.7 1.5 %collective-permute-start.1 = (bf16[16,3840]{1,0:T(8,128)(2,1)S(1)}, bf16[16,3840]{1,0:T(8,128)(2,1)S(1)}, u32[]{:S(2)}, u32[]{:S(2)}) collective-permute-start(bf16[16,3840]{1,0:T(8,128)(2,1)S(1)} %get-tuple-element.30), channel_id=1, source_target_pairs={{0,4},{1,5},{2,6},{3,7},{4,0},{5,1},{6,2},{7,3},{8,12},{9,13},{10,... | collective-permute-start | bytes 368648 | tf_op jit(solution)/shard_map/ppermute | solution.py:510
  7.3 2.8 %backward_chunks.1 = (bf16[32,3840]{1,0:T(8,128)(2,1)S(1)}, bf16[32,3840]{1,0:T(8,128)(2,1)S(1)}, bf16[32,3840]{1,0:T(8,128)(2,1)S(1)}, bf16[32,3840]{1,0:T(8,128)(2,1)S(1)}, f32[8,3584]{1,0:T(8,128)S(1)}) custom-call(s32[2]{0:T(128)S(1)} %pad_add_fusion.where, s32[1,64]{1,0:T(1,128)} %bitcast.7, bf16[64,3584]{1,0:T(8,128)(2,1)} %refs_0_.4, ...), custom_call_target="tpu_custom_call" | custom-call | flops 10000000000 | bytes 1000 | tf_op jit(solution)/shard_map/backward_chunks/pallas_call | solution.py:38
  10.1 2.0 %collective-permute-start.6 = (bf16[32,3840]{1,0:T(8,128)(2,1)S(1)}, bf16[32,3840]{1,0:T(8,128)(2,1)S(1)}, u32[]{:S(2)}, u32[]{:S(2)}) collective-permute-start(bf16[32,3840]{1,0:T(8,128)(2,1)S(1)} %get-tuple-element.40), channel_id=1, source_target_pairs={{0,2},{1,3},{2,0},{3,1},{4,6},{5,7},{6,4},{7,5},{8,10},{9,11},{10,... | collective-permute-start | bytes 737288 | tf_op jit(solution)/shard_map/ppermute | solution.py:510
  12.1 1.5 %collective-permute-start.7 = (bf16[32,3840]{1,0:T(8,128)(2,1)S(1)}, bf16[32,3840]{1,0:T(8,128)(2,1)S(1)}, u32[]{:S(2)}, u32[]{:S(2)}) collective-permute-start(bf16[32,3840]{1,0:T(8,128)(2,1)S(1)} %get-tuple-element.41), channel_id=1, source_target_pairs={{0,4},{1,5},{2,6},{3,7},{4,0},{5,1},{6,2},{7,3},{8,12},{9,13},{10,... | collective-permute-start | bytes 737288 | tf_op jit(solution)/shard_map/ppermute | solution.py:510
  13.6 0.5 %normed_rows.1 = (bf16[80,3584]{1,0:T(8,128)(2,1)S(1)}, f32[80,128]{1,0:T(8,128)S(1)}, f32[16,3584]{1,0:T(8,128)S(1)}) custom-call(bf16[16,3840]{1,0:T(8,128)(2,1)S(1)} %get-tuple-element.28.refs_4_.refs_0_, bf16[16,3840]{1,0:T(8,128)(2,1)S(1)} %collective-permute-done.refs_1_, bf16[16,3840]{1,0:T(8,128)(2,1)S(1)} %collective-permute-done.1.refs_2_.refs_0_, ...), custom_call_target="tpu_custom_call" | custom-call | flops 100000000 | bytes 1000 | tf_op jit(solution)/shard_map/normed_rows/pallas_call | solution.py:38
  14.2 1.6 %saved_rows.1.refs_4_.ordered_ref = f32[160,512]{1,0:T(8,128)S(1)} custom-call(s32[2]{0:T(128)S(1)} %pad_add_fusion.where, bf16[1,1,136,512]{3,2,1,0:T(8,128)(2,1)} %saved_any.1, bf16[1,3584,512]{2,1,0:T(8,128)(2,1)S(1)} %copy-done, bf16[1,512,3584]{2,1,0:T(8,128)(2,1)S(1)} %copy-done.1, f32[80,128]{1,0:T(8,128)S(1)} %get-tuple-element.35.refs_2_.refs_5_.refs_4_), custom_call_target="tpu_custom_call" | custom-call | flops 15000000512 | bytes 1000 | tf_op jit(solution)/shard_map/saved_rows/pallas_call | solution.py:38
  15.8 0.3 collective-permute-done.3.refs_1_
  16.2 1.5 %experts_forward.1 = (bf16[80,3584]{1,0:T(8,128)(2,1)S(1)}, bf16[80,3584]{1,0:T(8,128)(2,1)S(1)}) custom-call(bf16[80,3584]{1,0:T(8,128)(2,1)S(1)} %get-tuple-element.34.refs_0_, bf16[80,3584]{1,0:T(8,128)(2,1)S(1)} %collective-permute-done.3.refs_1_, bf16[1,3584,512]{2,1,0:T(8,128)(2,1)S(1)} %copy-done, bf16[1,512,3584]{2,1,0:T(8,128)(2,1)S(1)} %copy-done.1, ...), custom_call_target="tpu_custom_call" | custom-call | flops 100000000 | bytes 1000 | tf_op jit(solution)/shard_map/experts_forward/pallas_call | solution.py:38
  17.6 0.3 collective-permute-start.4
  18.0 1.7 %collective-permute-done.4.refs_4_.refs_3_ = bf16[80,3584]{1,0:T(8,128)(2,1)S(1)} collective-permute-done((bf16[80,3584]{1,0:T(8,128)(2,1)S(1)}, bf16[80,3584]{1,0:T(8,128)(2,1)S(1)}, u32[]{:S(2)}, u32[]{:S(2)}) %collective-permute-start.4) | collective-permute-done | bytes 573472 | tf_op jit(solution)/shard_map/ppermute | solution.py:520
  19.7 0.2 finish_forward_01.1.refs_6_
  19.9 2.1 %collective-permute-start.5 = (bf16[32,3840]{1,0:T(8,128)(2,1)S(1)}, bf16[32,3840]{1,0:T(8,128)(2,1)S(1)}, u32[]{:S(2)}, u32[]{:S(2)}) collective-permute-start(bf16[32,3840]{1,0:T(8,128)(2,1)S(1)} %finish_forward_01.1.refs_6_), channel_id=1, source_target_pairs={{0,8},{1,9},{2,10},{3,11},{4,12},{5,13},{6,14},{7,15},{8,16},{9,17... | collective-permute-start | bytes 737288 | tf_op jit(solution)/shard_map/ppermute | solution.py:531
  22.1 2.6 %collective-permute-start.11 = (bf16[16,3840]{1,0:T(8,128)(2,1)S(1)}, bf16[16,3840]{1,0:T(8,128)(2,1)S(1)}, u32[]{:S(2)}, u32[]{:S(2)}) collective-permute-start(bf16[16,3840]{1,0:T(8,128)(2,1)S(1)} %finish_forward_2.1.refs_4_), channel_id=1, source_target_pairs={{0,12},{1,13},{2,14},{3,15},{4,8},{5,9},{6,10},{7,11},{8,20},{9,21... | collective-permute-start | bytes 368648 | tf_op jit(solution)/shard_map/ppermute | solution.py:531
  24.9 0.2 act_norms.1
  25.1 0.2 finish_forward_3.1
  25.3 2.5 %collective-permute-start.12 = (bf16[16,3840]{1,0:T(8,128)(2,1)S(1)}, bf16[16,3840]{1,0:T(8,128)(2,1)S(1)}, u32[]{:S(2)}, u32[]{:S(2)}) collective-permute-start(bf16[16,3840]{1,0:T(8,128)(2,1)S(1)} %finish_forward_3.1), channel_id=1, source_target_pairs={{0,14},{1,15},{2,12},{3,13},{4,10},{5,11},{6,8},{7,9},{8,22},{9,23... | collective-permute-start | bytes 368648 | tf_op jit(solution)/shard_map/ppermute | solution.py:531
  27.8 2.6 %experts_backward.1 = (bf16[80,3712]{1,0:T(8,128)(2,1)S(1)}, bf16[80,3712]{1,0:T(8,128)(2,1)S(1)}) custom-call(bf16[80,3584]{1,0:T(8,128)(2,1)S(1)} %get-tuple-element.43.refs_4_.refs_0_, bf16[80,3584]{1,0:T(8,128)(2,1)S(1)} %collective-permute-done.9.refs_1_, bf16[160,512]{1,0:T(8,128)(2,1)S(1)} %get-tuple-element.38.refs_6_.refs_5_.refs_2_, ...), custom_call_target="tpu_custom_call" | custom-call | flops 100000000 | bytes 1000 | tf_op jit(solution)/shard_map/experts_backward/pallas_call | solution.py:38
  30.4 0.3 collective-permute-start.13
  30.7 0.4 act_gates.1.refs_0_.refs_7_
  31.2 1.8 %collective-permute-start.10 = (bf16[16,3840]{1,0:T(8,128)(2,1)S(1)}, bf16[16,3840]{1,0:T(8,128)(2,1)S(1)}, u32[]{:S(2)}, u32[]{:S(2)}) collective-permute-start(bf16[16,3840]{1,0:T(8,128)(2,1)S(1)} %lower_chunk.1), channel_id=1, source_target_pairs={{0,2},{1,3},{2,0},{3,1},{4,6},{5,7},{6,4},{7,5},{8,10},{9,11},{10,... | collective-permute-start | bytes 368648 | tf_op jit(solution)/shard_map/ppermute | solution.py:510
  33.0 0.7 %finish_backward.1 = (bf16[16,3840]{1,0:T(8,128)(2,1)S(1)}, bf16[16,3840]{1,0:T(8,128)(2,1)S(1)}, bf16[16,3840]{1,0:T(8,128)(2,1)S(1)}, bf16[16,3840]{1,0:T(8,128)(2,1)S(1)}) custom-call(bf16[32,3840]{1,0:T(8,128)(2,1)S(1)} %get-tuple-element.39.refs_0_, bf16[32,3840]{1,0:T(8,128)(2,1)S(1)} %collective-permute-done.6.refs_1_, ...), custom_call_target="tpu_custom_call" | custom-call | flops 100000000 | bytes 1000 | tf_op jit(solution)/shard_map/finish_backward/pallas_call | solution.py:38
  33.7 2.9 %collective-permute-start.14 = (bf16[16,3840]{1,0:T(8,128)(2,1)S(1)}, bf16[16,3840]{1,0:T(8,128)(2,1)S(1)}, u32[]{:S(2)}, u32[]{:S(2)}) collective-permute-start(bf16[16,3840]{1,0:T(8,128)(2,1)S(1)} %get-tuple-element.50), channel_id=1, source_target_pairs={{0,30},{1,31},{2,28},{3,29},{4,26},{5,27},{6,24},{7,25},{8,6},{9,7... | collective-permute-start | bytes 368648 | tf_op jit(solution)/shard_map/ppermute | solution.py:531
  36.6 1.5 %collective-permute-start.15 = (bf16[16,3840]{1,0:T(8,128)(2,1)S(1)}, bf16[16,3840]{1,0:T(8,128)(2,1)S(1)}, u32[]{:S(2)}, u32[]{:S(2)}) collective-permute-start(bf16[16,3840]{1,0:T(8,128)(2,1)S(1)} %get-tuple-element.51), channel_id=1, source_target_pairs={{0,26},{1,27},{2,24},{3,25},{4,30},{5,31},{6,28},{7,29},{8,2},{9,3... | collective-permute-start | bytes 368648 | tf_op jit(solution)/shard_map/ppermute | solution.py:531
  38.0 0.9 %collective-permute-start.16 = (bf16[16,3840]{1,0:T(8,128)(2,1)S(1)}, bf16[16,3840]{1,0:T(8,128)(2,1)S(1)}, u32[]{:S(2)}, u32[]{:S(2)}) collective-permute-start(bf16[16,3840]{1,0:T(8,128)(2,1)S(1)} %get-tuple-element.52), channel_id=1, source_target_pairs={{0,28},{1,29},{2,30},{3,31},{4,24},{5,25},{6,26},{7,27},{8,4},{9,5... | collective-permute-start | bytes 368648 | tf_op jit(solution)/shard_map/ppermute | solution.py:531
  38.9 1.5 %collective-permute-start.17 = (bf16[16,3840]{1,0:T(8,128)(2,1)S(1)}, bf16[16,3840]{1,0:T(8,128)(2,1)S(1)}, u32[]{:S(2)}, u32[]{:S(2)}) collective-permute-start(bf16[16,3840]{1,0:T(8,128)(2,1)S(1)} %get-tuple-element.53), channel_id=1, source_target_pairs={{0,24},{1,25},{2,26},{3,27},{4,28},{5,29},{6,30},{7,31},{8,0},{9,1... | collective-permute-start | bytes 368648 | tf_op jit(solution)/shard_map/ppermute | solution.py:531
  40.5 3.7 %collective-permute-done.10.refs_1_ = bf16[16,3840]{1,0:T(8,128)(2,1)S(1)} collective-permute-done((bf16[16,3840]{1,0:T(8,128)(2,1)S(1)}, bf16[16,3840]{1,0:T(8,128)(2,1)S(1)}, u32[]{:S(2)}, u32[]{:S(2)}) %collective-permute-start.10) | collective-permute-done | bytes 122912 | tf_op jit(solution)/shard_map/ppermute | solution.py:510
  44.2 1.0 %forward_rows.1 = bf16[64,3584]{1,0:T(8,128)(2,1)} custom-call(bf16[32,3840]{1,0:T(8,128)(2,1)S(1)} %collective-permute-done.5.refs_8_.double.refs_0_, bf16[16,3840]{1,0:T(8,128)(2,1)S(1)} %collective-permute-done.10.refs_1_, bf16[16,3840]{1,0:T(8,128)(2,1)S(1)} %collective-permute-done.11.refs_2_, bf16[16,3840]{1,0:T(8,128)(2,1)S(1)} %collective-permute-done.12.refs_3_), custom_call_target="tpu_custom_call" | custom-call | flops 100000000 | bytes 1000 | tf_op jit(solution)/shard_map/forward_rows/pallas_call | solution.py:38
  45.2 1.0 %collective-permute-done.16.refs_2_ = bf16[16,3840]{1,0:T(8,128)(2,1)S(1)} collective-permute-done((bf16[16,3840]{1,0:T(8,128)(2,1)S(1)}, bf16[16,3840]{1,0:T(8,128)(2,1)S(1)}, u32[]{:S(2)}, u32[]{:S(2)}) %collective-permute-start.16) | collective-permute-done | bytes 122912 | tf_op jit(solution)/shard_map/ppermute | solution.py:531
  46.2 1.6 %collective-permute-done.17.refs_3_ = bf16[16,3840]{1,0:T(8,128)(2,1)S(1)} collective-permute-done((bf16[16,3840]{1,0:T(8,128)(2,1)S(1)}, bf16[16,3840]{1,0:T(8,128)(2,1)S(1)}, u32[]{:S(2)}, u32[]{:S(2)}) %collective-permute-start.17) | collective-permute-done | bytes 122912 | tf_op jit(solution)/shard_map/ppermute | solution.py:531
  47.7 1.0 %backward_rows.1 = bf16[64,3584]{1,0:T(8,128)(2,1)} custom-call(bf16[16,3840]{1,0:T(8,128)(2,1)S(1)} %collective-permute-done.14.refs_0_, bf16[16,3840]{1,0:T(8,128)(2,1)S(1)} %collective-permute-done.15.refs_1_, bf16[16,3840]{1,0:T(8,128)(2,1)S(1)} %collective-permute-done.16.refs_2_, bf16[16,3840]{1,0:T(8,128)(2,1)S(1)} %collective-permute-done.17.refs_3_), custom_call_target="tpu_custom_call" | custom-call | flops 100000000 | bytes 1000 | tf_op jit(solution)/shard_map/backward_rows/pallas_call | solution.py:38
  (26 shorter events, 0.7 us)
Async XLA Ops:
  2.7 10.9 %collective-permute-start = (bf16[16,3840]{1,0:T(8,128)(2,1)S(1)}, bf16[16,3840]{1,0:T(8,128)(2,1)S(1)}, u32[]{:S(2)}, u32[]{:S(2)}) collective-permute-start(bf16[16,3840]{1,0:T(8,128)(2,1)S(1)} %get-tuple-element.29), channel_id=1, source_target_pairs={{0,2},{1,3},{2,0},{3,1},{4,6},{5,7},{6,4},{7,5},{8,10},{9,11},{10,... | collective-permute-start | bytes 368648 | tf_op jit(solution)/shard_map/ppermute | solution.py:510
  5.7 7.9 %collective-permute-start.1 = (bf16[16,3840]{1,0:T(8,128)(2,1)S(1)}, bf16[16,3840]{1,0:T(8,128)(2,1)S(1)}, u32[]{:S(2)}, u32[]{:S(2)}) collective-permute-start(bf16[16,3840]{1,0:T(8,128)(2,1)S(1)} %get-tuple-element.30), channel_id=1, source_target_pairs={{0,4},{1,5},{2,6},{3,7},{4,0},{5,1},{6,2},{7,3},{8,12},{9,13},{10,... | collective-permute-start | bytes 368648 | tf_op jit(solution)/shard_map/ppermute | solution.py:510
  7.2 6.4 %collective-permute-start.2 = (bf16[16,3840]{1,0:T(8,128)(2,1)S(1)}, bf16[16,3840]{1,0:T(8,128)(2,1)S(1)}, u32[]{:S(2)}, u32[]{:S(2)}) collective-permute-start(bf16[16,3840]{1,0:T(8,128)(2,1)S(1)} %get-tuple-element.31), channel_id=1, source_target_pairs={{0,6},{1,7},{2,4},{3,5},{4,2},{5,3},{6,0},{7,1},{8,14},{9,15},{10,... | collective-permute-start | bytes 368648 | tf_op jit(solution)/shard_map/ppermute | solution.py:510
  7.3 6.9 %copy-start = (bf16[1,3584,512]{2,1,0:T(8,128)(2,1)S(1)}, bf16[1,3584,512]{2,1,0:T(8,128)(2,1)}, u32[]{:S(2)}) copy-start(bf16[1,3584,512]{2,1,0:T(8,128)(2,1)} %refs_4_.1) | copy-start | bytes 11010052
  7.3 6.9 %copy-start.1 = (bf16[1,512,3584]{2,1,0:T(8,128)(2,1)S(1)}, bf16[1,512,3584]{2,1,0:T(8,128)(2,1)}, u32[]{:S(2)}) copy-start(bf16[1,512,3584]{2,1,0:T(8,128)(2,1)} %refs_5_.1) | copy-start | bytes 11010052
  10.1 14.6 %collective-permute-start.6 = (bf16[32,3840]{1,0:T(8,128)(2,1)S(1)}, bf16[32,3840]{1,0:T(8,128)(2,1)S(1)}, u32[]{:S(2)}, u32[]{:S(2)}) collective-permute-start(bf16[32,3840]{1,0:T(8,128)(2,1)S(1)} %get-tuple-element.40), channel_id=1, source_target_pairs={{0,2},{1,3},{2,0},{3,1},{4,6},{5,7},{6,4},{7,5},{8,10},{9,11},{10,... | collective-permute-start | bytes 737288 | tf_op jit(solution)/shard_map/ppermute | solution.py:510
  12.1 12.6 %collective-permute-start.7 = (bf16[32,3840]{1,0:T(8,128)(2,1)S(1)}, bf16[32,3840]{1,0:T(8,128)(2,1)S(1)}, u32[]{:S(2)}, u32[]{:S(2)}) collective-permute-start(bf16[32,3840]{1,0:T(8,128)(2,1)S(1)} %get-tuple-element.41), channel_id=1, source_target_pairs={{0,4},{1,5},{2,6},{3,7},{4,0},{5,1},{6,2},{7,3},{8,12},{9,13},{10,... | collective-permute-start | bytes 737288 | tf_op jit(solution)/shard_map/ppermute | solution.py:510
  13.6 11.1 %collective-permute-start.8 = (bf16[32,3840]{1,0:T(8,128)(2,1)S(1)}, bf16[32,3840]{1,0:T(8,128)(2,1)S(1)}, u32[]{:S(2)}, u32[]{:S(2)}) collective-permute-start(bf16[32,3840]{1,0:T(8,128)(2,1)S(1)} %get-tuple-element.42), channel_id=1, source_target_pairs={{0,6},{1,7},{2,4},{3,5},{4,2},{5,3},{6,0},{7,1},{8,14},{9,15},{10,... | collective-permute-start | bytes 737288 | tf_op jit(solution)/shard_map/ppermute | solution.py:510
  14.1 2.0 %collective-permute-start.3 = (bf16[80,3584]{1,0:T(8,128)(2,1)S(1)}, bf16[80,3584]{1,0:T(8,128)(2,1)S(1)}, u32[]{:S(2)}, u32[]{:S(2)}) collective-permute-start(bf16[80,3584]{1,0:T(8,128)(2,1)S(1)} %get-tuple-element.34.refs_0_), channel_id=1, source_target_pairs={{0,1},{1,0},{2,3},{3,2},{4,5},{5,4},{6,7},{7,6},{8,9},{9,8},{10,11... | collective-permute-start | bytes 1720328 | tf_op jit(solution)/shard_map/ppermute | solution.py:520
  17.6 2.0 %collective-permute-start.4 = (bf16[80,3584]{1,0:T(8,128)(2,1)S(1)}, bf16[80,3584]{1,0:T(8,128)(2,1)S(1)}, u32[]{:S(2)}, u32[]{:S(2)}) collective-permute-start(bf16[80,3584]{1,0:T(8,128)(2,1)S(1)} %get-tuple-element.37), channel_id=1, source_target_pairs={{0,1},{1,0},{2,3},{3,2},{4,5},{5,4},{6,7},{7,6},{8,9},{9,8},{10,11... | collective-permute-start | bytes 1720328 | tf_op jit(solution)/shard_map/ppermute | solution.py:520
  19.9 10.8 %collective-permute-start.5 = (bf16[32,3840]{1,0:T(8,128)(2,1)S(1)}, bf16[32,3840]{1,0:T(8,128)(2,1)S(1)}, u32[]{:S(2)}, u32[]{:S(2)}) collective-permute-start(bf16[32,3840]{1,0:T(8,128)(2,1)S(1)} %finish_forward_01.1.refs_6_), channel_id=1, source_target_pairs={{0,8},{1,9},{2,10},{3,11},{4,12},{5,13},{6,14},{7,15},{8,16},{9,17... | collective-permute-start | bytes 737288 | tf_op jit(solution)/shard_map/ppermute | solution.py:531
  22.1 15.9 %collective-permute-start.11 = (bf16[16,3840]{1,0:T(8,128)(2,1)S(1)}, bf16[16,3840]{1,0:T(8,128)(2,1)S(1)}, u32[]{:S(2)}, u32[]{:S(2)}) collective-permute-start(bf16[16,3840]{1,0:T(8,128)(2,1)S(1)} %finish_forward_2.1.refs_4_), channel_id=1, source_target_pairs={{0,12},{1,13},{2,14},{3,15},{4,8},{5,9},{6,10},{7,11},{8,20},{9,21... | collective-permute-start | bytes 368648 | tf_op jit(solution)/shard_map/ppermute | solution.py:531
  24.8 3.0 %collective-permute-start.9 = (bf16[80,3584]{1,0:T(8,128)(2,1)S(1)}, bf16[80,3584]{1,0:T(8,128)(2,1)S(1)}, u32[]{:S(2)}, u32[]{:S(2)}) collective-permute-start(bf16[80,3584]{1,0:T(8,128)(2,1)S(1)} %get-tuple-element.43.refs_4_.refs_0_), channel_id=1, source_target_pairs={{0,1},{1,0},{2,3},{3,2},{4,5},{5,4},{6,7},{7,6},{8,9},{9,8},{10,11... | collective-permute-start | bytes 1720328 | tf_op jit(solution)/shard_map/ppermute | solution.py:520
  25.3 13.6 %collective-permute-start.12 = (bf16[16,3840]{1,0:T(8,128)(2,1)S(1)}, bf16[16,3840]{1,0:T(8,128)(2,1)S(1)}, u32[]{:S(2)}, u32[]{:S(2)}) collective-permute-start(bf16[16,3840]{1,0:T(8,128)(2,1)S(1)} %finish_forward_3.1), channel_id=1, source_target_pairs={{0,14},{1,15},{2,12},{3,13},{4,10},{5,11},{6,8},{7,9},{8,22},{9,23... | collective-permute-start | bytes 368648 | tf_op jit(solution)/shard_map/ppermute | solution.py:531
  30.4 2.6 %collective-permute-start.13 = (bf16[80,3712]{1,0:T(8,128)(2,1)S(1)}, bf16[80,3712]{1,0:T(8,128)(2,1)S(1)}, u32[]{:S(2)}, u32[]{:S(2)}) collective-permute-start(bf16[80,3712]{1,0:T(8,128)(2,1)S(1)} %get-tuple-element.49), channel_id=1, source_target_pairs={{0,1},{1,0},{2,3},{3,2},{4,5},{5,4},{6,7},{7,6},{8,9},{9,8},{10,11... | collective-permute-start | bytes 1781768 | tf_op jit(solution)/shard_map/ppermute | solution.py:520
  31.2 13.0 %collective-permute-start.10 = (bf16[16,3840]{1,0:T(8,128)(2,1)S(1)}, bf16[16,3840]{1,0:T(8,128)(2,1)S(1)}, u32[]{:S(2)}, u32[]{:S(2)}) collective-permute-start(bf16[16,3840]{1,0:T(8,128)(2,1)S(1)} %lower_chunk.1), channel_id=1, source_target_pairs={{0,2},{1,3},{2,0},{3,1},{4,6},{5,7},{6,4},{7,5},{8,10},{9,11},{10,... | collective-permute-start | bytes 368648 | tf_op jit(solution)/shard_map/ppermute | solution.py:510
  33.7 11.5 %collective-permute-start.14 = (bf16[16,3840]{1,0:T(8,128)(2,1)S(1)}, bf16[16,3840]{1,0:T(8,128)(2,1)S(1)}, u32[]{:S(2)}, u32[]{:S(2)}) collective-permute-start(bf16[16,3840]{1,0:T(8,128)(2,1)S(1)} %get-tuple-element.50), channel_id=1, source_target_pairs={{0,30},{1,31},{2,28},{3,29},{4,26},{5,27},{6,24},{7,25},{8,6},{9,7... | collective-permute-start | bytes 368648 | tf_op jit(solution)/shard_map/ppermute | solution.py:531
  36.6 8.6 %collective-permute-start.15 = (bf16[16,3840]{1,0:T(8,128)(2,1)S(1)}, bf16[16,3840]{1,0:T(8,128)(2,1)S(1)}, u32[]{:S(2)}, u32[]{:S(2)}) collective-permute-start(bf16[16,3840]{1,0:T(8,128)(2,1)S(1)} %get-tuple-element.51), channel_id=1, source_target_pairs={{0,26},{1,27},{2,24},{3,25},{4,30},{5,31},{6,28},{7,29},{8,2},{9,3... | collective-permute-start | bytes 368648 | tf_op jit(solution)/shard_map/ppermute | solution.py:531
  38.0 8.1 %collective-permute-start.16 = (bf16[16,3840]{1,0:T(8,128)(2,1)S(1)}, bf16[16,3840]{1,0:T(8,128)(2,1)S(1)}, u32[]{:S(2)}, u32[]{:S(2)}) collective-permute-start(bf16[16,3840]{1,0:T(8,128)(2,1)S(1)} %get-tuple-element.52), channel_id=1, source_target_pairs={{0,28},{1,29},{2,30},{3,31},{4,24},{5,25},{6,26},{7,27},{8,4},{9,5... | collective-permute-start | bytes 368648 | tf_op jit(solution)/shard_map/ppermute | solution.py:531
  38.9 8.8 %collective-permute-start.17 = (bf16[16,3840]{1,0:T(8,128)(2,1)S(1)}, bf16[16,3840]{1,0:T(8,128)(2,1)S(1)}, u32[]{:S(2)}, u32[]{:S(2)}) collective-permute-start(bf16[16,3840]{1,0:T(8,128)(2,1)S(1)} %get-tuple-element.53), channel_id=1, source_target_pairs={{0,24},{1,25},{2,26},{3,27},{4,28},{5,29},{6,30},{7,31},{8,0},{9,1... | collective-permute-start | bytes 368648 | tf_op jit(solution)/shard_map/ppermute | solution.py:531

commit v9 on v8

--- a/solution.py
+++ b/solution.py
@@ -111,7 +111,8 @@
     step = z.width // 2
     tiles[...] = jnp.zeros_like(tiles)
     for half in range(2):
-        ready[half].wait()
+        if ready:
+            ready[half].wait()
         col = half * step
         got = jnp.dot(selector, rows_ref[:, col : col + step], preferred_element_type=f32)
         packed = got[: z.tokens].astype(bf16)
@@ -123,61 +124,83 @@
         chunks[k][base : base + 16, z.width :] = tiles[k].astype(bf16)
 
 
-def make_chunks(z, where, ids, sources, tables, after, name):
+def forward_chunks(z, where, ids, act, later_ids, later):
+    count = len(later)
+
+    def body(where, ids_any, later_ids_any, act_any, *refs):
+        later_any, chunks = refs[:count], refs[count : count + z.experts]
+        later_refs = refs[count + z.experts : 2 * count + z.experts]
+        selector_ref, token_ref, ids, rows, tiles, sems = refs[2 * count + z.experts :]
+        step = z.width // 2
+        first = [
+            pltpu.make_async_copy(source, ids.at[i : i + 1], sems.at[i])
+            for i, source in enumerate((ids_any, later_ids_any))
+        ]
+        ready = [
+            pltpu.make_async_copy(
+                act_any.at[:, pl.ds(i * step, step)], rows.at[:, pl.ds(i * step, step)], sems.at[2 + i]
+            )
+            for i in range(2)
+        ]
+        rest = [
+            pltpu.make_async_copy(source, target, sems.at[4 + i])
+            for i, (source, target) in enumerate(zip(later_any, later_refs))
+        ]
+        for copy in first + ready + rest:
+            copy.start()
+        for copy in first:
+            copy.wait()
+        selector, token_row = slot_matrices(ids[0:1, :], where[0], z)
+        later_selector, later_row = slot_matrices(ids[1:2, :], where[0], z)
+        selector_ref[...] = later_selector
+        token_ref[...] = jnp.broadcast_to(later_row, token_ref.shape)
+        write_chunks(z, selector, token_row, rows, ready, tiles, chunks, 0)
+        for copy in rest:
+            copy.wait()
+
+    outs = call(
+        body,
+        "shhh" + "h" * count,
+        [shape((z.main, z.wide))] * z.experts
+        + [shape(array.shape, array.dtype) for array in later]
+        + [shape((z.rows, z.tokens)), shape((8, fold), f32)],
+        [
+            pltpu.VMEM((2, z.tokens), jnp.int32),
+            pltpu.VMEM((z.tokens, z.width), bf16),
+            pltpu.VMEM((z.experts, 16, fold), f32),
+            pltpu.SemaphoreType.DMA((4 + count,)),
+        ],
+        8,
+        "forward_chunks",
+    )(where, ids.reshape(1, z.tokens), later_ids.reshape(1, z.tokens), act, *later)
+    return outs[: z.experts], outs[z.experts : z.experts + count], outs[z.experts + count :]
+
+
+def backward_chunks(z, where, slots, sources, gain, router):
     count = len(sources)
 
-    def body(where, ids_any, *refs):
-        anys, tables_any = refs[:count], refs[count : count + len(tables)]
-        outs, held = refs[count + len(tables) + len(after) :], ()
-        if tables:
-            *outs, gain_ref, router_ref, ids, rows, tiles, sems = outs
-            *outs, vectors = outs
-            held = (gain_ref, router_ref)
-        else:
-            *outs, ids, rows, tiles, sems = outs
-        copies = [pltpu.make_async_copy(ids_any, ids, sems.at[2 * count])]
-        step = z.width // 2
+    def body(where, selector, token_ref, *refs):
+        sources, (gain_ref, router_ref) = refs[:count], refs[count : count + 2]
+        *chunks, vectors, tiles = refs[count + 2 :]
         for j in range(count):
-            for half in range(2):
-                cols = pl.ds(half * step, step)
-                copies.append(
-                    pltpu.make_async_copy(
-                        anys[j].at[:, cols], rows.at[j, :, cols], sems.at[2 * j + half]
-                    )
-                )
-        for i, (source, target) in enumerate(zip(tables_any, held)):
-            copies.append(pltpu.make_async_copy(source, target, sems.at[2 * count + 1 + i]))
-        for copy in copies:
-            copy.start()
-        copies[0].wait()
-        selector, token_row = slot_matrices(ids[...], where[0], z)
-        for j in range(count):
-            ready = copies[1 + 2 * j : 3 + 2 * j]
-            write_chunks(z, selector, token_row, rows.at[j], ready, tiles, outs, 16 * j)
-        if tables:
-            for copy in copies[1 + 2 * count :]:
-                copy.wait()
-            vectors[...] = jnp.zeros_like(vectors)
-            vectors[0:1, :] = gain_ref[...].astype(f32)
-            mine = lax.broadcasted_iota(jnp.int32, (z.experts, 1), 0) == where[0]
-            table = jnp.where(mine, router_ref[0].astype(f32), 0.0)
-            vectors[1:2, :] = jnp.sum(table, axis=0, keepdims=True)
-
-    return call(
-        body,
-        "sh" + "h" * (count + len(tables)) + "a" * len(after),
-        [shape((z.main * count, z.wide))] * z.experts
-        + [shape((8, z.width), f32) for _ in tables[:1]],
-        [pltpu.VMEM(table.shape, bf16) for table in tables]
-        + [
-            pltpu.VMEM((1, z.tokens), jnp.int32),
-            pltpu.VMEM((count, z.tokens, z.width), bf16),
-            pltpu.VMEM((z.experts, 16, fold), f32),
-            pltpu.SemaphoreType.DMA((2 * count + 1 + len(tables),)),
-        ],
-        8,
-        name,
-    )(where, ids.reshape(1, z.tokens), *sources, *tables, *after)
+            write_chunks(
+                z, selector[...], token_ref[0:1, :], sources[j], None, tiles, chunks, 16 * j
+            )
+        vectors[...] = jnp.zeros_like(vectors)
+        vectors[0:1, :] = gain_ref[...].astype(f32)
+        mine = lax.broadcasted_iota(jnp.int32, (z.experts, 1), 0) == where[0]
+        table = jnp.where(mine, router_ref[0].astype(f32), 0.0)
+        vectors[1:2, :] = jnp.sum(table, axis=0, keepdims=True)
+
+    *chunks, vectors = call(
+        body,
+        "svv" + "v" * (count + 2),
+        [shape((z.main * count, z.wide))] * z.experts + [shape((8, z.width), f32)],
+        [pltpu.VMEM((z.experts, 16, fold), f32)],
+        8,
+        "backward_chunks",
+    )(where, *slots, *sources, gain, router)
+    return chunks, vectors
 
 
 def collect_rows(z, chunks, last, tile, base=0):
@@ -542,17 +565,11 @@
     router = jnp.swapaxes(router, 1, 2)
     others = range(1, z.split)
 
-    fwd_chunks = make_chunks(z, where, fwd_ids, [fwd_act], [], [], "forward_chunks")
+    fwd_chunks, (grad, act, gain_row, table), slots = forward_chunks(
+        z, where, fwd_ids, fwd_act, bwd_ids, [bwd_grad, bwd_act, norm_gain, router]
+    )
     fwd_own = dispatch(z, fwd_chunks)
-    *bwd_chunks, vectors = make_chunks(
-        z,
-        where,
-        bwd_ids,
-        [bwd_grad, bwd_act],
-        [norm_gain, router],
-        [fwd_chunks[0]],
-        "backward_chunks",
-    )
+    bwd_chunks, vectors = backward_chunks(z, where, slots, [grad, act], gain_row, table)
     bwd_own = dispatch(z, bwd_chunks)
 
     normed, gates, fwd_last = normed_rows(z, fwd_own, vectors)
@@ -563,6 +580,7 @@
     fwd_parts = [fwd_parts[0]] + [to_core(z, fwd_parts[m], m) for m in others]
 
     assert z.experts == 4
+
     def finish(ks, after):
         return finish_forward(z, ks, fwd_own, fwd_last, fwd_parts, gates, after)
 

time: 48.9 us -> 48.4 us (0.990)
  Pallas kernels: 15 us -> 13.3 us
  waiting for transfers between devices: 8.31 us -> 9.94 us
    pallas_call x17, Pallas kernels: 15 us -> 13.3 us  [run(): return kernel(*arrays)]
    ppermute x7, waiting for transfers between devices: 3.71 us -> 5.23 us  [permute_blocks(): return [lax.ppermute(array, 'ep', pairs) for array in arrays]]
    ppermute x7, starting transfers between devices: 14 us -> 13.1 us  [to_section(): return lax.ppermute(chunk, ('pp', 'ep'), pairs)]
  transfers between devices with their start and end apart: 18 -> 18, of which waited for: 6 -> 7; matrix products, arithmetic and copies ran while one was open for 0% -> 0% of each run, Pallas kernels for 25% -> 21%
where the time goes in v9:
time: 48.4 us; the launch traced here: 48.2 us
  starting transfers between devices  24.1 us (50%)
  Pallas kernels  13.3 us (27%)
  waiting for transfers between devices  9.94 us (21%)
  between operations  0.78 us (2%)
    pallas_call x17, Pallas kernels, run(): return kernel(*arrays)  13.3 us
    ppermute x7, starting transfers between devices, to_section(): return lax.ppermute(chunk, ('pp', 'ep'), pairs)  13.1 us
    ppermute x7, starting transfers between devices, permute_blocks(): return [lax.ppermute(array, 'ep', pairs) for array in arrays]  10.4 us
    ppermute x7, waiting for transfers between devices, permute_blocks(): return [lax.ppermute(array, 'ep', pairs) for array in arrays]  5.23 us
    ppermute x7, waiting for transfers between devices, to_section(): return lax.ppermute(chunk, ('pp', 'ep'), pairs)  2.73 us
    ppermute x4, waiting for transfers between devices, to_core(): return lax.ppermute(array, 'ep', pairs)  1.97 us
  transfers between devices with their start and end apart: 18, of which 7 were waited for; matrix products, arithmetic and copies ran while one was open for 0% of the time, Pallas kernels for 21%

profile of v9, /device:TPU:0, one launch (start us, length us, event | category | flops | bytes accessed | tf_op | source)
XLA Modules:
  0.0 48.2 jit_solution(8738690086977633836)
XLA Ops:
  0.7 2.0 %forward_chunks.1 = (bf16[16,3840]{1,0:T(8,128)(2,1)S(1)}, bf16[16,3840]{1,0:T(8,128)(2,1)S(1)}, bf16[16,3840]{1,0:T(8,128)(2,1)S(1)}, bf16[16,3840]{1,0:T(8,128...) custom-call(s32[2]{0:T(128)S(1)} %pad_add_fusion.where, ...), custom_call_target="tpu_custom_call" | custom-call | flops 100000000 | bytes 1000 | tf_op jit(solution)/shard_map/forward_chunks/pallas_call | solution.py:38
  2.8 3.0 %collective-permute-start = (bf16[16,3840]{1,0:T(8,128)(2,1)S(1)}, bf16[16,3840]{1,0:T(8,128)(2,1)S(1)}, u32[]{:S(2)}, u32[]{:S(2)}) collective-permute-start(bf16[16,3840]{1,0:T(8,128)(2,1)S(1)} %get-tuple-element.35), channel_id=1, source_target_pairs={{0,2},{1,3},{2,0},{3,1},{4,6},{5,7},{6,4},{7,5},{8,10},{9,11},{10,... | collective-permute-start | bytes 368648 | tf_op jit(solution)/shard_map/ppermute | solution.py:533
  5.8 1.5 %collective-permute-start.1 = (bf16[16,3840]{1,0:T(8,128)(2,1)S(1)}, bf16[16,3840]{1,0:T(8,128)(2,1)S(1)}, u32[]{:S(2)}, u32[]{:S(2)}) collective-permute-start(bf16[16,3840]{1,0:T(8,128)(2,1)S(1)} %get-tuple-element.36), channel_id=1, source_target_pairs={{0,4},{1,5},{2,6},{3,7},{4,0},{5,1},{6,2},{7,3},{8,12},{9,13},{10,... | collective-permute-start | bytes 368648 | tf_op jit(solution)/shard_map/ppermute | solution.py:533
  7.3 1.0 %backward_chunks.1 = (bf16[32,3840]{1,0:T(8,128)(2,1)S(1)}, bf16[32,3840]{1,0:T(8,128)(2,1)S(1)}, bf16[32,3840]{1,0:T(8,128)(2,1)S(1)}, bf16[32,3840]{1,0:T(8,128)(2,1)S(1)}, f32[8,3584]{1,0:T(8,128)S(1)}) custom-call(s32[2]{0:T(128)S(1)} %pad_add_fusion.where, bf16[80,64]{1,0:T(8,128)(2,1)S(1)} %get-tuple-element.38.selector, ...), custom_call_target="tpu_custom_call" | custom-call | flops 10000000000 | bytes 1000 | tf_op jit(solution)/shard_map/backward_chunks/pallas_call | solution.py:38
  8.3 2.0 %collective-permute-start.6 = (bf16[32,3840]{1,0:T(8,128)(2,1)S(1)}, bf16[32,3840]{1,0:T(8,128)(2,1)S(1)}, u32[]{:S(2)}, u32[]{:S(2)}) collective-permute-start(bf16[32,3840]{1,0:T(8,128)(2,1)S(1)} %get-tuple-element.52), channel_id=1, source_target_pairs={{0,2},{1,3},{2,0},{3,1},{4,6},{5,7},{6,4},{7,5},{8,10},{9,11},{10,... | collective-permute-start | bytes 737288 | tf_op jit(solution)/shard_map/ppermute | solution.py:533
  10.3 1.5 %collective-permute-start.7 = (bf16[32,3840]{1,0:T(8,128)(2,1)S(1)}, bf16[32,3840]{1,0:T(8,128)(2,1)S(1)}, u32[]{:S(2)}, u32[]{:S(2)}) collective-permute-start(bf16[32,3840]{1,0:T(8,128)(2,1)S(1)} %get-tuple-element.53), channel_id=1, source_target_pairs={{0,4},{1,5},{2,6},{3,7},{4,0},{5,1},{6,2},{7,3},{8,12},{9,13},{10,... | collective-permute-start | bytes 737288 | tf_op jit(solution)/shard_map/ppermute | solution.py:533
  11.9 1.1 %collective-permute-start.8 = (bf16[32,3840]{1,0:T(8,128)(2,1)S(1)}, bf16[32,3840]{1,0:T(8,128)(2,1)S(1)}, u32[]{:S(2)}, u32[]{:S(2)}) collective-permute-start(bf16[32,3840]{1,0:T(8,128)(2,1)S(1)} %get-tuple-element.54), channel_id=1, source_target_pairs={{0,6},{1,7},{2,4},{3,5},{4,2},{5,3},{6,0},{7,1},{8,14},{9,15},{10,... | collective-permute-start | bytes 737288 | tf_op jit(solution)/shard_map/ppermute | solution.py:533
  13.0 1.5 %collective-permute-done.2.refs_3_.refs_0_ = bf16[16,3840]{1,0:T(8,128)(2,1)S(1)} collective-permute-done((bf16[16,3840]{1,0:T(8,128)(2,1)S(1)}, bf16[16,3840]{1,0:T(8,128)(2,1)S(1)}, u32[]{:S(2)}, u32[]{:S(2)}) %collective-permute-start.2) | collective-permute-done | bytes 122912 | tf_op jit(solution)/shard_map/ppermute | solution.py:533
  14.5 0.5 %normed_rows.1 = (bf16[80,3584]{1,0:T(8,128)(2,1)S(1)}, f32[80,128]{1,0:T(8,128)S(1)}, f32[16,3584]{1,0:T(8,128)S(1)}) custom-call(bf16[16,3840]{1,0:T(8,128)(2,1)S(1)} %get-tuple-element.34.refs_0_, bf16[16,3840]{1,0:T(8,128)(2,1)S(1)} %collective-permute-done.refs_1_, bf16[16,3840]{1,0:T(8,128)(2,1)S(1)} %collective-permute-done.1.refs_2_.refs_0_, ...), custom_call_target="tpu_custom_call" | custom-call | flops 100000000 | bytes 1000 | tf_op jit(solution)/shard_map/normed_rows/pallas_call | solution.py:38
  15.0 1.6 %saved_rows.1.refs_4_.ordered_ref = f32[160,512]{1,0:T(8,128)S(1)} custom-call(s32[2]{0:T(128)S(1)} %pad_add_fusion.where, bf16[1,1,136,512]{3,2,1,0:T(8,128)(2,1)} %saved_any.1, bf16[1,3584,512]{2,1,0:T(8,128)(2,1)S(1)} %copy-done, bf16[1,512,3584]{2,1,0:T(8,128)(2,1)S(1)} %copy-done.1, f32[80,128]{1,0:T(8,128)S(1)} %get-tuple-element.47.refs_2_.refs_5_.refs_4_), custom_call_target="tpu_custom_call" | custom-call | flops 15000000512 | bytes 1000 | tf_op jit(solution)/shard_map/saved_rows/pallas_call | solution.py:38
  16.7 0.3 collective-permute-done.3.refs_1_
  17.0 1.5 %experts_forward.1 = (bf16[80,3584]{1,0:T(8,128)(2,1)S(1)}, bf16[80,3584]{1,0:T(8,128)(2,1)S(1)}) custom-call(bf16[80,3584]{1,0:T(8,128)(2,1)S(1)} %get-tuple-element.46.refs_0_, bf16[80,3584]{1,0:T(8,128)(2,1)S(1)} %collective-permute-done.3.refs_1_, bf16[1,3584,512]{2,1,0:T(8,128)(2,1)S(1)} %copy-done, bf16[1,512,3584]{2,1,0:T(8,128)(2,1)S(1)} %copy-done.1, ...), custom_call_target="tpu_custom_call" | custom-call | flops 100000000 | bytes 1000 | tf_op jit(solution)/shard_map/experts_forward/pallas_call | solution.py:38
  18.5 0.3 collective-permute-start.4
  18.8 1.7 %collective-permute-done.4.refs_4_.refs_3_ = bf16[80,3584]{1,0:T(8,128)(2,1)S(1)} collective-permute-done((bf16[80,3584]{1,0:T(8,128)(2,1)S(1)}, bf16[80,3584]{1,0:T(8,128)(2,1)S(1)}, u32[]{:S(2)}, u32[]{:S(2)}) %collective-permute-start.4) | collective-permute-done | bytes 573472 | tf_op jit(solution)/shard_map/ppermute | solution.py:543
  20.7 1.6 %collective-permute-start.5 = (bf16[32,3840]{1,0:T(8,128)(2,1)S(1)}, bf16[32,3840]{1,0:T(8,128)(2,1)S(1)}, u32[]{:S(2)}, u32[]{:S(2)}) collective-permute-start(bf16[32,3840]{1,0:T(8,128)(2,1)S(1)} %finish_forward_01.1.refs_6_), channel_id=1, source_target_pairs={{0,8},{1,9},{2,10},{3,11},{4,12},{5,13},{6,14},{7,15},{8,16},{9,17... | collective-permute-start | bytes 737288 | tf_op jit(solution)/shard_map/ppermute | solution.py:554
  22.5 1.9 %collective-permute-start.11 = (bf16[16,3840]{1,0:T(8,128)(2,1)S(1)}, bf16[16,3840]{1,0:T(8,128)(2,1)S(1)}, u32[]{:S(2)}, u32[]{:S(2)}) collective-permute-start(bf16[16,3840]{1,0:T(8,128)(2,1)S(1)} %finish_forward_2.1.refs_4_), channel_id=1, source_target_pairs={{0,12},{1,13},{2,14},{3,15},{4,8},{5,9},{6,10},{7,11},{8,20},{9,21... | collective-permute-start | bytes 368648 | tf_op jit(solution)/shard_map/ppermute | solution.py:554
  25.0 2.8 %collective-permute-start.12 = (bf16[16,3840]{1,0:T(8,128)(2,1)S(1)}, bf16[16,3840]{1,0:T(8,128)(2,1)S(1)}, u32[]{:S(2)}, u32[]{:S(2)}) collective-permute-start(bf16[16,3840]{1,0:T(8,128)(2,1)S(1)} %finish_forward_3.1), channel_id=1, source_target_pairs={{0,14},{1,15},{2,12},{3,13},{4,10},{5,11},{6,8},{7,9},{8,22},{9,23... | collective-permute-start | bytes 368648 | tf_op jit(solution)/shard_map/ppermute | solution.py:554
  27.8 2.6 %experts_backward.1 = (bf16[80,3712]{1,0:T(8,128)(2,1)S(1)}, bf16[80,3712]{1,0:T(8,128)(2,1)S(1)}) custom-call(bf16[80,3584]{1,0:T(8,128)(2,1)S(1)} %get-tuple-element.55.refs_4_.refs_0_, bf16[80,3584]{1,0:T(8,128)(2,1)S(1)} %collective-permute-done.9.refs_1_, bf16[160,512]{1,0:T(8,128)(2,1)S(1)} %get-tuple-element.50.refs_6_.refs_5_.refs_2_, ...), custom_call_target="tpu_custom_call" | custom-call | flops 100000000 | bytes 1000 | tf_op jit(solution)/shard_map/experts_backward/pallas_call | solution.py:38
  30.4 0.3 collective-permute-start.13
  30.6 0.7 %collective-permute-done.5.refs_8_.double.refs_0_ = bf16[32,3840]{1,0:T(8,128)(2,1)S(1)} collective-permute-done((bf16[32,3840]{1,0:T(8,128)(2,1)S(1)}, bf16[32,3840]{1,0:T(8,128)(2,1)S(1)}, u32[]{:S(2)}, u32[]{:S(2)}) %collective-permute-start.5) | collective-permute-done | bytes 245792 | tf_op jit(solution)/shard_map/ppermute | solution.py:554
  31.4 0.4 act_gates.1.refs_0_.refs_7_
  31.8 1.2 %collective-permute-start.10 = (bf16[16,3840]{1,0:T(8,128)(2,1)S(1)}, bf16[16,3840]{1,0:T(8,128)(2,1)S(1)}, u32[]{:S(2)}, u32[]{:S(2)}) collective-permute-start(bf16[16,3840]{1,0:T(8,128)(2,1)S(1)} %lower_chunk.1), channel_id=1, source_target_pairs={{0,2},{1,3},{2,0},{3,1},{4,6},{5,7},{6,4},{7,5},{8,10},{9,11},{10,... | collective-permute-start | bytes 368648 | tf_op jit(solution)/shard_map/ppermute | solution.py:533
  33.0 0.7 %finish_backward.1 = (bf16[16,3840]{1,0:T(8,128)(2,1)S(1)}, bf16[16,3840]{1,0:T(8,128)(2,1)S(1)}, bf16[16,3840]{1,0:T(8,128)(2,1)S(1)}, bf16[16,3840]{1,0:T(8,128)(2,1)S(1)}) custom-call(bf16[32,3840]{1,0:T(8,128)(2,1)S(1)} %get-tuple-element.51.refs_0_, bf16[32,3840]{1,0:T(8,128)(2,1)S(1)} %collective-permute-done.6.refs_1_, ...), custom_call_target="tpu_custom_call" | custom-call | flops 100000000 | bytes 1000 | tf_op jit(solution)/shard_map/finish_backward/pallas_call | solution.py:38
  33.6 2.5 %collective-permute-start.14 = (bf16[16,3840]{1,0:T(8,128)(2,1)S(1)}, bf16[16,3840]{1,0:T(8,128)(2,1)S(1)}, u32[]{:S(2)}, u32[]{:S(2)}) collective-permute-start(bf16[16,3840]{1,0:T(8,128)(2,1)S(1)} %get-tuple-element.62), channel_id=1, source_target_pairs={{0,30},{1,31},{2,28},{3,29},{4,26},{5,27},{6,24},{7,25},{8,6},{9,7... | collective-permute-start | bytes 368648 | tf_op jit(solution)/shard_map/ppermute | solution.py:554
  36.1 1.7 %collective-permute-start.15 = (bf16[16,3840]{1,0:T(8,128)(2,1)S(1)}, bf16[16,3840]{1,0:T(8,128)(2,1)S(1)}, u32[]{:S(2)}, u32[]{:S(2)}) collective-permute-start(bf16[16,3840]{1,0:T(8,128)(2,1)S(1)} %get-tuple-element.63), channel_id=1, source_target_pairs={{0,26},{1,27},{2,24},{3,25},{4,30},{5,31},{6,28},{7,29},{8,2},{9,3... | collective-permute-start | bytes 368648 | tf_op jit(solution)/shard_map/ppermute | solution.py:554
  37.9 0.9 %collective-permute-start.16 = (bf16[16,3840]{1,0:T(8,128)(2,1)S(1)}, bf16[16,3840]{1,0:T(8,128)(2,1)S(1)}, u32[]{:S(2)}, u32[]{:S(2)}) collective-permute-start(bf16[16,3840]{1,0:T(8,128)(2,1)S(1)} %get-tuple-element.64), channel_id=1, source_target_pairs={{0,28},{1,29},{2,30},{3,31},{4,24},{5,25},{6,26},{7,27},{8,4},{9,5... | collective-permute-start | bytes 368648 | tf_op jit(solution)/shard_map/ppermute | solution.py:554
  38.8 1.7 %collective-permute-start.17 = (bf16[16,3840]{1,0:T(8,128)(2,1)S(1)}, bf16[16,3840]{1,0:T(8,128)(2,1)S(1)}, u32[]{:S(2)}, u32[]{:S(2)}) collective-permute-start(bf16[16,3840]{1,0:T(8,128)(2,1)S(1)} %get-tuple-element.65), channel_id=1, source_target_pairs={{0,24},{1,25},{2,26},{3,27},{4,28},{5,29},{6,30},{7,31},{8,0},{9,1... | collective-permute-start | bytes 368648 | tf_op jit(solution)/shard_map/ppermute | solution.py:554
  40.5 3.7 %collective-permute-done.10.refs_1_ = bf16[16,3840]{1,0:T(8,128)(2,1)S(1)} collective-permute-done((bf16[16,3840]{1,0:T(8,128)(2,1)S(1)}, bf16[16,3840]{1,0:T(8,128)(2,1)S(1)}, u32[]{:S(2)}, u32[]{:S(2)}) %collective-permute-start.10) | collective-permute-done | bytes 122912 | tf_op jit(solution)/shard_map/ppermute | solution.py:533
  44.2 1.0 %forward_rows.1 = bf16[64,3584]{1,0:T(8,128)(2,1)} custom-call(bf16[32,3840]{1,0:T(8,128)(2,1)S(1)} %collective-permute-done.5.refs_8_.double.refs_0_, bf16[16,3840]{1,0:T(8,128)(2,1)S(1)} %collective-permute-done.10.refs_1_, bf16[16,3840]{1,0:T(8,128)(2,1)S(1)} %collective-permute-done.11.refs_2_, bf16[16,3840]{1,0:T(8,128)(2,1)S(1)} %collective-permute-done.12.refs_3_), custom_call_target="tpu_custom_call" | custom-call | flops 100000000 | bytes 1000 | tf_op jit(solution)/shard_map/forward_rows/pallas_call | solution.py:38
  45.2 1.0 %collective-permute-done.16.refs_2_ = bf16[16,3840]{1,0:T(8,128)(2,1)S(1)} collective-permute-done((bf16[16,3840]{1,0:T(8,128)(2,1)S(1)}, bf16[16,3840]{1,0:T(8,128)(2,1)S(1)}, u32[]{:S(2)}, u32[]{:S(2)}) %collective-permute-start.16) | collective-permute-done | bytes 122912 | tf_op jit(solution)/shard_map/ppermute | solution.py:554
  46.1 1.0 %collective-permute-done.17.refs_3_ = bf16[16,3840]{1,0:T(8,128)(2,1)S(1)} collective-permute-done((bf16[16,3840]{1,0:T(8,128)(2,1)S(1)}, bf16[16,3840]{1,0:T(8,128)(2,1)S(1)}, u32[]{:S(2)}, u32[]{:S(2)}) %collective-permute-start.17) | collective-permute-done | bytes 122912 | tf_op jit(solution)/shard_map/ppermute | solution.py:554
  47.2 1.0 %backward_rows.1 = bf16[64,3584]{1,0:T(8,128)(2,1)} custom-call(bf16[16,3840]{1,0:T(8,128)(2,1)S(1)} %collective-permute-done.14.refs_0_, bf16[16,3840]{1,0:T(8,128)(2,1)S(1)} %collective-permute-done.15.refs_1_, bf16[16,3840]{1,0:T(8,128)(2,1)S(1)} %collective-permute-done.16.refs_2_, bf16[16,3840]{1,0:T(8,128)(2,1)S(1)} %collective-permute-done.17.refs_3_), custom_call_target="tpu_custom_call" | custom-call | flops 100000000 | bytes 1000 | tf_op jit(solution)/shard_map/backward_rows/pallas_call | solution.py:38
  (26 shorter events, 1.2 us)
Async XLA Ops:
  2.8 9.1 %collective-permute-start = (bf16[16,3840]{1,0:T(8,128)(2,1)S(1)}, bf16[16,3840]{1,0:T(8,128)(2,1)S(1)}, u32[]{:S(2)}, u32[]{:S(2)}) collective-permute-start(bf16[16,3840]{1,0:T(8,128)(2,1)S(1)} %get-tuple-element.35), channel_id=1, source_target_pairs={{0,2},{1,3},{2,0},{3,1},{4,6},{5,7},{6,4},{7,5},{8,10},{9,11},{10,... | collective-permute-start | bytes 368648 | tf_op jit(solution)/shard_map/ppermute | solution.py:533
  5.8 7.2 %collective-permute-start.1 = (bf16[16,3840]{1,0:T(8,128)(2,1)S(1)}, bf16[16,3840]{1,0:T(8,128)(2,1)S(1)}, u32[]{:S(2)}, u32[]{:S(2)}) collective-permute-start(bf16[16,3840]{1,0:T(8,128)(2,1)S(1)} %get-tuple-element.36), channel_id=1, source_target_pairs={{0,4},{1,5},{2,6},{3,7},{4,0},{5,1},{6,2},{7,3},{8,12},{9,13},{10,... | collective-permute-start | bytes 368648 | tf_op jit(solution)/shard_map/ppermute | solution.py:533
  7.3 7.2 %collective-permute-start.2 = (bf16[16,3840]{1,0:T(8,128)(2,1)S(1)}, bf16[16,3840]{1,0:T(8,128)(2,1)S(1)}, u32[]{:S(2)}, u32[]{:S(2)}) collective-permute-start(bf16[16,3840]{1,0:T(8,128)(2,1)S(1)} %get-tuple-element.37), channel_id=1, source_target_pairs={{0,6},{1,7},{2,4},{3,5},{4,2},{5,3},{6,0},{7,1},{8,14},{9,15},{10,... | collective-permute-start | bytes 368648 | tf_op jit(solution)/shard_map/ppermute | solution.py:533
  7.3 7.7 %copy-start = (bf16[1,3584,512]{2,1,0:T(8,128)(2,1)S(1)}, bf16[1,3584,512]{2,1,0:T(8,128)(2,1)}, u32[]{:S(2)}) copy-start(bf16[1,3584,512]{2,1,0:T(8,128)(2,1)} %refs_4_.1) | copy-start | bytes 11010052
  7.3 7.7 %copy-start.1 = (bf16[1,512,3584]{2,1,0:T(8,128)(2,1)S(1)}, bf16[1,512,3584]{2,1,0:T(8,128)(2,1)}, u32[]{:S(2)}) copy-start(bf16[1,512,3584]{2,1,0:T(8,128)(2,1)} %refs_5_.1) | copy-start | bytes 11010052
  8.3 16.1 %collective-permute-start.6 = (bf16[32,3840]{1,0:T(8,128)(2,1)S(1)}, bf16[32,3840]{1,0:T(8,128)(2,1)S(1)}, u32[]{:S(2)}, u32[]{:S(2)}) collective-permute-start(bf16[32,3840]{1,0:T(8,128)(2,1)S(1)} %get-tuple-element.52), channel_id=1, source_target_pairs={{0,2},{1,3},{2,0},{3,1},{4,6},{5,7},{6,4},{7,5},{8,10},{9,11},{10,... | collective-permute-start | bytes 737288 | tf_op jit(solution)/shard_map/ppermute | solution.py:533
  10.3 14.1 %collective-permute-start.7 = (bf16[32,3840]{1,0:T(8,128)(2,1)S(1)}, bf16[32,3840]{1,0:T(8,128)(2,1)S(1)}, u32[]{:S(2)}, u32[]{:S(2)}) collective-permute-start(bf16[32,3840]{1,0:T(8,128)(2,1)S(1)} %get-tuple-element.53), channel_id=1, source_target_pairs={{0,4},{1,5},{2,6},{3,7},{4,0},{5,1},{6,2},{7,3},{8,12},{9,13},{10,... | collective-permute-start | bytes 737288 | tf_op jit(solution)/shard_map/ppermute | solution.py:533
  11.9 12.5 %collective-permute-start.8 = (bf16[32,3840]{1,0:T(8,128)(2,1)S(1)}, bf16[32,3840]{1,0:T(8,128)(2,1)S(1)}, u32[]{:S(2)}, u32[]{:S(2)}) collective-permute-start(bf16[32,3840]{1,0:T(8,128)(2,1)S(1)} %get-tuple-element.54), channel_id=1, source_target_pairs={{0,6},{1,7},{2,4},{3,5},{4,2},{5,3},{6,0},{7,1},{8,14},{9,15},{10,... | collective-permute-start | bytes 737288 | tf_op jit(solution)/shard_map/ppermute | solution.py:533
  15.0 2.0 %collective-permute-start.3 = (bf16[80,3584]{1,0:T(8,128)(2,1)S(1)}, bf16[80,3584]{1,0:T(8,128)(2,1)S(1)}, u32[]{:S(2)}, u32[]{:S(2)}) collective-permute-start(bf16[80,3584]{1,0:T(8,128)(2,1)S(1)} %get-tuple-element.46.refs_0_), channel_id=1, source_target_pairs={{0,1},{1,0},{2,3},{3,2},{4,5},{5,4},{6,7},{7,6},{8,9},{9,8},{10,11... | collective-permute-start | bytes 1720328 | tf_op jit(solution)/shard_map/ppermute | solution.py:543
  18.5 2.0 %collective-permute-start.4 = (bf16[80,3584]{1,0:T(8,128)(2,1)S(1)}, bf16[80,3584]{1,0:T(8,128)(2,1)S(1)}, u32[]{:S(2)}, u32[]{:S(2)}) collective-permute-start(bf16[80,3584]{1,0:T(8,128)(2,1)S(1)} %get-tuple-element.49), channel_id=1, source_target_pairs={{0,1},{1,0},{2,3},{3,2},{4,5},{5,4},{6,7},{7,6},{8,9},{9,8},{10,11... | collective-permute-start | bytes 1720328 | tf_op jit(solution)/shard_map/ppermute | solution.py:543
  20.7 10.6 %collective-permute-start.5 = (bf16[32,3840]{1,0:T(8,128)(2,1)S(1)}, bf16[32,3840]{1,0:T(8,128)(2,1)S(1)}, u32[]{:S(2)}, u32[]{:S(2)}) collective-permute-start(bf16[32,3840]{1,0:T(8,128)(2,1)S(1)} %finish_forward_01.1.refs_6_), channel_id=1, source_target_pairs={{0,8},{1,9},{2,10},{3,11},{4,12},{5,13},{6,14},{7,15},{8,16},{9,17... | collective-permute-start | bytes 737288 | tf_op jit(solution)/shard_map/ppermute | solution.py:554
  22.5 15.4 %collective-permute-start.11 = (bf16[16,3840]{1,0:T(8,128)(2,1)S(1)}, bf16[16,3840]{1,0:T(8,128)(2,1)S(1)}, u32[]{:S(2)}, u32[]{:S(2)}) collective-permute-start(bf16[16,3840]{1,0:T(8,128)(2,1)S(1)} %finish_forward_2.1.refs_4_), channel_id=1, source_target_pairs={{0,12},{1,13},{2,14},{3,15},{4,8},{5,9},{6,10},{7,11},{8,20},{9,21... | collective-permute-start | bytes 368648 | tf_op jit(solution)/shard_map/ppermute | solution.py:554
  24.5 3.3 %collective-permute-start.9 = (bf16[80,3584]{1,0:T(8,128)(2,1)S(1)}, bf16[80,3584]{1,0:T(8,128)(2,1)S(1)}, u32[]{:S(2)}, u32[]{:S(2)}) collective-permute-start(bf16[80,3584]{1,0:T(8,128)(2,1)S(1)} %get-tuple-element.55.refs_4_.refs_0_), channel_id=1, source_target_pairs={{0,1},{1,0},{2,3},{3,2},{4,5},{5,4},{6,7},{7,6},{8,9},{9,8},{10,11... | collective-permute-start | bytes 1720328 | tf_op jit(solution)/shard_map/ppermute | solution.py:543
  25.0 13.8 %collective-permute-start.12 = (bf16[16,3840]{1,0:T(8,128)(2,1)S(1)}, bf16[16,3840]{1,0:T(8,128)(2,1)S(1)}, u32[]{:S(2)}, u32[]{:S(2)}) collective-permute-start(bf16[16,3840]{1,0:T(8,128)(2,1)S(1)} %finish_forward_3.1), channel_id=1, source_target_pairs={{0,14},{1,15},{2,12},{3,13},{4,10},{5,11},{6,8},{7,9},{8,22},{9,23... | collective-permute-start | bytes 368648 | tf_op jit(solution)/shard_map/ppermute | solution.py:554
  30.4 2.6 %collective-permute-start.13 = (bf16[80,3712]{1,0:T(8,128)(2,1)S(1)}, bf16[80,3712]{1,0:T(8,128)(2,1)S(1)}, u32[]{:S(2)}, u32[]{:S(2)}) collective-permute-start(bf16[80,3712]{1,0:T(8,128)(2,1)S(1)} %get-tuple-element.61), channel_id=1, source_target_pairs={{0,1},{1,0},{2,3},{3,2},{4,5},{5,4},{6,7},{7,6},{8,9},{9,8},{10,11... | collective-permute-start | bytes 1781768 | tf_op jit(solution)/shard_map/ppermute | solution.py:543
  31.8 12.4 %collective-permute-start.10 = (bf16[16,3840]{1,0:T(8,128)(2,1)S(1)}, bf16[16,3840]{1,0:T(8,128)(2,1)S(1)}, u32[]{:S(2)}, u32[]{:S(2)}) collective-permute-start(bf16[16,3840]{1,0:T(8,128)(2,1)S(1)} %lower_chunk.1), channel_id=1, source_target_pairs={{0,2},{1,3},{2,0},{3,1},{4,6},{5,7},{6,4},{7,5},{8,10},{9,11},{10,... | collective-permute-start | bytes 368648 | tf_op jit(solution)/shard_map/ppermute | solution.py:533
  33.6 11.5 %collective-permute-start.14 = (bf16[16,3840]{1,0:T(8,128)(2,1)S(1)}, bf16[16,3840]{1,0:T(8,128)(2,1)S(1)}, u32[]{:S(2)}, u32[]{:S(2)}) collective-permute-start(bf16[16,3840]{1,0:T(8,128)(2,1)S(1)} %get-tuple-element.62), channel_id=1, source_target_pairs={{0,30},{1,31},{2,28},{3,29},{4,26},{5,27},{6,24},{7,25},{8,6},{9,7... | collective-permute-start | bytes 368648 | tf_op jit(solution)/shard_map/ppermute | solution.py:554
  36.1 9.0 %collective-permute-start.15 = (bf16[16,3840]{1,0:T(8,128)(2,1)S(1)}, bf16[16,3840]{1,0:T(8,128)(2,1)S(1)}, u32[]{:S(2)}, u32[]{:S(2)}) collective-permute-start(bf16[16,3840]{1,0:T(8,128)(2,1)S(1)} %get-tuple-element.63), channel_id=1, source_target_pairs={{0,26},{1,27},{2,24},{3,25},{4,30},{5,31},{6,28},{7,29},{8,2},{9,3... | collective-permute-start | bytes 368648 | tf_op jit(solution)/shard_map/ppermute | solution.py:554
  37.9 8.3 %collective-permute-start.16 = (bf16[16,3840]{1,0:T(8,128)(2,1)S(1)}, bf16[16,3840]{1,0:T(8,128)(2,1)S(1)}, u32[]{:S(2)}, u32[]{:S(2)}) collective-permute-start(bf16[16,3840]{1,0:T(8,128)(2,1)S(1)} %get-tuple-element.64), channel_id=1, source_target_pairs={{0,28},{1,29},{2,30},{3,31},{4,24},{5,25},{6,26},{7,27},{8,4},{9,5... | collective-permute-start | bytes 368648 | tf_op jit(solution)/shard_map/ppermute | solution.py:554
  38.8 8.4 %collective-permute-start.17 = (bf16[16,3840]{1,0:T(8,128)(2,1)S(1)}, bf16[16,3840]{1,0:T(8,128)(2,1)S(1)}, u32[]{:S(2)}, u32[]{:S(2)}) collective-permute-start(bf16[16,3840]{1,0:T(8,128)(2,1)S(1)} %get-tuple-element.65), channel_id=1, source_target_pairs={{0,24},{1,25},{2,26},{3,27},{4,28},{5,29},{6,30},{7,31},{8,0},{9,1... | collective-permute-start | bytes 368648 | tf_op jit(solution)/shard_map/ppermute | solution.py:554

commit v10 on v9

--- a/solution.py
+++ b/solution.py
@@ -11,7 +11,7 @@
 none = 255.0
 f32 = jnp.float32
 bf16 = jnp.bfloat16
-nt = (((1,), (1,)), ((), ()))
+nn = (((1,), (0,)), ((), ()))
 spaces = {
     "s": pl.BlockSpec(memory_space=pltpu.SMEM),
     "v": pl.BlockSpec(memory_space=pltpu.VMEM),
@@ -214,9 +214,10 @@
     return (h * inv * gain).astype(bf16), inv
 
 
-def normed_rows(z, chunks, vectors):
-    def body(*refs):
-        chunks, (vectors, normed_ref, gates_ref, last, tile) = refs[: z.experts], refs[z.experts :]
+def normed_rows(z, chunks, vectors, after):
+    def body(*refs):
+        chunks, vectors = refs[: z.experts], refs[z.experts]
+        normed_ref, gates_ref, last, tile = refs[z.experts + 1 + len(after) :]
         gain, router = vectors[0:1, :], vectors[1:2, :]
         collect_rows(z, chunks, last, tile)
         for k in range(z.experts + 1):
@@ -229,12 +230,12 @@
 
     return call(
         body,
-        "v" * (z.experts + 1),
+        "v" * (z.experts + 1) + "a" * len(after),
         [shape((z.rows, z.width)), shape((z.rows, 128), f32), shape((16, z.width), f32)],
         [pltpu.VMEM((16, fold), f32)],
         8,
         "normed_rows",
-    )(*chunks, vectors)
+    )(*chunks, vectors, *after)
 
 
 def grad_rows_of(z, chunks, after):
@@ -375,19 +376,34 @@
     )(ordered, *after)
 
 
+def turned(z, weights, held, after, name):
+    rows, columns = weights.shape[1:]
+    step = min(512, rows, columns)
+
+    def body(weights_ref, *refs):
+        for at in range(0, rows, step):
+            for col in range(0, columns, step):
+                block = weights_ref[0, at : at + step, col : col + step]
+                refs[-1][col : col + step, at : at + step] = block.T
+
+    return call(
+        body, "v" + "v" * len(held) + "a" * len(after), shape((columns, rows)), [], 12, name
+    )(weights, *held, *after)
+
+
 def experts_backward(z, rows, hidden, slope, w_gate, w_down, after):
     def body(*refs):
         rows = refs[: z.split]
         hidden_ref, slope_ref, gate_ref, down_ref = refs[z.split : z.split + 4]
         outs = refs[z.split + 4 + len(after) :]
         held = jnp.concatenate([part[...] for part in rows], axis=0)
-        grad_hidden = lax.dot_general(held, down_ref[0], nt, preferred_element_type=f32)
+        grad_hidden = lax.dot_general(held, down_ref[...], nn, preferred_element_type=f32)
         dots = jnp.sum(grad_hidden * hidden_ref[...].astype(f32), axis=-1, keepdims=True)
         grad_gate = (grad_hidden * slope_ref[...]).astype(bf16)
         step = 512
         for col in range(0, z.width, step):
             part = lax.dot_general(
-                grad_gate, gate_ref[0, col : col + step, :], nt, preferred_element_type=f32
+                grad_gate, gate_ref[:, col : col + step], nn, preferred_element_type=f32
             )
             write_parts(z, part, outs, col)
         write_parts(z, jnp.broadcast_to(dots, (dots.shape[0], 128)), outs, z.width)
@@ -572,11 +588,13 @@
     bwd_chunks, vectors = backward_chunks(z, where, slots, [grad, act], gain_row, table)
     bwd_own = dispatch(z, bwd_chunks)
 
-    normed, gates, fwd_last = normed_rows(z, fwd_own, vectors)
+    down_turned = turned(z, w_down, [w_gate], [bwd_chunks[0], fwd_own[1]], "turned_down")
+    normed, gates, fwd_last = normed_rows(z, fwd_own, vectors, [down_turned])
     fwd_all = [normed] + [to_core(z, normed, m) for m in others]
-    ordered = saved_rows(z, where, saved_gate, [w_gate, w_down], [gates])
+    ordered = saved_rows(z, where, saved_gate, [], [gates])
     fwd_parts = experts_forward(z, fwd_all, w_gate, w_down, [ordered])
     hidden, slope = saved_terms(z, ordered, [fwd_parts[0]])
+    gate_turned = turned(z, w_gate, [], [hidden], "turned_gate")
     fwd_parts = [fwd_parts[0]] + [to_core(z, fwd_parts[m], m) for m in others]
 
     assert z.experts == 4
@@ -584,7 +602,7 @@
     def finish(ks, after):
         return finish_forward(z, ks, fwd_own, fwd_last, fwd_parts, gates, after)
 
-    double = finish([0, 1], [hidden])
+    double = finish([0, 1], [gate_turned])
     got = to_section(z, double, 0, 1)
     out2 = finish([2], [hidden, double])
     got2 = to_section(z, out2, 2, 1)
@@ -593,7 +611,7 @@
     inv, act_last = act_norms(z, bwd_own, [grads])
     out3 = finish([3], [inv])
     got3 = to_section(z, out3, 3, 1)
-    bwd_parts = experts_backward(z, grad_all, hidden, slope, w_gate, w_down, [inv])
+    bwd_parts = experts_backward(z, grad_all, hidden, slope, gate_turned, down_turned, [inv])
     affinity = act_gates(z, bwd_own, act_last, inv, vectors, [bwd_parts[0], got])
     (relayed,) = permute_blocks(z, [lower_chunk(z, got, [affinity])], 1)
     fwd_done = [got2, got3]

time: 48.4 us -> 48.3 us (level)
  waiting for transfers between devices: 9.94 us -> 9 us
  Pallas kernels: 13.3 us -> 14.2 us
    ppermute x7, waiting for transfers between devices: 2.73 us -> 4.22 us  [to_section(): return lax.ppermute(chunk, ('pp', 'ep'), pairs)]
    ppermute x7, waiting for transfers between devices: 5.23 us -> 3.77 us  [permute_blocks(): return [lax.ppermute(array, 'ep', pairs) for array in arrays]]
    ppermute x4, waiting for transfers between devices: 1.97 us -> 1.01 us  [to_core(): return lax.ppermute(array, 'ep', pairs)]
    pallas_call x17 -> x19, Pallas kernels: 13.3 us -> 14.2 us  [run(): return kernel(*arrays)]
  transfers between devices with their start and end apart: 18 -> 18, of which waited for: 7 -> 7; matrix products, arithmetic and copies ran while one was open for 0% -> 0% of each run, Pallas kernels for 21% -> 23%
where the time goes in v10:
time: 48.3 us; the launch traced here: 48.1 us
  starting transfers between devices  24.1 us (50%)
  Pallas kernels  14.2 us (29%)
  waiting for transfers between devices  9 us (19%)
  between operations  0.8 us (2%)
    pallas_call x19, Pallas kernels, run(): return kernel(*arrays)  14.2 us
    ppermute x7, starting transfers between devices, to_section(): return lax.ppermute(chunk, ('pp', 'ep'), pairs)  13.1 us
    ppermute x7, starting transfers between devices, permute_blocks(): return [lax.ppermute(array, 'ep', pairs) for array in arrays]  10.4 us
    ppermute x7, waiting for transfers between devices, to_section(): return lax.ppermute(chunk, ('pp', 'ep'), pairs)  4.22 us
    ppermute x7, waiting for transfers between devices, permute_blocks(): return [lax.ppermute(array, 'ep', pairs) for array in arrays]  3.77 us
    ppermute x4, waiting for transfers between devices, to_core(): return lax.ppermute(array, 'ep', pairs)  1.01 us
  transfers between devices with their start and end apart: 18, of which 7 were waited for; matrix products, arithmetic and copies ran while one was open for 0% of the time, Pallas kernels for 23%

profile of v10, /device:TPU:0, one launch (start us, length us, event | category | flops | bytes accessed | tf_op | source)
XLA Modules:
  0.0 48.1 jit_solution(3571014156534716963)
XLA Ops:
  0.7 2.0 %forward_chunks.1 = (bf16[16,3840]{1,0:T(8,128)(2,1)S(1)}, bf16[16,3840]{1,0:T(8,128)(2,1)S(1)}, bf16[16,3840]{1,0:T(8,128)(2,1)S(1)}, bf16[16,3840]{1,0:T(8,128...) custom-call(s32[2]{0:T(128)S(1)} %pad_add_fusion.where, ...), custom_call_target="tpu_custom_call" | custom-call | flops 100000000 | bytes 1000 | tf_op jit(solution)/shard_map/forward_chunks/pallas_call | solution.py:38
  2.8 3.0 %collective-permute-start = (bf16[16,3840]{1,0:T(8,128)(2,1)S(1)}, bf16[16,3840]{1,0:T(8,128)(2,1)S(1)}, u32[]{:S(2)}, u32[]{:S(2)}) collective-permute-start(bf16[16,3840]{1,0:T(8,128)(2,1)S(1)} %get-tuple-element.35), channel_id=1, source_target_pairs={{0,2},{1,3},{2,0},{3,1},{4,6},{5,7},{6,4},{7,5},{8,10},{9,11},{10,... | collective-permute-start | bytes 368648 | tf_op jit(solution)/shard_map/ppermute | solution.py:549
  5.8 1.5 %collective-permute-start.1 = (bf16[16,3840]{1,0:T(8,128)(2,1)S(1)}, bf16[16,3840]{1,0:T(8,128)(2,1)S(1)}, u32[]{:S(2)}, u32[]{:S(2)}) collective-permute-start(bf16[16,3840]{1,0:T(8,128)(2,1)S(1)} %get-tuple-element.36), channel_id=1, source_target_pairs={{0,4},{1,5},{2,6},{3,7},{4,0},{5,1},{6,2},{7,3},{8,12},{9,13},{10,... | collective-permute-start | bytes 368648 | tf_op jit(solution)/shard_map/ppermute | solution.py:549
  7.3 1.0 %backward_chunks.1 = (bf16[32,3840]{1,0:T(8,128)(2,1)S(1)}, bf16[32,3840]{1,0:T(8,128)(2,1)S(1)}, bf16[32,3840]{1,0:T(8,128)(2,1)S(1)}, bf16[32,3840]{1,0:T(8,128)(2,1)S(1)}, f32[8,3584]{1,0:T(8,128)S(1)}) custom-call(s32[2]{0:T(128)S(1)} %pad_add_fusion.where, bf16[80,64]{1,0:T(8,128)(2,1)S(1)} %get-tuple-element.38.selector, ...), custom_call_target="tpu_custom_call" | custom-call | flops 10000000000 | bytes 1000 | tf_op jit(solution)/shard_map/backward_chunks/pallas_call | solution.py:38
  8.3 2.0 %collective-permute-start.6 = (bf16[32,3840]{1,0:T(8,128)(2,1)S(1)}, bf16[32,3840]{1,0:T(8,128)(2,1)S(1)}, u32[]{:S(2)}, u32[]{:S(2)}) collective-permute-start(bf16[32,3840]{1,0:T(8,128)(2,1)S(1)} %get-tuple-element.52), channel_id=1, source_target_pairs={{0,2},{1,3},{2,0},{3,1},{4,6},{5,7},{6,4},{7,5},{8,10},{9,11},{10,... | collective-permute-start | bytes 737288 | tf_op jit(solution)/shard_map/ppermute | solution.py:549
  10.3 1.5 %collective-permute-start.7 = (bf16[32,3840]{1,0:T(8,128)(2,1)S(1)}, bf16[32,3840]{1,0:T(8,128)(2,1)S(1)}, u32[]{:S(2)}, u32[]{:S(2)}) collective-permute-start(bf16[32,3840]{1,0:T(8,128)(2,1)S(1)} %get-tuple-element.53), channel_id=1, source_target_pairs={{0,4},{1,5},{2,6},{3,7},{4,0},{5,1},{6,2},{7,3},{8,12},{9,13},{10,... | collective-permute-start | bytes 737288 | tf_op jit(solution)/shard_map/ppermute | solution.py:549
  11.9 1.1 %collective-permute-start.8 = (bf16[32,3840]{1,0:T(8,128)(2,1)S(1)}, bf16[32,3840]{1,0:T(8,128)(2,1)S(1)}, u32[]{:S(2)}, u32[]{:S(2)}) collective-permute-start(bf16[32,3840]{1,0:T(8,128)(2,1)S(1)} %get-tuple-element.54), channel_id=1, source_target_pairs={{0,6},{1,7},{2,4},{3,5},{4,2},{5,3},{6,0},{7,1},{8,14},{9,15},{10,... | collective-permute-start | bytes 737288 | tf_op jit(solution)/shard_map/ppermute | solution.py:549
  13.0 1.0 %turned_down.1.refs_5_ = bf16[3584,512]{1,0:T(8,128)(2,1)S(1)} custom-call(bf16[1,512,3584]{2,1,0:T(8,128)(2,1)S(1)} %copy-done.1, bf16[1,3584,512]{2,1,0:T(8,128)(2,1)S(1)} %copy-done, bf16[32,3840]{1,0:T(8,128)(2,1)S(1)} %get-tuple-element.45.refs_1_.refs_0_, bf16[16,3840]{1,0:T(8,128)(2,1)S(1)} %collective-permute-done.refs_2_.refs_1_), custom_call_target="tpu_custom_call" | custom-call | flops 100000000 | bytes 1000 | tf_op jit(solution)/shard_map/turned_down/pallas_call | solution.py:38
  14.0 0.5 %collective-permute-done.2.refs_3_.refs_0_ = bf16[16,3840]{1,0:T(8,128)(2,1)S(1)} collective-permute-done((bf16[16,3840]{1,0:T(8,128)(2,1)S(1)}, bf16[16,3840]{1,0:T(8,128)(2,1)S(1)}, u32[]{:S(2)}, u32[]{:S(2)}) %collective-permute-start.2) | collective-permute-done | bytes 122912 | tf_op jit(solution)/shard_map/ppermute | solution.py:549
  14.5 0.5 %normed_rows.1 = (bf16[80,3584]{1,0:T(8,128)(2,1)S(1)}, f32[80,128]{1,0:T(8,128)S(1)}, f32[16,3584]{1,0:T(8,128)S(1)}) custom-call(bf16[16,3840]{1,0:T(8,128)(2,1)S(1)} %get-tuple-element.34.refs_0_, bf16[16,3840]{1,0:T(8,128)(2,1)S(1)} %collective-permute-done.refs_2_.refs_1_, bf16[16,3840]{1,0:T(8,128)(2,1)S(1)} %collective-permute-done.1.refs_2_.refs_0_, ...), custom_call_target="tpu_custom_call" | custom-call | flops 100000000 | bytes 1000 | tf_op jit(solution)/shard_map/normed_rows/pallas_call | solution.py:38
  15.0 1.6 %saved_rows.1.refs_4_.ordered_ref = f32[160,512]{1,0:T(8,128)S(1)} custom-call(s32[2]{0:T(128)S(1)} %pad_add_fusion.where, bf16[1,1,136,512]{3,2,1,0:T(8,128)(2,1)} %saved_any.1, f32[80,128]{1,0:T(8,128)S(1)} %get-tuple-element.48.refs_0_.refs_5_.refs_4_), custom_call_target="tpu_custom_call" | custom-call | flops 15000000512 | bytes 1000 | tf_op jit(solution)/shard_map/saved_rows/pallas_call | solution.py:38
  16.7 0.3 collective-permute-done.3.refs_1_
  17.0 1.5 %experts_forward.1 = (bf16[80,3584]{1,0:T(8,128)(2,1)S(1)}, bf16[80,3584]{1,0:T(8,128)(2,1)S(1)}) custom-call(bf16[80,3584]{1,0:T(8,128)(2,1)S(1)} %get-tuple-element.47.refs_0_, bf16[80,3584]{1,0:T(8,128)(2,1)S(1)} %collective-permute-done.3.refs_1_, bf16[1,3584,512]{2,1,0:T(8,128)(2,1)S(1)} %copy-done, bf16[1,512,3584]{2,1,0:T(8,128)(2,1)S(1)} %copy-done.1, ...), custom_call_target="tpu_custom_call" | custom-call | flops 100000000 | bytes 1000 | tf_op jit(solution)/shard_map/experts_forward/pallas_call | solution.py:38
  18.8 1.0 %turned_gate.1.refs_6_.refs_4_ = bf16[512,3584]{1,0:T(8,128)(2,1)S(1)} custom-call(bf16[1,3584,512]{2,1,0:T(8,128)(2,1)S(1)} %copy-done, bf16[160,512]{1,0:T(8,128)(2,1)S(1)} %get-tuple-element.51.refs_0_.refs_5_.refs_2_), custom_call_target="tpu_custom_call" | custom-call | flops 100000000 | bytes 1000 | tf_op jit(solution)/shard_map/turned_gate/pallas_call | solution.py:38
  19.8 0.7 %collective-permute-done.4.refs_4_.refs_3_ = bf16[80,3584]{1,0:T(8,128)(2,1)S(1)} collective-permute-done((bf16[80,3584]{1,0:T(8,128)(2,1)S(1)}, bf16[80,3584]{1,0:T(8,128)(2,1)S(1)}, u32[]{:S(2)}, u32[]{:S(2)}) %collective-permute-start.4) | collective-permute-done | bytes 573472 | tf_op jit(solution)/shard_map/ppermute | solution.py:559
  20.7 1.6 %collective-permute-start.5 = (bf16[32,3840]{1,0:T(8,128)(2,1)S(1)}, bf16[32,3840]{1,0:T(8,128)(2,1)S(1)}, u32[]{:S(2)}, u32[]{:S(2)}) collective-permute-start(bf16[32,3840]{1,0:T(8,128)(2,1)S(1)} %finish_forward_01.1.refs_6_), channel_id=1, source_target_pairs={{0,8},{1,9},{2,10},{3,11},{4,12},{5,13},{6,14},{7,15},{8,16},{9,17... | collective-permute-start | bytes 737288 | tf_op jit(solution)/shard_map/ppermute | solution.py:570
  22.5 1.9 %collective-permute-start.11 = (bf16[16,3840]{1,0:T(8,128)(2,1)S(1)}, bf16[16,3840]{1,0:T(8,128)(2,1)S(1)}, u32[]{:S(2)}, u32[]{:S(2)}) collective-permute-start(bf16[16,3840]{1,0:T(8,128)(2,1)S(1)} %finish_forward_2.1.refs_4_), channel_id=1, source_target_pairs={{0,12},{1,13},{2,14},{3,15},{4,8},{5,9},{6,10},{7,11},{8,20},{9,21... | collective-permute-start | bytes 368648 | tf_op jit(solution)/shard_map/ppermute | solution.py:570
  25.0 2.8 %collective-permute-start.12 = (bf16[16,3840]{1,0:T(8,128)(2,1)S(1)}, bf16[16,3840]{1,0:T(8,128)(2,1)S(1)}, u32[]{:S(2)}, u32[]{:S(2)}) collective-permute-start(bf16[16,3840]{1,0:T(8,128)(2,1)S(1)} %finish_forward_3.1), channel_id=1, source_target_pairs={{0,14},{1,15},{2,12},{3,13},{4,10},{5,11},{6,8},{7,9},{8,22},{9,23... | collective-permute-start | bytes 368648 | tf_op jit(solution)/shard_map/ppermute | solution.py:570
  27.8 1.5 %experts_backward.1 = (bf16[80,3712]{1,0:T(8,128)(2,1)S(1)}, bf16[80,3712]{1,0:T(8,128)(2,1)S(1)}) custom-call(bf16[80,3584]{1,0:T(8,128)(2,1)S(1)} %get-tuple-element.55.refs_4_.refs_0_, bf16[80,3584]{1,0:T(8,128)(2,1)S(1)} %collective-permute-done.9.refs_1_, bf16[160,512]{1,0:T(8,128)(2,1)S(1)} %get-tuple-element.51.refs_0_.refs_5_.refs_2_, ...), custom_call_target="tpu_custom_call" | custom-call | flops 100000000 | bytes 1000 | tf_op jit(solution)/shard_map/experts_backward/pallas_call | solution.py:38
  29.6 1.8 %collective-permute-done.5.refs_8_.double.refs_0_ = bf16[32,3840]{1,0:T(8,128)(2,1)S(1)} collective-permute-done((bf16[32,3840]{1,0:T(8,128)(2,1)S(1)}, bf16[32,3840]{1,0:T(8,128)(2,1)S(1)}, u32[]{:S(2)}, u32[]{:S(2)}) %collective-permute-start.5) | collective-permute-done | bytes 245792 | tf_op jit(solution)/shard_map/ppermute | solution.py:570
  31.4 0.4 act_gates.1.refs_0_.refs_7_
  31.8 1.2 %collective-permute-start.10 = (bf16[16,3840]{1,0:T(8,128)(2,1)S(1)}, bf16[16,3840]{1,0:T(8,128)(2,1)S(1)}, u32[]{:S(2)}, u32[]{:S(2)}) collective-permute-start(bf16[16,3840]{1,0:T(8,128)(2,1)S(1)} %lower_chunk.1), channel_id=1, source_target_pairs={{0,2},{1,3},{2,0},{3,1},{4,6},{5,7},{6,4},{7,5},{8,10},{9,11},{10,... | collective-permute-start | bytes 368648 | tf_op jit(solution)/shard_map/ppermute | solution.py:549
  33.0 0.7 %finish_backward.1 = (bf16[16,3840]{1,0:T(8,128)(2,1)S(1)}, bf16[16,3840]{1,0:T(8,128)(2,1)S(1)}, bf16[16,3840]{1,0:T(8,128)(2,1)S(1)}, bf16[16,3840]{1,0:T(8,128)(2,1)S(1)}) custom-call(bf16[32,3840]{1,0:T(8,128)(2,1)S(1)} %get-tuple-element.45.refs_1_.refs_0_, bf16[32,3840]{1,0:T(8,128)(2,1)S(1)} %collective-permute-done.6.refs_1_, ...), custom_call_target="tpu_custom_call" | custom-call | flops 100000000 | bytes 1000 | tf_op jit(solution)/shard_map/finish_backward/pallas_call | solution.py:38
  33.7 2.5 %collective-permute-start.14 = (bf16[16,3840]{1,0:T(8,128)(2,1)S(1)}, bf16[16,3840]{1,0:T(8,128)(2,1)S(1)}, u32[]{:S(2)}, u32[]{:S(2)}) collective-permute-start(bf16[16,3840]{1,0:T(8,128)(2,1)S(1)} %get-tuple-element.62), channel_id=1, source_target_pairs={{0,30},{1,31},{2,28},{3,29},{4,26},{5,27},{6,24},{7,25},{8,6},{9,7... | collective-permute-start | bytes 368648 | tf_op jit(solution)/shard_map/ppermute | solution.py:570
  36.1 1.0 %collective-permute-start.15 = (bf16[16,3840]{1,0:T(8,128)(2,1)S(1)}, bf16[16,3840]{1,0:T(8,128)(2,1)S(1)}, u32[]{:S(2)}, u32[]{:S(2)}) collective-permute-start(bf16[16,3840]{1,0:T(8,128)(2,1)S(1)} %get-tuple-element.63), channel_id=1, source_target_pairs={{0,26},{1,27},{2,24},{3,25},{4,30},{5,31},{6,28},{7,29},{8,2},{9,3... | collective-permute-start | bytes 368648 | tf_op jit(solution)/shard_map/ppermute | solution.py:570
  37.1 1.1 %collective-permute-start.16 = (bf16[16,3840]{1,0:T(8,128)(2,1)S(1)}, bf16[16,3840]{1,0:T(8,128)(2,1)S(1)}, u32[]{:S(2)}, u32[]{:S(2)}) collective-permute-start(bf16[16,3840]{1,0:T(8,128)(2,1)S(1)} %get-tuple-element.64), channel_id=1, source_target_pairs={{0,28},{1,29},{2,30},{3,31},{4,24},{5,25},{6,26},{7,27},{8,4},{9,5... | collective-permute-start | bytes 368648 | tf_op jit(solution)/shard_map/ppermute | solution.py:570
  38.2 2.3 %collective-permute-start.17 = (bf16[16,3840]{1,0:T(8,128)(2,1)S(1)}, bf16[16,3840]{1,0:T(8,128)(2,1)S(1)}, u32[]{:S(2)}, u32[]{:S(2)}) collective-permute-start(bf16[16,3840]{1,0:T(8,128)(2,1)S(1)} %get-tuple-element.65), channel_id=1, source_target_pairs={{0,24},{1,25},{2,26},{3,27},{4,28},{5,29},{6,30},{7,31},{8,0},{9,1... | collective-permute-start | bytes 368648 | tf_op jit(solution)/shard_map/ppermute | solution.py:570
  40.5 3.3 %collective-permute-done.10.refs_1_ = bf16[16,3840]{1,0:T(8,128)(2,1)S(1)} collective-permute-done((bf16[16,3840]{1,0:T(8,128)(2,1)S(1)}, bf16[16,3840]{1,0:T(8,128)(2,1)S(1)}, u32[]{:S(2)}, u32[]{:S(2)}) %collective-permute-start.10) | collective-permute-done | bytes 122912 | tf_op jit(solution)/shard_map/ppermute | solution.py:549
  43.7 1.0 %forward_rows.1 = bf16[64,3584]{1,0:T(8,128)(2,1)} custom-call(bf16[32,3840]{1,0:T(8,128)(2,1)S(1)} %collective-permute-done.5.refs_8_.double.refs_0_, bf16[16,3840]{1,0:T(8,128)(2,1)S(1)} %collective-permute-done.10.refs_1_, bf16[16,3840]{1,0:T(8,128)(2,1)S(1)} %collective-permute-done.11.refs_2_, bf16[16,3840]{1,0:T(8,128)(2,1)S(1)} %collective-permute-done.12.refs_3_), custom_call_target="tpu_custom_call" | custom-call | flops 100000000 | bytes 1000 | tf_op jit(solution)/shard_map/forward_rows/pallas_call | solution.py:38
  44.8 1.6 %collective-permute-done.16.refs_2_ = bf16[16,3840]{1,0:T(8,128)(2,1)S(1)} collective-permute-done((bf16[16,3840]{1,0:T(8,128)(2,1)S(1)}, bf16[16,3840]{1,0:T(8,128)(2,1)S(1)}, u32[]{:S(2)}, u32[]{:S(2)}) %collective-permute-start.16) | collective-permute-done | bytes 122912 | tf_op jit(solution)/shard_map/ppermute | solution.py:570
  46.3 0.8 %collective-permute-done.17.refs_3_ = bf16[16,3840]{1,0:T(8,128)(2,1)S(1)} collective-permute-done((bf16[16,3840]{1,0:T(8,128)(2,1)S(1)}, bf16[16,3840]{1,0:T(8,128)(2,1)S(1)}, u32[]{:S(2)}, u32[]{:S(2)}) %collective-permute-start.17) | collective-permute-done | bytes 122912 | tf_op jit(solution)/shard_map/ppermute | solution.py:570
  47.2 1.0 %backward_rows.1 = bf16[64,3584]{1,0:T(8,128)(2,1)} custom-call(bf16[16,3840]{1,0:T(8,128)(2,1)S(1)} %collective-permute-done.14.refs_0_, bf16[16,3840]{1,0:T(8,128)(2,1)S(1)} %collective-permute-done.15.refs_1_, bf16[16,3840]{1,0:T(8,128)(2,1)S(1)} %collective-permute-done.16.refs_2_, bf16[16,3840]{1,0:T(8,128)(2,1)S(1)} %collective-permute-done.17.refs_3_), custom_call_target="tpu_custom_call" | custom-call | flops 100000000 | bytes 1000 | tf_op jit(solution)/shard_map/backward_rows/pallas_call | solution.py:38
  (28 shorter events, 1.8 us)
Async XLA Ops:
  2.8 9.1 %collective-permute-start = (bf16[16,3840]{1,0:T(8,128)(2,1)S(1)}, bf16[16,3840]{1,0:T(8,128)(2,1)S(1)}, u32[]{:S(2)}, u32[]{:S(2)}) collective-permute-start(bf16[16,3840]{1,0:T(8,128)(2,1)S(1)} %get-tuple-element.35), channel_id=1, source_target_pairs={{0,2},{1,3},{2,0},{3,1},{4,6},{5,7},{6,4},{7,5},{8,10},{9,11},{10,... | collective-permute-start | bytes 368648 | tf_op jit(solution)/shard_map/ppermute | solution.py:549
  5.8 8.2 %collective-permute-start.1 = (bf16[16,3840]{1,0:T(8,128)(2,1)S(1)}, bf16[16,3840]{1,0:T(8,128)(2,1)S(1)}, u32[]{:S(2)}, u32[]{:S(2)}) collective-permute-start(bf16[16,3840]{1,0:T(8,128)(2,1)S(1)} %get-tuple-element.36), channel_id=1, source_target_pairs={{0,4},{1,5},{2,6},{3,7},{4,0},{5,1},{6,2},{7,3},{8,12},{9,13},{10,... | collective-permute-start | bytes 368648 | tf_op jit(solution)/shard_map/ppermute | solution.py:549
  7.3 7.2 %collective-permute-start.2 = (bf16[16,3840]{1,0:T(8,128)(2,1)S(1)}, bf16[16,3840]{1,0:T(8,128)(2,1)S(1)}, u32[]{:S(2)}, u32[]{:S(2)}) collective-permute-start(bf16[16,3840]{1,0:T(8,128)(2,1)S(1)} %get-tuple-element.37), channel_id=1, source_target_pairs={{0,6},{1,7},{2,4},{3,5},{4,2},{5,3},{6,0},{7,1},{8,14},{9,15},{10,... | collective-permute-start | bytes 368648 | tf_op jit(solution)/shard_map/ppermute | solution.py:549
  7.3 5.6 %copy-start = (bf16[1,3584,512]{2,1,0:T(8,128)(2,1)S(1)}, bf16[1,3584,512]{2,1,0:T(8,128)(2,1)}, u32[]{:S(2)}) copy-start(bf16[1,3584,512]{2,1,0:T(8,128)(2,1)} %weights_ref.3) | copy-start | bytes 11010052
  7.3 5.6 %copy-start.1 = (bf16[1,512,3584]{2,1,0:T(8,128)(2,1)S(1)}, bf16[1,512,3584]{2,1,0:T(8,128)(2,1)}, u32[]{:S(2)}) copy-start(bf16[1,512,3584]{2,1,0:T(8,128)(2,1)} %refs_3_.1) | copy-start | bytes 11010052
  8.3 16.1 %collective-permute-start.6 = (bf16[32,3840]{1,0:T(8,128)(2,1)S(1)}, bf16[32,3840]{1,0:T(8,128)(2,1)S(1)}, u32[]{:S(2)}, u32[]{:S(2)}) collective-permute-start(bf16[32,3840]{1,0:T(8,128)(2,1)S(1)} %get-tuple-element.52), channel_id=1, source_target_pairs={{0,2},{1,3},{2,0},{3,1},{4,6},{5,7},{6,4},{7,5},{8,10},{9,11},{10,... | collective-permute-start | bytes 737288 | tf_op jit(solution)/shard_map/ppermute | solution.py:549
  10.3 14.1 %collective-permute-start.7 = (bf16[32,3840]{1,0:T(8,128)(2,1)S(1)}, bf16[32,3840]{1,0:T(8,128)(2,1)S(1)}, u32[]{:S(2)}, u32[]{:S(2)}) collective-permute-start(bf16[32,3840]{1,0:T(8,128)(2,1)S(1)} %get-tuple-element.53), channel_id=1, source_target_pairs={{0,4},{1,5},{2,6},{3,7},{4,0},{5,1},{6,2},{7,3},{8,12},{9,13},{10,... | collective-permute-start | bytes 737288 | tf_op jit(solution)/shard_map/ppermute | solution.py:549
  11.9 12.6 %collective-permute-start.8 = (bf16[32,3840]{1,0:T(8,128)(2,1)S(1)}, bf16[32,3840]{1,0:T(8,128)(2,1)S(1)}, u32[]{:S(2)}, u32[]{:S(2)}) collective-permute-start(bf16[32,3840]{1,0:T(8,128)(2,1)S(1)} %get-tuple-element.54), channel_id=1, source_target_pairs={{0,6},{1,7},{2,4},{3,5},{4,2},{5,3},{6,0},{7,1},{8,14},{9,15},{10,... | collective-permute-start | bytes 737288 | tf_op jit(solution)/shard_map/ppermute | solution.py:549
  15.0 2.0 %collective-permute-start.3 = (bf16[80,3584]{1,0:T(8,128)(2,1)S(1)}, bf16[80,3584]{1,0:T(8,128)(2,1)S(1)}, u32[]{:S(2)}, u32[]{:S(2)}) collective-permute-start(bf16[80,3584]{1,0:T(8,128)(2,1)S(1)} %get-tuple-element.47.refs_0_), channel_id=1, source_target_pairs={{0,1},{1,0},{2,3},{3,2},{4,5},{5,4},{6,7},{7,6},{8,9},{9,8},{10,11... | collective-permute-start | bytes 1720328 | tf_op jit(solution)/shard_map/ppermute | solution.py:559
  18.5 2.0 %collective-permute-start.4 = (bf16[80,3584]{1,0:T(8,128)(2,1)S(1)}, bf16[80,3584]{1,0:T(8,128)(2,1)S(1)}, u32[]{:S(2)}, u32[]{:S(2)}) collective-permute-start(bf16[80,3584]{1,0:T(8,128)(2,1)S(1)} %get-tuple-element.50), channel_id=1, source_target_pairs={{0,1},{1,0},{2,3},{3,2},{4,5},{5,4},{6,7},{7,6},{8,9},{9,8},{10,11... | collective-permute-start | bytes 1720328 | tf_op jit(solution)/shard_map/ppermute | solution.py:559
  20.7 10.6 %collective-permute-start.5 = (bf16[32,3840]{1,0:T(8,128)(2,1)S(1)}, bf16[32,3840]{1,0:T(8,128)(2,1)S(1)}, u32[]{:S(2)}, u32[]{:S(2)}) collective-permute-start(bf16[32,3840]{1,0:T(8,128)(2,1)S(1)} %finish_forward_01.1.refs_6_), channel_id=1, source_target_pairs={{0,8},{1,9},{2,10},{3,11},{4,12},{5,13},{6,14},{7,15},{8,16},{9,17... | collective-permute-start | bytes 737288 | tf_op jit(solution)/shard_map/ppermute | solution.py:570
  22.5 14.6 %collective-permute-start.11 = (bf16[16,3840]{1,0:T(8,128)(2,1)S(1)}, bf16[16,3840]{1,0:T(8,128)(2,1)S(1)}, u32[]{:S(2)}, u32[]{:S(2)}) collective-permute-start(bf16[16,3840]{1,0:T(8,128)(2,1)S(1)} %finish_forward_2.1.refs_4_), channel_id=1, source_target_pairs={{0,12},{1,13},{2,14},{3,15},{4,8},{5,9},{6,10},{7,11},{8,20},{9,21... | collective-permute-start | bytes 368648 | tf_op jit(solution)/shard_map/ppermute | solution.py:570
  24.5 3.3 %collective-permute-start.9 = (bf16[80,3584]{1,0:T(8,128)(2,1)S(1)}, bf16[80,3584]{1,0:T(8,128)(2,1)S(1)}, u32[]{:S(2)}, u32[]{:S(2)}) collective-permute-start(bf16[80,3584]{1,0:T(8,128)(2,1)S(1)} %get-tuple-element.55.refs_4_.refs_0_), channel_id=1, source_target_pairs={{0,1},{1,0},{2,3},{3,2},{4,5},{5,4},{6,7},{7,6},{8,9},{9,8},{10,11... | collective-permute-start | bytes 1720328 | tf_op jit(solution)/shard_map/ppermute | solution.py:559
  25.0 13.2 %collective-permute-start.12 = (bf16[16,3840]{1,0:T(8,128)(2,1)S(1)}, bf16[16,3840]{1,0:T(8,128)(2,1)S(1)}, u32[]{:S(2)}, u32[]{:S(2)}) collective-permute-start(bf16[16,3840]{1,0:T(8,128)(2,1)S(1)} %finish_forward_3.1), channel_id=1, source_target_pairs={{0,14},{1,15},{2,12},{3,13},{4,10},{5,11},{6,8},{7,9},{8,22},{9,23... | collective-permute-start | bytes 368648 | tf_op jit(solution)/shard_map/ppermute | solution.py:570
  29.3 3.7 %collective-permute-start.13 = (bf16[80,3712]{1,0:T(8,128)(2,1)S(1)}, bf16[80,3712]{1,0:T(8,128)(2,1)S(1)}, u32[]{:S(2)}, u32[]{:S(2)}) collective-permute-start(bf16[80,3712]{1,0:T(8,128)(2,1)S(1)} %get-tuple-element.61), channel_id=1, source_target_pairs={{0,1},{1,0},{2,3},{3,2},{4,5},{5,4},{6,7},{7,6},{8,9},{9,8},{10,11... | collective-permute-start | bytes 1781768 | tf_op jit(solution)/shard_map/ppermute | solution.py:559
  31.8 11.9 %collective-permute-start.10 = (bf16[16,3840]{1,0:T(8,128)(2,1)S(1)}, bf16[16,3840]{1,0:T(8,128)(2,1)S(1)}, u32[]{:S(2)}, u32[]{:S(2)}) collective-permute-start(bf16[16,3840]{1,0:T(8,128)(2,1)S(1)} %lower_chunk.1), channel_id=1, source_target_pairs={{0,2},{1,3},{2,0},{3,1},{4,6},{5,7},{6,4},{7,5},{8,10},{9,11},{10,... | collective-permute-start | bytes 368648 | tf_op jit(solution)/shard_map/ppermute | solution.py:549
  33.7 11.1 %collective-permute-start.14 = (bf16[16,3840]{1,0:T(8,128)(2,1)S(1)}, bf16[16,3840]{1,0:T(8,128)(2,1)S(1)}, u32[]{:S(2)}, u32[]{:S(2)}) collective-permute-start(bf16[16,3840]{1,0:T(8,128)(2,1)S(1)} %get-tuple-element.62), channel_id=1, source_target_pairs={{0,30},{1,31},{2,28},{3,29},{4,26},{5,27},{6,24},{7,25},{8,6},{9,7... | collective-permute-start | bytes 368648 | tf_op jit(solution)/shard_map/ppermute | solution.py:570
  36.1 8.6 %collective-permute-start.15 = (bf16[16,3840]{1,0:T(8,128)(2,1)S(1)}, bf16[16,3840]{1,0:T(8,128)(2,1)S(1)}, u32[]{:S(2)}, u32[]{:S(2)}) collective-permute-start(bf16[16,3840]{1,0:T(8,128)(2,1)S(1)} %get-tuple-element.63), channel_id=1, source_target_pairs={{0,26},{1,27},{2,24},{3,25},{4,30},{5,31},{6,28},{7,29},{8,2},{9,3... | collective-permute-start | bytes 368648 | tf_op jit(solution)/shard_map/ppermute | solution.py:570
  37.1 9.2 %collective-permute-start.16 = (bf16[16,3840]{1,0:T(8,128)(2,1)S(1)}, bf16[16,3840]{1,0:T(8,128)(2,1)S(1)}, u32[]{:S(2)}, u32[]{:S(2)}) collective-permute-start(bf16[16,3840]{1,0:T(8,128)(2,1)S(1)} %get-tuple-element.64), channel_id=1, source_target_pairs={{0,28},{1,29},{2,30},{3,31},{4,24},{5,25},{6,26},{7,27},{8,4},{9,5... | collective-permute-start | bytes 368648 | tf_op jit(solution)/shard_map/ppermute | solution.py:570
  38.2 8.9 %collective-permute-start.17 = (bf16[16,3840]{1,0:T(8,128)(2,1)S(1)}, bf16[16,3840]{1,0:T(8,128)(2,1)S(1)}, u32[]{:S(2)}, u32[]{:S(2)}) collective-permute-start(bf16[16,3840]{1,0:T(8,128)(2,1)S(1)} %get-tuple-element.65), channel_id=1, source_target_pairs={{0,24},{1,25},{2,26},{3,27},{4,28},{5,29},{6,30},{7,31},{8,0},{9,1... | collective-permute-start | bytes 368648 | tf_op jit(solution)/shard_map/ppermute | solution.py:570

commit v11 on v10

--- a/solution.py
+++ b/solution.py
@@ -431,7 +431,7 @@
 
     def body(*refs):
         chunks, last, parts = refs[:count], refs[count], refs[count + 1 : count + 1 + z.split]
-        gates, out, tile = refs[count + 1 + z.split], refs[-2], refs[-1]
+        gates, outs, tile = refs[count + 1 + z.split], refs[-1 - count : -1], refs[-1]
 
         def mixed(at):
             y = parts[0][at : at + 16, :].astype(f32)
@@ -440,28 +440,19 @@
             return route_scale * (gates[at : at + 16, 0:1] * y)
 
         tail = last[...] + mixed(z.tokens)
-        for i, (k, chunk) in enumerate(zip(ks, chunks)):
+        for k, chunk, out in zip(ks, chunks, outs):
             h = chunk[:, : z.width].astype(f32)
-            rows = out.at[pl.ds(i * 16, 16)]
-            rows[:, : z.width] = (h + mixed(k * z.main)).astype(bf16)
-            put_last(z, tail[k : k + 1, :], chunk, tile, rows)
+            out[:, : z.width] = (h + mixed(k * z.main)).astype(bf16)
+            put_last(z, tail[k : k + 1, :], chunk, tile, out)
 
     return call(
         body,
         "v" * (count + z.split + 2) + "a" * len(after),
-        shape((count * z.main, z.wide)),
+        [shape((z.main, z.wide))] * count,
         [pltpu.VMEM((16, fold), f32)],
         8,
         "finish_forward_" + "".join(map(str, ks)),
     )(*[chunks[k] for k in ks], last, *parts, gates, *after)
-
-
-def lower_chunk(z, double, after):
-    def body(double, *refs):
-        refs[-1][...] = double[16:32, :]
-
-    places = "v" + "a" * len(after)
-    return call(body, places, shape((16, z.wide)), [], 8, "lower_chunk")(double, *after)
 
 
 def finish_backward(z, order, chunks, lasts, terms, parts, vectors, after):
@@ -597,32 +588,32 @@
     gate_turned = turned(z, w_gate, [], [hidden], "turned_gate")
     fwd_parts = [fwd_parts[0]] + [to_core(z, fwd_parts[m], m) for m in others]
 
-    assert z.experts == 4
+    done = {}
 
     def finish(ks, after):
-        return finish_forward(z, ks, fwd_own, fwd_last, fwd_parts, gates, after)
-
-    double = finish([0, 1], [gate_turned])
-    got = to_section(z, double, 0, 1)
-    out2 = finish([2], [hidden, double])
-    got2 = to_section(z, out2, 2, 1)
-    grads, grad_last = grad_rows_of(z, bwd_own, [out2])
+        outs = finish_forward(z, ks, fwd_own, fwd_last, fwd_parts, gates, after)
+        for k, out in zip(ks, outs):
+            done[k] = to_section(z, out, k, 1)
+        return outs[0]
+
+    first, second, third = ([0], [3, 1], [2])
+    out = finish(first, [gate_turned])
+    grads, grad_last = grad_rows_of(z, bwd_own, [out])
     grad_all = [grads] + [to_core(z, grads, m) for m in others]
     inv, act_last = act_norms(z, bwd_own, [grads])
-    out3 = finish([3], [inv])
-    got3 = to_section(z, out3, 3, 1)
-    bwd_parts = experts_backward(z, grad_all, hidden, slope, gate_turned, down_turned, [inv])
-    affinity = act_gates(z, bwd_own, act_last, inv, vectors, [bwd_parts[0], got])
-    (relayed,) = permute_blocks(z, [lower_chunk(z, got, [affinity])], 1)
-    fwd_done = [got2, got3]
+    out = finish(second, [inv])
+    bwd_parts = experts_backward(z, grad_all, hidden, slope, gate_turned, down_turned, [out])
+    affinity = act_gates(z, bwd_own, act_last, inv, vectors, [bwd_parts[0], done[0]])
+    out = finish(third, [affinity])
     bwd_parts = [bwd_parts[0]] + [to_core(z, bwd_parts[m], m) for m in others]
     bwd_out = finish_backward(
-        z, z.order, bwd_own, [grad_last, act_last], [inv, affinity], bwd_parts, vectors, []
+        z, z.order, bwd_own, [grad_last, act_last], [inv, affinity], bwd_parts, vectors, [out]
     )
+    fwd_done = [done[k] for k in range(z.experts)]
     bwd_done = {k: to_section(z, out, k, -1) for k, out in zip(z.order, bwd_out)}
 
     places = [(k, 0) for k in range(z.experts)]
-    fwd_next = order_rows(z, [got, relayed, *fwd_done], places, [], "forward_rows")
+    fwd_next = order_rows(z, fwd_done, places, [], "forward_rows")
     places = [(z.order.index(k), 0) for k in range(z.experts)]
     bwd_next = order_rows(z, [bwd_done[k] for k in z.order], places, [], "backward_rows")
     return (fwd_next, bwd_next)

time: 48.3 us -> 50.9 us (1.054)
  waiting for transfers between devices: 9 us -> 11 us
  starting transfers between devices: 24.1 us -> 24.7 us
    ppermute x7 -> x8, waiting for transfers between devices: 4.22 us -> 7.97 us  [to_section(): return lax.ppermute(chunk, ('pp', 'ep'), pairs)]
    ppermute x7 -> x8, starting transfers between devices: 13.1 us -> 15.1 us  [to_section(): return lax.ppermute(chunk, ('pp', 'ep'), pairs)]
    ppermute x7 -> x6, waiting for transfers between devices: 3.77 us -> 2.07 us  [permute_blocks(): return [lax.ppermute(array, 'ep', pairs) for array in arrays]]
    ppermute x7 -> x6, starting transfers between devices: 10.4 us -> 9.17 us  [permute_blocks(): return [lax.ppermute(array, 'ep', pairs) for array in arrays]]
    pallas_call x19 -> x18, Pallas kernels: 14.2 us -> 14.1 us  [run(): return kernel(*arrays)]
  transfers between devices with their start and end apart: 18 -> 18, of which waited for: 7 -> 8; matrix products, arithmetic and copies ran while one was open for 0% -> 0% of each run, Pallas kernels for 23% -> 22%
where the time goes in v11:
time: 50.9 us; the launch traced here: 50.7 us
  starting transfers between devices  24.7 us (49%)
  Pallas kernels  14.1 us (28%)
  waiting for transfers between devices  11 us (22%)
  between operations  0.79 us (2%)
    ppermute x8, starting transfers between devices, to_section(): return lax.ppermute(chunk, ('pp', 'ep'), pairs)  15.1 us
    pallas_call x18, Pallas kernels, run(): return kernel(*arrays)  14.1 us
    ppermute x6, starting transfers between devices, permute_blocks(): return [lax.ppermute(array, 'ep', pairs) for array in arrays]  9.17 us
    ppermute x8, waiting for transfers between devices, to_section(): return lax.ppermute(chunk, ('pp', 'ep'), pairs)  7.97 us
    ppermute x6, waiting for transfers between devices, permute_blocks(): return [lax.ppermute(array, 'ep', pairs) for array in arrays]  2.07 us
  transfers between devices with their start and end apart: 18, of which 8 were waited for; matrix products, arithmetic and copies ran while one was open for 0% of the time, Pallas kernels for 22%

profile of v11, /device:TPU:0, one launch (start us, length us, event | category | flops | bytes accessed | tf_op | source)
XLA Modules:
  0.0 50.7 jit_solution(11966754703025937603)
XLA Ops:
  0.7 2.0 %forward_chunks.1 = (bf16[16,3840]{1,0:T(8,128)(2,1)S(1)}, bf16[16,3840]{1,0:T(8,128)(2,1)S(1)}, bf16[16,3840]{1,0:T(8,128)(2,1)S(1)}, bf16[16,3840]{1,0:T(8,128...) custom-call(s32[2]{0:T(128)S(1)} %pad_add_fusion.where, ...), custom_call_target="tpu_custom_call" | custom-call | flops 100000000 | bytes 1000 | tf_op jit(solution)/shard_map/forward_chunks/pallas_call | solution.py:38
  2.8 3.0 %collective-permute-start = (bf16[16,3840]{1,0:T(8,128)(2,1)S(1)}, bf16[16,3840]{1,0:T(8,128)(2,1)S(1)}, u32[]{:S(2)}, u32[]{:S(2)}) collective-permute-start(bf16[16,3840]{1,0:T(8,128)(2,1)S(1)} %get-tuple-element.37), channel_id=1, source_target_pairs={{0,2},{1,3},{2,0},{3,1},{4,6},{5,7},{6,4},{7,5},{8,10},{9,11},{10,... | collective-permute-start | bytes 368648 | tf_op jit(solution)/shard_map/ppermute | solution.py:540
  5.8 1.5 %collective-permute-start.1 = (bf16[16,3840]{1,0:T(8,128)(2,1)S(1)}, bf16[16,3840]{1,0:T(8,128)(2,1)S(1)}, u32[]{:S(2)}, u32[]{:S(2)}) collective-permute-start(bf16[16,3840]{1,0:T(8,128)(2,1)S(1)} %get-tuple-element.38), channel_id=1, source_target_pairs={{0,4},{1,5},{2,6},{3,7},{4,0},{5,1},{6,2},{7,3},{8,12},{9,13},{10,... | collective-permute-start | bytes 368648 | tf_op jit(solution)/shard_map/ppermute | solution.py:540
  7.3 1.0 %backward_chunks.1 = (bf16[32,3840]{1,0:T(8,128)(2,1)S(1)}, bf16[32,3840]{1,0:T(8,128)(2,1)S(1)}, bf16[32,3840]{1,0:T(8,128)(2,1)S(1)}, bf16[32,3840]{1,0:T(8,128)(2,1)S(1)}, f32[8,3584]{1,0:T(8,128)S(1)}) custom-call(s32[2]{0:T(128)S(1)} %pad_add_fusion.where, bf16[80,64]{1,0:T(8,128)(2,1)S(1)} %get-tuple-element.40.selector, ...), custom_call_target="tpu_custom_call" | custom-call | flops 10000000000 | bytes 1000 | tf_op jit(solution)/shard_map/backward_chunks/pallas_call | solution.py:38
  8.3 2.0 %collective-permute-start.6 = (bf16[32,3840]{1,0:T(8,128)(2,1)S(1)}, bf16[32,3840]{1,0:T(8,128)(2,1)S(1)}, u32[]{:S(2)}, u32[]{:S(2)}) collective-permute-start(bf16[32,3840]{1,0:T(8,128)(2,1)S(1)} %get-tuple-element.54), channel_id=1, source_target_pairs={{0,2},{1,3},{2,0},{3,1},{4,6},{5,7},{6,4},{7,5},{8,10},{9,11},{10,... | collective-permute-start | bytes 737288 | tf_op jit(solution)/shard_map/ppermute | solution.py:540
  10.3 1.5 %collective-permute-start.7 = (bf16[32,3840]{1,0:T(8,128)(2,1)S(1)}, bf16[32,3840]{1,0:T(8,128)(2,1)S(1)}, u32[]{:S(2)}, u32[]{:S(2)}) collective-permute-start(bf16[32,3840]{1,0:T(8,128)(2,1)S(1)} %get-tuple-element.55), channel_id=1, source_target_pairs={{0,4},{1,5},{2,6},{3,7},{4,0},{5,1},{6,2},{7,3},{8,12},{9,13},{10,... | collective-permute-start | bytes 737288 | tf_op jit(solution)/shard_map/ppermute | solution.py:540
  11.9 1.1 %collective-permute-start.8 = (bf16[32,3840]{1,0:T(8,128)(2,1)S(1)}, bf16[32,3840]{1,0:T(8,128)(2,1)S(1)}, u32[]{:S(2)}, u32[]{:S(2)}) collective-permute-start(bf16[32,3840]{1,0:T(8,128)(2,1)S(1)} %get-tuple-element.56), channel_id=1, source_target_pairs={{0,6},{1,7},{2,4},{3,5},{4,2},{5,3},{6,0},{7,1},{8,14},{9,15},{10,... | collective-permute-start | bytes 737288 | tf_op jit(solution)/shard_map/ppermute | solution.py:540
  13.0 1.0 %turned_down.1.refs_5_ = bf16[3584,512]{1,0:T(8,128)(2,1)S(1)} custom-call(bf16[1,512,3584]{2,1,0:T(8,128)(2,1)S(1)} %copy-done.1, bf16[1,3584,512]{2,1,0:T(8,128)(2,1)S(1)} %copy-done, bf16[32,3840]{1,0:T(8,128)(2,1)S(1)} %get-tuple-element.47.refs_1_.refs_0_, bf16[16,3840]{1,0:T(8,128)(2,1)S(1)} %collective-permute-done.refs_2_.refs_1_), custom_call_target="tpu_custom_call" | custom-call | flops 100000000 | bytes 1000 | tf_op jit(solution)/shard_map/turned_down/pallas_call | solution.py:38
  14.0 0.5 collective-permute-done.2.refs_3_.refs_0_
  14.5 0.5 %normed_rows.1 = (bf16[80,3584]{1,0:T(8,128)(2,1)S(1)}, f32[80,128]{1,0:T(8,128)S(1)}, f32[16,3584]{1,0:T(8,128)S(1)}) custom-call(bf16[16,3840]{1,0:T(8,128)(2,1)S(1)} %get-tuple-element.36.refs_0_, bf16[16,3840]{1,0:T(8,128)(2,1)S(1)} %collective-permute-done.refs_2_.refs_1_, bf16[16,3840]{1,0:T(8,128)(2,1)S(1)} %collective-permute-done.1.refs_2_.refs_0_, ...), custom_call_target="tpu_custom_call" | custom-call | flops 100000000 | bytes 1000 | tf_op jit(solution)/shard_map/normed_rows/pallas_call | solution.py:38
  15.0 1.6 %saved_rows.1.refs_4_.ordered_ref = f32[160,512]{1,0:T(8,128)S(1)} custom-call(s32[2]{0:T(128)S(1)} %pad_add_fusion.where, bf16[1,1,136,512]{3,2,1,0:T(8,128)(2,1)} %saved_any.1, f32[80,128]{1,0:T(8,128)S(1)} %get-tuple-element.50.refs_0_.refs_4_.refs_5_), custom_call_target="tpu_custom_call" | custom-call | flops 15000000512 | bytes 1000 | tf_op jit(solution)/shard_map/saved_rows/pallas_call | solution.py:38
  17.0 1.5 %experts_forward.1 = (bf16[80,3584]{1,0:T(8,128)(2,1)S(1)}, bf16[80,3584]{1,0:T(8,128)(2,1)S(1)}) custom-call(bf16[80,3584]{1,0:T(8,128)(2,1)S(1)} %get-tuple-element.49.refs_0_, bf16[80,3584]{1,0:T(8,128)(2,1)S(1)} %collective-permute-done.3.refs_1_, bf16[1,3584,512]{2,1,0:T(8,128)(2,1)S(1)} %copy-done, bf16[1,512,3584]{2,1,0:T(8,128)(2,1)S(1)} %copy-done.1, ...), custom_call_target="tpu_custom_call" | custom-call | flops 100000000 | bytes 1000 | tf_op jit(solution)/shard_map/experts_forward/pallas_call | solution.py:38
  18.8 1.0 %turned_gate.1.refs_5_.refs_4_ = bf16[512,3584]{1,0:T(8,128)(2,1)S(1)} custom-call(bf16[1,3584,512]{2,1,0:T(8,128)(2,1)S(1)} %copy-done, bf16[160,512]{1,0:T(8,128)(2,1)S(1)} %get-tuple-element.53.refs_0_.refs_2_), custom_call_target="tpu_custom_call" | custom-call | flops 100000000 | bytes 1000 | tf_op jit(solution)/shard_map/turned_gate/pallas_call | solution.py:38
  19.8 0.7 %collective-permute-done.4.refs_3_.refs_4_ = bf16[80,3584]{1,0:T(8,128)(2,1)S(1)} collective-permute-done((bf16[80,3584]{1,0:T(8,128)(2,1)S(1)}, bf16[80,3584]{1,0:T(8,128)(2,1)S(1)}, u32[]{:S(2)}, u32[]{:S(2)}) %collective-permute-start.4) | collective-permute-done | bytes 573472 | tf_op jit(solution)/shard_map/ppermute | solution.py:550
  20.6 1.6 %collective-permute-start.5 = (bf16[16,3840]{1,0:T(8,128)(2,1)S(1)}, bf16[16,3840]{1,0:T(8,128)(2,1)S(1)}, u32[]{:S(2)}, u32[]{:S(2)}) collective-permute-start(bf16[16,3840]{1,0:T(8,128)(2,1)S(1)} %finish_forward_0.1.refs_4_), channel_id=1, source_target_pairs={{0,8},{1,9},{2,10},{3,11},{4,12},{5,13},{6,14},{7,15},{8,16},{9,17... | collective-permute-start | bytes 368648 | tf_op jit(solution)/shard_map/ppermute | solution.py:561
  22.3 1.6 %collective-permute-done.7.refs_2_ = bf16[32,3840]{1,0:T(8,128)(2,1)S(1)} collective-permute-done((bf16[32,3840]{1,0:T(8,128)(2,1)S(1)}, bf16[32,3840]{1,0:T(8,128)(2,1)S(1)}, u32[]{:S(2)}, u32[]{:S(2)}) %collective-permute-start.7) | collective-permute-done | bytes 245792 | tf_op jit(solution)/shard_map/ppermute | solution.py:540
  24.5 2.2 %collective-permute-start.9 = (bf16[16,3840]{1,0:T(8,128)(2,1)S(1)}, bf16[16,3840]{1,0:T(8,128)(2,1)S(1)}, u32[]{:S(2)}, u32[]{:S(2)}) collective-permute-start(bf16[16,3840]{1,0:T(8,128)(2,1)S(1)} %get-tuple-element.59), channel_id=1, source_target_pairs={{0,10},{1,11},{2,8},{3,9},{4,14},{5,15},{6,12},{7,13},{8,18},{9,19... | collective-permute-start | bytes 368648 | tf_op jit(solution)/shard_map/ppermute | solution.py:561
  26.7 2.8 %collective-permute-start.12 = (bf16[16,3840]{1,0:T(8,128)(2,1)S(1)}, bf16[16,3840]{1,0:T(8,128)(2,1)S(1)}, u32[]{:S(2)}, u32[]{:S(2)}) collective-permute-start(bf16[16,3840]{1,0:T(8,128)(2,1)S(1)} %get-tuple-element.62.refs_6_), channel_id=1, source_target_pairs={{0,14},{1,15},{2,12},{3,13},{4,10},{5,11},{6,8},{7,9},{8,22},{9,23... | collective-permute-start | bytes 368648 | tf_op jit(solution)/shard_map/ppermute | solution.py:561
  29.4 1.5 %experts_backward.1 = (bf16[80,3712]{1,0:T(8,128)(2,1)S(1)}, bf16[80,3712]{1,0:T(8,128)(2,1)S(1)}) custom-call(bf16[80,3584]{1,0:T(8,128)(2,1)S(1)} %get-tuple-element.57.refs_4_.refs_0_, bf16[80,3584]{1,0:T(8,128)(2,1)S(1)} %collective-permute-done.10.refs_1_, bf16[160,512]{1,0:T(8,128)(2,1)S(1)} %get-tuple-element.53.refs_0_.refs_2_, ...), custom_call_target="tpu_custom_call" | custom-call | flops 100000000 | bytes 1000 | tf_op jit(solution)/shard_map/experts_backward/pallas_call | solution.py:38
  31.0 0.4 act_gates.1.refs_5_.refs_7_
  31.6 1.7 %collective-permute-start.11 = (bf16[16,3840]{1,0:T(8,128)(2,1)S(1)}, bf16[16,3840]{1,0:T(8,128)(2,1)S(1)}, u32[]{:S(2)}, u32[]{:S(2)}) collective-permute-start(bf16[16,3840]{1,0:T(8,128)(2,1)S(1)} %finish_forward_2.1.refs_11_), channel_id=1, source_target_pairs={{0,12},{1,13},{2,14},{3,15},{4,8},{5,9},{6,10},{7,11},{8,20},{9,21... | collective-permute-start | bytes 368648 | tf_op jit(solution)/shard_map/ppermute | solution.py:561
  33.2 0.7 %finish_backward.1 = (bf16[16,3840]{1,0:T(8,128)(2,1)S(1)}, bf16[16,3840]{1,0:T(8,128)(2,1)S(1)}, bf16[16,3840]{1,0:T(8,128)(2,1)S(1)}, bf16[16,3840]{1,0:T(8,128)(2,1)S(1)}) custom-call(bf16[32,3840]{1,0:T(8,128)(2,1)S(1)} %get-tuple-element.47.refs_1_.refs_0_, bf16[32,3840]{1,0:T(8,128)(2,1)S(1)} %collective-permute-done.6.refs_1_, ...), custom_call_target="tpu_custom_call" | custom-call | flops 100000000 | bytes 1000 | tf_op jit(solution)/shard_map/finish_backward/pallas_call | solution.py:38
  33.9 3.1 %collective-permute-start.14 = (bf16[16,3840]{1,0:T(8,128)(2,1)S(1)}, bf16[16,3840]{1,0:T(8,128)(2,1)S(1)}, u32[]{:S(2)}, u32[]{:S(2)}) collective-permute-start(bf16[16,3840]{1,0:T(8,128)(2,1)S(1)} %get-tuple-element.66), channel_id=1, source_target_pairs={{0,30},{1,31},{2,28},{3,29},{4,26},{5,27},{6,24},{7,25},{8,6},{9,7... | collective-permute-start | bytes 368648 | tf_op jit(solution)/shard_map/ppermute | solution.py:561
  37.1 1.4 %collective-permute-start.15 = (bf16[16,3840]{1,0:T(8,128)(2,1)S(1)}, bf16[16,3840]{1,0:T(8,128)(2,1)S(1)}, u32[]{:S(2)}, u32[]{:S(2)}) collective-permute-start(bf16[16,3840]{1,0:T(8,128)(2,1)S(1)} %get-tuple-element.67), channel_id=1, source_target_pairs={{0,26},{1,27},{2,24},{3,25},{4,30},{5,31},{6,28},{7,29},{8,2},{9,3... | collective-permute-start | bytes 368648 | tf_op jit(solution)/shard_map/ppermute | solution.py:561
  38.4 1.6 %collective-permute-start.16 = (bf16[16,3840]{1,0:T(8,128)(2,1)S(1)}, bf16[16,3840]{1,0:T(8,128)(2,1)S(1)}, u32[]{:S(2)}, u32[]{:S(2)}) collective-permute-start(bf16[16,3840]{1,0:T(8,128)(2,1)S(1)} %get-tuple-element.68), channel_id=1, source_target_pairs={{0,28},{1,29},{2,30},{3,31},{4,24},{5,25},{6,26},{7,27},{8,4},{9,5... | collective-permute-start | bytes 368648 | tf_op jit(solution)/shard_map/ppermute | solution.py:561
  40.0 0.7 %collective-permute-start.17 = (bf16[16,3840]{1,0:T(8,128)(2,1)S(1)}, bf16[16,3840]{1,0:T(8,128)(2,1)S(1)}, u32[]{:S(2)}, u32[]{:S(2)}) collective-permute-start(bf16[16,3840]{1,0:T(8,128)(2,1)S(1)} %get-tuple-element.69), channel_id=1, source_target_pairs={{0,24},{1,25},{2,26},{3,27},{4,28},{5,29},{6,30},{7,31},{8,0},{9,1... | collective-permute-start | bytes 368648 | tf_op jit(solution)/shard_map/ppermute | solution.py:561
  40.7 1.0 %forward_rows.1 = bf16[64,3584]{1,0:T(8,128)(2,1)} custom-call(bf16[16,3840]{1,0:T(8,128)(2,1)S(1)} %collective-permute-done.5.refs_8_.refs_0_, bf16[16,3840]{1,0:T(8,128)(2,1)S(1)} %collective-permute-done.9.refs_1_, bf16[16,3840]{1,0:T(8,128)(2,1)S(1)} %collective-permute-done.11.refs_2_, bf16[16,3840]{1,0:T(8,128)(2,1)S(1)} %collective-permute-done.12.refs_3_), custom_call_target="tpu_custom_call" | custom-call | flops 100000000 | bytes 1000 | tf_op jit(solution)/shard_map/forward_rows/pallas_call | solution.py:38
  41.7 1.0 %collective-permute-done.14.refs_0_ = bf16[16,3840]{1,0:T(8,128)(2,1)S(1)} collective-permute-done((bf16[16,3840]{1,0:T(8,128)(2,1)S(1)}, bf16[16,3840]{1,0:T(8,128)(2,1)S(1)}, u32[]{:S(2)}, u32[]{:S(2)}) %collective-permute-start.14) | collective-permute-done | bytes 122912 | tf_op jit(solution)/shard_map/ppermute | solution.py:561
  42.7 2.4 %collective-permute-done.15.refs_1_ = bf16[16,3840]{1,0:T(8,128)(2,1)S(1)} collective-permute-done((bf16[16,3840]{1,0:T(8,128)(2,1)S(1)}, bf16[16,3840]{1,0:T(8,128)(2,1)S(1)}, u32[]{:S(2)}, u32[]{:S(2)}) %collective-permute-start.15) | collective-permute-done | bytes 122912 | tf_op jit(solution)/shard_map/ppermute | solution.py:561
  45.1 2.9 %collective-permute-done.16.refs_2_ = bf16[16,3840]{1,0:T(8,128)(2,1)S(1)} collective-permute-done((bf16[16,3840]{1,0:T(8,128)(2,1)S(1)}, bf16[16,3840]{1,0:T(8,128)(2,1)S(1)}, u32[]{:S(2)}, u32[]{:S(2)}) %collective-permute-start.16) | collective-permute-done | bytes 122912 | tf_op jit(solution)/shard_map/ppermute | solution.py:561
  48.0 1.7 %collective-permute-done.17.refs_3_ = bf16[16,3840]{1,0:T(8,128)(2,1)S(1)} collective-permute-done((bf16[16,3840]{1,0:T(8,128)(2,1)S(1)}, bf16[16,3840]{1,0:T(8,128)(2,1)S(1)}, u32[]{:S(2)}, u32[]{:S(2)}) %collective-permute-start.17) | collective-permute-done | bytes 122912 | tf_op jit(solution)/shard_map/ppermute | solution.py:561
  49.7 1.0 %backward_rows.1 = bf16[64,3584]{1,0:T(8,128)(2,1)} custom-call(bf16[16,3840]{1,0:T(8,128)(2,1)S(1)} %collective-permute-done.14.refs_0_, bf16[16,3840]{1,0:T(8,128)(2,1)S(1)} %collective-permute-done.15.refs_1_, bf16[16,3840]{1,0:T(8,128)(2,1)S(1)} %collective-permute-done.16.refs_2_, bf16[16,3840]{1,0:T(8,128)(2,1)S(1)} %collective-permute-done.17.refs_3_), custom_call_target="tpu_custom_call" | custom-call | flops 100000000 | bytes 1000 | tf_op jit(solution)/shard_map/backward_rows/pallas_call | solution.py:38
  (27 shorter events, 1.8 us)
Async XLA Ops:
  2.8 9.1 %collective-permute-start = (bf16[16,3840]{1,0:T(8,128)(2,1)S(1)}, bf16[16,3840]{1,0:T(8,128)(2,1)S(1)}, u32[]{:S(2)}, u32[]{:S(2)}) collective-permute-start(bf16[16,3840]{1,0:T(8,128)(2,1)S(1)} %get-tuple-element.37), channel_id=1, source_target_pairs={{0,2},{1,3},{2,0},{3,1},{4,6},{5,7},{6,4},{7,5},{8,10},{9,11},{10,... | collective-permute-start | bytes 368648 | tf_op jit(solution)/shard_map/ppermute | solution.py:540
  5.8 8.2 %collective-permute-start.1 = (bf16[16,3840]{1,0:T(8,128)(2,1)S(1)}, bf16[16,3840]{1,0:T(8,128)(2,1)S(1)}, u32[]{:S(2)}, u32[]{:S(2)}) collective-permute-start(bf16[16,3840]{1,0:T(8,128)(2,1)S(1)} %get-tuple-element.38), channel_id=1, source_target_pairs={{0,4},{1,5},{2,6},{3,7},{4,0},{5,1},{6,2},{7,3},{8,12},{9,13},{10,... | collective-permute-start | bytes 368648 | tf_op jit(solution)/shard_map/ppermute | solution.py:540
  7.3 7.2 %collective-permute-start.2 = (bf16[16,3840]{1,0:T(8,128)(2,1)S(1)}, bf16[16,3840]{1,0:T(8,128)(2,1)S(1)}, u32[]{:S(2)}, u32[]{:S(2)}) collective-permute-start(bf16[16,3840]{1,0:T(8,128)(2,1)S(1)} %get-tuple-element.39), channel_id=1, source_target_pairs={{0,6},{1,7},{2,4},{3,5},{4,2},{5,3},{6,0},{7,1},{8,14},{9,15},{10,... | collective-permute-start | bytes 368648 | tf_op jit(solution)/shard_map/ppermute | solution.py:540
  7.3 5.6 %copy-start = (bf16[1,3584,512]{2,1,0:T(8,128)(2,1)S(1)}, bf16[1,3584,512]{2,1,0:T(8,128)(2,1)}, u32[]{:S(2)}) copy-start(bf16[1,3584,512]{2,1,0:T(8,128)(2,1)} %weights_ref.3) | copy-start | bytes 11010052
  7.3 5.6 %copy-start.1 = (bf16[1,512,3584]{2,1,0:T(8,128)(2,1)S(1)}, bf16[1,512,3584]{2,1,0:T(8,128)(2,1)}, u32[]{:S(2)}) copy-start(bf16[1,512,3584]{2,1,0:T(8,128)(2,1)} %refs_3_.1) | copy-start | bytes 11010052
  8.3 14.0 %collective-permute-start.6 = (bf16[32,3840]{1,0:T(8,128)(2,1)S(1)}, bf16[32,3840]{1,0:T(8,128)(2,1)S(1)}, u32[]{:S(2)}, u32[]{:S(2)}) collective-permute-start(bf16[32,3840]{1,0:T(8,128)(2,1)S(1)} %get-tuple-element.54), channel_id=1, source_target_pairs={{0,2},{1,3},{2,0},{3,1},{4,6},{5,7},{6,4},{7,5},{8,10},{9,11},{10,... | collective-permute-start | bytes 737288 | tf_op jit(solution)/shard_map/ppermute | solution.py:540
  10.3 13.5 %collective-permute-start.7 = (bf16[32,3840]{1,0:T(8,128)(2,1)S(1)}, bf16[32,3840]{1,0:T(8,128)(2,1)S(1)}, u32[]{:S(2)}, u32[]{:S(2)}) collective-permute-start(bf16[32,3840]{1,0:T(8,128)(2,1)S(1)} %get-tuple-element.55), channel_id=1, source_target_pairs={{0,4},{1,5},{2,6},{3,7},{4,0},{5,1},{6,2},{7,3},{8,12},{9,13},{10,... | collective-permute-start | bytes 737288 | tf_op jit(solution)/shard_map/ppermute | solution.py:540
  11.9 12.0 %collective-permute-start.8 = (bf16[32,3840]{1,0:T(8,128)(2,1)S(1)}, bf16[32,3840]{1,0:T(8,128)(2,1)S(1)}, u32[]{:S(2)}, u32[]{:S(2)}) collective-permute-start(bf16[32,3840]{1,0:T(8,128)(2,1)S(1)} %get-tuple-element.56), channel_id=1, source_target_pairs={{0,6},{1,7},{2,4},{3,5},{4,2},{5,3},{6,0},{7,1},{8,14},{9,15},{10,... | collective-permute-start | bytes 737288 | tf_op jit(solution)/shard_map/ppermute | solution.py:540
  15.0 2.0 %collective-permute-start.3 = (bf16[80,3584]{1,0:T(8,128)(2,1)S(1)}, bf16[80,3584]{1,0:T(8,128)(2,1)S(1)}, u32[]{:S(2)}, u32[]{:S(2)}) collective-permute-start(bf16[80,3584]{1,0:T(8,128)(2,1)S(1)} %get-tuple-element.49.refs_0_), channel_id=1, source_target_pairs={{0,1},{1,0},{2,3},{3,2},{4,5},{5,4},{6,7},{7,6},{8,9},{9,8},{10,11... | collective-permute-start | bytes 1720328 | tf_op jit(solution)/shard_map/ppermute | solution.py:550
  18.5 2.0 %collective-permute-start.4 = (bf16[80,3584]{1,0:T(8,128)(2,1)S(1)}, bf16[80,3584]{1,0:T(8,128)(2,1)S(1)}, u32[]{:S(2)}, u32[]{:S(2)}) collective-permute-start(bf16[80,3584]{1,0:T(8,128)(2,1)S(1)} %get-tuple-element.52), channel_id=1, source_target_pairs={{0,1},{1,0},{2,3},{3,2},{4,5},{5,4},{6,7},{7,6},{8,9},{9,8},{10,11... | collective-permute-start | bytes 1720328 | tf_op jit(solution)/shard_map/ppermute | solution.py:550
  20.6 10.4 %collective-permute-start.5 = (bf16[16,3840]{1,0:T(8,128)(2,1)S(1)}, bf16[16,3840]{1,0:T(8,128)(2,1)S(1)}, u32[]{:S(2)}, u32[]{:S(2)}) collective-permute-start(bf16[16,3840]{1,0:T(8,128)(2,1)S(1)} %finish_forward_0.1.refs_4_), channel_id=1, source_target_pairs={{0,8},{1,9},{2,10},{3,11},{4,12},{5,13},{6,14},{7,15},{8,16},{9,17... | collective-permute-start | bytes 368648 | tf_op jit(solution)/shard_map/ppermute | solution.py:561
  23.9 5.5 %collective-permute-start.10 = (bf16[80,3584]{1,0:T(8,128)(2,1)S(1)}, bf16[80,3584]{1,0:T(8,128)(2,1)S(1)}, u32[]{:S(2)}, u32[]{:S(2)}) collective-permute-start(bf16[80,3584]{1,0:T(8,128)(2,1)S(1)} %get-tuple-element.57.refs_4_.refs_0_), channel_id=1, source_target_pairs={{0,1},{1,0},{2,3},{3,2},{4,5},{5,4},{6,7},{7,6},{8,9},{9,8},{10,11... | collective-permute-start | bytes 1720328 | tf_op jit(solution)/shard_map/ppermute | solution.py:550
  24.5 14.0 %collective-permute-start.9 = (bf16[16,3840]{1,0:T(8,128)(2,1)S(1)}, bf16[16,3840]{1,0:T(8,128)(2,1)S(1)}, u32[]{:S(2)}, u32[]{:S(2)}) collective-permute-start(bf16[16,3840]{1,0:T(8,128)(2,1)S(1)} %get-tuple-element.59), channel_id=1, source_target_pairs={{0,10},{1,11},{2,8},{3,9},{4,14},{5,15},{6,12},{7,13},{8,18},{9,19... | collective-permute-start | bytes 368648 | tf_op jit(solution)/shard_map/ppermute | solution.py:561
  26.7 13.4 %collective-permute-start.12 = (bf16[16,3840]{1,0:T(8,128)(2,1)S(1)}, bf16[16,3840]{1,0:T(8,128)(2,1)S(1)}, u32[]{:S(2)}, u32[]{:S(2)}) collective-permute-start(bf16[16,3840]{1,0:T(8,128)(2,1)S(1)} %get-tuple-element.62.refs_6_), channel_id=1, source_target_pairs={{0,14},{1,15},{2,12},{3,13},{4,10},{5,11},{6,8},{7,9},{8,22},{9,23... | collective-permute-start | bytes 368648 | tf_op jit(solution)/shard_map/ppermute | solution.py:561
  30.9 2.3 %collective-permute-start.13 = (bf16[80,3712]{1,0:T(8,128)(2,1)S(1)}, bf16[80,3712]{1,0:T(8,128)(2,1)S(1)}, u32[]{:S(2)}, u32[]{:S(2)}) collective-permute-start(bf16[80,3712]{1,0:T(8,128)(2,1)S(1)} %get-tuple-element.65), channel_id=1, source_target_pairs={{0,1},{1,0},{2,3},{3,2},{4,5},{5,4},{6,7},{7,6},{8,9},{9,8},{10,11... | collective-permute-start | bytes 1781768 | tf_op jit(solution)/shard_map/ppermute | solution.py:550
  31.6 9.2 %collective-permute-start.11 = (bf16[16,3840]{1,0:T(8,128)(2,1)S(1)}, bf16[16,3840]{1,0:T(8,128)(2,1)S(1)}, u32[]{:S(2)}, u32[]{:S(2)}) collective-permute-start(bf16[16,3840]{1,0:T(8,128)(2,1)S(1)} %finish_forward_2.1.refs_11_), channel_id=1, source_target_pairs={{0,12},{1,13},{2,14},{3,15},{4,8},{5,9},{6,10},{7,11},{8,20},{9,21... | collective-permute-start | bytes 368648 | tf_op jit(solution)/shard_map/ppermute | solution.py:561
  33.9 8.8 %collective-permute-start.14 = (bf16[16,3840]{1,0:T(8,128)(2,1)S(1)}, bf16[16,3840]{1,0:T(8,128)(2,1)S(1)}, u32[]{:S(2)}, u32[]{:S(2)}) collective-permute-start(bf16[16,3840]{1,0:T(8,128)(2,1)S(1)} %get-tuple-element.66), channel_id=1, source_target_pairs={{0,30},{1,31},{2,28},{3,29},{4,26},{5,27},{6,24},{7,25},{8,6},{9,7... | collective-permute-start | bytes 368648 | tf_op jit(solution)/shard_map/ppermute | solution.py:561
  37.1 8.1 %collective-permute-start.15 = (bf16[16,3840]{1,0:T(8,128)(2,1)S(1)}, bf16[16,3840]{1,0:T(8,128)(2,1)S(1)}, u32[]{:S(2)}, u32[]{:S(2)}) collective-permute-start(bf16[16,3840]{1,0:T(8,128)(2,1)S(1)} %get-tuple-element.67), channel_id=1, source_target_pairs={{0,26},{1,27},{2,24},{3,25},{4,30},{5,31},{6,28},{7,29},{8,2},{9,3... | collective-permute-start | bytes 368648 | tf_op jit(solution)/shard_map/ppermute | solution.py:561
  38.4 9.6 %collective-permute-start.16 = (bf16[16,3840]{1,0:T(8,128)(2,1)S(1)}, bf16[16,3840]{1,0:T(8,128)(2,1)S(1)}, u32[]{:S(2)}, u32[]{:S(2)}) collective-permute-start(bf16[16,3840]{1,0:T(8,128)(2,1)S(1)} %get-tuple-element.68), channel_id=1, source_target_pairs={{0,28},{1,29},{2,30},{3,31},{4,24},{5,25},{6,26},{7,27},{8,4},{9,5... | collective-permute-start | bytes 368648 | tf_op jit(solution)/shard_map/ppermute | solution.py:561
  40.0 9.7 %collective-permute-start.17 = (bf16[16,3840]{1,0:T(8,128)(2,1)S(1)}, bf16[16,3840]{1,0:T(8,128)(2,1)S(1)}, u32[]{:S(2)}, u32[]{:S(2)}) collective-permute-start(bf16[16,3840]{1,0:T(8,128)(2,1)S(1)} %get-tuple-element.69), channel_id=1, source_target_pairs={{0,24},{1,25},{2,26},{3,27},{4,28},{5,29},{6,30},{7,31},{8,0},{9,1... | collective-permute-start | bytes 368648 | tf_op jit(solution)/shard_map/ppermute | solution.py:561

commit v12 on v11

--- a/solution.py
+++ b/solution.py
@@ -534,14 +534,14 @@
     )(*arrays, *after)
 
 
-def permute_blocks(z, arrays, k):
+def to_block(z, array, k):
     groups = z.experts * z.split
     pairs = [(i, ((i // z.split) ^ k) * z.split + i % z.split) for i in range(groups)]
-    return [lax.ppermute(array, "ep", pairs) for array in arrays]
+    return lax.ppermute(array, "ep", pairs)
 
 
 def dispatch(z, chunks):
-    return [chunks[0]] + [permute_blocks(z, [chunks[k]], k)[0] for k in range(1, z.experts)]
+    return [chunks[0]] + [to_block(z, chunks[k], k) for k in range(1, z.experts)]
 
 
 def to_core(z, array, m):
@@ -596,15 +596,16 @@
             done[k] = to_section(z, out, k, 1)
         return outs[0]
 
-    first, second, third = ([0], [3, 1], [2])
-    out = finish(first, [gate_turned])
+    assert z.experts == 4
+    out = finish([0], [gate_turned])
+    out = finish([2], [gate_turned, out])
     grads, grad_last = grad_rows_of(z, bwd_own, [out])
     grad_all = [grads] + [to_core(z, grads, m) for m in others]
     inv, act_last = act_norms(z, bwd_own, [grads])
-    out = finish(second, [inv])
+    out = finish([3], [inv])
     bwd_parts = experts_backward(z, grad_all, hidden, slope, gate_turned, down_turned, [out])
     affinity = act_gates(z, bwd_own, act_last, inv, vectors, [bwd_parts[0], done[0]])
-    out = finish(third, [affinity])
+    out = finish([1], [affinity])
     bwd_parts = [bwd_parts[0]] + [to_core(z, bwd_parts[m], m) for m in others]
     bwd_out = finish_backward(
         z, z.order, bwd_own, [grad_last, act_last], [inv, affinity], bwd_parts, vectors, [out]

time: 50.9 us -> 49.4 us (0.971)
  waiting for transfers between devices: 11 us -> 9.58 us
    ppermute x6, waiting for transfers between devices: 2.07 us -> 0.52 us  [to_block(): return lax.ppermute(array, 'ep', pairs)]
    pallas_call x18 -> x19, Pallas kernels: 14.1 us -> 14.2 us  [run(): return kernel(*arrays)]
  transfers between devices with their start and end apart: 18 -> 18, of which waited for: 8 -> 7; matrix products, arithmetic and copies ran while one was open for 0% -> 0% of each run, Pallas kernels for 22% -> 23%
where the time goes in v12:
time: 49.4 us; the launch traced here: 49.3 us
  starting transfers between devices  24.6 us (50%)
  Pallas kernels  14.2 us (29%)
  waiting for transfers between devices  9.58 us (19%)
  between operations  0.78 us (2%)
    ppermute x8, starting transfers between devices, to_section(): return lax.ppermute(chunk, ('pp', 'ep'), pairs)  14.8 us
    pallas_call x19, Pallas kernels, run(): return kernel(*arrays)  14.2 us
    ppermute x6, starting transfers between devices, to_block(): return lax.ppermute(array, 'ep', pairs)  9.17 us
    ppermute x8, waiting for transfers between devices, to_section(): return lax.ppermute(chunk, ('pp', 'ep'), pairs)  8.06 us
    ppermute x4, waiting for transfers between devices, to_core(): return lax.ppermute(array, 'ep', pairs)  1 us
  transfers between devices with their start and end apart: 18, of which 7 were waited for; matrix products, arithmetic and copies ran while one was open for 0% of the time, Pallas kernels for 23%

profile of v12, /device:TPU:0, one launch (start us, length us, event | category | flops | bytes accessed | tf_op | source)
XLA Modules:
  0.0 49.3 jit_solution(5330561029035917977)
XLA Ops:
  0.7 2.0 %forward_chunks.1 = (bf16[16,3840]{1,0:T(8,128)(2,1)S(1)}, bf16[16,3840]{1,0:T(8,128)(2,1)S(1)}, bf16[16,3840]{1,0:T(8,128)(2,1)S(1)}, bf16[16,3840]{1,0:T(8,128...) custom-call(s32[2]{0:T(128)S(1)} %pad_add_fusion.where, ...), custom_call_target="tpu_custom_call" | custom-call | flops 100000000 | bytes 1000 | tf_op jit(solution)/shard_map/forward_chunks/pallas_call | solution.py:38
  2.8 3.0 %collective-permute-start = (bf16[16,3840]{1,0:T(8,128)(2,1)S(1)}, bf16[16,3840]{1,0:T(8,128)(2,1)S(1)}, u32[]{:S(2)}, u32[]{:S(2)}) collective-permute-start(bf16[16,3840]{1,0:T(8,128)(2,1)S(1)} %get-tuple-element.35), channel_id=1, source_target_pairs={{0,2},{1,3},{2,0},{3,1},{4,6},{5,7},{6,4},{7,5},{8,10},{9,11},{10,... | collective-permute-start | bytes 368648 | tf_op jit(solution)/shard_map/ppermute | solution.py:540
  5.8 1.5 %collective-permute-start.1 = (bf16[16,3840]{1,0:T(8,128)(2,1)S(1)}, bf16[16,3840]{1,0:T(8,128)(2,1)S(1)}, u32[]{:S(2)}, u32[]{:S(2)}) collective-permute-start(bf16[16,3840]{1,0:T(8,128)(2,1)S(1)} %get-tuple-element.36), channel_id=1, source_target_pairs={{0,4},{1,5},{2,6},{3,7},{4,0},{5,1},{6,2},{7,3},{8,12},{9,13},{10,... | collective-permute-start | bytes 368648 | tf_op jit(solution)/shard_map/ppermute | solution.py:540
  7.3 1.0 %backward_chunks.1 = (bf16[32,3840]{1,0:T(8,128)(2,1)S(1)}, bf16[32,3840]{1,0:T(8,128)(2,1)S(1)}, bf16[32,3840]{1,0:T(8,128)(2,1)S(1)}, bf16[32,3840]{1,0:T(8,128)(2,1)S(1)}, f32[8,3584]{1,0:T(8,128)S(1)}) custom-call(s32[2]{0:T(128)S(1)} %pad_add_fusion.where, bf16[80,64]{1,0:T(8,128)(2,1)S(1)} %get-tuple-element.38.selector, ...), custom_call_target="tpu_custom_call" | custom-call | flops 10000000000 | bytes 1000 | tf_op jit(solution)/shard_map/backward_chunks/pallas_call | solution.py:38
  8.3 2.0 %collective-permute-start.6 = (bf16[32,3840]{1,0:T(8,128)(2,1)S(1)}, bf16[32,3840]{1,0:T(8,128)(2,1)S(1)}, u32[]{:S(2)}, u32[]{:S(2)}) collective-permute-start(bf16[32,3840]{1,0:T(8,128)(2,1)S(1)} %get-tuple-element.52), channel_id=1, source_target_pairs={{0,2},{1,3},{2,0},{3,1},{4,6},{5,7},{6,4},{7,5},{8,10},{9,11},{10,... | collective-permute-start | bytes 737288 | tf_op jit(solution)/shard_map/ppermute | solution.py:540
  10.3 1.5 %collective-permute-start.7 = (bf16[32,3840]{1,0:T(8,128)(2,1)S(1)}, bf16[32,3840]{1,0:T(8,128)(2,1)S(1)}, u32[]{:S(2)}, u32[]{:S(2)}) collective-permute-start(bf16[32,3840]{1,0:T(8,128)(2,1)S(1)} %get-tuple-element.53), channel_id=1, source_target_pairs={{0,4},{1,5},{2,6},{3,7},{4,0},{5,1},{6,2},{7,3},{8,12},{9,13},{10,... | collective-permute-start | bytes 737288 | tf_op jit(solution)/shard_map/ppermute | solution.py:540
  11.9 1.1 %collective-permute-start.8 = (bf16[32,3840]{1,0:T(8,128)(2,1)S(1)}, bf16[32,3840]{1,0:T(8,128)(2,1)S(1)}, u32[]{:S(2)}, u32[]{:S(2)}) collective-permute-start(bf16[32,3840]{1,0:T(8,128)(2,1)S(1)} %get-tuple-element.54), channel_id=1, source_target_pairs={{0,6},{1,7},{2,4},{3,5},{4,2},{5,3},{6,0},{7,1},{8,14},{9,15},{10,... | collective-permute-start | bytes 737288 | tf_op jit(solution)/shard_map/ppermute | solution.py:540
  13.0 1.0 %turned_down.1.refs_5_ = bf16[3584,512]{1,0:T(8,128)(2,1)S(1)} custom-call(bf16[1,512,3584]{2,1,0:T(8,128)(2,1)S(1)} %copy-done.1, bf16[1,3584,512]{2,1,0:T(8,128)(2,1)S(1)} %copy-done, bf16[32,3840]{1,0:T(8,128)(2,1)S(1)} %get-tuple-element.45.refs_1_.refs_0_, bf16[16,3840]{1,0:T(8,128)(2,1)S(1)} %collective-permute-done.refs_2_.refs_1_.refs_0_), custom_call_target="tpu_custom_call" | custom-call | flops 100000000 | bytes 1000 | tf_op jit(solution)/shard_map/turned_down/pallas_call | solution.py:38
  14.0 0.5 %collective-permute-done.2.refs_3_.refs_0_ = bf16[16,3840]{1,0:T(8,128)(2,1)S(1)} collective-permute-done((bf16[16,3840]{1,0:T(8,128)(2,1)S(1)}, bf16[16,3840]{1,0:T(8,128)(2,1)S(1)}, u32[]{:S(2)}, u32[]{:S(2)}) %collective-permute-start.2) | collective-permute-done | bytes 122912 | tf_op jit(solution)/shard_map/ppermute | solution.py:540
  14.5 0.5 %normed_rows.1 = (bf16[80,3584]{1,0:T(8,128)(2,1)S(1)}, f32[80,128]{1,0:T(8,128)S(1)}, f32[16,3584]{1,0:T(8,128)S(1)}) custom-call(bf16[16,3840]{1,0:T(8,128)(2,1)S(1)} %get-tuple-element.34.refs_0_, bf16[16,3840]{1,0:T(8,128)(2,1)S(1)} %collective-permute-done.refs_2_.refs_1_.refs_0_, bf16[16,3840]{1,0:T(8,128)(2,1)S(1)} %collective-permute-done.1.refs_2_.refs_0_, ...), custom_call_target="tpu_custom_call" | custom-call | flops 100000000 | bytes 1000 | tf_op jit(solution)/shard_map/normed_rows/pallas_call | solution.py:38
  15.0 1.6 %saved_rows.1.refs_4_.ordered_ref = f32[160,512]{1,0:T(8,128)S(1)} custom-call(s32[2]{0:T(128)S(1)} %pad_add_fusion.where, bf16[1,1,136,512]{3,2,1,0:T(8,128)(2,1)} %saved_any.1, f32[80,128]{1,0:T(8,128)S(1)} %get-tuple-element.48.refs_0_.refs_4_), custom_call_target="tpu_custom_call" | custom-call | flops 15000000512 | bytes 1000 | tf_op jit(solution)/shard_map/saved_rows/pallas_call | solution.py:38
  16.7 0.3 collective-permute-done.3.refs_1_
  17.0 1.5 %experts_forward.1 = (bf16[80,3584]{1,0:T(8,128)(2,1)S(1)}, bf16[80,3584]{1,0:T(8,128)(2,1)S(1)}) custom-call(bf16[80,3584]{1,0:T(8,128)(2,1)S(1)} %get-tuple-element.47.refs_0_, bf16[80,3584]{1,0:T(8,128)(2,1)S(1)} %collective-permute-done.3.refs_1_, bf16[1,3584,512]{2,1,0:T(8,128)(2,1)S(1)} %copy-done, bf16[1,512,3584]{2,1,0:T(8,128)(2,1)S(1)} %copy-done.1, ...), custom_call_target="tpu_custom_call" | custom-call | flops 100000000 | bytes 1000 | tf_op jit(solution)/shard_map/experts_forward/pallas_call | solution.py:38
  18.8 1.0 %turned_gate.1.refs_5_.refs_4_ = bf16[512,3584]{1,0:T(8,128)(2,1)S(1)} custom-call(bf16[1,3584,512]{2,1,0:T(8,128)(2,1)S(1)} %copy-done, bf16[160,512]{1,0:T(8,128)(2,1)S(1)} %get-tuple-element.51.refs_0_.refs_2_), custom_call_target="tpu_custom_call" | custom-call | flops 100000000 | bytes 1000 | tf_op jit(solution)/shard_map/turned_gate/pallas_call | solution.py:38
  19.8 0.7 %collective-permute-done.4.refs_3_ = bf16[80,3584]{1,0:T(8,128)(2,1)S(1)} collective-permute-done((bf16[80,3584]{1,0:T(8,128)(2,1)S(1)}, bf16[80,3584]{1,0:T(8,128)(2,1)S(1)}, u32[]{:S(2)}, u32[]{:S(2)}) %collective-permute-start.4) | collective-permute-done | bytes 573472 | tf_op jit(solution)/shard_map/ppermute | solution.py:550
  20.6 1.6 %collective-permute-start.5 = (bf16[16,3840]{1,0:T(8,128)(2,1)S(1)}, bf16[16,3840]{1,0:T(8,128)(2,1)S(1)}, u32[]{:S(2)}, u32[]{:S(2)}) collective-permute-start(bf16[16,3840]{1,0:T(8,128)(2,1)S(1)} %finish_forward_0.1.refs_6_), channel_id=1, source_target_pairs={{0,8},{1,9},{2,10},{3,11},{4,12},{5,13},{6,14},{7,15},{8,16},{9,17... | collective-permute-start | bytes 368648 | tf_op jit(solution)/shard_map/ppermute | solution.py:561
  22.4 1.9 %collective-permute-start.11 = (bf16[16,3840]{1,0:T(8,128)(2,1)S(1)}, bf16[16,3840]{1,0:T(8,128)(2,1)S(1)}, u32[]{:S(2)}, u32[]{:S(2)}) collective-permute-start(bf16[16,3840]{1,0:T(8,128)(2,1)S(1)} %finish_forward_2.1.refs_4_), channel_id=1, source_target_pairs={{0,12},{1,13},{2,14},{3,15},{4,8},{5,9},{6,10},{7,11},{8,20},{9,21... | collective-permute-start | bytes 368648 | tf_op jit(solution)/shard_map/ppermute | solution.py:561
  24.9 2.8 %collective-permute-start.12 = (bf16[16,3840]{1,0:T(8,128)(2,1)S(1)}, bf16[16,3840]{1,0:T(8,128)(2,1)S(1)}, u32[]{:S(2)}, u32[]{:S(2)}) collective-permute-start(bf16[16,3840]{1,0:T(8,128)(2,1)S(1)} %finish_forward_3.1.refs_6_), channel_id=1, source_target_pairs={{0,14},{1,15},{2,12},{3,13},{4,10},{5,11},{6,8},{7,9},{8,22},{9,23... | collective-permute-start | bytes 368648 | tf_op jit(solution)/shard_map/ppermute | solution.py:561
  27.7 1.5 %experts_backward.1 = (bf16[80,3712]{1,0:T(8,128)(2,1)S(1)}, bf16[80,3712]{1,0:T(8,128)(2,1)S(1)}) custom-call(bf16[80,3584]{1,0:T(8,128)(2,1)S(1)} %get-tuple-element.55.refs_4_.refs_0_, bf16[80,3584]{1,0:T(8,128)(2,1)S(1)} %collective-permute-done.9.refs_1_, bf16[160,512]{1,0:T(8,128)(2,1)S(1)} %get-tuple-element.51.refs_0_.refs_2_, ...), custom_call_target="tpu_custom_call" | custom-call | flops 100000000 | bytes 1000 | tf_op jit(solution)/shard_map/experts_backward/pallas_call | solution.py:38
  29.5 0.4 act_gates.1.refs_5_.refs_7_
  30.0 1.7 %collective-permute-start.10 = (bf16[16,3840]{1,0:T(8,128)(2,1)S(1)}, bf16[16,3840]{1,0:T(8,128)(2,1)S(1)}, u32[]{:S(2)}, u32[]{:S(2)}) collective-permute-start(bf16[16,3840]{1,0:T(8,128)(2,1)S(1)} %finish_forward_1.1.refs_11_), channel_id=1, source_target_pairs={{0,10},{1,11},{2,8},{3,9},{4,14},{5,15},{6,12},{7,13},{8,18},{9,19... | collective-permute-start | bytes 368648 | tf_op jit(solution)/shard_map/ppermute | solution.py:561
  31.7 0.7 %finish_backward.1 = (bf16[16,3840]{1,0:T(8,128)(2,1)S(1)}, bf16[16,3840]{1,0:T(8,128)(2,1)S(1)}, bf16[16,3840]{1,0:T(8,128)(2,1)S(1)}, bf16[16,3840]{1,0:T(8,128)(2,1)S(1)}) custom-call(bf16[32,3840]{1,0:T(8,128)(2,1)S(1)} %get-tuple-element.45.refs_1_.refs_0_, bf16[32,3840]{1,0:T(8,128)(2,1)S(1)} %collective-permute-done.6.refs_1_, ...), custom_call_target="tpu_custom_call" | custom-call | flops 100000000 | bytes 1000 | tf_op jit(solution)/shard_map/finish_backward/pallas_call | solution.py:38
  32.4 3.3 %collective-permute-start.14 = (bf16[16,3840]{1,0:T(8,128)(2,1)S(1)}, bf16[16,3840]{1,0:T(8,128)(2,1)S(1)}, u32[]{:S(2)}, u32[]{:S(2)}) collective-permute-start(bf16[16,3840]{1,0:T(8,128)(2,1)S(1)} %get-tuple-element.62), channel_id=1, source_target_pairs={{0,30},{1,31},{2,28},{3,29},{4,26},{5,27},{6,24},{7,25},{8,6},{9,7... | collective-permute-start | bytes 368648 | tf_op jit(solution)/shard_map/ppermute | solution.py:561
  35.8 1.0 %collective-permute-start.15 = (bf16[16,3840]{1,0:T(8,128)(2,1)S(1)}, bf16[16,3840]{1,0:T(8,128)(2,1)S(1)}, u32[]{:S(2)}, u32[]{:S(2)}) collective-permute-start(bf16[16,3840]{1,0:T(8,128)(2,1)S(1)} %get-tuple-element.63), channel_id=1, source_target_pairs={{0,26},{1,27},{2,24},{3,25},{4,30},{5,31},{6,28},{7,29},{8,2},{9,3... | collective-permute-start | bytes 368648 | tf_op jit(solution)/shard_map/ppermute | solution.py:561
  36.7 2.0 %collective-permute-start.16 = (bf16[16,3840]{1,0:T(8,128)(2,1)S(1)}, bf16[16,3840]{1,0:T(8,128)(2,1)S(1)}, u32[]{:S(2)}, u32[]{:S(2)}) collective-permute-start(bf16[16,3840]{1,0:T(8,128)(2,1)S(1)} %get-tuple-element.64), channel_id=1, source_target_pairs={{0,28},{1,29},{2,30},{3,31},{4,24},{5,25},{6,26},{7,27},{8,4},{9,5... | collective-permute-start | bytes 368648 | tf_op jit(solution)/shard_map/ppermute | solution.py:561
  38.8 0.4 collective-permute-start.17
  39.2 1.0 %forward_rows.1 = bf16[64,3584]{1,0:T(8,128)(2,1)} custom-call(bf16[16,3840]{1,0:T(8,128)(2,1)S(1)} %collective-permute-done.5.refs_8_.refs_0_, bf16[16,3840]{1,0:T(8,128)(2,1)S(1)} %collective-permute-done.10.refs_1_, bf16[16,3840]{1,0:T(8,128)(2,1)S(1)} %collective-permute-done.11.refs_2_, bf16[16,3840]{1,0:T(8,128)(2,1)S(1)} %collective-permute-done.12.refs_3_), custom_call_target="tpu_custom_call" | custom-call | flops 100000000 | bytes 1000 | tf_op jit(solution)/shard_map/forward_rows/pallas_call | solution.py:38
  40.2 1.0 %collective-permute-done.14.refs_0_ = bf16[16,3840]{1,0:T(8,128)(2,1)S(1)} collective-permute-done((bf16[16,3840]{1,0:T(8,128)(2,1)S(1)}, bf16[16,3840]{1,0:T(8,128)(2,1)S(1)}, u32[]{:S(2)}, u32[]{:S(2)}) %collective-permute-start.14) | collective-permute-done | bytes 122912 | tf_op jit(solution)/shard_map/ppermute | solution.py:561
  41.3 2.4 %collective-permute-done.15.refs_1_ = bf16[16,3840]{1,0:T(8,128)(2,1)S(1)} collective-permute-done((bf16[16,3840]{1,0:T(8,128)(2,1)S(1)}, bf16[16,3840]{1,0:T(8,128)(2,1)S(1)}, u32[]{:S(2)}, u32[]{:S(2)}) %collective-permute-start.15) | collective-permute-done | bytes 122912 | tf_op jit(solution)/shard_map/ppermute | solution.py:561
  43.7 2.4 %collective-permute-done.16.refs_2_ = bf16[16,3840]{1,0:T(8,128)(2,1)S(1)} collective-permute-done((bf16[16,3840]{1,0:T(8,128)(2,1)S(1)}, bf16[16,3840]{1,0:T(8,128)(2,1)S(1)}, u32[]{:S(2)}, u32[]{:S(2)}) %collective-permute-start.16) | collective-permute-done | bytes 122912 | tf_op jit(solution)/shard_map/ppermute | solution.py:561
  46.0 2.3 %collective-permute-done.17.refs_3_ = bf16[16,3840]{1,0:T(8,128)(2,1)S(1)} collective-permute-done((bf16[16,3840]{1,0:T(8,128)(2,1)S(1)}, bf16[16,3840]{1,0:T(8,128)(2,1)S(1)}, u32[]{:S(2)}, u32[]{:S(2)}) %collective-permute-start.17) | collective-permute-done | bytes 122912 | tf_op jit(solution)/shard_map/ppermute | solution.py:561
  48.3 1.0 %backward_rows.1 = bf16[64,3584]{1,0:T(8,128)(2,1)} custom-call(bf16[16,3840]{1,0:T(8,128)(2,1)S(1)} %collective-permute-done.14.refs_0_, bf16[16,3840]{1,0:T(8,128)(2,1)S(1)} %collective-permute-done.15.refs_1_, bf16[16,3840]{1,0:T(8,128)(2,1)S(1)} %collective-permute-done.16.refs_2_, bf16[16,3840]{1,0:T(8,128)(2,1)S(1)} %collective-permute-done.17.refs_3_), custom_call_target="tpu_custom_call" | custom-call | flops 100000000 | bytes 1000 | tf_op jit(solution)/shard_map/backward_rows/pallas_call | solution.py:38
  (28 shorter events, 1.8 us)
Async XLA Ops:
  2.8 9.1 %collective-permute-start = (bf16[16,3840]{1,0:T(8,128)(2,1)S(1)}, bf16[16,3840]{1,0:T(8,128)(2,1)S(1)}, u32[]{:S(2)}, u32[]{:S(2)}) collective-permute-start(bf16[16,3840]{1,0:T(8,128)(2,1)S(1)} %get-tuple-element.35), channel_id=1, source_target_pairs={{0,2},{1,3},{2,0},{3,1},{4,6},{5,7},{6,4},{7,5},{8,10},{9,11},{10,... | collective-permute-start | bytes 368648 | tf_op jit(solution)/shard_map/ppermute | solution.py:540
  5.8 8.2 %collective-permute-start.1 = (bf16[16,3840]{1,0:T(8,128)(2,1)S(1)}, bf16[16,3840]{1,0:T(8,128)(2,1)S(1)}, u32[]{:S(2)}, u32[]{:S(2)}) collective-permute-start(bf16[16,3840]{1,0:T(8,128)(2,1)S(1)} %get-tuple-element.36), channel_id=1, source_target_pairs={{0,4},{1,5},{2,6},{3,7},{4,0},{5,1},{6,2},{7,3},{8,12},{9,13},{10,... | collective-permute-start | bytes 368648 | tf_op jit(solution)/shard_map/ppermute | solution.py:540
  7.3 7.2 %collective-permute-start.2 = (bf16[16,3840]{1,0:T(8,128)(2,1)S(1)}, bf16[16,3840]{1,0:T(8,128)(2,1)S(1)}, u32[]{:S(2)}, u32[]{:S(2)}) collective-permute-start(bf16[16,3840]{1,0:T(8,128)(2,1)S(1)} %get-tuple-element.37), channel_id=1, source_target_pairs={{0,6},{1,7},{2,4},{3,5},{4,2},{5,3},{6,0},{7,1},{8,14},{9,15},{10,... | collective-permute-start | bytes 368648 | tf_op jit(solution)/shard_map/ppermute | solution.py:540
  7.3 5.6 %copy-start = (bf16[1,3584,512]{2,1,0:T(8,128)(2,1)S(1)}, bf16[1,3584,512]{2,1,0:T(8,128)(2,1)}, u32[]{:S(2)}) copy-start(bf16[1,3584,512]{2,1,0:T(8,128)(2,1)} %weights_ref.3) | copy-start | bytes 11010052
  7.3 5.6 %copy-start.1 = (bf16[1,512,3584]{2,1,0:T(8,128)(2,1)S(1)}, bf16[1,512,3584]{2,1,0:T(8,128)(2,1)}, u32[]{:S(2)}) copy-start(bf16[1,512,3584]{2,1,0:T(8,128)(2,1)} %refs_3_.1) | copy-start | bytes 11010052
  8.3 16.0 %collective-permute-start.6 = (bf16[32,3840]{1,0:T(8,128)(2,1)S(1)}, bf16[32,3840]{1,0:T(8,128)(2,1)S(1)}, u32[]{:S(2)}, u32[]{:S(2)}) collective-permute-start(bf16[32,3840]{1,0:T(8,128)(2,1)S(1)} %get-tuple-element.52), channel_id=1, source_target_pairs={{0,2},{1,3},{2,0},{3,1},{4,6},{5,7},{6,4},{7,5},{8,10},{9,11},{10,... | collective-permute-start | bytes 737288 | tf_op jit(solution)/shard_map/ppermute | solution.py:540
  10.3 14.0 %collective-permute-start.7 = (bf16[32,3840]{1,0:T(8,128)(2,1)S(1)}, bf16[32,3840]{1,0:T(8,128)(2,1)S(1)}, u32[]{:S(2)}, u32[]{:S(2)}) collective-permute-start(bf16[32,3840]{1,0:T(8,128)(2,1)S(1)} %get-tuple-element.53), channel_id=1, source_target_pairs={{0,4},{1,5},{2,6},{3,7},{4,0},{5,1},{6,2},{7,3},{8,12},{9,13},{10,... | collective-permute-start | bytes 737288 | tf_op jit(solution)/shard_map/ppermute | solution.py:540
  11.9 12.5 %collective-permute-start.8 = (bf16[32,3840]{1,0:T(8,128)(2,1)S(1)}, bf16[32,3840]{1,0:T(8,128)(2,1)S(1)}, u32[]{:S(2)}, u32[]{:S(2)}) collective-permute-start(bf16[32,3840]{1,0:T(8,128)(2,1)S(1)} %get-tuple-element.54), channel_id=1, source_target_pairs={{0,6},{1,7},{2,4},{3,5},{4,2},{5,3},{6,0},{7,1},{8,14},{9,15},{10,... | collective-permute-start | bytes 737288 | tf_op jit(solution)/shard_map/ppermute | solution.py:540
  15.0 2.0 %collective-permute-start.3 = (bf16[80,3584]{1,0:T(8,128)(2,1)S(1)}, bf16[80,3584]{1,0:T(8,128)(2,1)S(1)}, u32[]{:S(2)}, u32[]{:S(2)}) collective-permute-start(bf16[80,3584]{1,0:T(8,128)(2,1)S(1)} %get-tuple-element.47.refs_0_), channel_id=1, source_target_pairs={{0,1},{1,0},{2,3},{3,2},{4,5},{5,4},{6,7},{7,6},{8,9},{9,8},{10,11... | collective-permute-start | bytes 1720328 | tf_op jit(solution)/shard_map/ppermute | solution.py:550
  18.5 2.0 %collective-permute-start.4 = (bf16[80,3584]{1,0:T(8,128)(2,1)S(1)}, bf16[80,3584]{1,0:T(8,128)(2,1)S(1)}, u32[]{:S(2)}, u32[]{:S(2)}) collective-permute-start(bf16[80,3584]{1,0:T(8,128)(2,1)S(1)} %get-tuple-element.50), channel_id=1, source_target_pairs={{0,1},{1,0},{2,3},{3,2},{4,5},{5,4},{6,7},{7,6},{8,9},{9,8},{10,11... | collective-permute-start | bytes 1720328 | tf_op jit(solution)/shard_map/ppermute | solution.py:550
  20.6 8.8 %collective-permute-start.5 = (bf16[16,3840]{1,0:T(8,128)(2,1)S(1)}, bf16[16,3840]{1,0:T(8,128)(2,1)S(1)}, u32[]{:S(2)}, u32[]{:S(2)}) collective-permute-start(bf16[16,3840]{1,0:T(8,128)(2,1)S(1)} %finish_forward_0.1.refs_6_), channel_id=1, source_target_pairs={{0,8},{1,9},{2,10},{3,11},{4,12},{5,13},{6,14},{7,15},{8,16},{9,17... | collective-permute-start | bytes 368648 | tf_op jit(solution)/shard_map/ppermute | solution.py:561
  22.4 14.3 %collective-permute-start.11 = (bf16[16,3840]{1,0:T(8,128)(2,1)S(1)}, bf16[16,3840]{1,0:T(8,128)(2,1)S(1)}, u32[]{:S(2)}, u32[]{:S(2)}) collective-permute-start(bf16[16,3840]{1,0:T(8,128)(2,1)S(1)} %finish_forward_2.1.refs_4_), channel_id=1, source_target_pairs={{0,12},{1,13},{2,14},{3,15},{4,8},{5,9},{6,10},{7,11},{8,20},{9,21... | collective-permute-start | bytes 368648 | tf_op jit(solution)/shard_map/ppermute | solution.py:561
  24.4 3.3 %collective-permute-start.9 = (bf16[80,3584]{1,0:T(8,128)(2,1)S(1)}, bf16[80,3584]{1,0:T(8,128)(2,1)S(1)}, u32[]{:S(2)}, u32[]{:S(2)}) collective-permute-start(bf16[80,3584]{1,0:T(8,128)(2,1)S(1)} %get-tuple-element.55.refs_4_.refs_0_), channel_id=1, source_target_pairs={{0,1},{1,0},{2,3},{3,2},{4,5},{5,4},{6,7},{7,6},{8,9},{9,8},{10,11... | collective-permute-start | bytes 1720328 | tf_op jit(solution)/shard_map/ppermute | solution.py:550
  24.9 13.9 %collective-permute-start.12 = (bf16[16,3840]{1,0:T(8,128)(2,1)S(1)}, bf16[16,3840]{1,0:T(8,128)(2,1)S(1)}, u32[]{:S(2)}, u32[]{:S(2)}) collective-permute-start(bf16[16,3840]{1,0:T(8,128)(2,1)S(1)} %finish_forward_3.1.refs_6_), channel_id=1, source_target_pairs={{0,14},{1,15},{2,12},{3,13},{4,10},{5,11},{6,8},{7,9},{8,22},{9,23... | collective-permute-start | bytes 368648 | tf_op jit(solution)/shard_map/ppermute | solution.py:561
  29.2 2.6 %collective-permute-start.13 = (bf16[80,3712]{1,0:T(8,128)(2,1)S(1)}, bf16[80,3712]{1,0:T(8,128)(2,1)S(1)}, u32[]{:S(2)}, u32[]{:S(2)}) collective-permute-start(bf16[80,3712]{1,0:T(8,128)(2,1)S(1)} %get-tuple-element.61), channel_id=1, source_target_pairs={{0,1},{1,0},{2,3},{3,2},{4,5},{5,4},{6,7},{7,6},{8,9},{9,8},{10,11... | collective-permute-start | bytes 1781768 | tf_op jit(solution)/shard_map/ppermute | solution.py:550
  30.0 9.2 %collective-permute-start.10 = (bf16[16,3840]{1,0:T(8,128)(2,1)S(1)}, bf16[16,3840]{1,0:T(8,128)(2,1)S(1)}, u32[]{:S(2)}, u32[]{:S(2)}) collective-permute-start(bf16[16,3840]{1,0:T(8,128)(2,1)S(1)} %finish_forward_1.1.refs_11_), channel_id=1, source_target_pairs={{0,10},{1,11},{2,8},{3,9},{4,14},{5,15},{6,12},{7,13},{8,18},{9,19... | collective-permute-start | bytes 368648 | tf_op jit(solution)/shard_map/ppermute | solution.py:561
  32.4 8.8 %collective-permute-start.14 = (bf16[16,3840]{1,0:T(8,128)(2,1)S(1)}, bf16[16,3840]{1,0:T(8,128)(2,1)S(1)}, u32[]{:S(2)}, u32[]{:S(2)}) collective-permute-start(bf16[16,3840]{1,0:T(8,128)(2,1)S(1)} %get-tuple-element.62), channel_id=1, source_target_pairs={{0,30},{1,31},{2,28},{3,29},{4,26},{5,27},{6,24},{7,25},{8,6},{9,7... | collective-permute-start | bytes 368648 | tf_op jit(solution)/shard_map/ppermute | solution.py:561
  35.8 7.9 %collective-permute-start.15 = (bf16[16,3840]{1,0:T(8,128)(2,1)S(1)}, bf16[16,3840]{1,0:T(8,128)(2,1)S(1)}, u32[]{:S(2)}, u32[]{:S(2)}) collective-permute-start(bf16[16,3840]{1,0:T(8,128)(2,1)S(1)} %get-tuple-element.63), channel_id=1, source_target_pairs={{0,26},{1,27},{2,24},{3,25},{4,30},{5,31},{6,28},{7,29},{8,2},{9,3... | collective-permute-start | bytes 368648 | tf_op jit(solution)/shard_map/ppermute | solution.py:561
  36.7 9.3 %collective-permute-start.16 = (bf16[16,3840]{1,0:T(8,128)(2,1)S(1)}, bf16[16,3840]{1,0:T(8,128)(2,1)S(1)}, u32[]{:S(2)}, u32[]{:S(2)}) collective-permute-start(bf16[16,3840]{1,0:T(8,128)(2,1)S(1)} %get-tuple-element.64), channel_id=1, source_target_pairs={{0,28},{1,29},{2,30},{3,31},{4,24},{5,25},{6,26},{7,27},{8,4},{9,5... | collective-permute-start | bytes 368648 | tf_op jit(solution)/shard_map/ppermute | solution.py:561
  38.8 9.5 %collective-permute-start.17 = (bf16[16,3840]{1,0:T(8,128)(2,1)S(1)}, bf16[16,3840]{1,0:T(8,128)(2,1)S(1)}, u32[]{:S(2)}, u32[]{:S(2)}) collective-permute-start(bf16[16,3840]{1,0:T(8,128)(2,1)S(1)} %get-tuple-element.65), channel_id=1, source_target_pairs={{0,24},{1,25},{2,26},{3,27},{4,28},{5,29},{6,30},{7,31},{8,0},{9,1... | collective-permute-start | bytes 368648 | tf_op jit(solution)/shard_map/ppermute | solution.py:561

commit v13 on v10

--- a/solution.py
+++ b/solution.py
@@ -1,3 +1,5 @@
+import functools
+
 import jax
 import jax.numpy as jnp
 from jax import lax
@@ -26,6 +28,7 @@
     "saved_terms": 15,
     "act_norms": 15,
     "act_gates": 15,
+    "forward_rows_early": 15,
 }
 
 
@@ -503,27 +506,48 @@
     )(*chunks, *lasts, *terms, *parts, vectors, *after)
 
 
-def order_rows(z, arrays, places, after, name):
-    count = len(arrays)
+def ordered_columns(z, chunks):
     lanes = z.tokens + 16 * z.experts
+    some = next(iter(chunks))
+    filled = [chunks.get(k, chunks[some]) for k in range(z.experts)]
+    tiles = [chunk[:16, z.width :] for chunk in filled]
+    token_row = tiles[some].astype(f32)[z.pieces : z.pieces + 1, :lanes]
+    token = lax.broadcasted_iota(jnp.int32, (z.tokens, lanes), 0).astype(f32)
+    lane = lax.broadcasted_iota(jnp.int32, (z.tokens, lanes), 1)
+    piece = jnp.where(lane < z.tokens, -1, lane % 16)
+    ours = token == token_row
+    if len(chunks) < z.experts:
+        held = [lane // 16 % z.experts == k for k in chunks]
+        ours = ours & functools.reduce(jnp.logical_or, held)
+    for i in range(z.pieces):
+        cols = pl.ds(i * fold, fold)
+        selector = jnp.where(ours & ((piece < 0) | (piece == i)), 1.0, 0.0).astype(bf16)
+        rows = jnp.concatenate([chunk[:16, cols] for chunk in filled] + tiles, axis=0)
+        yield cols, jnp.dot(selector, rows, preferred_element_type=f32)
+
+
+def some_rows(z, chunks, after, name):
+    ks = list(chunks)
+
+    def body(*refs):
+        for cols, rows in ordered_columns(z, dict(zip(ks, refs))):
+            refs[-1][:, cols] = rows.astype(bf16)
+
+    places = "v" * len(ks) + "a" * len(after)
+    return call(body, places, shape((z.tokens, z.width)), [], 8, name)(*chunks.values(), *after)
+
+
+def order_rows(z, chunks, others, name):
+    ks, count = list(chunks), len(chunks)
     steps = 7 if z.pieces % 7 == 0 else z.pieces
 
     def body(*refs):
-        arrays, (out_any, out, sems) = refs[:count], refs[count + len(after) :]
-        chunks = [arrays[i].at[pl.ds(at, 16)] for i, at in places]
-        tiles = [chunk[:, z.width :] for chunk in chunks]
-        token_row = tiles[0].astype(f32)[z.pieces : z.pieces + 1, :lanes]
-        token = lax.broadcasted_iota(jnp.int32, (z.tokens, lanes), 0).astype(f32)
-        lane = lax.broadcasted_iota(jnp.int32, (z.tokens, lanes), 1)
-        piece = jnp.where(lane < z.tokens, -1, lane % 16)
-        ours = token == token_row
+        others, (out_any, out, sems) = refs[count:-3], refs[-3:]
         copies = []
-        for i in range(z.pieces):
-            cols = pl.ds(i * fold, fold)
-            mine = ours & ((piece < 0) | (piece == i))
-            selector = jnp.where(mine, 1.0, 0.0).astype(bf16)
-            rows = jnp.concatenate([chunk[:, cols] for chunk in chunks] + tiles, axis=0)
-            out[:, cols] = jnp.dot(selector, rows, preferred_element_type=f32).astype(bf16)
+        for i, (cols, rows) in enumerate(ordered_columns(z, dict(zip(ks, refs)))):
+            for other in others:
+                rows = rows + other[:, cols].astype(f32)
+            out[:, cols] = rows.astype(bf16)
             if (i + 1) % (z.pieces // steps) == 0:
                 done = pl.ds((i + 1) * fold - z.width // steps, z.width // steps)
                 copy = pltpu.make_async_copy(out.at[:, done], out_any.at[:, done], sems.at[len(copies)])
@@ -534,13 +558,13 @@
 
     return call(
         body,
-        "v" * count + "a" * len(after),
+        "v" * (count + len(others)),
         shape((z.tokens, z.width)),
         [pltpu.VMEM((z.tokens, z.width), bf16), pltpu.SemaphoreType.DMA((steps,))],
         8,
         name,
         spaces["a"],
-    )(*arrays, *after)
+    )(*chunks.values(), *others)
 
 
 def permute_blocks(z, arrays, k):
@@ -612,19 +636,18 @@
     out3 = finish([3], [inv])
     got3 = to_section(z, out3, 3, 1)
     bwd_parts = experts_backward(z, grad_all, hidden, slope, gate_turned, down_turned, [inv])
-    affinity = act_gates(z, bwd_own, act_last, inv, vectors, [bwd_parts[0], got])
-    (relayed,) = permute_blocks(z, [lower_chunk(z, got, [affinity])], 1)
+    affinity = act_gates(z, bwd_own, act_last, inv, vectors, [bwd_parts[0]])
     fwd_done = [got2, got3]
     bwd_parts = [bwd_parts[0]] + [to_core(z, bwd_parts[m], m) for m in others]
     bwd_out = finish_backward(
         z, z.order, bwd_own, [grad_last, act_last], [inv, affinity], bwd_parts, vectors, []
     )
+    (relayed,) = permute_blocks(z, [lower_chunk(z, got, [bwd_out[0]])], 1)
     bwd_done = {k: to_section(z, out, k, -1) for k, out in zip(z.order, bwd_out)}
 
-    places = [(k, 0) for k in range(z.experts)]
-    fwd_next = order_rows(z, [got, relayed, *fwd_done], places, [], "forward_rows")
-    places = [(z.order.index(k), 0) for k in range(z.experts)]
-    bwd_next = order_rows(z, [bwd_done[k] for k in z.order], places, [], "backward_rows")
+    early = some_rows(z, {0: got, 2: got2, 3: got3}, [], "forward_rows_early")
+    fwd_next = order_rows(z, {1: relayed}, [early], "forward_rows")
+    bwd_next = order_rows(z, {k: bwd_done[k] for k in z.order}, [], "backward_rows")
     return (fwd_next, bwd_next)
 
 

time: 48.3 us -> 48.1 us (level)
    ppermute x7, waiting for transfers between devices: 4.22 us -> 0.02 us  [to_section(): return lax.ppermute(chunk, ('pp', 'ep'), pairs)]
    ppermute x7, waiting for transfers between devices: 3.77 us -> 6.27 us  [permute_blocks(): return [lax.ppermute(array, 'ep', pairs) for array in arrays]]
    ppermute x4, waiting for transfers between devices: 1.01 us -> 2.42 us  [to_core(): return lax.ppermute(array, 'ep', pairs)]
    pallas_call x19 -> x20, Pallas kernels: 14.2 us -> 14.4 us  [run(): return kernel(*arrays)]
  transfers between devices with their start and end apart: 18 -> 18, of which waited for: 7 -> 5; matrix products, arithmetic and copies ran while one was open for 0% -> 0% of each run, Pallas kernels for 23% -> 24%
where the time goes in v13:
time: 48.1 us; the launch traced here: 47.9 us
  starting transfers between devices  23.9 us (50%)
  Pallas kernels  14.4 us (30%)
  waiting for transfers between devices  8.7 us (18%)
  between operations  0.82 us (2%)
    pallas_call x20, Pallas kernels, run(): return kernel(*arrays)  14.4 us
    ppermute x7, starting transfers between devices, to_section(): return lax.ppermute(chunk, ('pp', 'ep'), pairs)  13.2 us
    ppermute x7, starting transfers between devices, permute_blocks(): return [lax.ppermute(array, 'ep', pairs) for array in arrays]  10.1 us
    ppermute x7, waiting for transfers between devices, permute_blocks(): return [lax.ppermute(array, 'ep', pairs) for array in arrays]  6.27 us
    ppermute x4, waiting for transfers between devices, to_core(): return lax.ppermute(array, 'ep', pairs)  2.42 us
  transfers between devices with their start and end apart: 18, of which 5 were waited for; matrix products, arithmetic and copies ran while one was open for 0% of the time, Pallas kernels for 24%

profile of v13, /device:TPU:0, one launch (start us, length us, event | category | flops | bytes accessed | tf_op | source)
XLA Modules:
  0.0 47.9 jit_solution(16435328182765610217)
XLA Ops:
  0.7 2.0 %forward_chunks.1 = (bf16[16,3840]{1,0:T(8,128)(2,1)S(1)}, bf16[16,3840]{1,0:T(8,128)(2,1)S(1)}, bf16[16,3840]{1,0:T(8,128)(2,1)S(1)}, bf16[16,3840]{1,0:T(8,128...) custom-call(s32[2]{0:T(128)S(1)} %pad_add_fusion.where, ...), custom_call_target="tpu_custom_call" | custom-call | flops 100000000 | bytes 1000 | tf_op jit(solution)/shard_map/forward_chunks/pallas_call | solution.py:41
  2.8 3.0 %collective-permute-start = (bf16[16,3840]{1,0:T(8,128)(2,1)S(1)}, bf16[16,3840]{1,0:T(8,128)(2,1)S(1)}, u32[]{:S(2)}, u32[]{:S(2)}) collective-permute-start(bf16[16,3840]{1,0:T(8,128)(2,1)S(1)} %get-tuple-element.35), channel_id=1, source_target_pairs={{0,2},{1,3},{2,0},{3,1},{4,6},{5,7},{6,4},{7,5},{8,10},{9,11},{10,... | collective-permute-start | bytes 368648 | tf_op jit(solution)/shard_map/ppermute | solution.py:573
  5.8 1.5 %collective-permute-start.1 = (bf16[16,3840]{1,0:T(8,128)(2,1)S(1)}, bf16[16,3840]{1,0:T(8,128)(2,1)S(1)}, u32[]{:S(2)}, u32[]{:S(2)}) collective-permute-start(bf16[16,3840]{1,0:T(8,128)(2,1)S(1)} %get-tuple-element.36), channel_id=1, source_target_pairs={{0,4},{1,5},{2,6},{3,7},{4,0},{5,1},{6,2},{7,3},{8,12},{9,13},{10,... | collective-permute-start | bytes 368648 | tf_op jit(solution)/shard_map/ppermute | solution.py:573
  7.3 1.0 %backward_chunks.1 = (bf16[32,3840]{1,0:T(8,128)(2,1)S(1)}, bf16[32,3840]{1,0:T(8,128)(2,1)S(1)}, bf16[32,3840]{1,0:T(8,128)(2,1)S(1)}, bf16[32,3840]{1,0:T(8,128)(2,1)S(1)}, f32[8,3584]{1,0:T(8,128)S(1)}) custom-call(s32[2]{0:T(128)S(1)} %pad_add_fusion.where, bf16[80,64]{1,0:T(8,128)(2,1)S(1)} %get-tuple-element.38.selector, ...), custom_call_target="tpu_custom_call" | custom-call | flops 10000000000 | bytes 1000 | tf_op jit(solution)/shard_map/backward_chunks/pallas_call | solution.py:41
  8.3 2.0 %collective-permute-start.6 = (bf16[32,3840]{1,0:T(8,128)(2,1)S(1)}, bf16[32,3840]{1,0:T(8,128)(2,1)S(1)}, u32[]{:S(2)}, u32[]{:S(2)}) collective-permute-start(bf16[32,3840]{1,0:T(8,128)(2,1)S(1)} %get-tuple-element.52), channel_id=1, source_target_pairs={{0,2},{1,3},{2,0},{3,1},{4,6},{5,7},{6,4},{7,5},{8,10},{9,11},{10,... | collective-permute-start | bytes 737288 | tf_op jit(solution)/shard_map/ppermute | solution.py:573
  10.3 1.5 %collective-permute-start.7 = (bf16[32,3840]{1,0:T(8,128)(2,1)S(1)}, bf16[32,3840]{1,0:T(8,128)(2,1)S(1)}, u32[]{:S(2)}, u32[]{:S(2)}) collective-permute-start(bf16[32,3840]{1,0:T(8,128)(2,1)S(1)} %get-tuple-element.53), channel_id=1, source_target_pairs={{0,4},{1,5},{2,6},{3,7},{4,0},{5,1},{6,2},{7,3},{8,12},{9,13},{10,... | collective-permute-start | bytes 737288 | tf_op jit(solution)/shard_map/ppermute | solution.py:573
  11.9 1.1 %collective-permute-start.8 = (bf16[32,3840]{1,0:T(8,128)(2,1)S(1)}, bf16[32,3840]{1,0:T(8,128)(2,1)S(1)}, u32[]{:S(2)}, u32[]{:S(2)}) collective-permute-start(bf16[32,3840]{1,0:T(8,128)(2,1)S(1)} %get-tuple-element.54), channel_id=1, source_target_pairs={{0,6},{1,7},{2,4},{3,5},{4,2},{5,3},{6,0},{7,1},{8,14},{9,15},{10,... | collective-permute-start | bytes 737288 | tf_op jit(solution)/shard_map/ppermute | solution.py:573
  13.0 1.0 %turned_down.1.refs_5_ = bf16[3584,512]{1,0:T(8,128)(2,1)S(1)} custom-call(bf16[1,512,3584]{2,1,0:T(8,128)(2,1)S(1)} %copy-done.1, bf16[1,3584,512]{2,1,0:T(8,128)(2,1)S(1)} %copy-done, bf16[32,3840]{1,0:T(8,128)(2,1)S(1)} %get-tuple-element.45.refs_1_.refs_0_, bf16[16,3840]{1,0:T(8,128)(2,1)S(1)} %collective-permute-done.refs_2_.refs_1_), custom_call_target="tpu_custom_call" | custom-call | flops 100000000 | bytes 1000 | tf_op jit(solution)/shard_map/turned_down/pallas_call | solution.py:41
  14.0 0.5 %collective-permute-done.2.refs_3_.refs_0_ = bf16[16,3840]{1,0:T(8,128)(2,1)S(1)} collective-permute-done((bf16[16,3840]{1,0:T(8,128)(2,1)S(1)}, bf16[16,3840]{1,0:T(8,128)(2,1)S(1)}, u32[]{:S(2)}, u32[]{:S(2)}) %collective-permute-start.2) | collective-permute-done | bytes 122912 | tf_op jit(solution)/shard_map/ppermute | solution.py:573
  14.5 0.5 %normed_rows.1 = (bf16[80,3584]{1,0:T(8,128)(2,1)S(1)}, f32[80,128]{1,0:T(8,128)S(1)}, f32[16,3584]{1,0:T(8,128)S(1)}) custom-call(bf16[16,3840]{1,0:T(8,128)(2,1)S(1)} %get-tuple-element.34.refs_0_, bf16[16,3840]{1,0:T(8,128)(2,1)S(1)} %collective-permute-done.refs_2_.refs_1_, bf16[16,3840]{1,0:T(8,128)(2,1)S(1)} %collective-permute-done.1.refs_2_.refs_0_, ...), custom_call_target="tpu_custom_call" | custom-call | flops 100000000 | bytes 1000 | tf_op jit(solution)/shard_map/normed_rows/pallas_call | solution.py:41
  15.0 1.6 %saved_rows.1.refs_4_.ordered_ref = f32[160,512]{1,0:T(8,128)S(1)} custom-call(s32[2]{0:T(128)S(1)} %pad_add_fusion.where, bf16[1,1,136,512]{3,2,1,0:T(8,128)(2,1)} %saved_any.1, f32[80,128]{1,0:T(8,128)S(1)} %get-tuple-element.48.refs_0_.refs_5_.refs_4_), custom_call_target="tpu_custom_call" | custom-call | flops 15000000512 | bytes 1000 | tf_op jit(solution)/shard_map/saved_rows/pallas_call | solution.py:41
  16.7 0.3 collective-permute-done.3.refs_1_
  17.0 1.5 %experts_forward.1 = (bf16[80,3584]{1,0:T(8,128)(2,1)S(1)}, bf16[80,3584]{1,0:T(8,128)(2,1)S(1)}) custom-call(bf16[80,3584]{1,0:T(8,128)(2,1)S(1)} %get-tuple-element.47.refs_0_, bf16[80,3584]{1,0:T(8,128)(2,1)S(1)} %collective-permute-done.3.refs_1_, bf16[1,3584,512]{2,1,0:T(8,128)(2,1)S(1)} %copy-done, bf16[1,512,3584]{2,1,0:T(8,128)(2,1)S(1)} %copy-done.1, ...), custom_call_target="tpu_custom_call" | custom-call | flops 100000000 | bytes 1000 | tf_op jit(solution)/shard_map/experts_forward/pallas_call | solution.py:41
  18.8 1.0 %turned_gate.1.refs_6_.refs_4_ = bf16[512,3584]{1,0:T(8,128)(2,1)S(1)} custom-call(bf16[1,3584,512]{2,1,0:T(8,128)(2,1)S(1)} %copy-done, bf16[160,512]{1,0:T(8,128)(2,1)S(1)} %get-tuple-element.51.refs_0_.refs_5_.refs_2_), custom_call_target="tpu_custom_call" | custom-call | flops 100000000 | bytes 1000 | tf_op jit(solution)/shard_map/turned_gate/pallas_call | solution.py:41
  19.8 0.7 %collective-permute-done.4.refs_4_.refs_3_ = bf16[80,3584]{1,0:T(8,128)(2,1)S(1)} collective-permute-done((bf16[80,3584]{1,0:T(8,128)(2,1)S(1)}, bf16[80,3584]{1,0:T(8,128)(2,1)S(1)}, u32[]{:S(2)}, u32[]{:S(2)}) %collective-permute-start.4) | collective-permute-done | bytes 573472 | tf_op jit(solution)/shard_map/ppermute | solution.py:583
  20.7 1.6 %collective-permute-start.5 = (bf16[32,3840]{1,0:T(8,128)(2,1)S(1)}, bf16[32,3840]{1,0:T(8,128)(2,1)S(1)}, u32[]{:S(2)}, u32[]{:S(2)}) collective-permute-start(bf16[32,3840]{1,0:T(8,128)(2,1)S(1)} %finish_forward_01.1.refs_6_), channel_id=1, source_target_pairs={{0,8},{1,9},{2,10},{3,11},{4,12},{5,13},{6,14},{7,15},{8,16},{9,17... | collective-permute-start | bytes 737288 | tf_op jit(solution)/shard_map/ppermute | solution.py:594
  22.5 1.9 %collective-permute-start.12 = (bf16[16,3840]{1,0:T(8,128)(2,1)S(1)}, bf16[16,3840]{1,0:T(8,128)(2,1)S(1)}, u32[]{:S(2)}, u32[]{:S(2)}) collective-permute-start(bf16[16,3840]{1,0:T(8,128)(2,1)S(1)} %finish_forward_2.1.refs_4_), channel_id=1, source_target_pairs={{0,12},{1,13},{2,14},{3,15},{4,8},{5,9},{6,10},{7,11},{8,20},{9,21... | collective-permute-start | bytes 368648 | tf_op jit(solution)/shard_map/ppermute | solution.py:594
  25.0 2.8 %collective-permute-start.13 = (bf16[16,3840]{1,0:T(8,128)(2,1)S(1)}, bf16[16,3840]{1,0:T(8,128)(2,1)S(1)}, u32[]{:S(2)}, u32[]{:S(2)}) collective-permute-start(bf16[16,3840]{1,0:T(8,128)(2,1)S(1)} %finish_forward_3.1), channel_id=1, source_target_pairs={{0,14},{1,15},{2,12},{3,13},{4,10},{5,11},{6,8},{7,9},{8,22},{9,23... | collective-permute-start | bytes 368648 | tf_op jit(solution)/shard_map/ppermute | solution.py:594
  27.8 1.5 %experts_backward.1 = (bf16[80,3712]{1,0:T(8,128)(2,1)S(1)}, bf16[80,3712]{1,0:T(8,128)(2,1)S(1)}) custom-call(bf16[80,3584]{1,0:T(8,128)(2,1)S(1)} %get-tuple-element.56.refs_4_.refs_0_, bf16[80,3584]{1,0:T(8,128)(2,1)S(1)} %collective-permute-done.9.refs_1_, bf16[160,512]{1,0:T(8,128)(2,1)S(1)} %get-tuple-element.51.refs_0_.refs_5_.refs_2_, ...), custom_call_target="tpu_custom_call" | custom-call | flops 100000000 | bytes 1000 | tf_op jit(solution)/shard_map/experts_backward/pallas_call | solution.py:41
  29.3 0.3 collective-permute-start.10
  29.5 0.4 act_gates.1.refs_7_
  29.9 1.4 %collective-permute-done.10.refs_9_ = bf16[80,3712]{1,0:T(8,128)(2,1)S(1)} collective-permute-done((bf16[80,3712]{1,0:T(8,128)(2,1)S(1)}, bf16[80,3712]{1,0:T(8,128)(2,1)S(1)}, u32[]{:S(2)}, u32[]{:S(2)}) %collective-permute-start.10) | collective-permute-done | bytes 593952 | tf_op jit(solution)/shard_map/ppermute | solution.py:583
  31.3 0.7 %finish_backward.1 = (bf16[16,3840]{1,0:T(8,128)(2,1)S(1)}, bf16[16,3840]{1,0:T(8,128)(2,1)S(1)}, bf16[16,3840]{1,0:T(8,128)(2,1)S(1)}, bf16[16,3840]{1,0:T(8,128)(2,1)S(1)}) custom-call(bf16[32,3840]{1,0:T(8,128)(2,1)S(1)} %get-tuple-element.45.refs_1_.refs_0_, bf16[32,3840]{1,0:T(8,128)(2,1)S(1)} %collective-permute-done.6.refs_1_, ...), custom_call_target="tpu_custom_call" | custom-call | flops 100000000 | bytes 1000 | tf_op jit(solution)/shard_map/finish_backward/pallas_call | solution.py:41
  32.0 2.6 %collective-permute-start.15 = (bf16[16,3840]{1,0:T(8,128)(2,1)S(1)}, bf16[16,3840]{1,0:T(8,128)(2,1)S(1)}, u32[]{:S(2)}, u32[]{:S(2)}) collective-permute-start(bf16[16,3840]{1,0:T(8,128)(2,1)S(1)} %get-tuple-element.63), channel_id=1, source_target_pairs={{0,26},{1,27},{2,24},{3,25},{4,30},{5,31},{6,28},{7,29},{8,2},{9,3... | collective-permute-start | bytes 368648 | tf_op jit(solution)/shard_map/ppermute | solution.py:594
  34.7 1.5 %collective-permute-start.16 = (bf16[16,3840]{1,0:T(8,128)(2,1)S(1)}, bf16[16,3840]{1,0:T(8,128)(2,1)S(1)}, u32[]{:S(2)}, u32[]{:S(2)}) collective-permute-start(bf16[16,3840]{1,0:T(8,128)(2,1)S(1)} %get-tuple-element.64), channel_id=1, source_target_pairs={{0,28},{1,29},{2,30},{3,31},{4,24},{5,25},{6,26},{7,27},{8,4},{9,5... | collective-permute-start | bytes 368648 | tf_op jit(solution)/shard_map/ppermute | solution.py:594
  36.2 1.3 %collective-permute-start.14 = (bf16[16,3840]{1,0:T(8,128)(2,1)S(1)}, bf16[16,3840]{1,0:T(8,128)(2,1)S(1)}, u32[]{:S(2)}, u32[]{:S(2)}) collective-permute-start(bf16[16,3840]{1,0:T(8,128)(2,1)S(1)} %get-tuple-element.62.refs_0_), channel_id=1, source_target_pairs={{0,30},{1,31},{2,28},{3,29},{4,26},{5,27},{6,24},{7,25},{8,6},{9,7... | collective-permute-start | bytes 368648 | tf_op jit(solution)/shard_map/ppermute | solution.py:594
  37.5 1.4 %collective-permute-start.17 = (bf16[16,3840]{1,0:T(8,128)(2,1)S(1)}, bf16[16,3840]{1,0:T(8,128)(2,1)S(1)}, u32[]{:S(2)}, u32[]{:S(2)}) collective-permute-start(bf16[16,3840]{1,0:T(8,128)(2,1)S(1)} %get-tuple-element.65), channel_id=1, source_target_pairs={{0,24},{1,25},{2,26},{3,27},{4,28},{5,29},{6,30},{7,31},{8,0},{9,1... | collective-permute-start | bytes 368648 | tf_op jit(solution)/shard_map/ppermute | solution.py:594
  38.9 0.9 %collective-permute-start.11 = (bf16[16,3840]{1,0:T(8,128)(2,1)S(1)}, bf16[16,3840]{1,0:T(8,128)(2,1)S(1)}, u32[]{:S(2)}, u32[]{:S(2)}) collective-permute-start(bf16[16,3840]{1,0:T(8,128)(2,1)S(1)} %lower_chunk.1), channel_id=1, source_target_pairs={{0,2},{1,3},{2,0},{3,1},{4,6},{5,7},{6,4},{7,5},{8,10},{9,11},{10,... | collective-permute-start | bytes 368648 | tf_op jit(solution)/shard_map/ppermute | solution.py:573
  39.8 0.3 forward_rows_early.1.refs_1_
  40.1 5.7 %collective-permute-done.11.refs_0_ = bf16[16,3840]{1,0:T(8,128)(2,1)S(1)} collective-permute-done((bf16[16,3840]{1,0:T(8,128)(2,1)S(1)}, bf16[16,3840]{1,0:T(8,128)(2,1)S(1)}, u32[]{:S(2)}, u32[]{:S(2)}) %collective-permute-start.11) | collective-permute-done | bytes 122912 | tf_op jit(solution)/shard_map/ppermute | solution.py:573
  45.9 1.0 %forward_rows.1 = bf16[64,3584]{1,0:T(8,128)(2,1)} custom-call(bf16[16,3840]{1,0:T(8,128)(2,1)S(1)} %collective-permute-done.11.refs_0_, bf16[64,3584]{1,0:T(8,128)(2,1)S(1)} %forward_rows_early.1.refs_1_), custom_call_target="tpu_custom_call" | custom-call | flops 100000000 | bytes 1000 | tf_op jit(solution)/shard_map/forward_rows/pallas_call | solution.py:41
  46.9 1.0 %backward_rows.1 = bf16[64,3584]{1,0:T(8,128)(2,1)} custom-call(bf16[16,3840]{1,0:T(8,128)(2,1)S(1)} %collective-permute-done.14.refs_0_, bf16[16,3840]{1,0:T(8,128)(2,1)S(1)} %collective-permute-done.15.refs_1_, bf16[16,3840]{1,0:T(8,128)(2,1)S(1)} %collective-permute-done.16.refs_2_, bf16[16,3840]{1,0:T(8,128)(2,1)S(1)} %collective-permute-done.17.refs_3_), custom_call_target="tpu_custom_call" | custom-call | flops 100000000 | bytes 1000 | tf_op jit(solution)/shard_map/backward_rows/pallas_call | solution.py:41
  (29 shorter events, 1.4 us)
Async XLA Ops:
  2.8 9.1 %collective-permute-start = (bf16[16,3840]{1,0:T(8,128)(2,1)S(1)}, bf16[16,3840]{1,0:T(8,128)(2,1)S(1)}, u32[]{:S(2)}, u32[]{:S(2)}) collective-permute-start(bf16[16,3840]{1,0:T(8,128)(2,1)S(1)} %get-tuple-element.35), channel_id=1, source_target_pairs={{0,2},{1,3},{2,0},{3,1},{4,6},{5,7},{6,4},{7,5},{8,10},{9,11},{10,... | collective-permute-start | bytes 368648 | tf_op jit(solution)/shard_map/ppermute | solution.py:573
  5.8 8.2 %collective-permute-start.1 = (bf16[16,3840]{1,0:T(8,128)(2,1)S(1)}, bf16[16,3840]{1,0:T(8,128)(2,1)S(1)}, u32[]{:S(2)}, u32[]{:S(2)}) collective-permute-start(bf16[16,3840]{1,0:T(8,128)(2,1)S(1)} %get-tuple-element.36), channel_id=1, source_target_pairs={{0,4},{1,5},{2,6},{3,7},{4,0},{5,1},{6,2},{7,3},{8,12},{9,13},{10,... | collective-permute-start | bytes 368648 | tf_op jit(solution)/shard_map/ppermute | solution.py:573
  7.3 7.2 %collective-permute-start.2 = (bf16[16,3840]{1,0:T(8,128)(2,1)S(1)}, bf16[16,3840]{1,0:T(8,128)(2,1)S(1)}, u32[]{:S(2)}, u32[]{:S(2)}) collective-permute-start(bf16[16,3840]{1,0:T(8,128)(2,1)S(1)} %get-tuple-element.37), channel_id=1, source_target_pairs={{0,6},{1,7},{2,4},{3,5},{4,2},{5,3},{6,0},{7,1},{8,14},{9,15},{10,... | collective-permute-start | bytes 368648 | tf_op jit(solution)/shard_map/ppermute | solution.py:573
  7.3 5.6 %copy-start = (bf16[1,3584,512]{2,1,0:T(8,128)(2,1)S(1)}, bf16[1,3584,512]{2,1,0:T(8,128)(2,1)}, u32[]{:S(2)}) copy-start(bf16[1,3584,512]{2,1,0:T(8,128)(2,1)} %weights_ref.3) | copy-start | bytes 11010052
  7.3 5.6 %copy-start.1 = (bf16[1,512,3584]{2,1,0:T(8,128)(2,1)S(1)}, bf16[1,512,3584]{2,1,0:T(8,128)(2,1)}, u32[]{:S(2)}) copy-start(bf16[1,512,3584]{2,1,0:T(8,128)(2,1)} %refs_3_.1) | copy-start | bytes 11010052
  8.3 16.1 %collective-permute-start.6 = (bf16[32,3840]{1,0:T(8,128)(2,1)S(1)}, bf16[32,3840]{1,0:T(8,128)(2,1)S(1)}, u32[]{:S(2)}, u32[]{:S(2)}) collective-permute-start(bf16[32,3840]{1,0:T(8,128)(2,1)S(1)} %get-tuple-element.52), channel_id=1, source_target_pairs={{0,2},{1,3},{2,0},{3,1},{4,6},{5,7},{6,4},{7,5},{8,10},{9,11},{10,... | collective-permute-start | bytes 737288 | tf_op jit(solution)/shard_map/ppermute | solution.py:573
  10.3 14.1 %collective-permute-start.7 = (bf16[32,3840]{1,0:T(8,128)(2,1)S(1)}, bf16[32,3840]{1,0:T(8,128)(2,1)S(1)}, u32[]{:S(2)}, u32[]{:S(2)}) collective-permute-start(bf16[32,3840]{1,0:T(8,128)(2,1)S(1)} %get-tuple-element.53), channel_id=1, source_target_pairs={{0,4},{1,5},{2,6},{3,7},{4,0},{5,1},{6,2},{7,3},{8,12},{9,13},{10,... | collective-permute-start | bytes 737288 | tf_op jit(solution)/shard_map/ppermute | solution.py:573
  11.9 12.5 %collective-permute-start.8 = (bf16[32,3840]{1,0:T(8,128)(2,1)S(1)}, bf16[32,3840]{1,0:T(8,128)(2,1)S(1)}, u32[]{:S(2)}, u32[]{:S(2)}) collective-permute-start(bf16[32,3840]{1,0:T(8,128)(2,1)S(1)} %get-tuple-element.54), channel_id=1, source_target_pairs={{0,6},{1,7},{2,4},{3,5},{4,2},{5,3},{6,0},{7,1},{8,14},{9,15},{10,... | collective-permute-start | bytes 737288 | tf_op jit(solution)/shard_map/ppermute | solution.py:573
  15.0 2.0 %collective-permute-start.3 = (bf16[80,3584]{1,0:T(8,128)(2,1)S(1)}, bf16[80,3584]{1,0:T(8,128)(2,1)S(1)}, u32[]{:S(2)}, u32[]{:S(2)}) collective-permute-start(bf16[80,3584]{1,0:T(8,128)(2,1)S(1)} %get-tuple-element.47.refs_0_), channel_id=1, source_target_pairs={{0,1},{1,0},{2,3},{3,2},{4,5},{5,4},{6,7},{7,6},{8,9},{9,8},{10,11... | collective-permute-start | bytes 1720328 | tf_op jit(solution)/shard_map/ppermute | solution.py:583
  18.5 2.0 %collective-permute-start.4 = (bf16[80,3584]{1,0:T(8,128)(2,1)S(1)}, bf16[80,3584]{1,0:T(8,128)(2,1)S(1)}, u32[]{:S(2)}, u32[]{:S(2)}) collective-permute-start(bf16[80,3584]{1,0:T(8,128)(2,1)S(1)} %get-tuple-element.50), channel_id=1, source_target_pairs={{0,1},{1,0},{2,3},{3,2},{4,5},{5,4},{6,7},{7,6},{8,9},{9,8},{10,11... | collective-permute-start | bytes 1720328 | tf_op jit(solution)/shard_map/ppermute | solution.py:583
  20.7 15.4 %collective-permute-start.5 = (bf16[32,3840]{1,0:T(8,128)(2,1)S(1)}, bf16[32,3840]{1,0:T(8,128)(2,1)S(1)}, u32[]{:S(2)}, u32[]{:S(2)}) collective-permute-start(bf16[32,3840]{1,0:T(8,128)(2,1)S(1)} %finish_forward_01.1.refs_6_), channel_id=1, source_target_pairs={{0,8},{1,9},{2,10},{3,11},{4,12},{5,13},{6,14},{7,15},{8,16},{9,17... | collective-permute-start | bytes 737288 | tf_op jit(solution)/shard_map/ppermute | solution.py:594
  22.5 15.0 %collective-permute-start.12 = (bf16[16,3840]{1,0:T(8,128)(2,1)S(1)}, bf16[16,3840]{1,0:T(8,128)(2,1)S(1)}, u32[]{:S(2)}, u32[]{:S(2)}) collective-permute-start(bf16[16,3840]{1,0:T(8,128)(2,1)S(1)} %finish_forward_2.1.refs_4_), channel_id=1, source_target_pairs={{0,12},{1,13},{2,14},{3,15},{4,8},{5,9},{6,10},{7,11},{8,20},{9,21... | collective-permute-start | bytes 368648 | tf_op jit(solution)/shard_map/ppermute | solution.py:594
  24.5 3.3 %collective-permute-start.9 = (bf16[80,3584]{1,0:T(8,128)(2,1)S(1)}, bf16[80,3584]{1,0:T(8,128)(2,1)S(1)}, u32[]{:S(2)}, u32[]{:S(2)}) collective-permute-start(bf16[80,3584]{1,0:T(8,128)(2,1)S(1)} %get-tuple-element.56.refs_4_.refs_0_), channel_id=1, source_target_pairs={{0,1},{1,0},{2,3},{3,2},{4,5},{5,4},{6,7},{7,6},{8,9},{9,8},{10,11... | collective-permute-start | bytes 1720328 | tf_op jit(solution)/shard_map/ppermute | solution.py:583
  25.0 13.9 %collective-permute-start.13 = (bf16[16,3840]{1,0:T(8,128)(2,1)S(1)}, bf16[16,3840]{1,0:T(8,128)(2,1)S(1)}, u32[]{:S(2)}, u32[]{:S(2)}) collective-permute-start(bf16[16,3840]{1,0:T(8,128)(2,1)S(1)} %finish_forward_3.1), channel_id=1, source_target_pairs={{0,14},{1,15},{2,12},{3,13},{4,10},{5,11},{6,8},{7,9},{8,22},{9,23... | collective-permute-start | bytes 368648 | tf_op jit(solution)/shard_map/ppermute | solution.py:594
  29.3 2.1 %collective-permute-start.10 = (bf16[80,3712]{1,0:T(8,128)(2,1)S(1)}, bf16[80,3712]{1,0:T(8,128)(2,1)S(1)}, u32[]{:S(2)}, u32[]{:S(2)}) collective-permute-start(bf16[80,3712]{1,0:T(8,128)(2,1)S(1)} %get-tuple-element.61), channel_id=1, source_target_pairs={{0,1},{1,0},{2,3},{3,2},{4,5},{5,4},{6,7},{7,6},{8,9},{9,8},{10,11... | collective-permute-start | bytes 1781768 | tf_op jit(solution)/shard_map/ppermute | solution.py:583
  32.0 14.8 %collective-permute-start.15 = (bf16[16,3840]{1,0:T(8,128)(2,1)S(1)}, bf16[16,3840]{1,0:T(8,128)(2,1)S(1)}, u32[]{:S(2)}, u32[]{:S(2)}) collective-permute-start(bf16[16,3840]{1,0:T(8,128)(2,1)S(1)} %get-tuple-element.63), channel_id=1, source_target_pairs={{0,26},{1,27},{2,24},{3,25},{4,30},{5,31},{6,28},{7,29},{8,2},{9,3... | collective-permute-start | bytes 368648 | tf_op jit(solution)/shard_map/ppermute | solution.py:594
  34.7 12.2 %collective-permute-start.16 = (bf16[16,3840]{1,0:T(8,128)(2,1)S(1)}, bf16[16,3840]{1,0:T(8,128)(2,1)S(1)}, u32[]{:S(2)}, u32[]{:S(2)}) collective-permute-start(bf16[16,3840]{1,0:T(8,128)(2,1)S(1)} %get-tuple-element.64), channel_id=1, source_target_pairs={{0,28},{1,29},{2,30},{3,31},{4,24},{5,25},{6,26},{7,27},{8,4},{9,5... | collective-permute-start | bytes 368648 | tf_op jit(solution)/shard_map/ppermute | solution.py:594
  36.2 10.7 %collective-permute-start.14 = (bf16[16,3840]{1,0:T(8,128)(2,1)S(1)}, bf16[16,3840]{1,0:T(8,128)(2,1)S(1)}, u32[]{:S(2)}, u32[]{:S(2)}) collective-permute-start(bf16[16,3840]{1,0:T(8,128)(2,1)S(1)} %get-tuple-element.62.refs_0_), channel_id=1, source_target_pairs={{0,30},{1,31},{2,28},{3,29},{4,26},{5,27},{6,24},{7,25},{8,6},{9,7... | collective-permute-start | bytes 368648 | tf_op jit(solution)/shard_map/ppermute | solution.py:594
  37.5 9.4 %collective-permute-start.17 = (bf16[16,3840]{1,0:T(8,128)(2,1)S(1)}, bf16[16,3840]{1,0:T(8,128)(2,1)S(1)}, u32[]{:S(2)}, u32[]{:S(2)}) collective-permute-start(bf16[16,3840]{1,0:T(8,128)(2,1)S(1)} %get-tuple-element.65), channel_id=1, source_target_pairs={{0,24},{1,25},{2,26},{3,27},{4,28},{5,29},{6,30},{7,31},{8,0},{9,1... | collective-permute-start | bytes 368648 | tf_op jit(solution)/shard_map/ppermute | solution.py:594
  38.9 7.0 %collective-permute-start.11 = (bf16[16,3840]{1,0:T(8,128)(2,1)S(1)}, bf16[16,3840]{1,0:T(8,128)(2,1)S(1)}, u32[]{:S(2)}, u32[]{:S(2)}) collective-permute-start(bf16[16,3840]{1,0:T(8,128)(2,1)S(1)} %lower_chunk.1), channel_id=1, source_target_pairs={{0,2},{1,3},{2,0},{3,1},{4,6},{5,7},{6,4},{7,5},{8,10},{9,11},{10,... | collective-permute-start | bytes 368648 | tf_op jit(solution)/shard_map/ppermute | solution.py:573

commit v14 on v13

--- a/solution.py
+++ b/solution.py
@@ -28,7 +28,6 @@
     "saved_terms": 15,
     "act_norms": 15,
     "act_gates": 15,
-    "forward_rows_early": 15,
 }
 
 
@@ -71,7 +70,7 @@
         self.pieces = width // fold
         self.wide = width + fold
         self.rows = tokens + 16
-        self.order = [experts - 1, *range(1, experts - 1), 0]
+        self.order = [*range(experts - 1, 1, -1), 0, 1]
         assert self.main == 16 and self.pieces <= 14 and width % fold == 0
         assert experts <= 8 and experts & (experts - 1) == 0 and self.split & (self.split - 1) == 0
 
@@ -537,34 +536,46 @@
     return call(body, places, shape((z.tokens, z.width)), [], 8, name)(*chunks.values(), *after)
 
 
-def order_rows(z, chunks, others, name):
-    ks, count = list(chunks), len(chunks)
+def order_rows(z, outputs, name):
     steps = 7 if z.pieces % 7 == 0 else z.pieces
-
-    def body(*refs):
-        others, (out_any, out, sems) = refs[count:-3], refs[-3:]
+    arrays, layout = [], []
+    for chunks, others in outputs:
+        layout.append((len(arrays), list(chunks), len(others)))
+        arrays += [*chunks.values(), *others]
+    number = len(outputs)
+
+    def body(*refs):
+        inputs, anys = refs[: len(arrays)], refs[len(arrays) : len(arrays) + number]
+        outs, sems = refs[-1 - number : -1], refs[-1]
         copies = []
-        for i, (cols, rows) in enumerate(ordered_columns(z, dict(zip(ks, refs)))):
-            for other in others:
-                rows = rows + other[:, cols].astype(f32)
-            out[:, cols] = rows.astype(bf16)
-            if (i + 1) % (z.pieces // steps) == 0:
-                done = pl.ds((i + 1) * fold - z.width // steps, z.width // steps)
-                copy = pltpu.make_async_copy(out.at[:, done], out_any.at[:, done], sems.at[len(copies)])
-                copy.start()
-                copies.append(copy)
+        for n, (at, ks, more) in enumerate(layout):
+            chunks = dict(zip(ks, inputs[at : at + len(ks)]))
+            others = inputs[at + len(ks) : at + len(ks) + more]
+            for i, (cols, rows) in enumerate(ordered_columns(z, chunks)):
+                for other in others:
+                    rows = rows + other[:, cols].astype(f32)
+                outs[n][:, cols] = rows.astype(bf16)
+                if (i + 1) % (z.pieces // steps) == 0:
+                    width = z.width // steps
+                    done = pl.ds((i + 1) * fold - width, width)
+                    copy = pltpu.make_async_copy(
+                        outs[n].at[:, done], anys[n].at[:, done], sems.at[len(copies)]
+                    )
+                    copy.start()
+                    copies.append(copy)
         for copy in copies:
             copy.wait()
 
     return call(
         body,
-        "v" * (count + len(others)),
-        shape((z.tokens, z.width)),
-        [pltpu.VMEM((z.tokens, z.width), bf16), pltpu.SemaphoreType.DMA((steps,))],
+        "v" * len(arrays),
+        [shape((z.tokens, z.width))] * number,
+        [pltpu.VMEM((z.tokens, z.width), bf16)] * number
+        + [pltpu.SemaphoreType.DMA((number * steps,))],
         8,
         name,
-        spaces["a"],
-    )(*chunks.values(), *others)
+        [spaces["a"]] * number,
+    )(*arrays)
 
 
 def permute_blocks(z, arrays, k):
@@ -639,15 +650,16 @@
     affinity = act_gates(z, bwd_own, act_last, inv, vectors, [bwd_parts[0]])
     fwd_done = [got2, got3]
     bwd_parts = [bwd_parts[0]] + [to_core(z, bwd_parts[m], m) for m in others]
+    order = [z.order[-1], *z.order[:-1]]
     bwd_out = finish_backward(
-        z, z.order, bwd_own, [grad_last, act_last], [inv, affinity], bwd_parts, vectors, []
+        z, order, bwd_own, [grad_last, act_last], [inv, affinity], bwd_parts, vectors, []
     )
     (relayed,) = permute_blocks(z, [lower_chunk(z, got, [bwd_out[0]])], 1)
-    bwd_done = {k: to_section(z, out, k, -1) for k, out in zip(z.order, bwd_out)}
+    bwd_done = {k: to_section(z, out, k, -1) for k, out in zip(order, bwd_out)}
 
     early = some_rows(z, {0: got, 2: got2, 3: got3}, [], "forward_rows_early")
-    fwd_next = order_rows(z, {1: relayed}, [early], "forward_rows")
-    bwd_next = order_rows(z, {k: bwd_done[k] for k in z.order}, [], "backward_rows")
+    outputs = [({1: relayed}, [early]), ({k: bwd_done[k] for k in z.order}, [])]
+    fwd_next, bwd_next = order_rows(z, outputs, "all_rows")
     return (fwd_next, bwd_next)
 
 

time: 48.1 us -> 48.7 us (1.012)
  waiting for transfers between devices: 8.7 us -> 10.1 us
  Pallas kernels: 14.4 us -> 13.6 us
    ppermute x7, waiting for transfers between devices: 0.02 us -> 7.21 us  [to_section(): return lax.ppermute(chunk, ('pp', 'ep'), pairs)]
    ppermute x7, waiting for transfers between devices: 6.27 us -> 0.52 us  [permute_blocks(): return [lax.ppermute(array, 'ep', pairs) for array in arrays]]
    pallas_call x20 -> x19, Pallas kernels: 14.4 us -> 13.6 us  [run(): return kernel(*arrays)]
  transfers between devices with their start and end apart: 18 -> 18, of which waited for: 5 -> 8; matrix products, arithmetic and copies ran while one was open for 0% -> 0% of each run, Pallas kernels for 24% -> 21%
where the time goes in v14:
time: 48.7 us; the launch traced here: 48.5 us
  starting transfers between devices  23.9 us (49%)
  Pallas kernels  13.6 us (28%)
  waiting for transfers between devices  10.1 us (21%)
  between operations  0.78 us (2%)
    pallas_call x19, Pallas kernels, run(): return kernel(*arrays)  13.6 us
    ppermute x7, starting transfers between devices, to_section(): return lax.ppermute(chunk, ('pp', 'ep'), pairs)  13.5 us
    ppermute x7, starting transfers between devices, permute_blocks(): return [lax.ppermute(array, 'ep', pairs) for array in arrays]  9.77 us
    ppermute x7, waiting for transfers between devices, to_section(): return lax.ppermute(chunk, ('pp', 'ep'), pairs)  7.21 us
    ppermute x4, waiting for transfers between devices, to_core(): return lax.ppermute(array, 'ep', pairs)  2.41 us
  transfers between devices with their start and end apart: 18, of which 8 were waited for; matrix products, arithmetic and copies ran while one was open for 0% of the time, Pallas kernels for 21%

profile of v14, /device:TPU:0, one launch (start us, length us, event | category | flops | bytes accessed | tf_op | source)
XLA Modules:
  0.0 48.5 jit_solution(3007334648825359391)
XLA Ops:
  0.7 2.0 %forward_chunks.1 = (bf16[16,3840]{1,0:T(8,128)(2,1)S(1)}, bf16[16,3840]{1,0:T(8,128)(2,1)S(1)}, bf16[16,3840]{1,0:T(8,128)(2,1)S(1)}, bf16[16,3840]{1,0:T(8,128...) custom-call(s32[2]{0:T(128)S(1)} %pad_add_fusion.where, ...), custom_call_target="tpu_custom_call" | custom-call | flops 100000000 | bytes 1000 | tf_op jit(solution)/shard_map/forward_chunks/pallas_call | solution.py:40
  2.8 3.0 %collective-permute-start = (bf16[16,3840]{1,0:T(8,128)(2,1)S(1)}, bf16[16,3840]{1,0:T(8,128)(2,1)S(1)}, u32[]{:S(2)}, u32[]{:S(2)}) collective-permute-start(bf16[16,3840]{1,0:T(8,128)(2,1)S(1)} %get-tuple-element.35), channel_id=1, source_target_pairs={{0,2},{1,3},{2,0},{3,1},{4,6},{5,7},{6,4},{7,5},{8,10},{9,11},{10,... | collective-permute-start | bytes 368648 | tf_op jit(solution)/shard_map/ppermute | solution.py:584
  5.8 1.5 %collective-permute-start.1 = (bf16[16,3840]{1,0:T(8,128)(2,1)S(1)}, bf16[16,3840]{1,0:T(8,128)(2,1)S(1)}, u32[]{:S(2)}, u32[]{:S(2)}) collective-permute-start(bf16[16,3840]{1,0:T(8,128)(2,1)S(1)} %get-tuple-element.36), channel_id=1, source_target_pairs={{0,4},{1,5},{2,6},{3,7},{4,0},{5,1},{6,2},{7,3},{8,12},{9,13},{10,... | collective-permute-start | bytes 368648 | tf_op jit(solution)/shard_map/ppermute | solution.py:584
  7.3 1.0 %backward_chunks.1 = (bf16[32,3840]{1,0:T(8,128)(2,1)S(1)}, bf16[32,3840]{1,0:T(8,128)(2,1)S(1)}, bf16[32,3840]{1,0:T(8,128)(2,1)S(1)}, bf16[32,3840]{1,0:T(8,128)(2,1)S(1)}, f32[8,3584]{1,0:T(8,128)S(1)}) custom-call(s32[2]{0:T(128)S(1)} %pad_add_fusion.where, bf16[80,64]{1,0:T(8,128)(2,1)S(1)} %get-tuple-element.38.selector, ...), custom_call_target="tpu_custom_call" | custom-call | flops 10000000000 | bytes 1000 | tf_op jit(solution)/shard_map/backward_chunks/pallas_call | solution.py:40
  8.3 2.0 %collective-permute-start.6 = (bf16[32,3840]{1,0:T(8,128)(2,1)S(1)}, bf16[32,3840]{1,0:T(8,128)(2,1)S(1)}, u32[]{:S(2)}, u32[]{:S(2)}) collective-permute-start(bf16[32,3840]{1,0:T(8,128)(2,1)S(1)} %get-tuple-element.52), channel_id=1, source_target_pairs={{0,2},{1,3},{2,0},{3,1},{4,6},{5,7},{6,4},{7,5},{8,10},{9,11},{10,... | collective-permute-start | bytes 737288 | tf_op jit(solution)/shard_map/ppermute | solution.py:584
  10.3 1.5 %collective-permute-start.7 = (bf16[32,3840]{1,0:T(8,128)(2,1)S(1)}, bf16[32,3840]{1,0:T(8,128)(2,1)S(1)}, u32[]{:S(2)}, u32[]{:S(2)}) collective-permute-start(bf16[32,3840]{1,0:T(8,128)(2,1)S(1)} %get-tuple-element.53), channel_id=1, source_target_pairs={{0,4},{1,5},{2,6},{3,7},{4,0},{5,1},{6,2},{7,3},{8,12},{9,13},{10,... | collective-permute-start | bytes 737288 | tf_op jit(solution)/shard_map/ppermute | solution.py:584
  11.9 1.1 %collective-permute-start.8 = (bf16[32,3840]{1,0:T(8,128)(2,1)S(1)}, bf16[32,3840]{1,0:T(8,128)(2,1)S(1)}, u32[]{:S(2)}, u32[]{:S(2)}) collective-permute-start(bf16[32,3840]{1,0:T(8,128)(2,1)S(1)} %get-tuple-element.54), channel_id=1, source_target_pairs={{0,6},{1,7},{2,4},{3,5},{4,2},{5,3},{6,0},{7,1},{8,14},{9,15},{10,... | collective-permute-start | bytes 737288 | tf_op jit(solution)/shard_map/ppermute | solution.py:584
  13.0 1.0 %turned_down.1.refs_5_ = bf16[3584,512]{1,0:T(8,128)(2,1)S(1)} custom-call(bf16[1,512,3584]{2,1,0:T(8,128)(2,1)S(1)} %copy-done.1, bf16[1,3584,512]{2,1,0:T(8,128)(2,1)S(1)} %copy-done, bf16[32,3840]{1,0:T(8,128)(2,1)S(1)} %get-tuple-element.45.refs_1_.refs_0_, bf16[16,3840]{1,0:T(8,128)(2,1)S(1)} %collective-permute-done.refs_2_.refs_1_), custom_call_target="tpu_custom_call" | custom-call | flops 100000000 | bytes 1000 | tf_op jit(solution)/shard_map/turned_down/pallas_call | solution.py:40
  14.0 0.5 %collective-permute-done.2.refs_3_.refs_0_ = bf16[16,3840]{1,0:T(8,128)(2,1)S(1)} collective-permute-done((bf16[16,3840]{1,0:T(8,128)(2,1)S(1)}, bf16[16,3840]{1,0:T(8,128)(2,1)S(1)}, u32[]{:S(2)}, u32[]{:S(2)}) %collective-permute-start.2) | collective-permute-done | bytes 122912 | tf_op jit(solution)/shard_map/ppermute | solution.py:584
  14.5 0.5 %normed_rows.1 = (bf16[80,3584]{1,0:T(8,128)(2,1)S(1)}, f32[80,128]{1,0:T(8,128)S(1)}, f32[16,3584]{1,0:T(8,128)S(1)}) custom-call(bf16[16,3840]{1,0:T(8,128)(2,1)S(1)} %get-tuple-element.34.refs_0_, bf16[16,3840]{1,0:T(8,128)(2,1)S(1)} %collective-permute-done.refs_2_.refs_1_, bf16[16,3840]{1,0:T(8,128)(2,1)S(1)} %collective-permute-done.1.refs_2_.refs_0_, ...), custom_call_target="tpu_custom_call" | custom-call | flops 100000000 | bytes 1000 | tf_op jit(solution)/shard_map/normed_rows/pallas_call | solution.py:40
  15.0 1.6 %saved_rows.1.refs_4_.ordered_ref = f32[160,512]{1,0:T(8,128)S(1)} custom-call(s32[2]{0:T(128)S(1)} %pad_add_fusion.where, bf16[1,1,136,512]{3,2,1,0:T(8,128)(2,1)} %saved_any.1, f32[80,128]{1,0:T(8,128)S(1)} %get-tuple-element.48.refs_0_.refs_5_.refs_4_), custom_call_target="tpu_custom_call" | custom-call | flops 15000000512 | bytes 1000 | tf_op jit(solution)/shard_map/saved_rows/pallas_call | solution.py:40
  16.7 0.3 collective-permute-done.3.refs_1_
  17.0 1.5 %experts_forward.1 = (bf16[80,3584]{1,0:T(8,128)(2,1)S(1)}, bf16[80,3584]{1,0:T(8,128)(2,1)S(1)}) custom-call(bf16[80,3584]{1,0:T(8,128)(2,1)S(1)} %get-tuple-element.47.refs_0_, bf16[80,3584]{1,0:T(8,128)(2,1)S(1)} %collective-permute-done.3.refs_1_, bf16[1,3584,512]{2,1,0:T(8,128)(2,1)S(1)} %copy-done, bf16[1,512,3584]{2,1,0:T(8,128)(2,1)S(1)} %copy-done.1, ...), custom_call_target="tpu_custom_call" | custom-call | flops 100000000 | bytes 1000 | tf_op jit(solution)/shard_map/experts_forward/pallas_call | solution.py:40
  18.8 1.0 %turned_gate.1.refs_6_.refs_4_ = bf16[512,3584]{1,0:T(8,128)(2,1)S(1)} custom-call(bf16[1,3584,512]{2,1,0:T(8,128)(2,1)S(1)} %copy-done, bf16[160,512]{1,0:T(8,128)(2,1)S(1)} %get-tuple-element.51.refs_0_.refs_5_.refs_2_), custom_call_target="tpu_custom_call" | custom-call | flops 100000000 | bytes 1000 | tf_op jit(solution)/shard_map/turned_gate/pallas_call | solution.py:40
  19.8 0.7 %collective-permute-done.4.refs_4_.refs_3_ = bf16[80,3584]{1,0:T(8,128)(2,1)S(1)} collective-permute-done((bf16[80,3584]{1,0:T(8,128)(2,1)S(1)}, bf16[80,3584]{1,0:T(8,128)(2,1)S(1)}, u32[]{:S(2)}, u32[]{:S(2)}) %collective-permute-start.4) | collective-permute-done | bytes 573472 | tf_op jit(solution)/shard_map/ppermute | solution.py:594
  20.7 1.6 %collective-permute-start.5 = (bf16[32,3840]{1,0:T(8,128)(2,1)S(1)}, bf16[32,3840]{1,0:T(8,128)(2,1)S(1)}, u32[]{:S(2)}, u32[]{:S(2)}) collective-permute-start(bf16[32,3840]{1,0:T(8,128)(2,1)S(1)} %finish_forward_01.1.refs_6_), channel_id=1, source_target_pairs={{0,8},{1,9},{2,10},{3,11},{4,12},{5,13},{6,14},{7,15},{8,16},{9,17... | collective-permute-start | bytes 737288 | tf_op jit(solution)/shard_map/ppermute | solution.py:605
  22.5 1.9 %collective-permute-start.12 = (bf16[16,3840]{1,0:T(8,128)(2,1)S(1)}, bf16[16,3840]{1,0:T(8,128)(2,1)S(1)}, u32[]{:S(2)}, u32[]{:S(2)}) collective-permute-start(bf16[16,3840]{1,0:T(8,128)(2,1)S(1)} %finish_forward_2.1.refs_4_), channel_id=1, source_target_pairs={{0,12},{1,13},{2,14},{3,15},{4,8},{5,9},{6,10},{7,11},{8,20},{9,21... | collective-permute-start | bytes 368648 | tf_op jit(solution)/shard_map/ppermute | solution.py:605
  25.0 2.8 %collective-permute-start.13 = (bf16[16,3840]{1,0:T(8,128)(2,1)S(1)}, bf16[16,3840]{1,0:T(8,128)(2,1)S(1)}, u32[]{:S(2)}, u32[]{:S(2)}) collective-permute-start(bf16[16,3840]{1,0:T(8,128)(2,1)S(1)} %finish_forward_3.1), channel_id=1, source_target_pairs={{0,14},{1,15},{2,12},{3,13},{4,10},{5,11},{6,8},{7,9},{8,22},{9,23... | collective-permute-start | bytes 368648 | tf_op jit(solution)/shard_map/ppermute | solution.py:605
  27.8 1.5 %experts_backward.1 = (bf16[80,3712]{1,0:T(8,128)(2,1)S(1)}, bf16[80,3712]{1,0:T(8,128)(2,1)S(1)}) custom-call(bf16[80,3584]{1,0:T(8,128)(2,1)S(1)} %get-tuple-element.56.refs_4_.refs_0_, bf16[80,3584]{1,0:T(8,128)(2,1)S(1)} %collective-permute-done.9.refs_1_, bf16[160,512]{1,0:T(8,128)(2,1)S(1)} %get-tuple-element.51.refs_0_.refs_5_.refs_2_, ...), custom_call_target="tpu_custom_call" | custom-call | flops 100000000 | bytes 1000 | tf_op jit(solution)/shard_map/experts_backward/pallas_call | solution.py:40
  29.3 0.3 collective-permute-start.10
  29.6 0.4 act_gates.1.refs_7_
  29.9 1.4 %collective-permute-done.10.refs_9_ = bf16[80,3712]{1,0:T(8,128)(2,1)S(1)} collective-permute-done((bf16[80,3712]{1,0:T(8,128)(2,1)S(1)}, bf16[80,3712]{1,0:T(8,128)(2,1)S(1)}, u32[]{:S(2)}, u32[]{:S(2)}) %collective-permute-start.10) | collective-permute-done | bytes 593952 | tf_op jit(solution)/shard_map/ppermute | solution.py:594
  31.3 0.7 %finish_backward.1 = (bf16[16,3840]{1,0:T(8,128)(2,1)S(1)}, bf16[16,3840]{1,0:T(8,128)(2,1)S(1)}, bf16[16,3840]{1,0:T(8,128)(2,1)S(1)}, bf16[16,3840]{1,0:T(8,128)(2,1)S(1)}) custom-call(bf16[32,3840]{1,0:T(8,128)(2,1)S(1)} %get-tuple-element.45.refs_1_.refs_0_, bf16[32,3840]{1,0:T(8,128)(2,1)S(1)} %collective-permute-done.6.refs_1_, ...), custom_call_target="tpu_custom_call" | custom-call | flops 100000000 | bytes 1000 | tf_op jit(solution)/shard_map/finish_backward/pallas_call | solution.py:40
  32.0 2.9 %collective-permute-start.14 = (bf16[16,3840]{1,0:T(8,128)(2,1)S(1)}, bf16[16,3840]{1,0:T(8,128)(2,1)S(1)}, u32[]{:S(2)}, u32[]{:S(2)}) collective-permute-start(bf16[16,3840]{1,0:T(8,128)(2,1)S(1)} %get-tuple-element.63), channel_id=1, source_target_pairs={{0,30},{1,31},{2,28},{3,29},{4,26},{5,27},{6,24},{7,25},{8,6},{9,7... | collective-permute-start | bytes 368648 | tf_op jit(solution)/shard_map/ppermute | solution.py:605
  34.9 2.1 %collective-permute-start.15 = (bf16[16,3840]{1,0:T(8,128)(2,1)S(1)}, bf16[16,3840]{1,0:T(8,128)(2,1)S(1)}, u32[]{:S(2)}, u32[]{:S(2)}) collective-permute-start(bf16[16,3840]{1,0:T(8,128)(2,1)S(1)} %get-tuple-element.64), channel_id=1, source_target_pairs={{0,28},{1,29},{2,30},{3,31},{4,24},{5,25},{6,26},{7,27},{8,4},{9,5... | collective-permute-start | bytes 368648 | tf_op jit(solution)/shard_map/ppermute | solution.py:605
  37.0 0.5 collective-permute-start.16
  37.5 0.6 %collective-permute-start.11 = (bf16[16,3840]{1,0:T(8,128)(2,1)S(1)}, bf16[16,3840]{1,0:T(8,128)(2,1)S(1)}, u32[]{:S(2)}, u32[]{:S(2)}) collective-permute-start(bf16[16,3840]{1,0:T(8,128)(2,1)S(1)} %lower_chunk.1), channel_id=1, source_target_pairs={{0,2},{1,3},{2,0},{3,1},{4,6},{5,7},{6,4},{7,5},{8,10},{9,11},{10,... | collective-permute-start | bytes 368648 | tf_op jit(solution)/shard_map/ppermute | solution.py:584
  38.1 1.7 %collective-permute-start.17 = (bf16[16,3840]{1,0:T(8,128)(2,1)S(1)}, bf16[16,3840]{1,0:T(8,128)(2,1)S(1)}, u32[]{:S(2)}, u32[]{:S(2)}) collective-permute-start(bf16[16,3840]{1,0:T(8,128)(2,1)S(1)} %get-tuple-element.62.refs_0_), channel_id=1, source_target_pairs={{0,26},{1,27},{2,24},{3,25},{4,30},{5,31},{6,28},{7,29},{8,2},{9,3... | collective-permute-start | bytes 368648 | tf_op jit(solution)/shard_map/ppermute | solution.py:605
  40.2 2.3 %collective-permute-done.15.refs_3_ = bf16[16,3840]{1,0:T(8,128)(2,1)S(1)} collective-permute-done((bf16[16,3840]{1,0:T(8,128)(2,1)S(1)}, bf16[16,3840]{1,0:T(8,128)(2,1)S(1)}, u32[]{:S(2)}, u32[]{:S(2)}) %collective-permute-start.15) | collective-permute-done | bytes 122912 | tf_op jit(solution)/shard_map/ppermute | solution.py:605
  42.5 2.4 %collective-permute-done.16.refs_4_ = bf16[16,3840]{1,0:T(8,128)(2,1)S(1)} collective-permute-done((bf16[16,3840]{1,0:T(8,128)(2,1)S(1)}, bf16[16,3840]{1,0:T(8,128)(2,1)S(1)}, u32[]{:S(2)}, u32[]{:S(2)}) %collective-permute-start.16) | collective-permute-done | bytes 122912 | tf_op jit(solution)/shard_map/ppermute | solution.py:605
  45.0 2.4 %collective-permute-done.17.refs_5_ = bf16[16,3840]{1,0:T(8,128)(2,1)S(1)} collective-permute-done((bf16[16,3840]{1,0:T(8,128)(2,1)S(1)}, bf16[16,3840]{1,0:T(8,128)(2,1)S(1)}, u32[]{:S(2)}, u32[]{:S(2)}) %collective-permute-start.17) | collective-permute-done | bytes 122912 | tf_op jit(solution)/shard_map/ppermute | solution.py:605
  47.3 1.2 %all_rows.1 = (bf16[64,3584]{1,0:T(8,128)(2,1)}, bf16[64,3584]{1,0:T(8,128)(2,1)}) custom-call(bf16[16,3840]{1,0:T(8,128)(2,1)S(1)} %collective-permute-done.11.refs_0_, bf16[64,3584]{1,0:T(8,128)(2,1)S(1)} %forward_rows_early.1.refs_1_, bf16[16,3840]{1,0:T(8,128)(2,1)S(1)} %collective-permute-done.14.refs_2_, ...), custom_call_target="tpu_custom_call" | custom-call | flops 100000000 | bytes 1000 | tf_op jit(solution)/shard_map/all_rows/pallas_call | solution.py:40
  (28 shorter events, 1.8 us)
Async XLA Ops:
  2.8 9.1 %collective-permute-start = (bf16[16,3840]{1,0:T(8,128)(2,1)S(1)}, bf16[16,3840]{1,0:T(8,128)(2,1)S(1)}, u32[]{:S(2)}, u32[]{:S(2)}) collective-permute-start(bf16[16,3840]{1,0:T(8,128)(2,1)S(1)} %get-tuple-element.35), channel_id=1, source_target_pairs={{0,2},{1,3},{2,0},{3,1},{4,6},{5,7},{6,4},{7,5},{8,10},{9,11},{10,... | collective-permute-start | bytes 368648 | tf_op jit(solution)/shard_map/ppermute | solution.py:584
  5.8 8.2 %collective-permute-start.1 = (bf16[16,3840]{1,0:T(8,128)(2,1)S(1)}, bf16[16,3840]{1,0:T(8,128)(2,1)S(1)}, u32[]{:S(2)}, u32[]{:S(2)}) collective-permute-start(bf16[16,3840]{1,0:T(8,128)(2,1)S(1)} %get-tuple-element.36), channel_id=1, source_target_pairs={{0,4},{1,5},{2,6},{3,7},{4,0},{5,1},{6,2},{7,3},{8,12},{9,13},{10,... | collective-permute-start | bytes 368648 | tf_op jit(solution)/shard_map/ppermute | solution.py:584
  7.3 7.2 %collective-permute-start.2 = (bf16[16,3840]{1,0:T(8,128)(2,1)S(1)}, bf16[16,3840]{1,0:T(8,128)(2,1)S(1)}, u32[]{:S(2)}, u32[]{:S(2)}) collective-permute-start(bf16[16,3840]{1,0:T(8,128)(2,1)S(1)} %get-tuple-element.37), channel_id=1, source_target_pairs={{0,6},{1,7},{2,4},{3,5},{4,2},{5,3},{6,0},{7,1},{8,14},{9,15},{10,... | collective-permute-start | bytes 368648 | tf_op jit(solution)/shard_map/ppermute | solution.py:584
  7.3 5.6 %copy-start = (bf16[1,3584,512]{2,1,0:T(8,128)(2,1)S(1)}, bf16[1,3584,512]{2,1,0:T(8,128)(2,1)}, u32[]{:S(2)}) copy-start(bf16[1,3584,512]{2,1,0:T(8,128)(2,1)} %weights_ref.3) | copy-start | bytes 11010052
  7.3 5.6 %copy-start.1 = (bf16[1,512,3584]{2,1,0:T(8,128)(2,1)S(1)}, bf16[1,512,3584]{2,1,0:T(8,128)(2,1)}, u32[]{:S(2)}) copy-start(bf16[1,512,3584]{2,1,0:T(8,128)(2,1)} %refs_3_.1) | copy-start | bytes 11010052
  8.3 16.1 %collective-permute-start.6 = (bf16[32,3840]{1,0:T(8,128)(2,1)S(1)}, bf16[32,3840]{1,0:T(8,128)(2,1)S(1)}, u32[]{:S(2)}, u32[]{:S(2)}) collective-permute-start(bf16[32,3840]{1,0:T(8,128)(2,1)S(1)} %get-tuple-element.52), channel_id=1, source_target_pairs={{0,2},{1,3},{2,0},{3,1},{4,6},{5,7},{6,4},{7,5},{8,10},{9,11},{10,... | collective-permute-start | bytes 737288 | tf_op jit(solution)/shard_map/ppermute | solution.py:584
  10.3 14.1 %collective-permute-start.7 = (bf16[32,3840]{1,0:T(8,128)(2,1)S(1)}, bf16[32,3840]{1,0:T(8,128)(2,1)S(1)}, u32[]{:S(2)}, u32[]{:S(2)}) collective-permute-start(bf16[32,3840]{1,0:T(8,128)(2,1)S(1)} %get-tuple-element.53), channel_id=1, source_target_pairs={{0,4},{1,5},{2,6},{3,7},{4,0},{5,1},{6,2},{7,3},{8,12},{9,13},{10,... | collective-permute-start | bytes 737288 | tf_op jit(solution)/shard_map/ppermute | solution.py:584
  11.9 12.5 %collective-permute-start.8 = (bf16[32,3840]{1,0:T(8,128)(2,1)S(1)}, bf16[32,3840]{1,0:T(8,128)(2,1)S(1)}, u32[]{:S(2)}, u32[]{:S(2)}) collective-permute-start(bf16[32,3840]{1,0:T(8,128)(2,1)S(1)} %get-tuple-element.54), channel_id=1, source_target_pairs={{0,6},{1,7},{2,4},{3,5},{4,2},{5,3},{6,0},{7,1},{8,14},{9,15},{10,... | collective-permute-start | bytes 737288 | tf_op jit(solution)/shard_map/ppermute | solution.py:584
  15.0 2.0 %collective-permute-start.3 = (bf16[80,3584]{1,0:T(8,128)(2,1)S(1)}, bf16[80,3584]{1,0:T(8,128)(2,1)S(1)}, u32[]{:S(2)}, u32[]{:S(2)}) collective-permute-start(bf16[80,3584]{1,0:T(8,128)(2,1)S(1)} %get-tuple-element.47.refs_0_), channel_id=1, source_target_pairs={{0,1},{1,0},{2,3},{3,2},{4,5},{5,4},{6,7},{7,6},{8,9},{9,8},{10,11... | collective-permute-start | bytes 1720328 | tf_op jit(solution)/shard_map/ppermute | solution.py:594
  18.5 2.0 %collective-permute-start.4 = (bf16[80,3584]{1,0:T(8,128)(2,1)S(1)}, bf16[80,3584]{1,0:T(8,128)(2,1)S(1)}, u32[]{:S(2)}, u32[]{:S(2)}) collective-permute-start(bf16[80,3584]{1,0:T(8,128)(2,1)S(1)} %get-tuple-element.50), channel_id=1, source_target_pairs={{0,1},{1,0},{2,3},{3,2},{4,5},{5,4},{6,7},{7,6},{8,9},{9,8},{10,11... | collective-permute-start | bytes 1720328 | tf_op jit(solution)/shard_map/ppermute | solution.py:594
  20.7 16.3 %collective-permute-start.5 = (bf16[32,3840]{1,0:T(8,128)(2,1)S(1)}, bf16[32,3840]{1,0:T(8,128)(2,1)S(1)}, u32[]{:S(2)}, u32[]{:S(2)}) collective-permute-start(bf16[32,3840]{1,0:T(8,128)(2,1)S(1)} %finish_forward_01.1.refs_6_), channel_id=1, source_target_pairs={{0,8},{1,9},{2,10},{3,11},{4,12},{5,13},{6,14},{7,15},{8,16},{9,17... | collective-permute-start | bytes 737288 | tf_op jit(solution)/shard_map/ppermute | solution.py:605
  22.5 15.0 %collective-permute-start.12 = (bf16[16,3840]{1,0:T(8,128)(2,1)S(1)}, bf16[16,3840]{1,0:T(8,128)(2,1)S(1)}, u32[]{:S(2)}, u32[]{:S(2)}) collective-permute-start(bf16[16,3840]{1,0:T(8,128)(2,1)S(1)} %finish_forward_2.1.refs_4_), channel_id=1, source_target_pairs={{0,12},{1,13},{2,14},{3,15},{4,8},{5,9},{6,10},{7,11},{8,20},{9,21... | collective-permute-start | bytes 368648 | tf_op jit(solution)/shard_map/ppermute | solution.py:605
  24.5 3.3 %collective-permute-start.9 = (bf16[80,3584]{1,0:T(8,128)(2,1)S(1)}, bf16[80,3584]{1,0:T(8,128)(2,1)S(1)}, u32[]{:S(2)}, u32[]{:S(2)}) collective-permute-start(bf16[80,3584]{1,0:T(8,128)(2,1)S(1)} %get-tuple-element.56.refs_4_.refs_0_), channel_id=1, source_target_pairs={{0,1},{1,0},{2,3},{3,2},{4,5},{5,4},{6,7},{7,6},{8,9},{9,8},{10,11... | collective-permute-start | bytes 1720328 | tf_op jit(solution)/shard_map/ppermute | solution.py:594
  25.0 13.1 %collective-permute-start.13 = (bf16[16,3840]{1,0:T(8,128)(2,1)S(1)}, bf16[16,3840]{1,0:T(8,128)(2,1)S(1)}, u32[]{:S(2)}, u32[]{:S(2)}) collective-permute-start(bf16[16,3840]{1,0:T(8,128)(2,1)S(1)} %finish_forward_3.1), channel_id=1, source_target_pairs={{0,14},{1,15},{2,12},{3,13},{4,10},{5,11},{6,8},{7,9},{8,22},{9,23... | collective-permute-start | bytes 368648 | tf_op jit(solution)/shard_map/ppermute | solution.py:605
  29.3 2.1 %collective-permute-start.10 = (bf16[80,3712]{1,0:T(8,128)(2,1)S(1)}, bf16[80,3712]{1,0:T(8,128)(2,1)S(1)}, u32[]{:S(2)}, u32[]{:S(2)}) collective-permute-start(bf16[80,3712]{1,0:T(8,128)(2,1)S(1)} %get-tuple-element.61), channel_id=1, source_target_pairs={{0,1},{1,0},{2,3},{3,2},{4,5},{5,4},{6,7},{7,6},{8,9},{9,8},{10,11... | collective-permute-start | bytes 1781768 | tf_op jit(solution)/shard_map/ppermute | solution.py:594
  32.0 8.2 %collective-permute-start.14 = (bf16[16,3840]{1,0:T(8,128)(2,1)S(1)}, bf16[16,3840]{1,0:T(8,128)(2,1)S(1)}, u32[]{:S(2)}, u32[]{:S(2)}) collective-permute-start(bf16[16,3840]{1,0:T(8,128)(2,1)S(1)} %get-tuple-element.63), channel_id=1, source_target_pairs={{0,30},{1,31},{2,28},{3,29},{4,26},{5,27},{6,24},{7,25},{8,6},{9,7... | collective-permute-start | bytes 368648 | tf_op jit(solution)/shard_map/ppermute | solution.py:605
  34.9 7.6 %collective-permute-start.15 = (bf16[16,3840]{1,0:T(8,128)(2,1)S(1)}, bf16[16,3840]{1,0:T(8,128)(2,1)S(1)}, u32[]{:S(2)}, u32[]{:S(2)}) collective-permute-start(bf16[16,3840]{1,0:T(8,128)(2,1)S(1)} %get-tuple-element.64), channel_id=1, source_target_pairs={{0,28},{1,29},{2,30},{3,31},{4,24},{5,25},{6,26},{7,27},{8,4},{9,5... | collective-permute-start | bytes 368648 | tf_op jit(solution)/shard_map/ppermute | solution.py:605
  37.0 7.9 %collective-permute-start.16 = (bf16[16,3840]{1,0:T(8,128)(2,1)S(1)}, bf16[16,3840]{1,0:T(8,128)(2,1)S(1)}, u32[]{:S(2)}, u32[]{:S(2)}) collective-permute-start(bf16[16,3840]{1,0:T(8,128)(2,1)S(1)} %get-tuple-element.65), channel_id=1, source_target_pairs={{0,24},{1,25},{2,26},{3,27},{4,28},{5,29},{6,30},{7,31},{8,0},{9,1... | collective-permute-start | bytes 368648 | tf_op jit(solution)/shard_map/ppermute | solution.py:605
  37.5 7.4 %collective-permute-start.11 = (bf16[16,3840]{1,0:T(8,128)(2,1)S(1)}, bf16[16,3840]{1,0:T(8,128)(2,1)S(1)}, u32[]{:S(2)}, u32[]{:S(2)}) collective-permute-start(bf16[16,3840]{1,0:T(8,128)(2,1)S(1)} %lower_chunk.1), channel_id=1, source_target_pairs={{0,2},{1,3},{2,0},{3,1},{4,6},{5,7},{6,4},{7,5},{8,10},{9,11},{10,... | collective-permute-start | bytes 368648 | tf_op jit(solution)/shard_map/ppermute | solution.py:584
  38.1 9.2 %collective-permute-start.17 = (bf16[16,3840]{1,0:T(8,128)(2,1)S(1)}, bf16[16,3840]{1,0:T(8,128)(2,1)S(1)}, u32[]{:S(2)}, u32[]{:S(2)}) collective-permute-start(bf16[16,3840]{1,0:T(8,128)(2,1)S(1)} %get-tuple-element.62.refs_0_), channel_id=1, source_target_pairs={{0,26},{1,27},{2,24},{3,25},{4,30},{5,31},{6,28},{7,29},{8,2},{9,3... | collective-permute-start | bytes 368648 | tf_op jit(solution)/shard_map/ppermute | solution.py:605

commit v15 on v14

--- a/solution.py
+++ b/solution.py
@@ -28,6 +28,7 @@
     "saved_terms": 15,
     "act_norms": 15,
     "act_gates": 15,
+    "forward_rows_early": 15,
 }
 
 
@@ -70,7 +71,7 @@
         self.pieces = width // fold
         self.wide = width + fold
         self.rows = tokens + 16
-        self.order = [*range(experts - 1, 1, -1), 0, 1]
+        self.order = [experts - 1, *range(1, experts - 1), 0]
         assert self.main == 16 and self.pieces <= 14 and width % fold == 0
         assert experts <= 8 and experts & (experts - 1) == 0 and self.split & (self.split - 1) == 0
 
@@ -650,7 +651,7 @@
     affinity = act_gates(z, bwd_own, act_last, inv, vectors, [bwd_parts[0]])
     fwd_done = [got2, got3]
     bwd_parts = [bwd_parts[0]] + [to_core(z, bwd_parts[m], m) for m in others]
-    order = [z.order[-1], *z.order[:-1]]
+    order = z.order
     bwd_out = finish_backward(
         z, order, bwd_own, [grad_last, act_last], [inv, affinity], bwd_parts, vectors, []
     )

time: 48.7 us -> 47.9 us (0.984)
  waiting for transfers between devices: 10.1 us -> 9.37 us
    ppermute x7, waiting for transfers between devices: 7.21 us -> 6.43 us  [to_section(): return lax.ppermute(chunk, ('pp', 'ep'), pairs)]
  transfers between devices with their start and end apart: 18 -> 18, of which waited for: 8 -> 6; matrix products, arithmetic and copies ran while one was open for 0% -> 0% of each run, Pallas kernels for 21% -> 22%
where the time goes in v15:
time: 47.9 us; the launch traced here: 47.7 us
  starting transfers between devices  23.9 us (50%)
  Pallas kernels  13.6 us (28%)
  waiting for transfers between devices  9.37 us (20%)
  between operations  0.79 us (2%)
    pallas_call x19, Pallas kernels, run(): return kernel(*arrays)  13.6 us
    ppermute x7, starting transfers between devices, to_section(): return lax.ppermute(chunk, ('pp', 'ep'), pairs)  13.2 us
    ppermute x7, starting transfers between devices, permute_blocks(): return [lax.ppermute(array, 'ep', pairs) for array in arrays]  10.1 us
    ppermute x7, waiting for transfers between devices, to_section(): return lax.ppermute(chunk, ('pp', 'ep'), pairs)  6.43 us
    ppermute x4, waiting for transfers between devices, to_core(): return lax.ppermute(array, 'ep', pairs)  2.42 us
  transfers between devices with their start and end apart: 18, of which 6 were waited for; matrix products, arithmetic and copies ran while one was open for 0% of the time, Pallas kernels for 22%

profile of v15, /device:TPU:0, one launch (start us, length us, event | category | flops | bytes accessed | tf_op | source)
XLA Modules:
  0.0 47.7 jit_solution(1102301457508098338)
XLA Ops:
  0.7 2.0 %forward_chunks.1 = (bf16[16,3840]{1,0:T(8,128)(2,1)S(1)}, bf16[16,3840]{1,0:T(8,128)(2,1)S(1)}, bf16[16,3840]{1,0:T(8,128)(2,1)S(1)}, bf16[16,3840]{1,0:T(8,128...) custom-call(s32[2]{0:T(128)S(1)} %pad_add_fusion.where, ...), custom_call_target="tpu_custom_call" | custom-call | flops 100000000 | bytes 1000 | tf_op jit(solution)/shard_map/forward_chunks/pallas_call | solution.py:41
  2.8 3.0 %collective-permute-start = (bf16[16,3840]{1,0:T(8,128)(2,1)S(1)}, bf16[16,3840]{1,0:T(8,128)(2,1)S(1)}, u32[]{:S(2)}, u32[]{:S(2)}) collective-permute-start(bf16[16,3840]{1,0:T(8,128)(2,1)S(1)} %get-tuple-element.35), channel_id=1, source_target_pairs={{0,2},{1,3},{2,0},{3,1},{4,6},{5,7},{6,4},{7,5},{8,10},{9,11},{10,... | collective-permute-start | bytes 368648 | tf_op jit(solution)/shard_map/ppermute | solution.py:585
  5.8 1.5 %collective-permute-start.1 = (bf16[16,3840]{1,0:T(8,128)(2,1)S(1)}, bf16[16,3840]{1,0:T(8,128)(2,1)S(1)}, u32[]{:S(2)}, u32[]{:S(2)}) collective-permute-start(bf16[16,3840]{1,0:T(8,128)(2,1)S(1)} %get-tuple-element.36), channel_id=1, source_target_pairs={{0,4},{1,5},{2,6},{3,7},{4,0},{5,1},{6,2},{7,3},{8,12},{9,13},{10,... | collective-permute-start | bytes 368648 | tf_op jit(solution)/shard_map/ppermute | solution.py:585
  7.3 1.0 %backward_chunks.1 = (bf16[32,3840]{1,0:T(8,128)(2,1)S(1)}, bf16[32,3840]{1,0:T(8,128)(2,1)S(1)}, bf16[32,3840]{1,0:T(8,128)(2,1)S(1)}, bf16[32,3840]{1,0:T(8,128)(2,1)S(1)}, f32[8,3584]{1,0:T(8,128)S(1)}) custom-call(s32[2]{0:T(128)S(1)} %pad_add_fusion.where, bf16[80,64]{1,0:T(8,128)(2,1)S(1)} %get-tuple-element.38.selector, ...), custom_call_target="tpu_custom_call" | custom-call | flops 10000000000 | bytes 1000 | tf_op jit(solution)/shard_map/backward_chunks/pallas_call | solution.py:41
  8.3 2.0 %collective-permute-start.6 = (bf16[32,3840]{1,0:T(8,128)(2,1)S(1)}, bf16[32,3840]{1,0:T(8,128)(2,1)S(1)}, u32[]{:S(2)}, u32[]{:S(2)}) collective-permute-start(bf16[32,3840]{1,0:T(8,128)(2,1)S(1)} %get-tuple-element.52), channel_id=1, source_target_pairs={{0,2},{1,3},{2,0},{3,1},{4,6},{5,7},{6,4},{7,5},{8,10},{9,11},{10,... | collective-permute-start | bytes 737288 | tf_op jit(solution)/shard_map/ppermute | solution.py:585
  10.3 1.5 %collective-permute-start.7 = (bf16[32,3840]{1,0:T(8,128)(2,1)S(1)}, bf16[32,3840]{1,0:T(8,128)(2,1)S(1)}, u32[]{:S(2)}, u32[]{:S(2)}) collective-permute-start(bf16[32,3840]{1,0:T(8,128)(2,1)S(1)} %get-tuple-element.53), channel_id=1, source_target_pairs={{0,4},{1,5},{2,6},{3,7},{4,0},{5,1},{6,2},{7,3},{8,12},{9,13},{10,... | collective-permute-start | bytes 737288 | tf_op jit(solution)/shard_map/ppermute | solution.py:585
  11.9 1.1 %collective-permute-start.8 = (bf16[32,3840]{1,0:T(8,128)(2,1)S(1)}, bf16[32,3840]{1,0:T(8,128)(2,1)S(1)}, u32[]{:S(2)}, u32[]{:S(2)}) collective-permute-start(bf16[32,3840]{1,0:T(8,128)(2,1)S(1)} %get-tuple-element.54), channel_id=1, source_target_pairs={{0,6},{1,7},{2,4},{3,5},{4,2},{5,3},{6,0},{7,1},{8,14},{9,15},{10,... | collective-permute-start | bytes 737288 | tf_op jit(solution)/shard_map/ppermute | solution.py:585
  13.0 1.0 %turned_down.1.refs_5_ = bf16[3584,512]{1,0:T(8,128)(2,1)S(1)} custom-call(bf16[1,512,3584]{2,1,0:T(8,128)(2,1)S(1)} %copy-done.1, bf16[1,3584,512]{2,1,0:T(8,128)(2,1)S(1)} %copy-done, bf16[32,3840]{1,0:T(8,128)(2,1)S(1)} %get-tuple-element.45.refs_1_.refs_0_, bf16[16,3840]{1,0:T(8,128)(2,1)S(1)} %collective-permute-done.refs_2_.refs_1_), custom_call_target="tpu_custom_call" | custom-call | flops 100000000 | bytes 1000 | tf_op jit(solution)/shard_map/turned_down/pallas_call | solution.py:41
  14.0 0.5 %collective-permute-done.2.refs_3_.refs_0_ = bf16[16,3840]{1,0:T(8,128)(2,1)S(1)} collective-permute-done((bf16[16,3840]{1,0:T(8,128)(2,1)S(1)}, bf16[16,3840]{1,0:T(8,128)(2,1)S(1)}, u32[]{:S(2)}, u32[]{:S(2)}) %collective-permute-start.2) | collective-permute-done | bytes 122912 | tf_op jit(solution)/shard_map/ppermute | solution.py:585
  14.5 0.5 %normed_rows.1 = (bf16[80,3584]{1,0:T(8,128)(2,1)S(1)}, f32[80,128]{1,0:T(8,128)S(1)}, f32[16,3584]{1,0:T(8,128)S(1)}) custom-call(bf16[16,3840]{1,0:T(8,128)(2,1)S(1)} %get-tuple-element.34.refs_0_, bf16[16,3840]{1,0:T(8,128)(2,1)S(1)} %collective-permute-done.refs_2_.refs_1_, bf16[16,3840]{1,0:T(8,128)(2,1)S(1)} %collective-permute-done.1.refs_2_.refs_0_, ...), custom_call_target="tpu_custom_call" | custom-call | flops 100000000 | bytes 1000 | tf_op jit(solution)/shard_map/normed_rows/pallas_call | solution.py:41
  15.0 1.6 %saved_rows.1.refs_4_.ordered_ref = f32[160,512]{1,0:T(8,128)S(1)} custom-call(s32[2]{0:T(128)S(1)} %pad_add_fusion.where, bf16[1,1,136,512]{3,2,1,0:T(8,128)(2,1)} %saved_any.1, f32[80,128]{1,0:T(8,128)S(1)} %get-tuple-element.48.refs_0_.refs_5_.refs_4_), custom_call_target="tpu_custom_call" | custom-call | flops 15000000512 | bytes 1000 | tf_op jit(solution)/shard_map/saved_rows/pallas_call | solution.py:41
  16.7 0.3 collective-permute-done.3.refs_1_
  17.0 1.5 %experts_forward.1 = (bf16[80,3584]{1,0:T(8,128)(2,1)S(1)}, bf16[80,3584]{1,0:T(8,128)(2,1)S(1)}) custom-call(bf16[80,3584]{1,0:T(8,128)(2,1)S(1)} %get-tuple-element.47.refs_0_, bf16[80,3584]{1,0:T(8,128)(2,1)S(1)} %collective-permute-done.3.refs_1_, bf16[1,3584,512]{2,1,0:T(8,128)(2,1)S(1)} %copy-done, bf16[1,512,3584]{2,1,0:T(8,128)(2,1)S(1)} %copy-done.1, ...), custom_call_target="tpu_custom_call" | custom-call | flops 100000000 | bytes 1000 | tf_op jit(solution)/shard_map/experts_forward/pallas_call | solution.py:41
  18.8 1.0 %turned_gate.1.refs_6_.refs_4_ = bf16[512,3584]{1,0:T(8,128)(2,1)S(1)} custom-call(bf16[1,3584,512]{2,1,0:T(8,128)(2,1)S(1)} %copy-done, bf16[160,512]{1,0:T(8,128)(2,1)S(1)} %get-tuple-element.51.refs_0_.refs_5_.refs_2_), custom_call_target="tpu_custom_call" | custom-call | flops 100000000 | bytes 1000 | tf_op jit(solution)/shard_map/turned_gate/pallas_call | solution.py:41
  19.8 0.7 %collective-permute-done.4.refs_4_.refs_3_ = bf16[80,3584]{1,0:T(8,128)(2,1)S(1)} collective-permute-done((bf16[80,3584]{1,0:T(8,128)(2,1)S(1)}, bf16[80,3584]{1,0:T(8,128)(2,1)S(1)}, u32[]{:S(2)}, u32[]{:S(2)}) %collective-permute-start.4) | collective-permute-done | bytes 573472 | tf_op jit(solution)/shard_map/ppermute | solution.py:595
  20.7 1.6 %collective-permute-start.5 = (bf16[32,3840]{1,0:T(8,128)(2,1)S(1)}, bf16[32,3840]{1,0:T(8,128)(2,1)S(1)}, u32[]{:S(2)}, u32[]{:S(2)}) collective-permute-start(bf16[32,3840]{1,0:T(8,128)(2,1)S(1)} %finish_forward_01.1.refs_6_), channel_id=1, source_target_pairs={{0,8},{1,9},{2,10},{3,11},{4,12},{5,13},{6,14},{7,15},{8,16},{9,17... | collective-permute-start | bytes 737288 | tf_op jit(solution)/shard_map/ppermute | solution.py:606
  22.5 1.9 %collective-permute-start.12 = (bf16[16,3840]{1,0:T(8,128)(2,1)S(1)}, bf16[16,3840]{1,0:T(8,128)(2,1)S(1)}, u32[]{:S(2)}, u32[]{:S(2)}) collective-permute-start(bf16[16,3840]{1,0:T(8,128)(2,1)S(1)} %finish_forward_2.1.refs_4_), channel_id=1, source_target_pairs={{0,12},{1,13},{2,14},{3,15},{4,8},{5,9},{6,10},{7,11},{8,20},{9,21... | collective-permute-start | bytes 368648 | tf_op jit(solution)/shard_map/ppermute | solution.py:606
  25.0 2.8 %collective-permute-start.13 = (bf16[16,3840]{1,0:T(8,128)(2,1)S(1)}, bf16[16,3840]{1,0:T(8,128)(2,1)S(1)}, u32[]{:S(2)}, u32[]{:S(2)}) collective-permute-start(bf16[16,3840]{1,0:T(8,128)(2,1)S(1)} %finish_forward_3.1), channel_id=1, source_target_pairs={{0,14},{1,15},{2,12},{3,13},{4,10},{5,11},{6,8},{7,9},{8,22},{9,23... | collective-permute-start | bytes 368648 | tf_op jit(solution)/shard_map/ppermute | solution.py:606
  27.8 1.5 %experts_backward.1 = (bf16[80,3712]{1,0:T(8,128)(2,1)S(1)}, bf16[80,3712]{1,0:T(8,128)(2,1)S(1)}) custom-call(bf16[80,3584]{1,0:T(8,128)(2,1)S(1)} %get-tuple-element.56.refs_4_.refs_0_, bf16[80,3584]{1,0:T(8,128)(2,1)S(1)} %collective-permute-done.9.refs_1_, bf16[160,512]{1,0:T(8,128)(2,1)S(1)} %get-tuple-element.51.refs_0_.refs_5_.refs_2_, ...), custom_call_target="tpu_custom_call" | custom-call | flops 100000000 | bytes 1000 | tf_op jit(solution)/shard_map/experts_backward/pallas_call | solution.py:41
  29.3 0.3 collective-permute-start.10
  29.5 0.4 act_gates.1.refs_7_
  29.9 1.4 %collective-permute-done.10.refs_9_ = bf16[80,3712]{1,0:T(8,128)(2,1)S(1)} collective-permute-done((bf16[80,3712]{1,0:T(8,128)(2,1)S(1)}, bf16[80,3712]{1,0:T(8,128)(2,1)S(1)}, u32[]{:S(2)}, u32[]{:S(2)}) %collective-permute-start.10) | collective-permute-done | bytes 593952 | tf_op jit(solution)/shard_map/ppermute | solution.py:595
  31.3 0.7 %finish_backward.1 = (bf16[16,3840]{1,0:T(8,128)(2,1)S(1)}, bf16[16,3840]{1,0:T(8,128)(2,1)S(1)}, bf16[16,3840]{1,0:T(8,128)(2,1)S(1)}, bf16[16,3840]{1,0:T(8,128)(2,1)S(1)}) custom-call(bf16[32,3840]{1,0:T(8,128)(2,1)S(1)} %get-tuple-element.45.refs_1_.refs_0_, bf16[32,3840]{1,0:T(8,128)(2,1)S(1)} %collective-permute-done.6.refs_1_, ...), custom_call_target="tpu_custom_call" | custom-call | flops 100000000 | bytes 1000 | tf_op jit(solution)/shard_map/finish_backward/pallas_call | solution.py:41
  32.0 2.6 %collective-permute-start.15 = (bf16[16,3840]{1,0:T(8,128)(2,1)S(1)}, bf16[16,3840]{1,0:T(8,128)(2,1)S(1)}, u32[]{:S(2)}, u32[]{:S(2)}) collective-permute-start(bf16[16,3840]{1,0:T(8,128)(2,1)S(1)} %get-tuple-element.63), channel_id=1, source_target_pairs={{0,26},{1,27},{2,24},{3,25},{4,30},{5,31},{6,28},{7,29},{8,2},{9,3... | collective-permute-start | bytes 368648 | tf_op jit(solution)/shard_map/ppermute | solution.py:606
  34.7 1.5 %collective-permute-start.16 = (bf16[16,3840]{1,0:T(8,128)(2,1)S(1)}, bf16[16,3840]{1,0:T(8,128)(2,1)S(1)}, u32[]{:S(2)}, u32[]{:S(2)}) collective-permute-start(bf16[16,3840]{1,0:T(8,128)(2,1)S(1)} %get-tuple-element.64), channel_id=1, source_target_pairs={{0,28},{1,29},{2,30},{3,31},{4,24},{5,25},{6,26},{7,27},{8,4},{9,5... | collective-permute-start | bytes 368648 | tf_op jit(solution)/shard_map/ppermute | solution.py:606
  36.2 1.3 %collective-permute-start.14 = (bf16[16,3840]{1,0:T(8,128)(2,1)S(1)}, bf16[16,3840]{1,0:T(8,128)(2,1)S(1)}, u32[]{:S(2)}, u32[]{:S(2)}) collective-permute-start(bf16[16,3840]{1,0:T(8,128)(2,1)S(1)} %get-tuple-element.62.refs_0_), channel_id=1, source_target_pairs={{0,30},{1,31},{2,28},{3,29},{4,26},{5,27},{6,24},{7,25},{8,6},{9,7... | collective-permute-start | bytes 368648 | tf_op jit(solution)/shard_map/ppermute | solution.py:606
  37.5 1.4 %collective-permute-start.17 = (bf16[16,3840]{1,0:T(8,128)(2,1)S(1)}, bf16[16,3840]{1,0:T(8,128)(2,1)S(1)}, u32[]{:S(2)}, u32[]{:S(2)}) collective-permute-start(bf16[16,3840]{1,0:T(8,128)(2,1)S(1)} %get-tuple-element.65), channel_id=1, source_target_pairs={{0,24},{1,25},{2,26},{3,27},{4,28},{5,29},{6,30},{7,31},{8,0},{9,1... | collective-permute-start | bytes 368648 | tf_op jit(solution)/shard_map/ppermute | solution.py:606
  38.9 0.9 %collective-permute-start.11 = (bf16[16,3840]{1,0:T(8,128)(2,1)S(1)}, bf16[16,3840]{1,0:T(8,128)(2,1)S(1)}, u32[]{:S(2)}, u32[]{:S(2)}) collective-permute-start(bf16[16,3840]{1,0:T(8,128)(2,1)S(1)} %lower_chunk.1), channel_id=1, source_target_pairs={{0,2},{1,3},{2,0},{3,1},{4,6},{5,7},{6,4},{7,5},{8,10},{9,11},{10,... | collective-permute-start | bytes 368648 | tf_op jit(solution)/shard_map/ppermute | solution.py:585
  39.8 0.3 forward_rows_early.1.refs_1_
  40.1 1.7 %collective-permute-done.16.refs_4_ = bf16[16,3840]{1,0:T(8,128)(2,1)S(1)} collective-permute-done((bf16[16,3840]{1,0:T(8,128)(2,1)S(1)}, bf16[16,3840]{1,0:T(8,128)(2,1)S(1)}, u32[]{:S(2)}, u32[]{:S(2)}) %collective-permute-start.16) | collective-permute-done | bytes 122912 | tf_op jit(solution)/shard_map/ppermute | solution.py:606
  41.8 4.7 %collective-permute-done.17.refs_5_ = bf16[16,3840]{1,0:T(8,128)(2,1)S(1)} collective-permute-done((bf16[16,3840]{1,0:T(8,128)(2,1)S(1)}, bf16[16,3840]{1,0:T(8,128)(2,1)S(1)}, u32[]{:S(2)}, u32[]{:S(2)}) %collective-permute-start.17) | collective-permute-done | bytes 122912 | tf_op jit(solution)/shard_map/ppermute | solution.py:606
  46.5 1.2 %all_rows.1 = (bf16[64,3584]{1,0:T(8,128)(2,1)}, bf16[64,3584]{1,0:T(8,128)(2,1)}) custom-call(bf16[16,3840]{1,0:T(8,128)(2,1)S(1)} %collective-permute-done.11.refs_0_, bf16[64,3584]{1,0:T(8,128)(2,1)S(1)} %forward_rows_early.1.refs_1_, bf16[16,3840]{1,0:T(8,128)(2,1)S(1)} %collective-permute-done.14.refs_2_, ...), custom_call_target="tpu_custom_call" | custom-call | flops 100000000 | bytes 1000 | tf_op jit(solution)/shard_map/all_rows/pallas_call | solution.py:41
  (28 shorter events, 1.4 us)
Async XLA Ops:
  2.8 9.1 %collective-permute-start = (bf16[16,3840]{1,0:T(8,128)(2,1)S(1)}, bf16[16,3840]{1,0:T(8,128)(2,1)S(1)}, u32[]{:S(2)}, u32[]{:S(2)}) collective-permute-start(bf16[16,3840]{1,0:T(8,128)(2,1)S(1)} %get-tuple-element.35), channel_id=1, source_target_pairs={{0,2},{1,3},{2,0},{3,1},{4,6},{5,7},{6,4},{7,5},{8,10},{9,11},{10,... | collective-permute-start | bytes 368648 | tf_op jit(solution)/shard_map/ppermute | solution.py:585
  5.8 8.2 %collective-permute-start.1 = (bf16[16,3840]{1,0:T(8,128)(2,1)S(1)}, bf16[16,3840]{1,0:T(8,128)(2,1)S(1)}, u32[]{:S(2)}, u32[]{:S(2)}) collective-permute-start(bf16[16,3840]{1,0:T(8,128)(2,1)S(1)} %get-tuple-element.36), channel_id=1, source_target_pairs={{0,4},{1,5},{2,6},{3,7},{4,0},{5,1},{6,2},{7,3},{8,12},{9,13},{10,... | collective-permute-start | bytes 368648 | tf_op jit(solution)/shard_map/ppermute | solution.py:585
  7.3 7.2 %collective-permute-start.2 = (bf16[16,3840]{1,0:T(8,128)(2,1)S(1)}, bf16[16,3840]{1,0:T(8,128)(2,1)S(1)}, u32[]{:S(2)}, u32[]{:S(2)}) collective-permute-start(bf16[16,3840]{1,0:T(8,128)(2,1)S(1)} %get-tuple-element.37), channel_id=1, source_target_pairs={{0,6},{1,7},{2,4},{3,5},{4,2},{5,3},{6,0},{7,1},{8,14},{9,15},{10,... | collective-permute-start | bytes 368648 | tf_op jit(solution)/shard_map/ppermute | solution.py:585
  7.3 5.6 %copy-start = (bf16[1,3584,512]{2,1,0:T(8,128)(2,1)S(1)}, bf16[1,3584,512]{2,1,0:T(8,128)(2,1)}, u32[]{:S(2)}) copy-start(bf16[1,3584,512]{2,1,0:T(8,128)(2,1)} %weights_ref.3) | copy-start | bytes 11010052
  7.3 5.6 %copy-start.1 = (bf16[1,512,3584]{2,1,0:T(8,128)(2,1)S(1)}, bf16[1,512,3584]{2,1,0:T(8,128)(2,1)}, u32[]{:S(2)}) copy-start(bf16[1,512,3584]{2,1,0:T(8,128)(2,1)} %refs_3_.1) | copy-start | bytes 11010052
  8.3 16.1 %collective-permute-start.6 = (bf16[32,3840]{1,0:T(8,128)(2,1)S(1)}, bf16[32,3840]{1,0:T(8,128)(2,1)S(1)}, u32[]{:S(2)}, u32[]{:S(2)}) collective-permute-start(bf16[32,3840]{1,0:T(8,128)(2,1)S(1)} %get-tuple-element.52), channel_id=1, source_target_pairs={{0,2},{1,3},{2,0},{3,1},{4,6},{5,7},{6,4},{7,5},{8,10},{9,11},{10,... | collective-permute-start | bytes 737288 | tf_op jit(solution)/shard_map/ppermute | solution.py:585
  10.3 14.1 %collective-permute-start.7 = (bf16[32,3840]{1,0:T(8,128)(2,1)S(1)}, bf16[32,3840]{1,0:T(8,128)(2,1)S(1)}, u32[]{:S(2)}, u32[]{:S(2)}) collective-permute-start(bf16[32,3840]{1,0:T(8,128)(2,1)S(1)} %get-tuple-element.53), channel_id=1, source_target_pairs={{0,4},{1,5},{2,6},{3,7},{4,0},{5,1},{6,2},{7,3},{8,12},{9,13},{10,... | collective-permute-start | bytes 737288 | tf_op jit(solution)/shard_map/ppermute | solution.py:585
  11.9 12.5 %collective-permute-start.8 = (bf16[32,3840]{1,0:T(8,128)(2,1)S(1)}, bf16[32,3840]{1,0:T(8,128)(2,1)S(1)}, u32[]{:S(2)}, u32[]{:S(2)}) collective-permute-start(bf16[32,3840]{1,0:T(8,128)(2,1)S(1)} %get-tuple-element.54), channel_id=1, source_target_pairs={{0,6},{1,7},{2,4},{3,5},{4,2},{5,3},{6,0},{7,1},{8,14},{9,15},{10,... | collective-permute-start | bytes 737288 | tf_op jit(solution)/shard_map/ppermute | solution.py:585
  15.0 2.0 %collective-permute-start.3 = (bf16[80,3584]{1,0:T(8,128)(2,1)S(1)}, bf16[80,3584]{1,0:T(8,128)(2,1)S(1)}, u32[]{:S(2)}, u32[]{:S(2)}) collective-permute-start(bf16[80,3584]{1,0:T(8,128)(2,1)S(1)} %get-tuple-element.47.refs_0_), channel_id=1, source_target_pairs={{0,1},{1,0},{2,3},{3,2},{4,5},{5,4},{6,7},{7,6},{8,9},{9,8},{10,11... | collective-permute-start | bytes 1720328 | tf_op jit(solution)/shard_map/ppermute | solution.py:595
  18.5 2.0 %collective-permute-start.4 = (bf16[80,3584]{1,0:T(8,128)(2,1)S(1)}, bf16[80,3584]{1,0:T(8,128)(2,1)S(1)}, u32[]{:S(2)}, u32[]{:S(2)}) collective-permute-start(bf16[80,3584]{1,0:T(8,128)(2,1)S(1)} %get-tuple-element.50), channel_id=1, source_target_pairs={{0,1},{1,0},{2,3},{3,2},{4,5},{5,4},{6,7},{7,6},{8,9},{9,8},{10,11... | collective-permute-start | bytes 1720328 | tf_op jit(solution)/shard_map/ppermute | solution.py:595
  20.7 15.4 %collective-permute-start.5 = (bf16[32,3840]{1,0:T(8,128)(2,1)S(1)}, bf16[32,3840]{1,0:T(8,128)(2,1)S(1)}, u32[]{:S(2)}, u32[]{:S(2)}) collective-permute-start(bf16[32,3840]{1,0:T(8,128)(2,1)S(1)} %finish_forward_01.1.refs_6_), channel_id=1, source_target_pairs={{0,8},{1,9},{2,10},{3,11},{4,12},{5,13},{6,14},{7,15},{8,16},{9,17... | collective-permute-start | bytes 737288 | tf_op jit(solution)/shard_map/ppermute | solution.py:606
  22.5 15.0 %collective-permute-start.12 = (bf16[16,3840]{1,0:T(8,128)(2,1)S(1)}, bf16[16,3840]{1,0:T(8,128)(2,1)S(1)}, u32[]{:S(2)}, u32[]{:S(2)}) collective-permute-start(bf16[16,3840]{1,0:T(8,128)(2,1)S(1)} %finish_forward_2.1.refs_4_), channel_id=1, source_target_pairs={{0,12},{1,13},{2,14},{3,15},{4,8},{5,9},{6,10},{7,11},{8,20},{9,21... | collective-permute-start | bytes 368648 | tf_op jit(solution)/shard_map/ppermute | solution.py:606
  24.5 3.3 %collective-permute-start.9 = (bf16[80,3584]{1,0:T(8,128)(2,1)S(1)}, bf16[80,3584]{1,0:T(8,128)(2,1)S(1)}, u32[]{:S(2)}, u32[]{:S(2)}) collective-permute-start(bf16[80,3584]{1,0:T(8,128)(2,1)S(1)} %get-tuple-element.56.refs_4_.refs_0_), channel_id=1, source_target_pairs={{0,1},{1,0},{2,3},{3,2},{4,5},{5,4},{6,7},{7,6},{8,9},{9,8},{10,11... | collective-permute-start | bytes 1720328 | tf_op jit(solution)/shard_map/ppermute | solution.py:595
  25.0 13.9 %collective-permute-start.13 = (bf16[16,3840]{1,0:T(8,128)(2,1)S(1)}, bf16[16,3840]{1,0:T(8,128)(2,1)S(1)}, u32[]{:S(2)}, u32[]{:S(2)}) collective-permute-start(bf16[16,3840]{1,0:T(8,128)(2,1)S(1)} %finish_forward_3.1), channel_id=1, source_target_pairs={{0,14},{1,15},{2,12},{3,13},{4,10},{5,11},{6,8},{7,9},{8,22},{9,23... | collective-permute-start | bytes 368648 | tf_op jit(solution)/shard_map/ppermute | solution.py:606
  29.3 2.1 %collective-permute-start.10 = (bf16[80,3712]{1,0:T(8,128)(2,1)S(1)}, bf16[80,3712]{1,0:T(8,128)(2,1)S(1)}, u32[]{:S(2)}, u32[]{:S(2)}) collective-permute-start(bf16[80,3712]{1,0:T(8,128)(2,1)S(1)} %get-tuple-element.61), channel_id=1, source_target_pairs={{0,1},{1,0},{2,3},{3,2},{4,5},{5,4},{6,7},{7,6},{8,9},{9,8},{10,11... | collective-permute-start | bytes 1781768 | tf_op jit(solution)/shard_map/ppermute | solution.py:595
  32.0 8.1 %collective-permute-start.15 = (bf16[16,3840]{1,0:T(8,128)(2,1)S(1)}, bf16[16,3840]{1,0:T(8,128)(2,1)S(1)}, u32[]{:S(2)}, u32[]{:S(2)}) collective-permute-start(bf16[16,3840]{1,0:T(8,128)(2,1)S(1)} %get-tuple-element.63), channel_id=1, source_target_pairs={{0,26},{1,27},{2,24},{3,25},{4,30},{5,31},{6,28},{7,29},{8,2},{9,3... | collective-permute-start | bytes 368648 | tf_op jit(solution)/shard_map/ppermute | solution.py:606
  34.7 7.2 %collective-permute-start.16 = (bf16[16,3840]{1,0:T(8,128)(2,1)S(1)}, bf16[16,3840]{1,0:T(8,128)(2,1)S(1)}, u32[]{:S(2)}, u32[]{:S(2)}) collective-permute-start(bf16[16,3840]{1,0:T(8,128)(2,1)S(1)} %get-tuple-element.64), channel_id=1, source_target_pairs={{0,28},{1,29},{2,30},{3,31},{4,24},{5,25},{6,26},{7,27},{8,4},{9,5... | collective-permute-start | bytes 368648 | tf_op jit(solution)/shard_map/ppermute | solution.py:606
  36.2 10.4 %collective-permute-start.14 = (bf16[16,3840]{1,0:T(8,128)(2,1)S(1)}, bf16[16,3840]{1,0:T(8,128)(2,1)S(1)}, u32[]{:S(2)}, u32[]{:S(2)}) collective-permute-start(bf16[16,3840]{1,0:T(8,128)(2,1)S(1)} %get-tuple-element.62.refs_0_), channel_id=1, source_target_pairs={{0,30},{1,31},{2,28},{3,29},{4,26},{5,27},{6,24},{7,25},{8,6},{9,7... | collective-permute-start | bytes 368648 | tf_op jit(solution)/shard_map/ppermute | solution.py:606
  37.5 9.1 %collective-permute-start.17 = (bf16[16,3840]{1,0:T(8,128)(2,1)S(1)}, bf16[16,3840]{1,0:T(8,128)(2,1)S(1)}, u32[]{:S(2)}, u32[]{:S(2)}) collective-permute-start(bf16[16,3840]{1,0:T(8,128)(2,1)S(1)} %get-tuple-element.65), channel_id=1, source_target_pairs={{0,24},{1,25},{2,26},{3,27},{4,28},{5,29},{6,30},{7,31},{8,0},{9,1... | collective-permute-start | bytes 368648 | tf_op jit(solution)/shard_map/ppermute | solution.py:606
  38.9 7.6 %collective-permute-start.11 = (bf16[16,3840]{1,0:T(8,128)(2,1)S(1)}, bf16[16,3840]{1,0:T(8,128)(2,1)S(1)}, u32[]{:S(2)}, u32[]{:S(2)}) collective-permute-start(bf16[16,3840]{1,0:T(8,128)(2,1)S(1)} %lower_chunk.1), channel_id=1, source_target_pairs={{0,2},{1,3},{2,0},{3,1},{4,6},{5,7},{6,4},{7,5},{8,10},{9,11},{10,... | collective-permute-start | bytes 368648 | tf_op jit(solution)/shard_map/ppermute | solution.py:585

commit v16 on v15

--- a/solution.py
+++ b/solution.py
@@ -467,13 +467,14 @@
     return call(body, places, shape((16, z.wide)), [], 8, "lower_chunk")(double, *after)
 
 
-def finish_backward(z, order, chunks, lasts, terms, parts, vectors, after):
-    def body(*refs):
-        e = z.experts
-        chunks, (last_grad, last_act, inv_ref, affinity_ref) = refs[:e], refs[e : e + 4]
-        parts, vectors = refs[e + 4 : e + 4 + z.split], refs[e + 4 + z.split]
-        outs, (tile,) = refs[-1 - e : -1], refs[-1:]
-        outs = [outs[order.index(k)] for k in range(e)]
+def finish_backward(z, ks, chunks, lasts, terms, parts, vectors, after):
+    count = len(ks)
+
+    def body(*refs):
+        chunks = refs[:count]
+        last_grad, last_act, inv_ref, affinity_ref = refs[count : count + 4]
+        parts, vectors = refs[count + 4 : count + 4 + z.split], refs[count + 4 + z.split]
+        outs, tile = refs[-1 - count : -1], refs[-1]
         gain, router = vectors[0:1, :], vectors[1:2, :]
 
         def finished(h, g, at):
@@ -490,20 +491,20 @@
             return g + inv * (grad_pre - h * (inv * inv * centre))
 
         tail = finished(last_act[...], last_grad[...], z.tokens)
-        for k in range(e):
-            g = chunks[k][:16, : z.width].astype(f32)
-            h = chunks[k][16:32, : z.width].astype(f32)
-            outs[k][:, : z.width] = finished(h, g, k * z.main).astype(bf16)
-            put_last(z, tail[k : k + 1, :], chunks[k], tile, outs[k])
-
-    return call(
-        body,
-        "v" * (z.experts + z.split + 5) + "a" * len(after),
-        [shape((z.main, z.wide))] * z.experts,
+        for k, chunk, out in zip(ks, chunks, outs):
+            g = chunk[:16, : z.width].astype(f32)
+            h = chunk[16:32, : z.width].astype(f32)
+            out[:, : z.width] = finished(h, g, k * z.main).astype(bf16)
+            put_last(z, tail[k : k + 1, :], chunk, tile, out)
+
+    return call(
+        body,
+        "v" * (count + z.split + 5) + "a" * len(after),
+        [shape((z.main, z.wide))] * count,
         [pltpu.VMEM((16, fold), f32)],
         8,
-        "finish_backward",
-    )(*chunks, *lasts, *terms, *parts, vectors, *after)
+        "finish_backward_" + "".join(map(str, ks)),
+    )(*[chunks[k] for k in ks], *lasts, *terms, *parts, vectors, *after)
 
 
 def ordered_columns(z, chunks):
@@ -651,12 +652,12 @@
     affinity = act_gates(z, bwd_own, act_last, inv, vectors, [bwd_parts[0]])
     fwd_done = [got2, got3]
     bwd_parts = [bwd_parts[0]] + [to_core(z, bwd_parts[m], m) for m in others]
-    order = z.order
-    bwd_out = finish_backward(
-        z, order, bwd_own, [grad_last, act_last], [inv, affinity], bwd_parts, vectors, []
-    )
+    first, order = [z.order[1]], [k for k in z.order if k != z.order[1]]
+    arguments = ([grad_last, act_last], [inv, affinity], bwd_parts, vectors)
+    bwd_first = finish_backward(z, first, bwd_own, *arguments, [])
+    bwd_out = finish_backward(z, order, bwd_own, *arguments, bwd_first)
     (relayed,) = permute_blocks(z, [lower_chunk(z, got, [bwd_out[0]])], 1)
-    bwd_done = {k: to_section(z, out, k, -1) for k, out in zip(order, bwd_out)}
+    bwd_done = {k: to_section(z, out, k, -1) for k, out in zip(first + order, bwd_first + bwd_out)}
 
     early = some_rows(z, {0: got, 2: got2, 3: got3}, [], "forward_rows_early")
     outputs = [({1: relayed}, [early]), ({k: bwd_done[k] for k in z.order}, [])]

time: 47.9 us -> 52.8 us (1.10)
  waiting for transfers between devices: 9.37 us -> 16.5 us
  starting transfers between devices: 23.9 us -> 21.4 us
    ppermute x7, waiting for transfers between devices: 0.52 us -> 5.6 us  [permute_blocks(): return [lax.ppermute(array, 'ep', pairs) for array in arrays]]
    ppermute x4, waiting for transfers between devices: 2.42 us -> 3.99 us  [to_core(): return lax.ppermute(array, 'ep', pairs)]
    ppermute x7, starting transfers between devices: 10.1 us -> 8.72 us  [permute_blocks(): return [lax.ppermute(array, 'ep', pairs) for array in arrays]]
    ppermute x7, starting transfers between devices: 13.2 us -> 12.1 us  [to_section(): return lax.ppermute(chunk, ('pp', 'ep'), pairs)]
    pallas_call x19 -> x20, Pallas kernels: 13.6 us -> 13.8 us  [run(): return kernel(*arrays)]
  transfers between devices with their start and end apart: 18 -> 18, of which waited for: 6 -> 7; matrix products, arithmetic and copies ran while one was open for 0% -> 0% of each run, Pallas kernels for 22% -> 20%
where the time goes in v16:
time: 52.8 us; the launch traced here: 52.6 us
  starting transfers between devices  21.4 us (41%)
  waiting for transfers between devices  16.5 us (31%)
  Pallas kernels  13.8 us (26%)
  between operations  0.79 us (1%)
    pallas_call x20, Pallas kernels, run(): return kernel(*arrays)  13.8 us
    ppermute x7, starting transfers between devices, to_section(): return lax.ppermute(chunk, ('pp', 'ep'), pairs)  12.1 us
    ppermute x7, starting transfers between devices, permute_blocks(): return [lax.ppermute(array, 'ep', pairs) for array in arrays]  8.72 us
    ppermute x7, waiting for transfers between devices, to_section(): return lax.ppermute(chunk, ('pp', 'ep'), pairs)  6.93 us
    ppermute x7, waiting for transfers between devices, permute_blocks(): return [lax.ppermute(array, 'ep', pairs) for array in arrays]  5.6 us
    ppermute x4, waiting for transfers between devices, to_core(): return lax.ppermute(array, 'ep', pairs)  3.99 us
  transfers between devices with their start and end apart: 18, of which 7 were waited for; matrix products, arithmetic and copies ran while one was open for 0% of the time, Pallas kernels for 20%

profile of v16, /device:TPU:0, one launch (start us, length us, event | category | flops | bytes accessed | tf_op | source)
XLA Modules:
  0.0 52.6 jit_solution(15359177919849408748)
XLA Ops:
  0.7 2.0 %forward_chunks.1 = (bf16[16,3840]{1,0:T(8,128)(2,1)S(1)}, bf16[16,3840]{1,0:T(8,128)(2,1)S(1)}, bf16[16,3840]{1,0:T(8,128)(2,1)S(1)}, bf16[16,3840]{1,0:T(8,128...) custom-call(s32[2]{0:T(128)S(1)} %pad_add_fusion.where, ...), custom_call_target="tpu_custom_call" | custom-call | flops 100000000 | bytes 1000 | tf_op jit(solution)/shard_map/forward_chunks/pallas_call | solution.py:41
  2.8 3.0 %collective-permute-start = (bf16[16,3840]{1,0:T(8,128)(2,1)S(1)}, bf16[16,3840]{1,0:T(8,128)(2,1)S(1)}, u32[]{:S(2)}, u32[]{:S(2)}) collective-permute-start(bf16[16,3840]{1,0:T(8,128)(2,1)S(1)} %get-tuple-element.34), channel_id=1, source_target_pairs={{0,2},{1,3},{2,0},{3,1},{4,6},{5,7},{6,4},{7,5},{8,10},{9,11},{10,... | collective-permute-start | bytes 368648 | tf_op jit(solution)/shard_map/ppermute | solution.py:586
  5.8 1.5 %collective-permute-start.1 = (bf16[16,3840]{1,0:T(8,128)(2,1)S(1)}, bf16[16,3840]{1,0:T(8,128)(2,1)S(1)}, u32[]{:S(2)}, u32[]{:S(2)}) collective-permute-start(bf16[16,3840]{1,0:T(8,128)(2,1)S(1)} %get-tuple-element.35), channel_id=1, source_target_pairs={{0,4},{1,5},{2,6},{3,7},{4,0},{5,1},{6,2},{7,3},{8,12},{9,13},{10,... | collective-permute-start | bytes 368648 | tf_op jit(solution)/shard_map/ppermute | solution.py:586
  7.3 1.0 %backward_chunks.1 = (bf16[32,3840]{1,0:T(8,128)(2,1)S(1)}, bf16[32,3840]{1,0:T(8,128)(2,1)S(1)}, bf16[32,3840]{1,0:T(8,128)(2,1)S(1)}, bf16[32,3840]{1,0:T(8,128)(2,1)S(1)}, f32[8,3584]{1,0:T(8,128)S(1)}) custom-call(s32[2]{0:T(128)S(1)} %pad_add_fusion.where, bf16[80,64]{1,0:T(8,128)(2,1)S(1)} %get-tuple-element.37.selector, ...), custom_call_target="tpu_custom_call" | custom-call | flops 10000000000 | bytes 1000 | tf_op jit(solution)/shard_map/backward_chunks/pallas_call | solution.py:41
  8.3 3.0 %collective-permute-start.6 = (bf16[32,3840]{1,0:T(8,128)(2,1)S(1)}, bf16[32,3840]{1,0:T(8,128)(2,1)S(1)}, u32[]{:S(2)}, u32[]{:S(2)}) collective-permute-start(bf16[32,3840]{1,0:T(8,128)(2,1)S(1)} %get-tuple-element.51), channel_id=1, source_target_pairs={{0,6},{1,7},{2,4},{3,5},{4,2},{5,3},{6,0},{7,1},{8,14},{9,15},{10,... | collective-permute-start | bytes 737288 | tf_op jit(solution)/shard_map/ppermute | solution.py:586
  11.3 0.5 collective-permute-start.7
  12.0 1.0 %turned_down.1.refs_5_ = bf16[3584,512]{1,0:T(8,128)(2,1)S(1)} custom-call(bf16[1,512,3584]{2,1,0:T(8,128)(2,1)S(1)} %copy-done.1, bf16[1,3584,512]{2,1,0:T(8,128)(2,1)S(1)} %copy-done, bf16[32,3840]{1,0:T(8,128)(2,1)S(1)} %get-tuple-element.44.refs_1_.refs_0_.refs_2_, bf16[16,3840]{1,0:T(8,128)(2,1)S(1)} %collective-permute-done.refs_2_.refs_1_), custom_call_target="tpu_custom_call" | custom-call | flops 100000000 | bytes 1000 | tf_op jit(solution)/shard_map/turned_down/pallas_call | solution.py:41
  13.0 5.6 %collective-permute-done.1.refs_2_.refs_0_ = bf16[16,3840]{1,0:T(8,128)(2,1)S(1)} collective-permute-done((bf16[16,3840]{1,0:T(8,128)(2,1)S(1)}, bf16[16,3840]{1,0:T(8,128)(2,1)S(1)}, u32[]{:S(2)}, u32[]{:S(2)}) %collective-permute-start.1) | collective-permute-done | bytes 122912 | tf_op jit(solution)/shard_map/ppermute | solution.py:586
  18.6 0.5 normed_rows.1
  19.1 1.6 %saved_rows.1.refs_4_.ordered_ref = f32[160,512]{1,0:T(8,128)S(1)} custom-call(s32[2]{0:T(128)S(1)} %pad_add_fusion.where, bf16[1,1,136,512]{3,2,1,0:T(8,128)(2,1)} %saved_any.1, f32[80,128]{1,0:T(8,128)S(1)} %get-tuple-element.47.refs_0_.refs_5_.refs_4_), custom_call_target="tpu_custom_call" | custom-call | flops 15000000512 | bytes 1000 | tf_op jit(solution)/shard_map/saved_rows/pallas_call | solution.py:41
  20.8 0.3 collective-permute-done.3.refs_1_
  21.1 1.5 %experts_forward.1 = (bf16[80,3584]{1,0:T(8,128)(2,1)S(1)}, bf16[80,3584]{1,0:T(8,128)(2,1)S(1)}) custom-call(bf16[80,3584]{1,0:T(8,128)(2,1)S(1)} %get-tuple-element.46.refs_0_, bf16[80,3584]{1,0:T(8,128)(2,1)S(1)} %collective-permute-done.3.refs_1_, bf16[1,3584,512]{2,1,0:T(8,128)(2,1)S(1)} %copy-done, bf16[1,512,3584]{2,1,0:T(8,128)(2,1)S(1)} %copy-done.1, ...), custom_call_target="tpu_custom_call" | custom-call | flops 100000000 | bytes 1000 | tf_op jit(solution)/shard_map/experts_forward/pallas_call | solution.py:41
  22.6 0.3 collective-permute-start.4
  23.0 1.0 %turned_gate.1.refs_6_.refs_4_ = bf16[512,3584]{1,0:T(8,128)(2,1)S(1)} custom-call(bf16[1,3584,512]{2,1,0:T(8,128)(2,1)S(1)} %copy-done, bf16[160,512]{1,0:T(8,128)(2,1)S(1)} %get-tuple-element.50.refs_0_.refs_5_.refs_2_), custom_call_target="tpu_custom_call" | custom-call | flops 100000000 | bytes 1000 | tf_op jit(solution)/shard_map/turned_gate/pallas_call | solution.py:41
  24.0 0.7 %collective-permute-done.4.refs_4_.refs_3_ = bf16[80,3584]{1,0:T(8,128)(2,1)S(1)} collective-permute-done((bf16[80,3584]{1,0:T(8,128)(2,1)S(1)}, bf16[80,3584]{1,0:T(8,128)(2,1)S(1)}, u32[]{:S(2)}, u32[]{:S(2)}) %collective-permute-start.4) | collective-permute-done | bytes 573472 | tf_op jit(solution)/shard_map/ppermute | solution.py:596
  24.8 1.6 %collective-permute-start.5 = (bf16[32,3840]{1,0:T(8,128)(2,1)S(1)}, bf16[32,3840]{1,0:T(8,128)(2,1)S(1)}, u32[]{:S(2)}, u32[]{:S(2)}) collective-permute-start(bf16[32,3840]{1,0:T(8,128)(2,1)S(1)} %finish_forward_01.1.refs_6_), channel_id=1, source_target_pairs={{0,8},{1,9},{2,10},{3,11},{4,12},{5,13},{6,14},{7,15},{8,16},{9,17... | collective-permute-start | bytes 737288 | tf_op jit(solution)/shard_map/ppermute | solution.py:607
  26.6 3.5 %collective-permute-start.12 = (bf16[16,3840]{1,0:T(8,128)(2,1)S(1)}, bf16[16,3840]{1,0:T(8,128)(2,1)S(1)}, u32[]{:S(2)}, u32[]{:S(2)}) collective-permute-start(bf16[16,3840]{1,0:T(8,128)(2,1)S(1)} %finish_forward_2.1.refs_4_), channel_id=1, source_target_pairs={{0,12},{1,13},{2,14},{3,15},{4,8},{5,9},{6,10},{7,11},{8,20},{9,21... | collective-permute-start | bytes 368648 | tf_op jit(solution)/shard_map/ppermute | solution.py:607
  30.8 1.5 %collective-permute-done.9.refs_1_ = bf16[80,3584]{1,0:T(8,128)(2,1)S(1)} collective-permute-done((bf16[80,3584]{1,0:T(8,128)(2,1)S(1)}, bf16[80,3584]{1,0:T(8,128)(2,1)S(1)}, u32[]{:S(2)}, u32[]{:S(2)}) %collective-permute-start.9) | collective-permute-done | bytes 573472 | tf_op jit(solution)/shard_map/ppermute | solution.py:596
  32.3 1.5 %experts_backward.1 = (bf16[80,3712]{1,0:T(8,128)(2,1)S(1)}, bf16[80,3712]{1,0:T(8,128)(2,1)S(1)}) custom-call(bf16[80,3584]{1,0:T(8,128)(2,1)S(1)} %get-tuple-element.55.refs_4_.refs_0_, bf16[80,3584]{1,0:T(8,128)(2,1)S(1)} %collective-permute-done.9.refs_1_, bf16[160,512]{1,0:T(8,128)(2,1)S(1)} %get-tuple-element.50.refs_0_.refs_5_.refs_2_, ...), custom_call_target="tpu_custom_call" | custom-call | flops 100000000 | bytes 1000 | tf_op jit(solution)/shard_map/experts_backward/pallas_call | solution.py:41
  34.0 0.4 act_gates.1.refs_4_.refs_6_
  34.4 1.5 %collective-permute-done.10.refs_6_.refs_8_ = bf16[80,3712]{1,0:T(8,128)(2,1)S(1)} collective-permute-done((bf16[80,3712]{1,0:T(8,128)(2,1)S(1)}, bf16[80,3712]{1,0:T(8,128)(2,1)S(1)}, u32[]{:S(2)}, u32[]{:S(2)}) %collective-permute-start.10) | collective-permute-done | bytes 593952 | tf_op jit(solution)/shard_map/ppermute | solution.py:596
  35.9 0.3 finish_backward_1.1.refs_10_
  36.2 2.2 %collective-permute-start.15 = (bf16[16,3840]{1,0:T(8,128)(2,1)S(1)}, bf16[16,3840]{1,0:T(8,128)(2,1)S(1)}, u32[]{:S(2)}, u32[]{:S(2)}) collective-permute-start(bf16[16,3840]{1,0:T(8,128)(2,1)S(1)} %finish_backward_1.1.refs_10_), channel_id=1, source_target_pairs={{0,26},{1,27},{2,24},{3,25},{4,30},{5,31},{6,28},{7,29},{8,2},{9,3... | collective-permute-start | bytes 368648 | tf_op jit(solution)/shard_map/ppermute | solution.py:607
  38.5 0.5 %finish_backward_320.1 = (bf16[16,3840]{1,0:T(8,128)(2,1)S(1)}, bf16[16,3840]{1,0:T(8,128)(2,1)S(1)}, bf16[16,3840]{1,0:T(8,128)(2,1)S(1)}) custom-call(bf16[32,3840]{1,0:T(8,128)(2,1)S(1)} %collective-permute-done.6.refs_3_.refs_0_, bf16[32,3840]{1,0:T(8,128)(2,1)S(1)} %collective-permute-done.7.refs_2_.refs_1_, ...), custom_call_target="tpu_custom_call" | custom-call | flops 100000000 | bytes 1000 | tf_op jit(solution)/shard_map/finish_backward_320/pallas_call | solution.py:41
  39.0 2.4 %collective-permute-start.16 = (bf16[16,3840]{1,0:T(8,128)(2,1)S(1)}, bf16[16,3840]{1,0:T(8,128)(2,1)S(1)}, u32[]{:S(2)}, u32[]{:S(2)}) collective-permute-start(bf16[16,3840]{1,0:T(8,128)(2,1)S(1)} %get-tuple-element.62), channel_id=1, source_target_pairs={{0,28},{1,29},{2,30},{3,31},{4,24},{5,25},{6,26},{7,27},{8,4},{9,5... | collective-permute-start | bytes 368648 | tf_op jit(solution)/shard_map/ppermute | solution.py:607
  41.4 1.7 %collective-permute-start.14 = (bf16[16,3840]{1,0:T(8,128)(2,1)S(1)}, bf16[16,3840]{1,0:T(8,128)(2,1)S(1)}, u32[]{:S(2)}, u32[]{:S(2)}) collective-permute-start(bf16[16,3840]{1,0:T(8,128)(2,1)S(1)} %get-tuple-element.61.refs_0_), channel_id=1, source_target_pairs={{0,30},{1,31},{2,28},{3,29},{4,26},{5,27},{6,24},{7,25},{8,6},{9,7... | collective-permute-start | bytes 368648 | tf_op jit(solution)/shard_map/ppermute | solution.py:607
  43.2 0.5 collective-permute-start.17
  43.7 0.5 collective-permute-start.11
  44.2 0.3 forward_rows_early.1.refs_1_
  44.5 3.7 %collective-permute-done.16.refs_4_ = bf16[16,3840]{1,0:T(8,128)(2,1)S(1)} collective-permute-done((bf16[16,3840]{1,0:T(8,128)(2,1)S(1)}, bf16[16,3840]{1,0:T(8,128)(2,1)S(1)}, u32[]{:S(2)}, u32[]{:S(2)}) %collective-permute-start.16) | collective-permute-done | bytes 122912 | tf_op jit(solution)/shard_map/ppermute | solution.py:607
  48.2 3.2 %collective-permute-done.17.refs_5_ = bf16[16,3840]{1,0:T(8,128)(2,1)S(1)} collective-permute-done((bf16[16,3840]{1,0:T(8,128)(2,1)S(1)}, bf16[16,3840]{1,0:T(8,128)(2,1)S(1)}, u32[]{:S(2)}, u32[]{:S(2)}) %collective-permute-start.17) | collective-permute-done | bytes 122912 | tf_op jit(solution)/shard_map/ppermute | solution.py:607
  51.4 1.2 %all_rows.1 = (bf16[64,3584]{1,0:T(8,128)(2,1)}, bf16[64,3584]{1,0:T(8,128)(2,1)}) custom-call(bf16[16,3840]{1,0:T(8,128)(2,1)S(1)} %collective-permute-done.11.refs_0_, bf16[64,3584]{1,0:T(8,128)(2,1)S(1)} %forward_rows_early.1.refs_1_, bf16[16,3840]{1,0:T(8,128)(2,1)S(1)} %collective-permute-done.14.refs_2_, ...), custom_call_target="tpu_custom_call" | custom-call | flops 100000000 | bytes 1000 | tf_op jit(solution)/shard_map/all_rows/pallas_call | solution.py:41
  (29 shorter events, 1.7 us)
Async XLA Ops:
  2.8 9.0 %collective-permute-start = (bf16[16,3840]{1,0:T(8,128)(2,1)S(1)}, bf16[16,3840]{1,0:T(8,128)(2,1)S(1)}, u32[]{:S(2)}, u32[]{:S(2)}) collective-permute-start(bf16[16,3840]{1,0:T(8,128)(2,1)S(1)} %get-tuple-element.34), channel_id=1, source_target_pairs={{0,2},{1,3},{2,0},{3,1},{4,6},{5,7},{6,4},{7,5},{8,10},{9,11},{10,... | collective-permute-start | bytes 368648 | tf_op jit(solution)/shard_map/ppermute | solution.py:586
  5.8 12.8 %collective-permute-start.1 = (bf16[16,3840]{1,0:T(8,128)(2,1)S(1)}, bf16[16,3840]{1,0:T(8,128)(2,1)S(1)}, u32[]{:S(2)}, u32[]{:S(2)}) collective-permute-start(bf16[16,3840]{1,0:T(8,128)(2,1)S(1)} %get-tuple-element.35), channel_id=1, source_target_pairs={{0,4},{1,5},{2,6},{3,7},{4,0},{5,1},{6,2},{7,3},{8,12},{9,13},{10,... | collective-permute-start | bytes 368648 | tf_op jit(solution)/shard_map/ppermute | solution.py:586
  7.3 11.3 %collective-permute-start.2 = (bf16[16,3840]{1,0:T(8,128)(2,1)S(1)}, bf16[16,3840]{1,0:T(8,128)(2,1)S(1)}, u32[]{:S(2)}, u32[]{:S(2)}) collective-permute-start(bf16[16,3840]{1,0:T(8,128)(2,1)S(1)} %get-tuple-element.36), channel_id=1, source_target_pairs={{0,6},{1,7},{2,4},{3,5},{4,2},{5,3},{6,0},{7,1},{8,14},{9,15},{10,... | collective-permute-start | bytes 368648 | tf_op jit(solution)/shard_map/ppermute | solution.py:586
  7.3 4.7 %copy-start = (bf16[1,3584,512]{2,1,0:T(8,128)(2,1)S(1)}, bf16[1,3584,512]{2,1,0:T(8,128)(2,1)}, u32[]{:S(2)}) copy-start(bf16[1,3584,512]{2,1,0:T(8,128)(2,1)} %weights_ref.3) | copy-start | bytes 11010052
  7.3 4.7 %copy-start.1 = (bf16[1,512,3584]{2,1,0:T(8,128)(2,1)S(1)}, bf16[1,512,3584]{2,1,0:T(8,128)(2,1)}, u32[]{:S(2)}) copy-start(bf16[1,512,3584]{2,1,0:T(8,128)(2,1)} %refs_3_.1) | copy-start | bytes 11010052
  8.3 21.8 %collective-permute-start.6 = (bf16[32,3840]{1,0:T(8,128)(2,1)S(1)}, bf16[32,3840]{1,0:T(8,128)(2,1)S(1)}, u32[]{:S(2)}, u32[]{:S(2)}) collective-permute-start(bf16[32,3840]{1,0:T(8,128)(2,1)S(1)} %get-tuple-element.51), channel_id=1, source_target_pairs={{0,6},{1,7},{2,4},{3,5},{4,2},{5,3},{6,0},{7,1},{8,14},{9,15},{10,... | collective-permute-start | bytes 737288 | tf_op jit(solution)/shard_map/ppermute | solution.py:586
  11.3 18.9 %collective-permute-start.7 = (bf16[32,3840]{1,0:T(8,128)(2,1)S(1)}, bf16[32,3840]{1,0:T(8,128)(2,1)S(1)}, u32[]{:S(2)}, u32[]{:S(2)}) collective-permute-start(bf16[32,3840]{1,0:T(8,128)(2,1)S(1)} %get-tuple-element.52), channel_id=1, source_target_pairs={{0,4},{1,5},{2,6},{3,7},{4,0},{5,1},{6,2},{7,3},{8,12},{9,13},{10,... | collective-permute-start | bytes 737288 | tf_op jit(solution)/shard_map/ppermute | solution.py:586
  11.8 18.4 %collective-permute-start.8 = (bf16[32,3840]{1,0:T(8,128)(2,1)S(1)}, bf16[32,3840]{1,0:T(8,128)(2,1)S(1)}, u32[]{:S(2)}, u32[]{:S(2)}) collective-permute-start(bf16[32,3840]{1,0:T(8,128)(2,1)S(1)} %get-tuple-element.53), channel_id=1, source_target_pairs={{0,2},{1,3},{2,0},{3,1},{4,6},{5,7},{6,4},{7,5},{8,10},{9,11},{10,... | collective-permute-start | bytes 737288 | tf_op jit(solution)/shard_map/ppermute | solution.py:586
  19.1 2.0 %collective-permute-start.3 = (bf16[80,3584]{1,0:T(8,128)(2,1)S(1)}, bf16[80,3584]{1,0:T(8,128)(2,1)S(1)}, u32[]{:S(2)}, u32[]{:S(2)}) collective-permute-start(bf16[80,3584]{1,0:T(8,128)(2,1)S(1)} %get-tuple-element.46.refs_0_), channel_id=1, source_target_pairs={{0,1},{1,0},{2,3},{3,2},{4,5},{5,4},{6,7},{7,6},{8,9},{9,8},{10,11... | collective-permute-start | bytes 1720328 | tf_op jit(solution)/shard_map/ppermute | solution.py:596
  22.6 2.0 %collective-permute-start.4 = (bf16[80,3584]{1,0:T(8,128)(2,1)S(1)}, bf16[80,3584]{1,0:T(8,128)(2,1)S(1)}, u32[]{:S(2)}, u32[]{:S(2)}) collective-permute-start(bf16[80,3584]{1,0:T(8,128)(2,1)S(1)} %get-tuple-element.49), channel_id=1, source_target_pairs={{0,1},{1,0},{2,3},{3,2},{4,5},{5,4},{6,7},{7,6},{8,9},{9,8},{10,11... | collective-permute-start | bytes 1720328 | tf_op jit(solution)/shard_map/ppermute | solution.py:596
  24.8 16.6 %collective-permute-start.5 = (bf16[32,3840]{1,0:T(8,128)(2,1)S(1)}, bf16[32,3840]{1,0:T(8,128)(2,1)S(1)}, u32[]{:S(2)}, u32[]{:S(2)}) collective-permute-start(bf16[32,3840]{1,0:T(8,128)(2,1)S(1)} %finish_forward_01.1.refs_6_), channel_id=1, source_target_pairs={{0,8},{1,9},{2,10},{3,11},{4,12},{5,13},{6,14},{7,15},{8,16},{9,17... | collective-permute-start | bytes 737288 | tf_op jit(solution)/shard_map/ppermute | solution.py:607
  26.6 16.6 %collective-permute-start.12 = (bf16[16,3840]{1,0:T(8,128)(2,1)S(1)}, bf16[16,3840]{1,0:T(8,128)(2,1)S(1)}, u32[]{:S(2)}, u32[]{:S(2)}) collective-permute-start(bf16[16,3840]{1,0:T(8,128)(2,1)S(1)} %finish_forward_2.1.refs_4_), channel_id=1, source_target_pairs={{0,12},{1,13},{2,14},{3,15},{4,8},{5,9},{6,10},{7,11},{8,20},{9,21... | collective-permute-start | bytes 368648 | tf_op jit(solution)/shard_map/ppermute | solution.py:607
  30.3 2.0 %collective-permute-start.9 = (bf16[80,3584]{1,0:T(8,128)(2,1)S(1)}, bf16[80,3584]{1,0:T(8,128)(2,1)S(1)}, u32[]{:S(2)}, u32[]{:S(2)}) collective-permute-start(bf16[80,3584]{1,0:T(8,128)(2,1)S(1)} %get-tuple-element.55.refs_4_.refs_0_), channel_id=1, source_target_pairs={{0,1},{1,0},{2,3},{3,2},{4,5},{5,4},{6,7},{7,6},{8,9},{9,8},{10,11... | collective-permute-start | bytes 1720328 | tf_op jit(solution)/shard_map/ppermute | solution.py:596
  30.7 12.9 %collective-permute-start.13 = (bf16[16,3840]{1,0:T(8,128)(2,1)S(1)}, bf16[16,3840]{1,0:T(8,128)(2,1)S(1)}, u32[]{:S(2)}, u32[]{:S(2)}) collective-permute-start(bf16[16,3840]{1,0:T(8,128)(2,1)S(1)} %finish_forward_3.1), channel_id=1, source_target_pairs={{0,14},{1,15},{2,12},{3,13},{4,10},{5,11},{6,8},{7,9},{8,22},{9,23... | collective-permute-start | bytes 368648 | tf_op jit(solution)/shard_map/ppermute | solution.py:607
  33.8 2.1 %collective-permute-start.10 = (bf16[80,3712]{1,0:T(8,128)(2,1)S(1)}, bf16[80,3712]{1,0:T(8,128)(2,1)S(1)}, u32[]{:S(2)}, u32[]{:S(2)}) collective-permute-start(bf16[80,3712]{1,0:T(8,128)(2,1)S(1)} %get-tuple-element.60), channel_id=1, source_target_pairs={{0,1},{1,0},{2,3},{3,2},{4,5},{5,4},{6,7},{7,6},{8,9},{9,8},{10,11... | collective-permute-start | bytes 1781768 | tf_op jit(solution)/shard_map/ppermute | solution.py:596
  36.2 15.2 %collective-permute-start.15 = (bf16[16,3840]{1,0:T(8,128)(2,1)S(1)}, bf16[16,3840]{1,0:T(8,128)(2,1)S(1)}, u32[]{:S(2)}, u32[]{:S(2)}) collective-permute-start(bf16[16,3840]{1,0:T(8,128)(2,1)S(1)} %finish_backward_1.1.refs_10_), channel_id=1, source_target_pairs={{0,26},{1,27},{2,24},{3,25},{4,30},{5,31},{6,28},{7,29},{8,2},{9,3... | collective-permute-start | bytes 368648 | tf_op jit(solution)/shard_map/ppermute | solution.py:607
  39.0 9.2 %collective-permute-start.16 = (bf16[16,3840]{1,0:T(8,128)(2,1)S(1)}, bf16[16,3840]{1,0:T(8,128)(2,1)S(1)}, u32[]{:S(2)}, u32[]{:S(2)}) collective-permute-start(bf16[16,3840]{1,0:T(8,128)(2,1)S(1)} %get-tuple-element.62), channel_id=1, source_target_pairs={{0,28},{1,29},{2,30},{3,31},{4,24},{5,25},{6,26},{7,27},{8,4},{9,5... | collective-permute-start | bytes 368648 | tf_op jit(solution)/shard_map/ppermute | solution.py:607
  41.4 10.0 %collective-permute-start.14 = (bf16[16,3840]{1,0:T(8,128)(2,1)S(1)}, bf16[16,3840]{1,0:T(8,128)(2,1)S(1)}, u32[]{:S(2)}, u32[]{:S(2)}) collective-permute-start(bf16[16,3840]{1,0:T(8,128)(2,1)S(1)} %get-tuple-element.61.refs_0_), channel_id=1, source_target_pairs={{0,30},{1,31},{2,28},{3,29},{4,26},{5,27},{6,24},{7,25},{8,6},{9,7... | collective-permute-start | bytes 368648 | tf_op jit(solution)/shard_map/ppermute | solution.py:607
  43.2 8.2 %collective-permute-start.17 = (bf16[16,3840]{1,0:T(8,128)(2,1)S(1)}, bf16[16,3840]{1,0:T(8,128)(2,1)S(1)}, u32[]{:S(2)}, u32[]{:S(2)}) collective-permute-start(bf16[16,3840]{1,0:T(8,128)(2,1)S(1)} %get-tuple-element.63), channel_id=1, source_target_pairs={{0,24},{1,25},{2,26},{3,27},{4,28},{5,29},{6,30},{7,31},{8,0},{9,1... | collective-permute-start | bytes 368648 | tf_op jit(solution)/shard_map/ppermute | solution.py:607
  43.7 7.7 %collective-permute-start.11 = (bf16[16,3840]{1,0:T(8,128)(2,1)S(1)}, bf16[16,3840]{1,0:T(8,128)(2,1)S(1)}, u32[]{:S(2)}, u32[]{:S(2)}) collective-permute-start(bf16[16,3840]{1,0:T(8,128)(2,1)S(1)} %lower_chunk.1), channel_id=1, source_target_pairs={{0,2},{1,3},{2,0},{3,1},{4,6},{5,7},{6,4},{7,5},{8,10},{9,11},{10,... | collective-permute-start | bytes 368648 | tf_op jit(solution)/shard_map/ppermute | solution.py:586

commit v17 on v16

--- a/solution.py
+++ b/solution.py
@@ -471,9 +471,10 @@
     count = len(ks)
 
     def body(*refs):
-        chunks = refs[:count]
-        last_grad, last_act, inv_ref, affinity_ref = refs[count : count + 4]
-        parts, vectors = refs[count + 4 : count + 4 + z.split], refs[count + 4 + z.split]
+        e = z.experts
+        chunks = [refs[k] for k in ks]
+        last_grad, last_act, inv_ref, affinity_ref = refs[e : e + 4]
+        parts, vectors = refs[e + 4 : e + 4 + z.split], refs[e + 4 + z.split]
         outs, tile = refs[-1 - count : -1], refs[-1]
         gain, router = vectors[0:1, :], vectors[1:2, :]
 
@@ -499,12 +500,12 @@
 
     return call(
         body,
-        "v" * (count + z.split + 5) + "a" * len(after),
+        "v" * (z.experts + z.split + 5) + "a" * len(after),
         [shape((z.main, z.wide))] * count,
         [pltpu.VMEM((16, fold), f32)],
         8,
         "finish_backward_" + "".join(map(str, ks)),
-    )(*[chunks[k] for k in ks], *lasts, *terms, *parts, vectors, *after)
+    )(*chunks, *lasts, *terms, *parts, vectors, *after)
 
 
 def ordered_columns(z, chunks):

time: 52.8 us -> 47.9 us (0.907)
  waiting for transfers between devices: 16.5 us -> 9.13 us
  starting transfers between devices: 21.4 us -> 24 us
    ppermute x7, waiting for transfers between devices: 5.6 us -> 0.52 us  [permute_blocks(): return [lax.ppermute(array, 'ep', pairs) for array in arrays]]
    ppermute x4, waiting for transfers between devices: 3.99 us -> 2.41 us  [to_core(): return lax.ppermute(array, 'ep', pairs)]
    ppermute x7, starting transfers between devices: 8.72 us -> 10.1 us  [permute_blocks(): return [lax.ppermute(array, 'ep', pairs) for array in arrays]]
    ppermute x7, starting transfers between devices: 12.1 us -> 13.2 us  [to_section(): return lax.ppermute(chunk, ('pp', 'ep'), pairs)]
    ppermute x7, waiting for transfers between devices: 6.93 us -> 6.2 us  [to_section(): return lax.ppermute(chunk, ('pp', 'ep'), pairs)]
  transfers between devices with their start and end apart: 18 -> 18, of which waited for: 7 -> 6; matrix products, arithmetic and copies ran while one was open for 0% -> 0% of each run, Pallas kernels for 20% -> 22%
where the time goes in v17:
time: 47.9 us; the launch traced here: 47.8 us
  starting transfers between devices  24 us (50%)
  Pallas kernels  13.8 us (29%)
  waiting for transfers between devices  9.13 us (19%)
  between operations  0.79 us (2%)
    pallas_call x20, Pallas kernels, run(): return kernel(*arrays)  13.8 us
    ppermute x7, starting transfers between devices, to_section(): return lax.ppermute(chunk, ('pp', 'ep'), pairs)  13.2 us
    ppermute x7, starting transfers between devices, permute_blocks(): return [lax.ppermute(array, 'ep', pairs) for array in arrays]  10.1 us
    ppermute x7, waiting for transfers between devices, to_section(): return lax.ppermute(chunk, ('pp', 'ep'), pairs)  6.2 us
    ppermute x4, waiting for transfers between devices, to_core(): return lax.ppermute(array, 'ep', pairs)  2.41 us
  transfers between devices with their start and end apart: 18, of which 6 were waited for; matrix products, arithmetic and copies ran while one was open for 0% of the time, Pallas kernels for 22%

profile of v17, /device:TPU:0, one launch (start us, length us, event | category | flops | bytes accessed | tf_op | source)
XLA Modules:
  0.0 47.8 jit_solution(3804524947831992302)
XLA Ops:
  0.7 2.0 %forward_chunks.1 = (bf16[16,3840]{1,0:T(8,128)(2,1)S(1)}, bf16[16,3840]{1,0:T(8,128)(2,1)S(1)}, bf16[16,3840]{1,0:T(8,128)(2,1)S(1)}, bf16[16,3840]{1,0:T(8,128...) custom-call(s32[2]{0:T(128)S(1)} %pad_add_fusion.where, ...), custom_call_target="tpu_custom_call" | custom-call | flops 100000000 | bytes 1000 | tf_op jit(solution)/shard_map/forward_chunks/pallas_call | solution.py:41
  2.8 3.0 %collective-permute-start = (bf16[16,3840]{1,0:T(8,128)(2,1)S(1)}, bf16[16,3840]{1,0:T(8,128)(2,1)S(1)}, u32[]{:S(2)}, u32[]{:S(2)}) collective-permute-start(bf16[16,3840]{1,0:T(8,128)(2,1)S(1)} %get-tuple-element.34), channel_id=1, source_target_pairs={{0,2},{1,3},{2,0},{3,1},{4,6},{5,7},{6,4},{7,5},{8,10},{9,11},{10,... | collective-permute-start | bytes 368648 | tf_op jit(solution)/shard_map/ppermute | solution.py:587
  5.8 1.5 %collective-permute-start.1 = (bf16[16,3840]{1,0:T(8,128)(2,1)S(1)}, bf16[16,3840]{1,0:T(8,128)(2,1)S(1)}, u32[]{:S(2)}, u32[]{:S(2)}) collective-permute-start(bf16[16,3840]{1,0:T(8,128)(2,1)S(1)} %get-tuple-element.35), channel_id=1, source_target_pairs={{0,4},{1,5},{2,6},{3,7},{4,0},{5,1},{6,2},{7,3},{8,12},{9,13},{10,... | collective-permute-start | bytes 368648 | tf_op jit(solution)/shard_map/ppermute | solution.py:587
  7.3 1.0 %backward_chunks.1 = (bf16[32,3840]{1,0:T(8,128)(2,1)S(1)}, bf16[32,3840]{1,0:T(8,128)(2,1)S(1)}, bf16[32,3840]{1,0:T(8,128)(2,1)S(1)}, bf16[32,3840]{1,0:T(8,128)(2,1)S(1)}, f32[8,3584]{1,0:T(8,128)S(1)}) custom-call(s32[2]{0:T(128)S(1)} %pad_add_fusion.where, bf16[80,64]{1,0:T(8,128)(2,1)S(1)} %get-tuple-element.37.selector, ...), custom_call_target="tpu_custom_call" | custom-call | flops 10000000000 | bytes 1000 | tf_op jit(solution)/shard_map/backward_chunks/pallas_call | solution.py:41
  8.3 2.0 %collective-permute-start.6 = (bf16[32,3840]{1,0:T(8,128)(2,1)S(1)}, bf16[32,3840]{1,0:T(8,128)(2,1)S(1)}, u32[]{:S(2)}, u32[]{:S(2)}) collective-permute-start(bf16[32,3840]{1,0:T(8,128)(2,1)S(1)} %get-tuple-element.51), channel_id=1, source_target_pairs={{0,2},{1,3},{2,0},{3,1},{4,6},{5,7},{6,4},{7,5},{8,10},{9,11},{10,... | collective-permute-start | bytes 737288 | tf_op jit(solution)/shard_map/ppermute | solution.py:587
  10.3 1.5 %collective-permute-start.7 = (bf16[32,3840]{1,0:T(8,128)(2,1)S(1)}, bf16[32,3840]{1,0:T(8,128)(2,1)S(1)}, u32[]{:S(2)}, u32[]{:S(2)}) collective-permute-start(bf16[32,3840]{1,0:T(8,128)(2,1)S(1)} %get-tuple-element.52), channel_id=1, source_target_pairs={{0,4},{1,5},{2,6},{3,7},{4,0},{5,1},{6,2},{7,3},{8,12},{9,13},{10,... | collective-permute-start | bytes 737288 | tf_op jit(solution)/shard_map/ppermute | solution.py:587
  11.9 1.1 %collective-permute-start.8 = (bf16[32,3840]{1,0:T(8,128)(2,1)S(1)}, bf16[32,3840]{1,0:T(8,128)(2,1)S(1)}, u32[]{:S(2)}, u32[]{:S(2)}) collective-permute-start(bf16[32,3840]{1,0:T(8,128)(2,1)S(1)} %get-tuple-element.53), channel_id=1, source_target_pairs={{0,6},{1,7},{2,4},{3,5},{4,2},{5,3},{6,0},{7,1},{8,14},{9,15},{10,... | collective-permute-start | bytes 737288 | tf_op jit(solution)/shard_map/ppermute | solution.py:587
  13.0 1.0 %turned_down.1.refs_5_ = bf16[3584,512]{1,0:T(8,128)(2,1)S(1)} custom-call(bf16[1,512,3584]{2,1,0:T(8,128)(2,1)S(1)} %copy-done.1, bf16[1,3584,512]{2,1,0:T(8,128)(2,1)S(1)} %copy-done, bf16[32,3840]{1,0:T(8,128)(2,1)S(1)} %get-tuple-element.44.refs_1_.refs_0_, bf16[16,3840]{1,0:T(8,128)(2,1)S(1)} %collective-permute-done.refs_2_.refs_1_), custom_call_target="tpu_custom_call" | custom-call | flops 100000000 | bytes 1000 | tf_op jit(solution)/shard_map/turned_down/pallas_call | solution.py:41
  14.0 0.5 %collective-permute-done.2.refs_3_.refs_0_ = bf16[16,3840]{1,0:T(8,128)(2,1)S(1)} collective-permute-done((bf16[16,3840]{1,0:T(8,128)(2,1)S(1)}, bf16[16,3840]{1,0:T(8,128)(2,1)S(1)}, u32[]{:S(2)}, u32[]{:S(2)}) %collective-permute-start.2) | collective-permute-done | bytes 122912 | tf_op jit(solution)/shard_map/ppermute | solution.py:587
  14.5 0.5 %normed_rows.1 = (bf16[80,3584]{1,0:T(8,128)(2,1)S(1)}, f32[80,128]{1,0:T(8,128)S(1)}, f32[16,3584]{1,0:T(8,128)S(1)}) custom-call(bf16[16,3840]{1,0:T(8,128)(2,1)S(1)} %get-tuple-element.33.refs_0_, bf16[16,3840]{1,0:T(8,128)(2,1)S(1)} %collective-permute-done.refs_2_.refs_1_, bf16[16,3840]{1,0:T(8,128)(2,1)S(1)} %collective-permute-done.1.refs_2_.refs_0_, ...), custom_call_target="tpu_custom_call" | custom-call | flops 100000000 | bytes 1000 | tf_op jit(solution)/shard_map/normed_rows/pallas_call | solution.py:41
  15.0 1.6 %saved_rows.1.refs_4_.ordered_ref = f32[160,512]{1,0:T(8,128)S(1)} custom-call(s32[2]{0:T(128)S(1)} %pad_add_fusion.where, bf16[1,1,136,512]{3,2,1,0:T(8,128)(2,1)} %saved_any.1, f32[80,128]{1,0:T(8,128)S(1)} %get-tuple-element.47.refs_0_.refs_5_.refs_4_), custom_call_target="tpu_custom_call" | custom-call | flops 15000000512 | bytes 1000 | tf_op jit(solution)/shard_map/saved_rows/pallas_call | solution.py:41
  16.7 0.3 collective-permute-done.3.refs_1_
  17.0 1.5 %experts_forward.1 = (bf16[80,3584]{1,0:T(8,128)(2,1)S(1)}, bf16[80,3584]{1,0:T(8,128)(2,1)S(1)}) custom-call(bf16[80,3584]{1,0:T(8,128)(2,1)S(1)} %get-tuple-element.46.refs_0_, bf16[80,3584]{1,0:T(8,128)(2,1)S(1)} %collective-permute-done.3.refs_1_, bf16[1,3584,512]{2,1,0:T(8,128)(2,1)S(1)} %copy-done, bf16[1,512,3584]{2,1,0:T(8,128)(2,1)S(1)} %copy-done.1, ...), custom_call_target="tpu_custom_call" | custom-call | flops 100000000 | bytes 1000 | tf_op jit(solution)/shard_map/experts_forward/pallas_call | solution.py:41
  18.8 1.0 %turned_gate.1.refs_6_.refs_4_ = bf16[512,3584]{1,0:T(8,128)(2,1)S(1)} custom-call(bf16[1,3584,512]{2,1,0:T(8,128)(2,1)S(1)} %copy-done, bf16[160,512]{1,0:T(8,128)(2,1)S(1)} %get-tuple-element.50.refs_0_.refs_5_.refs_2_), custom_call_target="tpu_custom_call" | custom-call | flops 100000000 | bytes 1000 | tf_op jit(solution)/shard_map/turned_gate/pallas_call | solution.py:41
  19.8 0.7 %collective-permute-done.4.refs_4_.refs_3_ = bf16[80,3584]{1,0:T(8,128)(2,1)S(1)} collective-permute-done((bf16[80,3584]{1,0:T(8,128)(2,1)S(1)}, bf16[80,3584]{1,0:T(8,128)(2,1)S(1)}, u32[]{:S(2)}, u32[]{:S(2)}) %collective-permute-start.4) | collective-permute-done | bytes 573472 | tf_op jit(solution)/shard_map/ppermute | solution.py:597
  20.7 1.6 %collective-permute-start.5 = (bf16[32,3840]{1,0:T(8,128)(2,1)S(1)}, bf16[32,3840]{1,0:T(8,128)(2,1)S(1)}, u32[]{:S(2)}, u32[]{:S(2)}) collective-permute-start(bf16[32,3840]{1,0:T(8,128)(2,1)S(1)} %finish_forward_01.1.refs_6_), channel_id=1, source_target_pairs={{0,8},{1,9},{2,10},{3,11},{4,12},{5,13},{6,14},{7,15},{8,16},{9,17... | collective-permute-start | bytes 737288 | tf_op jit(solution)/shard_map/ppermute | solution.py:608
  22.5 1.9 %collective-permute-start.12 = (bf16[16,3840]{1,0:T(8,128)(2,1)S(1)}, bf16[16,3840]{1,0:T(8,128)(2,1)S(1)}, u32[]{:S(2)}, u32[]{:S(2)}) collective-permute-start(bf16[16,3840]{1,0:T(8,128)(2,1)S(1)} %finish_forward_2.1.refs_4_), channel_id=1, source_target_pairs={{0,12},{1,13},{2,14},{3,15},{4,8},{5,9},{6,10},{7,11},{8,20},{9,21... | collective-permute-start | bytes 368648 | tf_op jit(solution)/shard_map/ppermute | solution.py:608
  25.0 2.8 %collective-permute-start.13 = (bf16[16,3840]{1,0:T(8,128)(2,1)S(1)}, bf16[16,3840]{1,0:T(8,128)(2,1)S(1)}, u32[]{:S(2)}, u32[]{:S(2)}) collective-permute-start(bf16[16,3840]{1,0:T(8,128)(2,1)S(1)} %finish_forward_3.1), channel_id=1, source_target_pairs={{0,14},{1,15},{2,12},{3,13},{4,10},{5,11},{6,8},{7,9},{8,22},{9,23... | collective-permute-start | bytes 368648 | tf_op jit(solution)/shard_map/ppermute | solution.py:608
  27.8 1.5 %experts_backward.1 = (bf16[80,3712]{1,0:T(8,128)(2,1)S(1)}, bf16[80,3712]{1,0:T(8,128)(2,1)S(1)}) custom-call(bf16[80,3584]{1,0:T(8,128)(2,1)S(1)} %get-tuple-element.55.refs_4_.refs_0_, bf16[80,3584]{1,0:T(8,128)(2,1)S(1)} %collective-permute-done.9.refs_1_, bf16[160,512]{1,0:T(8,128)(2,1)S(1)} %get-tuple-element.50.refs_0_.refs_5_.refs_2_, ...), custom_call_target="tpu_custom_call" | custom-call | flops 100000000 | bytes 1000 | tf_op jit(solution)/shard_map/experts_backward/pallas_call | solution.py:41
  29.3 0.3 collective-permute-start.10
  29.5 0.4 act_gates.1.refs_7_
  29.9 1.4 %collective-permute-done.10.refs_9_ = bf16[80,3712]{1,0:T(8,128)(2,1)S(1)} collective-permute-done((bf16[80,3712]{1,0:T(8,128)(2,1)S(1)}, bf16[80,3712]{1,0:T(8,128)(2,1)S(1)}, u32[]{:S(2)}, u32[]{:S(2)}) %collective-permute-start.10) | collective-permute-done | bytes 593952 | tf_op jit(solution)/shard_map/ppermute | solution.py:597
  31.3 0.3 finish_backward_1.1.refs_11_
  31.7 2.6 %collective-permute-start.15 = (bf16[16,3840]{1,0:T(8,128)(2,1)S(1)}, bf16[16,3840]{1,0:T(8,128)(2,1)S(1)}, u32[]{:S(2)}, u32[]{:S(2)}) collective-permute-start(bf16[16,3840]{1,0:T(8,128)(2,1)S(1)} %finish_backward_1.1.refs_11_), channel_id=1, source_target_pairs={{0,26},{1,27},{2,24},{3,25},{4,30},{5,31},{6,28},{7,29},{8,2},{9,3... | collective-permute-start | bytes 368648 | tf_op jit(solution)/shard_map/ppermute | solution.py:608
  34.3 0.5 %finish_backward_320.1 = (bf16[16,3840]{1,0:T(8,128)(2,1)S(1)}, bf16[16,3840]{1,0:T(8,128)(2,1)S(1)}, bf16[16,3840]{1,0:T(8,128)(2,1)S(1)}) custom-call(bf16[32,3840]{1,0:T(8,128)(2,1)S(1)} %get-tuple-element.44.refs_1_.refs_0_, bf16[32,3840]{1,0:T(8,128)(2,1)S(1)} %collective-permute-done.6.refs_1_, bf16[32,3840]{1,0:T(8,128)(2,1)S(1)} %collective-permute-done.7.refs_2_, ...), custom_call_target="tpu_custom_call" | custom-call | flops 100000000 | bytes 1000 | tf_op jit(solution)/shard_map/finish_backward_320/pallas_call | solution.py:41
  34.9 1.6 %collective-permute-start.16 = (bf16[16,3840]{1,0:T(8,128)(2,1)S(1)}, bf16[16,3840]{1,0:T(8,128)(2,1)S(1)}, u32[]{:S(2)}, u32[]{:S(2)}) collective-permute-start(bf16[16,3840]{1,0:T(8,128)(2,1)S(1)} %get-tuple-element.62), channel_id=1, source_target_pairs={{0,28},{1,29},{2,30},{3,31},{4,24},{5,25},{6,26},{7,27},{8,4},{9,5... | collective-permute-start | bytes 368648 | tf_op jit(solution)/shard_map/ppermute | solution.py:608
  36.4 1.3 %collective-permute-start.14 = (bf16[16,3840]{1,0:T(8,128)(2,1)S(1)}, bf16[16,3840]{1,0:T(8,128)(2,1)S(1)}, u32[]{:S(2)}, u32[]{:S(2)}) collective-permute-start(bf16[16,3840]{1,0:T(8,128)(2,1)S(1)} %get-tuple-element.61.refs_0_), channel_id=1, source_target_pairs={{0,30},{1,31},{2,28},{3,29},{4,26},{5,27},{6,24},{7,25},{8,6},{9,7... | collective-permute-start | bytes 368648 | tf_op jit(solution)/shard_map/ppermute | solution.py:608
  37.7 1.4 %collective-permute-start.17 = (bf16[16,3840]{1,0:T(8,128)(2,1)S(1)}, bf16[16,3840]{1,0:T(8,128)(2,1)S(1)}, u32[]{:S(2)}, u32[]{:S(2)}) collective-permute-start(bf16[16,3840]{1,0:T(8,128)(2,1)S(1)} %get-tuple-element.63), channel_id=1, source_target_pairs={{0,24},{1,25},{2,26},{3,27},{4,28},{5,29},{6,30},{7,31},{8,0},{9,1... | collective-permute-start | bytes 368648 | tf_op jit(solution)/shard_map/ppermute | solution.py:608
  39.2 0.9 %collective-permute-start.11 = (bf16[16,3840]{1,0:T(8,128)(2,1)S(1)}, bf16[16,3840]{1,0:T(8,128)(2,1)S(1)}, u32[]{:S(2)}, u32[]{:S(2)}) collective-permute-start(bf16[16,3840]{1,0:T(8,128)(2,1)S(1)} %lower_chunk.1), channel_id=1, source_target_pairs={{0,2},{1,3},{2,0},{3,1},{4,6},{5,7},{6,4},{7,5},{8,10},{9,11},{10,... | collective-permute-start | bytes 368648 | tf_op jit(solution)/shard_map/ppermute | solution.py:587
  40.4 1.7 %collective-permute-done.16.refs_4_ = bf16[16,3840]{1,0:T(8,128)(2,1)S(1)} collective-permute-done((bf16[16,3840]{1,0:T(8,128)(2,1)S(1)}, bf16[16,3840]{1,0:T(8,128)(2,1)S(1)}, u32[]{:S(2)}, u32[]{:S(2)}) %collective-permute-start.16) | collective-permute-done | bytes 122912 | tf_op jit(solution)/shard_map/ppermute | solution.py:608
  42.1 4.5 %collective-permute-done.17.refs_5_ = bf16[16,3840]{1,0:T(8,128)(2,1)S(1)} collective-permute-done((bf16[16,3840]{1,0:T(8,128)(2,1)S(1)}, bf16[16,3840]{1,0:T(8,128)(2,1)S(1)}, u32[]{:S(2)}, u32[]{:S(2)}) %collective-permute-start.17) | collective-permute-done | bytes 122912 | tf_op jit(solution)/shard_map/ppermute | solution.py:608
  46.6 1.2 %all_rows.1 = (bf16[64,3584]{1,0:T(8,128)(2,1)}, bf16[64,3584]{1,0:T(8,128)(2,1)}) custom-call(bf16[16,3840]{1,0:T(8,128)(2,1)S(1)} %collective-permute-done.11.refs_0_, bf16[64,3584]{1,0:T(8,128)(2,1)S(1)} %forward_rows_early.1.refs_1_, bf16[16,3840]{1,0:T(8,128)(2,1)S(1)} %collective-permute-done.14.refs_2_, ...), custom_call_target="tpu_custom_call" | custom-call | flops 100000000 | bytes 1000 | tf_op jit(solution)/shard_map/all_rows/pallas_call | solution.py:41
  (29 shorter events, 1.7 us)
Async XLA Ops:
  2.8 9.1 %collective-permute-start = (bf16[16,3840]{1,0:T(8,128)(2,1)S(1)}, bf16[16,3840]{1,0:T(8,128)(2,1)S(1)}, u32[]{:S(2)}, u32[]{:S(2)}) collective-permute-start(bf16[16,3840]{1,0:T(8,128)(2,1)S(1)} %get-tuple-element.34), channel_id=1, source_target_pairs={{0,2},{1,3},{2,0},{3,1},{4,6},{5,7},{6,4},{7,5},{8,10},{9,11},{10,... | collective-permute-start | bytes 368648 | tf_op jit(solution)/shard_map/ppermute | solution.py:587
  5.8 8.2 %collective-permute-start.1 = (bf16[16,3840]{1,0:T(8,128)(2,1)S(1)}, bf16[16,3840]{1,0:T(8,128)(2,1)S(1)}, u32[]{:S(2)}, u32[]{:S(2)}) collective-permute-start(bf16[16,3840]{1,0:T(8,128)(2,1)S(1)} %get-tuple-element.35), channel_id=1, source_target_pairs={{0,4},{1,5},{2,6},{3,7},{4,0},{5,1},{6,2},{7,3},{8,12},{9,13},{10,... | collective-permute-start | bytes 368648 | tf_op jit(solution)/shard_map/ppermute | solution.py:587
  7.3 7.2 %collective-permute-start.2 = (bf16[16,3840]{1,0:T(8,128)(2,1)S(1)}, bf16[16,3840]{1,0:T(8,128)(2,1)S(1)}, u32[]{:S(2)}, u32[]{:S(2)}) collective-permute-start(bf16[16,3840]{1,0:T(8,128)(2,1)S(1)} %get-tuple-element.36), channel_id=1, source_target_pairs={{0,6},{1,7},{2,4},{3,5},{4,2},{5,3},{6,0},{7,1},{8,14},{9,15},{10,... | collective-permute-start | bytes 368648 | tf_op jit(solution)/shard_map/ppermute | solution.py:587
  7.3 5.6 %copy-start = (bf16[1,3584,512]{2,1,0:T(8,128)(2,1)S(1)}, bf16[1,3584,512]{2,1,0:T(8,128)(2,1)}, u32[]{:S(2)}) copy-start(bf16[1,3584,512]{2,1,0:T(8,128)(2,1)} %weights_ref.3) | copy-start | bytes 11010052
  7.3 5.6 %copy-start.1 = (bf16[1,512,3584]{2,1,0:T(8,128)(2,1)S(1)}, bf16[1,512,3584]{2,1,0:T(8,128)(2,1)}, u32[]{:S(2)}) copy-start(bf16[1,512,3584]{2,1,0:T(8,128)(2,1)} %refs_3_.1) | copy-start | bytes 11010052
  8.3 16.1 %collective-permute-start.6 = (bf16[32,3840]{1,0:T(8,128)(2,1)S(1)}, bf16[32,3840]{1,0:T(8,128)(2,1)S(1)}, u32[]{:S(2)}, u32[]{:S(2)}) collective-permute-start(bf16[32,3840]{1,0:T(8,128)(2,1)S(1)} %get-tuple-element.51), channel_id=1, source_target_pairs={{0,2},{1,3},{2,0},{3,1},{4,6},{5,7},{6,4},{7,5},{8,10},{9,11},{10,... | collective-permute-start | bytes 737288 | tf_op jit(solution)/shard_map/ppermute | solution.py:587
  10.3 14.1 %collective-permute-start.7 = (bf16[32,3840]{1,0:T(8,128)(2,1)S(1)}, bf16[32,3840]{1,0:T(8,128)(2,1)S(1)}, u32[]{:S(2)}, u32[]{:S(2)}) collective-permute-start(bf16[32,3840]{1,0:T(8,128)(2,1)S(1)} %get-tuple-element.52), channel_id=1, source_target_pairs={{0,4},{1,5},{2,6},{3,7},{4,0},{5,1},{6,2},{7,3},{8,12},{9,13},{10,... | collective-permute-start | bytes 737288 | tf_op jit(solution)/shard_map/ppermute | solution.py:587
  11.9 12.6 %collective-permute-start.8 = (bf16[32,3840]{1,0:T(8,128)(2,1)S(1)}, bf16[32,3840]{1,0:T(8,128)(2,1)S(1)}, u32[]{:S(2)}, u32[]{:S(2)}) collective-permute-start(bf16[32,3840]{1,0:T(8,128)(2,1)S(1)} %get-tuple-element.53), channel_id=1, source_target_pairs={{0,6},{1,7},{2,4},{3,5},{4,2},{5,3},{6,0},{7,1},{8,14},{9,15},{10,... | collective-permute-start | bytes 737288 | tf_op jit(solution)/shard_map/ppermute | solution.py:587
  15.0 2.0 %collective-permute-start.3 = (bf16[80,3584]{1,0:T(8,128)(2,1)S(1)}, bf16[80,3584]{1,0:T(8,128)(2,1)S(1)}, u32[]{:S(2)}, u32[]{:S(2)}) collective-permute-start(bf16[80,3584]{1,0:T(8,128)(2,1)S(1)} %get-tuple-element.46.refs_0_), channel_id=1, source_target_pairs={{0,1},{1,0},{2,3},{3,2},{4,5},{5,4},{6,7},{7,6},{8,9},{9,8},{10,11... | collective-permute-start | bytes 1720328 | tf_op jit(solution)/shard_map/ppermute | solution.py:597
  18.5 2.0 %collective-permute-start.4 = (bf16[80,3584]{1,0:T(8,128)(2,1)S(1)}, bf16[80,3584]{1,0:T(8,128)(2,1)S(1)}, u32[]{:S(2)}, u32[]{:S(2)}) collective-permute-start(bf16[80,3584]{1,0:T(8,128)(2,1)S(1)} %get-tuple-element.49), channel_id=1, source_target_pairs={{0,1},{1,0},{2,3},{3,2},{4,5},{5,4},{6,7},{7,6},{8,9},{9,8},{10,11... | collective-permute-start | bytes 1720328 | tf_op jit(solution)/shard_map/ppermute | solution.py:597
  20.7 15.7 %collective-permute-start.5 = (bf16[32,3840]{1,0:T(8,128)(2,1)S(1)}, bf16[32,3840]{1,0:T(8,128)(2,1)S(1)}, u32[]{:S(2)}, u32[]{:S(2)}) collective-permute-start(bf16[32,3840]{1,0:T(8,128)(2,1)S(1)} %finish_forward_01.1.refs_6_), channel_id=1, source_target_pairs={{0,8},{1,9},{2,10},{3,11},{4,12},{5,13},{6,14},{7,15},{8,16},{9,17... | collective-permute-start | bytes 737288 | tf_op jit(solution)/shard_map/ppermute | solution.py:608
  22.5 15.2 %collective-permute-start.12 = (bf16[16,3840]{1,0:T(8,128)(2,1)S(1)}, bf16[16,3840]{1,0:T(8,128)(2,1)S(1)}, u32[]{:S(2)}, u32[]{:S(2)}) collective-permute-start(bf16[16,3840]{1,0:T(8,128)(2,1)S(1)} %finish_forward_2.1.refs_4_), channel_id=1, source_target_pairs={{0,12},{1,13},{2,14},{3,15},{4,8},{5,9},{6,10},{7,11},{8,20},{9,21... | collective-permute-start | bytes 368648 | tf_op jit(solution)/shard_map/ppermute | solution.py:608
  24.5 3.3 %collective-permute-start.9 = (bf16[80,3584]{1,0:T(8,128)(2,1)S(1)}, bf16[80,3584]{1,0:T(8,128)(2,1)S(1)}, u32[]{:S(2)}, u32[]{:S(2)}) collective-permute-start(bf16[80,3584]{1,0:T(8,128)(2,1)S(1)} %get-tuple-element.55.refs_4_.refs_0_), channel_id=1, source_target_pairs={{0,1},{1,0},{2,3},{3,2},{4,5},{5,4},{6,7},{7,6},{8,9},{9,8},{10,11... | collective-permute-start | bytes 1720328 | tf_op jit(solution)/shard_map/ppermute | solution.py:597
  25.0 14.2 %collective-permute-start.13 = (bf16[16,3840]{1,0:T(8,128)(2,1)S(1)}, bf16[16,3840]{1,0:T(8,128)(2,1)S(1)}, u32[]{:S(2)}, u32[]{:S(2)}) collective-permute-start(bf16[16,3840]{1,0:T(8,128)(2,1)S(1)} %finish_forward_3.1), channel_id=1, source_target_pairs={{0,14},{1,15},{2,12},{3,13},{4,10},{5,11},{6,8},{7,9},{8,22},{9,23... | collective-permute-start | bytes 368648 | tf_op jit(solution)/shard_map/ppermute | solution.py:608
  29.3 2.1 %collective-permute-start.10 = (bf16[80,3712]{1,0:T(8,128)(2,1)S(1)}, bf16[80,3712]{1,0:T(8,128)(2,1)S(1)}, u32[]{:S(2)}, u32[]{:S(2)}) collective-permute-start(bf16[80,3712]{1,0:T(8,128)(2,1)S(1)} %get-tuple-element.60), channel_id=1, source_target_pairs={{0,1},{1,0},{2,3},{3,2},{4,5},{5,4},{6,7},{7,6},{8,9},{9,8},{10,11... | collective-permute-start | bytes 1781768 | tf_op jit(solution)/shard_map/ppermute | solution.py:597
  31.7 14.9 %collective-permute-start.15 = (bf16[16,3840]{1,0:T(8,128)(2,1)S(1)}, bf16[16,3840]{1,0:T(8,128)(2,1)S(1)}, u32[]{:S(2)}, u32[]{:S(2)}) collective-permute-start(bf16[16,3840]{1,0:T(8,128)(2,1)S(1)} %finish_backward_1.1.refs_11_), channel_id=1, source_target_pairs={{0,26},{1,27},{2,24},{3,25},{4,30},{5,31},{6,28},{7,29},{8,2},{9,3... | collective-permute-start | bytes 368648 | tf_op jit(solution)/shard_map/ppermute | solution.py:608
  34.9 7.2 %collective-permute-start.16 = (bf16[16,3840]{1,0:T(8,128)(2,1)S(1)}, bf16[16,3840]{1,0:T(8,128)(2,1)S(1)}, u32[]{:S(2)}, u32[]{:S(2)}) collective-permute-start(bf16[16,3840]{1,0:T(8,128)(2,1)S(1)} %get-tuple-element.62), channel_id=1, source_target_pairs={{0,28},{1,29},{2,30},{3,31},{4,24},{5,25},{6,26},{7,27},{8,4},{9,5... | collective-permute-start | bytes 368648 | tf_op jit(solution)/shard_map/ppermute | solution.py:608
  36.4 10.1 %collective-permute-start.14 = (bf16[16,3840]{1,0:T(8,128)(2,1)S(1)}, bf16[16,3840]{1,0:T(8,128)(2,1)S(1)}, u32[]{:S(2)}, u32[]{:S(2)}) collective-permute-start(bf16[16,3840]{1,0:T(8,128)(2,1)S(1)} %get-tuple-element.61.refs_0_), channel_id=1, source_target_pairs={{0,30},{1,31},{2,28},{3,29},{4,26},{5,27},{6,24},{7,25},{8,6},{9,7... | collective-permute-start | bytes 368648 | tf_op jit(solution)/shard_map/ppermute | solution.py:608
  37.7 8.8 %collective-permute-start.17 = (bf16[16,3840]{1,0:T(8,128)(2,1)S(1)}, bf16[16,3840]{1,0:T(8,128)(2,1)S(1)}, u32[]{:S(2)}, u32[]{:S(2)}) collective-permute-start(bf16[16,3840]{1,0:T(8,128)(2,1)S(1)} %get-tuple-element.63), channel_id=1, source_target_pairs={{0,24},{1,25},{2,26},{3,27},{4,28},{5,29},{6,30},{7,31},{8,0},{9,1... | collective-permute-start | bytes 368648 | tf_op jit(solution)/shard_map/ppermute | solution.py:608
  39.2 7.4 %collective-permute-start.11 = (bf16[16,3840]{1,0:T(8,128)(2,1)S(1)}, bf16[16,3840]{1,0:T(8,128)(2,1)S(1)}, u32[]{:S(2)}, u32[]{:S(2)}) collective-permute-start(bf16[16,3840]{1,0:T(8,128)(2,1)S(1)} %lower_chunk.1), channel_id=1, source_target_pairs={{0,2},{1,3},{2,0},{3,1},{4,6},{5,7},{6,4},{7,5},{8,10},{9,11},{10,... | collective-permute-start | bytes 368648 | tf_op jit(solution)/shard_map/ppermute | solution.py:587

commit v18 on v15

--- a/solution.py
+++ b/solution.py
@@ -26,7 +26,7 @@
     "backward_chunks": 10,
     "saved_rows": 15,
     "saved_terms": 15,
-    "act_norms": 15,
+    "finish_forward_3": 15,
     "act_gates": 15,
     "forward_rows_early": 15,
 }
@@ -644,10 +644,10 @@
     got2 = to_section(z, out2, 2, 1)
     grads, grad_last = grad_rows_of(z, bwd_own, [out2])
     grad_all = [grads] + [to_core(z, grads, m) for m in others]
-    inv, act_last = act_norms(z, bwd_own, [grads])
-    out3 = finish([3], [inv])
+    out3 = finish([3], [grads])
     got3 = to_section(z, out3, 3, 1)
-    bwd_parts = experts_backward(z, grad_all, hidden, slope, gate_turned, down_turned, [inv])
+    bwd_parts = experts_backward(z, grad_all, hidden, slope, gate_turned, down_turned, [out3])
+    inv, act_last = act_norms(z, bwd_own, [bwd_parts[0]])
     affinity = act_gates(z, bwd_own, act_last, inv, vectors, [bwd_parts[0]])
     fwd_done = [got2, got3]
     bwd_parts = [bwd_parts[0]] + [to_core(z, bwd_parts[m], m) for m in others]

time: 47.9 us -> 47.9 us (level)
  no operation moved by 1% of the time
where the time goes in v18:
time: 47.9 us; the launch traced here: 47.7 us
  starting transfers between devices  23.9 us (50%)
  Pallas kernels  13.6 us (28%)
  waiting for transfers between devices  9.36 us (20%)
  between operations  0.79 us (2%)
    pallas_call x19, Pallas kernels, run(): return kernel(*arrays)  13.6 us
    ppermute x7, starting transfers between devices, to_section(): return lax.ppermute(chunk, ('pp', 'ep'), pairs)  13.2 us
    ppermute x7, starting transfers between devices, permute_blocks(): return [lax.ppermute(array, 'ep', pairs) for array in arrays]  10.1 us
    ppermute x7, waiting for transfers between devices, to_section(): return lax.ppermute(chunk, ('pp', 'ep'), pairs)  6.69 us
    ppermute x4, waiting for transfers between devices, to_core(): return lax.ppermute(array, 'ep', pairs)  2.15 us
  transfers between devices with their start and end apart: 18, of which 6 were waited for; matrix products, arithmetic and copies ran while one was open for 0% of the time, Pallas kernels for 22%

profile of v18, /device:TPU:0, one launch (start us, length us, event | category | flops | bytes accessed | tf_op | source)
XLA Modules:
  0.0 47.7 jit_solution(15834684150322887251)
XLA Ops:
  0.7 2.0 %forward_chunks.1 = (bf16[16,3840]{1,0:T(8,128)(2,1)S(1)}, bf16[16,3840]{1,0:T(8,128)(2,1)S(1)}, bf16[16,3840]{1,0:T(8,128)(2,1)S(1)}, bf16[16,3840]{1,0:T(8,128...) custom-call(s32[2]{0:T(128)S(1)} %pad_add_fusion.where, ...), custom_call_target="tpu_custom_call" | custom-call | flops 100000000 | bytes 1000 | tf_op jit(solution)/shard_map/forward_chunks/pallas_call | solution.py:41
  2.8 3.0 %collective-permute-start = (bf16[16,3840]{1,0:T(8,128)(2,1)S(1)}, bf16[16,3840]{1,0:T(8,128)(2,1)S(1)}, u32[]{:S(2)}, u32[]{:S(2)}) collective-permute-start(bf16[16,3840]{1,0:T(8,128)(2,1)S(1)} %get-tuple-element.35), channel_id=1, source_target_pairs={{0,2},{1,3},{2,0},{3,1},{4,6},{5,7},{6,4},{7,5},{8,10},{9,11},{10,... | collective-permute-start | bytes 368648 | tf_op jit(solution)/shard_map/ppermute | solution.py:585
  5.8 1.5 %collective-permute-start.1 = (bf16[16,3840]{1,0:T(8,128)(2,1)S(1)}, bf16[16,3840]{1,0:T(8,128)(2,1)S(1)}, u32[]{:S(2)}, u32[]{:S(2)}) collective-permute-start(bf16[16,3840]{1,0:T(8,128)(2,1)S(1)} %get-tuple-element.36), channel_id=1, source_target_pairs={{0,4},{1,5},{2,6},{3,7},{4,0},{5,1},{6,2},{7,3},{8,12},{9,13},{10,... | collective-permute-start | bytes 368648 | tf_op jit(solution)/shard_map/ppermute | solution.py:585
  7.3 1.0 %backward_chunks.1 = (bf16[32,3840]{1,0:T(8,128)(2,1)S(1)}, bf16[32,3840]{1,0:T(8,128)(2,1)S(1)}, bf16[32,3840]{1,0:T(8,128)(2,1)S(1)}, bf16[32,3840]{1,0:T(8,128)(2,1)S(1)}, f32[8,3584]{1,0:T(8,128)S(1)}) custom-call(s32[2]{0:T(128)S(1)} %pad_add_fusion.where, bf16[80,64]{1,0:T(8,128)(2,1)S(1)} %get-tuple-element.38.selector, ...), custom_call_target="tpu_custom_call" | custom-call | flops 10000000000 | bytes 1000 | tf_op jit(solution)/shard_map/backward_chunks/pallas_call | solution.py:41
  8.3 2.0 %collective-permute-start.6 = (bf16[32,3840]{1,0:T(8,128)(2,1)S(1)}, bf16[32,3840]{1,0:T(8,128)(2,1)S(1)}, u32[]{:S(2)}, u32[]{:S(2)}) collective-permute-start(bf16[32,3840]{1,0:T(8,128)(2,1)S(1)} %get-tuple-element.52), channel_id=1, source_target_pairs={{0,2},{1,3},{2,0},{3,1},{4,6},{5,7},{6,4},{7,5},{8,10},{9,11},{10,... | collective-permute-start | bytes 737288 | tf_op jit(solution)/shard_map/ppermute | solution.py:585
  10.3 1.5 %collective-permute-start.7 = (bf16[32,3840]{1,0:T(8,128)(2,1)S(1)}, bf16[32,3840]{1,0:T(8,128)(2,1)S(1)}, u32[]{:S(2)}, u32[]{:S(2)}) collective-permute-start(bf16[32,3840]{1,0:T(8,128)(2,1)S(1)} %get-tuple-element.53), channel_id=1, source_target_pairs={{0,4},{1,5},{2,6},{3,7},{4,0},{5,1},{6,2},{7,3},{8,12},{9,13},{10,... | collective-permute-start | bytes 737288 | tf_op jit(solution)/shard_map/ppermute | solution.py:585
  11.9 1.1 %collective-permute-start.8 = (bf16[32,3840]{1,0:T(8,128)(2,1)S(1)}, bf16[32,3840]{1,0:T(8,128)(2,1)S(1)}, u32[]{:S(2)}, u32[]{:S(2)}) collective-permute-start(bf16[32,3840]{1,0:T(8,128)(2,1)S(1)} %get-tuple-element.54), channel_id=1, source_target_pairs={{0,6},{1,7},{2,4},{3,5},{4,2},{5,3},{6,0},{7,1},{8,14},{9,15},{10,... | collective-permute-start | bytes 737288 | tf_op jit(solution)/shard_map/ppermute | solution.py:585
  13.0 1.0 %turned_down.1.refs_5_ = bf16[3584,512]{1,0:T(8,128)(2,1)S(1)} custom-call(bf16[1,512,3584]{2,1,0:T(8,128)(2,1)S(1)} %copy-done.1, bf16[1,3584,512]{2,1,0:T(8,128)(2,1)S(1)} %copy-done, bf16[32,3840]{1,0:T(8,128)(2,1)S(1)} %get-tuple-element.45.refs_1_.refs_0_, bf16[16,3840]{1,0:T(8,128)(2,1)S(1)} %collective-permute-done.refs_2_.refs_1_), custom_call_target="tpu_custom_call" | custom-call | flops 100000000 | bytes 1000 | tf_op jit(solution)/shard_map/turned_down/pallas_call | solution.py:41
  14.0 0.5 %collective-permute-done.2.refs_3_.refs_0_ = bf16[16,3840]{1,0:T(8,128)(2,1)S(1)} collective-permute-done((bf16[16,3840]{1,0:T(8,128)(2,1)S(1)}, bf16[16,3840]{1,0:T(8,128)(2,1)S(1)}, u32[]{:S(2)}, u32[]{:S(2)}) %collective-permute-start.2) | collective-permute-done | bytes 122912 | tf_op jit(solution)/shard_map/ppermute | solution.py:585
  14.5 0.5 %normed_rows.1 = (bf16[80,3584]{1,0:T(8,128)(2,1)S(1)}, f32[80,128]{1,0:T(8,128)S(1)}, f32[16,3584]{1,0:T(8,128)S(1)}) custom-call(bf16[16,3840]{1,0:T(8,128)(2,1)S(1)} %get-tuple-element.34.refs_0_, bf16[16,3840]{1,0:T(8,128)(2,1)S(1)} %collective-permute-done.refs_2_.refs_1_, bf16[16,3840]{1,0:T(8,128)(2,1)S(1)} %collective-permute-done.1.refs_2_.refs_0_, ...), custom_call_target="tpu_custom_call" | custom-call | flops 100000000 | bytes 1000 | tf_op jit(solution)/shard_map/normed_rows/pallas_call | solution.py:41
  15.0 1.6 %saved_rows.1.refs_4_.ordered_ref = f32[160,512]{1,0:T(8,128)S(1)} custom-call(s32[2]{0:T(128)S(1)} %pad_add_fusion.where, bf16[1,1,136,512]{3,2,1,0:T(8,128)(2,1)} %saved_any.1, f32[80,128]{1,0:T(8,128)S(1)} %get-tuple-element.48.refs_0_.refs_5_.refs_4_), custom_call_target="tpu_custom_call" | custom-call | flops 15000000512 | bytes 1000 | tf_op jit(solution)/shard_map/saved_rows/pallas_call | solution.py:41
  16.7 0.3 collective-permute-done.3.refs_1_
  17.0 1.5 %experts_forward.1 = (bf16[80,3584]{1,0:T(8,128)(2,1)S(1)}, bf16[80,3584]{1,0:T(8,128)(2,1)S(1)}) custom-call(bf16[80,3584]{1,0:T(8,128)(2,1)S(1)} %get-tuple-element.47.refs_0_, bf16[80,3584]{1,0:T(8,128)(2,1)S(1)} %collective-permute-done.3.refs_1_, bf16[1,3584,512]{2,1,0:T(8,128)(2,1)S(1)} %copy-done, bf16[1,512,3584]{2,1,0:T(8,128)(2,1)S(1)} %copy-done.1, ...), custom_call_target="tpu_custom_call" | custom-call | flops 100000000 | bytes 1000 | tf_op jit(solution)/shard_map/experts_forward/pallas_call | solution.py:41
  18.8 1.0 %turned_gate.1.refs_6_.refs_4_ = bf16[512,3584]{1,0:T(8,128)(2,1)S(1)} custom-call(bf16[1,3584,512]{2,1,0:T(8,128)(2,1)S(1)} %copy-done, bf16[160,512]{1,0:T(8,128)(2,1)S(1)} %get-tuple-element.51.refs_0_.refs_5_.refs_2_), custom_call_target="tpu_custom_call" | custom-call | flops 100000000 | bytes 1000 | tf_op jit(solution)/shard_map/turned_gate/pallas_call | solution.py:41
  19.8 0.7 %collective-permute-done.4.refs_4_.refs_3_ = bf16[80,3584]{1,0:T(8,128)(2,1)S(1)} collective-permute-done((bf16[80,3584]{1,0:T(8,128)(2,1)S(1)}, bf16[80,3584]{1,0:T(8,128)(2,1)S(1)}, u32[]{:S(2)}, u32[]{:S(2)}) %collective-permute-start.4) | collective-permute-done | bytes 573472 | tf_op jit(solution)/shard_map/ppermute | solution.py:595
  20.7 1.6 %collective-permute-start.5 = (bf16[32,3840]{1,0:T(8,128)(2,1)S(1)}, bf16[32,3840]{1,0:T(8,128)(2,1)S(1)}, u32[]{:S(2)}, u32[]{:S(2)}) collective-permute-start(bf16[32,3840]{1,0:T(8,128)(2,1)S(1)} %finish_forward_01.1.refs_6_), channel_id=1, source_target_pairs={{0,8},{1,9},{2,10},{3,11},{4,12},{5,13},{6,14},{7,15},{8,16},{9,17... | collective-permute-start | bytes 737288 | tf_op jit(solution)/shard_map/ppermute | solution.py:606
  22.5 1.9 %collective-permute-start.12 = (bf16[16,3840]{1,0:T(8,128)(2,1)S(1)}, bf16[16,3840]{1,0:T(8,128)(2,1)S(1)}, u32[]{:S(2)}, u32[]{:S(2)}) collective-permute-start(bf16[16,3840]{1,0:T(8,128)(2,1)S(1)} %finish_forward_2.1.refs_4_), channel_id=1, source_target_pairs={{0,12},{1,13},{2,14},{3,15},{4,8},{5,9},{6,10},{7,11},{8,20},{9,21... | collective-permute-start | bytes 368648 | tf_op jit(solution)/shard_map/ppermute | solution.py:606
  24.7 2.8 %collective-permute-start.13 = (bf16[16,3840]{1,0:T(8,128)(2,1)S(1)}, bf16[16,3840]{1,0:T(8,128)(2,1)S(1)}, u32[]{:S(2)}, u32[]{:S(2)}) collective-permute-start(bf16[16,3840]{1,0:T(8,128)(2,1)S(1)} %finish_forward_3.1.refs_6_), channel_id=1, source_target_pairs={{0,14},{1,15},{2,12},{3,13},{4,10},{5,11},{6,8},{7,9},{8,22},{9,23... | collective-permute-start | bytes 368648 | tf_op jit(solution)/shard_map/ppermute | solution.py:606
  27.5 1.5 %experts_backward.1 = (bf16[80,3712]{1,0:T(8,128)(2,1)S(1)}, bf16[80,3712]{1,0:T(8,128)(2,1)S(1)}) custom-call(bf16[80,3584]{1,0:T(8,128)(2,1)S(1)} %get-tuple-element.56.refs_5_.refs_0_, bf16[80,3584]{1,0:T(8,128)(2,1)S(1)} %collective-permute-done.9.refs_1_, bf16[160,512]{1,0:T(8,128)(2,1)S(1)} %get-tuple-element.51.refs_0_.refs_5_.refs_2_, ...), custom_call_target="tpu_custom_call" | custom-call | flops 100000000 | bytes 1000 | tf_op jit(solution)/shard_map/experts_backward/pallas_call | solution.py:41
  29.0 0.3 collective-permute-start.10
  29.5 0.4 act_gates.1.refs_7_
  29.9 1.2 %collective-permute-done.10.refs_9_ = bf16[80,3712]{1,0:T(8,128)(2,1)S(1)} collective-permute-done((bf16[80,3712]{1,0:T(8,128)(2,1)S(1)}, bf16[80,3712]{1,0:T(8,128)(2,1)S(1)}, u32[]{:S(2)}, u32[]{:S(2)}) %collective-permute-start.10) | collective-permute-done | bytes 593952 | tf_op jit(solution)/shard_map/ppermute | solution.py:595
  31.1 0.7 %finish_backward.1 = (bf16[16,3840]{1,0:T(8,128)(2,1)S(1)}, bf16[16,3840]{1,0:T(8,128)(2,1)S(1)}, bf16[16,3840]{1,0:T(8,128)(2,1)S(1)}, bf16[16,3840]{1,0:T(8,128)(2,1)S(1)}) custom-call(bf16[32,3840]{1,0:T(8,128)(2,1)S(1)} %get-tuple-element.45.refs_1_.refs_0_, bf16[32,3840]{1,0:T(8,128)(2,1)S(1)} %collective-permute-done.6.refs_1_, ...), custom_call_target="tpu_custom_call" | custom-call | flops 100000000 | bytes 1000 | tf_op jit(solution)/shard_map/finish_backward/pallas_call | solution.py:41
  31.8 2.7 %collective-permute-start.15 = (bf16[16,3840]{1,0:T(8,128)(2,1)S(1)}, bf16[16,3840]{1,0:T(8,128)(2,1)S(1)}, u32[]{:S(2)}, u32[]{:S(2)}) collective-permute-start(bf16[16,3840]{1,0:T(8,128)(2,1)S(1)} %get-tuple-element.63), channel_id=1, source_target_pairs={{0,26},{1,27},{2,24},{3,25},{4,30},{5,31},{6,28},{7,29},{8,2},{9,3... | collective-permute-start | bytes 368648 | tf_op jit(solution)/shard_map/ppermute | solution.py:606
  34.4 1.5 %collective-permute-start.16 = (bf16[16,3840]{1,0:T(8,128)(2,1)S(1)}, bf16[16,3840]{1,0:T(8,128)(2,1)S(1)}, u32[]{:S(2)}, u32[]{:S(2)}) collective-permute-start(bf16[16,3840]{1,0:T(8,128)(2,1)S(1)} %get-tuple-element.64), channel_id=1, source_target_pairs={{0,28},{1,29},{2,30},{3,31},{4,24},{5,25},{6,26},{7,27},{8,4},{9,5... | collective-permute-start | bytes 368648 | tf_op jit(solution)/shard_map/ppermute | solution.py:606
  35.9 1.3 %collective-permute-start.14 = (bf16[16,3840]{1,0:T(8,128)(2,1)S(1)}, bf16[16,3840]{1,0:T(8,128)(2,1)S(1)}, u32[]{:S(2)}, u32[]{:S(2)}) collective-permute-start(bf16[16,3840]{1,0:T(8,128)(2,1)S(1)} %get-tuple-element.62.refs_0_), channel_id=1, source_target_pairs={{0,30},{1,31},{2,28},{3,29},{4,26},{5,27},{6,24},{7,25},{8,6},{9,7... | collective-permute-start | bytes 368648 | tf_op jit(solution)/shard_map/ppermute | solution.py:606
  37.2 1.4 %collective-permute-start.17 = (bf16[16,3840]{1,0:T(8,128)(2,1)S(1)}, bf16[16,3840]{1,0:T(8,128)(2,1)S(1)}, u32[]{:S(2)}, u32[]{:S(2)}) collective-permute-start(bf16[16,3840]{1,0:T(8,128)(2,1)S(1)} %get-tuple-element.65), channel_id=1, source_target_pairs={{0,24},{1,25},{2,26},{3,27},{4,28},{5,29},{6,30},{7,31},{8,0},{9,1... | collective-permute-start | bytes 368648 | tf_op jit(solution)/shard_map/ppermute | solution.py:606
  38.7 0.9 %collective-permute-start.11 = (bf16[16,3840]{1,0:T(8,128)(2,1)S(1)}, bf16[16,3840]{1,0:T(8,128)(2,1)S(1)}, u32[]{:S(2)}, u32[]{:S(2)}) collective-permute-start(bf16[16,3840]{1,0:T(8,128)(2,1)S(1)} %lower_chunk.1), channel_id=1, source_target_pairs={{0,2},{1,3},{2,0},{3,1},{4,6},{5,7},{6,4},{7,5},{8,10},{9,11},{10,... | collective-permute-start | bytes 368648 | tf_op jit(solution)/shard_map/ppermute | solution.py:585
  39.6 0.3 forward_rows_early.1.refs_1_
  39.9 1.7 %collective-permute-done.16.refs_4_ = bf16[16,3840]{1,0:T(8,128)(2,1)S(1)} collective-permute-done((bf16[16,3840]{1,0:T(8,128)(2,1)S(1)}, bf16[16,3840]{1,0:T(8,128)(2,1)S(1)}, u32[]{:S(2)}, u32[]{:S(2)}) %collective-permute-start.16) | collective-permute-done | bytes 122912 | tf_op jit(solution)/shard_map/ppermute | solution.py:606
  41.6 5.0 %collective-permute-done.17.refs_5_ = bf16[16,3840]{1,0:T(8,128)(2,1)S(1)} collective-permute-done((bf16[16,3840]{1,0:T(8,128)(2,1)S(1)}, bf16[16,3840]{1,0:T(8,128)(2,1)S(1)}, u32[]{:S(2)}, u32[]{:S(2)}) %collective-permute-start.17) | collective-permute-done | bytes 122912 | tf_op jit(solution)/shard_map/ppermute | solution.py:606
  46.5 1.2 %all_rows.1 = (bf16[64,3584]{1,0:T(8,128)(2,1)}, bf16[64,3584]{1,0:T(8,128)(2,1)}) custom-call(bf16[16,3840]{1,0:T(8,128)(2,1)S(1)} %collective-permute-done.11.refs_0_, bf16[64,3584]{1,0:T(8,128)(2,1)S(1)} %forward_rows_early.1.refs_1_, bf16[16,3840]{1,0:T(8,128)(2,1)S(1)} %collective-permute-done.14.refs_2_, ...), custom_call_target="tpu_custom_call" | custom-call | flops 100000000 | bytes 1000 | tf_op jit(solution)/shard_map/all_rows/pallas_call | solution.py:41
  (28 shorter events, 1.4 us)
Async XLA Ops:
  2.8 9.1 %collective-permute-start = (bf16[16,3840]{1,0:T(8,128)(2,1)S(1)}, bf16[16,3840]{1,0:T(8,128)(2,1)S(1)}, u32[]{:S(2)}, u32[]{:S(2)}) collective-permute-start(bf16[16,3840]{1,0:T(8,128)(2,1)S(1)} %get-tuple-element.35), channel_id=1, source_target_pairs={{0,2},{1,3},{2,0},{3,1},{4,6},{5,7},{6,4},{7,5},{8,10},{9,11},{10,... | collective-permute-start | bytes 368648 | tf_op jit(solution)/shard_map/ppermute | solution.py:585
  5.8 8.2 %collective-permute-start.1 = (bf16[16,3840]{1,0:T(8,128)(2,1)S(1)}, bf16[16,3840]{1,0:T(8,128)(2,1)S(1)}, u32[]{:S(2)}, u32[]{:S(2)}) collective-permute-start(bf16[16,3840]{1,0:T(8,128)(2,1)S(1)} %get-tuple-element.36), channel_id=1, source_target_pairs={{0,4},{1,5},{2,6},{3,7},{4,0},{5,1},{6,2},{7,3},{8,12},{9,13},{10,... | collective-permute-start | bytes 368648 | tf_op jit(solution)/shard_map/ppermute | solution.py:585
  7.3 7.2 %collective-permute-start.2 = (bf16[16,3840]{1,0:T(8,128)(2,1)S(1)}, bf16[16,3840]{1,0:T(8,128)(2,1)S(1)}, u32[]{:S(2)}, u32[]{:S(2)}) collective-permute-start(bf16[16,3840]{1,0:T(8,128)(2,1)S(1)} %get-tuple-element.37), channel_id=1, source_target_pairs={{0,6},{1,7},{2,4},{3,5},{4,2},{5,3},{6,0},{7,1},{8,14},{9,15},{10,... | collective-permute-start | bytes 368648 | tf_op jit(solution)/shard_map/ppermute | solution.py:585
  7.3 5.6 %copy-start = (bf16[1,3584,512]{2,1,0:T(8,128)(2,1)S(1)}, bf16[1,3584,512]{2,1,0:T(8,128)(2,1)}, u32[]{:S(2)}) copy-start(bf16[1,3584,512]{2,1,0:T(8,128)(2,1)} %weights_ref.3) | copy-start | bytes 11010052
  7.3 5.6 %copy-start.1 = (bf16[1,512,3584]{2,1,0:T(8,128)(2,1)S(1)}, bf16[1,512,3584]{2,1,0:T(8,128)(2,1)}, u32[]{:S(2)}) copy-start(bf16[1,512,3584]{2,1,0:T(8,128)(2,1)} %refs_3_.1) | copy-start | bytes 11010052
  8.3 16.1 %collective-permute-start.6 = (bf16[32,3840]{1,0:T(8,128)(2,1)S(1)}, bf16[32,3840]{1,0:T(8,128)(2,1)S(1)}, u32[]{:S(2)}, u32[]{:S(2)}) collective-permute-start(bf16[32,3840]{1,0:T(8,128)(2,1)S(1)} %get-tuple-element.52), channel_id=1, source_target_pairs={{0,2},{1,3},{2,0},{3,1},{4,6},{5,7},{6,4},{7,5},{8,10},{9,11},{10,... | collective-permute-start | bytes 737288 | tf_op jit(solution)/shard_map/ppermute | solution.py:585
  10.3 14.1 %collective-permute-start.7 = (bf16[32,3840]{1,0:T(8,128)(2,1)S(1)}, bf16[32,3840]{1,0:T(8,128)(2,1)S(1)}, u32[]{:S(2)}, u32[]{:S(2)}) collective-permute-start(bf16[32,3840]{1,0:T(8,128)(2,1)S(1)} %get-tuple-element.53), channel_id=1, source_target_pairs={{0,4},{1,5},{2,6},{3,7},{4,0},{5,1},{6,2},{7,3},{8,12},{9,13},{10,... | collective-permute-start | bytes 737288 | tf_op jit(solution)/shard_map/ppermute | solution.py:585
  11.9 12.6 %collective-permute-start.8 = (bf16[32,3840]{1,0:T(8,128)(2,1)S(1)}, bf16[32,3840]{1,0:T(8,128)(2,1)S(1)}, u32[]{:S(2)}, u32[]{:S(2)}) collective-permute-start(bf16[32,3840]{1,0:T(8,128)(2,1)S(1)} %get-tuple-element.54), channel_id=1, source_target_pairs={{0,6},{1,7},{2,4},{3,5},{4,2},{5,3},{6,0},{7,1},{8,14},{9,15},{10,... | collective-permute-start | bytes 737288 | tf_op jit(solution)/shard_map/ppermute | solution.py:585
  15.0 2.0 %collective-permute-start.3 = (bf16[80,3584]{1,0:T(8,128)(2,1)S(1)}, bf16[80,3584]{1,0:T(8,128)(2,1)S(1)}, u32[]{:S(2)}, u32[]{:S(2)}) collective-permute-start(bf16[80,3584]{1,0:T(8,128)(2,1)S(1)} %get-tuple-element.47.refs_0_), channel_id=1, source_target_pairs={{0,1},{1,0},{2,3},{3,2},{4,5},{5,4},{6,7},{7,6},{8,9},{9,8},{10,11... | collective-permute-start | bytes 1720328 | tf_op jit(solution)/shard_map/ppermute | solution.py:595
  18.5 2.0 %collective-permute-start.4 = (bf16[80,3584]{1,0:T(8,128)(2,1)S(1)}, bf16[80,3584]{1,0:T(8,128)(2,1)S(1)}, u32[]{:S(2)}, u32[]{:S(2)}) collective-permute-start(bf16[80,3584]{1,0:T(8,128)(2,1)S(1)} %get-tuple-element.50), channel_id=1, source_target_pairs={{0,1},{1,0},{2,3},{3,2},{4,5},{5,4},{6,7},{7,6},{8,9},{9,8},{10,11... | collective-permute-start | bytes 1720328 | tf_op jit(solution)/shard_map/ppermute | solution.py:595
  20.7 15.2 %collective-permute-start.5 = (bf16[32,3840]{1,0:T(8,128)(2,1)S(1)}, bf16[32,3840]{1,0:T(8,128)(2,1)S(1)}, u32[]{:S(2)}, u32[]{:S(2)}) collective-permute-start(bf16[32,3840]{1,0:T(8,128)(2,1)S(1)} %finish_forward_01.1.refs_6_), channel_id=1, source_target_pairs={{0,8},{1,9},{2,10},{3,11},{4,12},{5,13},{6,14},{7,15},{8,16},{9,17... | collective-permute-start | bytes 737288 | tf_op jit(solution)/shard_map/ppermute | solution.py:606
  22.5 14.7 %collective-permute-start.12 = (bf16[16,3840]{1,0:T(8,128)(2,1)S(1)}, bf16[16,3840]{1,0:T(8,128)(2,1)S(1)}, u32[]{:S(2)}, u32[]{:S(2)}) collective-permute-start(bf16[16,3840]{1,0:T(8,128)(2,1)S(1)} %finish_forward_2.1.refs_4_), channel_id=1, source_target_pairs={{0,12},{1,13},{2,14},{3,15},{4,8},{5,9},{6,10},{7,11},{8,20},{9,21... | collective-permute-start | bytes 368648 | tf_op jit(solution)/shard_map/ppermute | solution.py:606
  24.5 3.0 %collective-permute-start.9 = (bf16[80,3584]{1,0:T(8,128)(2,1)S(1)}, bf16[80,3584]{1,0:T(8,128)(2,1)S(1)}, u32[]{:S(2)}, u32[]{:S(2)}) collective-permute-start(bf16[80,3584]{1,0:T(8,128)(2,1)S(1)} %get-tuple-element.56.refs_5_.refs_0_), channel_id=1, source_target_pairs={{0,1},{1,0},{2,3},{3,2},{4,5},{5,4},{6,7},{7,6},{8,9},{9,8},{10,11... | collective-permute-start | bytes 1720328 | tf_op jit(solution)/shard_map/ppermute | solution.py:595
  24.7 13.9 %collective-permute-start.13 = (bf16[16,3840]{1,0:T(8,128)(2,1)S(1)}, bf16[16,3840]{1,0:T(8,128)(2,1)S(1)}, u32[]{:S(2)}, u32[]{:S(2)}) collective-permute-start(bf16[16,3840]{1,0:T(8,128)(2,1)S(1)} %finish_forward_3.1.refs_6_), channel_id=1, source_target_pairs={{0,14},{1,15},{2,12},{3,13},{4,10},{5,11},{6,8},{7,9},{8,22},{9,23... | collective-permute-start | bytes 368648 | tf_op jit(solution)/shard_map/ppermute | solution.py:606
  29.0 2.1 %collective-permute-start.10 = (bf16[80,3712]{1,0:T(8,128)(2,1)S(1)}, bf16[80,3712]{1,0:T(8,128)(2,1)S(1)}, u32[]{:S(2)}, u32[]{:S(2)}) collective-permute-start(bf16[80,3712]{1,0:T(8,128)(2,1)S(1)} %get-tuple-element.61), channel_id=1, source_target_pairs={{0,1},{1,0},{2,3},{3,2},{4,5},{5,4},{6,7},{7,6},{8,9},{9,8},{10,11... | collective-permute-start | bytes 1781768 | tf_op jit(solution)/shard_map/ppermute | solution.py:595
  31.8 8.1 %collective-permute-start.15 = (bf16[16,3840]{1,0:T(8,128)(2,1)S(1)}, bf16[16,3840]{1,0:T(8,128)(2,1)S(1)}, u32[]{:S(2)}, u32[]{:S(2)}) collective-permute-start(bf16[16,3840]{1,0:T(8,128)(2,1)S(1)} %get-tuple-element.63), channel_id=1, source_target_pairs={{0,26},{1,27},{2,24},{3,25},{4,30},{5,31},{6,28},{7,29},{8,2},{9,3... | collective-permute-start | bytes 368648 | tf_op jit(solution)/shard_map/ppermute | solution.py:606
  34.4 7.1 %collective-permute-start.16 = (bf16[16,3840]{1,0:T(8,128)(2,1)S(1)}, bf16[16,3840]{1,0:T(8,128)(2,1)S(1)}, u32[]{:S(2)}, u32[]{:S(2)}) collective-permute-start(bf16[16,3840]{1,0:T(8,128)(2,1)S(1)} %get-tuple-element.64), channel_id=1, source_target_pairs={{0,28},{1,29},{2,30},{3,31},{4,24},{5,25},{6,26},{7,27},{8,4},{9,5... | collective-permute-start | bytes 368648 | tf_op jit(solution)/shard_map/ppermute | solution.py:606
  35.9 10.6 %collective-permute-start.14 = (bf16[16,3840]{1,0:T(8,128)(2,1)S(1)}, bf16[16,3840]{1,0:T(8,128)(2,1)S(1)}, u32[]{:S(2)}, u32[]{:S(2)}) collective-permute-start(bf16[16,3840]{1,0:T(8,128)(2,1)S(1)} %get-tuple-element.62.refs_0_), channel_id=1, source_target_pairs={{0,30},{1,31},{2,28},{3,29},{4,26},{5,27},{6,24},{7,25},{8,6},{9,7... | collective-permute-start | bytes 368648 | tf_op jit(solution)/shard_map/ppermute | solution.py:606
  37.2 9.3 %collective-permute-start.17 = (bf16[16,3840]{1,0:T(8,128)(2,1)S(1)}, bf16[16,3840]{1,0:T(8,128)(2,1)S(1)}, u32[]{:S(2)}, u32[]{:S(2)}) collective-permute-start(bf16[16,3840]{1,0:T(8,128)(2,1)S(1)} %get-tuple-element.65), channel_id=1, source_target_pairs={{0,24},{1,25},{2,26},{3,27},{4,28},{5,29},{6,30},{7,31},{8,0},{9,1... | collective-permute-start | bytes 368648 | tf_op jit(solution)/shard_map/ppermute | solution.py:606
  38.7 7.9 %collective-permute-start.11 = (bf16[16,3840]{1,0:T(8,128)(2,1)S(1)}, bf16[16,3840]{1,0:T(8,128)(2,1)S(1)}, u32[]{:S(2)}, u32[]{:S(2)}) collective-permute-start(bf16[16,3840]{1,0:T(8,128)(2,1)S(1)} %lower_chunk.1), channel_id=1, source_target_pairs={{0,2},{1,3},{2,0},{3,1},{4,6},{5,7},{6,4},{7,5},{8,10},{9,11},{10,... | collective-permute-start | bytes 368648 | tf_op jit(solution)/shard_map/ppermute | solution.py:585

commit v19 on v18

--- a/solution.py
+++ b/solution.py
@@ -624,7 +624,7 @@
     bwd_chunks, vectors = backward_chunks(z, where, slots, [grad, act], gain_row, table)
     bwd_own = dispatch(z, bwd_chunks)
 
-    down_turned = turned(z, w_down, [w_gate], [bwd_chunks[0], fwd_own[1]], "turned_down")
+    down_turned = turned(z, w_down, [w_gate], [bwd_chunks[0]], "turned_down")
     normed, gates, fwd_last = normed_rows(z, fwd_own, vectors, [down_turned])
     fwd_all = [normed] + [to_core(z, normed, m) for m in others]
     ordered = saved_rows(z, where, saved_gate, [], [gates])

time: 47.9 us -> 47.9 us (level)
  starting transfers between devices: 23.9 us -> 24.4 us
  waiting for transfers between devices: 9.36 us -> 8.86 us
    ppermute x7, starting transfers between devices: 10.1 us -> 10.6 us  [permute_blocks(): return [lax.ppermute(array, 'ep', pairs) for array in arrays]]
    ppermute x7, waiting for transfers between devices: 0.52 us -> 0.02 us  [permute_blocks(): return [lax.ppermute(array, 'ep', pairs) for array in arrays]]
  transfers between devices with their start and end apart: 18 -> 18, of which waited for: 6 -> 5; matrix products, arithmetic and copies ran while one was open for 0% -> 0% of each run, Pallas kernels for 22% -> 22%
where the time goes in v19:
time: 47.9 us; the launch traced here: 47.7 us
  starting transfers between devices  24.4 us (51%)
  Pallas kernels  13.6 us (28%)
  waiting for transfers between devices  8.86 us (18%)
  between operations  0.79 us (2%)
    pallas_call x19, Pallas kernels, run(): return kernel(*arrays)  13.6 us
    ppermute x7, starting transfers between devices, to_section(): return lax.ppermute(chunk, ('pp', 'ep'), pairs)  13.2 us
    ppermute x7, starting transfers between devices, permute_blocks(): return [lax.ppermute(array, 'ep', pairs) for array in arrays]  10.6 us
    ppermute x7, waiting for transfers between devices, to_section(): return lax.ppermute(chunk, ('pp', 'ep'), pairs)  6.67 us
    ppermute x4, waiting for transfers between devices, to_core(): return lax.ppermute(array, 'ep', pairs)  2.17 us
  transfers between devices with their start and end apart: 18, of which 5 were waited for; matrix products, arithmetic and copies ran while one was open for 0% of the time, Pallas kernels for 22%

profile of v19, /device:TPU:0, one launch (start us, length us, event | category | flops | bytes accessed | tf_op | source)
XLA Modules:
  0.0 47.7 jit_solution(7793720290957948383)
XLA Ops:
  0.7 2.0 %forward_chunks.1 = (bf16[16,3840]{1,0:T(8,128)(2,1)S(1)}, bf16[16,3840]{1,0:T(8,128)(2,1)S(1)}, bf16[16,3840]{1,0:T(8,128)(2,1)S(1)}, bf16[16,3840]{1,0:T(8,128...) custom-call(s32[2]{0:T(128)S(1)} %pad_add_fusion.where, ...), custom_call_target="tpu_custom_call" | custom-call | flops 100000000 | bytes 1000 | tf_op jit(solution)/shard_map/forward_chunks/pallas_call | solution.py:41
  2.8 3.0 %collective-permute-start = (bf16[16,3840]{1,0:T(8,128)(2,1)S(1)}, bf16[16,3840]{1,0:T(8,128)(2,1)S(1)}, u32[]{:S(2)}, u32[]{:S(2)}) collective-permute-start(bf16[16,3840]{1,0:T(8,128)(2,1)S(1)} %get-tuple-element.35), channel_id=1, source_target_pairs={{0,2},{1,3},{2,0},{3,1},{4,6},{5,7},{6,4},{7,5},{8,10},{9,11},{10,... | collective-permute-start | bytes 368648 | tf_op jit(solution)/shard_map/ppermute | solution.py:585
  5.8 1.5 %collective-permute-start.1 = (bf16[16,3840]{1,0:T(8,128)(2,1)S(1)}, bf16[16,3840]{1,0:T(8,128)(2,1)S(1)}, u32[]{:S(2)}, u32[]{:S(2)}) collective-permute-start(bf16[16,3840]{1,0:T(8,128)(2,1)S(1)} %get-tuple-element.36), channel_id=1, source_target_pairs={{0,4},{1,5},{2,6},{3,7},{4,0},{5,1},{6,2},{7,3},{8,12},{9,13},{10,... | collective-permute-start | bytes 368648 | tf_op jit(solution)/shard_map/ppermute | solution.py:585
  7.3 1.0 %backward_chunks.1 = (bf16[32,3840]{1,0:T(8,128)(2,1)S(1)}, bf16[32,3840]{1,0:T(8,128)(2,1)S(1)}, bf16[32,3840]{1,0:T(8,128)(2,1)S(1)}, bf16[32,3840]{1,0:T(8,128)(2,1)S(1)}, f32[8,3584]{1,0:T(8,128)S(1)}) custom-call(s32[2]{0:T(128)S(1)} %pad_add_fusion.where, bf16[80,64]{1,0:T(8,128)(2,1)S(1)} %get-tuple-element.38.selector, ...), custom_call_target="tpu_custom_call" | custom-call | flops 10000000000 | bytes 1000 | tf_op jit(solution)/shard_map/backward_chunks/pallas_call | solution.py:41
  8.3 2.0 %collective-permute-start.6 = (bf16[32,3840]{1,0:T(8,128)(2,1)S(1)}, bf16[32,3840]{1,0:T(8,128)(2,1)S(1)}, u32[]{:S(2)}, u32[]{:S(2)}) collective-permute-start(bf16[32,3840]{1,0:T(8,128)(2,1)S(1)} %get-tuple-element.52), channel_id=1, source_target_pairs={{0,2},{1,3},{2,0},{3,1},{4,6},{5,7},{6,4},{7,5},{8,10},{9,11},{10,... | collective-permute-start | bytes 737288 | tf_op jit(solution)/shard_map/ppermute | solution.py:585
  10.3 1.5 %collective-permute-start.7 = (bf16[32,3840]{1,0:T(8,128)(2,1)S(1)}, bf16[32,3840]{1,0:T(8,128)(2,1)S(1)}, u32[]{:S(2)}, u32[]{:S(2)}) collective-permute-start(bf16[32,3840]{1,0:T(8,128)(2,1)S(1)} %get-tuple-element.53), channel_id=1, source_target_pairs={{0,4},{1,5},{2,6},{3,7},{4,0},{5,1},{6,2},{7,3},{8,12},{9,13},{10,... | collective-permute-start | bytes 737288 | tf_op jit(solution)/shard_map/ppermute | solution.py:585
  11.9 1.0 %turned_down.1.refs_5_ = bf16[3584,512]{1,0:T(8,128)(2,1)S(1)} custom-call(bf16[1,512,3584]{2,1,0:T(8,128)(2,1)S(1)} %copy-done.1, bf16[1,3584,512]{2,1,0:T(8,128)(2,1)S(1)} %copy-done, bf16[32,3840]{1,0:T(8,128)(2,1)S(1)} %get-tuple-element.45.refs_1_.refs_0_), custom_call_target="tpu_custom_call" | custom-call | flops 100000000 | bytes 1000 | tf_op jit(solution)/shard_map/turned_down/pallas_call | solution.py:41
  12.9 1.6 %collective-permute-start.8 = (bf16[32,3840]{1,0:T(8,128)(2,1)S(1)}, bf16[32,3840]{1,0:T(8,128)(2,1)S(1)}, u32[]{:S(2)}, u32[]{:S(2)}) collective-permute-start(bf16[32,3840]{1,0:T(8,128)(2,1)S(1)} %get-tuple-element.54), channel_id=1, source_target_pairs={{0,6},{1,7},{2,4},{3,5},{4,2},{5,3},{6,0},{7,1},{8,14},{9,15},{10,... | collective-permute-start | bytes 737288 | tf_op jit(solution)/shard_map/ppermute | solution.py:585
  14.5 0.5 %normed_rows.1 = (bf16[80,3584]{1,0:T(8,128)(2,1)S(1)}, f32[80,128]{1,0:T(8,128)S(1)}, f32[16,3584]{1,0:T(8,128)S(1)}) custom-call(bf16[16,3840]{1,0:T(8,128)(2,1)S(1)} %get-tuple-element.34.refs_0_, bf16[16,3840]{1,0:T(8,128)(2,1)S(1)} %collective-permute-done.refs_1_, bf16[16,3840]{1,0:T(8,128)(2,1)S(1)} %collective-permute-done.1.refs_2_.refs_0_, ...), custom_call_target="tpu_custom_call" | custom-call | flops 100000000 | bytes 1000 | tf_op jit(solution)/shard_map/normed_rows/pallas_call | solution.py:41
  15.0 1.6 %saved_rows.1.refs_4_.ordered_ref = f32[160,512]{1,0:T(8,128)S(1)} custom-call(s32[2]{0:T(128)S(1)} %pad_add_fusion.where, bf16[1,1,136,512]{3,2,1,0:T(8,128)(2,1)} %saved_any.1, f32[80,128]{1,0:T(8,128)S(1)} %get-tuple-element.48.refs_0_.refs_5_.refs_4_), custom_call_target="tpu_custom_call" | custom-call | flops 15000000512 | bytes 1000 | tf_op jit(solution)/shard_map/saved_rows/pallas_call | solution.py:41
  16.7 0.3 collective-permute-done.3.refs_1_
  17.0 1.5 %experts_forward.1 = (bf16[80,3584]{1,0:T(8,128)(2,1)S(1)}, bf16[80,3584]{1,0:T(8,128)(2,1)S(1)}) custom-call(bf16[80,3584]{1,0:T(8,128)(2,1)S(1)} %get-tuple-element.47.refs_0_, bf16[80,3584]{1,0:T(8,128)(2,1)S(1)} %collective-permute-done.3.refs_1_, bf16[1,3584,512]{2,1,0:T(8,128)(2,1)S(1)} %copy-done, bf16[1,512,3584]{2,1,0:T(8,128)(2,1)S(1)} %copy-done.1, ...), custom_call_target="tpu_custom_call" | custom-call | flops 100000000 | bytes 1000 | tf_op jit(solution)/shard_map/experts_forward/pallas_call | solution.py:41
  18.5 0.2 collective-permute-start.4
  18.8 1.0 %turned_gate.1.refs_6_.refs_4_ = bf16[512,3584]{1,0:T(8,128)(2,1)S(1)} custom-call(bf16[1,3584,512]{2,1,0:T(8,128)(2,1)S(1)} %copy-done, bf16[160,512]{1,0:T(8,128)(2,1)S(1)} %get-tuple-element.51.refs_0_.refs_5_.refs_2_), custom_call_target="tpu_custom_call" | custom-call | flops 100000000 | bytes 1000 | tf_op jit(solution)/shard_map/turned_gate/pallas_call | solution.py:41
  19.8 0.7 %collective-permute-done.4.refs_4_.refs_3_ = bf16[80,3584]{1,0:T(8,128)(2,1)S(1)} collective-permute-done((bf16[80,3584]{1,0:T(8,128)(2,1)S(1)}, bf16[80,3584]{1,0:T(8,128)(2,1)S(1)}, u32[]{:S(2)}, u32[]{:S(2)}) %collective-permute-start.4) | collective-permute-done | bytes 573472 | tf_op jit(solution)/shard_map/ppermute | solution.py:595
  20.7 1.6 %collective-permute-start.5 = (bf16[32,3840]{1,0:T(8,128)(2,1)S(1)}, bf16[32,3840]{1,0:T(8,128)(2,1)S(1)}, u32[]{:S(2)}, u32[]{:S(2)}) collective-permute-start(bf16[32,3840]{1,0:T(8,128)(2,1)S(1)} %finish_forward_01.1.refs_6_), channel_id=1, source_target_pairs={{0,8},{1,9},{2,10},{3,11},{4,12},{5,13},{6,14},{7,15},{8,16},{9,17... | collective-permute-start | bytes 737288 | tf_op jit(solution)/shard_map/ppermute | solution.py:606
  22.5 1.9 %collective-permute-start.12 = (bf16[16,3840]{1,0:T(8,128)(2,1)S(1)}, bf16[16,3840]{1,0:T(8,128)(2,1)S(1)}, u32[]{:S(2)}, u32[]{:S(2)}) collective-permute-start(bf16[16,3840]{1,0:T(8,128)(2,1)S(1)} %finish_forward_2.1.refs_4_), channel_id=1, source_target_pairs={{0,12},{1,13},{2,14},{3,15},{4,8},{5,9},{6,10},{7,11},{8,20},{9,21... | collective-permute-start | bytes 368648 | tf_op jit(solution)/shard_map/ppermute | solution.py:606
  24.7 2.8 %collective-permute-start.13 = (bf16[16,3840]{1,0:T(8,128)(2,1)S(1)}, bf16[16,3840]{1,0:T(8,128)(2,1)S(1)}, u32[]{:S(2)}, u32[]{:S(2)}) collective-permute-start(bf16[16,3840]{1,0:T(8,128)(2,1)S(1)} %finish_forward_3.1.refs_6_), channel_id=1, source_target_pairs={{0,14},{1,15},{2,12},{3,13},{4,10},{5,11},{6,8},{7,9},{8,22},{9,23... | collective-permute-start | bytes 368648 | tf_op jit(solution)/shard_map/ppermute | solution.py:606
  27.5 1.5 %experts_backward.1 = (bf16[80,3712]{1,0:T(8,128)(2,1)S(1)}, bf16[80,3712]{1,0:T(8,128)(2,1)S(1)}) custom-call(bf16[80,3584]{1,0:T(8,128)(2,1)S(1)} %get-tuple-element.56.refs_5_.refs_0_, bf16[80,3584]{1,0:T(8,128)(2,1)S(1)} %collective-permute-done.9.refs_1_, bf16[160,512]{1,0:T(8,128)(2,1)S(1)} %get-tuple-element.51.refs_0_.refs_5_.refs_2_, ...), custom_call_target="tpu_custom_call" | custom-call | flops 100000000 | bytes 1000 | tf_op jit(solution)/shard_map/experts_backward/pallas_call | solution.py:41
  29.0 0.3 collective-permute-start.10
  29.5 0.4 act_gates.1.refs_7_
  29.9 1.2 %collective-permute-done.10.refs_9_ = bf16[80,3712]{1,0:T(8,128)(2,1)S(1)} collective-permute-done((bf16[80,3712]{1,0:T(8,128)(2,1)S(1)}, bf16[80,3712]{1,0:T(8,128)(2,1)S(1)}, u32[]{:S(2)}, u32[]{:S(2)}) %collective-permute-start.10) | collective-permute-done | bytes 593952 | tf_op jit(solution)/shard_map/ppermute | solution.py:595
  31.1 0.7 %finish_backward.1 = (bf16[16,3840]{1,0:T(8,128)(2,1)S(1)}, bf16[16,3840]{1,0:T(8,128)(2,1)S(1)}, bf16[16,3840]{1,0:T(8,128)(2,1)S(1)}, bf16[16,3840]{1,0:T(8,128)(2,1)S(1)}) custom-call(bf16[32,3840]{1,0:T(8,128)(2,1)S(1)} %get-tuple-element.45.refs_1_.refs_0_, bf16[32,3840]{1,0:T(8,128)(2,1)S(1)} %collective-permute-done.6.refs_1_, ...), custom_call_target="tpu_custom_call" | custom-call | flops 100000000 | bytes 1000 | tf_op jit(solution)/shard_map/finish_backward/pallas_call | solution.py:41
  31.8 2.7 %collective-permute-start.15 = (bf16[16,3840]{1,0:T(8,128)(2,1)S(1)}, bf16[16,3840]{1,0:T(8,128)(2,1)S(1)}, u32[]{:S(2)}, u32[]{:S(2)}) collective-permute-start(bf16[16,3840]{1,0:T(8,128)(2,1)S(1)} %get-tuple-element.63), channel_id=1, source_target_pairs={{0,26},{1,27},{2,24},{3,25},{4,30},{5,31},{6,28},{7,29},{8,2},{9,3... | collective-permute-start | bytes 368648 | tf_op jit(solution)/shard_map/ppermute | solution.py:606
  34.4 1.5 %collective-permute-start.16 = (bf16[16,3840]{1,0:T(8,128)(2,1)S(1)}, bf16[16,3840]{1,0:T(8,128)(2,1)S(1)}, u32[]{:S(2)}, u32[]{:S(2)}) collective-permute-start(bf16[16,3840]{1,0:T(8,128)(2,1)S(1)} %get-tuple-element.64), channel_id=1, source_target_pairs={{0,28},{1,29},{2,30},{3,31},{4,24},{5,25},{6,26},{7,27},{8,4},{9,5... | collective-permute-start | bytes 368648 | tf_op jit(solution)/shard_map/ppermute | solution.py:606
  35.9 1.3 %collective-permute-start.14 = (bf16[16,3840]{1,0:T(8,128)(2,1)S(1)}, bf16[16,3840]{1,0:T(8,128)(2,1)S(1)}, u32[]{:S(2)}, u32[]{:S(2)}) collective-permute-start(bf16[16,3840]{1,0:T(8,128)(2,1)S(1)} %get-tuple-element.62.refs_0_), channel_id=1, source_target_pairs={{0,30},{1,31},{2,28},{3,29},{4,26},{5,27},{6,24},{7,25},{8,6},{9,7... | collective-permute-start | bytes 368648 | tf_op jit(solution)/shard_map/ppermute | solution.py:606
  37.2 1.4 %collective-permute-start.17 = (bf16[16,3840]{1,0:T(8,128)(2,1)S(1)}, bf16[16,3840]{1,0:T(8,128)(2,1)S(1)}, u32[]{:S(2)}, u32[]{:S(2)}) collective-permute-start(bf16[16,3840]{1,0:T(8,128)(2,1)S(1)} %get-tuple-element.65), channel_id=1, source_target_pairs={{0,24},{1,25},{2,26},{3,27},{4,28},{5,29},{6,30},{7,31},{8,0},{9,1... | collective-permute-start | bytes 368648 | tf_op jit(solution)/shard_map/ppermute | solution.py:606
  38.7 0.9 %collective-permute-start.11 = (bf16[16,3840]{1,0:T(8,128)(2,1)S(1)}, bf16[16,3840]{1,0:T(8,128)(2,1)S(1)}, u32[]{:S(2)}, u32[]{:S(2)}) collective-permute-start(bf16[16,3840]{1,0:T(8,128)(2,1)S(1)} %lower_chunk.1), channel_id=1, source_target_pairs={{0,2},{1,3},{2,0},{3,1},{4,6},{5,7},{6,4},{7,5},{8,10},{9,11},{10,... | collective-permute-start | bytes 368648 | tf_op jit(solution)/shard_map/ppermute | solution.py:585
  39.6 0.3 forward_rows_early.1.refs_1_
  39.9 1.7 %collective-permute-done.16.refs_4_ = bf16[16,3840]{1,0:T(8,128)(2,1)S(1)} collective-permute-done((bf16[16,3840]{1,0:T(8,128)(2,1)S(1)}, bf16[16,3840]{1,0:T(8,128)(2,1)S(1)}, u32[]{:S(2)}, u32[]{:S(2)}) %collective-permute-start.16) | collective-permute-done | bytes 122912 | tf_op jit(solution)/shard_map/ppermute | solution.py:606
  41.6 5.0 %collective-permute-done.17.refs_5_ = bf16[16,3840]{1,0:T(8,128)(2,1)S(1)} collective-permute-done((bf16[16,3840]{1,0:T(8,128)(2,1)S(1)}, bf16[16,3840]{1,0:T(8,128)(2,1)S(1)}, u32[]{:S(2)}, u32[]{:S(2)}) %collective-permute-start.17) | collective-permute-done | bytes 122912 | tf_op jit(solution)/shard_map/ppermute | solution.py:606
  46.5 1.2 %all_rows.1 = (bf16[64,3584]{1,0:T(8,128)(2,1)}, bf16[64,3584]{1,0:T(8,128)(2,1)}) custom-call(bf16[16,3840]{1,0:T(8,128)(2,1)S(1)} %collective-permute-done.11.refs_0_, bf16[64,3584]{1,0:T(8,128)(2,1)S(1)} %forward_rows_early.1.refs_1_, bf16[16,3840]{1,0:T(8,128)(2,1)S(1)} %collective-permute-done.14.refs_2_, ...), custom_call_target="tpu_custom_call" | custom-call | flops 100000000 | bytes 1000 | tf_op jit(solution)/shard_map/all_rows/pallas_call | solution.py:41
  (28 shorter events, 1.2 us)
Async XLA Ops:
  2.8 10.1 %collective-permute-start = (bf16[16,3840]{1,0:T(8,128)(2,1)S(1)}, bf16[16,3840]{1,0:T(8,128)(2,1)S(1)}, u32[]{:S(2)}, u32[]{:S(2)}) collective-permute-start(bf16[16,3840]{1,0:T(8,128)(2,1)S(1)} %get-tuple-element.35), channel_id=1, source_target_pairs={{0,2},{1,3},{2,0},{3,1},{4,6},{5,7},{6,4},{7,5},{8,10},{9,11},{10,... | collective-permute-start | bytes 368648 | tf_op jit(solution)/shard_map/ppermute | solution.py:585
  5.8 8.7 %collective-permute-start.1 = (bf16[16,3840]{1,0:T(8,128)(2,1)S(1)}, bf16[16,3840]{1,0:T(8,128)(2,1)S(1)}, u32[]{:S(2)}, u32[]{:S(2)}) collective-permute-start(bf16[16,3840]{1,0:T(8,128)(2,1)S(1)} %get-tuple-element.36), channel_id=1, source_target_pairs={{0,4},{1,5},{2,6},{3,7},{4,0},{5,1},{6,2},{7,3},{8,12},{9,13},{10,... | collective-permute-start | bytes 368648 | tf_op jit(solution)/shard_map/ppermute | solution.py:585
  7.3 7.2 %collective-permute-start.2 = (bf16[16,3840]{1,0:T(8,128)(2,1)S(1)}, bf16[16,3840]{1,0:T(8,128)(2,1)S(1)}, u32[]{:S(2)}, u32[]{:S(2)}) collective-permute-start(bf16[16,3840]{1,0:T(8,128)(2,1)S(1)} %get-tuple-element.37), channel_id=1, source_target_pairs={{0,6},{1,7},{2,4},{3,5},{4,2},{5,3},{6,0},{7,1},{8,14},{9,15},{10,... | collective-permute-start | bytes 368648 | tf_op jit(solution)/shard_map/ppermute | solution.py:585
  7.3 4.5 %copy-start = (bf16[1,3584,512]{2,1,0:T(8,128)(2,1)S(1)}, bf16[1,3584,512]{2,1,0:T(8,128)(2,1)}, u32[]{:S(2)}) copy-start(bf16[1,3584,512]{2,1,0:T(8,128)(2,1)} %weights_ref.3) | copy-start | bytes 11010052
  7.3 4.5 %copy-start.1 = (bf16[1,512,3584]{2,1,0:T(8,128)(2,1)S(1)}, bf16[1,512,3584]{2,1,0:T(8,128)(2,1)}, u32[]{:S(2)}) copy-start(bf16[1,512,3584]{2,1,0:T(8,128)(2,1)} %refs_3_.1) | copy-start | bytes 11010052
  8.3 16.1 %collective-permute-start.6 = (bf16[32,3840]{1,0:T(8,128)(2,1)S(1)}, bf16[32,3840]{1,0:T(8,128)(2,1)S(1)}, u32[]{:S(2)}, u32[]{:S(2)}) collective-permute-start(bf16[32,3840]{1,0:T(8,128)(2,1)S(1)} %get-tuple-element.52), channel_id=1, source_target_pairs={{0,2},{1,3},{2,0},{3,1},{4,6},{5,7},{6,4},{7,5},{8,10},{9,11},{10,... | collective-permute-start | bytes 737288 | tf_op jit(solution)/shard_map/ppermute | solution.py:585
  10.3 14.1 %collective-permute-start.7 = (bf16[32,3840]{1,0:T(8,128)(2,1)S(1)}, bf16[32,3840]{1,0:T(8,128)(2,1)S(1)}, u32[]{:S(2)}, u32[]{:S(2)}) collective-permute-start(bf16[32,3840]{1,0:T(8,128)(2,1)S(1)} %get-tuple-element.53), channel_id=1, source_target_pairs={{0,4},{1,5},{2,6},{3,7},{4,0},{5,1},{6,2},{7,3},{8,12},{9,13},{10,... | collective-permute-start | bytes 737288 | tf_op jit(solution)/shard_map/ppermute | solution.py:585
  12.9 11.5 %collective-permute-start.8 = (bf16[32,3840]{1,0:T(8,128)(2,1)S(1)}, bf16[32,3840]{1,0:T(8,128)(2,1)S(1)}, u32[]{:S(2)}, u32[]{:S(2)}) collective-permute-start(bf16[32,3840]{1,0:T(8,128)(2,1)S(1)} %get-tuple-element.54), channel_id=1, source_target_pairs={{0,6},{1,7},{2,4},{3,5},{4,2},{5,3},{6,0},{7,1},{8,14},{9,15},{10,... | collective-permute-start | bytes 737288 | tf_op jit(solution)/shard_map/ppermute | solution.py:585
  15.0 2.0 %collective-permute-start.3 = (bf16[80,3584]{1,0:T(8,128)(2,1)S(1)}, bf16[80,3584]{1,0:T(8,128)(2,1)S(1)}, u32[]{:S(2)}, u32[]{:S(2)}) collective-permute-start(bf16[80,3584]{1,0:T(8,128)(2,1)S(1)} %get-tuple-element.47.refs_0_), channel_id=1, source_target_pairs={{0,1},{1,0},{2,3},{3,2},{4,5},{5,4},{6,7},{7,6},{8,9},{9,8},{10,11... | collective-permute-start | bytes 1720328 | tf_op jit(solution)/shard_map/ppermute | solution.py:595
  18.5 2.0 %collective-permute-start.4 = (bf16[80,3584]{1,0:T(8,128)(2,1)S(1)}, bf16[80,3584]{1,0:T(8,128)(2,1)S(1)}, u32[]{:S(2)}, u32[]{:S(2)}) collective-permute-start(bf16[80,3584]{1,0:T(8,128)(2,1)S(1)} %get-tuple-element.50), channel_id=1, source_target_pairs={{0,1},{1,0},{2,3},{3,2},{4,5},{5,4},{6,7},{7,6},{8,9},{9,8},{10,11... | collective-permute-start | bytes 1720328 | tf_op jit(solution)/shard_map/ppermute | solution.py:595
  20.7 15.2 %collective-permute-start.5 = (bf16[32,3840]{1,0:T(8,128)(2,1)S(1)}, bf16[32,3840]{1,0:T(8,128)(2,1)S(1)}, u32[]{:S(2)}, u32[]{:S(2)}) collective-permute-start(bf16[32,3840]{1,0:T(8,128)(2,1)S(1)} %finish_forward_01.1.refs_6_), channel_id=1, source_target_pairs={{0,8},{1,9},{2,10},{3,11},{4,12},{5,13},{6,14},{7,15},{8,16},{9,17... | collective-permute-start | bytes 737288 | tf_op jit(solution)/shard_map/ppermute | solution.py:606
  22.5 14.7 %collective-permute-start.12 = (bf16[16,3840]{1,0:T(8,128)(2,1)S(1)}, bf16[16,3840]{1,0:T(8,128)(2,1)S(1)}, u32[]{:S(2)}, u32[]{:S(2)}) collective-permute-start(bf16[16,3840]{1,0:T(8,128)(2,1)S(1)} %finish_forward_2.1.refs_4_), channel_id=1, source_target_pairs={{0,12},{1,13},{2,14},{3,15},{4,8},{5,9},{6,10},{7,11},{8,20},{9,21... | collective-permute-start | bytes 368648 | tf_op jit(solution)/shard_map/ppermute | solution.py:606
  24.5 3.0 %collective-permute-start.9 = (bf16[80,3584]{1,0:T(8,128)(2,1)S(1)}, bf16[80,3584]{1,0:T(8,128)(2,1)S(1)}, u32[]{:S(2)}, u32[]{:S(2)}) collective-permute-start(bf16[80,3584]{1,0:T(8,128)(2,1)S(1)} %get-tuple-element.56.refs_5_.refs_0_), channel_id=1, source_target_pairs={{0,1},{1,0},{2,3},{3,2},{4,5},{5,4},{6,7},{7,6},{8,9},{9,8},{10,11... | collective-permute-start | bytes 1720328 | tf_op jit(solution)/shard_map/ppermute | solution.py:595
  24.7 13.9 %collective-permute-start.13 = (bf16[16,3840]{1,0:T(8,128)(2,1)S(1)}, bf16[16,3840]{1,0:T(8,128)(2,1)S(1)}, u32[]{:S(2)}, u32[]{:S(2)}) collective-permute-start(bf16[16,3840]{1,0:T(8,128)(2,1)S(1)} %finish_forward_3.1.refs_6_), channel_id=1, source_target_pairs={{0,14},{1,15},{2,12},{3,13},{4,10},{5,11},{6,8},{7,9},{8,22},{9,23... | collective-permute-start | bytes 368648 | tf_op jit(solution)/shard_map/ppermute | solution.py:606
  29.0 2.1 %collective-permute-start.10 = (bf16[80,3712]{1,0:T(8,128)(2,1)S(1)}, bf16[80,3712]{1,0:T(8,128)(2,1)S(1)}, u32[]{:S(2)}, u32[]{:S(2)}) collective-permute-start(bf16[80,3712]{1,0:T(8,128)(2,1)S(1)} %get-tuple-element.61), channel_id=1, source_target_pairs={{0,1},{1,0},{2,3},{3,2},{4,5},{5,4},{6,7},{7,6},{8,9},{9,8},{10,11... | collective-permute-start | bytes 1781768 | tf_op jit(solution)/shard_map/ppermute | solution.py:595
  31.8 8.1 %collective-permute-start.15 = (bf16[16,3840]{1,0:T(8,128)(2,1)S(1)}, bf16[16,3840]{1,0:T(8,128)(2,1)S(1)}, u32[]{:S(2)}, u32[]{:S(2)}) collective-permute-start(bf16[16,3840]{1,0:T(8,128)(2,1)S(1)} %get-tuple-element.63), channel_id=1, source_target_pairs={{0,26},{1,27},{2,24},{3,25},{4,30},{5,31},{6,28},{7,29},{8,2},{9,3... | collective-permute-start | bytes 368648 | tf_op jit(solution)/shard_map/ppermute | solution.py:606
  34.4 7.1 %collective-permute-start.16 = (bf16[16,3840]{1,0:T(8,128)(2,1)S(1)}, bf16[16,3840]{1,0:T(8,128)(2,1)S(1)}, u32[]{:S(2)}, u32[]{:S(2)}) collective-permute-start(bf16[16,3840]{1,0:T(8,128)(2,1)S(1)} %get-tuple-element.64), channel_id=1, source_target_pairs={{0,28},{1,29},{2,30},{3,31},{4,24},{5,25},{6,26},{7,27},{8,4},{9,5... | collective-permute-start | bytes 368648 | tf_op jit(solution)/shard_map/ppermute | solution.py:606
  35.9 10.6 %collective-permute-start.14 = (bf16[16,3840]{1,0:T(8,128)(2,1)S(1)}, bf16[16,3840]{1,0:T(8,128)(2,1)S(1)}, u32[]{:S(2)}, u32[]{:S(2)}) collective-permute-start(bf16[16,3840]{1,0:T(8,128)(2,1)S(1)} %get-tuple-element.62.refs_0_), channel_id=1, source_target_pairs={{0,30},{1,31},{2,28},{3,29},{4,26},{5,27},{6,24},{7,25},{8,6},{9,7... | collective-permute-start | bytes 368648 | tf_op jit(solution)/shard_map/ppermute | solution.py:606
  37.2 9.3 %collective-permute-start.17 = (bf16[16,3840]{1,0:T(8,128)(2,1)S(1)}, bf16[16,3840]{1,0:T(8,128)(2,1)S(1)}, u32[]{:S(2)}, u32[]{:S(2)}) collective-permute-start(bf16[16,3840]{1,0:T(8,128)(2,1)S(1)} %get-tuple-element.65), channel_id=1, source_target_pairs={{0,24},{1,25},{2,26},{3,27},{4,28},{5,29},{6,30},{7,31},{8,0},{9,1... | collective-permute-start | bytes 368648 | tf_op jit(solution)/shard_map/ppermute | solution.py:606
  38.7 7.9 %collective-permute-start.11 = (bf16[16,3840]{1,0:T(8,128)(2,1)S(1)}, bf16[16,3840]{1,0:T(8,128)(2,1)S(1)}, u32[]{:S(2)}, u32[]{:S(2)}) collective-permute-start(bf16[16,3840]{1,0:T(8,128)(2,1)S(1)} %lower_chunk.1), channel_id=1, source_target_pairs={{0,2},{1,3},{2,0},{3,1},{4,6},{5,7},{6,4},{7,5},{8,10},{9,11},{10,... | collective-permute-start | bytes 368648 | tf_op jit(solution)/shard_map/ppermute | solution.py:585
